TPU v7x, 32 devices: a whole 2x2x4 slice. The times are simulated.
32 devices in a mesh: blk: 4 (over y, x), tile: 8 (over z, core).
Axes of the slice: x: 2, y: 2, z: 4, core: 2. Of those that a mesh axis runs over, the one named last changes fastest.
Arguments:
- qkv: bfloat16 [3, 1024, 1024], P(None, ('blk', 'tile')), may hold values from -33 to 33
- frame_clip: int32 [8], replicated, may hold values from 0 to 2, never falling along the last dimension, each value on 1 to 5 neighbouring positions
- w_out: bfloat16 [1024, 5120], P('tile'), may hold values from -0.5 to 0.5
Outputs:
- projected: bfloat16 [1024, 5120], P(('blk', 'tile'))
All inputs are finite; a program needn't handle non-finite values.
Results may differ from a plain program's by a relative error of at most 0.023.
Values may be sent and summed in bfloat16 or wider, within the bound.
No kernel may reach another device: no remote copies, remote signals or barrier semaphores. Data moves between devices by JAX's collectives and lax.ppermute only.
A program may use at most 64 MiB of HBM per device.

v0:
```python
import math

import jax
import jax.numpy as jnp
from jax import lax
from jax.sharding import PartitionSpec as P

FRB = 2
TPF = 16


def clip_lookup(frames, frame_clip):
    table = jnp.arange(frame_clip.shape[0], dtype=jnp.int32)
    hits = (frames[..., None] == table).astype(jnp.int32)
    return jnp.sum(hits * frame_clip, axis=-1)


def on_device(qkv, frame_clip, w_out):
    tiles = lax.axis_size("tile")
    blk_index = lax.axis_index("blk")
    tok_dev = qkv.shape[1]
    head_dim = w_out.shape[0]
    tok_blk = tok_dev * tiles
    scale = 1.0 / math.sqrt(head_dim)
    local = lax.all_to_all(qkv, "tile", split_axis=2, concat_axis=1, tiled=True)
    queries = local[0]
    keys_all = local[1]
    values_all = local[2]
    rows = jnp.arange(tok_blk, dtype=jnp.int32)
    query_clip = clip_lookup(blk_index * FRB + rows % tok_dev // TPF, frame_clip)
    start_state = (
        jnp.full((tok_blk,), -1e30, jnp.float32),
        jnp.zeros((tok_blk,), jnp.float32),
        jnp.zeros((tok_blk, head_dim), jnp.float32),
    )
    carry = start_state
    key_piece = lax.all_gather(keys_all, "blk", axis=0, tiled=True)
    value_piece = lax.all_gather(values_all, "blk", axis=0, tiled=True)
    count = key_piece.shape[0]
    width = math.gcd(count, tok_blk)
    key_blocks = key_piece.reshape(count // width, width, head_dim)
    value_blocks = value_piece.reshape(count // width, width, head_dim)
    firsts = width * jnp.arange(count // width, dtype=jnp.int32)

    def advance(state, item):
        key_block, value_block, first = item
        index = first + jnp.arange(width, dtype=jnp.int32)
        key_clip = clip_lookup(index // tok_blk * FRB + index % tok_dev // TPF, frame_clip)
        allowed = query_clip[:, None] == key_clip[None, :]
        run_max, run_sum, run_acc = state
        scores = (
            jnp.einsum("qd,kd->qk", queries, key_block, preferred_element_type=jnp.float32) * scale
        )
        masked = jnp.where(allowed, scores, -1e30)
        new_max = jnp.maximum(run_max, jnp.max(masked, axis=1))
        weights = jnp.where(allowed, jnp.exp(scores - new_max[:, None]), 0.0)
        factor = jnp.exp(run_max - new_max)
        new_sum = run_sum * factor + jnp.sum(weights, axis=1)
        new_acc = run_acc * factor[:, None] + jnp.dot(
            weights.astype(jnp.bfloat16), value_block, preferred_element_type=jnp.float32
        )
        state = (new_max, new_sum, new_acc)
        return (state, None)

    carry, unused = lax.scan(advance, carry, (key_blocks, value_blocks, firsts))
    run_max, run_sum, run_acc = carry
    attn = (run_acc / run_sum[:, None]).astype(jnp.bfloat16)
    return lax.psum_scatter(
        jnp.dot(attn, w_out, preferred_element_type=jnp.float32).astype(jnp.bfloat16),
        "tile",
        scatter_dimension=0,
        tiled=True,
    )


def solution(mesh):
    in_specs = (P(None, ("blk", "tile"), None), P(), P("tile", None))
    out_specs = P(("blk", "tile"), None)
    return jax.shard_map(
        on_device, mesh=mesh, in_specs=in_specs, out_specs=out_specs, check_vma=False
    )
```

profile of v0, /device:TPU:0, one launch (start us, length us, event | category | flops | bytes accessed | tf_op | source)
XLA Modules:
  0.0 96.7 jit_solution(16786690498225654799)
XLA Ops:
  6.5 0.0 copy-start
  6.5 0.0 copy-start.1
  6.5 1.7 %copy.17 = bf16[3,32,1024]{1,0,2:T(4,128)(2,1)S(1)} copy(bf16[3,32,1024]{2,1,0:T(8,128)(2,1)} %param.5) | data formatting | bytes 393216 | tf_op args[0]
  8.2 1.4 %reshape.88 = bf16[8,2,6144]{2,1,0:T(2,128)(2,1)} reshape(bf16[1024,3,32]{2,1,0:T(4,128)(2,1)S(1)} %bitcast.31) | data formatting | bytes 393216
  9.6 6.3 %all-to-all-start = ((bf16[8,2,6144]{2,1,0:T(2,128)(2,1)}), bf16[8,2,6144]{2,1,0:T(2,128)(2,1)S(1)}, u32[]{:S(2)}, u32[]{:S(2)}) async-start(bf16[8,2,6144]{2,1,0:T(2,128)(2,1)} %reshape.88), calls=%async_computation | async-start | bytes 393216 | tf_op jit(solution)/shard_map/all_to_all | solution.py:25
  16.0 0.0 reduce-scatter.2.cloned.1.call-start
  16.1 0.0 copy-done.1
  16.1 0.1 select_reduce_fusion.1
  16.2 8.1 %all-to-all-done = bf16[8,2,6144]{2,1,0:T(2,128)(2,1)S(1)} async-done(((bf16[8,2,6144]{2,1,0:T(2,128)(2,1)}), bf16[8,2,6144]{2,1,0:T(2,128)(2,1)S(1)}, u32[]{:S(2)}, u32[]{:S(2)}) %all-to-all-start) | async-done | bytes 196640 | tf_op jit(solution)/shard_map/all_to_all | solution.py:25
  24.3 0.7 reshape.89
  25.0 0.5 copy.22
  25.6 9.2 %all_gather.6 = bf16[1024,128]{1,0:T(8,128)(2,1)S(1)} all-gather(bf16[256,128]{1,0:T(8,128)(2,1)S(1)} %bitcast.36), channel_id=1, replica_groups=mesh['blk'=4,'tile'=8] {'blk'}, dimensions={0}, use_global_device_ids=true | all-gather | bytes 327680 | tf_op jit(solution)/shard_map/all_gather | solution.py:37
  34.8 8.8 %all_gather.7 = bf16[1024,128]{1,0:T(8,128)(2,1)S(1)} all-gather(bf16[256,128]{1,0:T(8,128)(2,1)S(1)} %bitcast.35), channel_id=1, replica_groups=mesh['blk'=4,'tile'=8] {'blk'}, dimensions={0}, use_global_device_ids=true | all-gather | bytes 327680 | tf_op jit(solution)/shard_map/all_gather | solution.py:38
  43.5 8.2 %while.18 = (s32[]{:T(128)}, f32[256]{0:T(256)S(1)}, f32[256]{0:T(256)S(1)}, f32[256,128]{1,0:T(8,128)S(1)}, s32[256]{0:T(256)S(1)}, /*index=5*/s32[4]{0:T(128)S...) while((s32[]{:T(128)}, f32[256]{0:T(256)S(1)}, ...), condition=%wide.region_5.6_spmd.clone, body=%wide.region_1.5_spmd.clone.sunk | while | flops 34456832 | bytes 1270977 | solution.py:65
  43.5 0.6 dynamic_slice.41
  44.1 0.7 fusion.35
  44.8 0.1 select_reduce_fusion.3
  44.9 0.2 fusion.36
  45.1 0.1 fusion.38
  45.2 0.3 convolution_add_fusion.2
  45.6 0.6 dynamic_slice.41
  46.2 0.7 fusion.35
  46.8 0.1 select_reduce_fusion.3
  46.9 0.2 fusion.36
  47.2 0.1 fusion.38
  47.3 0.3 convolution_add_fusion.2
  47.7 0.6 dynamic_slice.41
  48.2 0.7 fusion.35
  48.9 0.1 select_reduce_fusion.3
  49.0 0.2 fusion.36
  49.2 0.1 fusion.38
  49.4 0.3 convolution_add_fusion.2
  49.7 0.6 dynamic_slice.41
  50.3 0.7 fusion.35
  51.0 0.1 select_reduce_fusion.3
  51.1 0.2 fusion.36
  51.3 0.1 fusion.38
  51.4 0.3 convolution_add_fusion.2
  51.8 0.0 copy-done
  51.8 2.4 %convolution_convert_fusion = bf16[256,5120]{1,0:T(8,128)(2,1)} fusion(bf16[128,5120]{1,0:T(8,128)(2,1)S(1)} %copy-done, f32[256,128]{1,0:T(8,128)S(1)} %get-tuple-element.169, f32[256]{0:T(256)S(1)} %get-tuple-element.170), kind=kOutput, calls=%fused_computation.38 | convolution fusion | flops 336920576 | bytes 4064256 | tf_op jit(solution)/shard_map/dot_general | solution.py:69
  54.2 0.0 reduce-scatter.2.cloned.1.call-update
  54.2 35.6 %reduce-scatter.2.cloned.1.call-done = bf16[32,5120]{1,0:T(8,128)(2,1)} async-done(((bf16[256,5120]{1,0:T(8,128)(2,1)}), bf16[32,5120]{1,0:T(8,128)(2,1)}) %reduce-scatter.2.cloned.1.call-update) | async-done | bytes 327696 | tf_op jit(solution)/shard_map/reduce_scatter | solution.py:68
  (21 shorter events, 0.2 us)
Async XLA Ops:
  6.5 45.2 %copy-start = (bf16[128,5120]{1,0:T(8,128)(2,1)S(1)}, bf16[128,5120]{1,0:T(8,128)(2,1)}, u32[]{:S(2)}) copy-start(bf16[128,5120]{1,0:T(8,128)(2,1)} %param.7) | copy-start | bytes 3932164
  6.5 9.5 %copy-start.1 = (s32[8]{0:T(128)S(1)}, s32[8]{0:T(128)}, u32[]{:S(2)}) copy-start(s32[8]{0:T(128)} %param.6) | copy-start | bytes 100
  9.6 14.7 %all-to-all-start = ((bf16[8,2,6144]{2,1,0:T(2,128)(2,1)}), bf16[8,2,6144]{2,1,0:T(2,128)(2,1)S(1)}, u32[]{:S(2)}, u32[]{:S(2)}) async-start(bf16[8,2,6144]{2,1,0:T(2,128)(2,1)} %reshape.88), calls=%async_computation | async-start | bytes 393216 | tf_op jit(solution)/shard_map/all_to_all | solution.py:25
  16.0 73.9 %reduce-scatter.2.cloned.1.call-start = ((), (), s32[]{:S(2)}) async-start(), calls=%async_computation.2 | async-start | bytes 2949120 | tf_op jit(solution)/shard_map/reduce_scatter | solution.py:68
Sparse Core Ops, SparseCore 0:
  54.3 35.4 reduce-scatter.1
where the time goes:
time: 97 us; the launch traced here: 96.7 us
  waiting for transfers between devices  43.7 us (45%)
  blocking collectives  18 us (19%)
  between operations  13.5 us (14%)
  local copies, waits for them, and re-layouts  6.67 us (7%)
  starting transfers between devices  6.36 us (7%)
  matrix products  4.58 us (5%)
  other arithmetic  3.64 us (4%)
    reduce_scatter x1, waiting for transfers between devices, on_device(): lax.psum_scatter(jnp.dot(attn, w_out, preferred_element_type=jnp.float32)...  35.6 us
    all_gather x1, blocking collectives, on_device(): key_piece = lax.all_gather(keys_all, 'blk', axis=0, tiled=True)  9.18 us
    all_gather x1, blocking collectives, on_device(): value_piece = lax.all_gather(values_all, 'blk', axis=0, tiled=True)  8.78 us
    all_to_all x1, waiting for transfers between devices, on_device(): local = lax.all_to_all(qkv, 'tile', split_axis=2, concat_axis=1, tiled=True)  8.13 us
    all_to_all x1, starting transfers between devices, on_device(): local = lax.all_to_all(qkv, 'tile', split_axis=2, concat_axis=1, tiled=True)  6.33 us
    unnamed x7, local copies, waits for them, and re-layouts  3.76 us
    add x4, other arithmetic, advance(): index // tok_blk * FRB + index % tok_dev // TPF  2.65 us
    dot_general x1, matrix products, on_device(): jnp.dot(attn, w_out, preferred_element_type=jnp.float32)  2.4 us
  transfers between devices with their start and end apart: 2, of which 2 were waited for; matrix products, arithmetic and copies ran while one was open for 0% of the time, Pallas kernels for 0%

commit v1 on v0

v1 whole, which is shorter than its diff:
```python
import functools
import math

import jax
import jax.numpy as jnp
from jax import lax
from jax.experimental import pallas as pl
from jax.experimental.pallas import tpu as pltpu
from jax.sharding import Mesh
from jax.sharding import PartitionSpec as P

FRB = 2
TPF = 16
PLANE = ("blk", "core")
VMEM = pl.BlockSpec(memory_space=pltpu.VMEM)
SMEM = pl.BlockSpec(memory_space=pltpu.SMEM)
PARAMS = pltpu.CompilerParams(vmem_limit_bytes=48 * 1024 * 1024)


def pack_kernel(x_ref, out_ref):
    peers, _, width = out_ref.shape
    kinds, tok, _ = x_ref.shape
    for g in range(peers):
        for k in range(kinds):
            out_ref[g, k * tok:(k + 1) * tok, :] = x_ref[k, :, g * width:(g + 1) * width]


def pack(x, peers):
    kinds, tok, cols = x.shape
    return pl.pallas_call(
        pack_kernel,
        out_shape=jax.ShapeDtypeStruct((peers, kinds * tok, cols // peers), x.dtype),
        in_specs=[VMEM],
        out_specs=VMEM,
        compiler_params=PARAMS,
    )(x)


def clip_of(token, tok_dev, clip_ref):
    frame = token // (2 * tok_dev) * FRB + token % tok_dev // TPF
    clip = jnp.zeros_like(token)
    for f in range(clip_ref.shape[0]):
        clip = jnp.where(frame == f, clip_ref[f], clip)
    return clip


def attention_kernel(tok, head_dim, clip_ref, *refs):
    own_ref, *kv_refs, out_ref = refs
    peers, _, width = own_ref.shape
    count = peers * tok
    scale = 1.0 / math.sqrt(head_dim)
    row_clip = clip_of(lax.broadcasted_iota(jnp.int32, (count, 1), 0), tok, clip_ref)
    col_clip = clip_of(lax.broadcasted_iota(jnp.int32, (1, count), 1), tok, clip_ref)
    allowed = row_clip == col_clip
    sources = [(own_ref, tok)] + [(ref, 0) for ref in kv_refs]
    per_step = max(1, 1024 // count)
    for h in range(width // head_dim):
        cols = slice(h * head_dim, (h + 1) * head_dim)
        queries = own_ref[:, 0:tok, cols].reshape(count, head_dim)
        top = total = acc = None
        for first in range(0, len(sources), per_step):
            scores, values = [], []
            for ref, at in sources[first:first + per_step]:
                keys = ref[:, at:at + tok, cols].reshape(count, head_dim)
                values.append(ref[:, at + tok:at + 2 * tok, cols].reshape(count, head_dim))
                s = lax.dot_general(
                    queries, keys, (((1,), (1,)), ((), ())), preferred_element_type=jnp.float32
                )
                scores.append(jnp.where(allowed, s * scale, -1e30))
            new_top = functools.reduce(
                jnp.maximum, [jnp.max(s, axis=1, keepdims=True) for s in scores]
            )
            if top is not None:
                new_top = jnp.maximum(top, new_top)
                factor = jnp.exp(top - new_top)
                total, acc = total * factor, acc * factor
            top = new_top
            for s, v in zip(scores, values):
                p = jnp.where(allowed, jnp.exp(s - top), 0.0)
                part = jnp.sum(p, axis=1, keepdims=True)
                dot = jnp.dot(p.astype(jnp.bfloat16), v, preferred_element_type=jnp.float32)
                total = part if total is None else total + part
                acc = dot if acc is None else acc + dot
        out_ref[:, cols] = (acc / total).astype(out_ref.dtype)


def attention(own, others, frame_clip, tok, head_dim):
    peers, _, width = own.shape
    return pl.pallas_call(
        functools.partial(attention_kernel, tok, head_dim),
        out_shape=jax.ShapeDtypeStruct((peers * tok, width), own.dtype),
        in_specs=[SMEM] + [VMEM] * (1 + len(others)),
        out_specs=VMEM,
        compiler_params=PARAMS,
    )(frame_clip, own, *others)


def project_kernel(order_ref, attn_ref, *refs):
    *w_refs, out_ref, a_ref, w_all = refs
    peers, _, width = attn_ref.shape
    for g in range(peers):
        a_ref[:, g * width:(g + 1) * width] = attn_ref[g]
    rows = w_refs[0].shape[0]
    for i, ref in enumerate(w_refs):
        w_all[pl.ds(pl.multiple_of(order_ref[i] * rows, rows), rows), :] = ref[...]
    result = jnp.dot(a_ref[...], w_all[...], preferred_element_type=jnp.float32)
    out_ref[...] = result.astype(out_ref.dtype).reshape(out_ref.shape)


def project(attn_all, w_parts, order, tok):
    peers, count, width = attn_all.shape
    depth, cols = peers * width, w_parts[0].shape[1]
    return pl.pallas_call(
        project_kernel,
        out_shape=jax.ShapeDtypeStruct((peers, tok, cols), attn_all.dtype),
        in_specs=[SMEM] + [VMEM] * (1 + len(w_parts)),
        out_specs=VMEM,
        scratch_shapes=[
            pltpu.VMEM((count, depth), attn_all.dtype),
            pltpu.VMEM((depth, cols), attn_all.dtype),
        ],
        compiler_params=PARAMS,
    )(order, attn_all, *w_parts)


def unpack_kernel(x_ref, out_ref):
    peers, _, width = x_ref.shape
    for g in range(peers):
        out_ref[:, g * width:(g + 1) * width] = x_ref[g]


def unpack(x):
    peers, tok, width = x.shape
    return pl.pallas_call(
        unpack_kernel,
        out_shape=jax.ShapeDtypeStruct((tok, peers * width), x.dtype),
        in_specs=[VMEM],
        out_specs=VMEM,
        compiler_params=PARAMS,
    )(x)


def shift(x, axis, by):
    size = lax.axis_size(axis)
    return lax.ppermute(x, axis, [(i, (i + by) % size) for i in range(size)])


def on_device(qkv, frame_clip, w_out):
    rows, peers = lax.axis_size("row"), lax.axis_size("blk") * 2
    blk, row, core = lax.axis_index("blk"), lax.axis_index("row"), lax.axis_index("core")
    tok = qkv.shape[1]
    head_dim, model = w_out.shape
    cols = model // peers

    mine = lax.dynamic_slice(w_out, (0, (blk * 2 + core) * cols), (head_dim, cols))
    theirs = lax.dynamic_slice(w_out, (0, (blk * 2 + 1 - core) * cols), (head_dim, cols))
    got = shift(theirs, "core", 1)
    first = jnp.where(core == 0, mine, got)
    second = jnp.where(core == 0, got, mine)
    w_own = jnp.concatenate([first, second], axis=0)
    w_parts = [w_own] + [shift(w_own, "row", by) for by in range(1, rows)]
    order = jnp.stack([(row - by) % rows for by in range(rows)]).astype(jnp.int32)

    own = lax.all_to_all(pack(qkv, peers), PLANE, split_axis=0, concat_axis=0, tiled=True)
    kv = own[:, tok:]
    others = [shift(kv, "row", by) for by in range(1, rows)]
    attn = attention(own, others, frame_clip, tok, head_dim)
    attn_all = lax.all_gather(attn, PLANE, axis=0, tiled=False)
    part = project(attn_all, w_parts, order, tok)
    return unpack(lax.all_to_all(part, PLANE, split_axis=0, concat_axis=0, tiled=True))


def solution(mesh):
    blk, tile = mesh.shape["blk"], mesh.shape["tile"]
    fine = Mesh(mesh.devices.reshape(blk, tile // 2, 2), ("blk", "row", "core"))
    in_specs = (P(None, ("blk", "row", "core"), None), P(), P(("row", "core"), None))
    out_specs = P(("blk", "row", "core"), None)
    return jax.shard_map(
        on_device, mesh=fine, in_specs=in_specs, out_specs=out_specs, check_vma=False
    )
```

time: 97 us -> 79.5 us (0.82)
  between operations: 13.5 us -> 0.04 us
  starting transfers between devices: 6.36 us -> 14 us
  local copies, waits for them, and re-layouts: 6.67 us -> 1.87 us
  waiting for transfers between devices: 43.7 us -> 39 us
  matrix products: 4.58 us -> 0 us
  Pallas kernels: 0 us -> 3.95 us
  other arithmetic: 3.64 us -> 1.08 us
  blocking collectives: 18 us -> 19.2 us
    reduce_scatter x1 -> x0, waiting for transfers between devices: 35.6 us -> none  [on_device(): lax.psum_scatter(jnp.dot(attn, w_out, preferred_element_type=jnp.float32)...]
    ppermute x0 -> x7, waiting for transfers between devices: none -> 33.8 us  [shift(): return lax.ppermute(x, axis, [(i, (i + by) % size) for i in range(size)])]
    all_to_all x0 -> x1, blocking collectives: none -> 10.2 us  [on_device(): lax.all_to_all(part, PLANE, split_axis=0, concat_axis=0, tiled=True)]
    ppermute x0 -> x7, starting transfers between devices: none -> 9.18 us  [shift(): return lax.ppermute(x, axis, [(i, (i + by) % size) for i in range(size)])]
    all_gather x2 -> x1, blocking collectives: 18 us -> 9.03 us  [on_device(): attn_all = lax.all_gather(attn, PLANE, axis=0, tiled=False)]
    dot_general x9 -> x0, matrix products: 4.58 us -> none  [the longest x1 2.4 us: on_device(): jnp.dot(attn, w_out, preferred_element_type=jnp.float32)]
    pallas_call x0 -> x4, Pallas kernels: none -> 3.95 us  [the longest x1 1.25 us: project(): pl.pallas_call(project_kernel, out_shape=jax.ShapeDtypeStruct((peers, tok...]
    all_to_all x1, waiting for transfers between devices: 8.13 us -> 5.25 us  [on_device(): lax.all_to_all(pack(qkv, peers), PLANE, split_axis=0, concat_axis=0, tile...]
  transfers between devices with their start and end apart: 2 -> 8, of which waited for: 2 -> 2; matrix products, arithmetic and copies ran while one was open for 0% -> 1% of each run, Pallas kernels for 0% -> 2%
where the time goes in v1:
time: 79.5 us; the launch traced here: 79.2 us
  waiting for transfers between devices  39 us (49%)
  blocking collectives  19.2 us (24%)
  starting transfers between devices  14 us (18%)
  Pallas kernels  3.95 us (5%)
  local copies, waits for them, and re-layouts  1.87 us (2%)
  other arithmetic  1.08 us (1%)
    ppermute x7, waiting for transfers between devices, shift(): return lax.ppermute(x, axis, [(i, (i + by) % size) for i in range(size)])  33.8 us
    all_to_all x1, blocking collectives, on_device(): lax.all_to_all(part, PLANE, split_axis=0, concat_axis=0, tiled=True)  10.2 us
    ppermute x7, starting transfers between devices, shift(): return lax.ppermute(x, axis, [(i, (i + by) % size) for i in range(size)])  9.18 us
    all_gather x1, blocking collectives, on_device(): attn_all = lax.all_gather(attn, PLANE, axis=0, tiled=False)  9.03 us
    all_to_all x1, waiting for transfers between devices, on_device(): lax.all_to_all(pack(qkv, peers), PLANE, split_axis=0, concat_axis=0, tile...  5.25 us
    all_to_all x1, starting transfers between devices, on_device(): lax.all_to_all(pack(qkv, peers), PLANE, split_axis=0, concat_axis=0, tile...  4.83 us
  transfers between devices with their start and end apart: 8, of which 2 were waited for; matrix products, arithmetic and copies ran while one was open for 1% of the time, Pallas kernels for 2%

profile of v1, /device:TPU:0, one launch (start us, length us, event | category | flops | bytes accessed | tf_op | source)
XLA Modules:
  0.0 79.2 jit_solution(3531481675685244079)
XLA Ops:
  0.0 0.9 %constant_dynamic-slice_fusion = bf16[128,640]{1,0:T(8,128)(2,1)S(1)} fusion(bf16[128,5120]{1,0:T(8,128)(2,1)} %param.5, s32[]{:T(128)S(6)} %select_n.43), kind=kLoop, calls=%fused_computation.4 | loop fusion | bytes 327684 | tf_op jit(solution)/shard_map/dynamic_slice | solution.py:156
  0.9 0.5 collective-permute-start.3
  1.5 0.0 copy-start
  1.5 0.9 %copy-done = bf16[3,32,1024]{2,1,0:T(8,128)(2,1)S(1)} copy-done((bf16[3,32,1024]{2,1,0:T(8,128)(2,1)S(1)}, bf16[3,32,1024]{2,1,0:T(8,128)(2,1)}, u32[]{:S(2)}) %copy-start) | copy-done | bytes 196632
  2.4 0.0 copy-start.1
  2.4 0.7 shard_map.37
  3.1 4.8 %all-to-all-start = ((bf16[8,96,128]{2,1,0:T(8,128)(2,1)}), bf16[8,96,128]{2,1,0:T(8,128)(2,1)S(1)}, u32[]{:S(2)}, u32[]{:S(2)}) async-start(bf16[8,96,128]{2,1,0:T(8,128)(2,1)} %shard_map.37), calls=%async_computation | async-start | bytes 393216 | tf_op jit(solution)/shard_map/all_to_all | solution.py:164
  7.9 0.0 collective-permute-done.3
  7.9 1.0 %broadcast_select_fusion.1 = (bf16[128,640]{1,0:T(8,128)(2,1)S(1)}, bf16[128,640]{1,0:T(8,128)(2,1)S(1)}) fusion(bf16[128,640]{1,0:T(8,128)(2,1)S(1)} %collective-permute-done.3, pred[]{:T(512)S(6)} %eq.9, bf16[128,5120]{1,0:T(8,128)(2,1)} %param.5, s32[]{:T(128)S(6)} %select_n.42), kind=kLoop, calls=%fused_computation.2 | loop fusion | flops 163840 | bytes 655365 | tf_op jit(solution)/shard_map/jit(_where)/select_n | solution.py:158
  8.9 5.2 %all-to-all-done.refs_0_ = bf16[8,96,128]{2,1,0:T(8,128)(2,1)S(1)} async-done(((bf16[8,96,128]{2,1,0:T(8,128)(2,1)}), bf16[8,96,128]{2,1,0:T(8,128)(2,1)S(1)}, u32[]{:S(2)}, u32[]{:S(2)}) %all-to-all-start) | async-done | bytes 196640 | tf_op jit(solution)/shard_map/all_to_all | solution.py:164
  14.2 3.7 %collective-permute-start.2 = (bf16[8,64,128]{2,1,0:T(8,128)(2,1)S(1)}, bf16[8,64,128]{2,1,0:T(8,128)(2,1)S(1)}, u32[]{:S(2)}, u32[]{:S(2)}) collective-permute-start(bf16[8,64,128]{2,1,0:T(8,128)(2,1)S(1)} %slice.4), channel_id=1, source_target_pairs={{0,6},{2,0},{4,2},{6,4},{1,7},{3,1},{5,3},{7,5},{8,14},{10,8},{12,... | collective-permute-start | bytes 393224 | tf_op jit(solution)/shard_map/ppermute | solution.py:145
  17.9 0.5 collective-permute-start.6
  18.4 0.0 collective-permute-start.5
  18.4 1.6 %collective-permute-start.4 = (bf16[256,640]{1,0:T(8,128)(2,1)S(1)}, bf16[256,640]{1,0:T(8,128)(2,1)S(1)}, u32[]{:S(2)}, u32[]{:S(2)}) collective-permute-start(bf16[256,640]{1,0:T(8,128)(2,1)S(1)} %pad_maximum_fusion.refs_0_), channel_id=1, source_target_pairs={{0,2},{2,4},{4,6},{6,0},{1,3},{3,5},{5,7},{7,1},{8,10},{10,12},{12... | collective-permute-start | bytes 983048 | tf_op jit(solution)/shard_map/ppermute | solution.py:145
  19.9 2.9 %collective-permute-start.1 = (bf16[8,64,128]{2,1,0:T(8,128)(2,1)S(1)}, bf16[8,64,128]{2,1,0:T(8,128)(2,1)S(1)}, u32[]{:S(2)}, u32[]{:S(2)}) collective-permute-start(bf16[8,64,128]{2,1,0:T(8,128)(2,1)S(1)} %slice.4), channel_id=1, source_target_pairs={{0,4},{2,6},{4,0},{6,2},{1,5},{3,7},{5,1},{7,3},{8,12},{10,14},{12... | collective-permute-start | bytes 393224 | tf_op jit(solution)/shard_map/ppermute | solution.py:145
  22.9 0.0 collective-permute-done.2.refs_3_
  22.9 0.0 collective-permute-start
  22.9 0.1 pad_add_fusion.order_ref
  22.9 33.7 %collective-permute-done.1.refs_2_ = bf16[8,64,128]{2,1,0:T(8,128)(2,1)S(1)} collective-permute-done((bf16[8,64,128]{2,1,0:T(8,128)(2,1)S(1)}, bf16[8,64,128]{2,1,0:T(8,128)(2,1)S(1)}, u32[]{:S(2)}, u32[]{:S(2)}) %collective-permute-start.1) | collective-permute-done | bytes 131104 | tf_op jit(solution)/shard_map/ppermute | solution.py:145
  56.7 0.0 collective-permute-done.refs_1_
  56.7 0.0 copy-done.1
  56.7 1.2 %shard_map.38 = bf16[256,128]{1,0:T(8,128)(2,1)S(1)} custom-call(s32[8]{0:T(128)S(1)} %copy-done.1, bf16[8,96,128]{2,1,0:T(8,128)(2,1)S(1)} %all-to-all-done.refs_0_, bf16[8,64,128]{2,1,0:T(8,128)(2,1)S(1)} %collective-permute-done.refs_1_, bf16[8,64,128]{2,1,0:T(8,128)(2,1)S(1)} %collective-permute-done.1.refs_2_, ...), custom_call_target="tpu_custom_call" | custom-call | tf_op jit(solution)/shard_map/pallas_call | solution.py:89
  57.9 9.0 %all-gather = bf16[2048,128]{1,0:T(8,128)(2,1)S(1)} all-gather(bf16[256,128]{1,0:T(8,128)(2,1)S(1)} %shard_map.38), channel_id=2, replica_groups=mesh['blk'=4,'row'=4,'core'=2] {'blk','core'}, dimensions={0}, use_global_device_ids=true | all-gather | bytes 589824 | tf_op jit(solution)/shard_map/all_gather | solution.py:168
  67.0 0.0 collective-permute-done.6.refs_3_
  67.0 0.0 collective-permute-done.5.refs_2_
  67.0 0.0 collective-permute-done.4.refs_1_
  67.0 1.2 %shard_map.39 = bf16[8,32,640]{2,1,0:T(8,128)(2,1)S(1)} custom-call(s32[4]{0:T(128)S(1)} %pad_add_fusion.order_ref, bf16[8,256,128]{2,1,0:T(8,128)(2,1)S(1)} %bitcast.5, bf16[256,640]{1,0:T(8,128)(2,1)S(1)} %pad_maximum_fusion.refs_0_, bf16[256,640]{1,0:T(8,128)(2,1)S(1)} %collective-permute-done.4.refs_1_, ...), custom_call_target="tpu_custom_call" | custom-call | tf_op jit(solution)/shard_map/pallas_call | solution.py:113
  68.2 10.2 %all_to_all.10.x_ref = bf16[8,32,640]{2,1,0:T(8,128)(2,1)S(1)} all-to-all(bf16[8,32,640]{2,1,0:T(8,128)(2,1)S(1)} %shard_map.39), channel_id=1, replica_groups=mesh['blk'=4,'row'=4,'core'=2] {'blk','core'}, dimensions={0} | all-to-all | bytes 655360 | tf_op jit(solution)/shard_map/all_to_all | solution.py:170
  78.4 0.8 shard_map.40
  (2 shorter events, 0.0 us)
Async XLA Ops:
  0.9 7.0 %collective-permute-start.3 = (bf16[128,640]{1,0:T(8,128)(2,1)S(1)}, bf16[128,640]{1,0:T(8,128)(2,1)S(1)}, u32[]{:S(2)}, u32[]{:S(2)}) collective-permute-start(bf16[128,640]{1,0:T(8,128)(2,1)S(1)} %constant_dynamic-slice_fusion), channel_id=1, source_target_pairs={{0,1},{1,0},{2,3},{3,2},{4,5},{5,4},{6,7},{7,6},{8,9},{9,8},{10,11... | collective-permute-start | bytes 491528 | tf_op jit(solution)/shard_map/ppermute | solution.py:145
  1.5 0.9 %copy-start = (bf16[3,32,1024]{2,1,0:T(8,128)(2,1)S(1)}, bf16[3,32,1024]{2,1,0:T(8,128)(2,1)}, u32[]{:S(2)}) copy-start(bf16[3,32,1024]{2,1,0:T(8,128)(2,1)} %x_ref.1) | copy-start | bytes 589828
  2.4 54.3 %copy-start.1 = (s32[8]{0:T(128)S(1)}, s32[8]{0:T(128)}, u32[]{:S(2)}) copy-start(s32[8]{0:T(128)} %clip_ref.1) | copy-start | bytes 100
  3.1 11.1 %all-to-all-start = ((bf16[8,96,128]{2,1,0:T(8,128)(2,1)}), bf16[8,96,128]{2,1,0:T(8,128)(2,1)S(1)}, u32[]{:S(2)}, u32[]{:S(2)}) async-start(bf16[8,96,128]{2,1,0:T(8,128)(2,1)} %shard_map.37), calls=%async_computation | async-start | bytes 393216 | tf_op jit(solution)/shard_map/all_to_all | solution.py:164
  14.2 8.7 %collective-permute-start.2 = (bf16[8,64,128]{2,1,0:T(8,128)(2,1)S(1)}, bf16[8,64,128]{2,1,0:T(8,128)(2,1)S(1)}, u32[]{:S(2)}, u32[]{:S(2)}) collective-permute-start(bf16[8,64,128]{2,1,0:T(8,128)(2,1)S(1)} %slice.4), channel_id=1, source_target_pairs={{0,6},{2,0},{4,2},{6,4},{1,7},{3,1},{5,3},{7,5},{8,14},{10,8},{12,... | collective-permute-start | bytes 393224 | tf_op jit(solution)/shard_map/ppermute | solution.py:145
  17.9 49.1 %collective-permute-start.6 = (bf16[256,640]{1,0:T(8,128)(2,1)S(1)}, bf16[256,640]{1,0:T(8,128)(2,1)S(1)}, u32[]{:S(2)}, u32[]{:S(2)}) collective-permute-start(bf16[256,640]{1,0:T(8,128)(2,1)S(1)} %pad_maximum_fusion.refs_0_), channel_id=1, source_target_pairs={{0,6},{2,0},{4,2},{6,4},{1,7},{3,1},{5,3},{7,5},{8,14},{10,8},{12,... | collective-permute-start | bytes 983048 | tf_op jit(solution)/shard_map/ppermute | solution.py:145
  18.4 48.6 %collective-permute-start.5 = (bf16[256,640]{1,0:T(8,128)(2,1)S(1)}, bf16[256,640]{1,0:T(8,128)(2,1)S(1)}, u32[]{:S(2)}, u32[]{:S(2)}) collective-permute-start(bf16[256,640]{1,0:T(8,128)(2,1)S(1)} %pad_maximum_fusion.refs_0_), channel_id=1, source_target_pairs={{0,4},{2,6},{4,0},{6,2},{1,5},{3,7},{5,1},{7,3},{8,12},{10,14},{12... | collective-permute-start | bytes 983048 | tf_op jit(solution)/shard_map/ppermute | solution.py:145
  18.4 48.6 %collective-permute-start.4 = (bf16[256,640]{1,0:T(8,128)(2,1)S(1)}, bf16[256,640]{1,0:T(8,128)(2,1)S(1)}, u32[]{:S(2)}, u32[]{:S(2)}) collective-permute-start(bf16[256,640]{1,0:T(8,128)(2,1)S(1)} %pad_maximum_fusion.refs_0_), channel_id=1, source_target_pairs={{0,2},{2,4},{4,6},{6,0},{1,3},{3,5},{5,7},{7,1},{8,10},{10,12},{12... | collective-permute-start | bytes 983048 | tf_op jit(solution)/shard_map/ppermute | solution.py:145
  19.9 36.7 %collective-permute-start.1 = (bf16[8,64,128]{2,1,0:T(8,128)(2,1)S(1)}, bf16[8,64,128]{2,1,0:T(8,128)(2,1)S(1)}, u32[]{:S(2)}, u32[]{:S(2)}) collective-permute-start(bf16[8,64,128]{2,1,0:T(8,128)(2,1)S(1)} %slice.4), channel_id=1, source_target_pairs={{0,4},{2,6},{4,0},{6,2},{1,5},{3,7},{5,1},{7,3},{8,12},{10,14},{12... | collective-permute-start | bytes 393224 | tf_op jit(solution)/shard_map/ppermute | solution.py:145
  22.9 33.8 %collective-permute-start = (bf16[8,64,128]{2,1,0:T(8,128)(2,1)S(1)}, bf16[8,64,128]{2,1,0:T(8,128)(2,1)S(1)}, u32[]{:S(2)}, u32[]{:S(2)}) collective-permute-start(bf16[8,64,128]{2,1,0:T(8,128)(2,1)S(1)} %slice.4), channel_id=1, source_target_pairs={{0,2},{2,4},{4,6},{6,0},{1,3},{3,5},{5,7},{7,1},{8,10},{10,12},{12... | collective-permute-start | bytes 393224 | tf_op jit(solution)/shard_map/ppermute | solution.py:145

commit v2 on v1

v2 whole, which is shorter than its diff:
```python
import functools
import math

import jax
import jax.numpy as jnp
from jax import lax
from jax.experimental import pallas as pl
from jax.experimental.pallas import tpu as pltpu
from jax.sharding import Mesh
from jax.sharding import PartitionSpec as P

FRB = 2
TPF = 16
ALL = ("blk", "row", "core")
PLANE = ("blk", "core")
VMEM = pl.BlockSpec(memory_space=pltpu.VMEM)
SMEM = pl.BlockSpec(memory_space=pltpu.SMEM)
ANY = pl.BlockSpec(memory_space=pl.ANY)
PARAMS = pltpu.CompilerParams(vmem_limit_bytes=48 * 1024 * 1024)


def pack_kernel(rows, head_dim, x_ref, q_ref, kv_ref):
    peers, tok, width = q_ref.shape
    heads = width // head_dim
    for g in range(peers):
        for i in range(heads):
            head = (g // 2 * heads + i) * 2 + g % 2
            cols = slice(head * head_dim, (head + 1) * head_dim)
            at = slice(i * head_dim, (i + 1) * head_dim)
            q_ref[g, :, at] = x_ref[0, :, cols]
            for r in range(rows):
                to = (g // 2 * rows + r) * 2 + g % 2
                kv_ref[to, 0:tok, at] = x_ref[1, :, cols]
                kv_ref[to, tok:2 * tok, at] = x_ref[2, :, cols]


def pack(x, peers, rows, head_dim):
    _, tok, cols = x.shape
    width = cols // peers
    return pl.pallas_call(
        functools.partial(pack_kernel, rows, head_dim),
        out_shape=(
            jax.ShapeDtypeStruct((peers, tok, width), x.dtype),
            jax.ShapeDtypeStruct((peers * rows, 2 * tok, width), x.dtype),
        ),
        in_specs=[VMEM],
        out_specs=(VMEM, VMEM),
        compiler_params=PARAMS,
    )(x)


def clip_of(token, blk_tokens, tok_dev, clip_ref):
    frame = token // blk_tokens * FRB + token % tok_dev // TPF
    clip = jnp.zeros_like(token)
    for f in range(clip_ref.shape[0]):
        clip = jnp.where(frame == f, clip_ref[f], clip)
    return clip


def attention_kernel(tok, head_dim, clip_ref, q_ref, kv_ref, *refs):
    out_ref = refs[len(refs) // 2]
    peers, _, width = q_ref.shape
    count = peers * tok
    devices = kv_ref.shape[0]
    scale = 1.0 / math.sqrt(head_dim)
    row_clip = clip_of(
        lax.broadcasted_iota(jnp.int32, (count, 1), 0), 2 * tok, tok, clip_ref
    )
    step = min(devices, 32)
    for h in range(width // head_dim):
        cols = slice(h * head_dim, (h + 1) * head_dim)
        queries = q_ref[:, :, cols].reshape(count, head_dim)
        top = total = acc = None
        for at in range(0, devices, step):
            keys = kv_ref[at:at + step, 0:tok, cols].reshape(step * tok, head_dim)
            values = kv_ref[at:at + step, tok:2 * tok, cols].reshape(step * tok, head_dim)
            token = at * tok + lax.broadcasted_iota(jnp.int32, (1, step * tok), 1)
            col_clip = clip_of(token, devices // (peers // 2) * tok, tok, clip_ref)
            allowed = row_clip == col_clip
            s = lax.dot_general(
                queries, keys, (((1,), (1,)), ((), ())), preferred_element_type=jnp.float32
            )
            s = jnp.where(allowed, s * scale, -1e30)
            new_top = jnp.max(s, axis=1, keepdims=True)
            if top is not None:
                new_top = jnp.maximum(top, new_top)
                factor = jnp.exp(top - new_top)
                total, acc = total * factor, acc * factor
            top = new_top
            p = jnp.where(allowed, jnp.exp(s - top), 0.0)
            part = jnp.sum(p, axis=1, keepdims=True)
            dot = jnp.dot(p.astype(jnp.bfloat16), values, preferred_element_type=jnp.float32)
            total = part if total is None else total + part
            acc = dot if acc is None else acc + dot
        out_ref[:, cols] = (acc / total).astype(out_ref.dtype)


def attention(q, kv, frame_clip, head_dim, passed):
    peers, tok, width = q.shape
    like = jax.ShapeDtypeStruct((peers * tok, width), q.dtype)
    return pl.pallas_call(
        functools.partial(attention_kernel, tok, head_dim),
        out_shape=[like] + [jax.ShapeDtypeStruct(x.shape, x.dtype) for x in passed],
        in_specs=[SMEM, VMEM, VMEM] + [ANY] * len(passed),
        out_specs=[VMEM] + [ANY] * len(passed),
        input_output_aliases={3 + i: 1 + i for i in range(len(passed))},
        compiler_params=PARAMS,
    )(frame_clip, q, kv, *passed)


def project_kernel(row_ref, attn_ref, own_ref, *refs):
    *w_refs, out_ref, a_ref, w_all = refs
    blks, _, width = attn_ref.shape
    head_dim = own_ref.shape[0]
    rows = w_all.shape[0] // head_dim
    row = row_ref[0]
    for b in range(blks):
        a_ref[:, b * width:(b + 1) * width] = attn_ref[b]

    def put(ref, at):
        w_all[pl.ds(pl.multiple_of(at * head_dim, head_dim), head_dim), :] = ref[...]

    put(own_ref, row)
    for i in range(rows - 1):
        pl.when(row >= i + 1)(functools.partial(put, w_refs[2 * i], row - i - 1))
        pl.when(row + i + 1 < rows)(functools.partial(put, w_refs[2 * i + 1], row + i + 1))
    result = jnp.dot(a_ref[...], w_all[...], preferred_element_type=jnp.float32)
    out_ref[...] = result.astype(out_ref.dtype).reshape(out_ref.shape)


def project(attn_all, w_parts, row, tok):
    blks, count, width = attn_all.shape
    depth, cols = blks * width, w_parts[0].shape[1]
    return pl.pallas_call(
        project_kernel,
        out_shape=jax.ShapeDtypeStruct((count // tok, tok, cols), attn_all.dtype),
        in_specs=[SMEM] + [VMEM] * (1 + len(w_parts)),
        out_specs=VMEM,
        scratch_shapes=[
            pltpu.VMEM((count, depth), attn_all.dtype),
            pltpu.VMEM((depth, cols), attn_all.dtype),
        ],
        compiler_params=PARAMS,
    )(row, attn_all, *w_parts)


def unpack_kernel(x_ref, out_ref):
    peers, _, width = x_ref.shape
    for b in range(peers // 2):
        both = x_ref[2 * b].astype(jnp.float32) + x_ref[2 * b + 1].astype(jnp.float32)
        out_ref[:, b * width:(b + 1) * width] = both.astype(out_ref.dtype)


def unpack(x):
    peers, tok, width = x.shape
    return pl.pallas_call(
        unpack_kernel,
        out_shape=jax.ShapeDtypeStruct((tok, peers // 2 * width), x.dtype),
        in_specs=[VMEM],
        out_specs=VMEM,
        compiler_params=PARAMS,
    )(x)


def shift(x, axis, by):
    size = lax.axis_size(axis)
    return lax.ppermute(x, axis, [(i, i + by) for i in range(size) if 0 <= i + by < size])


def on_device(qkv, frame_clip, w_out):
    rows, blks = lax.axis_size("row"), lax.axis_size("blk")
    peers = 2 * blks
    head_dim, model = w_out.shape
    cols = model // blks

    own = lax.dynamic_slice(w_out, (0, lax.axis_index("blk") * cols), (head_dim, cols))
    below, above = shift(own, "row", 1), shift(own, "row", -1)

    q_out, kv_out = pack(qkv, peers, rows, head_dim)
    kv = lax.all_to_all(kv_out, ALL, split_axis=0, concat_axis=0, tiled=True)
    q = lax.all_to_all(q_out, PLANE, split_axis=0, concat_axis=0, tiled=True)
    attn, below, above = attention(q, kv, frame_clip, head_dim, (below, above))

    w_parts = [own, below, above]
    for by in range(1, rows - 1):
        w_parts += [shift(below, "row", by), shift(above, "row", -by)]
    attn_all = lax.all_gather(attn, "blk", axis=0, tiled=False)
    row = lax.axis_index("row").astype(jnp.int32).reshape(1)
    part = project(attn_all, w_parts, row, qkv.shape[1])
    return unpack(lax.all_to_all(part, PLANE, split_axis=0, concat_axis=0, tiled=True))


def solution(mesh):
    blk, tile = mesh.shape["blk"], mesh.shape["tile"]
    fine = Mesh(mesh.devices.reshape(blk, tile // 2, 2), ALL)
    in_specs = (P(None, ALL, None), P(), P(("row", "core"), None))
    return jax.shard_map(
        on_device, mesh=fine, in_specs=in_specs, out_specs=P(ALL, None), check_vma=False
    )
```

time: 79.5 us -> 84.5 us (1.063)
  the two profiles are of different devices: /device:TPU:0 before, /device:TPU:8 now
where the time goes in v2:
time: 84.5 us; the launch traced here: 84.1 us
  blocking collectives  32.3 us (38%)
  waiting for transfers between devices  27.4 us (32%)
  starting transfers between devices  18.5 us (22%)
  Pallas kernels  4.74 us (6%)
  local copies, waits for them, and re-layouts  1.07 us (1%)
    ppermute x6, waiting for transfers between devices, shift(): lax.ppermute(x, axis, [(i, i + by) for i in range(size) if 0 <= i + by <...  27.4 us
    all_to_all x1, blocking collectives, on_device(): lax.all_to_all(part, PLANE, split_axis=0, concat_axis=0, tiled=True)  14.8 us
    ppermute x6, starting transfers between devices, shift(): lax.ppermute(x, axis, [(i, i + by) for i in range(size) if 0 <= i + by <...  14.3 us
    all_gather x1, blocking collectives, on_device(): attn_all = lax.all_gather(attn, 'blk', axis=0, tiled=False)  8.96 us
    all_to_all x1, blocking collectives, on_device(): q = lax.all_to_all(q_out, PLANE, split_axis=0, concat_axis=0, tiled=True)  8.53 us
    all_to_all x1, starting transfers between devices, on_device(): kv = lax.all_to_all(kv_out, ALL, split_axis=0, concat_axis=0, tiled=True)  4.16 us
    pallas_call x1, Pallas kernels, project(): pl.pallas_call(project_kernel, out_shape=jax.ShapeDtypeStruct((count // t...  1.73 us
  transfers between devices with their start and end apart: 7, of which 3 were waited for; matrix products, arithmetic and copies ran while one was open for 0% of the time, Pallas kernels for 0%

profile of v2, /device:TPU:8, one launch (start us, length us, event | category | flops | bytes accessed | tf_op | source)
XLA Modules:
  0.0 84.1 jit_solution(14241855650010955605)
XLA Ops:
  0.0 0.0 copy-start
  0.0 0.0 copy-start.1
  0.0 1.0 %copy-done.1 = bf16[3,32,1024]{2,1,0:T(8,128)(2,1)S(1)} copy-done((bf16[3,32,1024]{2,1,0:T(8,128)(2,1)S(1)}, bf16[3,32,1024]{2,1,0:T(8,128)(2,1)}, u32[]{:S(2)}) %copy-start.1) | copy-done | bytes 196632
  1.0 0.0 copy-start.2
  1.0 0.9 %shard_map.37 = (bf16[8,32,128]{2,1,0:T(8,128)(2,1)S(1)}, bf16[32,64,128]{2,1,0:T(8,128)(2,1)}) custom-call(bf16[3,32,1024]{2,1,0:T(8,128)(2,1)S(1)} %copy-done.1), custom_call_target="tpu_custom_call" | custom-call | tf_op jit(solution)/shard_map/pallas_call | solution.py:40
  1.9 8.5 %all_to_all.15.q_ref = bf16[8,32,128]{2,1,0:T(8,128)(2,1)S(1)} all-to-all(bf16[8,32,128]{2,1,0:T(8,128)(2,1)S(1)} %get-tuple-element.10), channel_id=1, replica_groups=mesh['blk'=4,'row'=4,'core'=2] {'blk','core'}, dimensions={0} | all-to-all | bytes 131072 | tf_op jit(solution)/shard_map/all_to_all | solution.py:181
  10.4 4.2 %all-to-all-start.1 = ((bf16[32,64,128]{2,1,0:T(8,128)(2,1)}), bf16[32,64,128]{2,1,0:T(8,128)(2,1)S(1)}, u32[]{:S(2)}, u32[]{:S(2)}) async-start(bf16[32,64,128]{2,1,0:T(8,128)(2,1)} %get-tuple-element.11), calls=%async_computation.1 | async-start | bytes 1048576 | tf_op jit(solution)/shard_map/all_to_all | solution.py:180
  14.6 0.0 copy-done
  14.7 2.2 %collective-permute-start.1 = (bf16[128,1280]{1,0:T(8,128)(2,1)S(1)}, bf16[128,1280]{1,0:T(8,128)(2,1)S(1)}, u32[]{:S(2)}, u32[]{:S(2)}) collective-permute-start(bf16[128,1280]{1,0:T(8,128)(2,1)S(1)} %constant_dynamic-slice_fusion.own_ref), channel_id=1, source_target_pairs={{2,0},{4,2},{6,4},{3,1},{5,3},{7,5},{10,8},{12,10},{14,12},{11,9},... | collective-permute-start | bytes 983048 | tf_op jit(solution)/shard_map/ppermute | solution.py:167
  16.8 3.7 %collective-permute-start = (bf16[128,1280]{1,0:T(8,128)(2,1)S(1)}, bf16[128,1280]{1,0:T(8,128)(2,1)S(1)}, u32[]{:S(2)}, u32[]{:S(2)}) collective-permute-start(bf16[128,1280]{1,0:T(8,128)(2,1)S(1)} %constant_dynamic-slice_fusion.own_ref), channel_id=1, source_target_pairs={{0,2},{2,4},{4,6},{1,3},{3,5},{5,7},{8,10},{10,12},{12,14},{9,11},... | collective-permute-start | bytes 983048 | tf_op jit(solution)/shard_map/ppermute | solution.py:167
  20.5 14.9 %collective-permute-done.1.refs_1_ = bf16[128,1280]{1,0:T(8,128)(2,1)S(1)} collective-permute-done((bf16[128,1280]{1,0:T(8,128)(2,1)S(1)}, bf16[128,1280]{1,0:T(8,128)(2,1)S(1)}, u32[]{:S(2)}, u32[]{:S(2)}) %collective-permute-start.1) | collective-permute-done | bytes 327712 | tf_op jit(solution)/shard_map/ppermute | solution.py:167
  35.4 0.0 collective-permute-done.refs_0_
  35.4 0.0 all-to-all-done.1.kv_ref
  35.4 0.0 copy-done.2
  35.4 1.3 %shard_map.38 = (bf16[256,128]{1,0:T(8,128)(2,1)S(1)}, bf16[128,1280]{1,0:T(8,128)(2,1)S(1)}, bf16[128,1280]{1,0:T(8,128)(2,1)S(1)}) custom-call(s32[8]{0:T(128)S(1)} %copy-done.2, bf16[8,32,128]{2,1,0:T(8,128)(2,1)S(1)} %all_to_all.15.q_ref, bf16[32,64,128]{2,1,0:T(8,128)(2,1)S(1)} %all-to-all-done.1.kv_ref, ...), custom_call_target="tpu_custom_call", output_to_operand_aliasing={{1}: (3, {}), {2}: (4, {})} | custom-call | tf_op jit(solution)/shard_map/pallas_call | solution.py:101
  36.8 1.3 %collective-permute-start.4 = (bf16[128,1280]{1,0:T(8,128)(2,1)S(1)}, bf16[128,1280]{1,0:T(8,128)(2,1)S(1)}, u32[]{:S(2)}, u32[]{:S(2)}) collective-permute-start(bf16[128,1280]{1,0:T(8,128)(2,1)S(1)} %get-tuple-element.13.refs_0_), channel_id=1, source_target_pairs={{0,4},{2,6},{1,5},{3,7},{8,12},{10,14},{9,13},{11,15},{16,20},{18,... | collective-permute-start | bytes 983048 | tf_op jit(solution)/shard_map/ppermute | solution.py:167
  38.1 2.2 %collective-permute-start.2 = (bf16[128,1280]{1,0:T(8,128)(2,1)S(1)}, bf16[128,1280]{1,0:T(8,128)(2,1)S(1)}, u32[]{:S(2)}, u32[]{:S(2)}) collective-permute-start(bf16[128,1280]{1,0:T(8,128)(2,1)S(1)} %get-tuple-element.13.refs_0_), channel_id=1, source_target_pairs={{0,2},{2,4},{4,6},{1,3},{3,5},{5,7},{8,10},{10,12},{12,14},{9,11},... | collective-permute-start | bytes 983048 | tf_op jit(solution)/shard_map/ppermute | solution.py:167
  40.3 1.3 %collective-permute-start.5 = (bf16[128,1280]{1,0:T(8,128)(2,1)S(1)}, bf16[128,1280]{1,0:T(8,128)(2,1)}, u32[]{:S(2)}, u32[]{:S(2)}) collective-permute-start(bf16[128,1280]{1,0:T(8,128)(2,1)S(1)} %get-tuple-element.14.refs_1_), channel_id=1, source_target_pairs={{4,0},{6,2},{5,1},{7,3},{12,8},{14,10},{13,9},{15,11},{20,16},{22,... | collective-permute-start | bytes 983048 | tf_op jit(solution)/shard_map/ppermute | solution.py:167
  41.6 3.6 %collective-permute-start.3 = (bf16[128,1280]{1,0:T(8,128)(2,1)S(1)}, bf16[128,1280]{1,0:T(8,128)(2,1)}, u32[]{:S(2)}, u32[]{:S(2)}) collective-permute-start(bf16[128,1280]{1,0:T(8,128)(2,1)S(1)} %get-tuple-element.14.refs_1_), channel_id=1, source_target_pairs={{2,0},{4,2},{6,4},{3,1},{5,3},{7,5},{10,8},{12,10},{14,12},{11,9},... | collective-permute-start | bytes 983048 | tf_op jit(solution)/shard_map/ppermute | solution.py:167
  45.3 9.0 %all-gather = bf16[1024,128]{1,0:T(8,128)(2,1)S(1)} all-gather(bf16[256,128]{1,0:T(8,128)(2,1)S(1)} %get-tuple-element.12), channel_id=2, replica_groups=mesh['blk'=4,'row'=4,'core'=2] {'blk'}, dimensions={0}, use_global_device_ids=true | all-gather | bytes 327680 | tf_op jit(solution)/shard_map/all_gather | solution.py:187
  54.2 0.0 collective-permute-done.4.refs_4_
  54.2 4.9 %collective-permute-done.2.refs_2_ = bf16[128,1280]{1,0:T(8,128)(2,1)S(1)} collective-permute-done((bf16[128,1280]{1,0:T(8,128)(2,1)S(1)}, bf16[128,1280]{1,0:T(8,128)(2,1)S(1)}, u32[]{:S(2)}, u32[]{:S(2)}) %collective-permute-start.2) | collective-permute-done | bytes 327712 | tf_op jit(solution)/shard_map/ppermute | solution.py:167
  59.2 0.0 collective-permute-done.5.refs_5_
  59.2 7.6 %collective-permute-done.3.refs_3_ = bf16[128,1280]{1,0:T(8,128)(2,1)} collective-permute-done((bf16[128,1280]{1,0:T(8,128)(2,1)S(1)}, bf16[128,1280]{1,0:T(8,128)(2,1)}, u32[]{:S(2)}, u32[]{:S(2)}) %collective-permute-start.3) | collective-permute-done | bytes 327712 | tf_op jit(solution)/shard_map/ppermute | solution.py:167
  66.7 1.7 %shard_map.39 = bf16[8,32,1280]{2,1,0:T(8,128)(2,1)S(1)} custom-call(s32[1]{0:T(128)} %bitcast.row_ref, bf16[4,256,128]{2,1,0:T(8,128)(2,1)S(1)} %bitcast.2, bf16[128,1280]{1,0:T(8,128)(2,1)S(1)} %constant_dynamic-slice_fusion.own_ref, bf16[128,1280]{1,0:T(8,128)(2,1)S(1)} %get-tuple-element.13.refs_0_, bf16[128,1280]{1,0:T(8,128)(2,1)S(1)} %get-tuple-element.14.refs_1_, ...), custom_call_target="tpu_custom_call" | custom-call | tf_op jit(solution)/shard_map/pallas_call | solution.py:134
  68.5 14.8 %all_to_all.16.x_ref = bf16[8,32,1280]{2,1,0:T(8,128)(2,1)S(1)} all-to-all(bf16[8,32,1280]{2,1,0:T(8,128)(2,1)S(1)} %shard_map.39), channel_id=1, replica_groups=mesh['blk'=4,'row'=4,'core'=2] {'blk','core'}, dimensions={0} | all-to-all | bytes 1310720 | tf_op jit(solution)/shard_map/all_to_all | solution.py:190
  83.3 0.8 shard_map.40
  (1 shorter events, 0.0 us)
Async XLA Ops:
  0.0 14.6 %copy-start = (bf16[128,5120]{1,0:T(8,128)(2,1)S(1)}, bf16[128,5120]{1,0:T(8,128)(2,1)}, u32[]{:S(2)}) copy-start(bf16[128,5120]{1,0:T(8,128)(2,1)} %param.5) | copy-start | bytes 3932164
  0.0 1.0 %copy-start.1 = (bf16[3,32,1024]{2,1,0:T(8,128)(2,1)S(1)}, bf16[3,32,1024]{2,1,0:T(8,128)(2,1)}, u32[]{:S(2)}) copy-start(bf16[3,32,1024]{2,1,0:T(8,128)(2,1)} %x_ref.1) | copy-start | bytes 589828
  1.0 34.4 %copy-start.2 = (s32[8]{0:T(128)S(1)}, s32[8]{0:T(128)}, u32[]{:S(2)}) copy-start(s32[8]{0:T(128)} %clip_ref.1) | copy-start | bytes 100
  10.4 25.0 %all-to-all-start.1 = ((bf16[32,64,128]{2,1,0:T(8,128)(2,1)}), bf16[32,64,128]{2,1,0:T(8,128)(2,1)S(1)}, u32[]{:S(2)}, u32[]{:S(2)}) async-start(bf16[32,64,128]{2,1,0:T(8,128)(2,1)} %get-tuple-element.11), calls=%async_computation.1 | async-start | bytes 1048576 | tf_op jit(solution)/shard_map/all_to_all | solution.py:180
  14.7 20.8 %collective-permute-start.1 = (bf16[128,1280]{1,0:T(8,128)(2,1)S(1)}, bf16[128,1280]{1,0:T(8,128)(2,1)S(1)}, u32[]{:S(2)}, u32[]{:S(2)}) collective-permute-start(bf16[128,1280]{1,0:T(8,128)(2,1)S(1)} %constant_dynamic-slice_fusion.own_ref), channel_id=1, source_target_pairs={{2,0},{4,2},{6,4},{3,1},{5,3},{7,5},{10,8},{12,10},{14,12},{11,9},... | collective-permute-start | bytes 983048 | tf_op jit(solution)/shard_map/ppermute | solution.py:167
  16.8 18.6 %collective-permute-start = (bf16[128,1280]{1,0:T(8,128)(2,1)S(1)}, bf16[128,1280]{1,0:T(8,128)(2,1)S(1)}, u32[]{:S(2)}, u32[]{:S(2)}) collective-permute-start(bf16[128,1280]{1,0:T(8,128)(2,1)S(1)} %constant_dynamic-slice_fusion.own_ref), channel_id=1, source_target_pairs={{0,2},{2,4},{4,6},{1,3},{3,5},{5,7},{8,10},{10,12},{12,14},{9,11},... | collective-permute-start | bytes 983048 | tf_op jit(solution)/shard_map/ppermute | solution.py:167
  36.8 17.5 %collective-permute-start.4 = (bf16[128,1280]{1,0:T(8,128)(2,1)S(1)}, bf16[128,1280]{1,0:T(8,128)(2,1)S(1)}, u32[]{:S(2)}, u32[]{:S(2)}) collective-permute-start(bf16[128,1280]{1,0:T(8,128)(2,1)S(1)} %get-tuple-element.13.refs_0_), channel_id=1, source_target_pairs={{0,4},{2,6},{1,5},{3,7},{8,12},{10,14},{9,13},{11,15},{16,20},{18,... | collective-permute-start | bytes 983048 | tf_op jit(solution)/shard_map/ppermute | solution.py:167
  38.1 21.1 %collective-permute-start.2 = (bf16[128,1280]{1,0:T(8,128)(2,1)S(1)}, bf16[128,1280]{1,0:T(8,128)(2,1)S(1)}, u32[]{:S(2)}, u32[]{:S(2)}) collective-permute-start(bf16[128,1280]{1,0:T(8,128)(2,1)S(1)} %get-tuple-element.13.refs_0_), channel_id=1, source_target_pairs={{0,2},{2,4},{4,6},{1,3},{3,5},{5,7},{8,10},{10,12},{12,14},{9,11},... | collective-permute-start | bytes 983048 | tf_op jit(solution)/shard_map/ppermute | solution.py:167
  40.3 18.8 %collective-permute-start.5 = (bf16[128,1280]{1,0:T(8,128)(2,1)S(1)}, bf16[128,1280]{1,0:T(8,128)(2,1)}, u32[]{:S(2)}, u32[]{:S(2)}) collective-permute-start(bf16[128,1280]{1,0:T(8,128)(2,1)S(1)} %get-tuple-element.14.refs_1_), channel_id=1, source_target_pairs={{4,0},{6,2},{5,1},{7,3},{12,8},{14,10},{13,9},{15,11},{20,16},{22,... | collective-permute-start | bytes 983048 | tf_op jit(solution)/shard_map/ppermute | solution.py:167
  41.6 25.1 %collective-permute-start.3 = (bf16[128,1280]{1,0:T(8,128)(2,1)S(1)}, bf16[128,1280]{1,0:T(8,128)(2,1)}, u32[]{:S(2)}, u32[]{:S(2)}) collective-permute-start(bf16[128,1280]{1,0:T(8,128)(2,1)S(1)} %get-tuple-element.14.refs_1_), channel_id=1, source_target_pairs={{2,0},{4,2},{6,4},{3,1},{5,3},{7,5},{10,8},{12,10},{14,12},{11,9},... | collective-permute-start | bytes 983048 | tf_op jit(solution)/shard_map/ppermute | solution.py:167

commit v3 on v1

v3 whole, which is shorter than its diff:
```python
import functools
import math

import jax
import jax.numpy as jnp
from jax import lax
from jax.experimental import pallas as pl
from jax.experimental.pallas import tpu as pltpu
from jax.sharding import PartitionSpec as P

FRB = 2
TPF = 16
VMEM = pl.BlockSpec(memory_space=pltpu.VMEM)
SMEM = pl.BlockSpec(memory_space=pltpu.SMEM)
PARAMS = pltpu.CompilerParams(vmem_limit_bytes=48 * 1024 * 1024)


def pack_kernel(x_ref, out_ref):
    tiles, _, width = out_ref.shape
    kinds, tok, _ = x_ref.shape
    for g in range(tiles):
        for k in range(kinds):
            out_ref[g, k * tok:(k + 1) * tok, :] = x_ref[k, :, g * width:(g + 1) * width]


def pack(x, tiles):
    kinds, tok, cols = x.shape
    return pl.pallas_call(
        pack_kernel,
        out_shape=jax.ShapeDtypeStruct((tiles, kinds * tok, cols // tiles), x.dtype),
        in_specs=[VMEM],
        out_specs=VMEM,
        compiler_params=PARAMS,
    )(x)


def pack_rows_kernel(blk_ref, x_ref, out_ref):
    tiles, _, width = out_ref.shape
    for g in range(tiles):
        out_ref[g] = x_ref[:, g * width:(g + 1) * width]


def pack_rows(x, blk, blks, tiles):
    depth, cols = x.shape
    shape = (tiles, depth // blks, cols // tiles)
    return pl.pallas_call(
        pack_rows_kernel,
        out_shape=jax.ShapeDtypeStruct(shape, x.dtype),
        grid_spec=pltpu.PrefetchScalarGridSpec(
            num_scalar_prefetch=1,
            grid=(1,),
            in_specs=[pl.BlockSpec((depth // blks, cols), lambda i, at: (at[0], 0))],
            out_specs=pl.BlockSpec(shape, lambda i, at: (0, 0, 0)),
        ),
        compiler_params=PARAMS,
    )(blk, x)


def attention_kernel(tok, blk_ref, clip_ref, own_ref, *refs):
    *kv_refs, out_ref = refs
    tiles, _, head_dim = own_ref.shape
    count = tiles * tok
    scale = 1.0 / math.sqrt(head_dim)
    blk = blk_ref[0]

    def clips(at, shape, axis):
        first, second = clip_ref[at * FRB], clip_ref[at * FRB + 1]
        token = lax.broadcasted_iota(jnp.int32, shape, axis)
        return jnp.where(token % tok // TPF == 0, first, second)

    row_clip = clips(blk, (count, 1), 0)
    queries = own_ref[:, 0:tok, :].reshape(count, head_dim)
    sources = [(own_ref, tok)] + [(ref, 0) for ref in kv_refs]
    per_step = max(1, 1024 // count)
    top = total = acc = None
    for start in range(0, len(sources), per_step):
        scores, masks, values = [], [], []
        for k in range(start, min(start + per_step, len(sources))):
            ref, at = sources[k]
            keys = ref[:, at:at + tok, :].reshape(count, head_dim)
            values.append(ref[:, at + tok:at + 2 * tok, :].reshape(count, head_dim))
            s = lax.dot_general(
                queries, keys, (((1,), (1,)), ((), ())), preferred_element_type=jnp.float32
            )
            masks.append(row_clip == clips(blk ^ k, (1, count), 1))
            scores.append(jnp.where(masks[-1], s * scale, -1e30))
        new_top = functools.reduce(
            jnp.maximum, [jnp.max(s, axis=1, keepdims=True) for s in scores]
        )
        if top is not None:
            new_top = jnp.maximum(top, new_top)
            factor = jnp.exp(top - new_top)
            total, acc = total * factor, acc * factor
        top = new_top
        for s, allowed, v in zip(scores, masks, values):
            p = jnp.where(allowed, jnp.exp(s - top), 0.0)
            part = jnp.sum(p, axis=1, keepdims=True)
            dot = jnp.dot(p.astype(jnp.bfloat16), v, preferred_element_type=jnp.float32)
            total = part if total is None else total + part
            acc = dot if acc is None else acc + dot
    out_ref[...] = (acc / total).astype(out_ref.dtype)


def attention(own, others, blk, frame_clip):
    tiles, depth, head_dim = own.shape
    tok = depth // 3
    return pl.pallas_call(
        functools.partial(attention_kernel, tok),
        out_shape=jax.ShapeDtypeStruct((tiles * tok, head_dim), own.dtype),
        in_specs=[SMEM, SMEM] + [VMEM] * (1 + len(others)),
        out_specs=VMEM,
        compiler_params=PARAMS,
    )(blk, frame_clip, own, *others)


def project_kernel(blk_ref, attn_ref, *refs):
    *w_refs, out_ref, a_ref, w_all = refs
    tiles, _, head_dim = attn_ref.shape
    rows = w_refs[0].shape[1]
    for g in range(tiles):
        a_ref[:, g * head_dim:(g + 1) * head_dim] = attn_ref[g]
        for k, ref in enumerate(w_refs):
            at = pl.multiple_of(g * head_dim + (blk_ref[0] ^ k) * rows, rows)
            w_all[pl.ds(at, rows), :] = ref[g]
    result = jnp.dot(a_ref[...], w_all[...], preferred_element_type=jnp.float32)
    out_ref[...] = result.astype(out_ref.dtype).reshape(out_ref.shape)


def project(attn_all, w_parts, blk):
    tiles, count, head_dim = attn_all.shape
    depth, cols = tiles * head_dim, w_parts[0].shape[2]
    return pl.pallas_call(
        project_kernel,
        out_shape=jax.ShapeDtypeStruct((tiles, count // tiles, cols), attn_all.dtype),
        in_specs=[SMEM] + [VMEM] * (1 + len(w_parts)),
        out_specs=VMEM,
        scratch_shapes=[
            pltpu.VMEM((count, depth), attn_all.dtype),
            pltpu.VMEM((depth, cols), attn_all.dtype),
        ],
        compiler_params=PARAMS,
    )(blk, attn_all, *w_parts)


def unpack_kernel(x_ref, out_ref):
    tiles, _, width = x_ref.shape
    for g in range(tiles):
        out_ref[:, g * width:(g + 1) * width] = x_ref[g]


def unpack(x):
    tiles, tok, width = x.shape
    return pl.pallas_call(
        unpack_kernel,
        out_shape=jax.ShapeDtypeStruct((tok, tiles * width), x.dtype),
        in_specs=[VMEM],
        out_specs=VMEM,
        compiler_params=PARAMS,
    )(x)


def exchange(x, axis):
    return lax.all_to_all(x, axis, split_axis=0, concat_axis=0, tiled=True)


def from_others(x):
    blks = lax.axis_size("blk")
    return [
        lax.ppermute(x, "blk", [(i, i ^ k) for i in range(blks)]) for k in range(1, blks)
    ]


def on_device(qkv, frame_clip, w_out):
    tiles, blks = lax.axis_size("tile"), lax.axis_size("blk")
    blk = lax.axis_index("blk").astype(jnp.int32).reshape(1)
    tok = qkv.shape[1]

    own = exchange(pack(qkv, tiles), "tile")
    others = from_others(own[:, tok:])

    w_own = exchange(pack_rows(w_out, blk, blks, tiles), "tile")
    w_parts = [w_own] + from_others(w_own)

    attn = attention(own, others, blk, frame_clip)
    attn_all = lax.all_gather(attn, "tile", axis=0, tiled=False)
    return unpack(exchange(project(attn_all, w_parts, blk), "tile"))


def solution(mesh):
    in_specs = (P(None, ("blk", "tile"), None), P(), P("tile", None))
    out_specs = P(("blk", "tile"), None)
    return jax.shard_map(
        on_device, mesh=mesh, in_specs=in_specs, out_specs=out_specs, check_vma=False
    )
```

time: 79.5 us -> 65.8 us (0.83)
  waiting for transfers between devices: 39 us -> 13.8 us
  blocking collectives: 19.2 us -> 28.4 us
  starting transfers between devices: 14 us -> 16.8 us
  other arithmetic: 1.08 us -> 0 us
    ppermute x7 -> x6, waiting for transfers between devices: 33.8 us -> 0.02 us  [from_others(): lax.ppermute(x, 'blk', [(i, i ^ k) for i in range(blks)])]
    all_to_all x1 -> x2, waiting for transfers between devices: 5.25 us -> 13.7 us  [exchange(): return lax.all_to_all(x, axis, split_axis=0, concat_axis=0, tiled=True)]
    all_gather x1, blocking collectives: 9.03 us -> 14.8 us  [on_device(): attn_all = lax.all_gather(attn, 'tile', axis=0, tiled=False)]
    all_to_all x1 -> x2, starting transfers between devices: 4.83 us -> 9.76 us  [exchange(): return lax.all_to_all(x, axis, split_axis=0, concat_axis=0, tiled=True)]
    all_to_all x1, blocking collectives: 10.2 us -> 13.6 us  [exchange(): return lax.all_to_all(x, axis, split_axis=0, concat_axis=0, tiled=True)]
    ppermute x7 -> x6, starting transfers between devices: 9.18 us -> 7.04 us  [from_others(): lax.ppermute(x, 'blk', [(i, i ^ k) for i in range(blks)])]
    unnamed x4 -> x6, local copies, waits for them, and re-layouts: 0.93 us -> 2.24 us
    select_n x1 -> x0, other arithmetic: 0.98 us -> none  [on_device(): first = jnp.where(core == 0, mine, got)]
  transfers between devices with their start and end apart: 8 -> 8, of which waited for: 2 -> 2; matrix products, arithmetic and copies ran while one was open for 1% -> 0% of each run, Pallas kernels for 2% -> 3%
where the time goes in v3:
time: 65.8 us; the launch traced here: 65.4 us
  blocking collectives  28.4 us (43%)
  starting transfers between devices  16.8 us (26%)
  waiting for transfers between devices  13.8 us (21%)
  Pallas kernels  4.12 us (6%)
  local copies, waits for them, and re-layouts  2.26 us (3%)
    all_gather x1, blocking collectives, on_device(): attn_all = lax.all_gather(attn, 'tile', axis=0, tiled=False)  14.8 us
    all_to_all x2, waiting for transfers between devices, exchange(): return lax.all_to_all(x, axis, split_axis=0, concat_axis=0, tiled=True)  13.7 us
    all_to_all x1, blocking collectives, exchange(): return lax.all_to_all(x, axis, split_axis=0, concat_axis=0, tiled=True)  13.6 us
    all_to_all x2, starting transfers between devices, exchange(): return lax.all_to_all(x, axis, split_axis=0, concat_axis=0, tiled=True)  9.76 us
    ppermute x6, starting transfers between devices, from_others(): lax.ppermute(x, 'blk', [(i, i ^ k) for i in range(blks)])  7.04 us
    unnamed x6, local copies, waits for them, and re-layouts  2.24 us
  transfers between devices with their start and end apart: 8, of which 2 were waited for; matrix products, arithmetic and copies ran while one was open for 0% of the time, Pallas kernels for 3%

profile of v3, /device:TPU:0, one launch (start us, length us, event | category | flops | bytes accessed | tf_op | source)
XLA Modules:
  0.0 65.4 jit_solution(12308887573114618241)
XLA Ops:
  0.0 0.0 copy-start.1
  0.0 0.9 %copy-done.1 = bf16[3,32,1024]{2,1,0:T(8,128)(2,1)S(1)} copy-done((bf16[3,32,1024]{2,1,0:T(8,128)(2,1)S(1)}, bf16[3,32,1024]{2,1,0:T(8,128)(2,1)}, u32[]{:S(2)}) %copy-start.1) | copy-done | bytes 196632
  0.9 0.7 %shard_map.37 = bf16[8,96,128]{2,1,0:T(8,128)(2,1)} custom-call(bf16[3,32,1024]{2,1,0:T(8,128)(2,1)S(1)} %copy-done.1), custom_call_target="tpu_custom_call" | custom-call | tf_op jit(solution)/shard_map/pallas_call | solution.py:28
  1.6 6.3 %all-to-all-start = ((bf16[8,96,128]{2,1,0:T(8,128)(2,1)}), bf16[8,96,128]{2,1,0:T(8,128)(2,1)S(1)}, u32[]{:S(2)}, u32[]{:S(2)}) async-start(bf16[8,96,128]{2,1,0:T(8,128)(2,1)} %shard_map.37), calls=%async_computation | async-start | bytes 393216 | tf_op jit(solution)/shard_map/all_to_all | solution.py:163
  8.0 0.0 copy-start.2
  8.0 0.0 copy-start
  8.0 1.3 %copy-done = bf16[128,5120]{1,0:T(8,128)(2,1)S(1)} copy-done((bf16[128,5120]{1,0:T(8,128)(2,1)S(1)}, bf16[128,5120]{1,0:T(8,128)(2,1)}, u32[]{:S(2)}) %copy-start) | copy-done | bytes 1310744
  9.3 0.7 %shard_map.39 = bf16[8,32,640]{2,1,0:T(8,128)(2,1)} custom-call(s32[1]{0:T(128)} %bitcast.blk_ref, bf16[128,5120]{1,0:T(8,128)(2,1)S(1)} %copy-done), custom_call_target="tpu_custom_call" | custom-call | tf_op jit(solution)/shard_map/pallas_call | solution.py:46
  10.0 6.3 %all-to-all-done.own_ref = bf16[8,96,128]{2,1,0:T(8,128)(2,1)S(1)} async-done(((bf16[8,96,128]{2,1,0:T(8,128)(2,1)}), bf16[8,96,128]{2,1,0:T(8,128)(2,1)S(1)}, u32[]{:S(2)}, u32[]{:S(2)}) %all-to-all-start) | async-done | bytes 196640 | tf_op jit(solution)/shard_map/all_to_all | solution.py:163
  16.3 3.4 %all-to-all-start.1 = ((bf16[8,32,640]{2,1,0:T(8,128)(2,1)}), bf16[8,32,640]{2,1,0:T(8,128)(2,1)S(1)}, u32[]{:S(2)}, u32[]{:S(2)}) async-start(bf16[8,32,640]{2,1,0:T(8,128)(2,1)} %shard_map.39), calls=%async_computation.1 | async-start | bytes 655360 | tf_op jit(solution)/shard_map/all_to_all | solution.py:163
  19.8 2.5 %collective-permute-start.2 = (bf16[8,64,128]{2,1,0:T(8,128)(2,1)S(1)}, bf16[8,64,128]{2,1,0:T(8,128)(2,1)S(1)}, u32[]{:S(2)}, u32[]{:S(2)}) collective-permute-start(bf16[8,64,128]{2,1,0:T(8,128)(2,1)S(1)} %slice.4), channel_id=1, source_target_pairs={{0,24},{8,16},{16,8},{24,0},{1,25},{9,17},{17,9},{25,1},{2,26},{10... | collective-permute-start | bytes 393224 | tf_op jit(solution)/shard_map/ppermute | solution.py:169
  22.3 0.5 collective-permute-start.1
  22.8 0.5 collective-permute-start
  23.3 7.5 %all-to-all-done.1.refs_0_ = bf16[8,32,640]{2,1,0:T(8,128)(2,1)S(1)} async-done(((bf16[8,32,640]{2,1,0:T(8,128)(2,1)}), bf16[8,32,640]{2,1,0:T(8,128)(2,1)S(1)}, u32[]{:S(2)}, u32[]{:S(2)}) %all-to-all-start.1) | async-done | bytes 327712 | tf_op jit(solution)/shard_map/all_to_all | solution.py:163
  30.8 2.4 %collective-permute-start.5 = (bf16[8,32,640]{2,1,0:T(8,128)(2,1)S(1)}, bf16[8,32,640]{2,1,0:T(8,128)(2,1)S(1)}, u32[]{:S(2)}, u32[]{:S(2)}) collective-permute-start(bf16[8,32,640]{2,1,0:T(8,128)(2,1)S(1)} %all-to-all-done.1.refs_0_), channel_id=1, source_target_pairs={{0,24},{8,16},{16,8},{24,0},{1,25},{9,17},{17,9},{25,1},{2,26},{10... | collective-permute-start | bytes 983048 | tf_op jit(solution)/shard_map/ppermute | solution.py:169
  33.3 0.5 collective-permute-start.4
  33.8 0.0 collective-permute-done.2.refs_2_
  33.8 0.5 collective-permute-start.3
  34.3 0.0 collective-permute-done.1.refs_1_
  34.3 0.0 collective-permute-done.refs_0_
  34.3 0.0 copy-done.2
  34.3 1.2 %shard_map.38 = bf16[256,128]{1,0:T(8,128)(2,1)S(1)} custom-call(s32[1]{0:T(128)} %bitcast.blk_ref, s32[8]{0:T(128)S(1)} %copy-done.2, bf16[8,96,128]{2,1,0:T(8,128)(2,1)S(1)} %all-to-all-done.own_ref, bf16[8,64,128]{2,1,0:T(8,128)(2,1)S(1)} %collective-permute-done.refs_0_, bf16[8,64,128]{2,1,0:T(8,128)(2,1)S(1)} %collective-permute-done.1.refs_1_, ...), custom_call_target="tpu_custom_call" | custom-call | tf_op jit(solution)/shard_map/pallas_call | solution.py:107
  35.5 14.8 %all-gather = bf16[2048,128]{1,0:T(8,128)(2,1)S(1)} all-gather(bf16[256,128]{1,0:T(8,128)(2,1)S(1)} %shard_map.38), channel_id=2, replica_groups=mesh['blk'=4,'tile'=8] {'tile'}, dimensions={0}, use_global_device_ids=true | all-gather | bytes 589824 | tf_op jit(solution)/shard_map/all_gather | solution.py:185
  50.4 0.0 collective-permute-done.5.refs_3_
  50.4 0.0 collective-permute-done.4.refs_2_
  50.4 0.0 collective-permute-done.3.refs_1_
  50.4 0.7 %shard_map.40 = bf16[8,32,640]{2,1,0:T(8,128)(2,1)S(1)} custom-call(s32[1]{0:T(128)} %bitcast.blk_ref, bf16[8,256,128]{2,1,0:T(8,128)(2,1)S(1)} %bitcast.2, bf16[8,32,640]{2,1,0:T(8,128)(2,1)S(1)} %all-to-all-done.1.refs_0_, bf16[8,32,640]{2,1,0:T(8,128)(2,1)S(1)} %collective-permute-done.3.refs_1_, bf16[8,32,640]{2,1,0:T(8,128)(2,1)S(1)} %collective-permute-done.4.refs_2_, ...), custom_call_target="tpu_custom_call" | custom-call | tf_op jit(solution)/shard_map/pallas_call | solution.py:132
  51.1 13.6 %all_to_all.15.x_ref = bf16[8,32,640]{2,1,0:T(8,128)(2,1)S(1)} all-to-all(bf16[8,32,640]{2,1,0:T(8,128)(2,1)S(1)} %shard_map.40), channel_id=1, replica_groups=mesh['blk'=4,'tile'=8] {'tile'}, dimensions={0} | all-to-all | bytes 655360 | tf_op jit(solution)/shard_map/all_to_all | solution.py:163
  64.7 0.8 %shard_map.41 = bf16[32,5120]{1,0:T(8,128)(2,1)} custom-call(bf16[8,32,640]{2,1,0:T(8,128)(2,1)S(1)} %all_to_all.15.x_ref), custom_call_target="tpu_custom_call" | custom-call | tf_op jit(solution)/shard_map/pallas_call | solution.py:153
  (1 shorter events, 0.0 us)
Async XLA Ops:
  0.0 0.9 %copy-start.1 = (bf16[3,32,1024]{2,1,0:T(8,128)(2,1)S(1)}, bf16[3,32,1024]{2,1,0:T(8,128)(2,1)}, u32[]{:S(2)}) copy-start(bf16[3,32,1024]{2,1,0:T(8,128)(2,1)} %x_ref.2) | copy-start | bytes 589828
  1.6 14.7 %all-to-all-start = ((bf16[8,96,128]{2,1,0:T(8,128)(2,1)}), bf16[8,96,128]{2,1,0:T(8,128)(2,1)S(1)}, u32[]{:S(2)}, u32[]{:S(2)}) async-start(bf16[8,96,128]{2,1,0:T(8,128)(2,1)} %shard_map.37), calls=%async_computation | async-start | bytes 393216 | tf_op jit(solution)/shard_map/all_to_all | solution.py:163
  8.0 26.3 %copy-start.2 = (s32[8]{0:T(128)S(1)}, s32[8]{0:T(128)}, u32[]{:S(2)}) copy-start(s32[8]{0:T(128)} %clip_ref.1) | copy-start | bytes 100
  8.0 1.3 %copy-start = (bf16[128,5120]{1,0:T(8,128)(2,1)S(1)}, bf16[128,5120]{1,0:T(8,128)(2,1)}, u32[]{:S(2)}) copy-start(bf16[128,5120]{1,0:T(8,128)(2,1)} %x_ref.3) | copy-start | bytes 3932164
  16.3 14.5 %all-to-all-start.1 = ((bf16[8,32,640]{2,1,0:T(8,128)(2,1)}), bf16[8,32,640]{2,1,0:T(8,128)(2,1)S(1)}, u32[]{:S(2)}, u32[]{:S(2)}) async-start(bf16[8,32,640]{2,1,0:T(8,128)(2,1)} %shard_map.39), calls=%async_computation.1 | async-start | bytes 655360 | tf_op jit(solution)/shard_map/all_to_all | solution.py:163
  19.8 14.0 %collective-permute-start.2 = (bf16[8,64,128]{2,1,0:T(8,128)(2,1)S(1)}, bf16[8,64,128]{2,1,0:T(8,128)(2,1)S(1)}, u32[]{:S(2)}, u32[]{:S(2)}) collective-permute-start(bf16[8,64,128]{2,1,0:T(8,128)(2,1)S(1)} %slice.4), channel_id=1, source_target_pairs={{0,24},{8,16},{16,8},{24,0},{1,25},{9,17},{17,9},{25,1},{2,26},{10... | collective-permute-start | bytes 393224 | tf_op jit(solution)/shard_map/ppermute | solution.py:169
  22.3 12.0 %collective-permute-start.1 = (bf16[8,64,128]{2,1,0:T(8,128)(2,1)S(1)}, bf16[8,64,128]{2,1,0:T(8,128)(2,1)S(1)}, u32[]{:S(2)}, u32[]{:S(2)}) collective-permute-start(bf16[8,64,128]{2,1,0:T(8,128)(2,1)S(1)} %slice.4), channel_id=1, source_target_pairs={{0,16},{8,24},{16,0},{24,8},{1,17},{9,25},{17,1},{25,9},{2,18},{10... | collective-permute-start | bytes 393224 | tf_op jit(solution)/shard_map/ppermute | solution.py:169
  22.8 11.5 %collective-permute-start = (bf16[8,64,128]{2,1,0:T(8,128)(2,1)S(1)}, bf16[8,64,128]{2,1,0:T(8,128)(2,1)S(1)}, u32[]{:S(2)}, u32[]{:S(2)}) collective-permute-start(bf16[8,64,128]{2,1,0:T(8,128)(2,1)S(1)} %slice.4), channel_id=1, source_target_pairs={{0,8},{8,0},{16,24},{24,16},{1,9},{9,1},{17,25},{25,17},{2,10},{10... | collective-permute-start | bytes 393224 | tf_op jit(solution)/shard_map/ppermute | solution.py:169
  30.8 19.6 %collective-permute-start.5 = (bf16[8,32,640]{2,1,0:T(8,128)(2,1)S(1)}, bf16[8,32,640]{2,1,0:T(8,128)(2,1)S(1)}, u32[]{:S(2)}, u32[]{:S(2)}) collective-permute-start(bf16[8,32,640]{2,1,0:T(8,128)(2,1)S(1)} %all-to-all-done.1.refs_0_), channel_id=1, source_target_pairs={{0,24},{8,16},{16,8},{24,0},{1,25},{9,17},{17,9},{25,1},{2,26},{10... | collective-permute-start | bytes 983048 | tf_op jit(solution)/shard_map/ppermute | solution.py:169
  33.3 17.1 %collective-permute-start.4 = (bf16[8,32,640]{2,1,0:T(8,128)(2,1)S(1)}, bf16[8,32,640]{2,1,0:T(8,128)(2,1)S(1)}, u32[]{:S(2)}, u32[]{:S(2)}) collective-permute-start(bf16[8,32,640]{2,1,0:T(8,128)(2,1)S(1)} %all-to-all-done.1.refs_0_), channel_id=1, source_target_pairs={{0,16},{8,24},{16,0},{24,8},{1,17},{9,25},{17,1},{25,9},{2,18},{10... | collective-permute-start | bytes 983048 | tf_op jit(solution)/shard_map/ppermute | solution.py:169
  33.8 16.6 %collective-permute-start.3 = (bf16[8,32,640]{2,1,0:T(8,128)(2,1)S(1)}, bf16[8,32,640]{2,1,0:T(8,128)(2,1)S(1)}, u32[]{:S(2)}, u32[]{:S(2)}) collective-permute-start(bf16[8,32,640]{2,1,0:T(8,128)(2,1)S(1)} %all-to-all-done.1.refs_0_), channel_id=1, source_target_pairs={{0,8},{8,0},{16,24},{24,16},{1,9},{9,1},{17,25},{25,17},{2,10},{10... | collective-permute-start | bytes 983048 | tf_op jit(solution)/shard_map/ppermute | solution.py:169

commit v4 on v1

v4 whole, which is shorter than its diff:
```python
import functools
import math

import jax
import jax.numpy as jnp
from jax import lax
from jax.experimental import pallas as pl
from jax.experimental.pallas import tpu as pltpu
from jax.sharding import Mesh
from jax.sharding import PartitionSpec as P

FRB = 2
TPF = 16
ALL = ("blk", "row", "core")
PLANE = ("blk", "core")
VMEM = pl.BlockSpec(memory_space=pltpu.VMEM)
SMEM = pl.BlockSpec(memory_space=pltpu.SMEM)
ANY = pl.BlockSpec(memory_space=pl.ANY)
PARAMS = pltpu.CompilerParams(vmem_limit_bytes=48 * 1024 * 1024)


def pack_kernel(head_dim, x_ref, out_ref):
    peers, _, width = out_ref.shape
    kinds, tok, _ = x_ref.shape
    heads = width // head_dim
    for g in range(peers):
        for i in range(heads):
            head = (g // 2 * heads + i) * 2 + g % 2
            for k in range(kinds):
                out_ref[g, k * tok:(k + 1) * tok, i * head_dim:(i + 1) * head_dim] = x_ref[
                    k, :, head * head_dim:(head + 1) * head_dim
                ]


def pack(x, peers, head_dim):
    kinds, tok, cols = x.shape
    return pl.pallas_call(
        functools.partial(pack_kernel, head_dim),
        out_shape=jax.ShapeDtypeStruct((peers, kinds * tok, cols // peers), x.dtype),
        in_specs=[VMEM],
        out_specs=VMEM,
        compiler_params=PARAMS,
    )(x)


def columns_kernel(at_ref, x_ref, out_ref):
    out_ref[...] = x_ref[...]


def columns(x, at, parts):
    depth, cols = x.shape
    return pl.pallas_call(
        columns_kernel,
        out_shape=jax.ShapeDtypeStruct((depth, cols // parts), x.dtype),
        grid_spec=pltpu.PrefetchScalarGridSpec(
            num_scalar_prefetch=1,
            grid=(1,),
            in_specs=[pl.BlockSpec((depth, cols // parts), lambda i, at: (0, at[0]))],
            out_specs=pl.BlockSpec((depth, cols // parts), lambda i, at: (0, 0)),
        ),
        compiler_params=PARAMS,
    )(at, x)


def clip_of(token, blk_tokens, tok_dev, clip_ref):
    frame = token // blk_tokens * FRB + token % tok_dev // TPF
    clip = jnp.zeros_like(token)
    for f in range(clip_ref.shape[0]):
        clip = jnp.where(frame == f, clip_ref[f], clip)
    return clip


def attention_kernel(tok, head_dim, n_kv, clip_ref, own_ref, *refs):
    kv_refs, out_ref = refs[:n_kv], refs[len(refs) - 1 - (len(refs) - 1 - n_kv) // 2]
    peers, _, width = own_ref.shape
    count = peers * tok
    scale = 1.0 / math.sqrt(head_dim)
    row_clip = clip_of(
        lax.broadcasted_iota(jnp.int32, (count, 1), 0), 2 * tok, tok, clip_ref
    )
    col_clip = clip_of(
        lax.broadcasted_iota(jnp.int32, (1, count), 1), 2 * tok, tok, clip_ref
    )
    allowed = row_clip == col_clip
    sources = [(own_ref, tok)] + [(ref, 0) for ref in kv_refs]
    per_step = max(1, 1024 // count)
    for h in range(width // head_dim):
        cols = slice(h * head_dim, (h + 1) * head_dim)
        queries = own_ref[:, 0:tok, cols].reshape(count, head_dim)
        top = total = acc = None
        for first in range(0, len(sources), per_step):
            scores, values = [], []
            for ref, at in sources[first:first + per_step]:
                keys = ref[:, at:at + tok, cols].reshape(count, head_dim)
                values.append(ref[:, at + tok:at + 2 * tok, cols].reshape(count, head_dim))
                s = lax.dot_general(
                    queries, keys, (((1,), (1,)), ((), ())), preferred_element_type=jnp.float32
                )
                scores.append(jnp.where(allowed, s * scale, -1e30))
            new_top = functools.reduce(
                jnp.maximum, [jnp.max(s, axis=1, keepdims=True) for s in scores]
            )
            if top is not None:
                new_top = jnp.maximum(top, new_top)
                factor = jnp.exp(top - new_top)
                total, acc = total * factor, acc * factor
            top = new_top
            for s, v in zip(scores, values):
                p = jnp.where(allowed, jnp.exp(s - top), 0.0)
                part = jnp.sum(p, axis=1, keepdims=True)
                dot = jnp.dot(p.astype(jnp.bfloat16), v, preferred_element_type=jnp.float32)
                total = part if total is None else total + part
                acc = dot if acc is None else acc + dot
        out_ref[:, cols] = (acc / total).astype(out_ref.dtype)


def attention(own, others, frame_clip, tok, head_dim, passed):
    peers, _, width = own.shape
    like = jax.ShapeDtypeStruct((peers * tok, width), own.dtype)
    return pl.pallas_call(
        functools.partial(attention_kernel, tok, head_dim, len(others)),
        out_shape=[like] + [jax.ShapeDtypeStruct(x.shape, x.dtype) for x in passed],
        in_specs=[SMEM] + [VMEM] * (1 + len(others)) + [ANY] * len(passed),
        out_specs=[VMEM] + [ANY] * len(passed),
        input_output_aliases={2 + len(others) + i: 1 + i for i in range(len(passed))},
        compiler_params=PARAMS,
    )(frame_clip, own, *others, *passed)


def project_kernel(at_ref, core_ref, attn_ref, *refs):
    *w_refs, mine_ref, theirs_ref, a_ref, w_all = refs
    blks, _, width = attn_ref.shape
    head_dim, cols = w_refs[0].shape
    half = cols // 2
    for b in range(blks):
        a_ref[:, b * width:(b + 1) * width] = attn_ref[b]
    for i, ref in enumerate(w_refs):
        w_all[pl.ds(pl.multiple_of(at_ref[i] * head_dim, head_dim), head_dim), :] = ref[...]
    result = jnp.dot(a_ref[...], w_all[...], preferred_element_type=jnp.float32)
    result = result.astype(mine_ref.dtype)
    first = result[:, :half].reshape(mine_ref.shape)
    second = result[:, half:].reshape(mine_ref.shape)
    core = core_ref[0]

    @pl.when(core == 0)
    def _():
        mine_ref[...] = first
        theirs_ref[...] = second

    @pl.when(core != 0)
    def _():
        mine_ref[...] = second
        theirs_ref[...] = first


def project(attn_all, w_parts, at, core, tok):
    blks, count, width = attn_all.shape
    depth, cols = blks * width, w_parts[0].shape[1]
    like = jax.ShapeDtypeStruct((count // tok, tok, cols // 2), attn_all.dtype)
    return pl.pallas_call(
        project_kernel,
        out_shape=(like, like),
        in_specs=[SMEM, SMEM] + [VMEM] * (1 + len(w_parts)),
        out_specs=(VMEM, VMEM),
        scratch_shapes=[
            pltpu.VMEM((count, depth), attn_all.dtype),
            pltpu.VMEM((depth, cols), attn_all.dtype),
        ],
        compiler_params=PARAMS,
    )(at, core, attn_all, *w_parts)


def add_kernel(x_ref, y_ref, out_ref):
    both = x_ref[...].astype(jnp.float32) + y_ref[...].astype(jnp.float32)
    out_ref[...] = both.astype(out_ref.dtype)


def add(x, y):
    return pl.pallas_call(
        add_kernel,
        out_shape=jax.ShapeDtypeStruct(x.shape, x.dtype),
        in_specs=[VMEM, VMEM],
        out_specs=VMEM,
        compiler_params=PARAMS,
    )(x, y)


def unpack_kernel(x_ref, out_ref):
    peers, _, width = x_ref.shape
    for g in range(peers):
        out_ref[:, g * width:(g + 1) * width] = x_ref[g]


def unpack(x):
    peers, tok, width = x.shape
    return pl.pallas_call(
        unpack_kernel,
        out_shape=jax.ShapeDtypeStruct((tok, peers * width), x.dtype),
        in_specs=[VMEM],
        out_specs=VMEM,
        compiler_params=PARAMS,
    )(x)


def xor(x, axis, by):
    return lax.ppermute(x, axis, [(i, i ^ by) for i in range(lax.axis_size(axis))])


def inner(x):
    return lax.ppermute(x, "row", [(0, 0), (1, 2), (2, 1), (3, 3)])


def exchange(x, axis):
    return lax.all_to_all(x, axis, split_axis=0, concat_axis=0, tiled=True)


def on_device(qkv, frame_clip, w_out):
    rows, blks = lax.axis_size("row"), lax.axis_size("blk")
    row, core = lax.axis_index("row"), lax.axis_index("core")
    tok = qkv.shape[1]
    head_dim = w_out.shape[0]

    w_own = columns(w_out, lax.axis_index("blk").astype(jnp.int32).reshape(1), blks)
    chain = rows == 4
    if chain:
        w_next, w_mid = xor(w_own, "row", 1), inner(w_own)
    own = exchange(pack(qkv, 2 * blks, head_dim), PLANE)
    kv = own[:, tok:]
    if chain:
        w_far, w_end = inner(w_next), xor(w_mid, "row", 1)
    others = [xor(kv, "row", by) for by in range(1, rows)]
    passed = (w_far,) if chain else (w_own,)
    attn, passed = attention(own, others, frame_clip, tok, head_dim, passed)
    if chain:
        w_parts = [w_own, w_next, w_mid, w_end, passed, xor(passed, "row", 1)]
        middle = (row == 1) | (row == 2)
        pick = lambda a, b: jnp.where(middle, a, b)
        at = [
            row, row ^ 1, pick(3 - row, row), pick(row ^ 1, 3 - (row ^ 1)),
            pick((3 - row) ^ 1, row ^ 1), pick(row, (3 - (row ^ 1)) ^ 1),
        ]
    else:
        w_parts = [passed] + [xor(passed, "row", by) for by in range(1, rows)]
        at = [row ^ by for by in range(rows)]
    attn_all = lax.all_gather(attn, "blk", axis=0, tiled=False)
    mine, theirs = project(
        attn_all, w_parts, jnp.stack(at).astype(jnp.int32),
        core.astype(jnp.int32).reshape(1), tok,
    )
    return unpack(exchange(add(mine, xor(theirs, "core", 1)), PLANE))


def solution(mesh):
    blk, tile = mesh.shape["blk"], mesh.shape["tile"]
    fine = Mesh(mesh.devices.reshape(blk, tile // 2, 2), ALL)
    in_specs = (P(None, ALL, None), P(), P(("row", "core"), None))
    return jax.shard_map(
        on_device, mesh=fine, in_specs=in_specs, out_specs=P(ALL, None), check_vma=False
    )
```

time: 79.5 us -> 64 us (0.81)
  waiting for transfers between devices: 39 us -> 17.9 us
  blocking collectives: 19.2 us -> 28.1 us
  starting transfers between devices: 14 us -> 12.9 us
  other arithmetic: 1.08 us -> 0 us
    ppermute x7 -> x9, waiting for transfers between devices: 33.8 us -> 17.9 us  [the longest x7 17.9 us: xor(): lax.ppermute(x, axis, [(i, i ^ by) for i in range(lax.axis_size(axis))])]
    all_to_all x1 -> x2, blocking collectives: 10.2 us -> 19.9 us  [exchange(): return lax.all_to_all(x, axis, split_axis=0, concat_axis=0, tiled=True)]
    all_to_all x1 -> x0, waiting for transfers between devices: 5.25 us -> none  [on_device(): lax.all_to_all(pack(qkv, peers), PLANE, split_axis=0, concat_axis=0, tile...]
    all_to_all x1 -> x0, starting transfers between devices: 4.83 us -> none  [on_device(): lax.all_to_all(pack(qkv, peers), PLANE, split_axis=0, concat_axis=0, tile...]
    ppermute x7 -> x9, starting transfers between devices: 9.18 us -> 12.9 us  [the longest x7 11.6 us: xor(): lax.ppermute(x, axis, [(i, i ^ by) for i in range(lax.axis_size(axis))])]
    select_n x1 -> x0, other arithmetic: 0.98 us -> none  [on_device(): first = jnp.where(core == 0, mine, got)]
    dynamic_slice x1 -> x0, local copies, waits for them, and re-layouts: 0.93 us -> none  [on_device(): lax.dynamic_slice(w_out, (0, (blk * 2 + 1 - core) * cols), (head_dim, cols))]
    all_gather x1, blocking collectives: 9.03 us -> 8.16 us  [on_device(): attn_all = lax.all_gather(attn, 'blk', axis=0, tiled=False)]
  transfers between devices with their start and end apart: 8 -> 9, of which waited for: 2 -> 4; matrix products, arithmetic and copies ran while one was open for 1% -> 0% of each run, Pallas kernels for 2% -> 2%
where the time goes in v4:
time: 64 us; the launch traced here: 63.8 us
  blocking collectives  28.1 us (44%)
  waiting for transfers between devices  17.9 us (28%)
  starting transfers between devices  12.9 us (20%)
  Pallas kernels  3.4 us (5%)
  local copies, waits for them, and re-layouts  1.42 us (2%)
    all_to_all x2, blocking collectives, exchange(): return lax.all_to_all(x, axis, split_axis=0, concat_axis=0, tiled=True)  19.9 us
    ppermute x7, waiting for transfers between devices, xor(): lax.ppermute(x, axis, [(i, i ^ by) for i in range(lax.axis_size(axis))])  17.9 us
    ppermute x7, starting transfers between devices, xor(): lax.ppermute(x, axis, [(i, i ^ by) for i in range(lax.axis_size(axis))])  11.6 us
    all_gather x1, blocking collectives, on_device(): attn_all = lax.all_gather(attn, 'blk', axis=0, tiled=False)  8.16 us
    ppermute x2, starting transfers between devices, inner(): return lax.ppermute(x, 'row', [(0, 0), (1, 2), (2, 1), (3, 3)])  1.34 us
    unnamed x6, local copies, waits for them, and re-layouts  1.32 us
  transfers between devices with their start and end apart: 9, of which 4 were waited for; matrix products, arithmetic and copies ran while one was open for 0% of the time, Pallas kernels for 2%

profile of v4, /device:TPU:0, one launch (start us, length us, event | category | flops | bytes accessed | tf_op | source)
XLA Modules:
  0.0 63.8 jit_solution(12689615869026779025)
XLA Ops:
  0.0 0.0 copy-start
  0.0 1.3 %copy-done = bf16[128,5120]{1,0:T(8,128)(2,1)S(1)} copy-done((bf16[128,5120]{1,0:T(8,128)(2,1)S(1)}, bf16[128,5120]{1,0:T(8,128)(2,1)}, u32[]{:S(2)}) %copy-start) | copy-done | bytes 1310744
  1.3 0.0 copy-start.1
  1.3 0.0 copy-start.2
  1.3 3.1 %collective-permute-start.3 = (bf16[128,1280]{1,0:T(8,128)(2,1)S(1)}, bf16[128,1280]{1,0:T(8,128)(2,1)S(1)}, u32[]{:S(2)}, u32[]{:S(2)}) collective-permute-start(bf16[128,1280]{1,0:T(8,128)(2,1)S(1)} %shard_map.38.refs_0_), channel_id=1, source_target_pairs={{0,2},{2,0},{4,6},{6,4},{1,3},{3,1},{5,7},{7,5},{8,10},{10,8},{12,... | collective-permute-start | bytes 983048 | tf_op jit(solution)/shard_map/ppermute | solution.py:206
  4.4 0.7 %collective-permute-start.5 = (bf16[128,1280]{1,0:T(8,128)(2,1)S(1)}, bf16[128,1280]{1,0:T(8,128)(2,1)S(1)}, u32[]{:S(2)}, u32[]{:S(2)}) collective-permute-start(bf16[128,1280]{1,0:T(8,128)(2,1)S(1)} %shard_map.38.refs_0_), channel_id=1, source_target_pairs={{0,0},{2,4},{4,2},{6,6},{1,1},{3,5},{5,3},{7,7},{8,8},{10,12},{12,... | collective-permute-start | bytes 983048 | tf_op jit(solution)/shard_map/ppermute | solution.py:210
  5.1 7.0 %collective-permute-done.3.refs_1_ = bf16[128,1280]{1,0:T(8,128)(2,1)S(1)} collective-permute-done((bf16[128,1280]{1,0:T(8,128)(2,1)S(1)}, bf16[128,1280]{1,0:T(8,128)(2,1)S(1)}, u32[]{:S(2)}, u32[]{:S(2)}) %collective-permute-start.3) | collective-permute-done | bytes 327712 | tf_op jit(solution)/shard_map/ppermute | solution.py:206
  12.1 0.7 %collective-permute-start.4 = (bf16[128,1280]{1,0:T(8,128)(2,1)S(1)}, bf16[128,1280]{1,0:T(8,128)(2,1)S(1)}, u32[]{:S(2)}, u32[]{:S(2)}) collective-permute-start(bf16[128,1280]{1,0:T(8,128)(2,1)S(1)} %collective-permute-done.3.refs_1_), channel_id=1, source_target_pairs={{0,0},{2,4},{4,2},{6,6},{1,1},{3,5},{5,3},{7,7},{8,8},{10,12},{12,... | collective-permute-start | bytes 983048 | tf_op jit(solution)/shard_map/ppermute | solution.py:210
  12.8 0.0 copy-done.1
  12.9 9.9 %all_to_all.10.own_ref = bf16[8,96,128]{2,1,0:T(8,128)(2,1)S(1)} all-to-all(bf16[8,96,128]{2,1,0:T(8,128)(2,1)S(1)} %shard_map.37), channel_id=1, replica_groups=mesh['blk'=4,'row'=4,'core'=2] {'blk','core'}, dimensions={0} | all-to-all | bytes 393216 | tf_op jit(solution)/shard_map/all_to_all | solution.py:214
  22.8 3.7 %collective-permute-start.2 = (bf16[8,64,128]{2,1,0:T(8,128)(2,1)S(1)}, bf16[8,64,128]{2,1,0:T(8,128)(2,1)S(1)}, u32[]{:S(2)}, u32[]{:S(2)}) collective-permute-start(bf16[8,64,128]{2,1,0:T(8,128)(2,1)S(1)} %slice.4), channel_id=1, source_target_pairs={{0,6},{2,4},{4,2},{6,0},{1,7},{3,5},{5,3},{7,1},{8,14},{10,12},{12... | collective-permute-start | bytes 393224 | tf_op jit(solution)/shard_map/ppermute | solution.py:206
  26.5 2.2 %collective-permute-start.1 = (bf16[8,64,128]{2,1,0:T(8,128)(2,1)S(1)}, bf16[8,64,128]{2,1,0:T(8,128)(2,1)S(1)}, u32[]{:S(2)}, u32[]{:S(2)}) collective-permute-start(bf16[8,64,128]{2,1,0:T(8,128)(2,1)S(1)} %slice.4), channel_id=1, source_target_pairs={{0,4},{2,6},{4,0},{6,2},{1,5},{3,7},{5,1},{7,3},{8,12},{10,14},{12... | collective-permute-start | bytes 393224 | tf_op jit(solution)/shard_map/ppermute | solution.py:206
  28.7 0.0 collective-permute-start
  28.7 0.0 collective-permute-done.5.refs_2_
  28.7 2.0 %collective-permute-start.6 = (bf16[128,1280]{1,0:T(8,128)(2,1)S(1)}, bf16[128,1280]{1,0:T(8,128)(2,1)S(1)}, u32[]{:S(2)}, u32[]{:S(2)}) collective-permute-start(bf16[128,1280]{1,0:T(8,128)(2,1)S(1)} %collective-permute-done.5.refs_2_), channel_id=1, source_target_pairs={{0,2},{2,0},{4,6},{6,4},{1,3},{3,1},{5,7},{7,5},{8,10},{10,8},{12,... | collective-permute-start | bytes 983048 | tf_op jit(solution)/shard_map/ppermute | solution.py:206
  30.7 0.0 collective-permute-done.2.refs_2_
  30.8 7.5 %collective-permute-done.1.refs_1_ = bf16[8,64,128]{2,1,0:T(8,128)(2,1)S(1)} collective-permute-done((bf16[8,64,128]{2,1,0:T(8,128)(2,1)S(1)}, bf16[8,64,128]{2,1,0:T(8,128)(2,1)S(1)}, u32[]{:S(2)}, u32[]{:S(2)}) %collective-permute-start.1) | collective-permute-done | bytes 131104 | tf_op jit(solution)/shard_map/ppermute | solution.py:206
  38.2 0.0 collective-permute-done.refs_0_
  38.2 0.0 collective-permute-done.4.refs_3_
  38.2 0.0 copy-done.2
  38.2 1.3 %shard_map.39 = (bf16[256,128]{1,0:T(8,128)(2,1)S(1)}, bf16[128,1280]{1,0:T(8,128)(2,1)S(1)}) custom-call(s32[8]{0:T(128)S(1)} %copy-done.2, bf16[8,96,128]{2,1,0:T(8,128)(2,1)S(1)} %all_to_all.10.own_ref, bf16[8,64,128]{2,1,0:T(8,128)(2,1)S(1)} %collective-permute-done.refs_0_, ...), custom_call_target="tpu_custom_call", output_to_operand_aliasing={{1}: (5, {})} | custom-call | tf_op jit(solution)/shard_map/pallas_call | solution.py:120
  39.5 0.5 collective-permute-start.7
  40.0 0.1 stack.27.at_ref
  40.0 8.2 %all-gather = bf16[1024,128]{1,0:T(8,128)(2,1)S(1)} all-gather(bf16[256,128]{1,0:T(8,128)(2,1)S(1)} %get-tuple-element.9), channel_id=2, replica_groups=mesh['blk'=4,'row'=4,'core'=2] {'blk'}, dimensions={0}, use_global_device_ids=true | all-gather | bytes 327680 | tf_op jit(solution)/shard_map/all_gather | solution.py:245
  48.2 0.0 collective-permute-done.6.refs_3_
  48.2 1.7 %collective-permute-done.7.refs_5_ = bf16[128,1280]{1,0:T(8,128)(2,1)S(1)} collective-permute-done((bf16[128,1280]{1,0:T(8,128)(2,1)S(1)}, bf16[128,1280]{1,0:T(8,128)(2,1)S(1)}, u32[]{:S(2)}, u32[]{:S(2)}) %collective-permute-start.7) | collective-permute-done | bytes 327712 | tf_op jit(solution)/shard_map/ppermute | solution.py:206
  49.9 1.3 %shard_map.40 = (bf16[8,32,640]{2,1,0:T(8,128)(2,1)S(1)}, bf16[8,32,640]{2,1,0:T(8,128)(2,1)S(1)}) custom-call(s32[6]{0:T(128)S(1)} %stack.27.at_ref, s32[1]{0:T(128)} %bitcast.6.core_ref, bf16[4,256,128]{2,1,0:T(8,128)(2,1)S(1)} %bitcast.9, bf16[128,1280]{1,0:T(8,128)(2,1)S(1)} %shard_map.38.refs_0_, bf16[128,1280]{1,0:T(8,128)(2,1)S(1)} %collective-permute-done.3.refs_1_, ...), custom_call_target="tpu_custom_call" | custom-call | tf_op jit(solution)/shard_map/pallas_call | solution.py:160
  51.2 0.1 collective-permute-start.8
  51.3 1.6 %collective-permute-done.8.y_ref = bf16[8,32,640]{2,1,0:T(8,128)(2,1)S(1)} collective-permute-done((bf16[8,32,640]{2,1,0:T(8,128)(2,1)S(1)}, bf16[8,32,640]{2,1,0:T(8,128)(2,1)S(1)}, u32[]{:S(2)}, u32[]{:S(2)}) %collective-permute-start.8) | collective-permute-done | bytes 327712 | tf_op jit(solution)/shard_map/ppermute | solution.py:206
  52.9 0.1 shard_map.41
  53.0 10.0 %all_to_all.11.x_ref = bf16[8,32,640]{2,1,0:T(8,128)(2,1)S(1)} all-to-all(bf16[8,32,640]{2,1,0:T(8,128)(2,1)S(1)} %shard_map.41), channel_id=1, replica_groups=mesh['blk'=4,'row'=4,'core'=2] {'blk','core'}, dimensions={0} | all-to-all | bytes 655360 | tf_op jit(solution)/shard_map/all_to_all | solution.py:214
  63.0 0.8 %shard_map.42 = bf16[32,5120]{1,0:T(8,128)(2,1)} custom-call(bf16[8,32,640]{2,1,0:T(8,128)(2,1)S(1)} %all_to_all.11.x_ref), custom_call_target="tpu_custom_call" | custom-call | tf_op jit(solution)/shard_map/pallas_call | solution.py:196
  (3 shorter events, 0.1 us)
Async XLA Ops:
  0.0 1.3 %copy-start = (bf16[128,5120]{1,0:T(8,128)(2,1)S(1)}, bf16[128,5120]{1,0:T(8,128)(2,1)}, u32[]{:S(2)}) copy-start(bf16[128,5120]{1,0:T(8,128)(2,1)} %x_ref.3) | copy-start | bytes 3932164
  1.3 11.5 %copy-start.1 = (bf16[3,32,1024]{2,1,0:T(8,128)(2,1)S(1)}, bf16[3,32,1024]{2,1,0:T(8,128)(2,1)}, u32[]{:S(2)}) copy-start(bf16[3,32,1024]{2,1,0:T(8,128)(2,1)} %x_ref.2) | copy-start | bytes 589828
  1.3 36.9 %copy-start.2 = (s32[8]{0:T(128)S(1)}, s32[8]{0:T(128)}, u32[]{:S(2)}) copy-start(s32[8]{0:T(128)} %clip_ref.1) | copy-start | bytes 100
  1.3 10.8 %collective-permute-start.3 = (bf16[128,1280]{1,0:T(8,128)(2,1)S(1)}, bf16[128,1280]{1,0:T(8,128)(2,1)S(1)}, u32[]{:S(2)}, u32[]{:S(2)}) collective-permute-start(bf16[128,1280]{1,0:T(8,128)(2,1)S(1)} %shard_map.38.refs_0_), channel_id=1, source_target_pairs={{0,2},{2,0},{4,6},{6,4},{1,3},{3,1},{5,7},{7,5},{8,10},{10,8},{12,... | collective-permute-start | bytes 983048 | tf_op jit(solution)/shard_map/ppermute | solution.py:206
  4.4 24.3 %collective-permute-start.5 = (bf16[128,1280]{1,0:T(8,128)(2,1)S(1)}, bf16[128,1280]{1,0:T(8,128)(2,1)S(1)}, u32[]{:S(2)}, u32[]{:S(2)}) collective-permute-start(bf16[128,1280]{1,0:T(8,128)(2,1)S(1)} %shard_map.38.refs_0_), channel_id=1, source_target_pairs={{0,0},{2,4},{4,2},{6,6},{1,1},{3,5},{5,3},{7,7},{8,8},{10,12},{12,... | collective-permute-start | bytes 983048 | tf_op jit(solution)/shard_map/ppermute | solution.py:210
  12.1 26.1 %collective-permute-start.4 = (bf16[128,1280]{1,0:T(8,128)(2,1)S(1)}, bf16[128,1280]{1,0:T(8,128)(2,1)S(1)}, u32[]{:S(2)}, u32[]{:S(2)}) collective-permute-start(bf16[128,1280]{1,0:T(8,128)(2,1)S(1)} %collective-permute-done.3.refs_1_), channel_id=1, source_target_pairs={{0,0},{2,4},{4,2},{6,6},{1,1},{3,5},{5,3},{7,7},{8,8},{10,12},{12,... | collective-permute-start | bytes 983048 | tf_op jit(solution)/shard_map/ppermute | solution.py:210
  22.8 7.9 %collective-permute-start.2 = (bf16[8,64,128]{2,1,0:T(8,128)(2,1)S(1)}, bf16[8,64,128]{2,1,0:T(8,128)(2,1)S(1)}, u32[]{:S(2)}, u32[]{:S(2)}) collective-permute-start(bf16[8,64,128]{2,1,0:T(8,128)(2,1)S(1)} %slice.4), channel_id=1, source_target_pairs={{0,6},{2,4},{4,2},{6,0},{1,7},{3,5},{5,3},{7,1},{8,14},{10,12},{12... | collective-permute-start | bytes 393224 | tf_op jit(solution)/shard_map/ppermute | solution.py:206
  26.5 11.7 %collective-permute-start.1 = (bf16[8,64,128]{2,1,0:T(8,128)(2,1)S(1)}, bf16[8,64,128]{2,1,0:T(8,128)(2,1)S(1)}, u32[]{:S(2)}, u32[]{:S(2)}) collective-permute-start(bf16[8,64,128]{2,1,0:T(8,128)(2,1)S(1)} %slice.4), channel_id=1, source_target_pairs={{0,4},{2,6},{4,0},{6,2},{1,5},{3,7},{5,1},{7,3},{8,12},{10,14},{12... | collective-permute-start | bytes 393224 | tf_op jit(solution)/shard_map/ppermute | solution.py:206
  28.7 9.5 %collective-permute-start = (bf16[8,64,128]{2,1,0:T(8,128)(2,1)S(1)}, bf16[8,64,128]{2,1,0:T(8,128)(2,1)S(1)}, u32[]{:S(2)}, u32[]{:S(2)}) collective-permute-start(bf16[8,64,128]{2,1,0:T(8,128)(2,1)S(1)} %slice.4), channel_id=1, source_target_pairs={{0,2},{2,0},{4,6},{6,4},{1,3},{3,1},{5,7},{7,5},{8,10},{10,8},{12,... | collective-permute-start | bytes 393224 | tf_op jit(solution)/shard_map/ppermute | solution.py:206
  28.7 19.5 %collective-permute-start.6 = (bf16[128,1280]{1,0:T(8,128)(2,1)S(1)}, bf16[128,1280]{1,0:T(8,128)(2,1)S(1)}, u32[]{:S(2)}, u32[]{:S(2)}) collective-permute-start(bf16[128,1280]{1,0:T(8,128)(2,1)S(1)} %collective-permute-done.5.refs_2_), channel_id=1, source_target_pairs={{0,2},{2,0},{4,6},{6,4},{1,3},{3,1},{5,7},{7,5},{8,10},{10,8},{12,... | collective-permute-start | bytes 983048 | tf_op jit(solution)/shard_map/ppermute | solution.py:206
  39.5 10.5 %collective-permute-start.7 = (bf16[128,1280]{1,0:T(8,128)(2,1)S(1)}, bf16[128,1280]{1,0:T(8,128)(2,1)S(1)}, u32[]{:S(2)}, u32[]{:S(2)}) collective-permute-start(bf16[128,1280]{1,0:T(8,128)(2,1)S(1)} %get-tuple-element.10.refs_4_), channel_id=1, source_target_pairs={{0,2},{2,0},{4,6},{6,4},{1,3},{3,1},{5,7},{7,5},{8,10},{10,8},{12,... | collective-permute-start | bytes 983048 | tf_op jit(solution)/shard_map/ppermute | solution.py:206
  51.2 1.7 %collective-permute-start.8 = (bf16[8,32,640]{2,1,0:T(8,128)(2,1)S(1)}, bf16[8,32,640]{2,1,0:T(8,128)(2,1)S(1)}, u32[]{:S(2)}, u32[]{:S(2)}) collective-permute-start(bf16[8,32,640]{2,1,0:T(8,128)(2,1)S(1)} %get-tuple-element.12), channel_id=1, source_target_pairs={{0,1},{1,0},{2,3},{3,2},{4,5},{5,4},{6,7},{7,6},{8,9},{9,8},{10,11... | collective-permute-start | bytes 983048 | tf_op jit(solution)/shard_map/ppermute | solution.py:206

commit v5 on v4

--- a/solution.py
+++ b/solution.py
@@ -70,8 +70,26 @@
     return clip
 
 
-def attention_kernel(tok, head_dim, n_kv, clip_ref, own_ref, *refs):
-    kv_refs, out_ref = refs[:n_kv], refs[len(refs) - 1 - (len(refs) - 1 - n_kv) // 2]
+def cut_kernel(tok, x_ref, *refs):
+    refs[len(refs) // 2][...] = x_ref[:, tok:, :]
+
+
+def cut(x, tok, passed):
+    peers, depth, width = x.shape
+    like = jax.ShapeDtypeStruct((peers, depth - tok, width), x.dtype)
+    kv, *same = pl.pallas_call(
+        functools.partial(cut_kernel, tok),
+        out_shape=[like] + [jax.ShapeDtypeStruct(y.shape, y.dtype) for y in passed],
+        in_specs=[VMEM] + [ANY] * len(passed),
+        out_specs=[VMEM] + [ANY] * len(passed),
+        input_output_aliases={1 + i: 1 + i for i in range(len(passed))},
+        compiler_params=PARAMS,
+    )(x, *passed)
+    return kv, same
+
+
+def attention_kernel(tok, head_dim, clip_ref, own_ref, *refs):
+    *kv_refs, out_ref = refs
     peers, _, width = own_ref.shape
     count = peers * tok
     scale = 1.0 / math.sqrt(head_dim)
@@ -114,17 +132,15 @@
         out_ref[:, cols] = (acc / total).astype(out_ref.dtype)
 
 
-def attention(own, others, frame_clip, tok, head_dim, passed):
+def attention(own, others, frame_clip, tok, head_dim):
     peers, _, width = own.shape
-    like = jax.ShapeDtypeStruct((peers * tok, width), own.dtype)
-    return pl.pallas_call(
-        functools.partial(attention_kernel, tok, head_dim, len(others)),
-        out_shape=[like] + [jax.ShapeDtypeStruct(x.shape, x.dtype) for x in passed],
-        in_specs=[SMEM] + [VMEM] * (1 + len(others)) + [ANY] * len(passed),
-        out_specs=[VMEM] + [ANY] * len(passed),
-        input_output_aliases={2 + len(others) + i: 1 + i for i in range(len(passed))},
-        compiler_params=PARAMS,
-    )(frame_clip, own, *others, *passed)
+    return pl.pallas_call(
+        functools.partial(attention_kernel, tok, head_dim),
+        out_shape=jax.ShapeDtypeStruct((peers * tok, width), own.dtype),
+        in_specs=[SMEM] + [VMEM] * (1 + len(others)),
+        out_specs=VMEM,
+        compiler_params=PARAMS,
+    )(frame_clip, own, *others)
 
 
 def project_kernel(at_ref, core_ref, attn_ref, *refs):
@@ -206,10 +222,6 @@
     return lax.ppermute(x, axis, [(i, i ^ by) for i in range(lax.axis_size(axis))])
 
 
-def inner(x):
-    return lax.ppermute(x, "row", [(0, 0), (1, 2), (2, 1), (3, 3)])
-
-
 def exchange(x, axis):
     return lax.all_to_all(x, axis, split_axis=0, concat_axis=0, tiled=True)
 
@@ -221,27 +233,18 @@
     head_dim = w_out.shape[0]
 
     w_own = columns(w_out, lax.axis_index("blk").astype(jnp.int32).reshape(1), blks)
-    chain = rows == 4
-    if chain:
-        w_next, w_mid = xor(w_own, "row", 1), inner(w_own)
+    half = rows == 4
+    steps = [rows - 1] + list(range(1, 2 if half else rows - 1))
+    w_others = [xor(w_own, "row", by) for by in steps]
     own = exchange(pack(qkv, 2 * blks, head_dim), PLANE)
-    kv = own[:, tok:]
-    if chain:
-        w_far, w_end = inner(w_next), xor(w_mid, "row", 1)
+    kv, w_others = cut(own, tok, w_others)
     others = [xor(kv, "row", by) for by in range(1, rows)]
-    passed = (w_far,) if chain else (w_own,)
-    attn, passed = attention(own, others, frame_clip, tok, head_dim, passed)
-    if chain:
-        w_parts = [w_own, w_next, w_mid, w_end, passed, xor(passed, "row", 1)]
-        middle = (row == 1) | (row == 2)
-        pick = lambda a, b: jnp.where(middle, a, b)
-        at = [
-            row, row ^ 1, pick(3 - row, row), pick(row ^ 1, 3 - (row ^ 1)),
-            pick((3 - row) ^ 1, row ^ 1), pick(row, (3 - (row ^ 1)) ^ 1),
-        ]
-    else:
-        w_parts = [passed] + [xor(passed, "row", by) for by in range(1, rows)]
-        at = [row ^ by for by in range(rows)]
+    if half:
+        steps.append(2)
+        w_others.append(xor(w_others[0], "row", 1))
+    w_parts = [w_own] + w_others
+    at = [row] + [row ^ by for by in steps]
+    attn = attention(own, others, frame_clip, tok, head_dim)
     attn_all = lax.all_gather(attn, "blk", axis=0, tiled=False)
     mine, theirs = project(
         attn_all, w_parts, jnp.stack(at).astype(jnp.int32),

time: 64 us -> 63.1 us (0.986)
  starting transfers between devices: 12.9 us -> 10.7 us
  blocking collectives: 28.1 us -> 29.2 us
    ppermute x2 -> x0, starting transfers between devices: 1.34 us -> none  [inner(): return lax.ppermute(x, 'row', [(0, 0), (1, 2), (2, 1), (3, 3)])]
    all_gather x1, blocking collectives: 8.16 us -> 9.23 us  [on_device(): attn_all = lax.all_gather(attn, 'blk', axis=0, tiled=False)]
    ppermute x7, starting transfers between devices: 11.6 us -> 10.7 us  [xor(): lax.ppermute(x, axis, [(i, i ^ by) for i in range(lax.axis_size(axis))])]
  transfers between devices with their start and end apart: 9 -> 7, of which waited for: 4 -> 4; matrix products, arithmetic and copies ran while one was open for 0% -> 0% of each run, Pallas kernels for 2% -> 2%
where the time goes in v5:
time: 63.1 us; the launch traced here: 62.9 us
  blocking collectives  29.2 us (46%)
  waiting for transfers between devices  18.3 us (29%)
  starting transfers between devices  10.7 us (17%)
  Pallas kernels  3.36 us (5%)
  local copies, waits for them, and re-layouts  1.32 us (2%)
    all_to_all x2, blocking collectives, exchange(): return lax.all_to_all(x, axis, split_axis=0, concat_axis=0, tiled=True)  19.9 us
    ppermute x7, waiting for transfers between devices, xor(): lax.ppermute(x, axis, [(i, i ^ by) for i in range(lax.axis_size(axis))])  18.3 us
    ppermute x7, starting transfers between devices, xor(): lax.ppermute(x, axis, [(i, i ^ by) for i in range(lax.axis_size(axis))])  10.7 us
    all_gather x1, blocking collectives, on_device(): attn_all = lax.all_gather(attn, 'blk', axis=0, tiled=False)  9.23 us
    unnamed x6, local copies, waits for them, and re-layouts  1.32 us
  transfers between devices with their start and end apart: 7, of which 4 were waited for; matrix products, arithmetic and copies ran while one was open for 0% of the time, Pallas kernels for 2%

profile of v5, /device:TPU:0, one launch (start us, length us, event | category | flops | bytes accessed | tf_op | source)
XLA Modules:
  0.0 62.9 jit_solution(12538228295220678012)
XLA Ops:
  0.0 0.0 copy-start
  0.0 1.3 %copy-done = bf16[128,5120]{1,0:T(8,128)(2,1)S(1)} copy-done((bf16[128,5120]{1,0:T(8,128)(2,1)S(1)}, bf16[128,5120]{1,0:T(8,128)(2,1)}, u32[]{:S(2)}) %copy-start) | copy-done | bytes 1310744
  1.3 0.0 copy-start.1
  1.3 0.0 copy-start.2
  1.3 3.1 %collective-permute-start.1 = (bf16[128,1280]{1,0:T(8,128)(2,1)S(1)}, bf16[128,1280]{1,0:T(8,128)(2,1)S(1)}, u32[]{:S(2)}, u32[]{:S(2)}) collective-permute-start(bf16[128,1280]{1,0:T(8,128)(2,1)S(1)} %shard_map.38.refs_0_), channel_id=1, source_target_pairs={{0,2},{2,0},{4,6},{6,4},{1,3},{3,1},{5,7},{7,5},{8,10},{10,8},{12,... | collective-permute-start | bytes 983048 | tf_op jit(solution)/shard_map/ppermute | solution.py:222
  4.4 2.5 %collective-permute-start = (bf16[128,1280]{1,0:T(8,128)(2,1)S(1)}, bf16[128,1280]{1,0:T(8,128)(2,1)S(1)}, u32[]{:S(2)}, u32[]{:S(2)}) collective-permute-start(bf16[128,1280]{1,0:T(8,128)(2,1)S(1)} %shard_map.38.refs_0_), channel_id=1, source_target_pairs={{0,6},{2,4},{4,2},{6,0},{1,7},{3,5},{5,3},{7,1},{8,14},{10,12},{12... | collective-permute-start | bytes 983048 | tf_op jit(solution)/shard_map/ppermute | solution.py:222
  6.9 0.0 copy-done.1
  7.0 9.8 %all_to_all.10.x_ref.own_ref = bf16[8,96,128]{2,1,0:T(8,128)(2,1)S(1)} all-to-all(bf16[8,96,128]{2,1,0:T(8,128)(2,1)S(1)} %shard_map.37), channel_id=1, replica_groups=mesh['blk'=4,'row'=4,'core'=2] {'blk','core'}, dimensions={0} | all-to-all | bytes 393216 | tf_op jit(solution)/shard_map/all_to_all | solution.py:226
  16.7 0.0 collective-permute-done.1.refs_1_
  16.7 4.8 %collective-permute-done.refs_0_ = bf16[128,1280]{1,0:T(8,128)(2,1)S(1)} collective-permute-done((bf16[128,1280]{1,0:T(8,128)(2,1)S(1)}, bf16[128,1280]{1,0:T(8,128)(2,1)S(1)}, u32[]{:S(2)}, u32[]{:S(2)}) %collective-permute-start) | collective-permute-done | bytes 327712 | tf_op jit(solution)/shard_map/ppermute | solution.py:222
  21.5 0.6 %collective-permute-start.5 = (bf16[128,1280]{1,0:T(8,128)(2,1)S(1)}, bf16[128,1280]{1,0:T(8,128)(2,1)S(1)}, u32[]{:S(2)}, u32[]{:S(2)}) collective-permute-start(bf16[128,1280]{1,0:T(8,128)(2,1)S(1)} %get-tuple-element.11.refs_1_), channel_id=1, source_target_pairs={{0,2},{2,0},{4,6},{6,4},{1,3},{3,1},{5,7},{7,5},{8,10},{10,8},{12,... | collective-permute-start | bytes 983048 | tf_op jit(solution)/shard_map/ppermute | solution.py:222
  22.1 2.6 %collective-permute-start.4 = (bf16[8,64,128]{2,1,0:T(8,128)(2,1)S(1)}, bf16[8,64,128]{2,1,0:T(8,128)(2,1)S(1)}, u32[]{:S(2)}, u32[]{:S(2)}) collective-permute-start(bf16[8,64,128]{2,1,0:T(8,128)(2,1)S(1)} %get-tuple-element.10), channel_id=1, source_target_pairs={{0,6},{2,4},{4,2},{6,0},{1,7},{3,5},{5,3},{7,1},{8,14},{10,12},{12... | collective-permute-start | bytes 393224 | tf_op jit(solution)/shard_map/ppermute | solution.py:222
  24.8 0.3 collective-permute-start.3
  25.0 1.5 %collective-permute-start.2 = (bf16[8,64,128]{2,1,0:T(8,128)(2,1)S(1)}, bf16[8,64,128]{2,1,0:T(8,128)(2,1)S(1)}, u32[]{:S(2)}, u32[]{:S(2)}) collective-permute-start(bf16[8,64,128]{2,1,0:T(8,128)(2,1)S(1)} %get-tuple-element.10), channel_id=1, source_target_pairs={{0,2},{2,0},{4,6},{6,4},{1,3},{3,1},{5,7},{7,5},{8,10},{10,8},{12,... | collective-permute-start | bytes 393224 | tf_op jit(solution)/shard_map/ppermute | solution.py:222
  26.5 0.1 pad_add_fusion.at_ref
  26.6 8.8 %collective-permute-done.4.refs_2_ = bf16[8,64,128]{2,1,0:T(8,128)(2,1)S(1)} collective-permute-done((bf16[8,64,128]{2,1,0:T(8,128)(2,1)S(1)}, bf16[8,64,128]{2,1,0:T(8,128)(2,1)S(1)}, u32[]{:S(2)}, u32[]{:S(2)}) %collective-permute-start.4) | collective-permute-done | bytes 131104 | tf_op jit(solution)/shard_map/ppermute | solution.py:222
  35.4 0.0 collective-permute-done.3.refs_1_
  35.4 3.1 %collective-permute-done.2.refs_0_ = bf16[8,64,128]{2,1,0:T(8,128)(2,1)S(1)} collective-permute-done((bf16[8,64,128]{2,1,0:T(8,128)(2,1)S(1)}, bf16[8,64,128]{2,1,0:T(8,128)(2,1)S(1)}, u32[]{:S(2)}, u32[]{:S(2)}) %collective-permute-start.2) | collective-permute-done | bytes 131104 | tf_op jit(solution)/shard_map/ppermute | solution.py:222
  38.5 0.0 copy-done.2
  38.5 1.2 %shard_map.40 = bf16[256,128]{1,0:T(8,128)(2,1)S(1)} custom-call(s32[8]{0:T(128)S(1)} %copy-done.2, bf16[8,96,128]{2,1,0:T(8,128)(2,1)S(1)} %all_to_all.10.x_ref.own_ref, bf16[8,64,128]{2,1,0:T(8,128)(2,1)S(1)} %collective-permute-done.2.refs_0_, bf16[8,64,128]{2,1,0:T(8,128)(2,1)S(1)} %collective-permute-done.3.refs_1_, ...), custom_call_target="tpu_custom_call" | custom-call | tf_op jit(solution)/shard_map/pallas_call | solution.py:137
  39.7 9.2 %all-gather = bf16[1024,128]{1,0:T(8,128)(2,1)S(1)} all-gather(bf16[256,128]{1,0:T(8,128)(2,1)S(1)} %shard_map.40), channel_id=2, replica_groups=mesh['blk'=4,'row'=4,'core'=2] {'blk'}, dimensions={0}, use_global_device_ids=true | all-gather | bytes 327680 | tf_op jit(solution)/shard_map/all_gather | solution.py:248
  49.0 0.0 collective-permute-done.5.refs_3_
  49.0 1.2 %shard_map.41 = (bf16[8,32,640]{2,1,0:T(8,128)(2,1)S(1)}, bf16[8,32,640]{2,1,0:T(8,128)(2,1)S(1)}) custom-call(s32[4]{0:T(128)S(1)} %pad_add_fusion.at_ref, s32[1]{0:T(128)} %bitcast.4.core_ref, bf16[4,256,128]{2,1,0:T(8,128)(2,1)S(1)} %bitcast.7, bf16[128,1280]{1,0:T(8,128)(2,1)S(1)} %shard_map.38.refs_0_, bf16[128,1280]{1,0:T(8,128)(2,1)S(1)} %get-tuple-element.11.refs_1_, ...), custom_call_target="tpu_custom_call" | custom-call | tf_op jit(solution)/shard_map/pallas_call | solution.py:176
  50.2 0.1 collective-permute-start.6
  50.3 1.6 %collective-permute-done.6.y_ref = bf16[8,32,640]{2,1,0:T(8,128)(2,1)S(1)} collective-permute-done((bf16[8,32,640]{2,1,0:T(8,128)(2,1)S(1)}, bf16[8,32,640]{2,1,0:T(8,128)(2,1)S(1)}, u32[]{:S(2)}, u32[]{:S(2)}) %collective-permute-start.6) | collective-permute-done | bytes 327712 | tf_op jit(solution)/shard_map/ppermute | solution.py:222
  51.9 0.1 shard_map.42
  52.0 10.2 %all_to_all.11.x_ref = bf16[8,32,640]{2,1,0:T(8,128)(2,1)S(1)} all-to-all(bf16[8,32,640]{2,1,0:T(8,128)(2,1)S(1)} %shard_map.42), channel_id=1, replica_groups=mesh['blk'=4,'row'=4,'core'=2] {'blk','core'}, dimensions={0} | all-to-all | bytes 655360 | tf_op jit(solution)/shard_map/all_to_all | solution.py:226
  62.1 0.8 %shard_map.43 = bf16[32,5120]{1,0:T(8,128)(2,1)} custom-call(bf16[8,32,640]{2,1,0:T(8,128)(2,1)S(1)} %all_to_all.11.x_ref), custom_call_target="tpu_custom_call" | custom-call | tf_op jit(solution)/shard_map/pallas_call | solution.py:212
  (3 shorter events, 0.1 us)
Async XLA Ops:
  0.0 1.3 %copy-start = (bf16[128,5120]{1,0:T(8,128)(2,1)S(1)}, bf16[128,5120]{1,0:T(8,128)(2,1)}, u32[]{:S(2)}) copy-start(bf16[128,5120]{1,0:T(8,128)(2,1)} %x_ref.3) | copy-start | bytes 3932164
  1.3 5.6 %copy-start.1 = (bf16[3,32,1024]{2,1,0:T(8,128)(2,1)S(1)}, bf16[3,32,1024]{2,1,0:T(8,128)(2,1)}, u32[]{:S(2)}) copy-start(bf16[3,32,1024]{2,1,0:T(8,128)(2,1)} %x_ref.2) | copy-start | bytes 589828
  1.3 37.2 %copy-start.2 = (s32[8]{0:T(128)S(1)}, s32[8]{0:T(128)}, u32[]{:S(2)}) copy-start(s32[8]{0:T(128)} %clip_ref.1) | copy-start | bytes 100
  1.3 15.4 %collective-permute-start.1 = (bf16[128,1280]{1,0:T(8,128)(2,1)S(1)}, bf16[128,1280]{1,0:T(8,128)(2,1)S(1)}, u32[]{:S(2)}, u32[]{:S(2)}) collective-permute-start(bf16[128,1280]{1,0:T(8,128)(2,1)S(1)} %shard_map.38.refs_0_), channel_id=1, source_target_pairs={{0,2},{2,0},{4,6},{6,4},{1,3},{3,1},{5,7},{7,5},{8,10},{10,8},{12,... | collective-permute-start | bytes 983048 | tf_op jit(solution)/shard_map/ppermute | solution.py:222
  4.4 17.0 %collective-permute-start = (bf16[128,1280]{1,0:T(8,128)(2,1)S(1)}, bf16[128,1280]{1,0:T(8,128)(2,1)S(1)}, u32[]{:S(2)}, u32[]{:S(2)}) collective-permute-start(bf16[128,1280]{1,0:T(8,128)(2,1)S(1)} %shard_map.38.refs_0_), channel_id=1, source_target_pairs={{0,6},{2,4},{4,2},{6,0},{1,7},{3,5},{5,3},{7,1},{8,14},{10,12},{12... | collective-permute-start | bytes 983048 | tf_op jit(solution)/shard_map/ppermute | solution.py:222
  21.5 27.5 %collective-permute-start.5 = (bf16[128,1280]{1,0:T(8,128)(2,1)S(1)}, bf16[128,1280]{1,0:T(8,128)(2,1)S(1)}, u32[]{:S(2)}, u32[]{:S(2)}) collective-permute-start(bf16[128,1280]{1,0:T(8,128)(2,1)S(1)} %get-tuple-element.11.refs_1_), channel_id=1, source_target_pairs={{0,2},{2,0},{4,6},{6,4},{1,3},{3,1},{5,7},{7,5},{8,10},{10,8},{12,... | collective-permute-start | bytes 983048 | tf_op jit(solution)/shard_map/ppermute | solution.py:222
  22.1 13.3 %collective-permute-start.4 = (bf16[8,64,128]{2,1,0:T(8,128)(2,1)S(1)}, bf16[8,64,128]{2,1,0:T(8,128)(2,1)S(1)}, u32[]{:S(2)}, u32[]{:S(2)}) collective-permute-start(bf16[8,64,128]{2,1,0:T(8,128)(2,1)S(1)} %get-tuple-element.10), channel_id=1, source_target_pairs={{0,6},{2,4},{4,2},{6,0},{1,7},{3,5},{5,3},{7,1},{8,14},{10,12},{12... | collective-permute-start | bytes 393224 | tf_op jit(solution)/shard_map/ppermute | solution.py:222
  24.8 10.6 %collective-permute-start.3 = (bf16[8,64,128]{2,1,0:T(8,128)(2,1)S(1)}, bf16[8,64,128]{2,1,0:T(8,128)(2,1)S(1)}, u32[]{:S(2)}, u32[]{:S(2)}) collective-permute-start(bf16[8,64,128]{2,1,0:T(8,128)(2,1)S(1)} %get-tuple-element.10), channel_id=1, source_target_pairs={{0,4},{2,6},{4,0},{6,2},{1,5},{3,7},{5,1},{7,3},{8,12},{10,14},{12... | collective-permute-start | bytes 393224 | tf_op jit(solution)/shard_map/ppermute | solution.py:222
  25.0 13.5 %collective-permute-start.2 = (bf16[8,64,128]{2,1,0:T(8,128)(2,1)S(1)}, bf16[8,64,128]{2,1,0:T(8,128)(2,1)S(1)}, u32[]{:S(2)}, u32[]{:S(2)}) collective-permute-start(bf16[8,64,128]{2,1,0:T(8,128)(2,1)S(1)} %get-tuple-element.10), channel_id=1, source_target_pairs={{0,2},{2,0},{4,6},{6,4},{1,3},{3,1},{5,7},{7,5},{8,10},{10,8},{12,... | collective-permute-start | bytes 393224 | tf_op jit(solution)/shard_map/ppermute | solution.py:222
  50.2 1.7 %collective-permute-start.6 = (bf16[8,32,640]{2,1,0:T(8,128)(2,1)S(1)}, bf16[8,32,640]{2,1,0:T(8,128)(2,1)S(1)}, u32[]{:S(2)}, u32[]{:S(2)}) collective-permute-start(bf16[8,32,640]{2,1,0:T(8,128)(2,1)S(1)} %get-tuple-element.14), channel_id=1, source_target_pairs={{0,1},{1,0},{2,3},{3,2},{4,5},{5,4},{6,7},{7,6},{8,9},{9,8},{10,11... | collective-permute-start | bytes 983048 | tf_op jit(solution)/shard_map/ppermute | solution.py:222

commit v6 on v5

v6 whole, which is shorter than its diff:
```python
import functools
import math

import jax
import jax.numpy as jnp
from jax import lax
from jax.experimental import pallas as pl
from jax.experimental.pallas import tpu as pltpu
from jax.sharding import Mesh
from jax.sharding import PartitionSpec as P

FRB = 2
TPF = 16
ALL = ("blk", "row", "core")
PLANE = ("blk", "core")
VMEM = pl.BlockSpec(memory_space=pltpu.VMEM)
SMEM = pl.BlockSpec(memory_space=pltpu.SMEM)
ANY = pl.BlockSpec(memory_space=pl.ANY)
PARAMS = pltpu.CompilerParams(vmem_limit_bytes=48 * 1024 * 1024)


def pack_kernel(head_dim, at_ref, x_ref, *out_refs):
    kinds, tok, _ = x_ref.shape
    heads = out_refs[0].shape[1] // head_dim
    for m, out_ref in enumerate(out_refs):
        place = at_ref[0] ^ m
        for i in range(heads):
            head = (place // 2 * heads + i) * 2 + place % 2
            cols = pl.ds(pl.multiple_of(head * head_dim, head_dim), head_dim)
            for k in range(kinds):
                out_ref[k * tok:(k + 1) * tok, i * head_dim:(i + 1) * head_dim] = x_ref[k, :, cols]


def pack(x, place, peers, head_dim):
    kinds, tok, cols = x.shape
    like = jax.ShapeDtypeStruct((kinds * tok, cols // peers), x.dtype)
    return pl.pallas_call(
        functools.partial(pack_kernel, head_dim),
        out_shape=[like] * peers,
        in_specs=[SMEM, VMEM],
        out_specs=[VMEM] * peers,
        compiler_params=PARAMS,
    )(place, x)


def columns_kernel(at_ref, x_ref, out_ref, sem):
    cols = out_ref.shape[1]
    start = pl.multiple_of(at_ref[0] * cols, cols)
    copy = pltpu.make_async_copy(x_ref.at[:, pl.ds(start, cols)], out_ref, sem)
    copy.start()
    copy.wait()


def columns(x, at, parts):
    depth, cols = x.shape
    return pl.pallas_call(
        columns_kernel,
        out_shape=jax.ShapeDtypeStruct((depth, cols // parts), x.dtype),
        in_specs=[SMEM, pl.BlockSpec(memory_space=pltpu.HBM)],
        out_specs=VMEM,
        scratch_shapes=[pltpu.SemaphoreType.DMA],
        compiler_params=PARAMS,
    )(at, x)


def sort_kernel(at_ref, *refs):
    *in_refs, q_ref, kv_ref = refs
    tok = q_ref.shape[1]
    for m, ref in enumerate(in_refs):
        place = at_ref[0] ^ m
        q_ref[place] = ref[0:tok, :]
        kv_ref[place] = ref[tok:, :]


def sort(parts, place):
    depth, width = parts[0].shape
    tok, peers = depth // 3, len(parts)
    return pl.pallas_call(
        sort_kernel,
        out_shape=(
            jax.ShapeDtypeStruct((peers, tok, width), parts[0].dtype),
            jax.ShapeDtypeStruct((peers, 2 * tok, width), parts[0].dtype),
        ),
        in_specs=[SMEM] + [VMEM] * peers,
        out_specs=(VMEM, VMEM),
        compiler_params=PARAMS,
    )(place, *parts)


def clip_of(token, blk_tokens, tok_dev, clip_ref):
    frame = token // blk_tokens * FRB + token % tok_dev // TPF
    clip = jnp.zeros_like(token)
    for f in range(clip_ref.shape[0]):
        clip = jnp.where(frame == f, clip_ref[f], clip)
    return clip


def attention_kernel(head_dim, n_kv, clip_ref, q_ref, *refs):
    kv_refs, out_ref = refs[:n_kv], refs[(len(refs) + n_kv) // 2]
    peers, tok, width = q_ref.shape
    count = peers * tok
    scale = 1.0 / math.sqrt(head_dim)
    row_clip = clip_of(
        lax.broadcasted_iota(jnp.int32, (count, 1), 0), 2 * tok, tok, clip_ref
    )
    col_clip = clip_of(
        lax.broadcasted_iota(jnp.int32, (1, count), 1), 2 * tok, tok, clip_ref
    )
    allowed = row_clip == col_clip
    per_step = max(1, 1024 // count)
    for h in range(width // head_dim):
        cols = slice(h * head_dim, (h + 1) * head_dim)
        queries = q_ref[:, :, cols].reshape(count, head_dim)
        top = total = acc = None
        for first in range(0, n_kv, per_step):
            scores, values = [], []
            for ref in kv_refs[first:first + per_step]:
                keys = ref[:, 0:tok, cols].reshape(count, head_dim)
                values.append(ref[:, tok:2 * tok, cols].reshape(count, head_dim))
                s = lax.dot_general(
                    queries, keys, (((1,), (1,)), ((), ())), preferred_element_type=jnp.float32
                )
                scores.append(jnp.where(allowed, s * scale, -1e30))
            new_top = functools.reduce(
                jnp.maximum, [jnp.max(s, axis=1, keepdims=True) for s in scores]
            )
            if top is not None:
                new_top = jnp.maximum(top, new_top)
                factor = jnp.exp(top - new_top)
                total, acc = total * factor, acc * factor
            top = new_top
            for s, v in zip(scores, values):
                p = jnp.where(allowed, jnp.exp(s - top), 0.0)
                part = jnp.sum(p, axis=1, keepdims=True)
                dot = jnp.dot(p.astype(jnp.bfloat16), v, preferred_element_type=jnp.float32)
                total = part if total is None else total + part
                acc = dot if acc is None else acc + dot
        out_ref[:, cols] = (acc / total).astype(out_ref.dtype)


def attention(q, kvs, frame_clip, head_dim, passed):
    peers, tok, width = q.shape
    like = jax.ShapeDtypeStruct((peers * tok, width), q.dtype)
    attn, *same = pl.pallas_call(
        functools.partial(attention_kernel, head_dim, len(kvs)),
        out_shape=[like] + [jax.ShapeDtypeStruct(x.shape, x.dtype) for x in passed],
        in_specs=[SMEM] + [VMEM] * (1 + len(kvs)) + [ANY] * len(passed),
        out_specs=[VMEM] + [ANY] * len(passed),
        input_output_aliases={2 + len(kvs) + i: 1 + i for i in range(len(passed))},
        compiler_params=PARAMS,
    )(frame_clip, q, *kvs, *passed)
    return attn, same


def project_kernel(n_attn, at_ref, place_ref, *refs):
    attn_refs, w_refs = refs[:n_attn], refs[n_attn:-3]
    mine_ref, theirs_ref, a_ref = refs[-3:]
    width = attn_refs[0].shape[1]
    head_dim, _ = w_refs[0].shape
    blks, tok, cols = mine_ref.shape
    blk, core = place_ref[0] // 2, place_ref[0] % 2
    for k, ref in enumerate(attn_refs):
        a_ref[:, pl.ds(pl.multiple_of((blk ^ k) * width, width), width)] = ref[...]
    result = None
    for i in range(0, len(w_refs), 2):
        left = [
            a_ref[:, pl.ds(pl.multiple_of(at_ref[j] * head_dim, head_dim), head_dim)]
            for j in (i, i + 1)
        ]
        right = [w_refs[j][...] for j in (i, i + 1)]
        part = jnp.dot(
            jnp.concatenate(left, axis=1), jnp.concatenate(right, axis=0),
            preferred_element_type=jnp.float32,
        )
        result = part if result is None else result + part
    result = result.astype(mine_ref.dtype).reshape(blks, 2, tok, cols)

    @pl.when(core == 0)
    def _():
        mine_ref[...] = result[:, 0]
        theirs_ref[...] = result[:, 1]

    @pl.when(core != 0)
    def _():
        mine_ref[...] = result[:, 1]
        theirs_ref[...] = result[:, 0]


def project(attns, w_parts, at, place, tok):
    count, width = attns[0].shape
    blks, cols = len(attns), w_parts[0].shape[1]
    like = jax.ShapeDtypeStruct((blks, tok, cols), attns[0].dtype)
    return pl.pallas_call(
        functools.partial(project_kernel, blks),
        out_shape=(like, like),
        in_specs=[SMEM, SMEM] + [VMEM] * (blks + len(w_parts)),
        out_specs=(VMEM, VMEM),
        scratch_shapes=[pltpu.VMEM((count, blks * width), attns[0].dtype)],
        compiler_params=PARAMS,
    )(at, place, *attns, *w_parts)


def add_kernel(place_ref, x_ref, y_ref, *out_refs):
    for k, out_ref in enumerate(out_refs):
        at = place_ref[0] // 2 ^ k
        both = x_ref[at].astype(jnp.float32) + y_ref[at].astype(jnp.float32)
        out_ref[...] = both.astype(out_ref.dtype)


def add(x, y, place):
    blks = x.shape[0]
    return pl.pallas_call(
        add_kernel,
        out_shape=[jax.ShapeDtypeStruct(x.shape[1:], x.dtype)] * blks,
        in_specs=[SMEM, VMEM, VMEM],
        out_specs=[VMEM] * blks,
        compiler_params=PARAMS,
    )(place, x, y)


def unpack_kernel(place_ref, *refs):
    *in_refs, out_ref = refs
    width = in_refs[0].shape[1]
    for k, ref in enumerate(in_refs):
        at = place_ref[0] // 2 ^ k
        out_ref[:, pl.ds(pl.multiple_of(at * width, width), width)] = ref[...]


def unpack(parts, place):
    tok, width = parts[0].shape
    return pl.pallas_call(
        unpack_kernel,
        out_shape=jax.ShapeDtypeStruct((tok, len(parts) * width), parts[0].dtype),
        in_specs=[SMEM] + [VMEM] * len(parts),
        out_specs=VMEM,
        compiler_params=PARAMS,
    )(place, *parts)


def xor(x, axis, by):
    size = math.prod(lax.axis_size(name) for name in axis)
    return lax.ppermute(x, axis, [(i, i ^ by) for i in range(size)])


def swap_all(parts, axis):
    return [parts[0]] + [xor(x, axis, m) for m, x in enumerate(parts) if m]


def on_device(qkv, frame_clip, w_out):
    rows, blks = lax.axis_size("row"), lax.axis_size("blk")
    row = lax.axis_index("row")
    tok = qkv.shape[1]
    head_dim = w_out.shape[0]
    blk = lax.axis_index("blk").astype(jnp.int32).reshape(1)
    place = blk * 2 + lax.axis_index("core").astype(jnp.int32)

    w_own = columns(w_out, blk, blks)
    half = rows == 4
    steps = [rows - 1] + list(range(1, 2 if half else rows - 1))
    w_others = [xor(w_own, ("row",), by) for by in steps]

    q, kv = sort(swap_all(pack(qkv, place, 2 * blks, head_dim), PLANE), place)
    kvs = [kv] + [xor(kv, ("row",), by) for by in range(1, rows)]
    attn, w_others = attention(q, kvs, frame_clip, head_dim, w_others)
    if half:
        steps.append(2)
        w_others.append(xor(w_others[0], ("row",), 1))
    attns = swap_all([attn] * blks, ("blk",))
    at = jnp.stack([row] + [row ^ by for by in steps]).astype(jnp.int32)
    mine, theirs = project(attns, [w_own] + w_others, at, place, tok)
    parts = add(mine, xor(theirs, ("core",), 1), place)
    return unpack(swap_all(parts, ("blk",)), place)


def solution(mesh):
    blk, tile = mesh.shape["blk"], mesh.shape["tile"]
    fine = Mesh(mesh.devices.reshape(blk, tile // 2, 2), ALL)
    in_specs = (P(None, ALL, None), P(), P(("row", "core"), None))
    return jax.shard_map(
        on_device, mesh=fine, in_specs=in_specs, out_specs=P(ALL, None), check_vma=False
    )
```

time: 63.1 us -> 56 us (0.89)
  blocking collectives: 29.2 us -> 0 us
  starting transfers between devices: 10.7 us -> 24.4 us
  waiting for transfers between devices: 18.3 us -> 26.6 us
    all_to_all x2 -> x0, blocking collectives: 19.9 us -> none  [exchange(): return lax.all_to_all(x, axis, split_axis=0, concat_axis=0, tiled=True)]
    ppermute x7 -> x20, starting transfers between devices: 10.7 us -> 24.4 us  [xor(): return lax.ppermute(x, axis, [(i, i ^ by) for i in range(size)])]
    all_gather x1 -> x0, blocking collectives: 9.23 us -> none  [on_device(): attn_all = lax.all_gather(attn, 'blk', axis=0, tiled=False)]
    ppermute x7 -> x20, waiting for transfers between devices: 18.3 us -> 26.6 us  [xor(): return lax.ppermute(x, axis, [(i, i ^ by) for i in range(size)])]
  transfers between devices with their start and end apart: 7 -> 20, of which waited for: 4 -> 14; matrix products, arithmetic and copies ran while one was open for 0% -> 0% of each run, Pallas kernels for 2% -> 0%
where the time goes in v6:
time: 56 us; the launch traced here: 55.9 us
  waiting for transfers between devices  26.6 us (48%)
  starting transfers between devices  24.4 us (44%)
  Pallas kernels  3.34 us (6%)
  local copies, waits for them, and re-layouts  1.34 us (2%)
    ppermute x20, waiting for transfers between devices, xor(): return lax.ppermute(x, axis, [(i, i ^ by) for i in range(size)])  26.6 us
    ppermute x20, starting transfers between devices, xor(): return lax.ppermute(x, axis, [(i, i ^ by) for i in range(size)])  24.4 us
    unnamed x6, local copies, waits for them, and re-layouts  1.34 us
    pallas_call x1, Pallas kernels, attention(): pl.pallas_call(functools.partial(attention_kernel, head_dim, len(kvs)), o...  1.25 us
    pallas_call x1, Pallas kernels, project(): pl.pallas_call(functools.partial(project_kernel, blks), out_shape=(like,...  1.14 us
  transfers between devices with their start and end apart: 20, of which 14 were waited for; matrix products, arithmetic and copies ran while one was open for 0% of the time, Pallas kernels for 0%

profile of v6, /device:TPU:0, one launch (start us, length us, event | category | flops | bytes accessed | tf_op | source)
XLA Modules:
  0.0 55.9 jit_solution(16747390637617525281)
XLA Ops:
  0.0 0.0 copy-start.2
  0.0 0.0 copy-start
  0.0 1.3 %copy-done = bf16[128,5120]{1,0:T(8,128)(2,1)S(1)} copy-done((bf16[128,5120]{1,0:T(8,128)(2,1)S(1)}, bf16[128,5120]{1,0:T(8,128)(2,1)}, u32[]{:S(2)}) %copy-start) | copy-done | bytes 1310744
  1.3 0.0 copy-start.1
  1.4 3.1 %collective-permute-start.11 = (bf16[128,1280]{1,0:T(8,128)(2,1)S(1)}, bf16[128,1280]{1,0:T(8,128)(2,1)S(1)}, u32[]{:S(2)}, u32[]{:S(2)}) collective-permute-start(bf16[128,1280]{1,0:T(8,128)(2,1)S(1)} %shard_map.39.refs_4_), channel_id=1, source_target_pairs={{0,2},{2,0},{4,6},{6,4},{1,3},{3,1},{5,7},{7,5},{8,10},{10,8},{12,... | collective-permute-start | bytes 983048 | tf_op jit(solution)/shard_map/ppermute | solution.py:242
  4.5 2.5 %collective-permute-start.10 = (bf16[128,1280]{1,0:T(8,128)(2,1)S(1)}, bf16[128,1280]{1,0:T(8,128)(2,1)S(1)}, u32[]{:S(2)}, u32[]{:S(2)}) collective-permute-start(bf16[128,1280]{1,0:T(8,128)(2,1)S(1)} %shard_map.39.refs_4_), channel_id=1, source_target_pairs={{0,6},{2,4},{4,2},{6,0},{1,7},{3,5},{5,3},{7,1},{8,14},{10,12},{12... | collective-permute-start | bytes 983048 | tf_op jit(solution)/shard_map/ppermute | solution.py:242
  6.9 0.0 copy-done.1
  6.9 0.1 shard_map.37
  7.0 0.1 collective-permute-start
  7.1 1.6 %collective-permute-start.1 = (bf16[96,128]{1,0:T(8,128)(2,1)S(1)}, bf16[96,128]{1,0:T(8,128)(2,1)S(1)}, u32[]{:S(2)}, u32[]{:S(2)}) collective-permute-start(bf16[96,128]{1,0:T(8,128)(2,1)S(1)} %get-tuple-element.26), channel_id=1, source_target_pairs={{0,8},{1,9},{8,0},{9,1},{16,24},{17,25},{24,16},{25,17},{2,10},{3,... | collective-permute-start | bytes 73736 | tf_op jit(solution)/shard_map/ppermute | solution.py:242
  8.7 0.3 collective-permute-start.2
  9.0 0.0 collective-permute-done.refs_1_
  9.0 1.5 %collective-permute-start.3 = (bf16[96,128]{1,0:T(8,128)(2,1)S(1)}, bf16[96,128]{1,0:T(8,128)(2,1)S(1)}, u32[]{:S(2)}, u32[]{:S(2)}) collective-permute-start(bf16[96,128]{1,0:T(8,128)(2,1)S(1)} %get-tuple-element.28), channel_id=1, source_target_pairs={{0,16},{1,17},{8,24},{9,25},{16,0},{17,1},{24,8},{25,9},{2,18},{3,... | collective-permute-start | bytes 73736 | tf_op jit(solution)/shard_map/ppermute | solution.py:242
  10.5 0.5 collective-permute-done.1.refs_2_
  11.0 0.7 %collective-permute-start.4 = (bf16[96,128]{1,0:T(8,128)(2,1)S(1)}, bf16[96,128]{1,0:T(8,128)(2,1)S(1)}, u32[]{:S(2)}, u32[]{:S(2)}) collective-permute-start(bf16[96,128]{1,0:T(8,128)(2,1)S(1)} %get-tuple-element.29), channel_id=1, source_target_pairs={{0,17},{1,16},{8,25},{9,24},{16,1},{17,0},{24,9},{25,8},{2,19},{3,... | collective-permute-start | bytes 73736 | tf_op jit(solution)/shard_map/ppermute | solution.py:242
  11.7 0.2 collective-permute-done.2.refs_3_
  11.9 1.8 %collective-permute-start.5 = (bf16[96,128]{1,0:T(8,128)(2,1)S(1)}, bf16[96,128]{1,0:T(8,128)(2,1)S(1)}, u32[]{:S(2)}, u32[]{:S(2)}) collective-permute-start(bf16[96,128]{1,0:T(8,128)(2,1)S(1)} %get-tuple-element.30), channel_id=1, source_target_pairs={{0,24},{1,25},{8,16},{9,17},{16,8},{17,9},{24,0},{25,1},{2,26},{3,... | collective-permute-start | bytes 73736 | tf_op jit(solution)/shard_map/ppermute | solution.py:242
  13.7 0.0 collective-permute-done.3.refs_4_
  13.7 1.2 %collective-permute-start.6 = (bf16[96,128]{1,0:T(8,128)(2,1)S(1)}, bf16[96,128]{1,0:T(8,128)(2,1)S(1)}, u32[]{:S(2)}, u32[]{:S(2)}) collective-permute-start(bf16[96,128]{1,0:T(8,128)(2,1)S(1)} %get-tuple-element.31), channel_id=1, source_target_pairs={{0,25},{1,24},{8,17},{9,16},{16,9},{17,8},{24,1},{25,0},{2,27},{3,... | collective-permute-start | bytes 73736 | tf_op jit(solution)/shard_map/ppermute | solution.py:242
  14.9 0.0 collective-permute-done.4.refs_5_
  14.9 1.8 %collective-permute-done.5.refs_6_ = bf16[96,128]{1,0:T(8,128)(2,1)S(1)} collective-permute-done((bf16[96,128]{1,0:T(8,128)(2,1)S(1)}, bf16[96,128]{1,0:T(8,128)(2,1)S(1)}, u32[]{:S(2)}, u32[]{:S(2)}) %collective-permute-start.5) | collective-permute-done | bytes 24608 | tf_op jit(solution)/shard_map/ppermute | solution.py:242
  16.6 1.2 %collective-permute-done.6.refs_7_ = bf16[96,128]{1,0:T(8,128)(2,1)S(1)} collective-permute-done((bf16[96,128]{1,0:T(8,128)(2,1)S(1)}, bf16[96,128]{1,0:T(8,128)(2,1)S(1)}, u32[]{:S(2)}, u32[]{:S(2)}) %collective-permute-start.6) | collective-permute-done | bytes 24608 | tf_op jit(solution)/shard_map/ppermute | solution.py:242
  17.8 1.4 %collective-permute-start.9 = (bf16[8,64,128]{2,1,0:T(8,128)(2,1)S(1)}, bf16[8,64,128]{2,1,0:T(8,128)(2,1)S(1)}, u32[]{:S(2)}, u32[]{:S(2)}) collective-permute-start(bf16[8,64,128]{2,1,0:T(8,128)(2,1)S(1)} %get-tuple-element.33.refs_0_), channel_id=1, source_target_pairs={{0,6},{2,4},{4,2},{6,0},{1,7},{3,5},{5,3},{7,1},{8,14},{10,12},{12... | collective-permute-start | bytes 393224 | tf_op jit(solution)/shard_map/ppermute | solution.py:242
  19.3 0.8 %collective-permute-start.8 = (bf16[8,64,128]{2,1,0:T(8,128)(2,1)S(1)}, bf16[8,64,128]{2,1,0:T(8,128)(2,1)S(1)}, u32[]{:S(2)}, u32[]{:S(2)}) collective-permute-start(bf16[8,64,128]{2,1,0:T(8,128)(2,1)S(1)} %get-tuple-element.33.refs_0_), channel_id=1, source_target_pairs={{0,4},{2,6},{4,0},{6,2},{1,5},{3,7},{5,1},{7,3},{8,12},{10,14},{12... | collective-permute-start | bytes 393224 | tf_op jit(solution)/shard_map/ppermute | solution.py:242
  20.1 2.2 %collective-permute-start.7 = (bf16[8,64,128]{2,1,0:T(8,128)(2,1)S(1)}, bf16[8,64,128]{2,1,0:T(8,128)(2,1)S(1)}, u32[]{:S(2)}, u32[]{:S(2)}) collective-permute-start(bf16[8,64,128]{2,1,0:T(8,128)(2,1)S(1)} %get-tuple-element.33.refs_0_), channel_id=1, source_target_pairs={{0,2},{2,0},{4,6},{6,4},{1,3},{3,1},{5,7},{7,5},{8,10},{10,8},{12,... | collective-permute-start | bytes 393224 | tf_op jit(solution)/shard_map/ppermute | solution.py:242
  22.3 3.9 %collective-permute-done.9.refs_3_ = bf16[8,64,128]{2,1,0:T(8,128)(2,1)S(1)} collective-permute-done((bf16[8,64,128]{2,1,0:T(8,128)(2,1)S(1)}, bf16[8,64,128]{2,1,0:T(8,128)(2,1)S(1)}, u32[]{:S(2)}, u32[]{:S(2)}) %collective-permute-start.9) | collective-permute-done | bytes 131104 | tf_op jit(solution)/shard_map/ppermute | solution.py:242
  26.2 6.5 %collective-permute-done.8.refs_2_ = bf16[8,64,128]{2,1,0:T(8,128)(2,1)S(1)} collective-permute-done((bf16[8,64,128]{2,1,0:T(8,128)(2,1)S(1)}, bf16[8,64,128]{2,1,0:T(8,128)(2,1)S(1)}, u32[]{:S(2)}, u32[]{:S(2)}) %collective-permute-start.8) | collective-permute-done | bytes 131104 | tf_op jit(solution)/shard_map/ppermute | solution.py:242
  32.7 0.0 collective-permute-done.7.refs_1_
  32.7 0.0 collective-permute-done.11.refs_5_
  32.8 0.0 collective-permute-done.10.refs_4_
  32.8 0.0 copy-done.2
  32.8 1.2 %shard_map.40 = (bf16[256,128]{1,0:T(8,128)(2,1)S(1)}, bf16[128,1280]{1,0:T(8,128)(2,1)S(1)}, bf16[128,1280]{1,0:T(8,128)(2,1)S(1)}) custom-call(s32[8]{0:T(128)S(1)} %copy-done.2, bf16[8,32,128]{2,1,0:T(8,128)(2,1)S(1)} %get-tuple-element.32.q_ref, bf16[8,64,128]{2,1,0:T(8,128)(2,1)S(1)} %get-tuple-element.33.refs_0_, ...), custom_call_target="tpu_custom_call", output_to_operand_aliasing={{1}: (6, {}), {2}: (7, {})} | custom-call | tf_op jit(solution)/shard_map/pallas_call | solution.py:144
  34.0 0.1 collective-permute-start.15
  34.1 2.5 %collective-permute-start.14 = (bf16[256,128]{1,0:T(8,128)(2,1)S(1)}, bf16[256,128]{1,0:T(8,128)(2,1)S(1)}, u32[]{:S(2)}, u32[]{:S(2)}) collective-permute-start(bf16[256,128]{1,0:T(8,128)(2,1)S(1)} %get-tuple-element.34.refs_0_), channel_id=1, source_target_pairs={{0,24},{8,16},{16,8},{24,0},{1,25},{9,17},{17,9},{25,1},{2,26},{10... | collective-permute-start | bytes 196616 | tf_op jit(solution)/shard_map/ppermute | solution.py:242
  36.6 0.5 collective-permute-start.13
  37.1 0.6 %collective-permute-start.12 = (bf16[256,128]{1,0:T(8,128)(2,1)S(1)}, bf16[256,128]{1,0:T(8,128)(2,1)S(1)}, u32[]{:S(2)}, u32[]{:S(2)}) collective-permute-start(bf16[256,128]{1,0:T(8,128)(2,1)S(1)} %get-tuple-element.34.refs_0_), channel_id=1, source_target_pairs={{0,8},{8,0},{16,24},{24,16},{1,9},{9,1},{17,25},{25,17},{2,10},{10... | collective-permute-start | bytes 196616 | tf_op jit(solution)/shard_map/ppermute | solution.py:242
  37.7 0.1 pad_add_fusion.at_ref
  37.7 1.6 %collective-permute-done.14.refs_3_ = bf16[256,128]{1,0:T(8,128)(2,1)S(1)} collective-permute-done((bf16[256,128]{1,0:T(8,128)(2,1)S(1)}, bf16[256,128]{1,0:T(8,128)(2,1)S(1)}, u32[]{:S(2)}, u32[]{:S(2)}) %collective-permute-start.14) | collective-permute-done | bytes 65568 | tf_op jit(solution)/shard_map/ppermute | solution.py:242
  39.4 1.5 %collective-permute-done.13.refs_2_ = bf16[256,128]{1,0:T(8,128)(2,1)S(1)} collective-permute-done((bf16[256,128]{1,0:T(8,128)(2,1)S(1)}, bf16[256,128]{1,0:T(8,128)(2,1)S(1)}, u32[]{:S(2)}, u32[]{:S(2)}) %collective-permute-start.13) | collective-permute-done | bytes 65568 | tf_op jit(solution)/shard_map/ppermute | solution.py:242
  40.8 0.5 collective-permute-done.12.refs_1_
  41.3 2.4 %collective-permute-done.15.refs_7_ = bf16[128,1280]{1,0:T(8,128)(2,1)S(1)} collective-permute-done((bf16[128,1280]{1,0:T(8,128)(2,1)S(1)}, bf16[128,1280]{1,0:T(8,128)(2,1)S(1)}, u32[]{:S(2)}, u32[]{:S(2)}) %collective-permute-start.15) | collective-permute-done | bytes 327712 | tf_op jit(solution)/shard_map/ppermute | solution.py:242
  43.7 1.1 %shard_map.41 = (bf16[4,32,1280]{2,1,0:T(8,128)(2,1)S(1)}, bf16[4,32,1280]{2,1,0:T(8,128)(2,1)S(1)}) custom-call(s32[4]{0:T(128)S(1)} %pad_add_fusion.at_ref, s32[1]{0:T(128)S(6)} %add.7.at_ref.place_ref, bf16[256,128]{1,0:T(8,128)(2,1)S(1)} %get-tuple-element.34.refs_0_, bf16[256,128]{1,0:T(8,128)(2,1)S(1)} %collective-permute-done.12.refs_1_, ...), custom_call_target="tpu_custom_call" | custom-call | tf_op jit(solution)/shard_map/pallas_call | solution.py:193
  44.9 0.1 collective-permute-start.16
  45.0 1.6 %collective-permute-done.16.y_ref = bf16[4,32,1280]{2,1,0:T(8,128)(2,1)S(1)} collective-permute-done((bf16[4,32,1280]{2,1,0:T(8,128)(2,1)S(1)}, bf16[4,32,1280]{2,1,0:T(8,128)(2,1)S(1)}, u32[]{:S(2)}, u32[]{:S(2)}) %collective-permute-start.16) | collective-permute-done | bytes 327712 | tf_op jit(solution)/shard_map/ppermute | solution.py:242
  46.6 0.1 shard_map.42
  46.7 1.6 %collective-permute-start.17 = (bf16[32,1280]{1,0:T(8,128)(2,1)S(1)}, bf16[32,1280]{1,0:T(8,128)(2,1)S(1)}, u32[]{:S(2)}, u32[]{:S(2)}) collective-permute-start(bf16[32,1280]{1,0:T(8,128)(2,1)S(1)} %get-tuple-element.40), channel_id=1, source_target_pairs={{0,8},{8,0},{16,24},{24,16},{1,9},{9,1},{17,25},{25,17},{2,10},{10... | collective-permute-start | bytes 245768 | tf_op jit(solution)/shard_map/ppermute | solution.py:242
  48.2 1.5 %collective-permute-start.18 = (bf16[32,1280]{1,0:T(8,128)(2,1)S(1)}, bf16[32,1280]{1,0:T(8,128)(2,1)S(1)}, u32[]{:S(2)}, u32[]{:S(2)}) collective-permute-start(bf16[32,1280]{1,0:T(8,128)(2,1)S(1)} %get-tuple-element.41), channel_id=1, source_target_pairs={{0,16},{8,24},{16,0},{24,8},{1,17},{9,25},{17,1},{25,9},{2,18},{10... | collective-permute-start | bytes 245768 | tf_op jit(solution)/shard_map/ppermute | solution.py:242
  49.8 0.5 collective-permute-start.19
  50.2 1.0 %collective-permute-done.17.refs_1_ = bf16[32,1280]{1,0:T(8,128)(2,1)S(1)} collective-permute-done((bf16[32,1280]{1,0:T(8,128)(2,1)S(1)}, bf16[32,1280]{1,0:T(8,128)(2,1)S(1)}, u32[]{:S(2)}, u32[]{:S(2)}) %collective-permute-start.17) | collective-permute-done | bytes 81952 | tf_op jit(solution)/shard_map/ppermute | solution.py:242
  51.2 2.3 %collective-permute-done.18.refs_2_ = bf16[32,1280]{1,0:T(8,128)(2,1)S(1)} collective-permute-done((bf16[32,1280]{1,0:T(8,128)(2,1)S(1)}, bf16[32,1280]{1,0:T(8,128)(2,1)S(1)}, u32[]{:S(2)}, u32[]{:S(2)}) %collective-permute-start.18) | collective-permute-done | bytes 81952 | tf_op jit(solution)/shard_map/ppermute | solution.py:242
  53.5 1.6 %collective-permute-done.19.refs_3_ = bf16[32,1280]{1,0:T(8,128)(2,1)S(1)} collective-permute-done((bf16[32,1280]{1,0:T(8,128)(2,1)S(1)}, bf16[32,1280]{1,0:T(8,128)(2,1)S(1)}, u32[]{:S(2)}, u32[]{:S(2)}) %collective-permute-start.19) | collective-permute-done | bytes 81952 | tf_op jit(solution)/shard_map/ppermute | solution.py:242
  55.1 0.8 %shard_map.43 = bf16[32,5120]{1,0:T(8,128)(2,1)} custom-call(s32[1]{0:T(128)S(6)} %add.7.at_ref.place_ref, bf16[32,1280]{1,0:T(8,128)(2,1)S(1)} %get-tuple-element.39.refs_0_, bf16[32,1280]{1,0:T(8,128)(2,1)S(1)} %collective-permute-done.17.refs_1_, bf16[32,1280]{1,0:T(8,128)(2,1)S(1)} %collective-permute-done.18.refs_2_, ...), custom_call_target="tpu_custom_call" | custom-call | tf_op jit(solution)/shard_map/pallas_call | solution.py:231
  (2 shorter events, 0.1 us)
Async XLA Ops:
  0.0 32.8 %copy-start.2 = (s32[8]{0:T(128)S(1)}, s32[8]{0:T(128)}, u32[]{:S(2)}) copy-start(s32[8]{0:T(128)} %clip_ref.1) | copy-start | bytes 100
  0.0 1.3 %copy-start = (bf16[128,5120]{1,0:T(8,128)(2,1)S(1)}, bf16[128,5120]{1,0:T(8,128)(2,1)}, u32[]{:S(2)}) copy-start(bf16[128,5120]{1,0:T(8,128)(2,1)} %x_ref.3) | copy-start | bytes 3932164
  1.3 5.6 %copy-start.1 = (bf16[3,32,1024]{2,1,0:T(8,128)(2,1)S(1)}, bf16[3,32,1024]{2,1,0:T(8,128)(2,1)}, u32[]{:S(2)}) copy-start(bf16[3,32,1024]{2,1,0:T(8,128)(2,1)} %x_ref.2) | copy-start | bytes 589828
  1.4 31.4 %collective-permute-start.11 = (bf16[128,1280]{1,0:T(8,128)(2,1)S(1)}, bf16[128,1280]{1,0:T(8,128)(2,1)S(1)}, u32[]{:S(2)}, u32[]{:S(2)}) collective-permute-start(bf16[128,1280]{1,0:T(8,128)(2,1)S(1)} %shard_map.39.refs_4_), channel_id=1, source_target_pairs={{0,2},{2,0},{4,6},{6,4},{1,3},{3,1},{5,7},{7,5},{8,10},{10,8},{12,... | collective-permute-start | bytes 983048 | tf_op jit(solution)/shard_map/ppermute | solution.py:242
  4.5 28.3 %collective-permute-start.10 = (bf16[128,1280]{1,0:T(8,128)(2,1)S(1)}, bf16[128,1280]{1,0:T(8,128)(2,1)S(1)}, u32[]{:S(2)}, u32[]{:S(2)}) collective-permute-start(bf16[128,1280]{1,0:T(8,128)(2,1)S(1)} %shard_map.39.refs_4_), channel_id=1, source_target_pairs={{0,6},{2,4},{4,2},{6,0},{1,7},{3,5},{5,3},{7,1},{8,14},{10,12},{12... | collective-permute-start | bytes 983048 | tf_op jit(solution)/shard_map/ppermute | solution.py:242
  7.0 1.9 %collective-permute-start = (bf16[96,128]{1,0:T(8,128)(2,1)S(1)}, bf16[96,128]{1,0:T(8,128)(2,1)S(1)}, u32[]{:S(2)}, u32[]{:S(2)}) collective-permute-start(bf16[96,128]{1,0:T(8,128)(2,1)S(1)} %get-tuple-element.25), channel_id=1, source_target_pairs={{0,1},{1,0},{8,9},{9,8},{16,17},{17,16},{24,25},{25,24},{2,3},{3,2... | collective-permute-start | bytes 73736 | tf_op jit(solution)/shard_map/ppermute | solution.py:242
  7.1 3.9 %collective-permute-start.1 = (bf16[96,128]{1,0:T(8,128)(2,1)S(1)}, bf16[96,128]{1,0:T(8,128)(2,1)S(1)}, u32[]{:S(2)}, u32[]{:S(2)}) collective-permute-start(bf16[96,128]{1,0:T(8,128)(2,1)S(1)} %get-tuple-element.26), channel_id=1, source_target_pairs={{0,8},{1,9},{8,0},{9,1},{16,24},{17,25},{24,16},{25,17},{2,10},{3,... | collective-permute-start | bytes 73736 | tf_op jit(solution)/shard_map/ppermute | solution.py:242
  8.7 3.3 %collective-permute-start.2 = (bf16[96,128]{1,0:T(8,128)(2,1)S(1)}, bf16[96,128]{1,0:T(8,128)(2,1)S(1)}, u32[]{:S(2)}, u32[]{:S(2)}) collective-permute-start(bf16[96,128]{1,0:T(8,128)(2,1)S(1)} %get-tuple-element.27), channel_id=1, source_target_pairs={{0,9},{1,8},{8,1},{9,0},{16,25},{17,24},{24,17},{25,16},{2,11},{3,... | collective-permute-start | bytes 73736 | tf_op jit(solution)/shard_map/ppermute | solution.py:242
  9.0 4.7 %collective-permute-start.3 = (bf16[96,128]{1,0:T(8,128)(2,1)S(1)}, bf16[96,128]{1,0:T(8,128)(2,1)S(1)}, u32[]{:S(2)}, u32[]{:S(2)}) collective-permute-start(bf16[96,128]{1,0:T(8,128)(2,1)S(1)} %get-tuple-element.28), channel_id=1, source_target_pairs={{0,16},{1,17},{8,24},{9,25},{16,0},{17,1},{24,8},{25,9},{2,18},{3,... | collective-permute-start | bytes 73736 | tf_op jit(solution)/shard_map/ppermute | solution.py:242
  11.0 3.9 %collective-permute-start.4 = (bf16[96,128]{1,0:T(8,128)(2,1)S(1)}, bf16[96,128]{1,0:T(8,128)(2,1)S(1)}, u32[]{:S(2)}, u32[]{:S(2)}) collective-permute-start(bf16[96,128]{1,0:T(8,128)(2,1)S(1)} %get-tuple-element.29), channel_id=1, source_target_pairs={{0,17},{1,16},{8,25},{9,24},{16,1},{17,0},{24,9},{25,8},{2,19},{3,... | collective-permute-start | bytes 73736 | tf_op jit(solution)/shard_map/ppermute | solution.py:242
  11.9 4.7 %collective-permute-start.5 = (bf16[96,128]{1,0:T(8,128)(2,1)S(1)}, bf16[96,128]{1,0:T(8,128)(2,1)S(1)}, u32[]{:S(2)}, u32[]{:S(2)}) collective-permute-start(bf16[96,128]{1,0:T(8,128)(2,1)S(1)} %get-tuple-element.30), channel_id=1, source_target_pairs={{0,24},{1,25},{8,16},{9,17},{16,8},{17,9},{24,0},{25,1},{2,26},{3,... | collective-permute-start | bytes 73736 | tf_op jit(solution)/shard_map/ppermute | solution.py:242
  13.7 4.2 %collective-permute-start.6 = (bf16[96,128]{1,0:T(8,128)(2,1)S(1)}, bf16[96,128]{1,0:T(8,128)(2,1)S(1)}, u32[]{:S(2)}, u32[]{:S(2)}) collective-permute-start(bf16[96,128]{1,0:T(8,128)(2,1)S(1)} %get-tuple-element.31), channel_id=1, source_target_pairs={{0,25},{1,24},{8,17},{9,16},{16,9},{17,8},{24,1},{25,0},{2,27},{3,... | collective-permute-start | bytes 73736 | tf_op jit(solution)/shard_map/ppermute | solution.py:242
  17.8 8.4 %collective-permute-start.9 = (bf16[8,64,128]{2,1,0:T(8,128)(2,1)S(1)}, bf16[8,64,128]{2,1,0:T(8,128)(2,1)S(1)}, u32[]{:S(2)}, u32[]{:S(2)}) collective-permute-start(bf16[8,64,128]{2,1,0:T(8,128)(2,1)S(1)} %get-tuple-element.33.refs_0_), channel_id=1, source_target_pairs={{0,6},{2,4},{4,2},{6,0},{1,7},{3,5},{5,3},{7,1},{8,14},{10,12},{12... | collective-permute-start | bytes 393224 | tf_op jit(solution)/shard_map/ppermute | solution.py:242
  19.3 13.5 %collective-permute-start.8 = (bf16[8,64,128]{2,1,0:T(8,128)(2,1)S(1)}, bf16[8,64,128]{2,1,0:T(8,128)(2,1)S(1)}, u32[]{:S(2)}, u32[]{:S(2)}) collective-permute-start(bf16[8,64,128]{2,1,0:T(8,128)(2,1)S(1)} %get-tuple-element.33.refs_0_), channel_id=1, source_target_pairs={{0,4},{2,6},{4,0},{6,2},{1,5},{3,7},{5,1},{7,3},{8,12},{10,14},{12... | collective-permute-start | bytes 393224 | tf_op jit(solution)/shard_map/ppermute | solution.py:242
  20.1 12.7 %collective-permute-start.7 = (bf16[8,64,128]{2,1,0:T(8,128)(2,1)S(1)}, bf16[8,64,128]{2,1,0:T(8,128)(2,1)S(1)}, u32[]{:S(2)}, u32[]{:S(2)}) collective-permute-start(bf16[8,64,128]{2,1,0:T(8,128)(2,1)S(1)} %get-tuple-element.33.refs_0_), channel_id=1, source_target_pairs={{0,2},{2,0},{4,6},{6,4},{1,3},{3,1},{5,7},{7,5},{8,10},{10,8},{12,... | collective-permute-start | bytes 393224 | tf_op jit(solution)/shard_map/ppermute | solution.py:242
  34.0 9.7 %collective-permute-start.15 = (bf16[128,1280]{1,0:T(8,128)(2,1)S(1)}, bf16[128,1280]{1,0:T(8,128)(2,1)S(1)}, u32[]{:S(2)}, u32[]{:S(2)}) collective-permute-start(bf16[128,1280]{1,0:T(8,128)(2,1)S(1)} %get-tuple-element.35.refs_5_), channel_id=1, source_target_pairs={{0,2},{2,0},{4,6},{6,4},{1,3},{3,1},{5,7},{7,5},{8,10},{10,8},{12,... | collective-permute-start | bytes 983048 | tf_op jit(solution)/shard_map/ppermute | solution.py:242
  34.1 5.3 %collective-permute-start.14 = (bf16[256,128]{1,0:T(8,128)(2,1)S(1)}, bf16[256,128]{1,0:T(8,128)(2,1)S(1)}, u32[]{:S(2)}, u32[]{:S(2)}) collective-permute-start(bf16[256,128]{1,0:T(8,128)(2,1)S(1)} %get-tuple-element.34.refs_0_), channel_id=1, source_target_pairs={{0,24},{8,16},{16,8},{24,0},{1,25},{9,17},{17,9},{25,1},{2,26},{10... | collective-permute-start | bytes 196616 | tf_op jit(solution)/shard_map/ppermute | solution.py:242
  36.6 4.3 %collective-permute-start.13 = (bf16[256,128]{1,0:T(8,128)(2,1)S(1)}, bf16[256,128]{1,0:T(8,128)(2,1)S(1)}, u32[]{:S(2)}, u32[]{:S(2)}) collective-permute-start(bf16[256,128]{1,0:T(8,128)(2,1)S(1)} %get-tuple-element.34.refs_0_), channel_id=1, source_target_pairs={{0,16},{8,24},{16,0},{24,8},{1,17},{9,25},{17,1},{25,9},{2,18},{10... | collective-permute-start | bytes 196616 | tf_op jit(solution)/shard_map/ppermute | solution.py:242
  37.1 4.3 %collective-permute-start.12 = (bf16[256,128]{1,0:T(8,128)(2,1)S(1)}, bf16[256,128]{1,0:T(8,128)(2,1)S(1)}, u32[]{:S(2)}, u32[]{:S(2)}) collective-permute-start(bf16[256,128]{1,0:T(8,128)(2,1)S(1)} %get-tuple-element.34.refs_0_), channel_id=1, source_target_pairs={{0,8},{8,0},{16,24},{24,16},{1,9},{9,1},{17,25},{25,17},{2,10},{10... | collective-permute-start | bytes 196616 | tf_op jit(solution)/shard_map/ppermute | solution.py:242
  44.9 1.7 %collective-permute-start.16 = (bf16[4,32,1280]{2,1,0:T(8,128)(2,1)S(1)}, bf16[4,32,1280]{2,1,0:T(8,128)(2,1)S(1)}, u32[]{:S(2)}, u32[]{:S(2)}) collective-permute-start(bf16[4,32,1280]{2,1,0:T(8,128)(2,1)S(1)} %get-tuple-element.38), channel_id=1, source_target_pairs={{0,1},{1,0},{2,3},{3,2},{4,5},{5,4},{6,7},{7,6},{8,9},{9,8},{10,11... | collective-permute-start | bytes 983048 | tf_op jit(solution)/shard_map/ppermute | solution.py:242
  46.7 4.6 %collective-permute-start.17 = (bf16[32,1280]{1,0:T(8,128)(2,1)S(1)}, bf16[32,1280]{1,0:T(8,128)(2,1)S(1)}, u32[]{:S(2)}, u32[]{:S(2)}) collective-permute-start(bf16[32,1280]{1,0:T(8,128)(2,1)S(1)} %get-tuple-element.40), channel_id=1, source_target_pairs={{0,8},{8,0},{16,24},{24,16},{1,9},{9,1},{17,25},{25,17},{2,10},{10... | collective-permute-start | bytes 245768 | tf_op jit(solution)/shard_map/ppermute | solution.py:242
  48.2 5.3 %collective-permute-start.18 = (bf16[32,1280]{1,0:T(8,128)(2,1)S(1)}, bf16[32,1280]{1,0:T(8,128)(2,1)S(1)}, u32[]{:S(2)}, u32[]{:S(2)}) collective-permute-start(bf16[32,1280]{1,0:T(8,128)(2,1)S(1)} %get-tuple-element.41), channel_id=1, source_target_pairs={{0,16},{8,24},{16,0},{24,8},{1,17},{9,25},{17,1},{25,9},{2,18},{10... | collective-permute-start | bytes 245768 | tf_op jit(solution)/shard_map/ppermute | solution.py:242
  49.8 5.3 %collective-permute-start.19 = (bf16[32,1280]{1,0:T(8,128)(2,1)S(1)}, bf16[32,1280]{1,0:T(8,128)(2,1)S(1)}, u32[]{:S(2)}, u32[]{:S(2)}) collective-permute-start(bf16[32,1280]{1,0:T(8,128)(2,1)S(1)} %get-tuple-element.42), channel_id=1, source_target_pairs={{0,24},{8,16},{16,8},{24,0},{1,25},{9,17},{17,9},{25,1},{2,26},{10... | collective-permute-start | bytes 245768 | tf_op jit(solution)/shard_map/ppermute | solution.py:242

commit v7 on v6

--- a/solution.py
+++ b/solution.py
@@ -19,28 +19,28 @@
 PARAMS = pltpu.CompilerParams(vmem_limit_bytes=48 * 1024 * 1024)
 
 
-def pack_kernel(head_dim, at_ref, x_ref, *out_refs):
+def pack_kernel(head_dim, x_ref, out_ref):
+    peers, _, width = out_ref.shape
     kinds, tok, _ = x_ref.shape
-    heads = out_refs[0].shape[1] // head_dim
-    for m, out_ref in enumerate(out_refs):
-        place = at_ref[0] ^ m
+    heads = width // head_dim
+    for g in range(peers):
         for i in range(heads):
-            head = (place // 2 * heads + i) * 2 + place % 2
-            cols = pl.ds(pl.multiple_of(head * head_dim, head_dim), head_dim)
+            head = (g // 2 * heads + i) * 2 + g % 2
             for k in range(kinds):
-                out_ref[k * tok:(k + 1) * tok, i * head_dim:(i + 1) * head_dim] = x_ref[k, :, cols]
-
-
-def pack(x, place, peers, head_dim):
+                out_ref[g, k * tok:(k + 1) * tok, i * head_dim:(i + 1) * head_dim] = x_ref[
+                    k, :, head * head_dim:(head + 1) * head_dim
+                ]
+
+
+def pack(x, peers, head_dim):
     kinds, tok, cols = x.shape
-    like = jax.ShapeDtypeStruct((kinds * tok, cols // peers), x.dtype)
     return pl.pallas_call(
         functools.partial(pack_kernel, head_dim),
-        out_shape=[like] * peers,
-        in_specs=[SMEM, VMEM],
-        out_specs=[VMEM] * peers,
-        compiler_params=PARAMS,
-    )(place, x)
+        out_shape=jax.ShapeDtypeStruct((peers, kinds * tok, cols // peers), x.dtype),
+        in_specs=[VMEM],
+        out_specs=VMEM,
+        compiler_params=PARAMS,
+    )(x)
 
 
 def columns_kernel(at_ref, x_ref, out_ref, sem):
@@ -63,28 +63,25 @@
     )(at, x)
 
 
-def sort_kernel(at_ref, *refs):
-    *in_refs, q_ref, kv_ref = refs
+def cut_kernel(x_ref, q_ref, kv_ref):
     tok = q_ref.shape[1]
-    for m, ref in enumerate(in_refs):
-        place = at_ref[0] ^ m
-        q_ref[place] = ref[0:tok, :]
-        kv_ref[place] = ref[tok:, :]
-
-
-def sort(parts, place):
-    depth, width = parts[0].shape
-    tok, peers = depth // 3, len(parts)
-    return pl.pallas_call(
-        sort_kernel,
+    q_ref[...] = x_ref[:, :tok, :]
+    kv_ref[...] = x_ref[:, tok:, :]
+
+
+def cut(x):
+    peers, depth, width = x.shape
+    tok = depth // 3
+    return pl.pallas_call(
+        cut_kernel,
         out_shape=(
-            jax.ShapeDtypeStruct((peers, tok, width), parts[0].dtype),
-            jax.ShapeDtypeStruct((peers, 2 * tok, width), parts[0].dtype),
+            jax.ShapeDtypeStruct((peers, tok, width), x.dtype),
+            jax.ShapeDtypeStruct((peers, 2 * tok, width), x.dtype),
         ),
-        in_specs=[SMEM] + [VMEM] * peers,
+        in_specs=[VMEM],
         out_specs=(VMEM, VMEM),
         compiler_params=PARAMS,
-    )(place, *parts)
+    )(x)
 
 
 def clip_of(token, blk_tokens, tok_dev, clip_ref):
@@ -95,8 +92,9 @@
     return clip
 
 
-def attention_kernel(head_dim, n_kv, clip_ref, q_ref, *refs):
-    kv_refs, out_ref = refs[:n_kv], refs[(len(refs) + n_kv) // 2]
+def attention_kernel(head_dim, n_kv, n_passed, last, clip_ref, q_ref, *refs):
+    kv_refs, refs = refs[:n_kv], refs[n_kv:]
+    state_refs, out_refs = refs[:3 if last else 0], refs[-n_passed - 1:] if last else refs
     peers, tok, width = q_ref.shape
     count = peers * tok
     scale = 1.0 / math.sqrt(head_dim)
@@ -112,6 +110,8 @@
         cols = slice(h * head_dim, (h + 1) * head_dim)
         queries = q_ref[:, :, cols].reshape(count, head_dim)
         top = total = acc = None
+        if last:
+            top, total, acc = state_refs[0][h], state_refs[1][h], state_refs[2][:, cols]
         for first in range(0, n_kv, per_step):
             scores, values = [], []
             for ref in kv_refs[first:first + per_step]:
@@ -135,20 +135,36 @@
                 dot = jnp.dot(p.astype(jnp.bfloat16), v, preferred_element_type=jnp.float32)
                 total = part if total is None else total + part
                 acc = dot if acc is None else acc + dot
-        out_ref[:, cols] = (acc / total).astype(out_ref.dtype)
-
-
-def attention(q, kvs, frame_clip, head_dim, passed):
+        if last:
+            out_refs[0][:, cols] = (acc / total).astype(out_refs[0].dtype)
+        else:
+            out_refs[0][h], out_refs[1][h], out_refs[2][:, cols] = top, total, acc
+
+
+def attend(q, kvs, frame_clip, head_dim):
+    peers, tok, width = q.shape
+    count = peers * tok
+    stat = jax.ShapeDtypeStruct((width // head_dim, count, 1), jnp.float32)
+    return pl.pallas_call(
+        functools.partial(attention_kernel, head_dim, len(kvs), 0, False),
+        out_shape=(stat, stat, jax.ShapeDtypeStruct((count, width), jnp.float32)),
+        in_specs=[SMEM] + [VMEM] * (1 + len(kvs)),
+        out_specs=(VMEM, VMEM, VMEM),
+        compiler_params=PARAMS,
+    )(frame_clip, q, *kvs)
+
+
+def finish(q, kvs, state, frame_clip, head_dim, passed):
     peers, tok, width = q.shape
     like = jax.ShapeDtypeStruct((peers * tok, width), q.dtype)
     attn, *same = pl.pallas_call(
-        functools.partial(attention_kernel, head_dim, len(kvs)),
+        functools.partial(attention_kernel, head_dim, len(kvs), len(passed), True),
         out_shape=[like] + [jax.ShapeDtypeStruct(x.shape, x.dtype) for x in passed],
-        in_specs=[SMEM] + [VMEM] * (1 + len(kvs)) + [ANY] * len(passed),
+        in_specs=[SMEM] + [VMEM] * (4 + len(kvs)) + [ANY] * len(passed),
         out_specs=[VMEM] + [ANY] * len(passed),
-        input_output_aliases={2 + len(kvs) + i: 1 + i for i in range(len(passed))},
-        compiler_params=PARAMS,
-    )(frame_clip, q, *kvs, *passed)
+        input_output_aliases={5 + len(kvs) + i: 1 + i for i in range(len(passed))},
+        compiler_params=PARAMS,
+    )(frame_clip, q, *kvs, *state, *passed)
     return attn, same
 
 
@@ -246,6 +262,14 @@
     return [parts[0]] + [xor(x, axis, m) for m, x in enumerate(parts) if m]
 
 
+def along_rows(x):
+    rows = lax.axis_size("row")
+    if rows != 4:
+        steps = list(range(1, rows))
+        return [xor(x, ("row",), by) for by in steps], steps
+    return [xor(x, ("row",), 3), xor(x, ("row",), 1)], [3, 1]
+
+
 def on_device(qkv, frame_clip, w_out):
     rows, blks = lax.axis_size("row"), lax.axis_size("blk")
     row = lax.axis_index("row")
@@ -255,14 +279,16 @@
     place = blk * 2 + lax.axis_index("core").astype(jnp.int32)
 
     w_own = columns(w_out, blk, blks)
-    half = rows == 4
-    steps = [rows - 1] + list(range(1, 2 if half else rows - 1))
-    w_others = [xor(w_own, ("row",), by) for by in steps]
-
-    q, kv = sort(swap_all(pack(qkv, place, 2 * blks, head_dim), PLANE), place)
-    kvs = [kv] + [xor(kv, ("row",), by) for by in range(1, rows)]
-    attn, w_others = attention(q, kvs, frame_clip, head_dim, w_others)
-    if half:
+    w_others, steps = along_rows(w_own)
+
+    packed = pack(qkv, 2 * blks, head_dim)
+    q, kv = cut(lax.all_to_all(packed, PLANE, split_axis=0, concat_axis=0, tiled=True))
+    others, _ = along_rows(kv)
+    if rows == 4:
+        others.append(xor(others[0], ("row",), 1))
+    state = attend(q, [kv] + others[:-1], frame_clip, head_dim)
+    attn, w_others = finish(q, others[-1:], state, frame_clip, head_dim, w_others)
+    if rows == 4:
         steps.append(2)
         w_others.append(xor(w_others[0], ("row",), 1))
     attns = swap_all([attn] * blks, ("blk",))

time: 56 us -> 58.6 us (1.046)
  Pallas kernels: 3.34 us -> 5.03 us
  local copies, waits for them, and re-layouts: 1.34 us -> 2.24 us
  waiting for transfers between devices: 26.6 us -> 26 us
    all_to_all x0 -> x1, starting transfers between devices: none -> 5.17 us  [on_device(): lax.all_to_all(packed, PLANE, split_axis=0, concat_axis=0, tiled=True)]
    ppermute x20 -> x13, starting transfers between devices: 24.4 us -> 19.8 us  [xor(): return lax.ppermute(x, axis, [(i, i ^ by) for i in range(size)])]
    pallas_call x3 -> x4, Pallas kernels: 1.33 us -> 3.02 us  [the longest x1 1.21 us: attend(): pl.pallas_call(functools.partial(attention_kernel, head_dim, len(kvs), 0,...]
    ppermute x20 -> x13, waiting for transfers between devices: 26.6 us -> 25.2 us  [xor(): return lax.ppermute(x, axis, [(i, i ^ by) for i in range(size)])]
    unnamed x6, local copies, waits for them, and re-layouts: 1.34 us -> 2.24 us
    all_to_all x0 -> x1, waiting for transfers between devices: none -> 0.75 us  [on_device(): lax.all_to_all(packed, PLANE, split_axis=0, concat_axis=0, tiled=True)]
  transfers between devices with their start and end apart: 20 -> 14, of which waited for: 14 -> 10; matrix products, arithmetic and copies ran while one was open for 0% -> 0% of each run, Pallas kernels for 0% -> 2%
where the time goes in v7:
time: 58.6 us; the launch traced here: 58.4 us
  waiting for transfers between devices  26 us (44%)
  starting transfers between devices  24.9 us (42%)
  Pallas kernels  5.03 us (9%)
  local copies, waits for them, and re-layouts  2.24 us (4%)
    ppermute x13, waiting for transfers between devices, xor(): return lax.ppermute(x, axis, [(i, i ^ by) for i in range(size)])  25.2 us
    ppermute x13, starting transfers between devices, xor(): return lax.ppermute(x, axis, [(i, i ^ by) for i in range(size)])  19.8 us
    all_to_all x1, starting transfers between devices, on_device(): lax.all_to_all(packed, PLANE, split_axis=0, concat_axis=0, tiled=True)  5.17 us
    unnamed x6, local copies, waits for them, and re-layouts  2.24 us
    pallas_call x1, Pallas kernels, attend(): pl.pallas_call(functools.partial(attention_kernel, head_dim, len(kvs), 0,...  1.21 us
  transfers between devices with their start and end apart: 14, of which 10 were waited for; matrix products, arithmetic and copies ran while one was open for 0% of the time, Pallas kernels for 2%

profile of v7, /device:TPU:0, one launch (start us, length us, event | category | flops | bytes accessed | tf_op | source)
XLA Modules:
  0.0 58.4 jit_solution(14128178868262516424)
XLA Ops:
  0.0 0.0 copy-start.1
  0.0 0.9 %copy-done.1 = bf16[3,32,1024]{2,1,0:T(8,128)(2,1)S(1)} copy-done((bf16[3,32,1024]{2,1,0:T(8,128)(2,1)S(1)}, bf16[3,32,1024]{2,1,0:T(8,128)(2,1)}, u32[]{:S(2)}) %copy-start.1) | copy-done | bytes 196632
  0.9 0.0 copy-start.2
  0.9 0.7 %shard_map.37 = bf16[8,96,128]{2,1,0:T(8,128)(2,1)} custom-call(bf16[3,32,1024]{2,1,0:T(8,128)(2,1)S(1)} %copy-done.1), custom_call_target="tpu_custom_call" | custom-call | tf_op jit(solution)/shard_map/pallas_call | solution.py:37
  1.6 5.2 %all-to-all-start = ((bf16[8,96,128]{2,1,0:T(8,128)(2,1)}), bf16[8,96,128]{2,1,0:T(8,128)(2,1)S(1)}, u32[]{:S(2)}, u32[]{:S(2)}) async-start(bf16[8,96,128]{2,1,0:T(8,128)(2,1)} %shard_map.37), calls=%async_computation | async-start | bytes 393216 | tf_op jit(solution)/shard_map/all_to_all | solution.py:285
  6.8 0.0 copy-start
  6.8 1.3 %copy-done = bf16[128,5120]{1,0:T(8,128)(2,1)S(1)} copy-done((bf16[128,5120]{1,0:T(8,128)(2,1)S(1)}, bf16[128,5120]{1,0:T(8,128)(2,1)}, u32[]{:S(2)}) %copy-start) | copy-done | bytes 1310744
  8.2 1.6 %collective-permute-start.4 = (bf16[128,1280]{1,0:T(8,128)(2,1)S(1)}, bf16[128,1280]{1,0:T(8,128)(2,1)S(1)}, u32[]{:S(2)}, u32[]{:S(2)}) collective-permute-start(bf16[128,1280]{1,0:T(8,128)(2,1)S(1)} %shard_map.40.refs_4_), channel_id=1, source_target_pairs={{0,2},{2,0},{4,6},{6,4},{1,3},{3,1},{5,7},{7,5},{8,10},{10,8},{12,... | collective-permute-start | bytes 983048 | tf_op jit(solution)/shard_map/ppermute | solution.py:258
  9.8 2.5 %collective-permute-start.3 = (bf16[128,1280]{1,0:T(8,128)(2,1)S(1)}, bf16[128,1280]{1,0:T(8,128)(2,1)S(1)}, u32[]{:S(2)}, u32[]{:S(2)}) collective-permute-start(bf16[128,1280]{1,0:T(8,128)(2,1)S(1)} %shard_map.40.refs_4_), channel_id=1, source_target_pairs={{0,6},{2,4},{4,2},{6,0},{1,7},{3,5},{5,3},{7,1},{8,14},{10,12},{12... | collective-permute-start | bytes 983048 | tf_op jit(solution)/shard_map/ppermute | solution.py:258
  12.3 0.8 %all-to-all-done.x_ref = bf16[8,96,128]{2,1,0:T(8,128)(2,1)S(1)} async-done(((bf16[8,96,128]{2,1,0:T(8,128)(2,1)}), bf16[8,96,128]{2,1,0:T(8,128)(2,1)S(1)}, u32[]{:S(2)}, u32[]{:S(2)}) %all-to-all-start) | async-done | bytes 196640 | tf_op jit(solution)/shard_map/all_to_all | solution.py:285
  13.1 3.7 %collective-permute-start = (bf16[8,64,128]{2,1,0:T(8,128)(2,1)S(1)}, bf16[8,64,128]{2,1,0:T(8,128)(2,1)S(1)}, u32[]{:S(2)}, u32[]{:S(2)}) collective-permute-start(bf16[8,64,128]{2,1,0:T(8,128)(2,1)S(1)} %get-tuple-element.20.refs_0_), channel_id=1, source_target_pairs={{0,6},{2,4},{4,2},{6,0},{1,7},{3,5},{5,3},{7,1},{8,14},{10,12},{12... | collective-permute-start | bytes 393224 | tf_op jit(solution)/shard_map/ppermute | solution.py:258
  16.7 0.0 collective-permute-start.2
  16.7 13.9 %collective-permute-done.refs_1_ = bf16[8,64,128]{2,1,0:T(8,128)(2,1)S(1)} collective-permute-done((bf16[8,64,128]{2,1,0:T(8,128)(2,1)S(1)}, bf16[8,64,128]{2,1,0:T(8,128)(2,1)S(1)}, u32[]{:S(2)}, u32[]{:S(2)}) %collective-permute-start) | collective-permute-done | bytes 131104 | tf_op jit(solution)/shard_map/ppermute | solution.py:258
  30.6 3.1 %collective-permute-start.1 = (bf16[8,64,128]{2,1,0:T(8,128)(2,1)S(1)}, bf16[8,64,128]{2,1,0:T(8,128)(2,1)S(1)}, u32[]{:S(2)}, u32[]{:S(2)}) collective-permute-start(bf16[8,64,128]{2,1,0:T(8,128)(2,1)S(1)} %collective-permute-done.refs_1_), channel_id=1, source_target_pairs={{0,2},{2,0},{4,6},{6,4},{1,3},{3,1},{5,7},{7,5},{8,10},{10,8},{12,... | collective-permute-start | bytes 393224 | tf_op jit(solution)/shard_map/ppermute | solution.py:258
  33.7 0.0 collective-permute-done.2.refs_2_
  33.7 0.0 copy-done.2
  33.7 1.2 %shard_map.39 = (f32[1,256,1]{2,1,0:T(8,128)S(1)}, f32[1,256,1]{2,1,0:T(8,128)S(1)}, f32[256,128]{1,0:T(8,128)S(1)}) custom-call(s32[8]{0:T(128)S(1)} %copy-done.2, bf16[8,32,128]{2,1,0:T(8,128)(2,1)S(1)} %get-tuple-element.19.q_ref, bf16[8,64,128]{2,1,0:T(8,128)(2,1)S(1)} %get-tuple-element.20.refs_0_, ...), custom_call_target="tpu_custom_call" | custom-call | tf_op jit(solution)/shard_map/pallas_call | solution.py:148
  34.9 0.0 collective-permute-done.4.refs_5_
  34.9 0.0 collective-permute-done.3.refs_4_
  34.9 2.1 %collective-permute-done.1.refs_0_ = bf16[8,64,128]{2,1,0:T(8,128)(2,1)S(1)} collective-permute-done((bf16[8,64,128]{2,1,0:T(8,128)(2,1)S(1)}, bf16[8,64,128]{2,1,0:T(8,128)(2,1)S(1)}, u32[]{:S(2)}, u32[]{:S(2)}) %collective-permute-start.1) | collective-permute-done | bytes 131104 | tf_op jit(solution)/shard_map/ppermute | solution.py:258
  37.1 1.1 %shard_map.41 = (bf16[256,128]{1,0:T(8,128)(2,1)S(1)}, bf16[128,1280]{1,0:T(8,128)(2,1)S(1)}, bf16[128,1280]{1,0:T(8,128)(2,1)S(1)}) custom-call(s32[8]{0:T(128)S(1)} %copy-done.2, bf16[8,32,128]{2,1,0:T(8,128)(2,1)S(1)} %get-tuple-element.19.q_ref, ...), custom_call_target="tpu_custom_call", output_to_operand_aliasing={{1}: (6, {}), {2}: (7, {})} | custom-call | tf_op jit(solution)/shard_map/pallas_call | solution.py:160
  38.2 1.8 %collective-permute-start.8 = (bf16[128,1280]{1,0:T(8,128)(2,1)S(1)}, bf16[128,1280]{1,0:T(8,128)(2,1)S(1)}, u32[]{:S(2)}, u32[]{:S(2)}) collective-permute-start(bf16[128,1280]{1,0:T(8,128)(2,1)S(1)} %get-tuple-element.25.refs_5_), channel_id=1, source_target_pairs={{0,2},{2,0},{4,6},{6,4},{1,3},{3,1},{5,7},{7,5},{8,10},{10,8},{12,... | collective-permute-start | bytes 983048 | tf_op jit(solution)/shard_map/ppermute | solution.py:258
  40.0 2.4 %collective-permute-start.7 = (bf16[256,128]{1,0:T(8,128)(2,1)S(1)}, bf16[256,128]{1,0:T(8,128)(2,1)S(1)}, u32[]{:S(2)}, u32[]{:S(2)}) collective-permute-start(bf16[256,128]{1,0:T(8,128)(2,1)S(1)} %get-tuple-element.24.refs_0_), channel_id=1, source_target_pairs={{0,24},{8,16},{16,8},{24,0},{1,25},{9,17},{17,9},{25,1},{2,26},{10... | collective-permute-start | bytes 196616 | tf_op jit(solution)/shard_map/ppermute | solution.py:258
  42.4 0.6 collective-permute-start.6
  43.0 0.5 collective-permute-start.5
  43.5 0.1 pad_add_fusion.at_ref
  43.6 1.6 %collective-permute-done.7.refs_3_ = bf16[256,128]{1,0:T(8,128)(2,1)S(1)} collective-permute-done((bf16[256,128]{1,0:T(8,128)(2,1)S(1)}, bf16[256,128]{1,0:T(8,128)(2,1)S(1)}, u32[]{:S(2)}, u32[]{:S(2)}) %collective-permute-start.7) | collective-permute-done | bytes 65568 | tf_op jit(solution)/shard_map/ppermute | solution.py:258
  45.2 1.5 %collective-permute-done.6.refs_2_ = bf16[256,128]{1,0:T(8,128)(2,1)S(1)} collective-permute-done((bf16[256,128]{1,0:T(8,128)(2,1)S(1)}, bf16[256,128]{1,0:T(8,128)(2,1)S(1)}, u32[]{:S(2)}, u32[]{:S(2)}) %collective-permute-start.6) | collective-permute-done | bytes 65568 | tf_op jit(solution)/shard_map/ppermute | solution.py:258
  46.7 0.6 collective-permute-done.5.refs_1_
  47.2 0.0 collective-permute-done.8.refs_7_
  47.2 1.1 %shard_map.42 = (bf16[4,32,1280]{2,1,0:T(8,128)(2,1)S(1)}, bf16[4,32,1280]{2,1,0:T(8,128)(2,1)S(1)}) custom-call(s32[4]{0:T(128)S(1)} %pad_add_fusion.at_ref, s32[1]{0:T(128)S(6)} %add.7.place_ref, bf16[256,128]{1,0:T(8,128)(2,1)S(1)} %get-tuple-element.24.refs_0_, bf16[256,128]{1,0:T(8,128)(2,1)S(1)} %collective-permute-done.5.refs_1_, ...), custom_call_target="tpu_custom_call" | custom-call | tf_op jit(solution)/shard_map/pallas_call | solution.py:209
  48.4 0.1 collective-permute-start.9
  48.5 1.6 %collective-permute-done.9.y_ref = bf16[4,32,1280]{2,1,0:T(8,128)(2,1)S(1)} collective-permute-done((bf16[4,32,1280]{2,1,0:T(8,128)(2,1)S(1)}, bf16[4,32,1280]{2,1,0:T(8,128)(2,1)S(1)}, u32[]{:S(2)}, u32[]{:S(2)}) %collective-permute-start.9) | collective-permute-done | bytes 327712 | tf_op jit(solution)/shard_map/ppermute | solution.py:258
  50.1 0.1 shard_map.43
  50.2 0.6 %collective-permute-start.10 = (bf16[32,1280]{1,0:T(8,128)(2,1)S(1)}, bf16[32,1280]{1,0:T(8,128)(2,1)S(1)}, u32[]{:S(2)}, u32[]{:S(2)}) collective-permute-start(bf16[32,1280]{1,0:T(8,128)(2,1)S(1)} %get-tuple-element.30), channel_id=1, source_target_pairs={{0,8},{8,0},{16,24},{24,16},{1,9},{9,1},{17,25},{25,17},{2,10},{10... | collective-permute-start | bytes 245768 | tf_op jit(solution)/shard_map/ppermute | solution.py:258
  50.7 1.5 %collective-permute-start.11 = (bf16[32,1280]{1,0:T(8,128)(2,1)S(1)}, bf16[32,1280]{1,0:T(8,128)(2,1)S(1)}, u32[]{:S(2)}, u32[]{:S(2)}) collective-permute-start(bf16[32,1280]{1,0:T(8,128)(2,1)S(1)} %get-tuple-element.31), channel_id=1, source_target_pairs={{0,16},{8,24},{16,0},{24,8},{1,17},{9,25},{17,1},{25,9},{2,18},{10... | collective-permute-start | bytes 245768 | tf_op jit(solution)/shard_map/ppermute | solution.py:258
  52.3 1.5 %collective-permute-start.12 = (bf16[32,1280]{1,0:T(8,128)(2,1)S(1)}, bf16[32,1280]{1,0:T(8,128)(2,1)S(1)}, u32[]{:S(2)}, u32[]{:S(2)}) collective-permute-start(bf16[32,1280]{1,0:T(8,128)(2,1)S(1)} %get-tuple-element.32), channel_id=1, source_target_pairs={{0,24},{8,16},{16,8},{24,0},{1,25},{9,17},{17,9},{25,1},{2,26},{10... | collective-permute-start | bytes 245768 | tf_op jit(solution)/shard_map/ppermute | solution.py:258
  53.7 1.4 %collective-permute-done.10.refs_1_ = bf16[32,1280]{1,0:T(8,128)(2,1)S(1)} collective-permute-done((bf16[32,1280]{1,0:T(8,128)(2,1)S(1)}, bf16[32,1280]{1,0:T(8,128)(2,1)S(1)}, u32[]{:S(2)}, u32[]{:S(2)}) %collective-permute-start.10) | collective-permute-done | bytes 81952 | tf_op jit(solution)/shard_map/ppermute | solution.py:258
  55.1 0.9 %collective-permute-done.11.refs_2_ = bf16[32,1280]{1,0:T(8,128)(2,1)S(1)} collective-permute-done((bf16[32,1280]{1,0:T(8,128)(2,1)S(1)}, bf16[32,1280]{1,0:T(8,128)(2,1)S(1)}, u32[]{:S(2)}, u32[]{:S(2)}) %collective-permute-start.11) | collective-permute-done | bytes 81952 | tf_op jit(solution)/shard_map/ppermute | solution.py:258
  56.0 1.6 %collective-permute-done.12.refs_3_ = bf16[32,1280]{1,0:T(8,128)(2,1)S(1)} collective-permute-done((bf16[32,1280]{1,0:T(8,128)(2,1)S(1)}, bf16[32,1280]{1,0:T(8,128)(2,1)S(1)}, u32[]{:S(2)}, u32[]{:S(2)}) %collective-permute-start.12) | collective-permute-done | bytes 81952 | tf_op jit(solution)/shard_map/ppermute | solution.py:258
  57.6 0.8 %shard_map.44 = bf16[32,5120]{1,0:T(8,128)(2,1)} custom-call(s32[1]{0:T(128)S(6)} %add.7.place_ref, bf16[32,1280]{1,0:T(8,128)(2,1)S(1)} %get-tuple-element.29.refs_0_, bf16[32,1280]{1,0:T(8,128)(2,1)S(1)} %collective-permute-done.10.refs_1_, bf16[32,1280]{1,0:T(8,128)(2,1)S(1)} %collective-permute-done.11.refs_2_, ...), custom_call_target="tpu_custom_call" | custom-call | tf_op jit(solution)/shard_map/pallas_call | solution.py:247
  (2 shorter events, 0.1 us)
Async XLA Ops:
  0.0 0.9 %copy-start.1 = (bf16[3,32,1024]{2,1,0:T(8,128)(2,1)S(1)}, bf16[3,32,1024]{2,1,0:T(8,128)(2,1)}, u32[]{:S(2)}) copy-start(bf16[3,32,1024]{2,1,0:T(8,128)(2,1)} %x_ref.2) | copy-start | bytes 589828
  0.9 32.8 %copy-start.2 = (s32[8]{0:T(128)S(1)}, s32[8]{0:T(128)}, u32[]{:S(2)}) copy-start(s32[8]{0:T(128)} %clip_ref.3) | copy-start | bytes 100
  1.6 11.4 %all-to-all-start = ((bf16[8,96,128]{2,1,0:T(8,128)(2,1)}), bf16[8,96,128]{2,1,0:T(8,128)(2,1)S(1)}, u32[]{:S(2)}, u32[]{:S(2)}) async-start(bf16[8,96,128]{2,1,0:T(8,128)(2,1)} %shard_map.37), calls=%async_computation | async-start | bytes 393216 | tf_op jit(solution)/shard_map/all_to_all | solution.py:285
  6.8 1.3 %copy-start = (bf16[128,5120]{1,0:T(8,128)(2,1)S(1)}, bf16[128,5120]{1,0:T(8,128)(2,1)}, u32[]{:S(2)}) copy-start(bf16[128,5120]{1,0:T(8,128)(2,1)} %x_ref.3) | copy-start | bytes 3932164
  8.2 26.8 %collective-permute-start.4 = (bf16[128,1280]{1,0:T(8,128)(2,1)S(1)}, bf16[128,1280]{1,0:T(8,128)(2,1)S(1)}, u32[]{:S(2)}, u32[]{:S(2)}) collective-permute-start(bf16[128,1280]{1,0:T(8,128)(2,1)S(1)} %shard_map.40.refs_4_), channel_id=1, source_target_pairs={{0,2},{2,0},{4,6},{6,4},{1,3},{3,1},{5,7},{7,5},{8,10},{10,8},{12,... | collective-permute-start | bytes 983048 | tf_op jit(solution)/shard_map/ppermute | solution.py:258
  9.8 25.1 %collective-permute-start.3 = (bf16[128,1280]{1,0:T(8,128)(2,1)S(1)}, bf16[128,1280]{1,0:T(8,128)(2,1)S(1)}, u32[]{:S(2)}, u32[]{:S(2)}) collective-permute-start(bf16[128,1280]{1,0:T(8,128)(2,1)S(1)} %shard_map.40.refs_4_), channel_id=1, source_target_pairs={{0,6},{2,4},{4,2},{6,0},{1,7},{3,5},{5,3},{7,1},{8,14},{10,12},{12... | collective-permute-start | bytes 983048 | tf_op jit(solution)/shard_map/ppermute | solution.py:258
  13.1 17.6 %collective-permute-start = (bf16[8,64,128]{2,1,0:T(8,128)(2,1)S(1)}, bf16[8,64,128]{2,1,0:T(8,128)(2,1)S(1)}, u32[]{:S(2)}, u32[]{:S(2)}) collective-permute-start(bf16[8,64,128]{2,1,0:T(8,128)(2,1)S(1)} %get-tuple-element.20.refs_0_), channel_id=1, source_target_pairs={{0,6},{2,4},{4,2},{6,0},{1,7},{3,5},{5,3},{7,1},{8,14},{10,12},{12... | collective-permute-start | bytes 393224 | tf_op jit(solution)/shard_map/ppermute | solution.py:258
  16.7 17.0 %collective-permute-start.2 = (bf16[8,64,128]{2,1,0:T(8,128)(2,1)S(1)}, bf16[8,64,128]{2,1,0:T(8,128)(2,1)S(1)}, u32[]{:S(2)}, u32[]{:S(2)}) collective-permute-start(bf16[8,64,128]{2,1,0:T(8,128)(2,1)S(1)} %get-tuple-element.20.refs_0_), channel_id=1, source_target_pairs={{0,2},{2,0},{4,6},{6,4},{1,3},{3,1},{5,7},{7,5},{8,10},{10,8},{12,... | collective-permute-start | bytes 393224 | tf_op jit(solution)/shard_map/ppermute | solution.py:258
  30.6 6.4 %collective-permute-start.1 = (bf16[8,64,128]{2,1,0:T(8,128)(2,1)S(1)}, bf16[8,64,128]{2,1,0:T(8,128)(2,1)S(1)}, u32[]{:S(2)}, u32[]{:S(2)}) collective-permute-start(bf16[8,64,128]{2,1,0:T(8,128)(2,1)S(1)} %collective-permute-done.refs_1_), channel_id=1, source_target_pairs={{0,2},{2,0},{4,6},{6,4},{1,3},{3,1},{5,7},{7,5},{8,10},{10,8},{12,... | collective-permute-start | bytes 393224 | tf_op jit(solution)/shard_map/ppermute | solution.py:258
  38.2 9.0 %collective-permute-start.8 = (bf16[128,1280]{1,0:T(8,128)(2,1)S(1)}, bf16[128,1280]{1,0:T(8,128)(2,1)S(1)}, u32[]{:S(2)}, u32[]{:S(2)}) collective-permute-start(bf16[128,1280]{1,0:T(8,128)(2,1)S(1)} %get-tuple-element.25.refs_5_), channel_id=1, source_target_pairs={{0,2},{2,0},{4,6},{6,4},{1,3},{3,1},{5,7},{7,5},{8,10},{10,8},{12,... | collective-permute-start | bytes 983048 | tf_op jit(solution)/shard_map/ppermute | solution.py:258
  40.0 5.2 %collective-permute-start.7 = (bf16[256,128]{1,0:T(8,128)(2,1)S(1)}, bf16[256,128]{1,0:T(8,128)(2,1)S(1)}, u32[]{:S(2)}, u32[]{:S(2)}) collective-permute-start(bf16[256,128]{1,0:T(8,128)(2,1)S(1)} %get-tuple-element.24.refs_0_), channel_id=1, source_target_pairs={{0,24},{8,16},{16,8},{24,0},{1,25},{9,17},{17,9},{25,1},{2,26},{10... | collective-permute-start | bytes 196616 | tf_op jit(solution)/shard_map/ppermute | solution.py:258
  42.4 4.3 %collective-permute-start.6 = (bf16[256,128]{1,0:T(8,128)(2,1)S(1)}, bf16[256,128]{1,0:T(8,128)(2,1)S(1)}, u32[]{:S(2)}, u32[]{:S(2)}) collective-permute-start(bf16[256,128]{1,0:T(8,128)(2,1)S(1)} %get-tuple-element.24.refs_0_), channel_id=1, source_target_pairs={{0,16},{8,24},{16,0},{24,8},{1,17},{9,25},{17,1},{25,9},{2,18},{10... | collective-permute-start | bytes 196616 | tf_op jit(solution)/shard_map/ppermute | solution.py:258
  43.0 4.3 %collective-permute-start.5 = (bf16[256,128]{1,0:T(8,128)(2,1)S(1)}, bf16[256,128]{1,0:T(8,128)(2,1)S(1)}, u32[]{:S(2)}, u32[]{:S(2)}) collective-permute-start(bf16[256,128]{1,0:T(8,128)(2,1)S(1)} %get-tuple-element.24.refs_0_), channel_id=1, source_target_pairs={{0,8},{8,0},{16,24},{24,16},{1,9},{9,1},{17,25},{25,17},{2,10},{10... | collective-permute-start | bytes 196616 | tf_op jit(solution)/shard_map/ppermute | solution.py:258
  48.4 1.7 %collective-permute-start.9 = (bf16[4,32,1280]{2,1,0:T(8,128)(2,1)S(1)}, bf16[4,32,1280]{2,1,0:T(8,128)(2,1)S(1)}, u32[]{:S(2)}, u32[]{:S(2)}) collective-permute-start(bf16[4,32,1280]{2,1,0:T(8,128)(2,1)S(1)} %get-tuple-element.28), channel_id=1, source_target_pairs={{0,1},{1,0},{2,3},{3,2},{4,5},{5,4},{6,7},{7,6},{8,9},{9,8},{10,11... | collective-permute-start | bytes 983048 | tf_op jit(solution)/shard_map/ppermute | solution.py:258
  50.2 4.9 %collective-permute-start.10 = (bf16[32,1280]{1,0:T(8,128)(2,1)S(1)}, bf16[32,1280]{1,0:T(8,128)(2,1)S(1)}, u32[]{:S(2)}, u32[]{:S(2)}) collective-permute-start(bf16[32,1280]{1,0:T(8,128)(2,1)S(1)} %get-tuple-element.30), channel_id=1, source_target_pairs={{0,8},{8,0},{16,24},{24,16},{1,9},{9,1},{17,25},{25,17},{2,10},{10... | collective-permute-start | bytes 245768 | tf_op jit(solution)/shard_map/ppermute | solution.py:258
  50.7 5.3 %collective-permute-start.11 = (bf16[32,1280]{1,0:T(8,128)(2,1)S(1)}, bf16[32,1280]{1,0:T(8,128)(2,1)S(1)}, u32[]{:S(2)}, u32[]{:S(2)}) collective-permute-start(bf16[32,1280]{1,0:T(8,128)(2,1)S(1)} %get-tuple-element.31), channel_id=1, source_target_pairs={{0,16},{8,24},{16,0},{24,8},{1,17},{9,25},{17,1},{25,9},{2,18},{10... | collective-permute-start | bytes 245768 | tf_op jit(solution)/shard_map/ppermute | solution.py:258
  52.3 5.3 %collective-permute-start.12 = (bf16[32,1280]{1,0:T(8,128)(2,1)S(1)}, bf16[32,1280]{1,0:T(8,128)(2,1)S(1)}, u32[]{:S(2)}, u32[]{:S(2)}) collective-permute-start(bf16[32,1280]{1,0:T(8,128)(2,1)S(1)} %get-tuple-element.32), channel_id=1, source_target_pairs={{0,24},{8,16},{16,8},{24,0},{1,25},{9,17},{17,9},{25,1},{2,26},{10... | collective-permute-start | bytes 245768 | tf_op jit(solution)/shard_map/ppermute | solution.py:258

commit v8 on v7

--- a/solution.py
+++ b/solution.py
@@ -43,45 +43,69 @@
     )(x)
 
 
-def columns_kernel(at_ref, x_ref, out_ref, sem):
+def columns_kernel(at_ref, x_ref, out_ref, *refs):
+    *part_refs, sem = refs
     cols = out_ref.shape[1]
     start = pl.multiple_of(at_ref[0] * cols, cols)
     copy = pltpu.make_async_copy(x_ref.at[:, pl.ds(start, cols)], out_ref, sem)
     copy.start()
     copy.wait()
-
-
-def columns(x, at, parts):
+    first = 0
+    for ref in part_refs:
+        ref[...] = out_ref[first:first + ref.shape[0], :]
+        first += ref.shape[0]
+
+
+def columns(x, at, parts, cuts):
     depth, cols = x.shape
+    like = [jax.ShapeDtypeStruct((n, cols // parts), x.dtype) for n in (depth, *cuts)]
     return pl.pallas_call(
         columns_kernel,
-        out_shape=jax.ShapeDtypeStruct((depth, cols // parts), x.dtype),
+        out_shape=like,
         in_specs=[SMEM, pl.BlockSpec(memory_space=pltpu.HBM)],
-        out_specs=VMEM,
+        out_specs=[VMEM] * len(like),
         scratch_shapes=[pltpu.SemaphoreType.DMA],
         compiler_params=PARAMS,
     )(at, x)
 
 
-def cut_kernel(x_ref, q_ref, kv_ref):
+def cut_kernel(x_ref, *refs):
+    q_ref, kv_ref = refs[len(refs) // 2 - 1:][:2]
     tok = q_ref.shape[1]
     q_ref[...] = x_ref[:, :tok, :]
     kv_ref[...] = x_ref[:, tok:, :]
 
 
-def cut(x):
+def cut(x, passed):
     peers, depth, width = x.shape
-    tok = depth // 3
-    return pl.pallas_call(
+    tok, n = depth // 3, len(passed)
+    q, kv, *same = pl.pallas_call(
         cut_kernel,
-        out_shape=(
+        out_shape=[
             jax.ShapeDtypeStruct((peers, tok, width), x.dtype),
             jax.ShapeDtypeStruct((peers, 2 * tok, width), x.dtype),
-        ),
-        in_specs=[VMEM],
-        out_specs=(VMEM, VMEM),
-        compiler_params=PARAMS,
-    )(x)
+        ] + [jax.ShapeDtypeStruct(y.shape, y.dtype) for y in passed],
+        in_specs=[VMEM] + [ANY] * n,
+        out_specs=[VMEM, VMEM] + [ANY] * n,
+        input_output_aliases={1 + i: 2 + i for i in range(n)},
+        compiler_params=PARAMS,
+    )(x, *passed)
+    return q, kv, same
+
+
+def after_kernel(*refs):
+    pass
+
+
+def after(x, passed):
+    return pl.pallas_call(
+        after_kernel,
+        out_shape=jax.ShapeDtypeStruct(passed.shape, passed.dtype),
+        in_specs=[ANY, ANY],
+        out_specs=ANY,
+        input_output_aliases={1: 0},
+        compiler_params=PARAMS,
+    )(x, passed)
 
 
 def clip_of(token, blk_tokens, tok_dev, clip_ref):
@@ -94,7 +118,8 @@
 
 def attention_kernel(head_dim, n_kv, n_passed, last, clip_ref, q_ref, *refs):
     kv_refs, refs = refs[:n_kv], refs[n_kv:]
-    state_refs, out_refs = refs[:3 if last else 0], refs[-n_passed - 1:] if last else refs
+    state_refs = refs[:3 if last else 0]
+    out_refs = refs[len(state_refs) + n_passed:]
     peers, tok, width = q_ref.shape
     count = peers * tok
     scale = 1.0 / math.sqrt(head_dim)
@@ -141,38 +166,32 @@
             out_refs[0][h], out_refs[1][h], out_refs[2][:, cols] = top, total, acc
 
 
-def attend(q, kvs, frame_clip, head_dim):
+def attention(q, kvs, state, frame_clip, head_dim, passed):
     peers, tok, width = q.shape
     count = peers * tok
     stat = jax.ShapeDtypeStruct((width // head_dim, count, 1), jnp.float32)
-    return pl.pallas_call(
-        functools.partial(attention_kernel, head_dim, len(kvs), 0, False),
-        out_shape=(stat, stat, jax.ShapeDtypeStruct((count, width), jnp.float32)),
-        in_specs=[SMEM] + [VMEM] * (1 + len(kvs)),
-        out_specs=(VMEM, VMEM, VMEM),
-        compiler_params=PARAMS,
-    )(frame_clip, q, *kvs)
-
-
-def finish(q, kvs, state, frame_clip, head_dim, passed):
-    peers, tok, width = q.shape
-    like = jax.ShapeDtypeStruct((peers * tok, width), q.dtype)
-    attn, *same = pl.pallas_call(
-        functools.partial(attention_kernel, head_dim, len(kvs), len(passed), True),
-        out_shape=[like] + [jax.ShapeDtypeStruct(x.shape, x.dtype) for x in passed],
-        in_specs=[SMEM] + [VMEM] * (4 + len(kvs)) + [ANY] * len(passed),
-        out_specs=[VMEM] + [ANY] * len(passed),
-        input_output_aliases={5 + len(kvs) + i: 1 + i for i in range(len(passed))},
+    if state:
+        out = [jax.ShapeDtypeStruct((count, width), q.dtype)]
+    else:
+        out = [stat, stat, jax.ShapeDtypeStruct((count, width), jnp.float32)]
+    given, n = 2 + len(kvs) + len(state), len(passed)
+    result = pl.pallas_call(
+        functools.partial(attention_kernel, head_dim, len(kvs), n, bool(state)),
+        out_shape=out + [jax.ShapeDtypeStruct(x.shape, x.dtype) for x in passed],
+        in_specs=[SMEM] + [VMEM] * (given - 1) + [ANY] * n,
+        out_specs=[VMEM] * len(out) + [ANY] * n,
+        input_output_aliases={given + i: len(out) + i for i in range(n)},
         compiler_params=PARAMS,
     )(frame_clip, q, *kvs, *state, *passed)
-    return attn, same
-
-
-def project_kernel(n_attn, at_ref, place_ref, *refs):
-    attn_refs, w_refs = refs[:n_attn], refs[n_attn:-3]
+    return result[:len(out)], result[len(out):]
+
+
+def project_kernel(n_attn, sizes, at_ref, place_ref, *refs):
+    attn_refs, pieces = refs[:n_attn], list(refs[n_attn:-3])
     mine_ref, theirs_ref, a_ref = refs[-3:]
+    w_refs = [[pieces.pop(0) for _ in range(n)] for n in sizes]
     width = attn_refs[0].shape[1]
-    head_dim, _ = w_refs[0].shape
+    head_dim = sum(ref.shape[0] for ref in w_refs[0])
     blks, tok, cols = mine_ref.shape
     blk, core = place_ref[0] // 2, place_ref[0] % 2
     for k, ref in enumerate(attn_refs):
@@ -183,7 +202,7 @@
             a_ref[:, pl.ds(pl.multiple_of(at_ref[j] * head_dim, head_dim), head_dim)]
             for j in (i, i + 1)
         ]
-        right = [w_refs[j][...] for j in (i, i + 1)]
+        right = [ref[...] for j in (i, i + 1) for ref in w_refs[j]]
         part = jnp.dot(
             jnp.concatenate(left, axis=1), jnp.concatenate(right, axis=0),
             preferred_element_type=jnp.float32,
@@ -204,16 +223,17 @@
 
 def project(attns, w_parts, at, place, tok):
     count, width = attns[0].shape
-    blks, cols = len(attns), w_parts[0].shape[1]
+    blks, cols = len(attns), w_parts[0][0].shape[1]
+    sizes = [len(pieces) for pieces in w_parts]
     like = jax.ShapeDtypeStruct((blks, tok, cols), attns[0].dtype)
     return pl.pallas_call(
-        functools.partial(project_kernel, blks),
+        functools.partial(project_kernel, blks, sizes),
         out_shape=(like, like),
-        in_specs=[SMEM, SMEM] + [VMEM] * (blks + len(w_parts)),
+        in_specs=[SMEM, SMEM] + [VMEM] * (blks + sum(sizes)),
         out_specs=(VMEM, VMEM),
         scratch_shapes=[pltpu.VMEM((count, blks * width), attns[0].dtype)],
         compiler_params=PARAMS,
-    )(at, place, *attns, *w_parts)
+    )(at, place, *attns, *sum(w_parts, []))
 
 
 def add_kernel(place_ref, x_ref, y_ref, *out_refs):
@@ -260,14 +280,6 @@
 
 def swap_all(parts, axis):
     return [parts[0]] + [xor(x, axis, m) for m, x in enumerate(parts) if m]
-
-
-def along_rows(x):
-    rows = lax.axis_size("row")
-    if rows != 4:
-        steps = list(range(1, rows))
-        return [xor(x, ("row",), by) for by in steps], steps
-    return [xor(x, ("row",), 3), xor(x, ("row",), 1)], [3, 1]
 
 
 def on_device(qkv, frame_clip, w_out):
@@ -277,23 +289,34 @@
     head_dim = w_out.shape[0]
     blk = lax.axis_index("blk").astype(jnp.int32).reshape(1)
     place = blk * 2 + lax.axis_index("core").astype(jnp.int32)
-
-    w_own = columns(w_out, blk, blks)
-    w_others, steps = along_rows(w_own)
-
+    along = lambda x, by: xor(x, ("row",), by)
+
+    line = rows == 4
+    last = head_dim // 4
+    w_own, w_first, w_last = columns(w_out, blk, blks, (head_dim - last, last))
     packed = pack(qkv, 2 * blks, head_dim)
-    q, kv = cut(lax.all_to_all(packed, PLANE, split_axis=0, concat_axis=0, tiled=True))
-    others, _ = along_rows(kv)
-    if rows == 4:
-        others.append(xor(others[0], ("row",), 1))
-    state = attend(q, [kv] + others[:-1], frame_clip, head_dim)
-    attn, w_others = finish(q, others[-1:], state, frame_clip, head_dim, w_others)
-    if rows == 4:
-        steps.append(2)
-        w_others.append(xor(w_others[0], ("row",), 1))
+    own = lax.all_to_all(packed, PLANE, split_axis=0, concat_axis=0, tiled=True)
+    if line:
+        q, kv, (far_first, next_w) = cut(own, [along(w_first, 3), along(w_own, 1)])
+        far, near = along(kv, 3), along(kv, 1)
+        far_last = along(after(near, w_last), 3)
+        end = along(far, 1)
+        state, (far_first,) = attention(q, [kv, far, near], [], frame_clip, head_dim, [far_first])
+        end_first = along(far_first, 1)
+        (attn,), (far_last,) = attention(q, [end], state, frame_clip, head_dim, [far_last])
+        end_last = along(far_last, 1)
+        steps = [0, 1, 3, 2]
+        w_parts = [[w_own], [next_w], [far_first, far_last], [end_first, end_last]]
+    else:
+        steps = list(range(rows))
+        q, kv, _ = cut(own, [])
+        kvs = [kv] + [along(kv, by) for by in steps[1:]]
+        state, _ = attention(q, kvs[:-1], [], frame_clip, head_dim, [])
+        (attn,), _ = attention(q, kvs[-1:], state, frame_clip, head_dim, [])
+        w_parts = [[w_own]] + [[along(w_own, by)] for by in steps[1:]]
     attns = swap_all([attn] * blks, ("blk",))
-    at = jnp.stack([row] + [row ^ by for by in steps]).astype(jnp.int32)
-    mine, theirs = project(attns, [w_own] + w_others, at, place, tok)
+    at = jnp.stack([row ^ by for by in steps]).astype(jnp.int32)
+    mine, theirs = project(attns, w_parts, at, place, tok)
     parts = add(mine, xor(theirs, ("core",), 1), place)
     return unpack(swap_all(parts, ("blk",)), place)
 

time: 58.6 us -> 61.1 us (1.043)
  blocking collectives: 0 us -> 9.75 us
  starting transfers between devices: 24.9 us -> 18.2 us
  waiting for transfers between devices: 26 us -> 27.2 us
  local copies, waits for them, and re-layouts: 2.24 us -> 1.32 us
  Pallas kernels: 5.03 us -> 4.36 us
    all_to_all x0 -> x1, blocking collectives: none -> 9.75 us  [on_device(): own = lax.all_to_all(packed, PLANE, split_axis=0, concat_axis=0, tiled=True)]
    all_to_all x1 -> x0, starting transfers between devices: 5.17 us -> none  [on_device(): lax.all_to_all(packed, PLANE, split_axis=0, concat_axis=0, tiled=True)]
    ppermute x13 -> x15, waiting for transfers between devices: 25.2 us -> 27.2 us  [xor(): return lax.ppermute(x, axis, [(i, i ^ by) for i in range(size)])]
    ppermute x13 -> x15, starting transfers between devices: 19.8 us -> 18.2 us  [xor(): return lax.ppermute(x, axis, [(i, i ^ by) for i in range(size)])]
    unnamed x6, local copies, waits for them, and re-layouts: 2.24 us -> 1.32 us
    all_to_all x1 -> x0, waiting for transfers between devices: 0.75 us -> none  [on_device(): lax.all_to_all(packed, PLANE, split_axis=0, concat_axis=0, tiled=True)]
    pallas_call x1, Pallas kernels: 0.71 us -> 0.04 us  [pack(): pl.pallas_call(functools.partial(pack_kernel, head_dim), out_shape=jax.Sh...]
    pallas_call x5 -> x6, Pallas kernels: 3.49 us -> 3.5 us  [the longest x2 2.29 us: attention(): pl.pallas_call(functools.partial(attention_kernel, head_dim, len(kvs), n,...]
  transfers between devices with their start and end apart: 14 -> 15, of which waited for: 10 -> 12; matrix products, arithmetic and copies ran while one was open for 0% -> 0% of each run, Pallas kernels for 2% -> 2%
where the time goes in v8:
time: 61.1 us; the launch traced here: 61 us
  waiting for transfers between devices  27.2 us (45%)
  starting transfers between devices  18.2 us (30%)
  blocking collectives  9.75 us (16%)
  Pallas kernels  4.36 us (7%)
  local copies, waits for them, and re-layouts  1.32 us (2%)
    ppermute x15, waiting for transfers between devices, xor(): return lax.ppermute(x, axis, [(i, i ^ by) for i in range(size)])  27.2 us
    ppermute x15, starting transfers between devices, xor(): return lax.ppermute(x, axis, [(i, i ^ by) for i in range(size)])  18.2 us
    all_to_all x1, blocking collectives, on_device(): own = lax.all_to_all(packed, PLANE, split_axis=0, concat_axis=0, tiled=True)  9.75 us
    pallas_call x2, Pallas kernels, attention(): pl.pallas_call(functools.partial(attention_kernel, head_dim, len(kvs), n,...  2.29 us
    unnamed x6, local copies, waits for them, and re-layouts  1.32 us
  transfers between devices with their start and end apart: 15, of which 12 were waited for; matrix products, arithmetic and copies ran while one was open for 0% of the time, Pallas kernels for 2%

profile of v8, /device:TPU:0, one launch (start us, length us, event | category | flops | bytes accessed | tf_op | source)
XLA Modules:
  0.0 61.0 jit_solution(11547186203992536227)
XLA Ops:
  0.0 0.0 copy-start
  0.0 1.3 %copy-done = bf16[128,5120]{1,0:T(8,128)(2,1)S(1)} copy-done((bf16[128,5120]{1,0:T(8,128)(2,1)S(1)}, bf16[128,5120]{1,0:T(8,128)(2,1)}, u32[]{:S(2)}) %copy-start) | copy-done | bytes 1310744
  1.3 0.0 copy-start.1
  1.3 0.0 copy-start.2
  1.3 0.1 shard_map.38
  1.4 3.1 %collective-permute-start.1 = (bf16[128,1280]{1,0:T(8,128)(2,1)S(1)}, bf16[128,1280]{1,0:T(8,128)(2,1)S(1)}, u32[]{:S(2)}, u32[]{:S(2)}) collective-permute-start(bf16[128,1280]{1,0:T(8,128)(2,1)S(1)} %get-tuple-element.25.refs_4_), channel_id=1, source_target_pairs={{0,2},{2,0},{4,6},{6,4},{1,3},{3,1},{5,7},{7,5},{8,10},{10,8},{12,... | collective-permute-start | bytes 983048 | tf_op jit(solution)/shard_map/ppermute | solution.py:278
  4.5 2.5 %collective-permute-start = (bf16[96,1280]{1,0:T(8,128)(2,1)S(1)}, bf16[96,1280]{1,0:T(8,128)(2,1)S(1)}, u32[]{:S(2)}, u32[]{:S(2)}) collective-permute-start(bf16[96,1280]{1,0:T(8,128)(2,1)S(1)} %get-tuple-element.24), channel_id=1, source_target_pairs={{0,6},{2,4},{4,2},{6,0},{1,7},{3,5},{5,3},{7,1},{8,14},{10,12},{12... | collective-permute-start | bytes 737288 | tf_op jit(solution)/shard_map/ppermute | solution.py:278
  7.0 0.0 copy-done.1
  7.0 9.8 %all_to_all.5.x_ref = bf16[8,96,128]{2,1,0:T(8,128)(2,1)S(1)} all-to-all(bf16[8,96,128]{2,1,0:T(8,128)(2,1)S(1)} %shard_map.37), channel_id=1, replica_groups=mesh['blk'=4,'row'=4,'core'=2] {'blk','core'}, dimensions={0} | all-to-all | bytes 393216 | tf_op jit(solution)/shard_map/all_to_all | solution.py:298
  16.8 2.9 %collective-permute-done.refs_0_ = bf16[96,1280]{1,0:T(8,128)(2,1)S(1)} collective-permute-done((bf16[96,1280]{1,0:T(8,128)(2,1)S(1)}, bf16[96,1280]{1,0:T(8,128)(2,1)S(1)}, u32[]{:S(2)}, u32[]{:S(2)}) %collective-permute-start) | collective-permute-done | bytes 245792 | tf_op jit(solution)/shard_map/ppermute | solution.py:278
  19.6 0.0 collective-permute-done.1.refs_1_
  19.7 0.1 collective-permute-start.4
  19.7 1.6 %collective-permute-start.2 = (bf16[8,64,128]{2,1,0:T(8,128)(2,1)S(1)}, bf16[8,64,128]{2,1,0:T(8,128)(2,1)S(1)}, u32[]{:S(2)}, u32[]{:S(2)}) collective-permute-start(bf16[8,64,128]{2,1,0:T(8,128)(2,1)S(1)} %get-tuple-element.27.refs_0_), channel_id=1, source_target_pairs={{0,6},{2,4},{4,2},{6,0},{1,7},{3,5},{5,3},{7,1},{8,14},{10,12},{12... | collective-permute-start | bytes 393224 | tf_op jit(solution)/shard_map/ppermute | solution.py:278
  21.4 6.1 %collective-permute-done.4.refs_2_.refs_0_ = bf16[8,64,128]{2,1,0:T(8,128)(2,1)S(1)} collective-permute-done((bf16[8,64,128]{2,1,0:T(8,128)(2,1)S(1)}, bf16[8,64,128]{2,1,0:T(8,128)(2,1)S(1)}, u32[]{:S(2)}, u32[]{:S(2)}) %collective-permute-start.4) | collective-permute-done | bytes 131104 | tf_op jit(solution)/shard_map/ppermute | solution.py:278
  27.4 0.0 collective-permute-done.2.refs_1_
  27.4 0.0 copy-done.2
  27.4 1.2 %shard_map.40 = (f32[1,256,1]{2,1,0:T(8,128)S(1)}, f32[1,256,1]{2,1,0:T(8,128)S(1)}, f32[256,128]{1,0:T(8,128)S(1)}, bf16[96,1280]{1,0:T(8,128)(2,1)S(1)}) custom-call(s32[8]{0:T(128)S(1)} %copy-done.2, bf16[8,32,128]{2,1,0:T(8,128)(2,1)S(1)} %get-tuple-element.26.q_ref, ...), custom_call_target="tpu_custom_call", output_to_operand_aliasing={{3}: (5, {})} | custom-call | tf_op jit(solution)/shard_map/pallas_call | solution.py:178
  28.7 1.4 %collective-permute-start.9 = (bf16[96,1280]{1,0:T(8,128)(2,1)S(1)}, bf16[96,1280]{1,0:T(8,128)(2,1)S(1)}, u32[]{:S(2)}, u32[]{:S(2)}) collective-permute-start(bf16[96,1280]{1,0:T(8,128)(2,1)S(1)} %get-tuple-element.35.refs_6_), channel_id=1, source_target_pairs={{0,2},{2,0},{4,6},{6,4},{1,3},{3,1},{5,7},{7,5},{8,10},{10,8},{12,... | collective-permute-start | bytes 737288 | tf_op jit(solution)/shard_map/ppermute | solution.py:278
  30.0 0.7 %collective-permute-start.3 = (bf16[8,64,128]{2,1,0:T(8,128)(2,1)S(1)}, bf16[8,64,128]{2,1,0:T(8,128)(2,1)S(1)}, u32[]{:S(2)}, u32[]{:S(2)}) collective-permute-start(bf16[8,64,128]{2,1,0:T(8,128)(2,1)S(1)} %collective-permute-done.2.refs_1_), channel_id=1, source_target_pairs={{0,2},{2,0},{4,6},{6,4},{1,3},{3,1},{5,7},{7,5},{8,10},{10,8},{12,... | collective-permute-start | bytes 393224 | tf_op jit(solution)/shard_map/ppermute | solution.py:278
  30.7 1.6 %collective-permute-start.5 = (bf16[32,1280]{1,0:T(8,128)(2,1)S(1)}, bf16[32,1280]{1,0:T(8,128)(2,1)S(1)}, u32[]{:S(2)}, u32[]{:S(2)}) collective-permute-start(bf16[32,1280]{1,0:T(8,128)(2,1)S(1)} %shard_map.41), channel_id=1, source_target_pairs={{0,6},{2,4},{4,2},{6,0},{1,7},{3,5},{5,3},{7,1},{8,14},{10,12},{12... | collective-permute-start | bytes 245768 | tf_op jit(solution)/shard_map/ppermute | solution.py:278
  32.4 6.7 %collective-permute-done.5.refs_4_ = bf16[32,1280]{1,0:T(8,128)(2,1)S(1)} collective-permute-done((bf16[32,1280]{1,0:T(8,128)(2,1)S(1)}, bf16[32,1280]{1,0:T(8,128)(2,1)S(1)}, u32[]{:S(2)}, u32[]{:S(2)}) %collective-permute-start.5) | collective-permute-done | bytes 81952 | tf_op jit(solution)/shard_map/ppermute | solution.py:278
  39.1 0.7 %collective-permute-done.3.refs_0_ = bf16[8,64,128]{2,1,0:T(8,128)(2,1)S(1)} collective-permute-done((bf16[8,64,128]{2,1,0:T(8,128)(2,1)S(1)}, bf16[8,64,128]{2,1,0:T(8,128)(2,1)S(1)}, u32[]{:S(2)}, u32[]{:S(2)}) %collective-permute-start.3) | collective-permute-done | bytes 131104 | tf_op jit(solution)/shard_map/ppermute | solution.py:278
  39.8 1.1 %shard_map.42 = (bf16[256,128]{1,0:T(8,128)(2,1)S(1)}, bf16[32,1280]{1,0:T(8,128)(2,1)S(1)}) custom-call(s32[8]{0:T(128)S(1)} %copy-done.2, bf16[8,32,128]{2,1,0:T(8,128)(2,1)S(1)} %get-tuple-element.26.q_ref, bf16[8,64,128]{2,1,0:T(8,128)(2,1)S(1)} %collective-permute-done.3.refs_0_, ...), custom_call_target="tpu_custom_call", output_to_operand_aliasing={{1}: (6, {})} | custom-call | tf_op jit(solution)/shard_map/pallas_call | solution.py:178
  40.9 2.5 %collective-permute-start.8 = (bf16[256,128]{1,0:T(8,128)(2,1)S(1)}, bf16[256,128]{1,0:T(8,128)(2,1)S(1)}, u32[]{:S(2)}, u32[]{:S(2)}) collective-permute-start(bf16[256,128]{1,0:T(8,128)(2,1)S(1)} %get-tuple-element.33.refs_0_), channel_id=1, source_target_pairs={{0,24},{8,16},{16,8},{24,0},{1,25},{9,17},{17,9},{25,1},{2,26},{10... | collective-permute-start | bytes 196616 | tf_op jit(solution)/shard_map/ppermute | solution.py:278
  43.4 0.5 collective-permute-start.7
  43.9 0.5 collective-permute-start.6
  44.4 0.0 collective-permute-start.10
  44.4 0.1 pad_add_fusion.at_ref
  44.5 1.6 %collective-permute-done.8.refs_3_ = bf16[256,128]{1,0:T(8,128)(2,1)S(1)} collective-permute-done((bf16[256,128]{1,0:T(8,128)(2,1)S(1)}, bf16[256,128]{1,0:T(8,128)(2,1)S(1)}, u32[]{:S(2)}, u32[]{:S(2)}) %collective-permute-start.8) | collective-permute-done | bytes 65568 | tf_op jit(solution)/shard_map/ppermute | solution.py:278
  46.1 1.5 %collective-permute-done.7.refs_2_ = bf16[256,128]{1,0:T(8,128)(2,1)S(1)} collective-permute-done((bf16[256,128]{1,0:T(8,128)(2,1)S(1)}, bf16[256,128]{1,0:T(8,128)(2,1)S(1)}, u32[]{:S(2)}, u32[]{:S(2)}) %collective-permute-start.7) | collective-permute-done | bytes 65568 | tf_op jit(solution)/shard_map/ppermute | solution.py:278
  47.6 0.5 collective-permute-done.6.refs_1_
  48.2 0.7 %collective-permute-done.10.refs_9_ = bf16[32,1280]{1,0:T(8,128)(2,1)S(1)} collective-permute-done((bf16[32,1280]{1,0:T(8,128)(2,1)S(1)}, bf16[32,1280]{1,0:T(8,128)(2,1)S(1)}, u32[]{:S(2)}, u32[]{:S(2)}) %collective-permute-start.10) | collective-permute-done | bytes 81952 | tf_op jit(solution)/shard_map/ppermute | solution.py:278
  48.9 0.0 collective-permute-done.9.refs_8_
  48.9 1.1 %shard_map.43 = (bf16[4,32,1280]{2,1,0:T(8,128)(2,1)S(1)}, bf16[4,32,1280]{2,1,0:T(8,128)(2,1)S(1)}) custom-call(s32[4]{0:T(128)S(1)} %pad_add_fusion.at_ref, s32[1]{0:T(128)S(6)} %add.7.place_ref, bf16[256,128]{1,0:T(8,128)(2,1)S(1)} %get-tuple-element.33.refs_0_, bf16[256,128]{1,0:T(8,128)(2,1)S(1)} %collective-permute-done.6.refs_1_, ...), custom_call_target="tpu_custom_call" | custom-call | tf_op jit(solution)/shard_map/pallas_call | solution.py:229
  50.0 0.1 collective-permute-start.11
  50.1 1.6 %collective-permute-done.11.y_ref = bf16[4,32,1280]{2,1,0:T(8,128)(2,1)S(1)} collective-permute-done((bf16[4,32,1280]{2,1,0:T(8,128)(2,1)S(1)}, bf16[4,32,1280]{2,1,0:T(8,128)(2,1)S(1)}, u32[]{:S(2)}, u32[]{:S(2)}) %collective-permute-start.11) | collective-permute-done | bytes 327712 | tf_op jit(solution)/shard_map/ppermute | solution.py:278
  51.7 0.1 shard_map.44
  51.8 1.6 %collective-permute-start.12 = (bf16[32,1280]{1,0:T(8,128)(2,1)S(1)}, bf16[32,1280]{1,0:T(8,128)(2,1)S(1)}, u32[]{:S(2)}, u32[]{:S(2)}) collective-permute-start(bf16[32,1280]{1,0:T(8,128)(2,1)S(1)} %get-tuple-element.40), channel_id=1, source_target_pairs={{0,8},{8,0},{16,24},{24,16},{1,9},{9,1},{17,25},{25,17},{2,10},{10... | collective-permute-start | bytes 245768 | tf_op jit(solution)/shard_map/ppermute | solution.py:278
  53.3 1.5 %collective-permute-start.13 = (bf16[32,1280]{1,0:T(8,128)(2,1)S(1)}, bf16[32,1280]{1,0:T(8,128)(2,1)S(1)}, u32[]{:S(2)}, u32[]{:S(2)}) collective-permute-start(bf16[32,1280]{1,0:T(8,128)(2,1)S(1)} %get-tuple-element.41), channel_id=1, source_target_pairs={{0,16},{8,24},{16,0},{24,8},{1,17},{9,25},{17,1},{25,9},{2,18},{10... | collective-permute-start | bytes 245768 | tf_op jit(solution)/shard_map/ppermute | solution.py:278
  54.9 0.5 collective-permute-start.14
  55.3 1.0 %collective-permute-done.12.refs_1_ = bf16[32,1280]{1,0:T(8,128)(2,1)S(1)} collective-permute-done((bf16[32,1280]{1,0:T(8,128)(2,1)S(1)}, bf16[32,1280]{1,0:T(8,128)(2,1)S(1)}, u32[]{:S(2)}, u32[]{:S(2)}) %collective-permute-start.12) | collective-permute-done | bytes 81952 | tf_op jit(solution)/shard_map/ppermute | solution.py:278
  56.3 2.3 %collective-permute-done.13.refs_2_ = bf16[32,1280]{1,0:T(8,128)(2,1)S(1)} collective-permute-done((bf16[32,1280]{1,0:T(8,128)(2,1)S(1)}, bf16[32,1280]{1,0:T(8,128)(2,1)S(1)}, u32[]{:S(2)}, u32[]{:S(2)}) %collective-permute-start.13) | collective-permute-done | bytes 81952 | tf_op jit(solution)/shard_map/ppermute | solution.py:278
  58.6 1.6 %collective-permute-done.14.refs_3_ = bf16[32,1280]{1,0:T(8,128)(2,1)S(1)} collective-permute-done((bf16[32,1280]{1,0:T(8,128)(2,1)S(1)}, bf16[32,1280]{1,0:T(8,128)(2,1)S(1)}, u32[]{:S(2)}, u32[]{:S(2)}) %collective-permute-start.14) | collective-permute-done | bytes 81952 | tf_op jit(solution)/shard_map/ppermute | solution.py:278
  60.2 0.8 %shard_map.45 = bf16[32,5120]{1,0:T(8,128)(2,1)} custom-call(s32[1]{0:T(128)S(6)} %add.7.place_ref, bf16[32,1280]{1,0:T(8,128)(2,1)S(1)} %get-tuple-element.39.refs_0_, bf16[32,1280]{1,0:T(8,128)(2,1)S(1)} %collective-permute-done.12.refs_1_, bf16[32,1280]{1,0:T(8,128)(2,1)S(1)} %collective-permute-done.13.refs_2_, ...), custom_call_target="tpu_custom_call" | custom-call | tf_op jit(solution)/shard_map/pallas_call | solution.py:267
  (3 shorter events, 0.0 us)
Async XLA Ops:
  0.0 1.3 %copy-start = (bf16[128,5120]{1,0:T(8,128)(2,1)S(1)}, bf16[128,5120]{1,0:T(8,128)(2,1)}, u32[]{:S(2)}) copy-start(bf16[128,5120]{1,0:T(8,128)(2,1)} %x_ref.3) | copy-start | bytes 3932164
  1.3 5.6 %copy-start.1 = (bf16[3,32,1024]{2,1,0:T(8,128)(2,1)S(1)}, bf16[3,32,1024]{2,1,0:T(8,128)(2,1)}, u32[]{:S(2)}) copy-start(bf16[3,32,1024]{2,1,0:T(8,128)(2,1)} %x_ref.2) | copy-start | bytes 589828
  1.3 26.1 %copy-start.2 = (s32[8]{0:T(128)S(1)}, s32[8]{0:T(128)}, u32[]{:S(2)}) copy-start(s32[8]{0:T(128)} %clip_ref.3) | copy-start | bytes 100
  1.4 18.3 %collective-permute-start.1 = (bf16[128,1280]{1,0:T(8,128)(2,1)S(1)}, bf16[128,1280]{1,0:T(8,128)(2,1)S(1)}, u32[]{:S(2)}, u32[]{:S(2)}) collective-permute-start(bf16[128,1280]{1,0:T(8,128)(2,1)S(1)} %get-tuple-element.25.refs_4_), channel_id=1, source_target_pairs={{0,2},{2,0},{4,6},{6,4},{1,3},{3,1},{5,7},{7,5},{8,10},{10,8},{12,... | collective-permute-start | bytes 983048 | tf_op jit(solution)/shard_map/ppermute | solution.py:278
  4.5 15.2 %collective-permute-start = (bf16[96,1280]{1,0:T(8,128)(2,1)S(1)}, bf16[96,1280]{1,0:T(8,128)(2,1)S(1)}, u32[]{:S(2)}, u32[]{:S(2)}) collective-permute-start(bf16[96,1280]{1,0:T(8,128)(2,1)S(1)} %get-tuple-element.24), channel_id=1, source_target_pairs={{0,6},{2,4},{4,2},{6,0},{1,7},{3,5},{5,3},{7,1},{8,14},{10,12},{12... | collective-permute-start | bytes 737288 | tf_op jit(solution)/shard_map/ppermute | solution.py:278
  19.7 7.8 %collective-permute-start.4 = (bf16[8,64,128]{2,1,0:T(8,128)(2,1)S(1)}, bf16[8,64,128]{2,1,0:T(8,128)(2,1)S(1)}, u32[]{:S(2)}, u32[]{:S(2)}) collective-permute-start(bf16[8,64,128]{2,1,0:T(8,128)(2,1)S(1)} %get-tuple-element.27.refs_0_), channel_id=1, source_target_pairs={{0,2},{2,0},{4,6},{6,4},{1,3},{3,1},{5,7},{7,5},{8,10},{10,8},{12,... | collective-permute-start | bytes 393224 | tf_op jit(solution)/shard_map/ppermute | solution.py:278
  19.7 7.7 %collective-permute-start.2 = (bf16[8,64,128]{2,1,0:T(8,128)(2,1)S(1)}, bf16[8,64,128]{2,1,0:T(8,128)(2,1)S(1)}, u32[]{:S(2)}, u32[]{:S(2)}) collective-permute-start(bf16[8,64,128]{2,1,0:T(8,128)(2,1)S(1)} %get-tuple-element.27.refs_0_), channel_id=1, source_target_pairs={{0,6},{2,4},{4,2},{6,0},{1,7},{3,5},{5,3},{7,1},{8,14},{10,12},{12... | collective-permute-start | bytes 393224 | tf_op jit(solution)/shard_map/ppermute | solution.py:278
  28.7 20.2 %collective-permute-start.9 = (bf16[96,1280]{1,0:T(8,128)(2,1)S(1)}, bf16[96,1280]{1,0:T(8,128)(2,1)S(1)}, u32[]{:S(2)}, u32[]{:S(2)}) collective-permute-start(bf16[96,1280]{1,0:T(8,128)(2,1)S(1)} %get-tuple-element.35.refs_6_), channel_id=1, source_target_pairs={{0,2},{2,0},{4,6},{6,4},{1,3},{3,1},{5,7},{7,5},{8,10},{10,8},{12,... | collective-permute-start | bytes 737288 | tf_op jit(solution)/shard_map/ppermute | solution.py:278
  30.0 9.8 %collective-permute-start.3 = (bf16[8,64,128]{2,1,0:T(8,128)(2,1)S(1)}, bf16[8,64,128]{2,1,0:T(8,128)(2,1)S(1)}, u32[]{:S(2)}, u32[]{:S(2)}) collective-permute-start(bf16[8,64,128]{2,1,0:T(8,128)(2,1)S(1)} %collective-permute-done.2.refs_1_), channel_id=1, source_target_pairs={{0,2},{2,0},{4,6},{6,4},{1,3},{3,1},{5,7},{7,5},{8,10},{10,8},{12,... | collective-permute-start | bytes 393224 | tf_op jit(solution)/shard_map/ppermute | solution.py:278
  30.7 8.3 %collective-permute-start.5 = (bf16[32,1280]{1,0:T(8,128)(2,1)S(1)}, bf16[32,1280]{1,0:T(8,128)(2,1)S(1)}, u32[]{:S(2)}, u32[]{:S(2)}) collective-permute-start(bf16[32,1280]{1,0:T(8,128)(2,1)S(1)} %shard_map.41), channel_id=1, source_target_pairs={{0,6},{2,4},{4,2},{6,0},{1,7},{3,5},{5,3},{7,1},{8,14},{10,12},{12... | collective-permute-start | bytes 245768 | tf_op jit(solution)/shard_map/ppermute | solution.py:278
  40.9 5.2 %collective-permute-start.8 = (bf16[256,128]{1,0:T(8,128)(2,1)S(1)}, bf16[256,128]{1,0:T(8,128)(2,1)S(1)}, u32[]{:S(2)}, u32[]{:S(2)}) collective-permute-start(bf16[256,128]{1,0:T(8,128)(2,1)S(1)} %get-tuple-element.33.refs_0_), channel_id=1, source_target_pairs={{0,24},{8,16},{16,8},{24,0},{1,25},{9,17},{17,9},{25,1},{2,26},{10... | collective-permute-start | bytes 196616 | tf_op jit(solution)/shard_map/ppermute | solution.py:278
  43.4 4.3 %collective-permute-start.7 = (bf16[256,128]{1,0:T(8,128)(2,1)S(1)}, bf16[256,128]{1,0:T(8,128)(2,1)S(1)}, u32[]{:S(2)}, u32[]{:S(2)}) collective-permute-start(bf16[256,128]{1,0:T(8,128)(2,1)S(1)} %get-tuple-element.33.refs_0_), channel_id=1, source_target_pairs={{0,16},{8,24},{16,0},{24,8},{1,17},{9,25},{17,1},{25,9},{2,18},{10... | collective-permute-start | bytes 196616 | tf_op jit(solution)/shard_map/ppermute | solution.py:278
  43.9 4.3 %collective-permute-start.6 = (bf16[256,128]{1,0:T(8,128)(2,1)S(1)}, bf16[256,128]{1,0:T(8,128)(2,1)S(1)}, u32[]{:S(2)}, u32[]{:S(2)}) collective-permute-start(bf16[256,128]{1,0:T(8,128)(2,1)S(1)} %get-tuple-element.33.refs_0_), channel_id=1, source_target_pairs={{0,8},{8,0},{16,24},{24,16},{1,9},{9,1},{17,25},{25,17},{2,10},{10... | collective-permute-start | bytes 196616 | tf_op jit(solution)/shard_map/ppermute | solution.py:278
  44.4 4.4 %collective-permute-start.10 = (bf16[32,1280]{1,0:T(8,128)(2,1)S(1)}, bf16[32,1280]{1,0:T(8,128)(2,1)S(1)}, u32[]{:S(2)}, u32[]{:S(2)}) collective-permute-start(bf16[32,1280]{1,0:T(8,128)(2,1)S(1)} %get-tuple-element.36.refs_7_), channel_id=1, source_target_pairs={{0,2},{2,0},{4,6},{6,4},{1,3},{3,1},{5,7},{7,5},{8,10},{10,8},{12,... | collective-permute-start | bytes 245768 | tf_op jit(solution)/shard_map/ppermute | solution.py:278
  50.0 1.7 %collective-permute-start.11 = (bf16[4,32,1280]{2,1,0:T(8,128)(2,1)S(1)}, bf16[4,32,1280]{2,1,0:T(8,128)(2,1)S(1)}, u32[]{:S(2)}, u32[]{:S(2)}) collective-permute-start(bf16[4,32,1280]{2,1,0:T(8,128)(2,1)S(1)} %get-tuple-element.38), channel_id=1, source_target_pairs={{0,1},{1,0},{2,3},{3,2},{4,5},{5,4},{6,7},{7,6},{8,9},{9,8},{10,11... | collective-permute-start | bytes 983048 | tf_op jit(solution)/shard_map/ppermute | solution.py:278
  51.8 4.6 %collective-permute-start.12 = (bf16[32,1280]{1,0:T(8,128)(2,1)S(1)}, bf16[32,1280]{1,0:T(8,128)(2,1)S(1)}, u32[]{:S(2)}, u32[]{:S(2)}) collective-permute-start(bf16[32,1280]{1,0:T(8,128)(2,1)S(1)} %get-tuple-element.40), channel_id=1, source_target_pairs={{0,8},{8,0},{16,24},{24,16},{1,9},{9,1},{17,25},{25,17},{2,10},{10... | collective-permute-start | bytes 245768 | tf_op jit(solution)/shard_map/ppermute | solution.py:278
  53.3 5.3 %collective-permute-start.13 = (bf16[32,1280]{1,0:T(8,128)(2,1)S(1)}, bf16[32,1280]{1,0:T(8,128)(2,1)S(1)}, u32[]{:S(2)}, u32[]{:S(2)}) collective-permute-start(bf16[32,1280]{1,0:T(8,128)(2,1)S(1)} %get-tuple-element.41), channel_id=1, source_target_pairs={{0,16},{8,24},{16,0},{24,8},{1,17},{9,25},{17,1},{25,9},{2,18},{10... | collective-permute-start | bytes 245768 | tf_op jit(solution)/shard_map/ppermute | solution.py:278
  54.9 5.3 %collective-permute-start.14 = (bf16[32,1280]{1,0:T(8,128)(2,1)S(1)}, bf16[32,1280]{1,0:T(8,128)(2,1)S(1)}, u32[]{:S(2)}, u32[]{:S(2)}) collective-permute-start(bf16[32,1280]{1,0:T(8,128)(2,1)S(1)} %get-tuple-element.42), channel_id=1, source_target_pairs={{0,24},{8,16},{16,8},{24,0},{1,25},{9,17},{17,9},{25,1},{2,26},{10... | collective-permute-start | bytes 245768 | tf_op jit(solution)/shard_map/ppermute | solution.py:278

commit v9 on v8

v9 whole, which is shorter than its diff:
```python
import functools
import math

import jax
import jax.numpy as jnp
from jax import lax
from jax.experimental import pallas as pl
from jax.experimental.pallas import tpu as pltpu
from jax.sharding import Mesh
from jax.sharding import PartitionSpec as P

FRB = 2
TPF = 16
VMEM = pl.BlockSpec(memory_space=pltpu.VMEM)
SMEM = pl.BlockSpec(memory_space=pltpu.SMEM)
ANY = pl.BlockSpec(memory_space=pl.ANY)
AHEAD = pl.CostEstimate(flops=20_000_000_000, bytes_accessed=1_000_000, transcendentals=0)
PARAMS = pltpu.CompilerParams(vmem_limit_bytes=48 * 1024 * 1024)


def pack_kernel(head_dim, x_ref, out_ref):
    peers, _, width = out_ref.shape
    kinds, tok, _ = x_ref.shape
    heads = width // head_dim
    for g in range(peers):
        for i in range(heads):
            head = (g // 2 * heads + i) * 2 + g % 2
            for k in range(kinds):
                out_ref[g, k * tok:(k + 1) * tok, i * head_dim:(i + 1) * head_dim] = x_ref[
                    k, :, head * head_dim:(head + 1) * head_dim
                ]


def pack(x, peers, head_dim):
    kinds, tok, cols = x.shape
    return pl.pallas_call(
        functools.partial(pack_kernel, head_dim),
        out_shape=jax.ShapeDtypeStruct((peers, kinds * tok, cols // peers), x.dtype),
        in_specs=[VMEM],
        out_specs=VMEM,
        compiler_params=PARAMS,
    )(x)


def columns_kernel(at_ref, x_ref, *refs):
    *out_refs, sems = refs
    copies = []
    for i, ref in enumerate(out_refs):
        depth, cols = ref.shape
        first = pl.multiple_of(at_ref[2 * i] * depth, depth)
        start = pl.multiple_of(at_ref[2 * i + 1] * cols, cols)
        copies.append(
            pltpu.make_async_copy(
                x_ref.at[pl.ds(first, depth), pl.ds(start, cols)], ref, sems.at[i]
            )
        )
    for copy in copies:
        copy.start()
    for copy in copies:
        copy.wait()


def columns(x, pieces, cols):
    at = jnp.stack([jnp.asarray(i, jnp.int32) for piece in pieces for i in piece[1:]])
    return pl.pallas_call(
        columns_kernel,
        out_shape=[jax.ShapeDtypeStruct((piece[0], cols), x.dtype) for piece in pieces],
        in_specs=[SMEM, pl.BlockSpec(memory_space=pltpu.HBM)],
        out_specs=[VMEM] * len(pieces),
        scratch_shapes=[pltpu.SemaphoreType.DMA((len(pieces),))],
        compiler_params=PARAMS,
    )(at, x)


def cut_kernel(x_ref, *refs):
    q_ref, kv_ref = refs[len(refs) // 2 - 1:][:2]
    tok = q_ref.shape[1]
    q_ref[...] = x_ref[:, :tok, :]
    kv_ref[...] = x_ref[:, tok:, :]


def cut(x, passed):
    peers, depth, width = x.shape
    tok, n = depth // 3, len(passed)
    q, kv, *same = pl.pallas_call(
        cut_kernel,
        out_shape=[
            jax.ShapeDtypeStruct((peers, tok, width), x.dtype),
            jax.ShapeDtypeStruct((peers, 2 * tok, width), x.dtype),
        ] + [jax.ShapeDtypeStruct(y.shape, y.dtype) for y in passed],
        in_specs=[VMEM] + [ANY] * n,
        out_specs=[VMEM, VMEM] + [ANY] * n,
        input_output_aliases={1 + i: 2 + i for i in range(n)},
        compiler_params=PARAMS,
    )(x, *passed)
    return q, kv, same


def after_kernel(*refs):
    pass


def after(x, passed):
    return pl.pallas_call(
        after_kernel,
        out_shape=jax.ShapeDtypeStruct(passed.shape, passed.dtype),
        in_specs=[ANY, ANY],
        out_specs=ANY,
        input_output_aliases={1: 0},
        compiler_params=PARAMS,
    )(x, passed)


def clip_of(token, base, span, tok_dev, clip_ref):
    frame = base + token // span * FRB + token % tok_dev // TPF
    clip = jnp.zeros_like(token)
    for f in range(clip_ref.shape[0]):
        clip = jnp.where(frame == f, clip_ref[f], clip)
    return clip


def attention_kernel(head_dim, span, base_ref, clip_ref, q_ref, *refs):
    *kv_refs, out_ref = refs
    peers, tok, width = q_ref.shape
    count = peers * tok
    scale = 1.0 / math.sqrt(head_dim)
    row = lax.broadcasted_iota(jnp.int32, (count, 1), 0)
    col = lax.broadcasted_iota(jnp.int32, (1, count), 1)
    row_clip = clip_of(row, base_ref[0], span, tok, clip_ref)
    per_step = max(1, 1024 // count)
    for h in range(width // head_dim):
        cols = slice(h * head_dim, (h + 1) * head_dim)
        queries = q_ref[:, :, cols].reshape(count, head_dim)
        top = total = acc = None
        for first in range(0, len(kv_refs), per_step):
            scores, masks, values = [], [], []
            for i, ref in enumerate(kv_refs[first:first + per_step], first):
                keys = ref[:, 0:tok, cols].reshape(count, head_dim)
                values.append(ref[:, tok:2 * tok, cols].reshape(count, head_dim))
                s = lax.dot_general(
                    queries, keys, (((1,), (1,)), ((), ())), preferred_element_type=jnp.float32
                )
                masks.append(row_clip == clip_of(col, base_ref[i], span, tok, clip_ref))
                scores.append(jnp.where(masks[-1], s * scale, -1e30))
            new_top = functools.reduce(
                jnp.maximum, [jnp.max(s, axis=1, keepdims=True) for s in scores]
            )
            if top is not None:
                new_top = jnp.maximum(top, new_top)
                factor = jnp.exp(top - new_top)
                total, acc = total * factor, acc * factor
            top = new_top
            for s, allowed, v in zip(scores, masks, values):
                p = jnp.where(allowed, jnp.exp(s - top), 0.0)
                part = jnp.sum(p, axis=1, keepdims=True)
                dot = jnp.dot(p.astype(jnp.bfloat16), v, preferred_element_type=jnp.float32)
                total = part if total is None else total + part
                acc = dot if acc is None else acc + dot
        out_ref[:, cols] = (acc / total).astype(out_ref.dtype)


def attention(q, kvs, bases, span, frame_clip, head_dim):
    peers, tok, width = q.shape
    return pl.pallas_call(
        functools.partial(attention_kernel, head_dim, span),
        out_shape=jax.ShapeDtypeStruct((peers * tok, width), q.dtype),
        in_specs=[SMEM, SMEM] + [VMEM] * (1 + len(kvs)),
        out_specs=VMEM,
        compiler_params=PARAMS,
        cost_estimate=AHEAD,
    )(jnp.stack([jnp.asarray(i, jnp.int32) for i in bases]), frame_clip, q, *kvs)


def project_kernel(n_attn, at_ref, place_ref, *refs):
    attn_refs, w_refs = refs[:n_attn], refs[n_attn:-4]
    mine_ref, theirs_ref, a_ref, w_all = refs[-4:]
    width = attn_refs[0].shape[1]
    blks, tok, cols = mine_ref.shape
    blk, core = place_ref[0] // 2, place_ref[0] % 2
    for k, ref in enumerate(attn_refs):
        a_ref[:, pl.ds(pl.multiple_of((blk ^ k) * width, width), width)] = ref[...]
    for i, ref in enumerate(w_refs):
        rows = ref.shape[0]
        w_all[pl.ds(pl.multiple_of(at_ref[i] * rows, rows), rows), :] = ref[...]
    result = jnp.dot(a_ref[...], w_all[...], preferred_element_type=jnp.float32)
    result = result.astype(mine_ref.dtype).reshape(blks, 2, tok, cols)

    @pl.when(core == 0)
    def _():
        mine_ref[...] = result[:, 0]
        theirs_ref[...] = result[:, 1]

    @pl.when(core != 0)
    def _():
        mine_ref[...] = result[:, 1]
        theirs_ref[...] = result[:, 0]


def project(attns, w_parts, at, place, tok):
    count, width = attns[0].shape
    blks, cols = len(attns), w_parts[0].shape[1]
    like = jax.ShapeDtypeStruct((blks, tok, cols), attns[0].dtype)
    return pl.pallas_call(
        functools.partial(project_kernel, blks),
        out_shape=(like, like),
        in_specs=[SMEM, SMEM] + [VMEM] * (blks + len(w_parts)),
        out_specs=(VMEM, VMEM),
        scratch_shapes=[
            pltpu.VMEM((count, blks * width), attns[0].dtype),
            pltpu.VMEM((blks * width, cols), attns[0].dtype),
        ],
        compiler_params=PARAMS,
    )(jnp.stack(at).astype(jnp.int32), place, *attns, *w_parts)


def add_kernel(place_ref, x_ref, y_ref, *out_refs):
    for k, out_ref in enumerate(out_refs):
        at = place_ref[0] // 2 ^ k
        both = x_ref[at].astype(jnp.float32) + y_ref[at].astype(jnp.float32)
        out_ref[...] = both.astype(out_ref.dtype)


def add(x, y, place):
    blks = x.shape[0]
    return pl.pallas_call(
        add_kernel,
        out_shape=[jax.ShapeDtypeStruct(x.shape[1:], x.dtype)] * blks,
        in_specs=[SMEM, VMEM, VMEM],
        out_specs=[VMEM] * blks,
        compiler_params=PARAMS,
    )(place, x, y)


def unpack_kernel(place_ref, *refs):
    *in_refs, out_ref = refs
    width = in_refs[0].shape[1]
    for k, ref in enumerate(in_refs):
        at = place_ref[0] // 2 ^ k
        out_ref[:, pl.ds(pl.multiple_of(at * width, width), width)] = ref[...]


def unpack(parts, place):
    tok, width = parts[0].shape
    return pl.pallas_call(
        unpack_kernel,
        out_shape=jax.ShapeDtypeStruct((tok, len(parts) * width), parts[0].dtype),
        in_specs=[SMEM] + [VMEM] * len(parts),
        out_specs=VMEM,
        compiler_params=PARAMS,
    )(place, *parts)


def xor(x, axis, by):
    size = math.prod(lax.axis_size(name) for name in axis)
    return lax.ppermute(x, axis, [(i, i ^ by) for i in range(size)])


def swap_all(parts, axis):
    return [parts[0]] + [xor(x, axis, m) for m, x in enumerate(parts) if m]


def squares(qkv, frame_clip, w_out):
    group, quarter = ("x", "zl", "core"), ("x", "zl")
    y, x, zh, zl, core = (lax.axis_index(n) for n in ("y", "x", "zh", "zl", "core"))
    tok, head_dim, cols = qkv.shape[1], w_out.shape[0], w_out.shape[1] // 4
    place = ((x * 2 + zl) * 2 + core).astype(jnp.int32).reshape(1)
    mine, theirs = x * 2 + zl, x * 2 + 1 - zl
    row, half = zh * 2 + zl, head_dim // 2

    w_own, w_far, w_corner, w_near = columns(
        w_out,
        [(head_dim, 0, mine), (half, y, mine), (half, y, theirs), (head_dim, 0, theirs)],
        cols,
    )
    far = xor(w_far, ("zh",), 1)
    near = xor(w_near, ("zl",), 1)
    packed = pack(qkv, 8, head_dim)
    own = lax.all_to_all(packed, group, split_axis=0, concat_axis=0, tiled=True)
    q, kv, (far, w_corner) = cut(own, [far, w_corner])
    kv_far, kv_near = xor(kv, ("zh",), 1), xor(kv, ("y",), 1)
    corner = xor(w_corner, ("zh", "zl"), 3)
    far_rest = xor(far, ("y",), 1)
    kv_end = xor(kv_far, ("y",), 1)

    base, other = y * 2 * FRB, (1 - y) * 2 * FRB
    attn = attention(
        q, [kv, kv_far, kv_near, kv_end], [base, base, other, other], 4 * tok, frame_clip, head_dim
    )
    corner = after(attn, corner)
    corner_rest = xor(corner, ("y",), 1)
    attns = swap_all([attn] * 4, quarter)
    w_parts = [w_own, near, far, far_rest, corner, corner_rest]
    at = [row, row ^ 1] + [2 * (row ^ by) + h for by in (2, 3) for h in (y, 1 - y)]
    ours, other_core = project(attns, w_parts, at, place, tok)
    parts = add(ours, xor(other_core, ("core",), 1), place)
    return unpack(swap_all(parts, quarter), place)


def layers(qkv, frame_clip, w_out):
    rows, blks = lax.axis_size("row"), lax.axis_size("blk")
    row, blk = lax.axis_index("row"), lax.axis_index("blk")
    tok, head_dim, cols = qkv.shape[1], w_out.shape[0], w_out.shape[1] // blks
    place = (blk * 2 + lax.axis_index("core")).astype(jnp.int32).reshape(1)
    others = range(1, rows)

    (w_own,) = columns(w_out, [(head_dim, 0, blk)], cols)
    w_parts = [w_own] + [xor(w_own, ("row",), by) for by in others]
    packed = pack(qkv, 2 * blks, head_dim)
    own = lax.all_to_all(packed, ("blk", "core"), split_axis=0, concat_axis=0, tiled=True)
    q, kv, _ = cut(own, [])
    kvs = [kv] + [xor(kv, ("row",), by) for by in others]
    attn = attention(q, kvs, [0] * rows, 2 * tok, frame_clip, head_dim)
    attns = swap_all([attn] * blks, ("blk",))
    ours, other_core = project(attns, w_parts, [row ^ by for by in range(rows)], place, tok)
    parts = add(ours, xor(other_core, ("core",), 1), place)
    return unpack(swap_all(parts, ("blk",)), place)


def solution(mesh):
    blk, tile = mesh.shape["blk"], mesh.shape["tile"]
    if (blk, tile) == (4, 8):
        plan, names, shape = squares, ("y", "x", "zh", "zl", "core"), (2, 2, 2, 2, 2)
    else:
        plan, names, shape = layers, ("blk", "row", "core"), (blk, tile // 2, 2)
    fine = Mesh(mesh.devices.reshape(shape), names)
    tiles = names[2:] if plan is squares else names[1:]
    in_specs = (P(None, names, None), P(), P(tiles, None))
    return jax.shard_map(
        plan, mesh=fine, in_specs=in_specs, out_specs=P(names, None), check_vma=False
    )
```

time: 61.1 us -> 61.2 us (level)
  blocking collectives: 9.75 us -> 0 us
  waiting for transfers between devices: 27.2 us -> 33.1 us
  starting transfers between devices: 18.2 us -> 20.4 us
  local copies, waits for them, and re-layouts: 1.32 us -> 2.42 us
    all_to_all x1 -> x0, blocking collectives: 9.75 us -> none  [on_device(): own = lax.all_to_all(packed, PLANE, split_axis=0, concat_axis=0, tiled=True)]
    ppermute x15, waiting for transfers between devices: 27.2 us -> 33.1 us  [xor(): return lax.ppermute(x, axis, [(i, i ^ by) for i in range(size)])]
    all_to_all x0 -> x1, starting transfers between devices: none -> 5.23 us  [squares(): own = lax.all_to_all(packed, group, split_axis=0, concat_axis=0, tiled=True)]
    ppermute x15, starting transfers between devices: 18.2 us -> 15.2 us  [xor(): return lax.ppermute(x, axis, [(i, i ^ by) for i in range(size)])]
    unnamed x6, local copies, waits for them, and re-layouts: 1.32 us -> 2.25 us
    pallas_call x1, Pallas kernels: 0.04 us -> 0.71 us  [pack(): pl.pallas_call(functools.partial(pack_kernel, head_dim), out_shape=jax.Sh...]
    pallas_call x4 -> x3, Pallas kernels: 3.48 us -> 3.22 us  [the longest x1 1.3 us: attention(): pl.pallas_call(functools.partial(attention_kernel, head_dim, span), out_s...]
  transfers between devices with their start and end apart: 15 -> 16, of which waited for: 12 -> 10; matrix products, arithmetic and copies ran while one was open for 0% -> 0% of each run, Pallas kernels for 2% -> 3%
where the time goes in v9:
time: 61.2 us; the launch traced here: 60.9 us
  waiting for transfers between devices  33.1 us (54%)
  starting transfers between devices  20.4 us (33%)
  Pallas kernels  4.78 us (8%)
  local copies, waits for them, and re-layouts  2.42 us (4%)
    ppermute x15, waiting for transfers between devices, xor(): return lax.ppermute(x, axis, [(i, i ^ by) for i in range(size)])  33.1 us
    ppermute x15, starting transfers between devices, xor(): return lax.ppermute(x, axis, [(i, i ^ by) for i in range(size)])  15.2 us
    all_to_all x1, starting transfers between devices, squares(): own = lax.all_to_all(packed, group, split_axis=0, concat_axis=0, tiled=True)  5.23 us
    unnamed x6, local copies, waits for them, and re-layouts  2.25 us
    pallas_call x1, Pallas kernels, attention(): pl.pallas_call(functools.partial(attention_kernel, head_dim, span), out_s...  1.3 us
  transfers between devices with their start and end apart: 16, of which 10 were waited for; matrix products, arithmetic and copies ran while one was open for 0% of the time, Pallas kernels for 3%

profile of v9, /device:TPU:0, one launch (start us, length us, event | category | flops | bytes accessed | tf_op | source)
XLA Modules:
  0.0 60.9 jit_solution(8711541561177193754)
XLA Ops:
  0.0 0.0 copy-start.1
  0.0 0.9 %copy-done.1 = bf16[3,32,1024]{2,1,0:T(8,128)(2,1)S(1)} copy-done((bf16[3,32,1024]{2,1,0:T(8,128)(2,1)S(1)}, bf16[3,32,1024]{2,1,0:T(8,128)(2,1)}, u32[]{:S(2)}) %copy-start.1) | copy-done | bytes 196632
  0.9 0.0 copy-start.2
  0.9 0.7 %shard_map.37 = bf16[8,96,128]{2,1,0:T(8,128)(2,1)} custom-call(bf16[3,32,1024]{2,1,0:T(8,128)(2,1)S(1)} %copy-done.1), custom_call_target="tpu_custom_call" | custom-call | tf_op jit(solution)/shard_map/pallas_call | solution.py:36
  1.6 5.2 %all-to-all-start = ((bf16[8,96,128]{2,1,0:T(8,128)(2,1)}), bf16[8,96,128]{2,1,0:T(8,128)(2,1)S(1)}, u32[]{:S(2)}, u32[]{:S(2)}) async-start(bf16[8,96,128]{2,1,0:T(8,128)(2,1)} %shard_map.37), calls=%async_computation | async-start | bytes 393216 | tf_op jit(solution)/shard_map/all_to_all | solution.py:278
  6.9 0.1 stack.60.at_ref
  7.0 0.0 copy-start
  7.0 1.3 %copy-done = bf16[128,5120]{1,0:T(8,128)(2,1)S(1)} copy-done((bf16[128,5120]{1,0:T(8,128)(2,1)S(1)}, bf16[128,5120]{1,0:T(8,128)(2,1)}, u32[]{:S(2)}) %copy-start) | copy-done | bytes 1310744
  8.3 0.7 %shard_map.38 = (bf16[128,1280]{1,0:T(8,128)(2,1)S(1)}, bf16[64,1280]{1,0:T(8,128)(2,1)S(1)}, bf16[64,1280]{1,0:T(8,128)(2,1)S(1)}, bf16[128,1280]{1,0:T(8,128)(2,1)S(1)}) custom-call(s32[8]{0:T(128)S(1)} %stack.60.at_ref, bf16[128,5120]{1,0:T(8,128)(2,1)S(1)} %copy-done), custom_call_target="tpu_custom_call" | custom-call | tf_op jit(solution)/shard_map/pallas_call | solution.py:65
  9.0 2.7 %collective-permute-start = (bf16[64,1280]{1,0:T(8,128)(2,1)S(1)}, bf16[64,1280]{1,0:T(8,128)(2,1)S(1)}, u32[]{:S(2)}, u32[]{:S(2)}) collective-permute-start(bf16[64,1280]{1,0:T(8,128)(2,1)S(1)} %get-tuple-element.19), channel_id=1, source_target_pairs={{0,4},{4,0},{1,5},{5,1},{2,6},{6,2},{3,7},{7,3},{8,12},{12,8},{9,1... | collective-permute-start | bytes 491528 | tf_op jit(solution)/shard_map/ppermute | solution.py:255
  11.6 8.4 %collective-permute-done.refs_0_ = bf16[64,1280]{1,0:T(8,128)(2,1)S(1)} collective-permute-done((bf16[64,1280]{1,0:T(8,128)(2,1)S(1)}, bf16[64,1280]{1,0:T(8,128)(2,1)S(1)}, u32[]{:S(2)}, u32[]{:S(2)}) %collective-permute-start) | collective-permute-done | bytes 163872 | tf_op jit(solution)/shard_map/ppermute | solution.py:255
  20.1 0.0 all-to-all-done.x_ref
  20.1 0.1 collective-permute-start.1
  20.2 1.6 %collective-permute-start.2 = (bf16[8,64,128]{2,1,0:T(8,128)(2,1)S(1)}, bf16[8,64,128]{2,1,0:T(8,128)(2,1)S(1)}, u32[]{:S(2)}, u32[]{:S(2)}) collective-permute-start(bf16[8,64,128]{2,1,0:T(8,128)(2,1)S(1)} %get-tuple-element.22.refs_0_), channel_id=1, source_target_pairs={{0,16},{16,0},{1,17},{17,1},{2,18},{18,2},{3,19},{19,3},{4,20},{20... | collective-permute-start | bytes 393224 | tf_op jit(solution)/shard_map/ppermute | solution.py:255
  21.8 7.2 %collective-permute-done.1.refs_1_ = bf16[8,64,128]{2,1,0:T(8,128)(2,1)S(1)} collective-permute-done((bf16[8,64,128]{2,1,0:T(8,128)(2,1)S(1)}, bf16[8,64,128]{2,1,0:T(8,128)(2,1)S(1)}, u32[]{:S(2)}, u32[]{:S(2)}) %collective-permute-start.1) | collective-permute-done | bytes 131104 | tf_op jit(solution)/shard_map/ppermute | solution.py:255
  29.0 1.5 %collective-permute-start.3 = (bf16[8,64,128]{2,1,0:T(8,128)(2,1)S(1)}, bf16[8,64,128]{2,1,0:T(8,128)(2,1)S(1)}, u32[]{:S(2)}, u32[]{:S(2)}) collective-permute-start(bf16[8,64,128]{2,1,0:T(8,128)(2,1)S(1)} %collective-permute-done.1.refs_1_), channel_id=1, source_target_pairs={{0,16},{16,0},{1,17},{17,1},{2,18},{18,2},{3,19},{19,3},{4,20},{20... | collective-permute-start | bytes 393224 | tf_op jit(solution)/shard_map/ppermute | solution.py:255
  30.5 0.0 collective-permute-start.7
  30.5 0.1 pad_add_fusion.base_ref
  30.6 1.2 %collective-permute-start.9 = (bf16[64,1280]{1,0:T(8,128)(2,1)S(1)}, bf16[64,1280]{1,0:T(8,128)(2,1)S(1)}, u32[]{:S(2)}, u32[]{:S(2)}) collective-permute-start(bf16[64,1280]{1,0:T(8,128)(2,1)S(1)} %get-tuple-element.26), channel_id=1, source_target_pairs={{0,6},{2,4},{4,2},{6,0},{1,7},{3,5},{5,3},{7,1},{8,14},{10,12},{12... | collective-permute-start | bytes 491528 | tf_op jit(solution)/shard_map/ppermute | solution.py:255
  31.8 0.5 collective-permute-start.8
  32.3 0.0 collective-permute-done.2.refs_2_
  32.3 2.5 %collective-permute-done.3.refs_3_ = bf16[8,64,128]{2,1,0:T(8,128)(2,1)S(1)} collective-permute-done((bf16[8,64,128]{2,1,0:T(8,128)(2,1)S(1)}, bf16[8,64,128]{2,1,0:T(8,128)(2,1)S(1)}, u32[]{:S(2)}, u32[]{:S(2)}) %collective-permute-start.3) | collective-permute-done | bytes 131104 | tf_op jit(solution)/shard_map/ppermute | solution.py:255
  34.8 0.0 copy-done.2
  34.8 1.3 %shard_map.40.refs_0_ = bf16[256,128]{1,0:T(8,128)(2,1)S(1)} custom-call(s32[4]{0:T(128)S(1)} %pad_add_fusion.base_ref, s32[8]{0:T(128)S(1)} %copy-done.2, bf16[8,32,128]{2,1,0:T(8,128)(2,1)S(1)} %get-tuple-element.21.q_ref, bf16[8,64,128]{2,1,0:T(8,128)(2,1)S(1)} %get-tuple-element.22.refs_0_, bf16[8,64,128]{2,1,0:T(8,128)(2,1)S(1)} %collective-permute-done.1.refs_1_, ...), custom_call_target="tpu_custom_call" | custom-call | flops 20000000000 | bytes 1000000 | tf_op jit(solution)/shard_map/pallas_call | solution.py:164
  36.1 6.1 %collective-permute-done.9.refs_1_ = bf16[64,1280]{1,0:T(8,128)(2,1)S(1)} collective-permute-done((bf16[64,1280]{1,0:T(8,128)(2,1)S(1)}, bf16[64,1280]{1,0:T(8,128)(2,1)S(1)}, u32[]{:S(2)}, u32[]{:S(2)}) %collective-permute-start.9) | collective-permute-done | bytes 163872 | tf_op jit(solution)/shard_map/ppermute | solution.py:255
  42.2 0.5 collective-permute-start.10
  42.7 0.0 collective-permute-start.6
  42.7 1.3 %collective-permute-start.5 = (bf16[256,128]{1,0:T(8,128)(2,1)S(1)}, bf16[256,128]{1,0:T(8,128)(2,1)S(1)}, u32[]{:S(2)}, u32[]{:S(2)}) collective-permute-start(bf16[256,128]{1,0:T(8,128)(2,1)S(1)} %shard_map.40.refs_0_), channel_id=1, source_target_pairs={{0,8},{2,10},{8,0},{10,2},{1,9},{3,11},{9,1},{11,3},{4,12},{6,14},... | collective-permute-start | bytes 196616 | tf_op jit(solution)/shard_map/ppermute | solution.py:255
  44.0 0.0 collective-permute-done.7.refs_5_
  44.0 2.2 %collective-permute-start.4 = (bf16[256,128]{1,0:T(8,128)(2,1)S(1)}, bf16[256,128]{1,0:T(8,128)(2,1)S(1)}, u32[]{:S(2)}, u32[]{:S(2)}) collective-permute-start(bf16[256,128]{1,0:T(8,128)(2,1)S(1)} %shard_map.40.refs_0_), channel_id=1, source_target_pairs={{0,2},{2,0},{8,10},{10,8},{1,3},{3,1},{9,11},{11,9},{4,6},{6,4},{1... | collective-permute-start | bytes 196616 | tf_op jit(solution)/shard_map/ppermute | solution.py:255
  46.2 0.1 stack.53.at_ref
  46.3 0.0 collective-permute-done.8.refs_7_
  46.3 1.6 %collective-permute-done.6.refs_3_ = bf16[256,128]{1,0:T(8,128)(2,1)S(1)} collective-permute-done((bf16[256,128]{1,0:T(8,128)(2,1)S(1)}, bf16[256,128]{1,0:T(8,128)(2,1)S(1)}, u32[]{:S(2)}, u32[]{:S(2)}) %collective-permute-start.6) | collective-permute-done | bytes 65568 | tf_op jit(solution)/shard_map/ppermute | solution.py:255
  47.9 0.0 collective-permute-done.5.refs_2_
  47.9 0.6 collective-permute-done.4.refs_1_
  48.5 0.0 collective-permute-done.10.refs_9_
  48.5 1.2 %shard_map.42 = (bf16[4,32,1280]{2,1,0:T(8,128)(2,1)S(1)}, bf16[4,32,1280]{2,1,0:T(8,128)(2,1)S(1)}) custom-call(s32[6]{0:T(128)S(1)} %stack.53.at_ref, s32[1]{0:T(128)} %bitcast.place_ref, bf16[256,128]{1,0:T(8,128)(2,1)S(1)} %shard_map.40.refs_0_, bf16[256,128]{1,0:T(8,128)(2,1)S(1)} %collective-permute-done.4.refs_1_, ...), custom_call_target="tpu_custom_call" | custom-call | tf_op jit(solution)/shard_map/pallas_call | solution.py:203
  49.7 0.1 collective-permute-start.11
  49.8 1.6 %collective-permute-done.11.y_ref = bf16[4,32,1280]{2,1,0:T(8,128)(2,1)S(1)} collective-permute-done((bf16[4,32,1280]{2,1,0:T(8,128)(2,1)S(1)}, bf16[4,32,1280]{2,1,0:T(8,128)(2,1)S(1)}, u32[]{:S(2)}, u32[]{:S(2)}) %collective-permute-start.11) | collective-permute-done | bytes 327712 | tf_op jit(solution)/shard_map/ppermute | solution.py:255
  51.4 0.1 shard_map.43
  51.5 2.1 %collective-permute-start.12 = (bf16[32,1280]{1,0:T(8,128)(2,1)S(1)}, bf16[32,1280]{1,0:T(8,128)(2,1)S(1)}, u32[]{:S(2)}, u32[]{:S(2)}) collective-permute-start(bf16[32,1280]{1,0:T(8,128)(2,1)S(1)} %get-tuple-element.30), channel_id=1, source_target_pairs={{0,2},{2,0},{8,10},{10,8},{1,3},{3,1},{9,11},{11,9},{4,6},{6,4},{1... | collective-permute-start | bytes 245768 | tf_op jit(solution)/shard_map/ppermute | solution.py:255
  53.6 1.3 %collective-permute-start.13 = (bf16[32,1280]{1,0:T(8,128)(2,1)S(1)}, bf16[32,1280]{1,0:T(8,128)(2,1)S(1)}, u32[]{:S(2)}, u32[]{:S(2)}) collective-permute-start(bf16[32,1280]{1,0:T(8,128)(2,1)S(1)} %get-tuple-element.31), channel_id=1, source_target_pairs={{0,8},{2,10},{8,0},{10,2},{1,9},{3,11},{9,1},{11,3},{4,12},{6,14},... | collective-permute-start | bytes 245768 | tf_op jit(solution)/shard_map/ppermute | solution.py:255
  54.8 0.3 collective-permute-start.14
  55.1 1.2 %collective-permute-done.12.refs_1_ = bf16[32,1280]{1,0:T(8,128)(2,1)S(1)} collective-permute-done((bf16[32,1280]{1,0:T(8,128)(2,1)S(1)}, bf16[32,1280]{1,0:T(8,128)(2,1)S(1)}, u32[]{:S(2)}, u32[]{:S(2)}) %collective-permute-start.12) | collective-permute-done | bytes 81952 | tf_op jit(solution)/shard_map/ppermute | solution.py:255
  56.3 2.6 %collective-permute-done.13.refs_2_ = bf16[32,1280]{1,0:T(8,128)(2,1)S(1)} collective-permute-done((bf16[32,1280]{1,0:T(8,128)(2,1)S(1)}, bf16[32,1280]{1,0:T(8,128)(2,1)S(1)}, u32[]{:S(2)}, u32[]{:S(2)}) %collective-permute-start.13) | collective-permute-done | bytes 81952 | tf_op jit(solution)/shard_map/ppermute | solution.py:255
  58.9 1.3 %collective-permute-done.14.refs_3_ = bf16[32,1280]{1,0:T(8,128)(2,1)S(1)} collective-permute-done((bf16[32,1280]{1,0:T(8,128)(2,1)S(1)}, bf16[32,1280]{1,0:T(8,128)(2,1)S(1)}, u32[]{:S(2)}, u32[]{:S(2)}) %collective-permute-start.14) | collective-permute-done | bytes 81952 | tf_op jit(solution)/shard_map/ppermute | solution.py:255
  60.2 0.8 %shard_map.44 = bf16[32,5120]{1,0:T(8,128)(2,1)} custom-call(s32[1]{0:T(128)} %bitcast.place_ref, bf16[32,1280]{1,0:T(8,128)(2,1)S(1)} %get-tuple-element.29.refs_0_, bf16[32,1280]{1,0:T(8,128)(2,1)S(1)} %collective-permute-done.12.refs_1_, bf16[32,1280]{1,0:T(8,128)(2,1)S(1)} %collective-permute-done.13.refs_2_, ...), custom_call_target="tpu_custom_call" | custom-call | tf_op jit(solution)/shard_map/pallas_call | solution.py:244
  (2 shorter events, 0.0 us)
Async XLA Ops:
  0.0 0.9 %copy-start.1 = (bf16[3,32,1024]{2,1,0:T(8,128)(2,1)S(1)}, bf16[3,32,1024]{2,1,0:T(8,128)(2,1)}, u32[]{:S(2)}) copy-start(bf16[3,32,1024]{2,1,0:T(8,128)(2,1)} %x_ref.2) | copy-start | bytes 589828
  0.9 33.9 %copy-start.2 = (s32[8]{0:T(128)S(1)}, s32[8]{0:T(128)}, u32[]{:S(2)}) copy-start(s32[8]{0:T(128)} %clip_ref.1) | copy-start | bytes 100
  1.6 18.4 %all-to-all-start = ((bf16[8,96,128]{2,1,0:T(8,128)(2,1)}), bf16[8,96,128]{2,1,0:T(8,128)(2,1)S(1)}, u32[]{:S(2)}, u32[]{:S(2)}) async-start(bf16[8,96,128]{2,1,0:T(8,128)(2,1)} %shard_map.37), calls=%async_computation | async-start | bytes 393216 | tf_op jit(solution)/shard_map/all_to_all | solution.py:278
  7.0 1.3 %copy-start = (bf16[128,5120]{1,0:T(8,128)(2,1)S(1)}, bf16[128,5120]{1,0:T(8,128)(2,1)}, u32[]{:S(2)}) copy-start(bf16[128,5120]{1,0:T(8,128)(2,1)} %x_ref.3) | copy-start | bytes 3932164
  9.0 11.1 %collective-permute-start = (bf16[64,1280]{1,0:T(8,128)(2,1)S(1)}, bf16[64,1280]{1,0:T(8,128)(2,1)S(1)}, u32[]{:S(2)}, u32[]{:S(2)}) collective-permute-start(bf16[64,1280]{1,0:T(8,128)(2,1)S(1)} %get-tuple-element.19), channel_id=1, source_target_pairs={{0,4},{4,0},{1,5},{5,1},{2,6},{6,2},{3,7},{7,3},{8,12},{12,8},{9,1... | collective-permute-start | bytes 491528 | tf_op jit(solution)/shard_map/ppermute | solution.py:255
  20.1 8.9 %collective-permute-start.1 = (bf16[8,64,128]{2,1,0:T(8,128)(2,1)S(1)}, bf16[8,64,128]{2,1,0:T(8,128)(2,1)S(1)}, u32[]{:S(2)}, u32[]{:S(2)}) collective-permute-start(bf16[8,64,128]{2,1,0:T(8,128)(2,1)S(1)} %get-tuple-element.22.refs_0_), channel_id=1, source_target_pairs={{0,4},{4,0},{1,5},{5,1},{2,6},{6,2},{3,7},{7,3},{8,12},{12,8},{9,1... | collective-permute-start | bytes 393224 | tf_op jit(solution)/shard_map/ppermute | solution.py:255
  20.2 12.1 %collective-permute-start.2 = (bf16[8,64,128]{2,1,0:T(8,128)(2,1)S(1)}, bf16[8,64,128]{2,1,0:T(8,128)(2,1)S(1)}, u32[]{:S(2)}, u32[]{:S(2)}) collective-permute-start(bf16[8,64,128]{2,1,0:T(8,128)(2,1)S(1)} %get-tuple-element.22.refs_0_), channel_id=1, source_target_pairs={{0,16},{16,0},{1,17},{17,1},{2,18},{18,2},{3,19},{19,3},{4,20},{20... | collective-permute-start | bytes 393224 | tf_op jit(solution)/shard_map/ppermute | solution.py:255
  29.0 5.8 %collective-permute-start.3 = (bf16[8,64,128]{2,1,0:T(8,128)(2,1)S(1)}, bf16[8,64,128]{2,1,0:T(8,128)(2,1)S(1)}, u32[]{:S(2)}, u32[]{:S(2)}) collective-permute-start(bf16[8,64,128]{2,1,0:T(8,128)(2,1)S(1)} %collective-permute-done.1.refs_1_), channel_id=1, source_target_pairs={{0,16},{16,0},{1,17},{17,1},{2,18},{18,2},{3,19},{19,3},{4,20},{20... | collective-permute-start | bytes 393224 | tf_op jit(solution)/shard_map/ppermute | solution.py:255
  30.5 13.5 %collective-permute-start.7 = (bf16[128,1280]{1,0:T(8,128)(2,1)S(1)}, bf16[128,1280]{1,0:T(8,128)(2,1)S(1)}, u32[]{:S(2)}, u32[]{:S(2)}) collective-permute-start(bf16[128,1280]{1,0:T(8,128)(2,1)S(1)} %get-tuple-element.24), channel_id=1, source_target_pairs={{0,2},{2,0},{1,3},{3,1},{4,6},{6,4},{5,7},{7,5},{8,10},{10,8},{9,1... | collective-permute-start | bytes 983048 | tf_op jit(solution)/shard_map/ppermute | solution.py:255
  30.6 11.6 %collective-permute-start.9 = (bf16[64,1280]{1,0:T(8,128)(2,1)S(1)}, bf16[64,1280]{1,0:T(8,128)(2,1)S(1)}, u32[]{:S(2)}, u32[]{:S(2)}) collective-permute-start(bf16[64,1280]{1,0:T(8,128)(2,1)S(1)} %get-tuple-element.26), channel_id=1, source_target_pairs={{0,6},{2,4},{4,2},{6,0},{1,7},{3,5},{5,3},{7,1},{8,14},{10,12},{12... | collective-permute-start | bytes 491528 | tf_op jit(solution)/shard_map/ppermute | solution.py:255
  31.8 14.5 %collective-permute-start.8 = (bf16[64,1280]{1,0:T(8,128)(2,1)S(1)}, bf16[64,1280]{1,0:T(8,128)(2,1)S(1)}, u32[]{:S(2)}, u32[]{:S(2)}) collective-permute-start(bf16[64,1280]{1,0:T(8,128)(2,1)S(1)} %get-tuple-element.25.refs_6_), channel_id=1, source_target_pairs={{0,16},{16,0},{1,17},{17,1},{2,18},{18,2},{3,19},{19,3},{4,20},{20... | collective-permute-start | bytes 491528 | tf_op jit(solution)/shard_map/ppermute | solution.py:255
  42.2 6.2 %collective-permute-start.10 = (bf16[64,1280]{1,0:T(8,128)(2,1)S(1)}, bf16[64,1280]{1,0:T(8,128)(2,1)S(1)}, u32[]{:S(2)}, u32[]{:S(2)}) collective-permute-start(bf16[64,1280]{1,0:T(8,128)(2,1)S(1)} %shard_map.41.refs_8_), channel_id=1, source_target_pairs={{0,16},{16,0},{1,17},{17,1},{2,18},{18,2},{3,19},{19,3},{4,20},{20... | collective-permute-start | bytes 491528 | tf_op jit(solution)/shard_map/ppermute | solution.py:255
  42.7 5.2 %collective-permute-start.6 = (bf16[256,128]{1,0:T(8,128)(2,1)S(1)}, bf16[256,128]{1,0:T(8,128)(2,1)S(1)}, u32[]{:S(2)}, u32[]{:S(2)}) collective-permute-start(bf16[256,128]{1,0:T(8,128)(2,1)S(1)} %shard_map.40.refs_0_), channel_id=1, source_target_pairs={{0,10},{2,8},{8,2},{10,0},{1,11},{3,9},{9,3},{11,1},{4,14},{6,12},... | collective-permute-start | bytes 196616 | tf_op jit(solution)/shard_map/ppermute | solution.py:255
  42.7 5.2 %collective-permute-start.5 = (bf16[256,128]{1,0:T(8,128)(2,1)S(1)}, bf16[256,128]{1,0:T(8,128)(2,1)S(1)}, u32[]{:S(2)}, u32[]{:S(2)}) collective-permute-start(bf16[256,128]{1,0:T(8,128)(2,1)S(1)} %shard_map.40.refs_0_), channel_id=1, source_target_pairs={{0,8},{2,10},{8,0},{10,2},{1,9},{3,11},{9,1},{11,3},{4,12},{6,14},... | collective-permute-start | bytes 196616 | tf_op jit(solution)/shard_map/ppermute | solution.py:255
  44.0 4.5 %collective-permute-start.4 = (bf16[256,128]{1,0:T(8,128)(2,1)S(1)}, bf16[256,128]{1,0:T(8,128)(2,1)S(1)}, u32[]{:S(2)}, u32[]{:S(2)}) collective-permute-start(bf16[256,128]{1,0:T(8,128)(2,1)S(1)} %shard_map.40.refs_0_), channel_id=1, source_target_pairs={{0,2},{2,0},{8,10},{10,8},{1,3},{3,1},{9,11},{11,9},{4,6},{6,4},{1... | collective-permute-start | bytes 196616 | tf_op jit(solution)/shard_map/ppermute | solution.py:255
  49.7 1.7 %collective-permute-start.11 = (bf16[4,32,1280]{2,1,0:T(8,128)(2,1)S(1)}, bf16[4,32,1280]{2,1,0:T(8,128)(2,1)S(1)}, u32[]{:S(2)}, u32[]{:S(2)}) collective-permute-start(bf16[4,32,1280]{2,1,0:T(8,128)(2,1)S(1)} %get-tuple-element.28), channel_id=1, source_target_pairs={{0,1},{1,0},{2,3},{3,2},{4,5},{5,4},{6,7},{7,6},{8,9},{9,8},{10,11... | collective-permute-start | bytes 983048 | tf_op jit(solution)/shard_map/ppermute | solution.py:255
  51.5 4.8 %collective-permute-start.12 = (bf16[32,1280]{1,0:T(8,128)(2,1)S(1)}, bf16[32,1280]{1,0:T(8,128)(2,1)S(1)}, u32[]{:S(2)}, u32[]{:S(2)}) collective-permute-start(bf16[32,1280]{1,0:T(8,128)(2,1)S(1)} %get-tuple-element.30), channel_id=1, source_target_pairs={{0,2},{2,0},{8,10},{10,8},{1,3},{3,1},{9,11},{11,9},{4,6},{6,4},{1... | collective-permute-start | bytes 245768 | tf_op jit(solution)/shard_map/ppermute | solution.py:255
  53.6 5.3 %collective-permute-start.13 = (bf16[32,1280]{1,0:T(8,128)(2,1)S(1)}, bf16[32,1280]{1,0:T(8,128)(2,1)S(1)}, u32[]{:S(2)}, u32[]{:S(2)}) collective-permute-start(bf16[32,1280]{1,0:T(8,128)(2,1)S(1)} %get-tuple-element.31), channel_id=1, source_target_pairs={{0,8},{2,10},{8,0},{10,2},{1,9},{3,11},{9,1},{11,3},{4,12},{6,14},... | collective-permute-start | bytes 245768 | tf_op jit(solution)/shard_map/ppermute | solution.py:255
  54.8 5.3 %collective-permute-start.14 = (bf16[32,1280]{1,0:T(8,128)(2,1)S(1)}, bf16[32,1280]{1,0:T(8,128)(2,1)S(1)}, u32[]{:S(2)}, u32[]{:S(2)}) collective-permute-start(bf16[32,1280]{1,0:T(8,128)(2,1)S(1)} %get-tuple-element.32), channel_id=1, source_target_pairs={{0,10},{2,8},{8,2},{10,0},{1,11},{3,9},{9,3},{11,1},{4,14},{6,12},... | collective-permute-start | bytes 245768 | tf_op jit(solution)/shard_map/ppermute | solution.py:255

commit v10 on v9

--- a/solution.py
+++ b/solution.py
@@ -100,15 +100,16 @@
     pass
 
 
-def after(x, passed):
+def after(passed, *first, cost=None):
     return pl.pallas_call(
         after_kernel,
         out_shape=jax.ShapeDtypeStruct(passed.shape, passed.dtype),
-        in_specs=[ANY, ANY],
+        in_specs=[ANY] * (1 + len(first)),
         out_specs=ANY,
-        input_output_aliases={1: 0},
-        compiler_params=PARAMS,
-    )(x, passed)
+        input_output_aliases={0: 0},
+        compiler_params=PARAMS,
+        cost_estimate=cost,
+    )(passed, *first)
 
 
 def clip_of(token, base, span, tok_dev, clip_ref):
@@ -167,7 +168,6 @@
         in_specs=[SMEM, SMEM] + [VMEM] * (1 + len(kvs)),
         out_specs=VMEM,
         compiler_params=PARAMS,
-        cost_estimate=AHEAD,
     )(jnp.stack([jnp.asarray(i, jnp.int32) for i in bases]), frame_clip, q, *kvs)
 
 
@@ -272,7 +272,7 @@
         [(head_dim, 0, mine), (half, y, mine), (half, y, theirs), (head_dim, 0, theirs)],
         cols,
     )
-    far = xor(w_far, ("zh",), 1)
+    far = after(xor(w_far, ("zh",), 1), cost=AHEAD)
     near = xor(w_near, ("zl",), 1)
     packed = pack(qkv, 8, head_dim)
     own = lax.all_to_all(packed, group, split_axis=0, concat_axis=0, tiled=True)
@@ -286,7 +286,7 @@
     attn = attention(
         q, [kv, kv_far, kv_near, kv_end], [base, base, other, other], 4 * tok, frame_clip, head_dim
     )
-    corner = after(attn, corner)
+    corner = after(corner, attn)
     corner_rest = xor(corner, ("y",), 1)
     attns = swap_all([attn] * 4, quarter)
     w_parts = [w_own, near, far, far_rest, corner, corner_rest]

time: 61.2 us -> 53.2 us (0.87)
  waiting for transfers between devices: 33.1 us -> 21.9 us
  starting transfers between devices: 20.4 us -> 24.7 us
  local copies, waits for them, and re-layouts: 2.42 us -> 1.49 us
    ppermute x15, waiting for transfers between devices: 33.1 us -> 18.8 us  [xor(): return lax.ppermute(x, axis, [(i, i ^ by) for i in range(size)])]
    ppermute x15, starting transfers between devices: 15.2 us -> 20.9 us  [xor(): return lax.ppermute(x, axis, [(i, i ^ by) for i in range(size)])]
    all_to_all x1, waiting for transfers between devices: 0.01 us -> 3.08 us  [squares(): own = lax.all_to_all(packed, group, split_axis=0, concat_axis=0, tiled=True)]
    all_to_all x1, starting transfers between devices: 5.23 us -> 3.78 us  [squares(): own = lax.all_to_all(packed, group, split_axis=0, concat_axis=0, tiled=True)]
    unnamed x6, local copies, waits for them, and re-layouts: 2.25 us -> 1.33 us
  transfers between devices with their start and end apart: 16 -> 16, of which waited for: 10 -> 10; matrix products, arithmetic and copies ran while one was open for 0% -> 0% of each run, Pallas kernels for 3% -> 4%
where the time goes in v10:
time: 53.2 us; the launch traced here: 53 us
  starting transfers between devices  24.7 us (46%)
  waiting for transfers between devices  21.9 us (41%)
  Pallas kernels  4.78 us (9%)
  local copies, waits for them, and re-layouts  1.49 us (3%)
    ppermute x15, starting transfers between devices, xor(): return lax.ppermute(x, axis, [(i, i ^ by) for i in range(size)])  20.9 us
    ppermute x15, waiting for transfers between devices, xor(): return lax.ppermute(x, axis, [(i, i ^ by) for i in range(size)])  18.8 us
    all_to_all x1, starting transfers between devices, squares(): own = lax.all_to_all(packed, group, split_axis=0, concat_axis=0, tiled=True)  3.78 us
    all_to_all x1, waiting for transfers between devices, squares(): own = lax.all_to_all(packed, group, split_axis=0, concat_axis=0, tiled=True)  3.08 us
    unnamed x6, local copies, waits for them, and re-layouts  1.33 us
    pallas_call x1, Pallas kernels, attention(): pl.pallas_call(functools.partial(attention_kernel, head_dim, span), out_s...  1.29 us
    pallas_call x1, Pallas kernels, project(): pl.pallas_call(functools.partial(project_kernel, blks), out_shape=(like,...  1.22 us
  transfers between devices with their start and end apart: 16, of which 10 were waited for; matrix products, arithmetic and copies ran while one was open for 0% of the time, Pallas kernels for 4%

profile of v10, /device:TPU:0, one launch (start us, length us, event | category | flops | bytes accessed | tf_op | source)
XLA Modules:
  0.0 53.0 jit_solution(919680953833871674)
XLA Ops:
  0.0 0.1 stack.60.at_ref
  0.1 0.0 copy-start
  0.1 1.3 %copy-done = bf16[128,5120]{1,0:T(8,128)(2,1)S(1)} copy-done((bf16[128,5120]{1,0:T(8,128)(2,1)S(1)}, bf16[128,5120]{1,0:T(8,128)(2,1)}, u32[]{:S(2)}) %copy-start) | copy-done | bytes 1310744
  1.4 0.0 copy-start.1
  1.4 0.7 %shard_map.38 = (bf16[128,1280]{1,0:T(8,128)(2,1)S(1)}, bf16[64,1280]{1,0:T(8,128)(2,1)S(1)}, bf16[64,1280]{1,0:T(8,128)(2,1)S(1)}, bf16[128,1280]{1,0:T(8,128)(2,1)S(1)}) custom-call(s32[8]{0:T(128)S(1)} %stack.60.at_ref, bf16[128,5120]{1,0:T(8,128)(2,1)S(1)} %copy-done), custom_call_target="tpu_custom_call" | custom-call | tf_op jit(solution)/shard_map/pallas_call | solution.py:65
  2.1 4.1 %collective-permute-start = (bf16[64,1280]{1,0:T(8,128)(2,1)S(1)}, bf16[64,1280]{1,0:T(8,128)(2,1)S(1)}, u32[]{:S(2)}, u32[]{:S(2)}) collective-permute-start(bf16[64,1280]{1,0:T(8,128)(2,1)S(1)} %get-tuple-element.19), channel_id=1, source_target_pairs={{0,4},{4,0},{1,5},{5,1},{2,6},{6,2},{3,7},{7,3},{8,12},{12,8},{9,1... | collective-permute-start | bytes 491528 | tf_op jit(solution)/shard_map/ppermute | solution.py:255
  6.2 0.0 copy-done.1
  6.2 0.7 %shard_map.37 = bf16[8,96,128]{2,1,0:T(8,128)(2,1)} custom-call(bf16[3,32,1024]{2,1,0:T(8,128)(2,1)S(1)} %copy-done.1), custom_call_target="tpu_custom_call" | custom-call | tf_op jit(solution)/shard_map/pallas_call | solution.py:36
  6.9 3.8 %all-to-all-start = ((bf16[8,96,128]{2,1,0:T(8,128)(2,1)}), bf16[8,96,128]{2,1,0:T(8,128)(2,1)S(1)}, u32[]{:S(2)}, u32[]{:S(2)}) async-start(bf16[8,96,128]{2,1,0:T(8,128)(2,1)} %shard_map.37), calls=%async_computation | async-start | bytes 393216 | tf_op jit(solution)/shard_map/all_to_all | solution.py:278
  10.7 0.0 copy-start.2
  10.7 3.2 %collective-permute-done.refs_0_ = bf16[64,1280]{1,0:T(8,128)(2,1)S(1)} collective-permute-done((bf16[64,1280]{1,0:T(8,128)(2,1)S(1)}, bf16[64,1280]{1,0:T(8,128)(2,1)S(1)}, u32[]{:S(2)}, u32[]{:S(2)}) %collective-permute-start) | collective-permute-done | bytes 163872 | tf_op jit(solution)/shard_map/ppermute | solution.py:255
  13.9 3.1 %all-to-all-done.x_ref = bf16[8,96,128]{2,1,0:T(8,128)(2,1)S(1)} async-done(((bf16[8,96,128]{2,1,0:T(8,128)(2,1)}), bf16[8,96,128]{2,1,0:T(8,128)(2,1)S(1)}, u32[]{:S(2)}, u32[]{:S(2)}) %all-to-all-start) | async-done | bytes 196640 | tf_op jit(solution)/shard_map/all_to_all | solution.py:278
  17.0 0.7 %collective-permute-start.1 = (bf16[8,64,128]{2,1,0:T(8,128)(2,1)S(1)}, bf16[8,64,128]{2,1,0:T(8,128)(2,1)S(1)}, u32[]{:S(2)}, u32[]{:S(2)}) collective-permute-start(bf16[8,64,128]{2,1,0:T(8,128)(2,1)S(1)} %get-tuple-element.22.refs_0_), channel_id=1, source_target_pairs={{0,4},{4,0},{1,5},{5,1},{2,6},{6,2},{3,7},{7,3},{8,12},{12,8},{9,1... | collective-permute-start | bytes 393224 | tf_op jit(solution)/shard_map/ppermute | solution.py:255
  17.8 2.9 %collective-permute-start.7 = (bf16[128,1280]{1,0:T(8,128)(2,1)S(1)}, bf16[128,1280]{1,0:T(8,128)(2,1)S(1)}, u32[]{:S(2)}, u32[]{:S(2)}) collective-permute-start(bf16[128,1280]{1,0:T(8,128)(2,1)S(1)} %get-tuple-element.24), channel_id=1, source_target_pairs={{0,2},{2,0},{1,3},{3,1},{4,6},{6,4},{5,7},{7,5},{8,10},{10,8},{9,1... | collective-permute-start | bytes 983048 | tf_op jit(solution)/shard_map/ppermute | solution.py:255
  20.7 0.8 %collective-permute-start.9 = (bf16[64,1280]{1,0:T(8,128)(2,1)S(1)}, bf16[64,1280]{1,0:T(8,128)(2,1)S(1)}, u32[]{:S(2)}, u32[]{:S(2)}) collective-permute-start(bf16[64,1280]{1,0:T(8,128)(2,1)S(1)} %get-tuple-element.26), channel_id=1, source_target_pairs={{0,6},{2,4},{4,2},{6,0},{1,7},{3,5},{5,3},{7,1},{8,14},{10,12},{12... | collective-permute-start | bytes 491528 | tf_op jit(solution)/shard_map/ppermute | solution.py:255
  21.5 1.5 %collective-permute-start.2 = (bf16[8,64,128]{2,1,0:T(8,128)(2,1)S(1)}, bf16[8,64,128]{2,1,0:T(8,128)(2,1)S(1)}, u32[]{:S(2)}, u32[]{:S(2)}) collective-permute-start(bf16[8,64,128]{2,1,0:T(8,128)(2,1)S(1)} %get-tuple-element.22.refs_0_), channel_id=1, source_target_pairs={{0,16},{16,0},{1,17},{17,1},{2,18},{18,2},{3,19},{19,3},{4,20},{20... | collective-permute-start | bytes 393224 | tf_op jit(solution)/shard_map/ppermute | solution.py:255
  23.0 2.9 %collective-permute-done.1.refs_1_ = bf16[8,64,128]{2,1,0:T(8,128)(2,1)S(1)} collective-permute-done((bf16[8,64,128]{2,1,0:T(8,128)(2,1)S(1)}, bf16[8,64,128]{2,1,0:T(8,128)(2,1)S(1)}, u32[]{:S(2)}, u32[]{:S(2)}) %collective-permute-start.1) | collective-permute-done | bytes 131104 | tf_op jit(solution)/shard_map/ppermute | solution.py:255
  25.9 1.5 %collective-permute-start.3 = (bf16[8,64,128]{2,1,0:T(8,128)(2,1)S(1)}, bf16[8,64,128]{2,1,0:T(8,128)(2,1)S(1)}, u32[]{:S(2)}, u32[]{:S(2)}) collective-permute-start(bf16[8,64,128]{2,1,0:T(8,128)(2,1)S(1)} %collective-permute-done.1.refs_1_), channel_id=1, source_target_pairs={{0,16},{16,0},{1,17},{17,1},{2,18},{18,2},{3,19},{19,3},{4,20},{20... | collective-permute-start | bytes 393224 | tf_op jit(solution)/shard_map/ppermute | solution.py:255
  27.4 0.1 pad_add_fusion.base_ref
  27.5 0.5 collective-permute-start.8
  28.0 0.0 collective-permute-done.2.refs_2_
  28.0 4.3 %collective-permute-done.3.refs_3_ = bf16[8,64,128]{2,1,0:T(8,128)(2,1)S(1)} collective-permute-done((bf16[8,64,128]{2,1,0:T(8,128)(2,1)S(1)}, bf16[8,64,128]{2,1,0:T(8,128)(2,1)S(1)}, u32[]{:S(2)}, u32[]{:S(2)}) %collective-permute-start.3) | collective-permute-done | bytes 131104 | tf_op jit(solution)/shard_map/ppermute | solution.py:255
  32.3 0.0 copy-done.2
  32.3 1.3 %shard_map.41.refs_1_.refs_0_ = bf16[256,128]{1,0:T(8,128)(2,1)S(1)} custom-call(s32[4]{0:T(128)S(1)} %pad_add_fusion.base_ref, s32[8]{0:T(128)S(1)} %copy-done.2, bf16[8,32,128]{2,1,0:T(8,128)(2,1)S(1)} %get-tuple-element.21.q_ref, bf16[8,64,128]{2,1,0:T(8,128)(2,1)S(1)} %get-tuple-element.22.refs_0_, ...), custom_call_target="tpu_custom_call" | custom-call | tf_op jit(solution)/shard_map/pallas_call | solution.py:165
  33.6 0.0 collective-permute-done.9.refs_0_
  33.6 1.6 %collective-permute-start.10 = (bf16[64,1280]{1,0:T(8,128)(2,1)S(1)}, bf16[64,1280]{1,0:T(8,128)(2,1)S(1)}, u32[]{:S(2)}, u32[]{:S(2)}) collective-permute-start(bf16[64,1280]{1,0:T(8,128)(2,1)S(1)} %shard_map.42.refs_8_), channel_id=1, source_target_pairs={{0,16},{16,0},{1,17},{17,1},{2,18},{18,2},{3,19},{19,3},{4,20},{20... | collective-permute-start | bytes 491528 | tf_op jit(solution)/shard_map/ppermute | solution.py:255
  35.2 0.2 collective-permute-start.6
  35.3 0.7 %collective-permute-start.5 = (bf16[256,128]{1,0:T(8,128)(2,1)S(1)}, bf16[256,128]{1,0:T(8,128)(2,1)S(1)}, u32[]{:S(2)}, u32[]{:S(2)}) collective-permute-start(bf16[256,128]{1,0:T(8,128)(2,1)S(1)} %shard_map.41.refs_1_.refs_0_), channel_id=1, source_target_pairs={{0,8},{2,10},{8,0},{10,2},{1,9},{3,11},{9,1},{11,3},{4,12},{6,14},... | collective-permute-start | bytes 196616 | tf_op jit(solution)/shard_map/ppermute | solution.py:255
  36.1 0.0 collective-permute-done.7.refs_5_
  36.1 2.6 %collective-permute-start.4 = (bf16[256,128]{1,0:T(8,128)(2,1)S(1)}, bf16[256,128]{1,0:T(8,128)(2,1)S(1)}, u32[]{:S(2)}, u32[]{:S(2)}) collective-permute-start(bf16[256,128]{1,0:T(8,128)(2,1)S(1)} %shard_map.41.refs_1_.refs_0_), channel_id=1, source_target_pairs={{0,2},{2,0},{8,10},{10,8},{1,3},{3,1},{9,11},{11,9},{4,6},{6,4},{1... | collective-permute-start | bytes 196616 | tf_op jit(solution)/shard_map/ppermute | solution.py:255
  38.7 0.1 stack.53.at_ref
  38.8 0.0 collective-permute-done.8.refs_7_
  38.8 1.6 %collective-permute-done.6.refs_3_ = bf16[256,128]{1,0:T(8,128)(2,1)S(1)} collective-permute-done((bf16[256,128]{1,0:T(8,128)(2,1)S(1)}, bf16[256,128]{1,0:T(8,128)(2,1)S(1)}, u32[]{:S(2)}, u32[]{:S(2)}) %collective-permute-start.6) | collective-permute-done | bytes 65568 | tf_op jit(solution)/shard_map/ppermute | solution.py:255
  40.4 0.0 collective-permute-done.5.refs_2_
  40.4 0.6 %collective-permute-done.4.refs_1_ = bf16[256,128]{1,0:T(8,128)(2,1)S(1)} collective-permute-done((bf16[256,128]{1,0:T(8,128)(2,1)S(1)}, bf16[256,128]{1,0:T(8,128)(2,1)S(1)}, u32[]{:S(2)}, u32[]{:S(2)}) %collective-permute-start.4) | collective-permute-done | bytes 65568 | tf_op jit(solution)/shard_map/ppermute | solution.py:255
  40.9 0.0 collective-permute-done.10.refs_9_
  40.9 1.2 %shard_map.43 = (bf16[4,32,1280]{2,1,0:T(8,128)(2,1)S(1)}, bf16[4,32,1280]{2,1,0:T(8,128)(2,1)S(1)}) custom-call(s32[6]{0:T(128)S(1)} %stack.53.at_ref, s32[1]{0:T(128)} %bitcast.place_ref, bf16[256,128]{1,0:T(8,128)(2,1)S(1)} %shard_map.41.refs_1_.refs_0_, bf16[256,128]{1,0:T(8,128)(2,1)S(1)} %collective-permute-done.4.refs_1_, ...), custom_call_target="tpu_custom_call" | custom-call | tf_op jit(solution)/shard_map/pallas_call | solution.py:203
  42.2 0.1 collective-permute-start.11
  42.2 1.6 %collective-permute-done.11.y_ref = bf16[4,32,1280]{2,1,0:T(8,128)(2,1)S(1)} collective-permute-done((bf16[4,32,1280]{2,1,0:T(8,128)(2,1)S(1)}, bf16[4,32,1280]{2,1,0:T(8,128)(2,1)S(1)}, u32[]{:S(2)}, u32[]{:S(2)}) %collective-permute-start.11) | collective-permute-done | bytes 327712 | tf_op jit(solution)/shard_map/ppermute | solution.py:255
  43.9 0.1 shard_map.44
  43.9 2.1 %collective-permute-start.12 = (bf16[32,1280]{1,0:T(8,128)(2,1)S(1)}, bf16[32,1280]{1,0:T(8,128)(2,1)S(1)}, u32[]{:S(2)}, u32[]{:S(2)}) collective-permute-start(bf16[32,1280]{1,0:T(8,128)(2,1)S(1)} %get-tuple-element.30), channel_id=1, source_target_pairs={{0,2},{2,0},{8,10},{10,8},{1,3},{3,1},{9,11},{11,9},{4,6},{6,4},{1... | collective-permute-start | bytes 245768 | tf_op jit(solution)/shard_map/ppermute | solution.py:255
  46.0 0.8 %collective-permute-start.13 = (bf16[32,1280]{1,0:T(8,128)(2,1)S(1)}, bf16[32,1280]{1,0:T(8,128)(2,1)S(1)}, u32[]{:S(2)}, u32[]{:S(2)}) collective-permute-start(bf16[32,1280]{1,0:T(8,128)(2,1)S(1)} %get-tuple-element.31), channel_id=1, source_target_pairs={{0,8},{2,10},{8,0},{10,2},{1,9},{3,11},{9,1},{11,3},{4,12},{6,14},... | collective-permute-start | bytes 245768 | tf_op jit(solution)/shard_map/ppermute | solution.py:255
  46.9 0.7 %collective-permute-start.14 = (bf16[32,1280]{1,0:T(8,128)(2,1)S(1)}, bf16[32,1280]{1,0:T(8,128)(2,1)S(1)}, u32[]{:S(2)}, u32[]{:S(2)}) collective-permute-start(bf16[32,1280]{1,0:T(8,128)(2,1)S(1)} %get-tuple-element.32), channel_id=1, source_target_pairs={{0,10},{2,8},{8,2},{10,0},{1,11},{3,9},{9,3},{11,1},{4,14},{6,12},... | collective-permute-start | bytes 245768 | tf_op jit(solution)/shard_map/ppermute | solution.py:255
  47.6 1.2 %collective-permute-done.12.refs_1_ = bf16[32,1280]{1,0:T(8,128)(2,1)S(1)} collective-permute-done((bf16[32,1280]{1,0:T(8,128)(2,1)S(1)}, bf16[32,1280]{1,0:T(8,128)(2,1)S(1)}, u32[]{:S(2)}, u32[]{:S(2)}) %collective-permute-start.12) | collective-permute-done | bytes 81952 | tf_op jit(solution)/shard_map/ppermute | solution.py:255
  48.8 2.8 %collective-permute-done.13.refs_2_ = bf16[32,1280]{1,0:T(8,128)(2,1)S(1)} collective-permute-done((bf16[32,1280]{1,0:T(8,128)(2,1)S(1)}, bf16[32,1280]{1,0:T(8,128)(2,1)S(1)}, u32[]{:S(2)}, u32[]{:S(2)}) %collective-permute-start.13) | collective-permute-done | bytes 81952 | tf_op jit(solution)/shard_map/ppermute | solution.py:255
  51.6 0.6 %collective-permute-done.14.refs_3_ = bf16[32,1280]{1,0:T(8,128)(2,1)S(1)} collective-permute-done((bf16[32,1280]{1,0:T(8,128)(2,1)S(1)}, bf16[32,1280]{1,0:T(8,128)(2,1)S(1)}, u32[]{:S(2)}, u32[]{:S(2)}) %collective-permute-start.14) | collective-permute-done | bytes 81952 | tf_op jit(solution)/shard_map/ppermute | solution.py:255
  52.2 0.8 %shard_map.45 = bf16[32,5120]{1,0:T(8,128)(2,1)} custom-call(s32[1]{0:T(128)} %bitcast.place_ref, bf16[32,1280]{1,0:T(8,128)(2,1)S(1)} %get-tuple-element.29.refs_0_, bf16[32,1280]{1,0:T(8,128)(2,1)S(1)} %collective-permute-done.12.refs_1_, bf16[32,1280]{1,0:T(8,128)(2,1)S(1)} %collective-permute-done.13.refs_2_, ...), custom_call_target="tpu_custom_call" | custom-call | tf_op jit(solution)/shard_map/pallas_call | solution.py:244
  (3 shorter events, 0.0 us)
Async XLA Ops:
  0.1 1.3 %copy-start = (bf16[128,5120]{1,0:T(8,128)(2,1)S(1)}, bf16[128,5120]{1,0:T(8,128)(2,1)}, u32[]{:S(2)}) copy-start(bf16[128,5120]{1,0:T(8,128)(2,1)} %x_ref.3) | copy-start | bytes 3932164
  1.4 4.8 %copy-start.1 = (bf16[3,32,1024]{2,1,0:T(8,128)(2,1)S(1)}, bf16[3,32,1024]{2,1,0:T(8,128)(2,1)}, u32[]{:S(2)}) copy-start(bf16[3,32,1024]{2,1,0:T(8,128)(2,1)} %x_ref.2) | copy-start | bytes 589828
  2.1 11.8 %collective-permute-start = (bf16[64,1280]{1,0:T(8,128)(2,1)S(1)}, bf16[64,1280]{1,0:T(8,128)(2,1)S(1)}, u32[]{:S(2)}, u32[]{:S(2)}) collective-permute-start(bf16[64,1280]{1,0:T(8,128)(2,1)S(1)} %get-tuple-element.19), channel_id=1, source_target_pairs={{0,4},{4,0},{1,5},{5,1},{2,6},{6,2},{3,7},{7,3},{8,12},{12,8},{9,1... | collective-permute-start | bytes 491528 | tf_op jit(solution)/shard_map/ppermute | solution.py:255
  6.9 10.1 %all-to-all-start = ((bf16[8,96,128]{2,1,0:T(8,128)(2,1)}), bf16[8,96,128]{2,1,0:T(8,128)(2,1)S(1)}, u32[]{:S(2)}, u32[]{:S(2)}) async-start(bf16[8,96,128]{2,1,0:T(8,128)(2,1)} %shard_map.37), calls=%async_computation | async-start | bytes 393216 | tf_op jit(solution)/shard_map/all_to_all | solution.py:278
  10.7 21.6 %copy-start.2 = (s32[8]{0:T(128)S(1)}, s32[8]{0:T(128)}, u32[]{:S(2)}) copy-start(s32[8]{0:T(128)} %clip_ref.1) | copy-start | bytes 100
  17.0 8.8 %collective-permute-start.1 = (bf16[8,64,128]{2,1,0:T(8,128)(2,1)S(1)}, bf16[8,64,128]{2,1,0:T(8,128)(2,1)S(1)}, u32[]{:S(2)}, u32[]{:S(2)}) collective-permute-start(bf16[8,64,128]{2,1,0:T(8,128)(2,1)S(1)} %get-tuple-element.22.refs_0_), channel_id=1, source_target_pairs={{0,4},{4,0},{1,5},{5,1},{2,6},{6,2},{3,7},{7,3},{8,12},{12,8},{9,1... | collective-permute-start | bytes 393224 | tf_op jit(solution)/shard_map/ppermute | solution.py:255
  17.8 18.3 %collective-permute-start.7 = (bf16[128,1280]{1,0:T(8,128)(2,1)S(1)}, bf16[128,1280]{1,0:T(8,128)(2,1)S(1)}, u32[]{:S(2)}, u32[]{:S(2)}) collective-permute-start(bf16[128,1280]{1,0:T(8,128)(2,1)S(1)} %get-tuple-element.24), channel_id=1, source_target_pairs={{0,2},{2,0},{1,3},{3,1},{4,6},{6,4},{5,7},{7,5},{8,10},{10,8},{9,1... | collective-permute-start | bytes 983048 | tf_op jit(solution)/shard_map/ppermute | solution.py:255
  20.7 12.9 %collective-permute-start.9 = (bf16[64,1280]{1,0:T(8,128)(2,1)S(1)}, bf16[64,1280]{1,0:T(8,128)(2,1)S(1)}, u32[]{:S(2)}, u32[]{:S(2)}) collective-permute-start(bf16[64,1280]{1,0:T(8,128)(2,1)S(1)} %get-tuple-element.26), channel_id=1, source_target_pairs={{0,6},{2,4},{4,2},{6,0},{1,7},{3,5},{5,3},{7,1},{8,14},{10,12},{12... | collective-permute-start | bytes 491528 | tf_op jit(solution)/shard_map/ppermute | solution.py:255
  21.5 6.5 %collective-permute-start.2 = (bf16[8,64,128]{2,1,0:T(8,128)(2,1)S(1)}, bf16[8,64,128]{2,1,0:T(8,128)(2,1)S(1)}, u32[]{:S(2)}, u32[]{:S(2)}) collective-permute-start(bf16[8,64,128]{2,1,0:T(8,128)(2,1)S(1)} %get-tuple-element.22.refs_0_), channel_id=1, source_target_pairs={{0,16},{16,0},{1,17},{17,1},{2,18},{18,2},{3,19},{19,3},{4,20},{20... | collective-permute-start | bytes 393224 | tf_op jit(solution)/shard_map/ppermute | solution.py:255
  25.9 6.4 %collective-permute-start.3 = (bf16[8,64,128]{2,1,0:T(8,128)(2,1)S(1)}, bf16[8,64,128]{2,1,0:T(8,128)(2,1)S(1)}, u32[]{:S(2)}, u32[]{:S(2)}) collective-permute-start(bf16[8,64,128]{2,1,0:T(8,128)(2,1)S(1)} %collective-permute-done.1.refs_1_), channel_id=1, source_target_pairs={{0,16},{16,0},{1,17},{17,1},{2,18},{18,2},{3,19},{19,3},{4,20},{20... | collective-permute-start | bytes 393224 | tf_op jit(solution)/shard_map/ppermute | solution.py:255
  27.5 11.3 %collective-permute-start.8 = (bf16[64,1280]{1,0:T(8,128)(2,1)S(1)}, bf16[64,1280]{1,0:T(8,128)(2,1)S(1)}, u32[]{:S(2)}, u32[]{:S(2)}) collective-permute-start(bf16[64,1280]{1,0:T(8,128)(2,1)S(1)} %get-tuple-element.25.refs_6_), channel_id=1, source_target_pairs={{0,16},{16,0},{1,17},{17,1},{2,18},{18,2},{3,19},{19,3},{4,20},{20... | collective-permute-start | bytes 491528 | tf_op jit(solution)/shard_map/ppermute | solution.py:255
  33.6 7.3 %collective-permute-start.10 = (bf16[64,1280]{1,0:T(8,128)(2,1)S(1)}, bf16[64,1280]{1,0:T(8,128)(2,1)S(1)}, u32[]{:S(2)}, u32[]{:S(2)}) collective-permute-start(bf16[64,1280]{1,0:T(8,128)(2,1)S(1)} %shard_map.42.refs_8_), channel_id=1, source_target_pairs={{0,16},{16,0},{1,17},{17,1},{2,18},{18,2},{3,19},{19,3},{4,20},{20... | collective-permute-start | bytes 491528 | tf_op jit(solution)/shard_map/ppermute | solution.py:255
  35.2 5.2 %collective-permute-start.6 = (bf16[256,128]{1,0:T(8,128)(2,1)S(1)}, bf16[256,128]{1,0:T(8,128)(2,1)S(1)}, u32[]{:S(2)}, u32[]{:S(2)}) collective-permute-start(bf16[256,128]{1,0:T(8,128)(2,1)S(1)} %shard_map.41.refs_1_.refs_0_), channel_id=1, source_target_pairs={{0,10},{2,8},{8,2},{10,0},{1,11},{3,9},{9,3},{11,1},{4,14},{6,12},... | collective-permute-start | bytes 196616 | tf_op jit(solution)/shard_map/ppermute | solution.py:255
  35.3 5.0 %collective-permute-start.5 = (bf16[256,128]{1,0:T(8,128)(2,1)S(1)}, bf16[256,128]{1,0:T(8,128)(2,1)S(1)}, u32[]{:S(2)}, u32[]{:S(2)}) collective-permute-start(bf16[256,128]{1,0:T(8,128)(2,1)S(1)} %shard_map.41.refs_1_.refs_0_), channel_id=1, source_target_pairs={{0,8},{2,10},{8,0},{10,2},{1,9},{3,11},{9,1},{11,3},{4,12},{6,14},... | collective-permute-start | bytes 196616 | tf_op jit(solution)/shard_map/ppermute | solution.py:255
  36.1 4.9 %collective-permute-start.4 = (bf16[256,128]{1,0:T(8,128)(2,1)S(1)}, bf16[256,128]{1,0:T(8,128)(2,1)S(1)}, u32[]{:S(2)}, u32[]{:S(2)}) collective-permute-start(bf16[256,128]{1,0:T(8,128)(2,1)S(1)} %shard_map.41.refs_1_.refs_0_), channel_id=1, source_target_pairs={{0,2},{2,0},{8,10},{10,8},{1,3},{3,1},{9,11},{11,9},{4,6},{6,4},{1... | collective-permute-start | bytes 196616 | tf_op jit(solution)/shard_map/ppermute | solution.py:255
  42.2 1.7 %collective-permute-start.11 = (bf16[4,32,1280]{2,1,0:T(8,128)(2,1)S(1)}, bf16[4,32,1280]{2,1,0:T(8,128)(2,1)S(1)}, u32[]{:S(2)}, u32[]{:S(2)}) collective-permute-start(bf16[4,32,1280]{2,1,0:T(8,128)(2,1)S(1)} %get-tuple-element.28), channel_id=1, source_target_pairs={{0,1},{1,0},{2,3},{3,2},{4,5},{5,4},{6,7},{7,6},{8,9},{9,8},{10,11... | collective-permute-start | bytes 983048 | tf_op jit(solution)/shard_map/ppermute | solution.py:255
  43.9 4.8 %collective-permute-start.12 = (bf16[32,1280]{1,0:T(8,128)(2,1)S(1)}, bf16[32,1280]{1,0:T(8,128)(2,1)S(1)}, u32[]{:S(2)}, u32[]{:S(2)}) collective-permute-start(bf16[32,1280]{1,0:T(8,128)(2,1)S(1)} %get-tuple-element.30), channel_id=1, source_target_pairs={{0,2},{2,0},{8,10},{10,8},{1,3},{3,1},{9,11},{11,9},{4,6},{6,4},{1... | collective-permute-start | bytes 245768 | tf_op jit(solution)/shard_map/ppermute | solution.py:255
  46.0 5.6 %collective-permute-start.13 = (bf16[32,1280]{1,0:T(8,128)(2,1)S(1)}, bf16[32,1280]{1,0:T(8,128)(2,1)S(1)}, u32[]{:S(2)}, u32[]{:S(2)}) collective-permute-start(bf16[32,1280]{1,0:T(8,128)(2,1)S(1)} %get-tuple-element.31), channel_id=1, source_target_pairs={{0,8},{2,10},{8,0},{10,2},{1,9},{3,11},{9,1},{11,3},{4,12},{6,14},... | collective-permute-start | bytes 245768 | tf_op jit(solution)/shard_map/ppermute | solution.py:255
  46.9 5.4 %collective-permute-start.14 = (bf16[32,1280]{1,0:T(8,128)(2,1)S(1)}, bf16[32,1280]{1,0:T(8,128)(2,1)S(1)}, u32[]{:S(2)}, u32[]{:S(2)}) collective-permute-start(bf16[32,1280]{1,0:T(8,128)(2,1)S(1)} %get-tuple-element.32), channel_id=1, source_target_pairs={{0,10},{2,8},{8,2},{10,0},{1,11},{3,9},{9,3},{11,1},{4,14},{6,12},... | collective-permute-start | bytes 245768 | tf_op jit(solution)/shard_map/ppermute | solution.py:255

commit v11 on v10

--- a/solution.py
+++ b/solution.py
@@ -69,31 +69,98 @@
         out_specs=[VMEM] * len(pieces),
         scratch_shapes=[pltpu.SemaphoreType.DMA((len(pieces),))],
         compiler_params=PARAMS,
-    )(at, x)
-
-
-def cut_kernel(x_ref, *refs):
-    q_ref, kv_ref = refs[len(refs) // 2 - 1:][:2]
+    )(at, pltpu.with_memory_space_constraint(x, pltpu.HBM))
+
+
+def lane_kernel(head_dim, core_ref, x_ref, mine_ref, theirs_ref):
+    kinds, tok, _ = x_ref.shape
+    for out_ref, core in ((mine_ref, core_ref[0]), (theirs_ref, 1 - core_ref[0])):
+        for g in range(out_ref.shape[0]):
+            cols = pl.ds(pl.multiple_of((2 * g + core) * head_dim, head_dim), head_dim)
+            for k in range(kinds):
+                out_ref[g, k * tok:(k + 1) * tok, :] = x_ref[k, :, cols]
+
+
+def lanes(x, core, head_dim):
+    kinds, tok, cols = x.shape
+    like = jax.ShapeDtypeStruct((cols // head_dim // 2, kinds * tok, head_dim), x.dtype)
+    return pl.pallas_call(
+        functools.partial(lane_kernel, head_dim),
+        out_shape=(like, like),
+        in_specs=[SMEM, VMEM],
+        out_specs=(VMEM, VMEM),
+        compiler_params=PARAMS,
+    )(core, x)
+
+
+def deal_kernel(place_ref, mine_ref, got_ref, *out_refs):
+    quarter, core = place_ref[0] // 2, place_ref[0] % 2
+    for k, out_ref in enumerate(out_refs):
+        out_ref[core] = mine_ref[quarter ^ k]
+        out_ref[1 - core] = got_ref[quarter ^ k]
+
+
+def deal(mine, got, place):
+    quarters, depth, width = mine.shape
+    return pl.pallas_call(
+        deal_kernel,
+        out_shape=[jax.ShapeDtypeStruct((2, depth, width), mine.dtype)] * quarters,
+        in_specs=[SMEM, VMEM, VMEM],
+        out_specs=[VMEM] * quarters,
+        compiler_params=PARAMS,
+    )(place, mine, got)
+
+
+def sort_kernel(n, place_ref, *refs):
+    in_refs, (q_ref, k_ref, v_ref, kv_ref) = refs[:n], refs[-4:]
+    tok = q_ref.shape[1]
+    for i, ref in enumerate(in_refs):
+        for core in range(2):
+            at = (place_ref[0] // 2 ^ i) * 2 + core
+            keys, values = ref[core, tok:2 * tok, :], ref[core, 2 * tok:, :]
+            q_ref[at] = ref[core, 0:tok, :]
+            k_ref[at] = keys
+            v_ref[at] = values
+            kv_ref[0, at] = keys
+            kv_ref[1, at] = values
+
+
+def sort(parts, place, passed):
+    _, depth, width = parts[0].shape
+    n = len(parts)
+    one = (2 * n, depth // 3, width)
+    like = [jax.ShapeDtypeStruct(shape, parts[0].dtype) for shape in (one, one, one, (2, *one))]
+    same, *rest = pl.pallas_call(
+        functools.partial(sort_kernel, n),
+        out_shape=[jax.ShapeDtypeStruct(passed.shape, passed.dtype)] + like,
+        in_specs=[SMEM] + [VMEM] * n + [ANY],
+        out_specs=[ANY] + [VMEM] * 4,
+        input_output_aliases={1 + n: 0},
+        compiler_params=PARAMS,
+    )(place, *parts, passed)
+    return (*rest, same)
+
+
+def cut_kernel(x_ref, q_ref, kv_ref):
     tok = q_ref.shape[1]
     q_ref[...] = x_ref[:, :tok, :]
-    kv_ref[...] = x_ref[:, tok:, :]
-
-
-def cut(x, passed):
+    kv_ref[0] = x_ref[:, tok:2 * tok, :]
+    kv_ref[1] = x_ref[:, 2 * tok:, :]
+
+
+def cut(x):
     peers, depth, width = x.shape
-    tok, n = depth // 3, len(passed)
-    q, kv, *same = pl.pallas_call(
+    tok = depth // 3
+    return pl.pallas_call(
         cut_kernel,
-        out_shape=[
+        out_shape=(
             jax.ShapeDtypeStruct((peers, tok, width), x.dtype),
-            jax.ShapeDtypeStruct((peers, 2 * tok, width), x.dtype),
-        ] + [jax.ShapeDtypeStruct(y.shape, y.dtype) for y in passed],
-        in_specs=[VMEM] + [ANY] * n,
-        out_specs=[VMEM, VMEM] + [ANY] * n,
-        input_output_aliases={1 + i: 2 + i for i in range(n)},
-        compiler_params=PARAMS,
-    )(x, *passed)
-    return q, kv, same
+            jax.ShapeDtypeStruct((2, peers, tok, width), x.dtype),
+        ),
+        in_specs=[VMEM],
+        out_specs=(VMEM, VMEM),
+        compiler_params=PARAMS,
+    )(x)
 
 
 def after_kernel(*refs):
@@ -120,11 +187,18 @@
     return clip
 
 
-def attention_kernel(head_dim, span, base_ref, clip_ref, q_ref, *refs):
-    *kv_refs, out_ref = refs
+def attention_kernel(head_dim, span, joint, base_ref, clip_ref, q_ref, *refs):
+    *refs, out_ref = refs
+    k_refs, v_refs = [], []
+    for both in joint:
+        ref, *refs = refs
+        k_refs.append(ref.at[0] if both else ref)
+        if not both:
+            value_ref, *refs = refs
+        v_refs.append(ref.at[1] if both else value_ref)
     peers, tok, width = q_ref.shape
     count = peers * tok
-    scale = 1.0 / math.sqrt(head_dim)
+    scale = math.log2(math.e) / math.sqrt(head_dim)
     row = lax.broadcasted_iota(jnp.int32, (count, 1), 0)
     col = lax.broadcasted_iota(jnp.int32, (1, count), 1)
     row_clip = clip_of(row, base_ref[0], span, tok, clip_ref)
@@ -133,28 +207,31 @@
         cols = slice(h * head_dim, (h + 1) * head_dim)
         queries = q_ref[:, :, cols].reshape(count, head_dim)
         top = total = acc = None
-        for first in range(0, len(kv_refs), per_step):
-            scores, masks, values = [], [], []
-            for i, ref in enumerate(kv_refs[first:first + per_step], first):
-                keys = ref[:, 0:tok, cols].reshape(count, head_dim)
-                values.append(ref[:, tok:2 * tok, cols].reshape(count, head_dim))
+        for first in range(0, len(k_refs), per_step):
+            here = range(first, min(first + per_step, len(k_refs)))
+            scores = []
+            for i in here:
+                keys = k_refs[i][:, :, cols].reshape(count, head_dim)
                 s = lax.dot_general(
                     queries, keys, (((1,), (1,)), ((), ())), preferred_element_type=jnp.float32
                 )
-                masks.append(row_clip == clip_of(col, base_ref[i], span, tok, clip_ref))
-                scores.append(jnp.where(masks[-1], s * scale, -1e30))
+                allowed = row_clip == clip_of(col, base_ref[i], span, tok, clip_ref)
+                scores.append(jnp.where(allowed, s * scale, -1e30))
             new_top = functools.reduce(
                 jnp.maximum, [jnp.max(s, axis=1, keepdims=True) for s in scores]
             )
             if top is not None:
                 new_top = jnp.maximum(top, new_top)
-                factor = jnp.exp(top - new_top)
+                factor = jnp.exp2(top - new_top)
                 total, acc = total * factor, acc * factor
             top = new_top
-            for s, allowed, v in zip(scores, masks, values):
-                p = jnp.where(allowed, jnp.exp(s - top), 0.0)
+            for i, s in zip(here, scores):
+                p = jnp.exp2(s - top)
                 part = jnp.sum(p, axis=1, keepdims=True)
-                dot = jnp.dot(p.astype(jnp.bfloat16), v, preferred_element_type=jnp.float32)
+                values = v_refs[i][:, :, cols].reshape(count, head_dim)
+                dot = jnp.dot(
+                    p.astype(jnp.bfloat16), values, preferred_element_type=jnp.float32
+                )
                 total = part if total is None else total + part
                 acc = dot if acc is None else acc + dot
         out_ref[:, cols] = (acc / total).astype(out_ref.dtype)
@@ -162,13 +239,15 @@
 
 def attention(q, kvs, bases, span, frame_clip, head_dim):
     peers, tok, width = q.shape
-    return pl.pallas_call(
-        functools.partial(attention_kernel, head_dim, span),
+    joint = [not isinstance(kv, tuple) for kv in kvs]
+    arrays = [x for kv, both in zip(kvs, joint) for x in ((kv,) if both else kv)]
+    return pl.pallas_call(
+        functools.partial(attention_kernel, head_dim, span, joint),
         out_shape=jax.ShapeDtypeStruct((peers * tok, width), q.dtype),
-        in_specs=[SMEM, SMEM] + [VMEM] * (1 + len(kvs)),
+        in_specs=[SMEM, SMEM] + [VMEM] * (1 + len(arrays)),
         out_specs=VMEM,
         compiler_params=PARAMS,
-    )(jnp.stack([jnp.asarray(i, jnp.int32) for i in bases]), frame_clip, q, *kvs)
+    )(jnp.stack([jnp.asarray(i, jnp.int32) for i in bases]), frame_clip, q, *arrays)
 
 
 def project_kernel(n_attn, at_ref, place_ref, *refs):
@@ -260,7 +339,7 @@
 
 
 def squares(qkv, frame_clip, w_out):
-    group, quarter = ("x", "zl", "core"), ("x", "zl")
+    quarter = ("x", "zl")
     y, x, zh, zl, core = (lax.axis_index(n) for n in ("y", "x", "zh", "zl", "core"))
     tok, head_dim, cols = qkv.shape[1], w_out.shape[0], w_out.shape[1] // 4
     place = ((x * 2 + zl) * 2 + core).astype(jnp.int32).reshape(1)
@@ -274,18 +353,18 @@
     )
     far = after(xor(w_far, ("zh",), 1), cost=AHEAD)
     near = xor(w_near, ("zl",), 1)
-    packed = pack(qkv, 8, head_dim)
-    own = lax.all_to_all(packed, group, split_axis=0, concat_axis=0, tiled=True)
-    q, kv, (far, w_corner) = cut(own, [far, w_corner])
-    kv_far, kv_near = xor(kv, ("zh",), 1), xor(kv, ("y",), 1)
+    kept, given = lanes(qkv, core.astype(jnp.int32).reshape(1), head_dim)
+    parts = deal(kept, xor(given, ("core",), 1), place)
+    q, k, v, kv, far = sort(swap_all(parts, quarter), place, far)
+    w_corner = after(w_corner, k)
+    k_far, v_far = xor(k, ("zh",), 1), xor(v, ("zh",), 1)
     corner = xor(w_corner, ("zh", "zl"), 3)
+    kv_near = xor(kv, ("y",), 1)
     far_rest = xor(far, ("y",), 1)
-    kv_end = xor(kv_far, ("y",), 1)
+    kvs = [kv, (k_far, v_far), kv_near, (xor(k_far, ("y",), 1), xor(v_far, ("y",), 1))]
 
     base, other = y * 2 * FRB, (1 - y) * 2 * FRB
-    attn = attention(
-        q, [kv, kv_far, kv_near, kv_end], [base, base, other, other], 4 * tok, frame_clip, head_dim
-    )
+    attn = attention(q, kvs, [base, base, other, other], 4 * tok, frame_clip, head_dim)
     corner = after(corner, attn)
     corner_rest = xor(corner, ("y",), 1)
     attns = swap_all([attn] * 4, quarter)
@@ -307,7 +386,7 @@
     w_parts = [w_own] + [xor(w_own, ("row",), by) for by in others]
     packed = pack(qkv, 2 * blks, head_dim)
     own = lax.all_to_all(packed, ("blk", "core"), split_axis=0, concat_axis=0, tiled=True)
-    q, kv, _ = cut(own, [])
+    q, kv = cut(own)
     kvs = [kv] + [xor(kv, ("row",), by) for by in others]
     attn = attention(q, kvs, [0] * rows, 2 * tok, frame_clip, head_dim)
     attns = swap_all([attn] * blks, ("blk",))

time: 53.2 us -> 53 us (level)
  local copies, waits for them, and re-layouts: 1.49 us -> 0.17 us
  starting transfers between devices: 24.7 us -> 25.4 us
    ppermute x15 -> x21, starting transfers between devices: 20.9 us -> 25.4 us  [xor(): return lax.ppermute(x, axis, [(i, i ^ by) for i in range(size)])]
    all_to_all x1 -> x0, starting transfers between devices: 3.78 us -> none  [squares(): own = lax.all_to_all(packed, group, split_axis=0, concat_axis=0, tiled=True)]
    ppermute x15 -> x21, waiting for transfers between devices: 18.8 us -> 21.9 us  [xor(): return lax.ppermute(x, axis, [(i, i ^ by) for i in range(size)])]
    all_to_all x1 -> x0, waiting for transfers between devices: 3.08 us -> none  [squares(): own = lax.all_to_all(packed, group, split_axis=0, concat_axis=0, tiled=True)]
    unnamed x6 -> x4, local copies, waits for them, and re-layouts: 1.33 us -> 0.01 us
    pallas_call x1, Pallas kernels: 0.71 us -> 1.81 us  [columns(): pl.pallas_call(columns_kernel, out_shape=[jax.ShapeDtypeStruct((piece[0],...]
    pallas_call x3 -> x4, Pallas kernels: 2.02 us -> 1.34 us  [the longest x1 1.23 us: attention(): pl.pallas_call(functools.partial(attention_kernel, head_dim, span, joint)...]
  transfers between devices with their start and end apart: 16 -> 21, of which waited for: 10 -> 13; matrix products, arithmetic and copies ran while one was open for 0% -> 0% of each run, Pallas kernels for 4% -> 2%
where the time goes in v11:
time: 53 us; the launch traced here: 52.9 us
  starting transfers between devices  25.4 us (48%)
  waiting for transfers between devices  21.9 us (41%)
  Pallas kernels  5.21 us (10%)
    ppermute x21, starting transfers between devices, xor(): return lax.ppermute(x, axis, [(i, i ^ by) for i in range(size)])  25.4 us
    ppermute x21, waiting for transfers between devices, xor(): return lax.ppermute(x, axis, [(i, i ^ by) for i in range(size)])  21.9 us
    pallas_call x1, Pallas kernels, columns(): pl.pallas_call(columns_kernel, out_shape=[jax.ShapeDtypeStruct((piece[0],...  1.81 us
    pallas_call x1, Pallas kernels, attention(): pl.pallas_call(functools.partial(attention_kernel, head_dim, span, joint)...  1.23 us
    pallas_call x1, Pallas kernels, project(): pl.pallas_call(functools.partial(project_kernel, blks), out_shape=(like,...  1.22 us
  transfers between devices with their start and end apart: 21, of which 13 were waited for; matrix products, arithmetic and copies ran while one was open for 0% of the time, Pallas kernels for 2%

profile of v11, /device:TPU:0, one launch (start us, length us, event | category | flops | bytes accessed | tf_op | source)
XLA Modules:
  0.0 52.9 jit_solution(11913077800523087942)
XLA Ops:
  0.0 0.0 copy-start
  0.0 0.1 stack.60.at_ref
  0.1 1.8 %shard_map.39 = (bf16[128,1280]{1,0:T(8,128)(2,1)S(1)}, bf16[64,1280]{1,0:T(8,128)(2,1)S(1)}, bf16[64,1280]{1,0:T(8,128)(2,1)S(1)}, bf16[128,1280]{1,0:T(8,128)(2,1)S(1)}) custom-call(s32[8]{0:T(128)S(1)} %stack.60.at_ref, bf16[128,5120]{1,0:T(8,128)(2,1)} %x_ref.3), custom_call_target="tpu_custom_call" | custom-call | tf_op jit(solution)/shard_map/pallas_call | solution.py:65
  1.9 4.1 %collective-permute-start.4 = (bf16[64,1280]{1,0:T(8,128)(2,1)S(1)}, bf16[64,1280]{1,0:T(8,128)(2,1)S(1)}, u32[]{:S(2)}, u32[]{:S(2)}) collective-permute-start(bf16[64,1280]{1,0:T(8,128)(2,1)S(1)} %get-tuple-element.32), channel_id=1, source_target_pairs={{0,4},{4,0},{1,5},{5,1},{2,6},{6,2},{3,7},{7,3},{8,12},{12,8},{9,1... | collective-permute-start | bytes 491528 | tf_op jit(solution)/shard_map/ppermute | solution.py:334
  6.0 0.0 copy-done
  6.0 0.1 shard_map.37
  6.1 0.1 collective-permute-start
  6.2 1.3 %collective-permute-done.got_ref = bf16[4,96,128]{2,1,0:T(8,128)(2,1)S(1)} collective-permute-done((bf16[4,96,128]{2,1,0:T(8,128)(2,1)S(1)}, bf16[4,96,128]{2,1,0:T(8,128)(2,1)S(1)}, u32[]{:S(2)}, u32[]{:S(2)}) %collective-permute-start) | collective-permute-done | bytes 98336 | tf_op jit(solution)/shard_map/ppermute | solution.py:334
  7.5 1.6 %collective-permute-start.1 = (bf16[2,96,128]{2,1,0:T(8,128)(2,1)S(1)}, bf16[2,96,128]{2,1,0:T(8,128)(2,1)S(1)}, u32[]{:S(2)}, u32[]{:S(2)}) collective-permute-start(bf16[2,96,128]{2,1,0:T(8,128)(2,1)S(1)} %get-tuple-element.29), channel_id=1, source_target_pairs={{0,2},{2,0},{8,10},{10,8},{1,3},{3,1},{9,11},{11,9},{4,6},{6,4},{1... | collective-permute-start | bytes 147464 | tf_op jit(solution)/shard_map/ppermute | solution.py:334
  9.1 1.5 %collective-permute-start.2 = (bf16[2,96,128]{2,1,0:T(8,128)(2,1)S(1)}, bf16[2,96,128]{2,1,0:T(8,128)(2,1)S(1)}, u32[]{:S(2)}, u32[]{:S(2)}) collective-permute-start(bf16[2,96,128]{2,1,0:T(8,128)(2,1)S(1)} %get-tuple-element.30), channel_id=1, source_target_pairs={{0,8},{2,10},{8,0},{10,2},{1,9},{3,11},{9,1},{11,3},{4,12},{6,14},... | collective-permute-start | bytes 147464 | tf_op jit(solution)/shard_map/ppermute | solution.py:334
  10.6 0.0 copy-start.1
  10.6 0.4 collective-permute-start.3
  11.0 2.8 %collective-permute-done.4.refs_0_ = bf16[64,1280]{1,0:T(8,128)(2,1)S(1)} collective-permute-done((bf16[64,1280]{1,0:T(8,128)(2,1)S(1)}, bf16[64,1280]{1,0:T(8,128)(2,1)S(1)}, u32[]{:S(2)}, u32[]{:S(2)}) %collective-permute-start.4) | collective-permute-done | bytes 163872 | tf_op jit(solution)/shard_map/ppermute | solution.py:334
  13.8 0.0 collective-permute-done.1.refs_1_
  13.8 0.0 collective-permute-done.2.refs_2_
  13.8 1.9 %collective-permute-done.3.refs_3_ = bf16[2,96,128]{2,1,0:T(8,128)(2,1)S(1)} collective-permute-done((bf16[2,96,128]{2,1,0:T(8,128)(2,1)S(1)}, bf16[2,96,128]{2,1,0:T(8,128)(2,1)S(1)}, u32[]{:S(2)}, u32[]{:S(2)}) %collective-permute-start.3) | collective-permute-done | bytes 49184 | tf_op jit(solution)/shard_map/ppermute | solution.py:334
  15.8 1.6 %collective-permute-start.7 = (bf16[2,8,32,128]{3,2,1,0:T(8,128)(2,1)S(1)}, bf16[2,8,32,128]{3,2,1,0:T(8,128)(2,1)S(1)}, u32[]{:S(2)}, u32[]{:S(2)}) collective-permute-start(bf16[2,8,32,128]{3,2,1,0:T(8,128)(2,1)S(1)} %get-tuple-element.34.refs_0_), channel_id=1, source_target_pairs={{0,16},{16,0},{1,17},{17,1},{2,18},{18,2},{3,19},{19,3},{4,20},{20... | collective-permute-start | bytes 393224 | tf_op jit(solution)/shard_map/ppermute | solution.py:334
  17.4 0.2 collective-permute-start.6
  17.6 2.8 %collective-permute-start.5 = (bf16[8,32,128]{2,1,0:T(8,128)(2,1)S(1)}, bf16[8,32,128]{2,1,0:T(8,128)(2,1)S(1)}, u32[]{:S(2)}, u32[]{:S(2)}) collective-permute-start(bf16[8,32,128]{2,1,0:T(8,128)(2,1)S(1)} %get-tuple-element.35.refs_1_), channel_id=1, source_target_pairs={{0,4},{4,0},{1,5},{5,1},{2,6},{6,2},{3,7},{7,3},{8,12},{12,8},{9,1... | collective-permute-start | bytes 196616 | tf_op jit(solution)/shard_map/ppermute | solution.py:334
  20.3 0.6 %collective-permute-start.13 = (bf16[128,1280]{1,0:T(8,128)(2,1)S(1)}, bf16[128,1280]{1,0:T(8,128)(2,1)S(1)}, u32[]{:S(2)}, u32[]{:S(2)}) collective-permute-start(bf16[128,1280]{1,0:T(8,128)(2,1)S(1)} %get-tuple-element.38), channel_id=1, source_target_pairs={{0,2},{2,0},{1,3},{3,1},{4,6},{6,4},{5,7},{7,5},{8,10},{10,8},{9,1... | collective-permute-start | bytes 983048 | tf_op jit(solution)/shard_map/ppermute | solution.py:334
  21.0 2.3 %collective-permute-start.15 = (bf16[64,1280]{1,0:T(8,128)(2,1)S(1)}, bf16[64,1280]{1,0:T(8,128)(2,1)S(1)}, u32[]{:S(2)}, u32[]{:S(2)}) collective-permute-start(bf16[64,1280]{1,0:T(8,128)(2,1)S(1)} %shard_map.43), channel_id=1, source_target_pairs={{0,6},{2,4},{4,2},{6,0},{1,7},{3,5},{5,3},{7,1},{8,14},{10,12},{12... | collective-permute-start | bytes 491528 | tf_op jit(solution)/shard_map/ppermute | solution.py:334
  23.3 1.2 %collective-permute-done.6.refs_2_ = bf16[8,32,128]{2,1,0:T(8,128)(2,1)S(1)} collective-permute-done((bf16[8,32,128]{2,1,0:T(8,128)(2,1)S(1)}, bf16[8,32,128]{2,1,0:T(8,128)(2,1)S(1)}, u32[]{:S(2)}, u32[]{:S(2)}) %collective-permute-start.6) | collective-permute-done | bytes 65568 | tf_op jit(solution)/shard_map/ppermute | solution.py:334
  24.5 0.5 collective-permute-start.14
  25.0 1.6 %collective-permute-done.5.refs_1_ = bf16[8,32,128]{2,1,0:T(8,128)(2,1)S(1)} collective-permute-done((bf16[8,32,128]{2,1,0:T(8,128)(2,1)S(1)}, bf16[8,32,128]{2,1,0:T(8,128)(2,1)S(1)}, u32[]{:S(2)}, u32[]{:S(2)}) %collective-permute-start.5) | collective-permute-done | bytes 65568 | tf_op jit(solution)/shard_map/ppermute | solution.py:334
  26.6 0.5 collective-permute-start.9
  27.1 0.0 collective-permute-done.7.refs_3_
  27.1 1.5 %collective-permute-start.8 = (bf16[8,32,128]{2,1,0:T(8,128)(2,1)S(1)}, bf16[8,32,128]{2,1,0:T(8,128)(2,1)S(1)}, u32[]{:S(2)}, u32[]{:S(2)}) collective-permute-start(bf16[8,32,128]{2,1,0:T(8,128)(2,1)S(1)} %collective-permute-done.5.refs_1_), channel_id=1, source_target_pairs={{0,16},{16,0},{1,17},{17,1},{2,18},{18,2},{3,19},{19,3},{4,20},{20... | collective-permute-start | bytes 196616 | tf_op jit(solution)/shard_map/ppermute | solution.py:334
  28.7 0.1 pad_add_fusion.base_ref
  28.7 2.2 %collective-permute-done.9.refs_5_ = bf16[8,32,128]{2,1,0:T(8,128)(2,1)S(1)} collective-permute-done((bf16[8,32,128]{2,1,0:T(8,128)(2,1)S(1)}, bf16[8,32,128]{2,1,0:T(8,128)(2,1)S(1)}, u32[]{:S(2)}, u32[]{:S(2)}) %collective-permute-start.9) | collective-permute-done | bytes 65568 | tf_op jit(solution)/shard_map/ppermute | solution.py:334
  30.9 0.7 %collective-permute-done.8.refs_4_ = bf16[8,32,128]{2,1,0:T(8,128)(2,1)S(1)} collective-permute-done((bf16[8,32,128]{2,1,0:T(8,128)(2,1)S(1)}, bf16[8,32,128]{2,1,0:T(8,128)(2,1)S(1)}, u32[]{:S(2)}, u32[]{:S(2)}) %collective-permute-start.8) | collective-permute-done | bytes 65568 | tf_op jit(solution)/shard_map/ppermute | solution.py:334
  31.6 0.0 copy-done.1
  31.6 1.2 %shard_map.42.refs_1_.refs_0_ = bf16[256,128]{1,0:T(8,128)(2,1)S(1)} custom-call(s32[4]{0:T(128)S(1)} %pad_add_fusion.base_ref, s32[8]{0:T(128)S(1)} %copy-done.1, bf16[8,32,128]{2,1,0:T(8,128)(2,1)S(1)} %get-tuple-element.33.q_ref, bf16[2,8,32,128]{3,2,1,0:T(8,128)(2,1)S(1)} %get-tuple-element.34.refs_0_, ...), custom_call_target="tpu_custom_call" | custom-call | tf_op jit(solution)/shard_map/pallas_call | solution.py:244
  32.8 1.7 %collective-permute-done.15.refs_0_ = bf16[64,1280]{1,0:T(8,128)(2,1)S(1)} collective-permute-done((bf16[64,1280]{1,0:T(8,128)(2,1)S(1)}, bf16[64,1280]{1,0:T(8,128)(2,1)S(1)}, u32[]{:S(2)}, u32[]{:S(2)}) %collective-permute-start.15) | collective-permute-done | bytes 163872 | tf_op jit(solution)/shard_map/ppermute | solution.py:334
  34.6 0.5 collective-permute-start.16
  35.1 0.0 collective-permute-start.12
  35.1 0.8 %collective-permute-start.11 = (bf16[256,128]{1,0:T(8,128)(2,1)S(1)}, bf16[256,128]{1,0:T(8,128)(2,1)S(1)}, u32[]{:S(2)}, u32[]{:S(2)}) collective-permute-start(bf16[256,128]{1,0:T(8,128)(2,1)S(1)} %shard_map.42.refs_1_.refs_0_), channel_id=1, source_target_pairs={{0,8},{2,10},{8,0},{10,2},{1,9},{3,11},{9,1},{11,3},{4,12},{6,14},... | collective-permute-start | bytes 196616 | tf_op jit(solution)/shard_map/ppermute | solution.py:334
  35.9 0.0 collective-permute-done.14.refs_7_
  35.9 2.7 %collective-permute-start.10 = (bf16[256,128]{1,0:T(8,128)(2,1)S(1)}, bf16[256,128]{1,0:T(8,128)(2,1)S(1)}, u32[]{:S(2)}, u32[]{:S(2)}) collective-permute-start(bf16[256,128]{1,0:T(8,128)(2,1)S(1)} %shard_map.42.refs_1_.refs_0_), channel_id=1, source_target_pairs={{0,2},{2,0},{8,10},{10,8},{1,3},{3,1},{9,11},{11,9},{4,6},{6,4},{1... | collective-permute-start | bytes 196616 | tf_op jit(solution)/shard_map/ppermute | solution.py:334
  38.6 0.1 stack.53.at_ref
  38.7 0.0 collective-permute-done.13.refs_5_
  38.7 1.6 %collective-permute-done.12.refs_3_ = bf16[256,128]{1,0:T(8,128)(2,1)S(1)} collective-permute-done((bf16[256,128]{1,0:T(8,128)(2,1)S(1)}, bf16[256,128]{1,0:T(8,128)(2,1)S(1)}, u32[]{:S(2)}, u32[]{:S(2)}) %collective-permute-start.12) | collective-permute-done | bytes 65568 | tf_op jit(solution)/shard_map/ppermute | solution.py:334
  40.3 0.0 collective-permute-done.11.refs_2_
  40.3 0.6 %collective-permute-done.10.refs_1_ = bf16[256,128]{1,0:T(8,128)(2,1)S(1)} collective-permute-done((bf16[256,128]{1,0:T(8,128)(2,1)S(1)}, bf16[256,128]{1,0:T(8,128)(2,1)S(1)}, u32[]{:S(2)}, u32[]{:S(2)}) %collective-permute-start.10) | collective-permute-done | bytes 65568 | tf_op jit(solution)/shard_map/ppermute | solution.py:334
  40.8 0.0 collective-permute-done.16.refs_9_
  40.8 1.2 %shard_map.45 = (bf16[4,32,1280]{2,1,0:T(8,128)(2,1)S(1)}, bf16[4,32,1280]{2,1,0:T(8,128)(2,1)S(1)}) custom-call(s32[6]{0:T(128)S(1)} %stack.53.at_ref, s32[1]{0:T(128)} %bitcast.place_ref, bf16[256,128]{1,0:T(8,128)(2,1)S(1)} %shard_map.42.refs_1_.refs_0_, bf16[256,128]{1,0:T(8,128)(2,1)S(1)} %collective-permute-done.10.refs_1_, ...), custom_call_target="tpu_custom_call" | custom-call | tf_op jit(solution)/shard_map/pallas_call | solution.py:282
  42.1 0.1 collective-permute-start.17
  42.1 1.6 %collective-permute-done.17.y_ref = bf16[4,32,1280]{2,1,0:T(8,128)(2,1)S(1)} collective-permute-done((bf16[4,32,1280]{2,1,0:T(8,128)(2,1)S(1)}, bf16[4,32,1280]{2,1,0:T(8,128)(2,1)S(1)}, u32[]{:S(2)}, u32[]{:S(2)}) %collective-permute-start.17) | collective-permute-done | bytes 327712 | tf_op jit(solution)/shard_map/ppermute | solution.py:334
  43.8 0.1 shard_map.46
  43.8 2.1 %collective-permute-start.18 = (bf16[32,1280]{1,0:T(8,128)(2,1)S(1)}, bf16[32,1280]{1,0:T(8,128)(2,1)S(1)}, u32[]{:S(2)}, u32[]{:S(2)}) collective-permute-start(bf16[32,1280]{1,0:T(8,128)(2,1)S(1)} %get-tuple-element.44), channel_id=1, source_target_pairs={{0,2},{2,0},{8,10},{10,8},{1,3},{3,1},{9,11},{11,9},{4,6},{6,4},{1... | collective-permute-start | bytes 245768 | tf_op jit(solution)/shard_map/ppermute | solution.py:334
  45.9 0.8 %collective-permute-start.19 = (bf16[32,1280]{1,0:T(8,128)(2,1)S(1)}, bf16[32,1280]{1,0:T(8,128)(2,1)S(1)}, u32[]{:S(2)}, u32[]{:S(2)}) collective-permute-start(bf16[32,1280]{1,0:T(8,128)(2,1)S(1)} %get-tuple-element.45), channel_id=1, source_target_pairs={{0,8},{2,10},{8,0},{10,2},{1,9},{3,11},{9,1},{11,3},{4,12},{6,14},... | collective-permute-start | bytes 245768 | tf_op jit(solution)/shard_map/ppermute | solution.py:334
  46.7 0.8 %collective-permute-start.20 = (bf16[32,1280]{1,0:T(8,128)(2,1)S(1)}, bf16[32,1280]{1,0:T(8,128)(2,1)S(1)}, u32[]{:S(2)}, u32[]{:S(2)}) collective-permute-start(bf16[32,1280]{1,0:T(8,128)(2,1)S(1)} %get-tuple-element.46), channel_id=1, source_target_pairs={{0,10},{2,8},{8,2},{10,0},{1,11},{3,9},{9,3},{11,1},{4,14},{6,12},... | collective-permute-start | bytes 245768 | tf_op jit(solution)/shard_map/ppermute | solution.py:334
  47.5 1.2 %collective-permute-done.18.refs_1_ = bf16[32,1280]{1,0:T(8,128)(2,1)S(1)} collective-permute-done((bf16[32,1280]{1,0:T(8,128)(2,1)S(1)}, bf16[32,1280]{1,0:T(8,128)(2,1)S(1)}, u32[]{:S(2)}, u32[]{:S(2)}) %collective-permute-start.18) | collective-permute-done | bytes 81952 | tf_op jit(solution)/shard_map/ppermute | solution.py:334
  48.7 3.5 %collective-permute-done.19.refs_2_ = bf16[32,1280]{1,0:T(8,128)(2,1)S(1)} collective-permute-done((bf16[32,1280]{1,0:T(8,128)(2,1)S(1)}, bf16[32,1280]{1,0:T(8,128)(2,1)S(1)}, u32[]{:S(2)}, u32[]{:S(2)}) %collective-permute-start.19) | collective-permute-done | bytes 81952 | tf_op jit(solution)/shard_map/ppermute | solution.py:334
  52.1 0.0 collective-permute-done.20.refs_3_
  52.1 0.8 %shard_map.47 = bf16[32,5120]{1,0:T(8,128)(2,1)} custom-call(s32[1]{0:T(128)} %bitcast.place_ref, bf16[32,1280]{1,0:T(8,128)(2,1)S(1)} %get-tuple-element.43.refs_0_, bf16[32,1280]{1,0:T(8,128)(2,1)S(1)} %collective-permute-done.18.refs_1_, bf16[32,1280]{1,0:T(8,128)(2,1)S(1)} %collective-permute-done.19.refs_2_, ...), custom_call_target="tpu_custom_call" | custom-call | tf_op jit(solution)/shard_map/pallas_call | solution.py:323
  (5 shorter events, 0.1 us)
Async XLA Ops:
  0.0 6.0 %copy-start = (bf16[3,32,1024]{2,1,0:T(8,128)(2,1)S(1)}, bf16[3,32,1024]{2,1,0:T(8,128)(2,1)}, u32[]{:S(2)}) copy-start(bf16[3,32,1024]{2,1,0:T(8,128)(2,1)} %x_ref.2) | copy-start | bytes 589828
  1.9 11.9 %collective-permute-start.4 = (bf16[64,1280]{1,0:T(8,128)(2,1)S(1)}, bf16[64,1280]{1,0:T(8,128)(2,1)S(1)}, u32[]{:S(2)}, u32[]{:S(2)}) collective-permute-start(bf16[64,1280]{1,0:T(8,128)(2,1)S(1)} %get-tuple-element.32), channel_id=1, source_target_pairs={{0,4},{4,0},{1,5},{5,1},{2,6},{6,2},{3,7},{7,3},{8,12},{12,8},{9,1... | collective-permute-start | bytes 491528 | tf_op jit(solution)/shard_map/ppermute | solution.py:334
  6.1 1.4 %collective-permute-start = (bf16[4,96,128]{2,1,0:T(8,128)(2,1)S(1)}, bf16[4,96,128]{2,1,0:T(8,128)(2,1)S(1)}, u32[]{:S(2)}, u32[]{:S(2)}) collective-permute-start(bf16[4,96,128]{2,1,0:T(8,128)(2,1)S(1)} %get-tuple-element.27), channel_id=1, source_target_pairs={{0,1},{1,0},{2,3},{3,2},{4,5},{5,4},{6,7},{7,6},{8,9},{9,8},{10,11... | collective-permute-start | bytes 294920 | tf_op jit(solution)/shard_map/ppermute | solution.py:334
  7.5 6.4 %collective-permute-start.1 = (bf16[2,96,128]{2,1,0:T(8,128)(2,1)S(1)}, bf16[2,96,128]{2,1,0:T(8,128)(2,1)S(1)}, u32[]{:S(2)}, u32[]{:S(2)}) collective-permute-start(bf16[2,96,128]{2,1,0:T(8,128)(2,1)S(1)} %get-tuple-element.29), channel_id=1, source_target_pairs={{0,2},{2,0},{8,10},{10,8},{1,3},{3,1},{9,11},{11,9},{4,6},{6,4},{1... | collective-permute-start | bytes 147464 | tf_op jit(solution)/shard_map/ppermute | solution.py:334
  9.1 4.7 %collective-permute-start.2 = (bf16[2,96,128]{2,1,0:T(8,128)(2,1)S(1)}, bf16[2,96,128]{2,1,0:T(8,128)(2,1)S(1)}, u32[]{:S(2)}, u32[]{:S(2)}) collective-permute-start(bf16[2,96,128]{2,1,0:T(8,128)(2,1)S(1)} %get-tuple-element.30), channel_id=1, source_target_pairs={{0,8},{2,10},{8,0},{10,2},{1,9},{3,11},{9,1},{11,3},{4,12},{6,14},... | collective-permute-start | bytes 147464 | tf_op jit(solution)/shard_map/ppermute | solution.py:334
  10.6 21.0 %copy-start.1 = (s32[8]{0:T(128)S(1)}, s32[8]{0:T(128)}, u32[]{:S(2)}) copy-start(s32[8]{0:T(128)} %clip_ref.1) | copy-start | bytes 100
  10.6 5.2 %collective-permute-start.3 = (bf16[2,96,128]{2,1,0:T(8,128)(2,1)S(1)}, bf16[2,96,128]{2,1,0:T(8,128)(2,1)S(1)}, u32[]{:S(2)}, u32[]{:S(2)}) collective-permute-start(bf16[2,96,128]{2,1,0:T(8,128)(2,1)S(1)} %get-tuple-element.31), channel_id=1, source_target_pairs={{0,10},{2,8},{8,2},{10,0},{1,11},{3,9},{9,3},{11,1},{4,14},{6,12},... | collective-permute-start | bytes 147464 | tf_op jit(solution)/shard_map/ppermute | solution.py:334
  15.8 11.3 %collective-permute-start.7 = (bf16[2,8,32,128]{3,2,1,0:T(8,128)(2,1)S(1)}, bf16[2,8,32,128]{3,2,1,0:T(8,128)(2,1)S(1)}, u32[]{:S(2)}, u32[]{:S(2)}) collective-permute-start(bf16[2,8,32,128]{3,2,1,0:T(8,128)(2,1)S(1)} %get-tuple-element.34.refs_0_), channel_id=1, source_target_pairs={{0,16},{16,0},{1,17},{17,1},{2,18},{18,2},{3,19},{19,3},{4,20},{20... | collective-permute-start | bytes 393224 | tf_op jit(solution)/shard_map/ppermute | solution.py:334
  17.4 7.1 %collective-permute-start.6 = (bf16[8,32,128]{2,1,0:T(8,128)(2,1)S(1)}, bf16[8,32,128]{2,1,0:T(8,128)(2,1)S(1)}, u32[]{:S(2)}, u32[]{:S(2)}) collective-permute-start(bf16[8,32,128]{2,1,0:T(8,128)(2,1)S(1)} %get-tuple-element.36), channel_id=1, source_target_pairs={{0,4},{4,0},{1,5},{5,1},{2,6},{6,2},{3,7},{7,3},{8,12},{12,8},{9,1... | collective-permute-start | bytes 196616 | tf_op jit(solution)/shard_map/ppermute | solution.py:334
  17.6 9.1 %collective-permute-start.5 = (bf16[8,32,128]{2,1,0:T(8,128)(2,1)S(1)}, bf16[8,32,128]{2,1,0:T(8,128)(2,1)S(1)}, u32[]{:S(2)}, u32[]{:S(2)}) collective-permute-start(bf16[8,32,128]{2,1,0:T(8,128)(2,1)S(1)} %get-tuple-element.35.refs_1_), channel_id=1, source_target_pairs={{0,4},{4,0},{1,5},{5,1},{2,6},{6,2},{3,7},{7,3},{8,12},{12,8},{9,1... | collective-permute-start | bytes 196616 | tf_op jit(solution)/shard_map/ppermute | solution.py:334
  20.3 18.4 %collective-permute-start.13 = (bf16[128,1280]{1,0:T(8,128)(2,1)S(1)}, bf16[128,1280]{1,0:T(8,128)(2,1)S(1)}, u32[]{:S(2)}, u32[]{:S(2)}) collective-permute-start(bf16[128,1280]{1,0:T(8,128)(2,1)S(1)} %get-tuple-element.38), channel_id=1, source_target_pairs={{0,2},{2,0},{1,3},{3,1},{4,6},{6,4},{5,7},{7,5},{8,10},{10,8},{9,1... | collective-permute-start | bytes 983048 | tf_op jit(solution)/shard_map/ppermute | solution.py:334
  21.0 13.6 %collective-permute-start.15 = (bf16[64,1280]{1,0:T(8,128)(2,1)S(1)}, bf16[64,1280]{1,0:T(8,128)(2,1)S(1)}, u32[]{:S(2)}, u32[]{:S(2)}) collective-permute-start(bf16[64,1280]{1,0:T(8,128)(2,1)S(1)} %shard_map.43), channel_id=1, source_target_pairs={{0,6},{2,4},{4,2},{6,0},{1,7},{3,5},{5,3},{7,1},{8,14},{10,12},{12... | collective-permute-start | bytes 491528 | tf_op jit(solution)/shard_map/ppermute | solution.py:334
  24.5 11.4 %collective-permute-start.14 = (bf16[64,1280]{1,0:T(8,128)(2,1)S(1)}, bf16[64,1280]{1,0:T(8,128)(2,1)S(1)}, u32[]{:S(2)}, u32[]{:S(2)}) collective-permute-start(bf16[64,1280]{1,0:T(8,128)(2,1)S(1)} %get-tuple-element.39.refs_6_), channel_id=1, source_target_pairs={{0,16},{16,0},{1,17},{17,1},{2,18},{18,2},{3,19},{19,3},{4,20},{20... | collective-permute-start | bytes 491528 | tf_op jit(solution)/shard_map/ppermute | solution.py:334
  26.6 4.3 %collective-permute-start.9 = (bf16[8,32,128]{2,1,0:T(8,128)(2,1)S(1)}, bf16[8,32,128]{2,1,0:T(8,128)(2,1)S(1)}, u32[]{:S(2)}, u32[]{:S(2)}) collective-permute-start(bf16[8,32,128]{2,1,0:T(8,128)(2,1)S(1)} %collective-permute-done.6.refs_2_), channel_id=1, source_target_pairs={{0,16},{16,0},{1,17},{17,1},{2,18},{18,2},{3,19},{19,3},{4,20},{20... | collective-permute-start | bytes 196616 | tf_op jit(solution)/shard_map/ppermute | solution.py:334
  27.1 4.4 %collective-permute-start.8 = (bf16[8,32,128]{2,1,0:T(8,128)(2,1)S(1)}, bf16[8,32,128]{2,1,0:T(8,128)(2,1)S(1)}, u32[]{:S(2)}, u32[]{:S(2)}) collective-permute-start(bf16[8,32,128]{2,1,0:T(8,128)(2,1)S(1)} %collective-permute-done.5.refs_1_), channel_id=1, source_target_pairs={{0,16},{16,0},{1,17},{17,1},{2,18},{18,2},{3,19},{19,3},{4,20},{20... | collective-permute-start | bytes 196616 | tf_op jit(solution)/shard_map/ppermute | solution.py:334
  34.6 6.3 %collective-permute-start.16 = (bf16[64,1280]{1,0:T(8,128)(2,1)S(1)}, bf16[64,1280]{1,0:T(8,128)(2,1)S(1)}, u32[]{:S(2)}, u32[]{:S(2)}) collective-permute-start(bf16[64,1280]{1,0:T(8,128)(2,1)S(1)} %shard_map.44.refs_8_), channel_id=1, source_target_pairs={{0,16},{16,0},{1,17},{17,1},{2,18},{18,2},{3,19},{19,3},{4,20},{20... | collective-permute-start | bytes 491528 | tf_op jit(solution)/shard_map/ppermute | solution.py:334
  35.1 5.2 %collective-permute-start.12 = (bf16[256,128]{1,0:T(8,128)(2,1)S(1)}, bf16[256,128]{1,0:T(8,128)(2,1)S(1)}, u32[]{:S(2)}, u32[]{:S(2)}) collective-permute-start(bf16[256,128]{1,0:T(8,128)(2,1)S(1)} %shard_map.42.refs_1_.refs_0_), channel_id=1, source_target_pairs={{0,10},{2,8},{8,2},{10,0},{1,11},{3,9},{9,3},{11,1},{4,14},{6,12},... | collective-permute-start | bytes 196616 | tf_op jit(solution)/shard_map/ppermute | solution.py:334
  35.1 5.2 %collective-permute-start.11 = (bf16[256,128]{1,0:T(8,128)(2,1)S(1)}, bf16[256,128]{1,0:T(8,128)(2,1)S(1)}, u32[]{:S(2)}, u32[]{:S(2)}) collective-permute-start(bf16[256,128]{1,0:T(8,128)(2,1)S(1)} %shard_map.42.refs_1_.refs_0_), channel_id=1, source_target_pairs={{0,8},{2,10},{8,0},{10,2},{1,9},{3,11},{9,1},{11,3},{4,12},{6,14},... | collective-permute-start | bytes 196616 | tf_op jit(solution)/shard_map/ppermute | solution.py:334
  35.9 4.9 %collective-permute-start.10 = (bf16[256,128]{1,0:T(8,128)(2,1)S(1)}, bf16[256,128]{1,0:T(8,128)(2,1)S(1)}, u32[]{:S(2)}, u32[]{:S(2)}) collective-permute-start(bf16[256,128]{1,0:T(8,128)(2,1)S(1)} %shard_map.42.refs_1_.refs_0_), channel_id=1, source_target_pairs={{0,2},{2,0},{8,10},{10,8},{1,3},{3,1},{9,11},{11,9},{4,6},{6,4},{1... | collective-permute-start | bytes 196616 | tf_op jit(solution)/shard_map/ppermute | solution.py:334
  42.1 1.7 %collective-permute-start.17 = (bf16[4,32,1280]{2,1,0:T(8,128)(2,1)S(1)}, bf16[4,32,1280]{2,1,0:T(8,128)(2,1)S(1)}, u32[]{:S(2)}, u32[]{:S(2)}) collective-permute-start(bf16[4,32,1280]{2,1,0:T(8,128)(2,1)S(1)} %get-tuple-element.42), channel_id=1, source_target_pairs={{0,1},{1,0},{2,3},{3,2},{4,5},{5,4},{6,7},{7,6},{8,9},{9,8},{10,11... | collective-permute-start | bytes 983048 | tf_op jit(solution)/shard_map/ppermute | solution.py:334
  43.8 4.8 %collective-permute-start.18 = (bf16[32,1280]{1,0:T(8,128)(2,1)S(1)}, bf16[32,1280]{1,0:T(8,128)(2,1)S(1)}, u32[]{:S(2)}, u32[]{:S(2)}) collective-permute-start(bf16[32,1280]{1,0:T(8,128)(2,1)S(1)} %get-tuple-element.44), channel_id=1, source_target_pairs={{0,2},{2,0},{8,10},{10,8},{1,3},{3,1},{9,11},{11,9},{4,6},{6,4},{1... | collective-permute-start | bytes 245768 | tf_op jit(solution)/shard_map/ppermute | solution.py:334
  45.9 6.2 %collective-permute-start.19 = (bf16[32,1280]{1,0:T(8,128)(2,1)S(1)}, bf16[32,1280]{1,0:T(8,128)(2,1)S(1)}, u32[]{:S(2)}, u32[]{:S(2)}) collective-permute-start(bf16[32,1280]{1,0:T(8,128)(2,1)S(1)} %get-tuple-element.45), channel_id=1, source_target_pairs={{0,8},{2,10},{8,0},{10,2},{1,9},{3,11},{9,1},{11,3},{4,12},{6,14},... | collective-permute-start | bytes 245768 | tf_op jit(solution)/shard_map/ppermute | solution.py:334
  46.7 5.4 %collective-permute-start.20 = (bf16[32,1280]{1,0:T(8,128)(2,1)S(1)}, bf16[32,1280]{1,0:T(8,128)(2,1)S(1)}, u32[]{:S(2)}, u32[]{:S(2)}) collective-permute-start(bf16[32,1280]{1,0:T(8,128)(2,1)S(1)} %get-tuple-element.46), channel_id=1, source_target_pairs={{0,10},{2,8},{8,2},{10,0},{1,11},{3,9},{9,3},{11,1},{4,14},{6,12},... | collective-permute-start | bytes 245768 | tf_op jit(solution)/shard_map/ppermute | solution.py:334

commit v12 on v11

v12 whole, which is shorter than its diff:
```python
import functools
import math

import jax
import jax.numpy as jnp
from jax import lax
from jax.experimental import pallas as pl
from jax.experimental.pallas import tpu as pltpu
from jax.sharding import Mesh
from jax.sharding import PartitionSpec as P

FRB = 2
TPF = 16
LANES = 128
VMEM = pl.BlockSpec(memory_space=pltpu.VMEM)
SMEM = pl.BlockSpec(memory_space=pltpu.SMEM)
ANY = pl.BlockSpec(memory_space=pl.ANY)
PARAMS = pltpu.CompilerParams(vmem_limit_bytes=48 * 1024 * 1024)
AHEAD = pl.CostEstimate(flops=20_000_000_000, bytes_accessed=1_000_000, transcendentals=0)


def rows_at(index, size):
    return pl.ds(pl.multiple_of(index * size, size), size)


def index_array(*numbers):
    return jnp.stack([jnp.asarray(i, jnp.int32) for i in numbers])


def pack_kernel(head_dim, x_ref, out_ref):
    peers, _, width = out_ref.shape
    kinds, tok, _ = x_ref.shape
    heads = width // head_dim
    for g in range(peers):
        for i in range(heads):
            head = (g // 2 * heads + i) * 2 + g % 2
            for k in range(kinds):
                out_ref[g, k * tok:(k + 1) * tok, i * head_dim:(i + 1) * head_dim] = x_ref[
                    k, :, head * head_dim:(head + 1) * head_dim
                ]


def pack(x, peers, head_dim):
    kinds, tok, cols = x.shape
    return pl.pallas_call(
        functools.partial(pack_kernel, head_dim),
        out_shape=jax.ShapeDtypeStruct((peers, kinds * tok, cols // peers), x.dtype),
        in_specs=[VMEM],
        out_specs=VMEM,
        compiler_params=PARAMS,
    )(x)


def copy_all(copies):
    for copy in copies:
        copy.start()
    for copy in copies:
        copy.wait()


def columns_kernel(at_ref, x_ref, *refs):
    *out_refs, sems = refs
    copies = []
    for i, ref in enumerate(out_refs):
        depth, cols = ref.shape
        piece = x_ref.at[rows_at(at_ref[2 * i], depth), rows_at(at_ref[2 * i + 1], cols)]
        copies.append(pltpu.make_async_copy(piece, ref, sems.at[i]))
    copy_all(copies)


def columns(x, pieces, cols):
    return pl.pallas_call(
        columns_kernel,
        out_shape=[jax.ShapeDtypeStruct((piece[0], cols), x.dtype) for piece in pieces],
        in_specs=[SMEM, pl.BlockSpec(memory_space=pltpu.HBM)],
        out_specs=[VMEM] * len(pieces),
        scratch_shapes=[pltpu.SemaphoreType.DMA((len(pieces),))],
        compiler_params=PARAMS,
    )(
        index_array(*[i for piece in pieces for i in piece[1:]]),
        pltpu.with_memory_space_constraint(x, pltpu.HBM),
    )


def blocks_kernel(depth, at_ref, x_ref, out_ref, sems):
    blocks = out_ref.shape[0] // depth
    copies = []
    for j in range(blocks):
        piece = x_ref.at[rows_at(at_ref[0], depth), rows_at(at_ref[1] * blocks + j, LANES)]
        copies.append(pltpu.make_async_copy(piece, out_ref.at[j * depth:(j + 1) * depth], sems.at[j]))
    copy_all(copies)


def blocks(x, depth, row_at, col_at, cols):
    count = cols // LANES
    return pl.pallas_call(
        functools.partial(blocks_kernel, depth),
        out_shape=jax.ShapeDtypeStruct((count * depth, LANES), x.dtype),
        in_specs=[SMEM, pl.BlockSpec(memory_space=pltpu.HBM)],
        out_specs=VMEM,
        scratch_shapes=[pltpu.SemaphoreType.DMA((count,))],
        compiler_params=PARAMS,
    )(index_array(row_at, col_at), pltpu.with_memory_space_constraint(x, pltpu.HBM))


def lane_kernel(head_dim, core_ref, x_ref, mine_ref, theirs_ref):
    kinds, tok, _ = x_ref.shape
    for out_ref, core in ((mine_ref, core_ref[0]), (theirs_ref, 1 - core_ref[0])):
        for g in range(out_ref.shape[0]):
            cols = rows_at(2 * g + core, head_dim)
            for k in range(kinds):
                out_ref[g, k * tok:(k + 1) * tok, :] = x_ref[k, :, cols]


def lanes(x, core, head_dim):
    kinds, tok, cols = x.shape
    like = jax.ShapeDtypeStruct((cols // head_dim // 2, kinds * tok, head_dim), x.dtype)
    return pl.pallas_call(
        functools.partial(lane_kernel, head_dim),
        out_shape=(like, like),
        in_specs=[SMEM, VMEM],
        out_specs=(VMEM, VMEM),
        compiler_params=PARAMS,
    )(index_array(core), x)


def deal_kernel(place_ref, mine_ref, got_ref, *out_refs):
    quarter, core = place_ref[0] // 2, place_ref[0] % 2
    for k, out_ref in enumerate(out_refs):
        out_ref[core] = mine_ref[quarter ^ k]
        out_ref[1 - core] = got_ref[quarter ^ k]


def deal(mine, got, place):
    quarters, depth, width = mine.shape
    return pl.pallas_call(
        deal_kernel,
        out_shape=[jax.ShapeDtypeStruct((2, depth, width), mine.dtype)] * quarters,
        in_specs=[SMEM, VMEM, VMEM],
        out_specs=[VMEM] * quarters,
        compiler_params=PARAMS,
    )(place, mine, got)


def sort_kernel(n, place_ref, *refs):
    in_refs, (more_ref, q_ref, k_ref, v_ref, all_ref) = refs[:n], refs[n:]
    count = q_ref.shape[0]
    tok = count // (2 * n)
    for i, ref in enumerate(in_refs):
        for core in range(2):
            at = (place_ref[0] // 2 ^ i) * 2 + core
            keys, values = ref[core, tok:2 * tok, :], ref[core, 2 * tok:, :]
            q_ref[rows_at(at, tok), :] = ref[core, 0:tok, :]
            k_ref[rows_at(at, tok), :] = keys
            v_ref[rows_at(at, tok), :] = values
            all_ref[rows_at(at, tok), :] = keys
            all_ref[rows_at(at + 2 * n, tok), :] = values
    all_ref[2 * count:, :] = more_ref[...]


def sort(parts, place, more):
    _, depth, width = parts[0].shape
    n = len(parts)
    count = 2 * n * (depth // 3)
    sizes = (count, count, count, 2 * count + more.shape[0])
    return pl.pallas_call(
        functools.partial(sort_kernel, n),
        out_shape=[jax.ShapeDtypeStruct((size, width), more.dtype) for size in sizes],
        in_specs=[SMEM] + [VMEM] * (n + 1),
        out_specs=[VMEM] * 4,
        compiler_params=PARAMS,
    )(place, *parts, more)


def cut_kernel(x_ref, q_ref, kv_ref):
    peers, depth, _ = x_ref.shape
    tok = depth // 3
    for g in range(peers):
        q_ref[g * tok:(g + 1) * tok, :] = x_ref[g, :tok, :]
        for i in range(2):
            kv_ref[(i * peers + g) * tok:(i * peers + g + 1) * tok, :] = x_ref[
                g, (i + 1) * tok:(i + 2) * tok, :
            ]


def cut(x):
    peers, depth, width = x.shape
    count = peers * depth // 3
    return pl.pallas_call(
        cut_kernel,
        out_shape=[jax.ShapeDtypeStruct((size, width), x.dtype) for size in (count, 2 * count)],
        in_specs=[VMEM],
        out_specs=[VMEM, VMEM],
        compiler_params=PARAMS,
    )(x)


def after_kernel(*refs):
    pass


def after(passed, *first, cost=None):
    return pl.pallas_call(
        after_kernel,
        out_shape=jax.ShapeDtypeStruct(passed.shape, passed.dtype),
        in_specs=[ANY] * (1 + len(first)),
        out_specs=ANY,
        input_output_aliases={0: 0},
        compiler_params=PARAMS,
        cost_estimate=cost,
    )(passed, *first)


def clip_of(token, base, span, tok_dev, clip_ref):
    frame = base + token // span * FRB + token % tok_dev // TPF
    clip = jnp.zeros_like(token)
    for f in range(clip_ref.shape[0]):
        clip = jnp.where(frame == f, clip_ref[f], clip)
    return clip


def mask_kernel(span, tok, base_ref, clip_ref, *out_refs):
    count = out_refs[0].shape[0]
    row = lax.broadcasted_iota(jnp.int32, (count, 1), 0)
    col = lax.broadcasted_iota(jnp.int32, (1, count), 1)
    row_clip = clip_of(row, base_ref[0], span, tok, clip_ref)
    for i, out_ref in enumerate(out_refs):
        allowed = row_clip == clip_of(col, base_ref[i], span, tok, clip_ref)
        out_ref[...] = jnp.where(allowed, 0.0, -1e30)


def masks(bases, span, tok, count, frame_clip):
    return pl.pallas_call(
        functools.partial(mask_kernel, span, tok),
        out_shape=[jax.ShapeDtypeStruct((count, count), jnp.float32)] * len(bases),
        in_specs=[SMEM, SMEM],
        out_specs=[VMEM] * len(bases),
        compiler_params=PARAMS,
    )(index_array(*bases), frame_clip)


def attention_kernel(head_dim, n_mask, which, joint, q_ref, *refs):
    *refs, out_ref = refs
    mask_refs, refs = refs[:n_mask], refs[n_mask:]
    count, width = q_ref.shape
    k_refs, v_refs = [], []
    for both in joint:
        ref, *refs = refs
        if both:
            k_refs.append(ref.at[0:count])
            v_refs.append(ref.at[count:2 * count])
        else:
            value_ref, *refs = refs
            k_refs.append(ref)
            v_refs.append(value_ref)
    scale = math.log2(math.e) / math.sqrt(head_dim)
    per_step = max(1, 1024 // count)
    for h in range(width // head_dim):
        cols = slice(h * head_dim, (h + 1) * head_dim)
        queries = q_ref[:, cols]
        top = total = acc = None
        for first in range(0, len(k_refs), per_step):
            here = range(first, min(first + per_step, len(k_refs)))
            scores = []
            for i in here:
                s = lax.dot_general(
                    queries, k_refs[i][:, cols], (((1,), (1,)), ((), ())),
                    preferred_element_type=jnp.float32,
                )
                scores.append(s * scale + mask_refs[which[i]][...])
            new_top = functools.reduce(
                jnp.maximum, [jnp.max(s, axis=1, keepdims=True) for s in scores]
            )
            if top is not None:
                new_top = jnp.maximum(top, new_top)
                factor = jnp.exp2(top - new_top)
                total, acc = total * factor, acc * factor
            top = new_top
            for i, s in zip(here, scores):
                p = jnp.exp2(s - top)
                part = jnp.sum(p, axis=1, keepdims=True)
                dot = jnp.dot(
                    p.astype(jnp.bfloat16), v_refs[i][:, cols], preferred_element_type=jnp.float32
                )
                total = part if total is None else total + part
                acc = dot if acc is None else acc + dot
        out_ref[:, cols] = (acc / total).astype(out_ref.dtype)


def attention(q, kvs, mask_of, which, head_dim):
    joint = [not isinstance(kv, tuple) for kv in kvs]
    arrays = [x for kv, both in zip(kvs, joint) for x in ((kv,) if both else kv)]
    return pl.pallas_call(
        functools.partial(attention_kernel, head_dim, len(mask_of), which, joint),
        out_shape=jax.ShapeDtypeStruct(q.shape, q.dtype),
        in_specs=[VMEM] * (1 + len(mask_of) + len(arrays)),
        out_specs=VMEM,
        compiler_params=PARAMS,
    )(q, *mask_of, *arrays)


def project_kernel(n_attn, sizes, at_ref, place_ref, *refs):
    attn_refs, w_refs = refs[:n_attn], refs[n_attn:-4]
    mine_ref, theirs_ref, a_ref, w_all = refs[-4:]
    width = attn_refs[0].shape[1]
    blks, tok, cols = mine_ref.shape
    blk, core = place_ref[0] // 2, place_ref[0] % 2
    for k, ref in enumerate(attn_refs):
        a_ref[:, rows_at(blk ^ k, width)] = ref[...]
    for i, (ref, rows) in enumerate(zip(w_refs, sizes)):
        at = rows_at(at_ref[i], rows)
        if ref.shape[1] == cols:
            w_all[at, :] = ref[...]
        else:
            first = ref.shape[0] - cols // LANES * rows
            for j in range(cols // LANES):
                w_all[at, j * LANES:(j + 1) * LANES] = ref[first + j * rows:first + (j + 1) * rows]
    result = jnp.dot(a_ref[...], w_all[...], preferred_element_type=jnp.float32)
    result = result.astype(mine_ref.dtype).reshape(blks, 2, tok, cols)

    @pl.when(core == 0)
    def _():
        mine_ref[...] = result[:, 0]
        theirs_ref[...] = result[:, 1]

    @pl.when(core != 0)
    def _():
        mine_ref[...] = result[:, 1]
        theirs_ref[...] = result[:, 0]


def project(attns, w_parts, sizes, at, place, tok, cols):
    count, width = attns[0].shape
    blks = len(attns)
    like = jax.ShapeDtypeStruct((blks, tok, cols), attns[0].dtype)
    return pl.pallas_call(
        functools.partial(project_kernel, blks, sizes),
        out_shape=(like, like),
        in_specs=[SMEM, SMEM] + [VMEM] * (blks + len(w_parts)),
        out_specs=(VMEM, VMEM),
        scratch_shapes=[
            pltpu.VMEM((count, blks * width), attns[0].dtype),
            pltpu.VMEM((blks * width, cols), attns[0].dtype),
        ],
        compiler_params=PARAMS,
    )(index_array(*at), place, *attns, *w_parts)


def add_kernel(place_ref, x_ref, y_ref, *out_refs):
    for k, out_ref in enumerate(out_refs):
        at = place_ref[0] // 2 ^ k
        both = x_ref[at].astype(jnp.float32) + y_ref[at].astype(jnp.float32)
        out_ref[...] = both.astype(out_ref.dtype)


def add(x, y, place):
    blks = x.shape[0]
    return pl.pallas_call(
        add_kernel,
        out_shape=[jax.ShapeDtypeStruct(x.shape[1:], x.dtype)] * blks,
        in_specs=[SMEM, VMEM, VMEM],
        out_specs=[VMEM] * blks,
        compiler_params=PARAMS,
    )(place, x, y)


def unpack_kernel(place_ref, *refs):
    *in_refs, out_ref = refs
    width = in_refs[0].shape[1]
    for k, ref in enumerate(in_refs):
        out_ref[:, rows_at(place_ref[0] // 2 ^ k, width)] = ref[...]


def unpack(parts, place):
    tok, width = parts[0].shape
    return pl.pallas_call(
        unpack_kernel,
        out_shape=jax.ShapeDtypeStruct((tok, len(parts) * width), parts[0].dtype),
        in_specs=[SMEM] + [VMEM] * len(parts),
        out_specs=VMEM,
        compiler_params=PARAMS,
    )(place, *parts)


def xor(x, axis, by):
    size = math.prod(lax.axis_size(name) for name in axis)
    return lax.ppermute(x, axis, [(i, i ^ by) for i in range(size)])


def swap_all(parts, axis):
    last_first = [xor(parts[m], axis, m) for m in range(len(parts) - 1, 0, -1)]
    return [parts[0]] + last_first[::-1]


def squares(qkv, frame_clip, w_out):
    quarter = ("x", "zl")
    y, x, zh, zl, core = (lax.axis_index(n) for n in ("y", "x", "zh", "zl", "core"))
    tok, head_dim, cols = qkv.shape[1], w_out.shape[0], w_out.shape[1] // 4
    place = index_array((x * 2 + zl) * 2 + core)
    mine, theirs = x * 2 + zl, x * 2 + 1 - zl
    row, half = zh * 2 + zl, head_dim // 2

    far = after(xor(blocks(w_out, half, y, mine, cols), ("zh",), 1), cost=AHEAD)
    w_own, w_corner, w_near = columns(
        w_out, [(head_dim, 0, mine), (half, y, theirs), (head_dim, 0, theirs)], cols
    )
    kept, given = lanes(qkv, core, head_dim)
    parts = deal(kept, xor(given, ("core",), 1), place)
    q, k, v, k_v_far = sort(swap_all(parts, quarter), place, far)
    k_far, v_far = xor(k, ("zh",), 1), xor(v, ("zh",), 1)
    near = xor(k_v_far, ("y",), 1)
    corner = xor(after(w_corner, k), ("zh", "zl"), 3)
    w_next = xor(after(w_near, k), ("zl",), 1)
    kvs = [(k, v), (k_far, v_far), near, (xor(k_far, ("y",), 1), xor(v_far, ("y",), 1))]

    bases = [y * 2 * FRB, (1 - y) * 2 * FRB]
    mask_of = masks(bases, 4 * tok, tok, 8 * tok, frame_clip)
    attn = attention(q, kvs, mask_of, [0, 0, 1, 1], head_dim)
    corner = after(corner, attn)
    corner_rest = xor(corner, ("y",), 1)
    attns = swap_all([attn] * 4, quarter)
    w_parts = [w_own, w_next, far, near, corner, corner_rest]
    sizes = [head_dim, head_dim, half, half, half, half]
    at = [row, row ^ 1] + [2 * (row ^ by) + h for by in (2, 3) for h in (y, 1 - y)]
    ours, other_core = project(attns, w_parts, sizes, at, place, tok, cols)
    parts = add(ours, xor(other_core, ("core",), 1), place)
    return unpack(swap_all(parts, quarter), place)


def layers(qkv, frame_clip, w_out):
    rows, blks = lax.axis_size("row"), lax.axis_size("blk")
    row, blk = lax.axis_index("row"), lax.axis_index("blk")
    tok, head_dim, cols = qkv.shape[1], w_out.shape[0], w_out.shape[1] // blks
    place = index_array(blk * 2 + lax.axis_index("core"))
    others = range(1, rows)

    (w_own,) = columns(w_out, [(head_dim, 0, blk)], cols)
    w_parts = [w_own] + [xor(w_own, ("row",), by) for by in others]
    packed = pack(qkv, 2 * blks, head_dim)
    own = lax.all_to_all(packed, ("blk", "core"), split_axis=0, concat_axis=0, tiled=True)
    q, kv = cut(own)
    kvs = [kv] + [xor(kv, ("row",), by) for by in others]
    mask_of = masks([0], 2 * tok, tok, 2 * blks * tok, frame_clip)
    attn = attention(q, kvs, mask_of, [0] * rows, head_dim)
    attns = swap_all([attn] * blks, ("blk",))
    at = [row ^ by for by in range(rows)]
    ours, other_core = project(attns, w_parts, [head_dim] * rows, at, place, tok, cols)
    parts = add(ours, xor(other_core, ("core",), 1), place)
    return unpack(swap_all(parts, ("blk",)), place)


def solution(mesh):
    blk, tile = mesh.shape["blk"], mesh.shape["tile"]
    if (blk, tile) == (4, 8):
        plan, names, shape = squares, ("y", "x", "zh", "zl", "core"), (2, 2, 2, 2, 2)
    else:
        plan, names, shape = layers, ("blk", "row", "core"), (blk, tile // 2, 2)
    fine = Mesh(mesh.devices.reshape(shape), names)
    tiles = names[2:] if plan is squares else names[1:]
    in_specs = (P(None, names, None), P(), P(tiles, None))
    return jax.shard_map(
        plan, mesh=fine, in_specs=in_specs, out_specs=P(names, None), check_vma=False
    )
```

time: 53 us -> 53.9 us (1.017)
  Pallas kernels: 5.21 us -> 6.8 us
    pallas_call x2 -> x4, Pallas kernels: 2.45 us -> 4.09 us  [the longest x1 1.5 us: blocks(): pl.pallas_call(functools.partial(blocks_kernel, depth), out_shape=jax.Sha...]
    ppermute x21 -> x20, starting transfers between devices: 25.4 us -> 25 us  [xor(): return lax.ppermute(x, axis, [(i, i ^ by) for i in range(size)])]
    ppermute x21 -> x20, waiting for transfers between devices: 21.9 us -> 21.5 us  [xor(): return lax.ppermute(x, axis, [(i, i ^ by) for i in range(size)])]
  transfers between devices with their start and end apart: 21 -> 20, of which waited for: 13 -> 12; matrix products, arithmetic and copies ran while one was open for 0% -> 0% of each run, Pallas kernels for 2% -> 6%
where the time goes in v12:
time: 53.9 us; the launch traced here: 53.7 us
  starting transfers between devices  25 us (46%)
  waiting for transfers between devices  21.5 us (40%)
  Pallas kernels  6.8 us (13%)
    ppermute x20, starting transfers between devices, xor(): return lax.ppermute(x, axis, [(i, i ^ by) for i in range(size)])  25 us
    ppermute x20, waiting for transfers between devices, xor(): return lax.ppermute(x, axis, [(i, i ^ by) for i in range(size)])  21.5 us
    pallas_call x1, Pallas kernels, columns(): pl.pallas_call(columns_kernel, out_shape=[jax.ShapeDtypeStruct((piece[0],...  1.72 us
    pallas_call x1, Pallas kernels, blocks(): pl.pallas_call(functools.partial(blocks_kernel, depth), out_shape=jax.Sha...  1.5 us
    pallas_call x1, Pallas kernels, project(): pl.pallas_call(functools.partial(project_kernel, blks, sizes), out_shape=...  1.25 us
  transfers between devices with their start and end apart: 20, of which 12 were waited for; matrix products, arithmetic and copies ran while one was open for 0% of the time, Pallas kernels for 6%

profile of v12, /device:TPU:0, one launch (start us, length us, event | category | flops | bytes accessed | tf_op | source)
XLA Modules:
  0.0 53.7 jit_solution(12762389937022553771)
XLA Ops:
  0.0 0.0 copy-start
  0.0 0.1 pad_add_fusion.at_ref
  0.1 1.5 %shard_map.39 = bf16[640,128]{1,0:T(8,128)(2,1)S(1)} custom-call(s32[2]{0:T(128)S(1)} %pad_add_fusion.at_ref, bf16[128,5120]{1,0:T(8,128)(2,1)} %x_ref.5), custom_call_target="tpu_custom_call" | custom-call | tf_op jit(solution)/shard_map/pallas_call | solution.py:96
  1.6 4.1 %collective-permute-start.4 = (bf16[640,128]{1,0:T(8,128)(2,1)S(1)}, bf16[640,128]{1,0:T(8,128)(2,1)S(1)}, u32[]{:S(2)}, u32[]{:S(2)}) collective-permute-start(bf16[640,128]{1,0:T(8,128)(2,1)S(1)} %shard_map.39), channel_id=1, source_target_pairs={{0,4},{4,0},{1,5},{5,1},{2,6},{6,2},{3,7},{7,3},{8,12},{12,8},{9,1... | collective-permute-start | bytes 491528 | tf_op jit(solution)/shard_map/ppermute | solution.py:387
  5.7 0.0 copy-done
  5.7 0.1 shard_map.37
  5.8 0.1 collective-permute-start
  5.8 1.3 %collective-permute-done.got_ref = bf16[4,96,128]{2,1,0:T(8,128)(2,1)S(1)} collective-permute-done((bf16[4,96,128]{2,1,0:T(8,128)(2,1)S(1)}, bf16[4,96,128]{2,1,0:T(8,128)(2,1)S(1)}, u32[]{:S(2)}, u32[]{:S(2)}) %collective-permute-start) | collective-permute-done | bytes 98336 | tf_op jit(solution)/shard_map/ppermute | solution.py:387
  7.1 1.6 %collective-permute-start.1 = (bf16[2,96,128]{2,1,0:T(8,128)(2,1)S(1)}, bf16[2,96,128]{2,1,0:T(8,128)(2,1)S(1)}, u32[]{:S(2)}, u32[]{:S(2)}) collective-permute-start(bf16[2,96,128]{2,1,0:T(8,128)(2,1)S(1)} %get-tuple-element.29), channel_id=1, source_target_pairs={{0,2},{2,0},{8,10},{10,8},{1,3},{3,1},{9,11},{11,9},{4,6},{6,4},{1... | collective-permute-start | bytes 147464 | tf_op jit(solution)/shard_map/ppermute | solution.py:387
  8.8 1.5 %collective-permute-start.2 = (bf16[2,96,128]{2,1,0:T(8,128)(2,1)S(1)}, bf16[2,96,128]{2,1,0:T(8,128)(2,1)S(1)}, u32[]{:S(2)}, u32[]{:S(2)}) collective-permute-start(bf16[2,96,128]{2,1,0:T(8,128)(2,1)S(1)} %get-tuple-element.30), channel_id=1, source_target_pairs={{0,8},{2,10},{8,0},{10,2},{1,9},{3,11},{9,1},{11,3},{4,12},{6,14},... | collective-permute-start | bytes 147464 | tf_op jit(solution)/shard_map/ppermute | solution.py:387
  10.3 0.4 collective-permute-start.3
  10.7 2.8 %collective-permute-done.4.refs_0_ = bf16[640,128]{1,0:T(8,128)(2,1)S(1)} collective-permute-done((bf16[640,128]{1,0:T(8,128)(2,1)S(1)}, bf16[640,128]{1,0:T(8,128)(2,1)S(1)}, u32[]{:S(2)}, u32[]{:S(2)}) %collective-permute-start.4) | collective-permute-done | bytes 163872 | tf_op jit(solution)/shard_map/ppermute | solution.py:387
  13.5 0.0 collective-permute-done.1.refs_1_
  13.5 0.0 collective-permute-done.2.refs_2_
  13.5 1.9 %collective-permute-done.3.refs_3_ = bf16[2,96,128]{2,1,0:T(8,128)(2,1)S(1)} collective-permute-done((bf16[2,96,128]{2,1,0:T(8,128)(2,1)S(1)}, bf16[2,96,128]{2,1,0:T(8,128)(2,1)S(1)}, u32[]{:S(2)}, u32[]{:S(2)}) %collective-permute-start.3) | collective-permute-done | bytes 49184 | tf_op jit(solution)/shard_map/ppermute | solution.py:387
  15.4 0.1 shard_map.41
  15.5 0.0 copy-start.1
  15.5 1.6 %collective-permute-start.7 = (bf16[1152,128]{1,0:T(8,128)(2,1)S(1)}, bf16[1152,128]{1,0:T(8,128)(2,1)S(1)}, u32[]{:S(2)}, u32[]{:S(2)}) collective-permute-start(bf16[1152,128]{1,0:T(8,128)(2,1)S(1)} %get-tuple-element.37), channel_id=1, source_target_pairs={{0,16},{16,0},{1,17},{17,1},{2,18},{18,2},{3,19},{19,3},{4,20},{20... | collective-permute-start | bytes 884744 | tf_op jit(solution)/shard_map/ppermute | solution.py:387
  17.1 0.2 collective-permute-start.6
  17.3 2.8 %collective-permute-start.5 = (bf16[256,128]{1,0:T(8,128)(2,1)S(1)}, bf16[256,128]{1,0:T(8,128)(2,1)S(1)}, u32[]{:S(2)}, u32[]{:S(2)}) collective-permute-start(bf16[256,128]{1,0:T(8,128)(2,1)S(1)} %get-tuple-element.35.refs_2_.refs_1_), channel_id=1, source_target_pairs={{0,4},{4,0},{1,5},{5,1},{2,6},{6,2},{3,7},{7,3},{8,12},{12,8},{9,1... | collective-permute-start | bytes 196616 | tf_op jit(solution)/shard_map/ppermute | solution.py:387
  20.0 0.1 stack.70.at_ref
  20.1 1.7 %shard_map.44 = (bf16[128,1280]{1,0:T(8,128)(2,1)S(1)}, bf16[64,1280]{1,0:T(8,128)(2,1)S(1)}, bf16[128,1280]{1,0:T(8,128)(2,1)S(1)}) custom-call(s32[6]{0:T(128)S(1)} %stack.70.at_ref, bf16[128,5120]{1,0:T(8,128)(2,1)} %x_ref.5), custom_call_target="tpu_custom_call" | custom-call | tf_op jit(solution)/shard_map/pallas_call | solution.py:72
  21.9 0.7 %collective-permute-start.13 = (bf16[128,1280]{1,0:T(8,128)(2,1)S(1)}, bf16[128,1280]{1,0:T(8,128)(2,1)S(1)}, u32[]{:S(2)}, u32[]{:S(2)}) collective-permute-start(bf16[128,1280]{1,0:T(8,128)(2,1)S(1)} %shard_map.45), channel_id=1, source_target_pairs={{0,2},{2,0},{1,3},{3,1},{4,6},{6,4},{5,7},{7,5},{8,10},{10,8},{9,1... | collective-permute-start | bytes 983048 | tf_op jit(solution)/shard_map/ppermute | solution.py:387
  22.6 2.4 %collective-permute-start.14 = (bf16[64,1280]{1,0:T(8,128)(2,1)S(1)}, bf16[64,1280]{1,0:T(8,128)(2,1)S(1)}, u32[]{:S(2)}, u32[]{:S(2)}) collective-permute-start(bf16[64,1280]{1,0:T(8,128)(2,1)S(1)} %shard_map.46), channel_id=1, source_target_pairs={{0,6},{2,4},{4,2},{6,0},{1,7},{3,5},{5,3},{7,1},{8,14},{10,12},{12... | collective-permute-start | bytes 491528 | tf_op jit(solution)/shard_map/ppermute | solution.py:387
  25.0 0.0 collective-permute-done.6.refs_5_
  25.0 0.5 collective-permute-start.9
  25.5 0.0 collective-permute-done.5.refs_4_
  25.5 1.5 %collective-permute-start.8 = (bf16[256,128]{1,0:T(8,128)(2,1)S(1)}, bf16[256,128]{1,0:T(8,128)(2,1)S(1)}, u32[]{:S(2)}, u32[]{:S(2)}) collective-permute-start(bf16[256,128]{1,0:T(8,128)(2,1)S(1)} %collective-permute-done.5.refs_4_), channel_id=1, source_target_pairs={{0,16},{16,0},{1,17},{17,1},{2,18},{18,2},{3,19},{19,3},{4,20},{20... | collective-permute-start | bytes 196616 | tf_op jit(solution)/shard_map/ppermute | solution.py:387
  27.0 0.1 pad_add_fusion.1.base_ref
  27.1 0.0 copy-done.1
  27.1 0.7 %shard_map.42 = (f32[256,256]{1,0:T(8,128)S(1)}, f32[256,256]{1,0:T(8,128)S(1)}) custom-call(s32[2]{0:T(128)S(1)} %pad_add_fusion.1.base_ref, s32[8]{0:T(128)S(1)} %copy-done.1), custom_call_target="tpu_custom_call" | custom-call | tf_op jit(solution)/shard_map/pallas_call | solution.py:233
  27.8 1.4 %collective-permute-done.9.refs_8_ = bf16[256,128]{1,0:T(8,128)(2,1)S(1)} collective-permute-done((bf16[256,128]{1,0:T(8,128)(2,1)S(1)}, bf16[256,128]{1,0:T(8,128)(2,1)S(1)}, u32[]{:S(2)}, u32[]{:S(2)}) %collective-permute-start.9) | collective-permute-done | bytes 65568 | tf_op jit(solution)/shard_map/ppermute | solution.py:387
  29.3 0.7 %collective-permute-done.8.refs_7_ = bf16[256,128]{1,0:T(8,128)(2,1)S(1)} collective-permute-done((bf16[256,128]{1,0:T(8,128)(2,1)S(1)}, bf16[256,128]{1,0:T(8,128)(2,1)S(1)}, u32[]{:S(2)}, u32[]{:S(2)}) %collective-permute-start.8) | collective-permute-done | bytes 65568 | tf_op jit(solution)/shard_map/ppermute | solution.py:387
  30.0 0.0 collective-permute-done.7.refs_6_.refs_7_
  30.0 0.6 %shard_map.43.refs_1_.refs_0_ = bf16[256,128]{1,0:T(8,128)(2,1)S(1)} custom-call(bf16[256,128]{1,0:T(8,128)(2,1)S(1)} %get-tuple-element.32.q_ref, f32[256,256]{1,0:T(8,128)S(1)} %get-tuple-element.33.refs_0_, f32[256,256]{1,0:T(8,128)S(1)} %get-tuple-element.34.refs_1_, bf16[256,128]{1,0:T(8,128)(2,1)S(1)} %get-tuple-element.35.refs_2_.refs_1_, ...), custom_call_target="tpu_custom_call" | custom-call | tf_op jit(solution)/shard_map/pallas_call | solution.py:293
  30.6 4.3 %collective-permute-done.14.refs_0_ = bf16[64,1280]{1,0:T(8,128)(2,1)S(1)} collective-permute-done((bf16[64,1280]{1,0:T(8,128)(2,1)S(1)}, bf16[64,1280]{1,0:T(8,128)(2,1)S(1)}, u32[]{:S(2)}, u32[]{:S(2)}) %collective-permute-start.14) | collective-permute-done | bytes 163872 | tf_op jit(solution)/shard_map/ppermute | solution.py:387
  34.9 0.5 collective-permute-start.15
  35.4 0.0 collective-permute-start.12
  35.4 1.4 %collective-permute-start.11 = (bf16[256,128]{1,0:T(8,128)(2,1)S(1)}, bf16[256,128]{1,0:T(8,128)(2,1)S(1)}, u32[]{:S(2)}, u32[]{:S(2)}) collective-permute-start(bf16[256,128]{1,0:T(8,128)(2,1)S(1)} %shard_map.43.refs_1_.refs_0_), channel_id=1, source_target_pairs={{0,8},{2,10},{8,0},{10,2},{1,9},{3,11},{9,1},{11,3},{4,12},{6,14},... | collective-permute-start | bytes 196616 | tf_op jit(solution)/shard_map/ppermute | solution.py:387
  36.8 2.1 %collective-permute-start.10 = (bf16[256,128]{1,0:T(8,128)(2,1)S(1)}, bf16[256,128]{1,0:T(8,128)(2,1)S(1)}, u32[]{:S(2)}, u32[]{:S(2)}) collective-permute-start(bf16[256,128]{1,0:T(8,128)(2,1)S(1)} %shard_map.43.refs_1_.refs_0_), channel_id=1, source_target_pairs={{0,2},{2,0},{8,10},{10,8},{1,3},{3,1},{9,11},{11,9},{4,6},{6,4},{1... | collective-permute-start | bytes 196616 | tf_op jit(solution)/shard_map/ppermute | solution.py:387
  38.9 0.1 stack.61.at_ref
  39.0 0.0 collective-permute-done.13.refs_5_
  39.0 1.6 %collective-permute-done.12.refs_3_ = bf16[256,128]{1,0:T(8,128)(2,1)S(1)} collective-permute-done((bf16[256,128]{1,0:T(8,128)(2,1)S(1)}, bf16[256,128]{1,0:T(8,128)(2,1)S(1)}, u32[]{:S(2)}, u32[]{:S(2)}) %collective-permute-start.12) | collective-permute-done | bytes 65568 | tf_op jit(solution)/shard_map/ppermute | solution.py:387
  40.6 0.0 collective-permute-done.11.refs_2_
  40.6 0.6 %collective-permute-done.10.refs_1_ = bf16[256,128]{1,0:T(8,128)(2,1)S(1)} collective-permute-done((bf16[256,128]{1,0:T(8,128)(2,1)S(1)}, bf16[256,128]{1,0:T(8,128)(2,1)S(1)}, u32[]{:S(2)}, u32[]{:S(2)}) %collective-permute-start.10) | collective-permute-done | bytes 65568 | tf_op jit(solution)/shard_map/ppermute | solution.py:387
  41.2 0.0 collective-permute-done.15.refs_9_
  41.2 1.3 %shard_map.48 = (bf16[4,32,1280]{2,1,0:T(8,128)(2,1)S(1)}, bf16[4,32,1280]{2,1,0:T(8,128)(2,1)S(1)}) custom-call(s32[6]{0:T(128)S(1)} %stack.61.at_ref, s32[1]{0:T(128)} %bitcast.place_ref, bf16[256,128]{1,0:T(8,128)(2,1)S(1)} %shard_map.43.refs_1_.refs_0_, bf16[256,128]{1,0:T(8,128)(2,1)S(1)} %collective-permute-done.10.refs_1_, ...), custom_call_target="tpu_custom_call" | custom-call | tf_op jit(solution)/shard_map/pallas_call | solution.py:336
  42.4 0.1 collective-permute-start.16
  42.5 1.6 %collective-permute-done.16.y_ref = bf16[4,32,1280]{2,1,0:T(8,128)(2,1)S(1)} collective-permute-done((bf16[4,32,1280]{2,1,0:T(8,128)(2,1)S(1)}, bf16[4,32,1280]{2,1,0:T(8,128)(2,1)S(1)}, u32[]{:S(2)}, u32[]{:S(2)}) %collective-permute-start.16) | collective-permute-done | bytes 327712 | tf_op jit(solution)/shard_map/ppermute | solution.py:387
  44.1 0.1 shard_map.49
  44.2 2.0 %collective-permute-start.17 = (bf16[32,1280]{1,0:T(8,128)(2,1)S(1)}, bf16[32,1280]{1,0:T(8,128)(2,1)S(1)}, u32[]{:S(2)}, u32[]{:S(2)}) collective-permute-start(bf16[32,1280]{1,0:T(8,128)(2,1)S(1)} %get-tuple-element.44), channel_id=1, source_target_pairs={{0,2},{2,0},{8,10},{10,8},{1,3},{3,1},{9,11},{11,9},{4,6},{6,4},{1... | collective-permute-start | bytes 245768 | tf_op jit(solution)/shard_map/ppermute | solution.py:387
  46.2 1.4 %collective-permute-start.18 = (bf16[32,1280]{1,0:T(8,128)(2,1)S(1)}, bf16[32,1280]{1,0:T(8,128)(2,1)S(1)}, u32[]{:S(2)}, u32[]{:S(2)}) collective-permute-start(bf16[32,1280]{1,0:T(8,128)(2,1)S(1)} %get-tuple-element.45), channel_id=1, source_target_pairs={{0,8},{2,10},{8,0},{10,2},{1,9},{3,11},{9,1},{11,3},{4,12},{6,14},... | collective-permute-start | bytes 245768 | tf_op jit(solution)/shard_map/ppermute | solution.py:387
  47.6 0.2 collective-permute-start.19
  47.8 1.2 %collective-permute-done.17.refs_1_ = bf16[32,1280]{1,0:T(8,128)(2,1)S(1)} collective-permute-done((bf16[32,1280]{1,0:T(8,128)(2,1)S(1)}, bf16[32,1280]{1,0:T(8,128)(2,1)S(1)}, u32[]{:S(2)}, u32[]{:S(2)}) %collective-permute-start.17) | collective-permute-done | bytes 81952 | tf_op jit(solution)/shard_map/ppermute | solution.py:387
  49.0 1.9 %collective-permute-done.18.refs_2_ = bf16[32,1280]{1,0:T(8,128)(2,1)S(1)} collective-permute-done((bf16[32,1280]{1,0:T(8,128)(2,1)S(1)}, bf16[32,1280]{1,0:T(8,128)(2,1)S(1)}, u32[]{:S(2)}, u32[]{:S(2)}) %collective-permute-start.18) | collective-permute-done | bytes 81952 | tf_op jit(solution)/shard_map/ppermute | solution.py:387
  50.9 2.1 %collective-permute-done.19.refs_3_ = bf16[32,1280]{1,0:T(8,128)(2,1)S(1)} collective-permute-done((bf16[32,1280]{1,0:T(8,128)(2,1)S(1)}, bf16[32,1280]{1,0:T(8,128)(2,1)S(1)}, u32[]{:S(2)}, u32[]{:S(2)}) %collective-permute-start.19) | collective-permute-done | bytes 81952 | tf_op jit(solution)/shard_map/ppermute | solution.py:387
  53.0 0.8 %shard_map.50 = bf16[32,5120]{1,0:T(8,128)(2,1)} custom-call(s32[1]{0:T(128)} %bitcast.place_ref, bf16[32,1280]{1,0:T(8,128)(2,1)S(1)} %get-tuple-element.43.refs_0_, bf16[32,1280]{1,0:T(8,128)(2,1)S(1)} %collective-permute-done.17.refs_1_, bf16[32,1280]{1,0:T(8,128)(2,1)S(1)} %collective-permute-done.18.refs_2_, ...), custom_call_target="tpu_custom_call" | custom-call | tf_op jit(solution)/shard_map/pallas_call | solution.py:376
  (5 shorter events, 0.0 us)
Async XLA Ops:
  0.0 5.7 %copy-start = (bf16[3,32,1024]{2,1,0:T(8,128)(2,1)S(1)}, bf16[3,32,1024]{2,1,0:T(8,128)(2,1)}, u32[]{:S(2)}) copy-start(bf16[3,32,1024]{2,1,0:T(8,128)(2,1)} %x_ref.3) | copy-start | bytes 589828
  1.6 11.9 %collective-permute-start.4 = (bf16[640,128]{1,0:T(8,128)(2,1)S(1)}, bf16[640,128]{1,0:T(8,128)(2,1)S(1)}, u32[]{:S(2)}, u32[]{:S(2)}) collective-permute-start(bf16[640,128]{1,0:T(8,128)(2,1)S(1)} %shard_map.39), channel_id=1, source_target_pairs={{0,4},{4,0},{1,5},{5,1},{2,6},{6,2},{3,7},{7,3},{8,12},{12,8},{9,1... | collective-permute-start | bytes 491528 | tf_op jit(solution)/shard_map/ppermute | solution.py:387
  5.8 1.4 %collective-permute-start = (bf16[4,96,128]{2,1,0:T(8,128)(2,1)S(1)}, bf16[4,96,128]{2,1,0:T(8,128)(2,1)S(1)}, u32[]{:S(2)}, u32[]{:S(2)}) collective-permute-start(bf16[4,96,128]{2,1,0:T(8,128)(2,1)S(1)} %get-tuple-element.27), channel_id=1, source_target_pairs={{0,1},{1,0},{2,3},{3,2},{4,5},{5,4},{6,7},{7,6},{8,9},{9,8},{10,11... | collective-permute-start | bytes 294920 | tf_op jit(solution)/shard_map/ppermute | solution.py:387
  7.1 6.4 %collective-permute-start.1 = (bf16[2,96,128]{2,1,0:T(8,128)(2,1)S(1)}, bf16[2,96,128]{2,1,0:T(8,128)(2,1)S(1)}, u32[]{:S(2)}, u32[]{:S(2)}) collective-permute-start(bf16[2,96,128]{2,1,0:T(8,128)(2,1)S(1)} %get-tuple-element.29), channel_id=1, source_target_pairs={{0,2},{2,0},{8,10},{10,8},{1,3},{3,1},{9,11},{11,9},{4,6},{6,4},{1... | collective-permute-start | bytes 147464 | tf_op jit(solution)/shard_map/ppermute | solution.py:387
  8.8 4.7 %collective-permute-start.2 = (bf16[2,96,128]{2,1,0:T(8,128)(2,1)S(1)}, bf16[2,96,128]{2,1,0:T(8,128)(2,1)S(1)}, u32[]{:S(2)}, u32[]{:S(2)}) collective-permute-start(bf16[2,96,128]{2,1,0:T(8,128)(2,1)S(1)} %get-tuple-element.30), channel_id=1, source_target_pairs={{0,8},{2,10},{8,0},{10,2},{1,9},{3,11},{9,1},{11,3},{4,12},{6,14},... | collective-permute-start | bytes 147464 | tf_op jit(solution)/shard_map/ppermute | solution.py:387
  10.3 5.2 %collective-permute-start.3 = (bf16[2,96,128]{2,1,0:T(8,128)(2,1)S(1)}, bf16[2,96,128]{2,1,0:T(8,128)(2,1)S(1)}, u32[]{:S(2)}, u32[]{:S(2)}) collective-permute-start(bf16[2,96,128]{2,1,0:T(8,128)(2,1)S(1)} %get-tuple-element.31), channel_id=1, source_target_pairs={{0,10},{2,8},{8,2},{10,0},{1,11},{3,9},{9,3},{11,1},{4,14},{6,12},... | collective-permute-start | bytes 147464 | tf_op jit(solution)/shard_map/ppermute | solution.py:387
  15.5 11.6 %copy-start.1 = (s32[8]{0:T(128)S(1)}, s32[8]{0:T(128)}, u32[]{:S(2)}) copy-start(s32[8]{0:T(128)} %clip_ref.1) | copy-start | bytes 100
  15.5 14.4 %collective-permute-start.7 = (bf16[1152,128]{1,0:T(8,128)(2,1)S(1)}, bf16[1152,128]{1,0:T(8,128)(2,1)S(1)}, u32[]{:S(2)}, u32[]{:S(2)}) collective-permute-start(bf16[1152,128]{1,0:T(8,128)(2,1)S(1)} %get-tuple-element.37), channel_id=1, source_target_pairs={{0,16},{16,0},{1,17},{17,1},{2,18},{18,2},{3,19},{19,3},{4,20},{20... | collective-permute-start | bytes 884744 | tf_op jit(solution)/shard_map/ppermute | solution.py:387
  17.1 7.9 %collective-permute-start.6 = (bf16[256,128]{1,0:T(8,128)(2,1)S(1)}, bf16[256,128]{1,0:T(8,128)(2,1)S(1)}, u32[]{:S(2)}, u32[]{:S(2)}) collective-permute-start(bf16[256,128]{1,0:T(8,128)(2,1)S(1)} %get-tuple-element.36.refs_3_), channel_id=1, source_target_pairs={{0,4},{4,0},{1,5},{5,1},{2,6},{6,2},{3,7},{7,3},{8,12},{12,8},{9,1... | collective-permute-start | bytes 196616 | tf_op jit(solution)/shard_map/ppermute | solution.py:387
  17.3 8.2 %collective-permute-start.5 = (bf16[256,128]{1,0:T(8,128)(2,1)S(1)}, bf16[256,128]{1,0:T(8,128)(2,1)S(1)}, u32[]{:S(2)}, u32[]{:S(2)}) collective-permute-start(bf16[256,128]{1,0:T(8,128)(2,1)S(1)} %get-tuple-element.35.refs_2_.refs_1_), channel_id=1, source_target_pairs={{0,4},{4,0},{1,5},{5,1},{2,6},{6,2},{3,7},{7,3},{8,12},{12,8},{9,1... | collective-permute-start | bytes 196616 | tf_op jit(solution)/shard_map/ppermute | solution.py:387
  21.9 17.1 %collective-permute-start.13 = (bf16[128,1280]{1,0:T(8,128)(2,1)S(1)}, bf16[128,1280]{1,0:T(8,128)(2,1)S(1)}, u32[]{:S(2)}, u32[]{:S(2)}) collective-permute-start(bf16[128,1280]{1,0:T(8,128)(2,1)S(1)} %shard_map.45), channel_id=1, source_target_pairs={{0,2},{2,0},{1,3},{3,1},{4,6},{6,4},{5,7},{7,5},{8,10},{10,8},{9,1... | collective-permute-start | bytes 983048 | tf_op jit(solution)/shard_map/ppermute | solution.py:387
  22.6 12.3 %collective-permute-start.14 = (bf16[64,1280]{1,0:T(8,128)(2,1)S(1)}, bf16[64,1280]{1,0:T(8,128)(2,1)S(1)}, u32[]{:S(2)}, u32[]{:S(2)}) collective-permute-start(bf16[64,1280]{1,0:T(8,128)(2,1)S(1)} %shard_map.46), channel_id=1, source_target_pairs={{0,6},{2,4},{4,2},{6,0},{1,7},{3,5},{5,3},{7,1},{8,14},{10,12},{12... | collective-permute-start | bytes 491528 | tf_op jit(solution)/shard_map/ppermute | solution.py:387
  25.0 4.3 %collective-permute-start.9 = (bf16[256,128]{1,0:T(8,128)(2,1)S(1)}, bf16[256,128]{1,0:T(8,128)(2,1)S(1)}, u32[]{:S(2)}, u32[]{:S(2)}) collective-permute-start(bf16[256,128]{1,0:T(8,128)(2,1)S(1)} %collective-permute-done.6.refs_5_), channel_id=1, source_target_pairs={{0,16},{16,0},{1,17},{17,1},{2,18},{18,2},{3,19},{19,3},{4,20},{20... | collective-permute-start | bytes 196616 | tf_op jit(solution)/shard_map/ppermute | solution.py:387
  25.5 4.5 %collective-permute-start.8 = (bf16[256,128]{1,0:T(8,128)(2,1)S(1)}, bf16[256,128]{1,0:T(8,128)(2,1)S(1)}, u32[]{:S(2)}, u32[]{:S(2)}) collective-permute-start(bf16[256,128]{1,0:T(8,128)(2,1)S(1)} %collective-permute-done.5.refs_4_), channel_id=1, source_target_pairs={{0,16},{16,0},{1,17},{17,1},{2,18},{18,2},{3,19},{19,3},{4,20},{20... | collective-permute-start | bytes 196616 | tf_op jit(solution)/shard_map/ppermute | solution.py:387
  34.9 6.3 %collective-permute-start.15 = (bf16[64,1280]{1,0:T(8,128)(2,1)S(1)}, bf16[64,1280]{1,0:T(8,128)(2,1)S(1)}, u32[]{:S(2)}, u32[]{:S(2)}) collective-permute-start(bf16[64,1280]{1,0:T(8,128)(2,1)S(1)} %shard_map.47.refs_8_), channel_id=1, source_target_pairs={{0,16},{16,0},{1,17},{17,1},{2,18},{18,2},{3,19},{19,3},{4,20},{20... | collective-permute-start | bytes 491528 | tf_op jit(solution)/shard_map/ppermute | solution.py:387
  35.4 5.2 %collective-permute-start.12 = (bf16[256,128]{1,0:T(8,128)(2,1)S(1)}, bf16[256,128]{1,0:T(8,128)(2,1)S(1)}, u32[]{:S(2)}, u32[]{:S(2)}) collective-permute-start(bf16[256,128]{1,0:T(8,128)(2,1)S(1)} %shard_map.43.refs_1_.refs_0_), channel_id=1, source_target_pairs={{0,10},{2,8},{8,2},{10,0},{1,11},{3,9},{9,3},{11,1},{4,14},{6,12},... | collective-permute-start | bytes 196616 | tf_op jit(solution)/shard_map/ppermute | solution.py:387
  35.4 5.2 %collective-permute-start.11 = (bf16[256,128]{1,0:T(8,128)(2,1)S(1)}, bf16[256,128]{1,0:T(8,128)(2,1)S(1)}, u32[]{:S(2)}, u32[]{:S(2)}) collective-permute-start(bf16[256,128]{1,0:T(8,128)(2,1)S(1)} %shard_map.43.refs_1_.refs_0_), channel_id=1, source_target_pairs={{0,8},{2,10},{8,0},{10,2},{1,9},{3,11},{9,1},{11,3},{4,12},{6,14},... | collective-permute-start | bytes 196616 | tf_op jit(solution)/shard_map/ppermute | solution.py:387
  36.8 4.4 %collective-permute-start.10 = (bf16[256,128]{1,0:T(8,128)(2,1)S(1)}, bf16[256,128]{1,0:T(8,128)(2,1)S(1)}, u32[]{:S(2)}, u32[]{:S(2)}) collective-permute-start(bf16[256,128]{1,0:T(8,128)(2,1)S(1)} %shard_map.43.refs_1_.refs_0_), channel_id=1, source_target_pairs={{0,2},{2,0},{8,10},{10,8},{1,3},{3,1},{9,11},{11,9},{4,6},{6,4},{1... | collective-permute-start | bytes 196616 | tf_op jit(solution)/shard_map/ppermute | solution.py:387
  42.4 1.7 %collective-permute-start.16 = (bf16[4,32,1280]{2,1,0:T(8,128)(2,1)S(1)}, bf16[4,32,1280]{2,1,0:T(8,128)(2,1)S(1)}, u32[]{:S(2)}, u32[]{:S(2)}) collective-permute-start(bf16[4,32,1280]{2,1,0:T(8,128)(2,1)S(1)} %get-tuple-element.42), channel_id=1, source_target_pairs={{0,1},{1,0},{2,3},{3,2},{4,5},{5,4},{6,7},{7,6},{8,9},{9,8},{10,11... | collective-permute-start | bytes 983048 | tf_op jit(solution)/shard_map/ppermute | solution.py:387
  44.2 4.8 %collective-permute-start.17 = (bf16[32,1280]{1,0:T(8,128)(2,1)S(1)}, bf16[32,1280]{1,0:T(8,128)(2,1)S(1)}, u32[]{:S(2)}, u32[]{:S(2)}) collective-permute-start(bf16[32,1280]{1,0:T(8,128)(2,1)S(1)} %get-tuple-element.44), channel_id=1, source_target_pairs={{0,2},{2,0},{8,10},{10,8},{1,3},{3,1},{9,11},{11,9},{4,6},{6,4},{1... | collective-permute-start | bytes 245768 | tf_op jit(solution)/shard_map/ppermute | solution.py:387
  46.2 4.6 %collective-permute-start.18 = (bf16[32,1280]{1,0:T(8,128)(2,1)S(1)}, bf16[32,1280]{1,0:T(8,128)(2,1)S(1)}, u32[]{:S(2)}, u32[]{:S(2)}) collective-permute-start(bf16[32,1280]{1,0:T(8,128)(2,1)S(1)} %get-tuple-element.45), channel_id=1, source_target_pairs={{0,8},{2,10},{8,0},{10,2},{1,9},{3,11},{9,1},{11,3},{4,12},{6,14},... | collective-permute-start | bytes 245768 | tf_op jit(solution)/shard_map/ppermute | solution.py:387
  47.6 5.3 %collective-permute-start.19 = (bf16[32,1280]{1,0:T(8,128)(2,1)S(1)}, bf16[32,1280]{1,0:T(8,128)(2,1)S(1)}, u32[]{:S(2)}, u32[]{:S(2)}) collective-permute-start(bf16[32,1280]{1,0:T(8,128)(2,1)S(1)} %get-tuple-element.46), channel_id=1, source_target_pairs={{0,10},{2,8},{8,2},{10,0},{1,11},{3,9},{9,3},{11,1},{4,14},{6,12},... | collective-permute-start | bytes 245768 | tf_op jit(solution)/shard_map/ppermute | solution.py:387

commit v13 on v12

--- a/solution.py
+++ b/solution.py
@@ -17,6 +17,7 @@
 ANY = pl.BlockSpec(memory_space=pl.ANY)
 PARAMS = pltpu.CompilerParams(vmem_limit_bytes=48 * 1024 * 1024)
 AHEAD = pl.CostEstimate(flops=20_000_000_000, bytes_accessed=1_000_000, transcendentals=0)
+SOON = pl.CostEstimate(flops=6_000_000_000, bytes_accessed=1_000_000, transcendentals=0)
 
 
 def rows_at(index, size):
@@ -51,13 +52,6 @@
     )(x)
 
 
-def copy_all(copies):
-    for copy in copies:
-        copy.start()
-    for copy in copies:
-        copy.wait()
-
-
 def columns_kernel(at_ref, x_ref, *refs):
     *out_refs, sems = refs
     copies = []
@@ -65,7 +59,10 @@
         depth, cols = ref.shape
         piece = x_ref.at[rows_at(at_ref[2 * i], depth), rows_at(at_ref[2 * i + 1], cols)]
         copies.append(pltpu.make_async_copy(piece, ref, sems.at[i]))
-    copy_all(copies)
+    for copy in copies:
+        copy.start()
+    for copy in copies:
+        copy.wait()
 
 
 def columns(x, pieces, cols):
@@ -82,25 +79,28 @@
     )
 
 
-def blocks_kernel(depth, at_ref, x_ref, out_ref, sems):
-    blocks = out_ref.shape[0] // depth
-    copies = []
-    for j in range(blocks):
-        piece = x_ref.at[rows_at(at_ref[0], depth), rows_at(at_ref[1] * blocks + j, LANES)]
-        copies.append(pltpu.make_async_copy(piece, out_ref.at[j * depth:(j + 1) * depth], sems.at[j]))
-    copy_all(copies)
-
-
-def blocks(x, depth, row_at, col_at, cols):
+def pieces_kernel(at_ref, x_ref, far_ref, corner_ref, near_ref):
+    half, cols = corner_ref.shape
+    rows = rows_at(at_ref[0], half)
     count = cols // LANES
-    return pl.pallas_call(
-        functools.partial(blocks_kernel, depth),
-        out_shape=jax.ShapeDtypeStruct((count * depth, LANES), x.dtype),
-        in_specs=[SMEM, pl.BlockSpec(memory_space=pltpu.HBM)],
-        out_specs=VMEM,
-        scratch_shapes=[pltpu.SemaphoreType.DMA((count,))],
-        compiler_params=PARAMS,
-    )(index_array(row_at, col_at), pltpu.with_memory_space_constraint(x, pltpu.HBM))
+    for j in range(count):
+        far_ref[j * half:(j + 1) * half, :] = x_ref[rows, rows_at(at_ref[1] * count + j, LANES)]
+    corner_ref[...] = x_ref[rows, rows_at(at_ref[2], cols)]
+    near_ref[...] = x_ref[:, rows_at(at_ref[2], cols)]
+
+
+def pieces(x, half, first_at, second_at, cols):
+    return pl.pallas_call(
+        pieces_kernel,
+        out_shape=(
+            jax.ShapeDtypeStruct((cols // LANES * (x.shape[0] // 2), LANES), x.dtype),
+            jax.ShapeDtypeStruct((x.shape[0] // 2, cols), x.dtype),
+            jax.ShapeDtypeStruct((x.shape[0], cols), x.dtype),
+        ),
+        in_specs=[SMEM, VMEM],
+        out_specs=(VMEM, VMEM, VMEM),
+        compiler_params=PARAMS,
+    )(index_array(half, first_at, second_at), x)
 
 
 def lane_kernel(head_dim, core_ref, x_ref, mine_ref, theirs_ref):
@@ -142,34 +142,45 @@
     )(place, mine, got)
 
 
-def sort_kernel(n, place_ref, *refs):
-    in_refs, (more_ref, q_ref, k_ref, v_ref, all_ref) = refs[:n], refs[n:]
-    count = q_ref.shape[0]
-    tok = count // (2 * n)
+def sort_kernel(place_ref, *refs):
+    *in_refs, q_ref, k_ref, v_ref = refs
+    tok = q_ref.shape[0] // (2 * len(in_refs))
     for i, ref in enumerate(in_refs):
         for core in range(2):
-            at = (place_ref[0] // 2 ^ i) * 2 + core
-            keys, values = ref[core, tok:2 * tok, :], ref[core, 2 * tok:, :]
-            q_ref[rows_at(at, tok), :] = ref[core, 0:tok, :]
-            k_ref[rows_at(at, tok), :] = keys
-            v_ref[rows_at(at, tok), :] = values
-            all_ref[rows_at(at, tok), :] = keys
-            all_ref[rows_at(at + 2 * n, tok), :] = values
-    all_ref[2 * count:, :] = more_ref[...]
-
-
-def sort(parts, place, more):
-    _, depth, width = parts[0].shape
-    n = len(parts)
-    count = 2 * n * (depth // 3)
-    sizes = (count, count, count, 2 * count + more.shape[0])
-    return pl.pallas_call(
-        functools.partial(sort_kernel, n),
-        out_shape=[jax.ShapeDtypeStruct((size, width), more.dtype) for size in sizes],
-        in_specs=[SMEM] + [VMEM] * (n + 1),
-        out_specs=[VMEM] * 4,
-        compiler_params=PARAMS,
-    )(place, *parts, more)
+            at = rows_at((place_ref[0] // 2 ^ i) * 2 + core, tok)
+            for j, out_ref in enumerate((q_ref, k_ref, v_ref)):
+                out_ref[at, :] = ref[core, j * tok:(j + 1) * tok, :]
+
+
+def sort(parts, place):
+    both, depth, width = parts[0].shape
+    count = both * len(parts) * (depth // 3)
+    return pl.pallas_call(
+        sort_kernel,
+        out_shape=[jax.ShapeDtypeStruct((count, width), parts[0].dtype)] * 3,
+        in_specs=[SMEM] + [VMEM] * len(parts),
+        out_specs=[VMEM] * 3,
+        compiler_params=PARAMS,
+    )(place, *parts)
+
+
+def join_kernel(*refs):
+    *in_refs, out_ref = refs
+    first = 0
+    for ref in in_refs:
+        out_ref[first:first + ref.shape[0], :] = ref[...]
+        first += ref.shape[0]
+
+
+def join(*arrays):
+    depth = sum(x.shape[0] for x in arrays)
+    return pl.pallas_call(
+        join_kernel,
+        out_shape=jax.ShapeDtypeStruct((depth, arrays[0].shape[1]), arrays[0].dtype),
+        in_specs=[VMEM] * len(arrays),
+        out_specs=VMEM,
+        compiler_params=PARAMS,
+    )(*arrays)
 
 
 def cut_kernel(x_ref, q_ref, kv_ref):
@@ -309,8 +320,8 @@
         a_ref[:, rows_at(blk ^ k, width)] = ref[...]
     for i, (ref, rows) in enumerate(zip(w_refs, sizes)):
         at = rows_at(at_ref[i], rows)
-        if ref.shape[1] == cols:
-            w_all[at, :] = ref[...]
+        if ref.shape[1] >= cols:
+            w_all[at, :] = ref[:, rows_at(blk, cols)] if ref.shape[1] > cols else ref[...]
         else:
             first = ref.shape[0] - cols // LANES * rows
             for j in range(cols // LANES):
@@ -400,26 +411,25 @@
     mine, theirs = x * 2 + zl, x * 2 + 1 - zl
     row, half = zh * 2 + zl, head_dim // 2
 
-    far = after(xor(blocks(w_out, half, y, mine, cols), ("zh",), 1), cost=AHEAD)
-    w_own, w_corner, w_near = columns(
-        w_out, [(head_dim, 0, mine), (half, y, theirs), (head_dim, 0, theirs)], cols
-    )
+    w_far, w_corner, w_near = pieces(w_out, y, mine, theirs, cols)
+    far = after(xor(w_far, ("zh",), 1), cost=AHEAD)
     kept, given = lanes(qkv, core, head_dim)
-    parts = deal(kept, xor(given, ("core",), 1), place)
-    q, k, v, k_v_far = sort(swap_all(parts, quarter), place, far)
+    shared = swap_all(deal(kept, xor(given, ("core",), 1), place), quarter)
+    w_next = after(xor(after(w_near, shared[1]), ("zl",), 1), cost=AHEAD)
+    q, k, v = sort(shared, place)
     k_far, v_far = xor(k, ("zh",), 1), xor(v, ("zh",), 1)
-    near = xor(k_v_far, ("y",), 1)
+    near = xor(join(k, v, far), ("y",), 1)
     corner = xor(after(w_corner, k), ("zh", "zl"), 3)
-    w_next = xor(after(w_near, k), ("zl",), 1)
     kvs = [(k, v), (k_far, v_far), near, (xor(k_far, ("y",), 1), xor(v_far, ("y",), 1))]
 
     bases = [y * 2 * FRB, (1 - y) * 2 * FRB]
     mask_of = masks(bases, 4 * tok, tok, 8 * tok, frame_clip)
-    attn = attention(q, kvs, mask_of, [0, 0, 1, 1], head_dim)
-    corner = after(corner, attn)
+    attn = attention(after(q, w_next), kvs, mask_of, [0, 0, 1, 1], head_dim)
+    corner = after(corner, attn, cost=SOON)
     corner_rest = xor(corner, ("y",), 1)
     attns = swap_all([attn] * 4, quarter)
-    w_parts = [w_own, w_next, far, near, corner, corner_rest]
+    w_next = after(w_next, attn, cost=AHEAD)
+    w_parts = [w_out, w_next, far, near, corner, corner_rest]
     sizes = [head_dim, head_dim, half, half, half, half]
     at = [row, row ^ 1] + [2 * (row ^ by) + h for by in (2, 3) for h in (y, 1 - y)]
     ours, other_core = project(attns, w_parts, sizes, at, place, tok, cols)
@@ -435,7 +445,7 @@
     others = range(1, rows)
 
     (w_own,) = columns(w_out, [(head_dim, 0, blk)], cols)
-    w_parts = [w_own] + [xor(w_own, ("row",), by) for by in others]
+    w_parts = [w_out] + [xor(w_own, ("row",), by) for by in others]
     packed = pack(qkv, 2 * blks, head_dim)
     own = lax.all_to_all(packed, ("blk", "core"), split_axis=0, concat_axis=0, tiled=True)
     q, kv = cut(own)

time: 53.9 us -> 55.3 us (1.026)
  Pallas kernels: 6.8 us -> 4.16 us
  local copies, waits for them, and re-layouts: 0.18 us -> 2.35 us
  starting transfers between devices: 25 us -> 26.5 us
    pallas_call x3, Pallas kernels: 3.31 us -> 0.67 us  [the longest x1 0.62 us: pieces(): pl.pallas_call(pieces_kernel, out_shape=(jax.ShapeDtypeStruct((cols // LA...]
    unnamed x4 -> x8, local copies, waits for them, and re-layouts: 0.01 us -> 2.26 us
    ppermute x20, starting transfers between devices: 25 us -> 26.5 us  [xor(): return lax.ppermute(x, axis, [(i, i ^ by) for i in range(size)])]
  transfers between devices with their start and end apart: 20 -> 20, of which waited for: 12 -> 10; matrix products, arithmetic and copies ran while one was open for 0% -> 0% of each run, Pallas kernels for 6% -> 4%
where the time goes in v13:
time: 55.3 us; the launch traced here: 55.2 us
  starting transfers between devices  26.5 us (48%)
  waiting for transfers between devices  21.9 us (40%)
  Pallas kernels  4.16 us (8%)
  local copies, waits for them, and re-layouts  2.35 us (4%)
    ppermute x20, starting transfers between devices, xor(): return lax.ppermute(x, axis, [(i, i ^ by) for i in range(size)])  26.5 us
    ppermute x20, waiting for transfers between devices, xor(): return lax.ppermute(x, axis, [(i, i ^ by) for i in range(size)])  21.9 us
    unnamed x8, local copies, waits for them, and re-layouts  2.26 us
    pallas_call x1, Pallas kernels, project(): pl.pallas_call(functools.partial(project_kernel, blks, sizes), out_shape=...  1.26 us
  transfers between devices with their start and end apart: 20, of which 10 were waited for; matrix products, arithmetic and copies ran while one was open for 0% of the time, Pallas kernels for 4%

profile of v13, /device:TPU:0, one launch (start us, length us, event | category | flops | bytes accessed | tf_op | source)
XLA Modules:
  0.0 55.2 jit_solution(8366681163032908486)
XLA Ops:
  0.0 0.0 copy-start.3
  0.0 0.0 copy-start.2
  0.0 0.9 %copy-done.2 = bf16[3,32,1024]{2,1,0:T(8,128)(2,1)S(1)} copy-done((bf16[3,32,1024]{2,1,0:T(8,128)(2,1)S(1)}, bf16[3,32,1024]{2,1,0:T(8,128)(2,1)}, u32[]{:S(2)}) %copy-start.2) | copy-done | bytes 196632
  0.9 0.1 shard_map.37
  1.0 0.5 collective-permute-start
  1.5 0.1 pad_add_fusion.at_ref
  1.6 0.0 copy-start
  1.6 1.3 %copy-done = bf16[128,5120]{1,0:T(8,128)(2,1)S(1)} copy-done((bf16[128,5120]{1,0:T(8,128)(2,1)S(1)}, bf16[128,5120]{1,0:T(8,128)(2,1)}, u32[]{:S(2)}) %copy-start) | copy-done | bytes 1310744
  2.9 0.6 %shard_map.40 = (bf16[640,128]{1,0:T(8,128)(2,1)S(1)}, bf16[64,1280]{1,0:T(8,128)(2,1)S(1)}, bf16[128,1280]{1,0:T(8,128)(2,1)S(1)}) custom-call(s32[3]{0:T(128)S(1)} %pad_add_fusion.at_ref, bf16[128,5120]{1,0:T(8,128)(2,1)S(1)} %copy-done), custom_call_target="tpu_custom_call" | custom-call | tf_op jit(solution)/shard_map/pallas_call | solution.py:93
  3.5 3.7 %collective-permute-start.7 = (bf16[640,128]{1,0:T(8,128)(2,1)S(1)}, bf16[640,128]{1,0:T(8,128)(2,1)S(1)}, u32[]{:S(2)}, u32[]{:S(2)}) collective-permute-start(bf16[640,128]{1,0:T(8,128)(2,1)S(1)} %get-tuple-element.37), channel_id=1, source_target_pairs={{0,4},{4,0},{1,5},{5,1},{2,6},{6,2},{3,7},{7,3},{8,12},{12,8},{9,1... | collective-permute-start | bytes 491528 | tf_op jit(solution)/shard_map/ppermute | solution.py:398
  7.2 0.0 collective-permute-done.got_ref
  7.2 1.6 %collective-permute-start.1 = (bf16[2,96,128]{2,1,0:T(8,128)(2,1)S(1)}, bf16[2,96,128]{2,1,0:T(8,128)(2,1)S(1)}, u32[]{:S(2)}, u32[]{:S(2)}) collective-permute-start(bf16[2,96,128]{2,1,0:T(8,128)(2,1)S(1)} %get-tuple-element.28), channel_id=1, source_target_pairs={{0,2},{2,0},{8,10},{10,8},{1,3},{3,1},{9,11},{11,9},{4,6},{6,4},{1... | collective-permute-start | bytes 147464 | tf_op jit(solution)/shard_map/ppermute | solution.py:398
  8.9 1.5 %collective-permute-start.2 = (bf16[2,96,128]{2,1,0:T(8,128)(2,1)S(1)}, bf16[2,96,128]{2,1,0:T(8,128)(2,1)S(1)}, u32[]{:S(2)}, u32[]{:S(2)}) collective-permute-start(bf16[2,96,128]{2,1,0:T(8,128)(2,1)S(1)} %get-tuple-element.29), channel_id=1, source_target_pairs={{0,8},{2,10},{8,0},{10,2},{1,9},{3,11},{9,1},{11,3},{4,12},{6,14},... | collective-permute-start | bytes 147464 | tf_op jit(solution)/shard_map/ppermute | solution.py:398
  10.4 0.4 collective-permute-start.3
  10.8 0.1 pad_add_fusion.1.base_ref
  10.9 0.0 copy-done.3
  10.9 0.7 %shard_map.44 = (f32[256,256]{1,0:T(8,128)S(1)}, f32[256,256]{1,0:T(8,128)S(1)}) custom-call(s32[2]{0:T(128)S(1)} %pad_add_fusion.1.base_ref, s32[8]{0:T(128)S(1)} %copy-done.3), custom_call_target="tpu_custom_call" | custom-call | tf_op jit(solution)/shard_map/pallas_call | solution.py:244
  11.6 0.1 stack.55.at_ref
  11.7 1.2 %collective-permute-done.1.refs_1_ = bf16[2,96,128]{2,1,0:T(8,128)(2,1)S(1)} collective-permute-done((bf16[2,96,128]{2,1,0:T(8,128)(2,1)S(1)}, bf16[2,96,128]{2,1,0:T(8,128)(2,1)S(1)}, u32[]{:S(2)}, u32[]{:S(2)}) %collective-permute-start.1) | collective-permute-done | bytes 49184 | tf_op jit(solution)/shard_map/ppermute | solution.py:398
  12.8 2.5 %collective-permute-start.4 = (bf16[128,1280]{1,0:T(8,128)(2,1)S(1)}, bf16[128,1280]{1,0:T(8,128)(2,1)S(1)}, u32[]{:S(2)}, u32[]{:S(2)}) collective-permute-start(bf16[128,1280]{1,0:T(8,128)(2,1)S(1)} %shard_map.41), channel_id=1, source_target_pairs={{0,2},{2,0},{1,3},{3,1},{4,6},{6,4},{5,7},{7,5},{8,10},{10,8},{9,1... | collective-permute-start | bytes 983048 | tf_op jit(solution)/shard_map/ppermute | solution.py:398
  15.3 0.0 collective-permute-done.2.refs_2_
  15.3 2.2 %collective-permute-done.3.refs_3_ = bf16[2,96,128]{2,1,0:T(8,128)(2,1)S(1)} collective-permute-done((bf16[2,96,128]{2,1,0:T(8,128)(2,1)S(1)}, bf16[2,96,128]{2,1,0:T(8,128)(2,1)S(1)}, u32[]{:S(2)}, u32[]{:S(2)}) %collective-permute-start.3) | collective-permute-done | bytes 49184 | tf_op jit(solution)/shard_map/ppermute | solution.py:398
  17.5 0.1 collective-permute-start.6
  17.6 2.9 %collective-permute-start.5 = (bf16[256,128]{1,0:T(8,128)(2,1)S(1)}, bf16[256,128]{1,0:T(8,128)(2,1)S(1)}, u32[]{:S(2)}, u32[]{:S(2)}) collective-permute-start(bf16[256,128]{1,0:T(8,128)(2,1)S(1)} %get-tuple-element.35.refs_0_.refs_2_.refs_1_), channel_id=1, source_target_pairs={{0,4},{4,0},{1,5},{5,1},{2,6},{6,2},{3,7},{7,3},{8,12},{12,8},{9,1... | collective-permute-start | bytes 196616 | tf_op jit(solution)/shard_map/ppermute | solution.py:398
  20.5 0.0 collective-permute-start.14
  20.5 0.0 collective-permute-done.7.refs_0_
  20.6 1.6 %collective-permute-start.8 = (bf16[1152,128]{1,0:T(8,128)(2,1)S(1)}, bf16[1152,128]{1,0:T(8,128)(2,1)S(1)}, u32[]{:S(2)}, u32[]{:S(2)}) collective-permute-start(bf16[1152,128]{1,0:T(8,128)(2,1)S(1)} %shard_map.46), channel_id=1, source_target_pairs={{0,16},{16,0},{1,17},{17,1},{2,18},{18,2},{3,19},{19,3},{4,20},{20... | collective-permute-start | bytes 884744 | tf_op jit(solution)/shard_map/ppermute | solution.py:398
  22.2 2.8 %collective-permute-done.6.refs_5_ = bf16[256,128]{1,0:T(8,128)(2,1)S(1)} collective-permute-done((bf16[256,128]{1,0:T(8,128)(2,1)S(1)}, bf16[256,128]{1,0:T(8,128)(2,1)S(1)}, u32[]{:S(2)}, u32[]{:S(2)}) %collective-permute-start.6) | collective-permute-done | bytes 65568 | tf_op jit(solution)/shard_map/ppermute | solution.py:398
  24.9 1.5 %collective-permute-start.10 = (bf16[256,128]{1,0:T(8,128)(2,1)S(1)}, bf16[256,128]{1,0:T(8,128)(2,1)S(1)}, u32[]{:S(2)}, u32[]{:S(2)}) collective-permute-start(bf16[256,128]{1,0:T(8,128)(2,1)S(1)} %collective-permute-done.6.refs_5_), channel_id=1, source_target_pairs={{0,16},{16,0},{1,17},{17,1},{2,18},{18,2},{3,19},{19,3},{4,20},{20... | collective-permute-start | bytes 196616 | tf_op jit(solution)/shard_map/ppermute | solution.py:398
  26.4 4.1 %collective-permute-done.5.refs_4_ = bf16[256,128]{1,0:T(8,128)(2,1)S(1)} collective-permute-done((bf16[256,128]{1,0:T(8,128)(2,1)S(1)}, bf16[256,128]{1,0:T(8,128)(2,1)S(1)}, u32[]{:S(2)}, u32[]{:S(2)}) %collective-permute-start.5) | collective-permute-done | bytes 65568 | tf_op jit(solution)/shard_map/ppermute | solution.py:398
  30.5 1.5 %collective-permute-start.9 = (bf16[256,128]{1,0:T(8,128)(2,1)S(1)}, bf16[256,128]{1,0:T(8,128)(2,1)S(1)}, u32[]{:S(2)}, u32[]{:S(2)}) collective-permute-start(bf16[256,128]{1,0:T(8,128)(2,1)S(1)} %collective-permute-done.5.refs_4_), channel_id=1, source_target_pairs={{0,16},{16,0},{1,17},{17,1},{2,18},{18,2},{3,19},{19,3},{4,20},{20... | collective-permute-start | bytes 196616 | tf_op jit(solution)/shard_map/ppermute | solution.py:398
  32.1 0.0 collective-permute-done.4.refs_0_
  32.1 0.0 collective-permute-done.10.refs_8_
  32.1 3.4 %collective-permute-done.9.refs_7_ = bf16[256,128]{1,0:T(8,128)(2,1)S(1)} collective-permute-done((bf16[256,128]{1,0:T(8,128)(2,1)S(1)}, bf16[256,128]{1,0:T(8,128)(2,1)S(1)}, u32[]{:S(2)}, u32[]{:S(2)}) %collective-permute-start.9) | collective-permute-done | bytes 65568 | tf_op jit(solution)/shard_map/ppermute | solution.py:398
  35.5 0.0 collective-permute-done.8.refs_6_.refs_7_
  35.5 0.6 %shard_map.47.refs_1_.refs_0_ = bf16[256,128]{1,0:T(8,128)(2,1)S(1)} custom-call(bf16[256,128]{1,0:T(8,128)(2,1)S(1)} %shard_map.43.q_ref, f32[256,256]{1,0:T(8,128)S(1)} %get-tuple-element.33.refs_0_, f32[256,256]{1,0:T(8,128)S(1)} %get-tuple-element.34.refs_1_, bf16[256,128]{1,0:T(8,128)(2,1)S(1)} %get-tuple-element.35.refs_0_.refs_2_.refs_1_, ...), custom_call_target="tpu_custom_call" | custom-call | tf_op jit(solution)/shard_map/pallas_call | solution.py:304
  36.1 0.1 collective-permute-start.11
  36.2 0.1 collective-permute-start.12
  36.3 3.4 %collective-permute-start.13 = (bf16[256,128]{1,0:T(8,128)(2,1)S(1)}, bf16[256,128]{1,0:T(8,128)(2,1)S(1)}, u32[]{:S(2)}, u32[]{:S(2)}) collective-permute-start(bf16[256,128]{1,0:T(8,128)(2,1)S(1)} %shard_map.47.refs_1_.refs_0_), channel_id=1, source_target_pairs={{0,10},{2,8},{8,2},{10,0},{1,11},{3,9},{9,3},{11,1},{4,14},{6,12},... | collective-permute-start | bytes 196616 | tf_op jit(solution)/shard_map/ppermute | solution.py:398
  39.7 0.0 collective-permute-done.14.refs_0_
  39.7 0.0 copy-start.1
  39.7 1.5 %collective-permute-start.15 = (bf16[64,1280]{1,0:T(8,128)(2,1)S(1)}, bf16[64,1280]{1,0:T(8,128)(2,1)S(1)}, u32[]{:S(2)}, u32[]{:S(2)}) collective-permute-start(bf16[64,1280]{1,0:T(8,128)(2,1)S(1)} %shard_map.50.refs_8_), channel_id=1, source_target_pairs={{0,16},{16,0},{1,17},{17,1},{2,18},{18,2},{3,19},{19,3},{4,20},{20... | collective-permute-start | bytes 491528 | tf_op jit(solution)/shard_map/ppermute | solution.py:398
  41.2 0.0 collective-permute-done.11.refs_1_
  41.2 0.0 collective-permute-done.12.refs_2_
  41.2 0.7 %collective-permute-done.13.refs_3_ = bf16[256,128]{1,0:T(8,128)(2,1)S(1)} collective-permute-done((bf16[256,128]{1,0:T(8,128)(2,1)S(1)}, bf16[256,128]{1,0:T(8,128)(2,1)S(1)}, u32[]{:S(2)}, u32[]{:S(2)}) %collective-permute-start.13) | collective-permute-done | bytes 65568 | tf_op jit(solution)/shard_map/ppermute | solution.py:398
  41.9 3.1 %collective-permute-done.15.refs_9_ = bf16[64,1280]{1,0:T(8,128)(2,1)S(1)} collective-permute-done((bf16[64,1280]{1,0:T(8,128)(2,1)S(1)}, bf16[64,1280]{1,0:T(8,128)(2,1)S(1)}, u32[]{:S(2)}, u32[]{:S(2)}) %collective-permute-start.15) | collective-permute-done | bytes 163872 | tf_op jit(solution)/shard_map/ppermute | solution.py:398
  45.0 0.0 copy-done.1
  45.0 1.3 %shard_map.51 = (bf16[4,32,1280]{2,1,0:T(8,128)(2,1)S(1)}, bf16[4,32,1280]{2,1,0:T(8,128)(2,1)S(1)}) custom-call(s32[6]{0:T(128)S(1)} %stack.55.at_ref, s32[1]{0:T(128)} %bitcast.place_ref, bf16[256,128]{1,0:T(8,128)(2,1)S(1)} %shard_map.47.refs_1_.refs_0_, bf16[256,128]{1,0:T(8,128)(2,1)S(1)} %collective-permute-done.11.refs_1_, ...), custom_call_target="tpu_custom_call" | custom-call | tf_op jit(solution)/shard_map/pallas_call | solution.py:347
  46.3 0.1 collective-permute-start.16
  46.3 1.6 %collective-permute-done.16.y_ref = bf16[4,32,1280]{2,1,0:T(8,128)(2,1)S(1)} collective-permute-done((bf16[4,32,1280]{2,1,0:T(8,128)(2,1)S(1)}, bf16[4,32,1280]{2,1,0:T(8,128)(2,1)S(1)}, u32[]{:S(2)}, u32[]{:S(2)}) %collective-permute-start.16) | collective-permute-done | bytes 327712 | tf_op jit(solution)/shard_map/ppermute | solution.py:398
  48.0 0.1 shard_map.52
  48.0 0.1 collective-permute-start.17
  48.2 0.6 %collective-permute-start.18 = (bf16[32,1280]{1,0:T(8,128)(2,1)S(1)}, bf16[32,1280]{1,0:T(8,128)(2,1)S(1)}, u32[]{:S(2)}, u32[]{:S(2)}) collective-permute-start(bf16[32,1280]{1,0:T(8,128)(2,1)S(1)} %get-tuple-element.43), channel_id=1, source_target_pairs={{0,8},{2,10},{8,0},{10,2},{1,9},{3,11},{9,1},{11,3},{4,12},{6,14},... | collective-permute-start | bytes 245768 | tf_op jit(solution)/shard_map/ppermute | solution.py:398
  48.7 2.9 %collective-permute-start.19 = (bf16[32,1280]{1,0:T(8,128)(2,1)S(1)}, bf16[32,1280]{1,0:T(8,128)(2,1)S(1)}, u32[]{:S(2)}, u32[]{:S(2)}) collective-permute-start(bf16[32,1280]{1,0:T(8,128)(2,1)S(1)} %get-tuple-element.44), channel_id=1, source_target_pairs={{0,10},{2,8},{8,2},{10,0},{1,11},{3,9},{9,3},{11,1},{4,14},{6,12},... | collective-permute-start | bytes 245768 | tf_op jit(solution)/shard_map/ppermute | solution.py:398
  51.6 1.6 %collective-permute-done.17.refs_1_ = bf16[32,1280]{1,0:T(8,128)(2,1)S(1)} collective-permute-done((bf16[32,1280]{1,0:T(8,128)(2,1)S(1)}, bf16[32,1280]{1,0:T(8,128)(2,1)S(1)}, u32[]{:S(2)}, u32[]{:S(2)}) %collective-permute-start.17) | collective-permute-done | bytes 81952 | tf_op jit(solution)/shard_map/ppermute | solution.py:398
  53.2 1.3 %collective-permute-done.18.refs_2_ = bf16[32,1280]{1,0:T(8,128)(2,1)S(1)} collective-permute-done((bf16[32,1280]{1,0:T(8,128)(2,1)S(1)}, bf16[32,1280]{1,0:T(8,128)(2,1)S(1)}, u32[]{:S(2)}, u32[]{:S(2)}) %collective-permute-start.18) | collective-permute-done | bytes 81952 | tf_op jit(solution)/shard_map/ppermute | solution.py:398
  54.4 0.0 collective-permute-done.19.refs_3_
  54.4 0.8 %shard_map.53 = bf16[32,5120]{1,0:T(8,128)(2,1)} custom-call(s32[1]{0:T(128)} %bitcast.place_ref, bf16[32,1280]{1,0:T(8,128)(2,1)S(1)} %get-tuple-element.41.refs_0_, bf16[32,1280]{1,0:T(8,128)(2,1)S(1)} %collective-permute-done.17.refs_1_, bf16[32,1280]{1,0:T(8,128)(2,1)S(1)} %collective-permute-done.18.refs_2_, ...), custom_call_target="tpu_custom_call" | custom-call | tf_op jit(solution)/shard_map/pallas_call | solution.py:387
  (10 shorter events, 0.1 us)
Async XLA Ops:
  0.0 10.9 %copy-start.3 = (s32[8]{0:T(128)S(1)}, s32[8]{0:T(128)}, u32[]{:S(2)}) copy-start(s32[8]{0:T(128)} %clip_ref.1) | copy-start | bytes 100
  0.0 0.9 %copy-start.2 = (bf16[3,32,1024]{2,1,0:T(8,128)(2,1)S(1)}, bf16[3,32,1024]{2,1,0:T(8,128)(2,1)}, u32[]{:S(2)}) copy-start(bf16[3,32,1024]{2,1,0:T(8,128)(2,1)} %x_ref.2) | copy-start | bytes 589828
  1.0 6.2 %collective-permute-start = (bf16[4,96,128]{2,1,0:T(8,128)(2,1)S(1)}, bf16[4,96,128]{2,1,0:T(8,128)(2,1)S(1)}, u32[]{:S(2)}, u32[]{:S(2)}) collective-permute-start(bf16[4,96,128]{2,1,0:T(8,128)(2,1)S(1)} %get-tuple-element.26), channel_id=1, source_target_pairs={{0,1},{1,0},{2,3},{3,2},{4,5},{5,4},{6,7},{7,6},{8,9},{9,8},{10,11... | collective-permute-start | bytes 294920 | tf_op jit(solution)/shard_map/ppermute | solution.py:398
  1.6 1.3 %copy-start = (bf16[128,5120]{1,0:T(8,128)(2,1)S(1)}, bf16[128,5120]{1,0:T(8,128)(2,1)}, u32[]{:S(2)}) copy-start(bf16[128,5120]{1,0:T(8,128)(2,1)} %refs_4_.1) | copy-start | bytes 3932164
  3.5 17.0 %collective-permute-start.7 = (bf16[640,128]{1,0:T(8,128)(2,1)S(1)}, bf16[640,128]{1,0:T(8,128)(2,1)S(1)}, u32[]{:S(2)}, u32[]{:S(2)}) collective-permute-start(bf16[640,128]{1,0:T(8,128)(2,1)S(1)} %get-tuple-element.37), channel_id=1, source_target_pairs={{0,4},{4,0},{1,5},{5,1},{2,6},{6,2},{3,7},{7,3},{8,12},{12,8},{9,1... | collective-permute-start | bytes 491528 | tf_op jit(solution)/shard_map/ppermute | solution.py:398
  7.2 5.6 %collective-permute-start.1 = (bf16[2,96,128]{2,1,0:T(8,128)(2,1)S(1)}, bf16[2,96,128]{2,1,0:T(8,128)(2,1)S(1)}, u32[]{:S(2)}, u32[]{:S(2)}) collective-permute-start(bf16[2,96,128]{2,1,0:T(8,128)(2,1)S(1)} %get-tuple-element.28), channel_id=1, source_target_pairs={{0,2},{2,0},{8,10},{10,8},{1,3},{3,1},{9,11},{11,9},{4,6},{6,4},{1... | collective-permute-start | bytes 147464 | tf_op jit(solution)/shard_map/ppermute | solution.py:398
  8.9 6.4 %collective-permute-start.2 = (bf16[2,96,128]{2,1,0:T(8,128)(2,1)S(1)}, bf16[2,96,128]{2,1,0:T(8,128)(2,1)S(1)}, u32[]{:S(2)}, u32[]{:S(2)}) collective-permute-start(bf16[2,96,128]{2,1,0:T(8,128)(2,1)S(1)} %get-tuple-element.29), channel_id=1, source_target_pairs={{0,8},{2,10},{8,0},{10,2},{1,9},{3,11},{9,1},{11,3},{4,12},{6,14},... | collective-permute-start | bytes 147464 | tf_op jit(solution)/shard_map/ppermute | solution.py:398
  10.4 7.1 %collective-permute-start.3 = (bf16[2,96,128]{2,1,0:T(8,128)(2,1)S(1)}, bf16[2,96,128]{2,1,0:T(8,128)(2,1)S(1)}, u32[]{:S(2)}, u32[]{:S(2)}) collective-permute-start(bf16[2,96,128]{2,1,0:T(8,128)(2,1)S(1)} %get-tuple-element.30), channel_id=1, source_target_pairs={{0,10},{2,8},{8,2},{10,0},{1,11},{3,9},{9,3},{11,1},{4,14},{6,12},... | collective-permute-start | bytes 147464 | tf_op jit(solution)/shard_map/ppermute | solution.py:398
  12.8 19.2 %collective-permute-start.4 = (bf16[128,1280]{1,0:T(8,128)(2,1)S(1)}, bf16[128,1280]{1,0:T(8,128)(2,1)S(1)}, u32[]{:S(2)}, u32[]{:S(2)}) collective-permute-start(bf16[128,1280]{1,0:T(8,128)(2,1)S(1)} %shard_map.41), channel_id=1, source_target_pairs={{0,2},{2,0},{1,3},{3,1},{4,6},{6,4},{5,7},{7,5},{8,10},{10,8},{9,1... | collective-permute-start | bytes 983048 | tf_op jit(solution)/shard_map/ppermute | solution.py:398
  17.5 7.4 %collective-permute-start.6 = (bf16[256,128]{1,0:T(8,128)(2,1)S(1)}, bf16[256,128]{1,0:T(8,128)(2,1)S(1)}, u32[]{:S(2)}, u32[]{:S(2)}) collective-permute-start(bf16[256,128]{1,0:T(8,128)(2,1)S(1)} %get-tuple-element.36.refs_1_.refs_3_), channel_id=1, source_target_pairs={{0,4},{4,0},{1,5},{5,1},{2,6},{6,2},{3,7},{7,3},{8,12},{12,8},{9,1... | collective-permute-start | bytes 196616 | tf_op jit(solution)/shard_map/ppermute | solution.py:398
  17.6 12.9 %collective-permute-start.5 = (bf16[256,128]{1,0:T(8,128)(2,1)S(1)}, bf16[256,128]{1,0:T(8,128)(2,1)S(1)}, u32[]{:S(2)}, u32[]{:S(2)}) collective-permute-start(bf16[256,128]{1,0:T(8,128)(2,1)S(1)} %get-tuple-element.35.refs_0_.refs_2_.refs_1_), channel_id=1, source_target_pairs={{0,4},{4,0},{1,5},{5,1},{2,6},{6,2},{3,7},{7,3},{8,12},{12,8},{9,1... | collective-permute-start | bytes 196616 | tf_op jit(solution)/shard_map/ppermute | solution.py:398
  20.5 19.1 %collective-permute-start.14 = (bf16[64,1280]{1,0:T(8,128)(2,1)S(1)}, bf16[64,1280]{1,0:T(8,128)(2,1)S(1)}, u32[]{:S(2)}, u32[]{:S(2)}) collective-permute-start(bf16[64,1280]{1,0:T(8,128)(2,1)S(1)} %shard_map.49), channel_id=1, source_target_pairs={{0,6},{2,4},{4,2},{6,0},{1,7},{3,5},{5,3},{7,1},{8,14},{10,12},{12... | collective-permute-start | bytes 491528 | tf_op jit(solution)/shard_map/ppermute | solution.py:398
  20.6 14.9 %collective-permute-start.8 = (bf16[1152,128]{1,0:T(8,128)(2,1)S(1)}, bf16[1152,128]{1,0:T(8,128)(2,1)S(1)}, u32[]{:S(2)}, u32[]{:S(2)}) collective-permute-start(bf16[1152,128]{1,0:T(8,128)(2,1)S(1)} %shard_map.46), channel_id=1, source_target_pairs={{0,16},{16,0},{1,17},{17,1},{2,18},{18,2},{3,19},{19,3},{4,20},{20... | collective-permute-start | bytes 884744 | tf_op jit(solution)/shard_map/ppermute | solution.py:398
  24.9 7.1 %collective-permute-start.10 = (bf16[256,128]{1,0:T(8,128)(2,1)S(1)}, bf16[256,128]{1,0:T(8,128)(2,1)S(1)}, u32[]{:S(2)}, u32[]{:S(2)}) collective-permute-start(bf16[256,128]{1,0:T(8,128)(2,1)S(1)} %collective-permute-done.6.refs_5_), channel_id=1, source_target_pairs={{0,16},{16,0},{1,17},{17,1},{2,18},{18,2},{3,19},{19,3},{4,20},{20... | collective-permute-start | bytes 196616 | tf_op jit(solution)/shard_map/ppermute | solution.py:398
  30.5 4.9 %collective-permute-start.9 = (bf16[256,128]{1,0:T(8,128)(2,1)S(1)}, bf16[256,128]{1,0:T(8,128)(2,1)S(1)}, u32[]{:S(2)}, u32[]{:S(2)}) collective-permute-start(bf16[256,128]{1,0:T(8,128)(2,1)S(1)} %collective-permute-done.5.refs_4_), channel_id=1, source_target_pairs={{0,16},{16,0},{1,17},{17,1},{2,18},{18,2},{3,19},{19,3},{4,20},{20... | collective-permute-start | bytes 196616 | tf_op jit(solution)/shard_map/ppermute | solution.py:398
  36.1 5.1 %collective-permute-start.11 = (bf16[256,128]{1,0:T(8,128)(2,1)S(1)}, bf16[256,128]{1,0:T(8,128)(2,1)S(1)}, u32[]{:S(2)}, u32[]{:S(2)}) collective-permute-start(bf16[256,128]{1,0:T(8,128)(2,1)S(1)} %shard_map.47.refs_1_.refs_0_), channel_id=1, source_target_pairs={{0,2},{2,0},{8,10},{10,8},{1,3},{3,1},{9,11},{11,9},{4,6},{6,4},{1... | collective-permute-start | bytes 196616 | tf_op jit(solution)/shard_map/ppermute | solution.py:398
  36.2 5.0 %collective-permute-start.12 = (bf16[256,128]{1,0:T(8,128)(2,1)S(1)}, bf16[256,128]{1,0:T(8,128)(2,1)S(1)}, u32[]{:S(2)}, u32[]{:S(2)}) collective-permute-start(bf16[256,128]{1,0:T(8,128)(2,1)S(1)} %shard_map.47.refs_1_.refs_0_), channel_id=1, source_target_pairs={{0,8},{2,10},{8,0},{10,2},{1,9},{3,11},{9,1},{11,3},{4,12},{6,14},... | collective-permute-start | bytes 196616 | tf_op jit(solution)/shard_map/ppermute | solution.py:398
  36.3 5.6 %collective-permute-start.13 = (bf16[256,128]{1,0:T(8,128)(2,1)S(1)}, bf16[256,128]{1,0:T(8,128)(2,1)S(1)}, u32[]{:S(2)}, u32[]{:S(2)}) collective-permute-start(bf16[256,128]{1,0:T(8,128)(2,1)S(1)} %shard_map.47.refs_1_.refs_0_), channel_id=1, source_target_pairs={{0,10},{2,8},{8,2},{10,0},{1,11},{3,9},{9,3},{11,1},{4,14},{6,12},... | collective-permute-start | bytes 196616 | tf_op jit(solution)/shard_map/ppermute | solution.py:398
  39.7 5.3 %copy-start.1 = (bf16[128,5120]{1,0:T(8,128)(2,1)S(1)}, bf16[128,5120]{1,0:T(8,128)(2,1)}, u32[]{:S(2)}) copy-start(bf16[128,5120]{1,0:T(8,128)(2,1)} %refs_4_.1) | copy-start | bytes 3932164
  39.7 5.3 %collective-permute-start.15 = (bf16[64,1280]{1,0:T(8,128)(2,1)S(1)}, bf16[64,1280]{1,0:T(8,128)(2,1)S(1)}, u32[]{:S(2)}, u32[]{:S(2)}) collective-permute-start(bf16[64,1280]{1,0:T(8,128)(2,1)S(1)} %shard_map.50.refs_8_), channel_id=1, source_target_pairs={{0,16},{16,0},{1,17},{17,1},{2,18},{18,2},{3,19},{19,3},{4,20},{20... | collective-permute-start | bytes 491528 | tf_op jit(solution)/shard_map/ppermute | solution.py:398
  46.3 1.7 %collective-permute-start.16 = (bf16[4,32,1280]{2,1,0:T(8,128)(2,1)S(1)}, bf16[4,32,1280]{2,1,0:T(8,128)(2,1)S(1)}, u32[]{:S(2)}, u32[]{:S(2)}) collective-permute-start(bf16[4,32,1280]{2,1,0:T(8,128)(2,1)S(1)} %get-tuple-element.40), channel_id=1, source_target_pairs={{0,1},{1,0},{2,3},{3,2},{4,5},{5,4},{6,7},{7,6},{8,9},{9,8},{10,11... | collective-permute-start | bytes 983048 | tf_op jit(solution)/shard_map/ppermute | solution.py:398
  48.0 5.1 %collective-permute-start.17 = (bf16[32,1280]{1,0:T(8,128)(2,1)S(1)}, bf16[32,1280]{1,0:T(8,128)(2,1)S(1)}, u32[]{:S(2)}, u32[]{:S(2)}) collective-permute-start(bf16[32,1280]{1,0:T(8,128)(2,1)S(1)} %get-tuple-element.42), channel_id=1, source_target_pairs={{0,2},{2,0},{8,10},{10,8},{1,3},{3,1},{9,11},{11,9},{4,6},{6,4},{1... | collective-permute-start | bytes 245768 | tf_op jit(solution)/shard_map/ppermute | solution.py:398
  48.2 6.2 %collective-permute-start.18 = (bf16[32,1280]{1,0:T(8,128)(2,1)S(1)}, bf16[32,1280]{1,0:T(8,128)(2,1)S(1)}, u32[]{:S(2)}, u32[]{:S(2)}) collective-permute-start(bf16[32,1280]{1,0:T(8,128)(2,1)S(1)} %get-tuple-element.43), channel_id=1, source_target_pairs={{0,8},{2,10},{8,0},{10,2},{1,9},{3,11},{9,1},{11,3},{4,12},{6,14},... | collective-permute-start | bytes 245768 | tf_op jit(solution)/shard_map/ppermute | solution.py:398
  48.7 5.7 %collective-permute-start.19 = (bf16[32,1280]{1,0:T(8,128)(2,1)S(1)}, bf16[32,1280]{1,0:T(8,128)(2,1)S(1)}, u32[]{:S(2)}, u32[]{:S(2)}) collective-permute-start(bf16[32,1280]{1,0:T(8,128)(2,1)S(1)} %get-tuple-element.44), channel_id=1, source_target_pairs={{0,10},{2,8},{8,2},{10,0},{1,11},{3,9},{9,3},{11,1},{4,14},{6,12},... | collective-permute-start | bytes 245768 | tf_op jit(solution)/shard_map/ppermute | solution.py:398

commit v14 on v13

--- a/solution.py
+++ b/solution.py
@@ -79,26 +79,25 @@
     )
 
 
-def pieces_kernel(at_ref, x_ref, far_ref, corner_ref, near_ref):
+def pieces_kernel(at_ref, x_ref, far_ref, corner_ref, *near_refs):
     half, cols = corner_ref.shape
     rows = rows_at(at_ref[0], half)
     count = cols // LANES
     for j in range(count):
         far_ref[j * half:(j + 1) * half, :] = x_ref[rows, rows_at(at_ref[1] * count + j, LANES)]
     corner_ref[...] = x_ref[rows, rows_at(at_ref[2], cols)]
-    near_ref[...] = x_ref[:, rows_at(at_ref[2], cols)]
+    for i, near_ref in enumerate(near_refs):
+        near_ref[...] = x_ref[i * half:(i + 1) * half, rows_at(at_ref[2], cols)]
 
 
 def pieces(x, half, first_at, second_at, cols):
+    depth = x.shape[0] // 2
+    like = jax.ShapeDtypeStruct((depth, cols), x.dtype)
     return pl.pallas_call(
         pieces_kernel,
-        out_shape=(
-            jax.ShapeDtypeStruct((cols // LANES * (x.shape[0] // 2), LANES), x.dtype),
-            jax.ShapeDtypeStruct((x.shape[0] // 2, cols), x.dtype),
-            jax.ShapeDtypeStruct((x.shape[0], cols), x.dtype),
-        ),
+        out_shape=[jax.ShapeDtypeStruct((cols // LANES * depth, LANES), x.dtype)] + [like] * 3,
         in_specs=[SMEM, VMEM],
-        out_specs=(VMEM, VMEM, VMEM),
+        out_specs=[VMEM] * 4,
         compiler_params=PARAMS,
     )(index_array(half, first_at, second_at), x)
 
@@ -411,27 +410,29 @@
     mine, theirs = x * 2 + zl, x * 2 + 1 - zl
     row, half = zh * 2 + zl, head_dim // 2
 
-    w_far, w_corner, w_near = pieces(w_out, y, mine, theirs, cols)
+    w_far, w_corner, w_first, w_second = pieces(w_out, y, mine, theirs, cols)
     far = after(xor(w_far, ("zh",), 1), cost=AHEAD)
     kept, given = lanes(qkv, core, head_dim)
     shared = swap_all(deal(kept, xor(given, ("core",), 1), place), quarter)
-    w_next = after(xor(after(w_near, shared[1]), ("zl",), 1), cost=AHEAD)
+    next_first = after(xor(after(w_first, shared[1]), ("zl",), 1), cost=AHEAD)
     q, k, v = sort(shared, place)
     k_far, v_far = xor(k, ("zh",), 1), xor(v, ("zh",), 1)
     near = xor(join(k, v, far), ("y",), 1)
     corner = xor(after(w_corner, k), ("zh", "zl"), 3)
+    next_second = xor(after(w_second, k_far, v_far), ("zl",), 1)
     kvs = [(k, v), (k_far, v_far), near, (xor(k_far, ("y",), 1), xor(v_far, ("y",), 1))]
 
     bases = [y * 2 * FRB, (1 - y) * 2 * FRB]
     mask_of = masks(bases, 4 * tok, tok, 8 * tok, frame_clip)
-    attn = attention(after(q, w_next), kvs, mask_of, [0, 0, 1, 1], head_dim)
+    attn = attention(after(q, next_first), kvs, mask_of, [0, 0, 1, 1], head_dim)
     corner = after(corner, attn, cost=SOON)
     corner_rest = xor(corner, ("y",), 1)
     attns = swap_all([attn] * 4, quarter)
-    w_next = after(w_next, attn, cost=AHEAD)
-    w_parts = [w_out, w_next, far, near, corner, corner_rest]
-    sizes = [head_dim, head_dim, half, half, half, half]
-    at = [row, row ^ 1] + [2 * (row ^ by) + h for by in (2, 3) for h in (y, 1 - y)]
+    next_second = after(next_second, attn, cost=AHEAD)
+    w_parts = [w_out, next_first, next_second, far, near, corner, corner_rest]
+    sizes = [head_dim] + [half] * 6
+    at = [row] + [2 * (row ^ 1) + h for h in (0, 1)]
+    at += [2 * (row ^ by) + h for by in (2, 3) for h in (y, 1 - y)]
     ours, other_core = project(attns, w_parts, sizes, at, place, tok, cols)
     parts = add(ours, xor(other_core, ("core",), 1), place)
     return unpack(swap_all(parts, quarter), place)

time: 55.3 us -> 57.4 us (1.038)
  waiting for transfers between devices: 21.9 us -> 25.7 us
  starting transfers between devices: 26.5 us -> 24.8 us
    ppermute x20 -> x21, waiting for transfers between devices: 21.9 us -> 25.7 us  [xor(): return lax.ppermute(x, axis, [(i, i ^ by) for i in range(size)])]
    ppermute x20 -> x21, starting transfers between devices: 26.5 us -> 24.8 us  [xor(): return lax.ppermute(x, axis, [(i, i ^ by) for i in range(size)])]
  transfers between devices with their start and end apart: 20 -> 21, of which waited for: 10 -> 13; matrix products, arithmetic and copies ran while one was open for 0% -> 0% of each run, Pallas kernels for 4% -> 4%
where the time goes in v14:
time: 57.4 us; the launch traced here: 57.2 us
  waiting for transfers between devices  25.7 us (45%)
  starting transfers between devices  24.8 us (43%)
  Pallas kernels  4.16 us (7%)
  local copies, waits for them, and re-layouts  2.36 us (4%)
    ppermute x21, waiting for transfers between devices, xor(): return lax.ppermute(x, axis, [(i, i ^ by) for i in range(size)])  25.7 us
    ppermute x21, starting transfers between devices, xor(): return lax.ppermute(x, axis, [(i, i ^ by) for i in range(size)])  24.8 us
    unnamed x8, local copies, waits for them, and re-layouts  2.26 us
    pallas_call x1, Pallas kernels, project(): pl.pallas_call(functools.partial(project_kernel, blks, sizes), out_shape=...  1.26 us
  transfers between devices with their start and end apart: 21, of which 13 were waited for; matrix products, arithmetic and copies ran while one was open for 0% of the time, Pallas kernels for 4%

profile of v14, /device:TPU:0, one launch (start us, length us, event | category | flops | bytes accessed | tf_op | source)
XLA Modules:
  0.0 57.2 jit_solution(13763486993194901771)
XLA Ops:
  0.0 0.0 copy-start.3
  0.0 0.0 copy-start.2
  0.0 0.9 %copy-done.2 = bf16[3,32,1024]{2,1,0:T(8,128)(2,1)S(1)} copy-done((bf16[3,32,1024]{2,1,0:T(8,128)(2,1)S(1)}, bf16[3,32,1024]{2,1,0:T(8,128)(2,1)}, u32[]{:S(2)}) %copy-start.2) | copy-done | bytes 196632
  0.9 0.1 shard_map.37
  1.0 0.5 collective-permute-start
  1.5 0.1 pad_add_fusion.at_ref
  1.6 0.0 copy-start
  1.6 1.3 %copy-done = bf16[128,5120]{1,0:T(8,128)(2,1)S(1)} copy-done((bf16[128,5120]{1,0:T(8,128)(2,1)S(1)}, bf16[128,5120]{1,0:T(8,128)(2,1)}, u32[]{:S(2)}) %copy-start) | copy-done | bytes 1310744
  2.9 0.6 %shard_map.40 = (bf16[640,128]{1,0:T(8,128)(2,1)S(1)}, bf16[64,1280]{1,0:T(8,128)(2,1)S(1)}, bf16[64,1280]{1,0:T(8,128)(2,1)S(1)}, bf16[64,1280]{1,0:T(8,128)(2,1)S(1)}) custom-call(s32[3]{0:T(128)S(1)} %pad_add_fusion.at_ref, bf16[128,5120]{1,0:T(8,128)(2,1)S(1)} %copy-done), custom_call_target="tpu_custom_call" | custom-call | tf_op jit(solution)/shard_map/pallas_call | solution.py:96
  3.5 3.7 %collective-permute-start.7 = (bf16[640,128]{1,0:T(8,128)(2,1)S(1)}, bf16[640,128]{1,0:T(8,128)(2,1)S(1)}, u32[]{:S(2)}, u32[]{:S(2)}) collective-permute-start(bf16[640,128]{1,0:T(8,128)(2,1)S(1)} %get-tuple-element.38), channel_id=1, source_target_pairs={{0,4},{4,0},{1,5},{5,1},{2,6},{6,2},{3,7},{7,3},{8,12},{12,8},{9,1... | collective-permute-start | bytes 491528 | tf_op jit(solution)/shard_map/ppermute | solution.py:397
  7.2 0.0 collective-permute-done.got_ref
  7.2 1.6 %collective-permute-start.1 = (bf16[2,96,128]{2,1,0:T(8,128)(2,1)S(1)}, bf16[2,96,128]{2,1,0:T(8,128)(2,1)S(1)}, u32[]{:S(2)}, u32[]{:S(2)}) collective-permute-start(bf16[2,96,128]{2,1,0:T(8,128)(2,1)S(1)} %get-tuple-element.29), channel_id=1, source_target_pairs={{0,2},{2,0},{8,10},{10,8},{1,3},{3,1},{9,11},{11,9},{4,6},{6,4},{1... | collective-permute-start | bytes 147464 | tf_op jit(solution)/shard_map/ppermute | solution.py:397
  8.9 1.5 %collective-permute-start.2 = (bf16[2,96,128]{2,1,0:T(8,128)(2,1)S(1)}, bf16[2,96,128]{2,1,0:T(8,128)(2,1)S(1)}, u32[]{:S(2)}, u32[]{:S(2)}) collective-permute-start(bf16[2,96,128]{2,1,0:T(8,128)(2,1)S(1)} %get-tuple-element.30), channel_id=1, source_target_pairs={{0,8},{2,10},{8,0},{10,2},{1,9},{3,11},{9,1},{11,3},{4,12},{6,14},... | collective-permute-start | bytes 147464 | tf_op jit(solution)/shard_map/ppermute | solution.py:397
  10.4 0.4 collective-permute-start.3
  10.8 0.1 pad_add_fusion.1.base_ref
  10.9 0.0 copy-done.3
  10.9 0.7 %shard_map.44 = (f32[256,256]{1,0:T(8,128)S(1)}, f32[256,256]{1,0:T(8,128)S(1)}) custom-call(s32[2]{0:T(128)S(1)} %pad_add_fusion.1.base_ref, s32[8]{0:T(128)S(1)} %copy-done.3), custom_call_target="tpu_custom_call" | custom-call | tf_op jit(solution)/shard_map/pallas_call | solution.py:243
  11.6 0.1 stack.59.at_ref
  11.7 1.2 %collective-permute-done.1.refs_1_ = bf16[2,96,128]{2,1,0:T(8,128)(2,1)S(1)} collective-permute-done((bf16[2,96,128]{2,1,0:T(8,128)(2,1)S(1)}, bf16[2,96,128]{2,1,0:T(8,128)(2,1)S(1)}, u32[]{:S(2)}, u32[]{:S(2)}) %collective-permute-start.1) | collective-permute-done | bytes 49184 | tf_op jit(solution)/shard_map/ppermute | solution.py:397
  12.8 2.5 %collective-permute-start.4 = (bf16[64,1280]{1,0:T(8,128)(2,1)S(1)}, bf16[64,1280]{1,0:T(8,128)(2,1)S(1)}, u32[]{:S(2)}, u32[]{:S(2)}) collective-permute-start(bf16[64,1280]{1,0:T(8,128)(2,1)S(1)} %shard_map.41), channel_id=1, source_target_pairs={{0,2},{2,0},{1,3},{3,1},{4,6},{6,4},{5,7},{7,5},{8,10},{10,8},{9,1... | collective-permute-start | bytes 491528 | tf_op jit(solution)/shard_map/ppermute | solution.py:397
  15.3 0.0 collective-permute-done.2.refs_2_
  15.3 2.2 %collective-permute-done.3.refs_3_ = bf16[2,96,128]{2,1,0:T(8,128)(2,1)S(1)} collective-permute-done((bf16[2,96,128]{2,1,0:T(8,128)(2,1)S(1)}, bf16[2,96,128]{2,1,0:T(8,128)(2,1)S(1)}, u32[]{:S(2)}, u32[]{:S(2)}) %collective-permute-start.3) | collective-permute-done | bytes 49184 | tf_op jit(solution)/shard_map/ppermute | solution.py:397
  17.5 0.1 collective-permute-start.6
  17.6 2.9 %collective-permute-start.5 = (bf16[256,128]{1,0:T(8,128)(2,1)S(1)}, bf16[256,128]{1,0:T(8,128)(2,1)S(1)}, u32[]{:S(2)}, u32[]{:S(2)}) collective-permute-start(bf16[256,128]{1,0:T(8,128)(2,1)S(1)} %get-tuple-element.36.refs_0_.refs_2_.refs_1_), channel_id=1, source_target_pairs={{0,4},{4,0},{1,5},{5,1},{2,6},{6,2},{3,7},{7,3},{8,12},{12,8},{9,1... | collective-permute-start | bytes 196616 | tf_op jit(solution)/shard_map/ppermute | solution.py:397
  20.5 0.0 collective-permute-start.15
  20.5 0.0 collective-permute-done.7.refs_0_
  20.6 1.6 %collective-permute-start.8 = (bf16[1152,128]{1,0:T(8,128)(2,1)S(1)}, bf16[1152,128]{1,0:T(8,128)(2,1)S(1)}, u32[]{:S(2)}, u32[]{:S(2)}) collective-permute-start(bf16[1152,128]{1,0:T(8,128)(2,1)S(1)} %shard_map.46), channel_id=1, source_target_pairs={{0,16},{16,0},{1,17},{17,1},{2,18},{18,2},{3,19},{19,3},{4,20},{20... | collective-permute-start | bytes 884744 | tf_op jit(solution)/shard_map/ppermute | solution.py:397
  22.2 5.1 %collective-permute-done.6.refs_5_.refs_2_ = bf16[256,128]{1,0:T(8,128)(2,1)S(1)} collective-permute-done((bf16[256,128]{1,0:T(8,128)(2,1)S(1)}, bf16[256,128]{1,0:T(8,128)(2,1)S(1)}, u32[]{:S(2)}, u32[]{:S(2)}) %collective-permute-start.6) | collective-permute-done | bytes 65568 | tf_op jit(solution)/shard_map/ppermute | solution.py:397
  27.3 2.1 %collective-permute-done.5.refs_4_.refs_1_ = bf16[256,128]{1,0:T(8,128)(2,1)S(1)} collective-permute-done((bf16[256,128]{1,0:T(8,128)(2,1)S(1)}, bf16[256,128]{1,0:T(8,128)(2,1)S(1)}, u32[]{:S(2)}, u32[]{:S(2)}) %collective-permute-start.5) | collective-permute-done | bytes 65568 | tf_op jit(solution)/shard_map/ppermute | solution.py:397
  29.3 0.0 collective-permute-start.14
  29.3 1.5 %collective-permute-start.10 = (bf16[256,128]{1,0:T(8,128)(2,1)S(1)}, bf16[256,128]{1,0:T(8,128)(2,1)S(1)}, u32[]{:S(2)}, u32[]{:S(2)}) collective-permute-start(bf16[256,128]{1,0:T(8,128)(2,1)S(1)} %collective-permute-done.6.refs_5_.refs_2_), channel_id=1, source_target_pairs={{0,16},{16,0},{1,17},{17,1},{2,18},{18,2},{3,19},{19,3},{4,20},{20... | collective-permute-start | bytes 196616 | tf_op jit(solution)/shard_map/ppermute | solution.py:397
  30.8 0.0 collective-permute-done.4.refs_0_
  30.8 0.5 collective-permute-start.9
  31.4 2.2 %collective-permute-done.10.refs_8_ = bf16[256,128]{1,0:T(8,128)(2,1)S(1)} collective-permute-done((bf16[256,128]{1,0:T(8,128)(2,1)S(1)}, bf16[256,128]{1,0:T(8,128)(2,1)S(1)}, u32[]{:S(2)}, u32[]{:S(2)}) %collective-permute-start.10) | collective-permute-done | bytes 65568 | tf_op jit(solution)/shard_map/ppermute | solution.py:397
  33.6 1.5 %collective-permute-done.9.refs_7_ = bf16[256,128]{1,0:T(8,128)(2,1)S(1)} collective-permute-done((bf16[256,128]{1,0:T(8,128)(2,1)S(1)}, bf16[256,128]{1,0:T(8,128)(2,1)S(1)}, u32[]{:S(2)}, u32[]{:S(2)}) %collective-permute-start.9) | collective-permute-done | bytes 65568 | tf_op jit(solution)/shard_map/ppermute | solution.py:397
  35.1 0.0 collective-permute-done.8.refs_6_.refs_8_
  35.1 0.6 %shard_map.47.refs_1_.refs_0_ = bf16[256,128]{1,0:T(8,128)(2,1)S(1)} custom-call(bf16[256,128]{1,0:T(8,128)(2,1)S(1)} %shard_map.43.q_ref, f32[256,256]{1,0:T(8,128)S(1)} %get-tuple-element.34.refs_0_, f32[256,256]{1,0:T(8,128)S(1)} %get-tuple-element.35.refs_1_, bf16[256,128]{1,0:T(8,128)(2,1)S(1)} %get-tuple-element.36.refs_0_.refs_2_.refs_1_, ...), custom_call_target="tpu_custom_call" | custom-call | tf_op jit(solution)/shard_map/pallas_call | solution.py:303
  35.7 2.1 %collective-permute-start.11 = (bf16[256,128]{1,0:T(8,128)(2,1)S(1)}, bf16[256,128]{1,0:T(8,128)(2,1)S(1)}, u32[]{:S(2)}, u32[]{:S(2)}) collective-permute-start(bf16[256,128]{1,0:T(8,128)(2,1)S(1)} %shard_map.47.refs_1_.refs_0_), channel_id=1, source_target_pairs={{0,2},{2,0},{8,10},{10,8},{1,3},{3,1},{9,11},{11,9},{4,6},{6,4},{1... | collective-permute-start | bytes 196616 | tf_op jit(solution)/shard_map/ppermute | solution.py:397
  37.8 1.3 %collective-permute-start.12 = (bf16[256,128]{1,0:T(8,128)(2,1)S(1)}, bf16[256,128]{1,0:T(8,128)(2,1)S(1)}, u32[]{:S(2)}, u32[]{:S(2)}) collective-permute-start(bf16[256,128]{1,0:T(8,128)(2,1)S(1)} %shard_map.47.refs_1_.refs_0_), channel_id=1, source_target_pairs={{0,8},{2,10},{8,0},{10,2},{1,9},{3,11},{9,1},{11,3},{4,12},{6,14},... | collective-permute-start | bytes 196616 | tf_op jit(solution)/shard_map/ppermute | solution.py:397
  39.2 0.2 collective-permute-start.13
  39.4 0.0 collective-permute-done.15.refs_0_
  39.4 0.0 copy-start.1
  39.4 0.7 %collective-permute-start.16 = (bf16[64,1280]{1,0:T(8,128)(2,1)S(1)}, bf16[64,1280]{1,0:T(8,128)(2,1)S(1)}, u32[]{:S(2)}, u32[]{:S(2)}) collective-permute-start(bf16[64,1280]{1,0:T(8,128)(2,1)S(1)} %shard_map.51.refs_9_), channel_id=1, source_target_pairs={{0,16},{16,0},{1,17},{17,1},{2,18},{18,2},{3,19},{19,3},{4,20},{20... | collective-permute-start | bytes 491528 | tf_op jit(solution)/shard_map/ppermute | solution.py:397
  40.1 0.0 collective-permute-done.14.refs_0_
  40.1 0.0 collective-permute-done.11.refs_1_
  40.1 2.0 %collective-permute-done.12.refs_2_ = bf16[256,128]{1,0:T(8,128)(2,1)S(1)} collective-permute-done((bf16[256,128]{1,0:T(8,128)(2,1)S(1)}, bf16[256,128]{1,0:T(8,128)(2,1)S(1)}, u32[]{:S(2)}, u32[]{:S(2)}) %collective-permute-start.12) | collective-permute-done | bytes 65568 | tf_op jit(solution)/shard_map/ppermute | solution.py:397
  42.1 2.2 %collective-permute-done.13.refs_3_ = bf16[256,128]{1,0:T(8,128)(2,1)S(1)} collective-permute-done((bf16[256,128]{1,0:T(8,128)(2,1)S(1)}, bf16[256,128]{1,0:T(8,128)(2,1)S(1)}, u32[]{:S(2)}, u32[]{:S(2)}) %collective-permute-start.13) | collective-permute-done | bytes 65568 | tf_op jit(solution)/shard_map/ppermute | solution.py:397
  44.3 0.4 collective-permute-done.16.refs_10_
  44.7 0.0 copy-done.1
  44.7 1.3 %shard_map.52 = (bf16[4,32,1280]{2,1,0:T(8,128)(2,1)S(1)}, bf16[4,32,1280]{2,1,0:T(8,128)(2,1)S(1)}) custom-call(s32[7]{0:T(128)S(1)} %stack.59.at_ref, s32[1]{0:T(128)} %bitcast.place_ref, bf16[256,128]{1,0:T(8,128)(2,1)S(1)} %shard_map.47.refs_1_.refs_0_, bf16[256,128]{1,0:T(8,128)(2,1)S(1)} %collective-permute-done.11.refs_1_, ...), custom_call_target="tpu_custom_call" | custom-call | tf_op jit(solution)/shard_map/pallas_call | solution.py:346
  46.0 0.1 collective-permute-start.17
  46.1 1.6 %collective-permute-done.17.y_ref = bf16[4,32,1280]{2,1,0:T(8,128)(2,1)S(1)} collective-permute-done((bf16[4,32,1280]{2,1,0:T(8,128)(2,1)S(1)}, bf16[4,32,1280]{2,1,0:T(8,128)(2,1)S(1)}, u32[]{:S(2)}, u32[]{:S(2)}) %collective-permute-start.17) | collective-permute-done | bytes 327712 | tf_op jit(solution)/shard_map/ppermute | solution.py:397
  47.7 0.1 shard_map.53
  47.8 2.0 %collective-permute-start.18 = (bf16[32,1280]{1,0:T(8,128)(2,1)S(1)}, bf16[32,1280]{1,0:T(8,128)(2,1)S(1)}, u32[]{:S(2)}, u32[]{:S(2)}) collective-permute-start(bf16[32,1280]{1,0:T(8,128)(2,1)S(1)} %get-tuple-element.44), channel_id=1, source_target_pairs={{0,2},{2,0},{8,10},{10,8},{1,3},{3,1},{9,11},{11,9},{4,6},{6,4},{1... | collective-permute-start | bytes 245768 | tf_op jit(solution)/shard_map/ppermute | solution.py:397
  49.8 1.3 %collective-permute-start.19 = (bf16[32,1280]{1,0:T(8,128)(2,1)S(1)}, bf16[32,1280]{1,0:T(8,128)(2,1)S(1)}, u32[]{:S(2)}, u32[]{:S(2)}) collective-permute-start(bf16[32,1280]{1,0:T(8,128)(2,1)S(1)} %get-tuple-element.45), channel_id=1, source_target_pairs={{0,8},{2,10},{8,0},{10,2},{1,9},{3,11},{9,1},{11,3},{4,12},{6,14},... | collective-permute-start | bytes 245768 | tf_op jit(solution)/shard_map/ppermute | solution.py:397
  51.1 0.2 collective-permute-start.20
  51.3 1.2 %collective-permute-done.18.refs_1_ = bf16[32,1280]{1,0:T(8,128)(2,1)S(1)} collective-permute-done((bf16[32,1280]{1,0:T(8,128)(2,1)S(1)}, bf16[32,1280]{1,0:T(8,128)(2,1)S(1)}, u32[]{:S(2)}, u32[]{:S(2)}) %collective-permute-start.18) | collective-permute-done | bytes 81952 | tf_op jit(solution)/shard_map/ppermute | solution.py:397
  52.5 1.7 %collective-permute-done.19.refs_2_ = bf16[32,1280]{1,0:T(8,128)(2,1)S(1)} collective-permute-done((bf16[32,1280]{1,0:T(8,128)(2,1)S(1)}, bf16[32,1280]{1,0:T(8,128)(2,1)S(1)}, u32[]{:S(2)}, u32[]{:S(2)}) %collective-permute-start.19) | collective-permute-done | bytes 81952 | tf_op jit(solution)/shard_map/ppermute | solution.py:397
  54.2 2.2 %collective-permute-done.20.refs_3_ = bf16[32,1280]{1,0:T(8,128)(2,1)S(1)} collective-permute-done((bf16[32,1280]{1,0:T(8,128)(2,1)S(1)}, bf16[32,1280]{1,0:T(8,128)(2,1)S(1)}, u32[]{:S(2)}, u32[]{:S(2)}) %collective-permute-start.20) | collective-permute-done | bytes 81952 | tf_op jit(solution)/shard_map/ppermute | solution.py:397
  56.5 0.8 %shard_map.54 = bf16[32,5120]{1,0:T(8,128)(2,1)} custom-call(s32[1]{0:T(128)} %bitcast.place_ref, bf16[32,1280]{1,0:T(8,128)(2,1)S(1)} %get-tuple-element.43.refs_0_, bf16[32,1280]{1,0:T(8,128)(2,1)S(1)} %collective-permute-done.18.refs_1_, bf16[32,1280]{1,0:T(8,128)(2,1)S(1)} %collective-permute-done.19.refs_2_, ...), custom_call_target="tpu_custom_call" | custom-call | tf_op jit(solution)/shard_map/pallas_call | solution.py:386
  (11 shorter events, 0.1 us)
Async XLA Ops:
  0.0 10.9 %copy-start.3 = (s32[8]{0:T(128)S(1)}, s32[8]{0:T(128)}, u32[]{:S(2)}) copy-start(s32[8]{0:T(128)} %clip_ref.1) | copy-start | bytes 100
  0.0 0.9 %copy-start.2 = (bf16[3,32,1024]{2,1,0:T(8,128)(2,1)S(1)}, bf16[3,32,1024]{2,1,0:T(8,128)(2,1)}, u32[]{:S(2)}) copy-start(bf16[3,32,1024]{2,1,0:T(8,128)(2,1)} %x_ref.2) | copy-start | bytes 589828
  1.0 6.2 %collective-permute-start = (bf16[4,96,128]{2,1,0:T(8,128)(2,1)S(1)}, bf16[4,96,128]{2,1,0:T(8,128)(2,1)S(1)}, u32[]{:S(2)}, u32[]{:S(2)}) collective-permute-start(bf16[4,96,128]{2,1,0:T(8,128)(2,1)S(1)} %get-tuple-element.27), channel_id=1, source_target_pairs={{0,1},{1,0},{2,3},{3,2},{4,5},{5,4},{6,7},{7,6},{8,9},{9,8},{10,11... | collective-permute-start | bytes 294920 | tf_op jit(solution)/shard_map/ppermute | solution.py:397
  1.6 1.3 %copy-start = (bf16[128,5120]{1,0:T(8,128)(2,1)S(1)}, bf16[128,5120]{1,0:T(8,128)(2,1)}, u32[]{:S(2)}) copy-start(bf16[128,5120]{1,0:T(8,128)(2,1)} %refs_4_.1) | copy-start | bytes 3932164
  3.5 17.0 %collective-permute-start.7 = (bf16[640,128]{1,0:T(8,128)(2,1)S(1)}, bf16[640,128]{1,0:T(8,128)(2,1)S(1)}, u32[]{:S(2)}, u32[]{:S(2)}) collective-permute-start(bf16[640,128]{1,0:T(8,128)(2,1)S(1)} %get-tuple-element.38), channel_id=1, source_target_pairs={{0,4},{4,0},{1,5},{5,1},{2,6},{6,2},{3,7},{7,3},{8,12},{12,8},{9,1... | collective-permute-start | bytes 491528 | tf_op jit(solution)/shard_map/ppermute | solution.py:397
  7.2 5.6 %collective-permute-start.1 = (bf16[2,96,128]{2,1,0:T(8,128)(2,1)S(1)}, bf16[2,96,128]{2,1,0:T(8,128)(2,1)S(1)}, u32[]{:S(2)}, u32[]{:S(2)}) collective-permute-start(bf16[2,96,128]{2,1,0:T(8,128)(2,1)S(1)} %get-tuple-element.29), channel_id=1, source_target_pairs={{0,2},{2,0},{8,10},{10,8},{1,3},{3,1},{9,11},{11,9},{4,6},{6,4},{1... | collective-permute-start | bytes 147464 | tf_op jit(solution)/shard_map/ppermute | solution.py:397
  8.9 6.4 %collective-permute-start.2 = (bf16[2,96,128]{2,1,0:T(8,128)(2,1)S(1)}, bf16[2,96,128]{2,1,0:T(8,128)(2,1)S(1)}, u32[]{:S(2)}, u32[]{:S(2)}) collective-permute-start(bf16[2,96,128]{2,1,0:T(8,128)(2,1)S(1)} %get-tuple-element.30), channel_id=1, source_target_pairs={{0,8},{2,10},{8,0},{10,2},{1,9},{3,11},{9,1},{11,3},{4,12},{6,14},... | collective-permute-start | bytes 147464 | tf_op jit(solution)/shard_map/ppermute | solution.py:397
  10.4 7.1 %collective-permute-start.3 = (bf16[2,96,128]{2,1,0:T(8,128)(2,1)S(1)}, bf16[2,96,128]{2,1,0:T(8,128)(2,1)S(1)}, u32[]{:S(2)}, u32[]{:S(2)}) collective-permute-start(bf16[2,96,128]{2,1,0:T(8,128)(2,1)S(1)} %get-tuple-element.31), channel_id=1, source_target_pairs={{0,10},{2,8},{8,2},{10,0},{1,11},{3,9},{9,3},{11,1},{4,14},{6,12},... | collective-permute-start | bytes 147464 | tf_op jit(solution)/shard_map/ppermute | solution.py:397
  12.8 18.0 %collective-permute-start.4 = (bf16[64,1280]{1,0:T(8,128)(2,1)S(1)}, bf16[64,1280]{1,0:T(8,128)(2,1)S(1)}, u32[]{:S(2)}, u32[]{:S(2)}) collective-permute-start(bf16[64,1280]{1,0:T(8,128)(2,1)S(1)} %shard_map.41), channel_id=1, source_target_pairs={{0,2},{2,0},{1,3},{3,1},{4,6},{6,4},{5,7},{7,5},{8,10},{10,8},{9,1... | collective-permute-start | bytes 491528 | tf_op jit(solution)/shard_map/ppermute | solution.py:397
  17.5 9.7 %collective-permute-start.6 = (bf16[256,128]{1,0:T(8,128)(2,1)S(1)}, bf16[256,128]{1,0:T(8,128)(2,1)S(1)}, u32[]{:S(2)}, u32[]{:S(2)}) collective-permute-start(bf16[256,128]{1,0:T(8,128)(2,1)S(1)} %get-tuple-element.37.refs_1_.refs_3_), channel_id=1, source_target_pairs={{0,4},{4,0},{1,5},{5,1},{2,6},{6,2},{3,7},{7,3},{8,12},{12,8},{9,1... | collective-permute-start | bytes 196616 | tf_op jit(solution)/shard_map/ppermute | solution.py:397
  17.6 11.7 %collective-permute-start.5 = (bf16[256,128]{1,0:T(8,128)(2,1)S(1)}, bf16[256,128]{1,0:T(8,128)(2,1)S(1)}, u32[]{:S(2)}, u32[]{:S(2)}) collective-permute-start(bf16[256,128]{1,0:T(8,128)(2,1)S(1)} %get-tuple-element.36.refs_0_.refs_2_.refs_1_), channel_id=1, source_target_pairs={{0,4},{4,0},{1,5},{5,1},{2,6},{6,2},{3,7},{7,3},{8,12},{12,8},{9,1... | collective-permute-start | bytes 196616 | tf_op jit(solution)/shard_map/ppermute | solution.py:397
  20.5 18.8 %collective-permute-start.15 = (bf16[64,1280]{1,0:T(8,128)(2,1)S(1)}, bf16[64,1280]{1,0:T(8,128)(2,1)S(1)}, u32[]{:S(2)}, u32[]{:S(2)}) collective-permute-start(bf16[64,1280]{1,0:T(8,128)(2,1)S(1)} %shard_map.50), channel_id=1, source_target_pairs={{0,6},{2,4},{4,2},{6,0},{1,7},{3,5},{5,3},{7,1},{8,14},{10,12},{12... | collective-permute-start | bytes 491528 | tf_op jit(solution)/shard_map/ppermute | solution.py:397
  20.6 14.5 %collective-permute-start.8 = (bf16[1152,128]{1,0:T(8,128)(2,1)S(1)}, bf16[1152,128]{1,0:T(8,128)(2,1)S(1)}, u32[]{:S(2)}, u32[]{:S(2)}) collective-permute-start(bf16[1152,128]{1,0:T(8,128)(2,1)S(1)} %shard_map.46), channel_id=1, source_target_pairs={{0,16},{16,0},{1,17},{17,1},{2,18},{18,2},{3,19},{19,3},{4,20},{20... | collective-permute-start | bytes 884744 | tf_op jit(solution)/shard_map/ppermute | solution.py:397
  29.3 10.8 %collective-permute-start.14 = (bf16[64,1280]{1,0:T(8,128)(2,1)S(1)}, bf16[64,1280]{1,0:T(8,128)(2,1)S(1)}, u32[]{:S(2)}, u32[]{:S(2)}) collective-permute-start(bf16[64,1280]{1,0:T(8,128)(2,1)S(1)} %shard_map.48), channel_id=1, source_target_pairs={{0,2},{2,0},{1,3},{3,1},{4,6},{6,4},{5,7},{7,5},{8,10},{10,8},{9,1... | collective-permute-start | bytes 491528 | tf_op jit(solution)/shard_map/ppermute | solution.py:397
  29.3 4.3 %collective-permute-start.10 = (bf16[256,128]{1,0:T(8,128)(2,1)S(1)}, bf16[256,128]{1,0:T(8,128)(2,1)S(1)}, u32[]{:S(2)}, u32[]{:S(2)}) collective-permute-start(bf16[256,128]{1,0:T(8,128)(2,1)S(1)} %collective-permute-done.6.refs_5_.refs_2_), channel_id=1, source_target_pairs={{0,16},{16,0},{1,17},{17,1},{2,18},{18,2},{3,19},{19,3},{4,20},{20... | collective-permute-start | bytes 196616 | tf_op jit(solution)/shard_map/ppermute | solution.py:397
  30.8 4.3 %collective-permute-start.9 = (bf16[256,128]{1,0:T(8,128)(2,1)S(1)}, bf16[256,128]{1,0:T(8,128)(2,1)S(1)}, u32[]{:S(2)}, u32[]{:S(2)}) collective-permute-start(bf16[256,128]{1,0:T(8,128)(2,1)S(1)} %collective-permute-done.5.refs_4_.refs_1_), channel_id=1, source_target_pairs={{0,16},{16,0},{1,17},{17,1},{2,18},{18,2},{3,19},{19,3},{4,20},{20... | collective-permute-start | bytes 196616 | tf_op jit(solution)/shard_map/ppermute | solution.py:397
  35.7 4.3 %collective-permute-start.11 = (bf16[256,128]{1,0:T(8,128)(2,1)S(1)}, bf16[256,128]{1,0:T(8,128)(2,1)S(1)}, u32[]{:S(2)}, u32[]{:S(2)}) collective-permute-start(bf16[256,128]{1,0:T(8,128)(2,1)S(1)} %shard_map.47.refs_1_.refs_0_), channel_id=1, source_target_pairs={{0,2},{2,0},{8,10},{10,8},{1,3},{3,1},{9,11},{11,9},{4,6},{6,4},{1... | collective-permute-start | bytes 196616 | tf_op jit(solution)/shard_map/ppermute | solution.py:397
  37.8 4.3 %collective-permute-start.12 = (bf16[256,128]{1,0:T(8,128)(2,1)S(1)}, bf16[256,128]{1,0:T(8,128)(2,1)S(1)}, u32[]{:S(2)}, u32[]{:S(2)}) collective-permute-start(bf16[256,128]{1,0:T(8,128)(2,1)S(1)} %shard_map.47.refs_1_.refs_0_), channel_id=1, source_target_pairs={{0,8},{2,10},{8,0},{10,2},{1,9},{3,11},{9,1},{11,3},{4,12},{6,14},... | collective-permute-start | bytes 196616 | tf_op jit(solution)/shard_map/ppermute | solution.py:397
  39.2 5.2 %collective-permute-start.13 = (bf16[256,128]{1,0:T(8,128)(2,1)S(1)}, bf16[256,128]{1,0:T(8,128)(2,1)S(1)}, u32[]{:S(2)}, u32[]{:S(2)}) collective-permute-start(bf16[256,128]{1,0:T(8,128)(2,1)S(1)} %shard_map.47.refs_1_.refs_0_), channel_id=1, source_target_pairs={{0,10},{2,8},{8,2},{10,0},{1,11},{3,9},{9,3},{11,1},{4,14},{6,12},... | collective-permute-start | bytes 196616 | tf_op jit(solution)/shard_map/ppermute | solution.py:397
  39.4 5.3 %copy-start.1 = (bf16[128,5120]{1,0:T(8,128)(2,1)S(1)}, bf16[128,5120]{1,0:T(8,128)(2,1)}, u32[]{:S(2)}) copy-start(bf16[128,5120]{1,0:T(8,128)(2,1)} %refs_4_.1) | copy-start | bytes 3932164
  39.4 5.3 %collective-permute-start.16 = (bf16[64,1280]{1,0:T(8,128)(2,1)S(1)}, bf16[64,1280]{1,0:T(8,128)(2,1)S(1)}, u32[]{:S(2)}, u32[]{:S(2)}) collective-permute-start(bf16[64,1280]{1,0:T(8,128)(2,1)S(1)} %shard_map.51.refs_9_), channel_id=1, source_target_pairs={{0,16},{16,0},{1,17},{17,1},{2,18},{18,2},{3,19},{19,3},{4,20},{20... | collective-permute-start | bytes 491528 | tf_op jit(solution)/shard_map/ppermute | solution.py:397
  46.0 1.7 %collective-permute-start.17 = (bf16[4,32,1280]{2,1,0:T(8,128)(2,1)S(1)}, bf16[4,32,1280]{2,1,0:T(8,128)(2,1)S(1)}, u32[]{:S(2)}, u32[]{:S(2)}) collective-permute-start(bf16[4,32,1280]{2,1,0:T(8,128)(2,1)S(1)} %get-tuple-element.42), channel_id=1, source_target_pairs={{0,1},{1,0},{2,3},{3,2},{4,5},{5,4},{6,7},{7,6},{8,9},{9,8},{10,11... | collective-permute-start | bytes 983048 | tf_op jit(solution)/shard_map/ppermute | solution.py:397
  47.8 4.8 %collective-permute-start.18 = (bf16[32,1280]{1,0:T(8,128)(2,1)S(1)}, bf16[32,1280]{1,0:T(8,128)(2,1)S(1)}, u32[]{:S(2)}, u32[]{:S(2)}) collective-permute-start(bf16[32,1280]{1,0:T(8,128)(2,1)S(1)} %get-tuple-element.44), channel_id=1, source_target_pairs={{0,2},{2,0},{8,10},{10,8},{1,3},{3,1},{9,11},{11,9},{4,6},{6,4},{1... | collective-permute-start | bytes 245768 | tf_op jit(solution)/shard_map/ppermute | solution.py:397
  49.8 4.5 %collective-permute-start.19 = (bf16[32,1280]{1,0:T(8,128)(2,1)S(1)}, bf16[32,1280]{1,0:T(8,128)(2,1)S(1)}, u32[]{:S(2)}, u32[]{:S(2)}) collective-permute-start(bf16[32,1280]{1,0:T(8,128)(2,1)S(1)} %get-tuple-element.45), channel_id=1, source_target_pairs={{0,8},{2,10},{8,0},{10,2},{1,9},{3,11},{9,1},{11,3},{4,12},{6,14},... | collective-permute-start | bytes 245768 | tf_op jit(solution)/shard_map/ppermute | solution.py:397
  51.1 5.3 %collective-permute-start.20 = (bf16[32,1280]{1,0:T(8,128)(2,1)S(1)}, bf16[32,1280]{1,0:T(8,128)(2,1)S(1)}, u32[]{:S(2)}, u32[]{:S(2)}) collective-permute-start(bf16[32,1280]{1,0:T(8,128)(2,1)S(1)} %get-tuple-element.46), channel_id=1, source_target_pairs={{0,10},{2,8},{8,2},{10,0},{1,11},{3,9},{9,3},{11,1},{4,14},{6,12},... | collective-permute-start | bytes 245768 | tf_op jit(solution)/shard_map/ppermute | solution.py:397

commit v15 on v13

--- a/solution.py
+++ b/solution.py
@@ -415,16 +415,16 @@
     far = after(xor(w_far, ("zh",), 1), cost=AHEAD)
     kept, given = lanes(qkv, core, head_dim)
     shared = swap_all(deal(kept, xor(given, ("core",), 1), place), quarter)
-    w_next = after(xor(after(w_near, shared[1]), ("zl",), 1), cost=AHEAD)
     q, k, v = sort(shared, place)
     k_far, v_far = xor(k, ("zh",), 1), xor(v, ("zh",), 1)
     near = xor(join(k, v, far), ("y",), 1)
     corner = xor(after(w_corner, k), ("zh", "zl"), 3)
+    w_next = xor(after(w_near, k), ("zl",), 1)
     kvs = [(k, v), (k_far, v_far), near, (xor(k_far, ("y",), 1), xor(v_far, ("y",), 1))]
 
     bases = [y * 2 * FRB, (1 - y) * 2 * FRB]
     mask_of = masks(bases, 4 * tok, tok, 8 * tok, frame_clip)
-    attn = attention(after(q, w_next), kvs, mask_of, [0, 0, 1, 1], head_dim)
+    attn = attention(q, kvs, mask_of, [0, 0, 1, 1], head_dim)
     corner = after(corner, attn, cost=SOON)
     corner_rest = xor(corner, ("y",), 1)
     attns = swap_all([attn] * 4, quarter)

time: 55.3 us -> 54.6 us (0.987)
  waiting for transfers between devices: 21.9 us -> 24.5 us
  starting transfers between devices: 26.5 us -> 24.1 us
  local copies, waits for them, and re-layouts: 2.35 us -> 1.42 us
    ppermute x20, waiting for transfers between devices: 21.9 us -> 24.5 us  [xor(): return lax.ppermute(x, axis, [(i, i ^ by) for i in range(size)])]
    ppermute x20, starting transfers between devices: 26.5 us -> 24.1 us  [xor(): return lax.ppermute(x, axis, [(i, i ^ by) for i in range(size)])]
    unnamed x8, local copies, waits for them, and re-layouts: 2.26 us -> 1.33 us
  transfers between devices with their start and end apart: 20 -> 20, of which waited for: 10 -> 15; matrix products, arithmetic and copies ran while one was open for 0% -> 0% of each run, Pallas kernels for 4% -> 3%
where the time goes in v15:
time: 54.6 us; the launch traced here: 54.5 us
  waiting for transfers between devices  24.5 us (45%)
  starting transfers between devices  24.1 us (44%)
  Pallas kernels  4.16 us (8%)
  local copies, waits for them, and re-layouts  1.42 us (3%)
    ppermute x20, waiting for transfers between devices, xor(): return lax.ppermute(x, axis, [(i, i ^ by) for i in range(size)])  24.5 us
    ppermute x20, starting transfers between devices, xor(): return lax.ppermute(x, axis, [(i, i ^ by) for i in range(size)])  24.1 us
    unnamed x8, local copies, waits for them, and re-layouts  1.33 us
    pallas_call x1, Pallas kernels, project(): pl.pallas_call(functools.partial(project_kernel, blks, sizes), out_shape=...  1.26 us
  transfers between devices with their start and end apart: 20, of which 15 were waited for; matrix products, arithmetic and copies ran while one was open for 0% of the time, Pallas kernels for 3%

profile of v15, /device:TPU:0, one launch (start us, length us, event | category | flops | bytes accessed | tf_op | source)
XLA Modules:
  0.0 54.5 jit_solution(10585666159532761222)
XLA Ops:
  0.0 0.1 pad_add_fusion.1.at_ref
  0.1 0.0 copy-start
  0.1 1.3 %copy-done = bf16[128,5120]{1,0:T(8,128)(2,1)S(1)} copy-done((bf16[128,5120]{1,0:T(8,128)(2,1)S(1)}, bf16[128,5120]{1,0:T(8,128)(2,1)}, u32[]{:S(2)}) %copy-start) | copy-done | bytes 1310744
  1.4 0.0 copy-start.2
  1.4 0.6 %shard_map.41 = (bf16[640,128]{1,0:T(8,128)(2,1)S(1)}, bf16[64,1280]{1,0:T(8,128)(2,1)S(1)}, bf16[128,1280]{1,0:T(8,128)(2,1)S(1)}) custom-call(s32[3]{0:T(128)S(1)} %pad_add_fusion.1.at_ref, bf16[128,5120]{1,0:T(8,128)(2,1)S(1)} %copy-done), custom_call_target="tpu_custom_call" | custom-call | tf_op jit(solution)/shard_map/pallas_call | solution.py:93
  2.0 4.1 %collective-permute-start.6 = (bf16[640,128]{1,0:T(8,128)(2,1)S(1)}, bf16[640,128]{1,0:T(8,128)(2,1)S(1)}, u32[]{:S(2)}, u32[]{:S(2)}) collective-permute-start(bf16[640,128]{1,0:T(8,128)(2,1)S(1)} %get-tuple-element.36), channel_id=1, source_target_pairs={{0,4},{4,0},{1,5},{5,1},{2,6},{6,2},{3,7},{7,3},{8,12},{12,8},{9,1... | collective-permute-start | bytes 491528 | tf_op jit(solution)/shard_map/ppermute | solution.py:398
  6.1 0.0 copy-done.2
  6.1 0.1 shard_map.37
  6.2 0.1 collective-permute-start
  6.3 1.3 %collective-permute-done.got_ref = bf16[4,96,128]{2,1,0:T(8,128)(2,1)S(1)} collective-permute-done((bf16[4,96,128]{2,1,0:T(8,128)(2,1)S(1)}, bf16[4,96,128]{2,1,0:T(8,128)(2,1)S(1)}, u32[]{:S(2)}, u32[]{:S(2)}) %collective-permute-start) | collective-permute-done | bytes 98336 | tf_op jit(solution)/shard_map/ppermute | solution.py:398
  7.6 1.6 %collective-permute-start.1 = (bf16[2,96,128]{2,1,0:T(8,128)(2,1)S(1)}, bf16[2,96,128]{2,1,0:T(8,128)(2,1)S(1)}, u32[]{:S(2)}, u32[]{:S(2)}) collective-permute-start(bf16[2,96,128]{2,1,0:T(8,128)(2,1)S(1)} %get-tuple-element.28), channel_id=1, source_target_pairs={{0,2},{2,0},{8,10},{10,8},{1,3},{3,1},{9,11},{11,9},{4,6},{6,4},{1... | collective-permute-start | bytes 147464 | tf_op jit(solution)/shard_map/ppermute | solution.py:398
  9.2 1.5 %collective-permute-start.2 = (bf16[2,96,128]{2,1,0:T(8,128)(2,1)S(1)}, bf16[2,96,128]{2,1,0:T(8,128)(2,1)S(1)}, u32[]{:S(2)}, u32[]{:S(2)}) collective-permute-start(bf16[2,96,128]{2,1,0:T(8,128)(2,1)S(1)} %get-tuple-element.29), channel_id=1, source_target_pairs={{0,8},{2,10},{8,0},{10,2},{1,9},{3,11},{9,1},{11,3},{4,12},{6,14},... | collective-permute-start | bytes 147464 | tf_op jit(solution)/shard_map/ppermute | solution.py:398
  10.7 0.4 collective-permute-start.3
  11.1 0.8 %collective-permute-done.1.refs_1_ = bf16[2,96,128]{2,1,0:T(8,128)(2,1)S(1)} collective-permute-done((bf16[2,96,128]{2,1,0:T(8,128)(2,1)S(1)}, bf16[2,96,128]{2,1,0:T(8,128)(2,1)S(1)}, u32[]{:S(2)}, u32[]{:S(2)}) %collective-permute-start.1) | collective-permute-done | bytes 49184 | tf_op jit(solution)/shard_map/ppermute | solution.py:398
  11.9 1.4 %collective-permute-done.2.refs_2_ = bf16[2,96,128]{2,1,0:T(8,128)(2,1)S(1)} collective-permute-done((bf16[2,96,128]{2,1,0:T(8,128)(2,1)S(1)}, bf16[2,96,128]{2,1,0:T(8,128)(2,1)S(1)}, u32[]{:S(2)}, u32[]{:S(2)}) %collective-permute-start.2) | collective-permute-done | bytes 49184 | tf_op jit(solution)/shard_map/ppermute | solution.py:398
  13.3 2.6 %collective-permute-done.3.refs_3_ = bf16[2,96,128]{2,1,0:T(8,128)(2,1)S(1)} collective-permute-done((bf16[2,96,128]{2,1,0:T(8,128)(2,1)S(1)}, bf16[2,96,128]{2,1,0:T(8,128)(2,1)S(1)}, u32[]{:S(2)}, u32[]{:S(2)}) %collective-permute-start.3) | collective-permute-done | bytes 49184 | tf_op jit(solution)/shard_map/ppermute | solution.py:398
  15.9 0.0 copy-start.3
  15.9 0.0 collective-permute-done.6.refs_0_
  16.0 1.6 %collective-permute-start.7 = (bf16[1152,128]{1,0:T(8,128)(2,1)S(1)}, bf16[1152,128]{1,0:T(8,128)(2,1)S(1)}, u32[]{:S(2)}, u32[]{:S(2)}) collective-permute-start(bf16[1152,128]{1,0:T(8,128)(2,1)S(1)} %shard_map.43), channel_id=1, source_target_pairs={{0,16},{16,0},{1,17},{17,1},{2,18},{18,2},{3,19},{19,3},{4,20},{20... | collective-permute-start | bytes 884744 | tf_op jit(solution)/shard_map/ppermute | solution.py:398
  17.5 0.2 collective-permute-start.4
  17.7 2.8 %collective-permute-start.5 = (bf16[256,128]{1,0:T(8,128)(2,1)S(1)}, bf16[256,128]{1,0:T(8,128)(2,1)S(1)}, u32[]{:S(2)}, u32[]{:S(2)}) collective-permute-start(bf16[256,128]{1,0:T(8,128)(2,1)S(1)} %get-tuple-element.35.refs_1_.refs_3_), channel_id=1, source_target_pairs={{0,4},{4,0},{1,5},{5,1},{2,6},{6,2},{3,7},{7,3},{8,12},{12,8},{9,1... | collective-permute-start | bytes 196616 | tf_op jit(solution)/shard_map/ppermute | solution.py:398
  20.5 3.0 %collective-permute-start.14 = (bf16[64,1280]{1,0:T(8,128)(2,1)S(1)}, bf16[64,1280]{1,0:T(8,128)(2,1)S(1)}, u32[]{:S(2)}, u32[]{:S(2)}) collective-permute-start(bf16[64,1280]{1,0:T(8,128)(2,1)S(1)} %shard_map.47), channel_id=1, source_target_pairs={{0,6},{2,4},{4,2},{6,0},{1,7},{3,5},{5,3},{7,1},{8,14},{10,12},{12... | collective-permute-start | bytes 491528 | tf_op jit(solution)/shard_map/ppermute | solution.py:398
  23.4 5.7 %collective-permute-done.4.refs_4_ = bf16[256,128]{1,0:T(8,128)(2,1)S(1)} collective-permute-done((bf16[256,128]{1,0:T(8,128)(2,1)S(1)}, bf16[256,128]{1,0:T(8,128)(2,1)S(1)}, u32[]{:S(2)}, u32[]{:S(2)}) %collective-permute-start.4) | collective-permute-done | bytes 65568 | tf_op jit(solution)/shard_map/ppermute | solution.py:398
  29.1 0.5 collective-permute-start.8
  29.6 0.9 %collective-permute-done.5.refs_5_ = bf16[256,128]{1,0:T(8,128)(2,1)S(1)} collective-permute-done((bf16[256,128]{1,0:T(8,128)(2,1)S(1)}, bf16[256,128]{1,0:T(8,128)(2,1)S(1)}, u32[]{:S(2)}, u32[]{:S(2)}) %collective-permute-start.5) | collective-permute-done | bytes 65568 | tf_op jit(solution)/shard_map/ppermute | solution.py:398
  30.5 0.6 %collective-permute-start.9 = (bf16[256,128]{1,0:T(8,128)(2,1)S(1)}, bf16[256,128]{1,0:T(8,128)(2,1)S(1)}, u32[]{:S(2)}, u32[]{:S(2)}) collective-permute-start(bf16[256,128]{1,0:T(8,128)(2,1)S(1)} %collective-permute-done.5.refs_5_), channel_id=1, source_target_pairs={{0,16},{16,0},{1,17},{17,1},{2,18},{18,2},{3,19},{19,3},{4,20},{20... | collective-permute-start | bytes 196616 | tf_op jit(solution)/shard_map/ppermute | solution.py:398
  31.2 0.1 pad_add_fusion.base_ref
  31.2 0.0 copy-done.3
  31.2 0.7 %shard_map.40 = (f32[256,256]{1,0:T(8,128)S(1)}, f32[256,256]{1,0:T(8,128)S(1)}) custom-call(s32[2]{0:T(128)S(1)} %pad_add_fusion.base_ref, s32[8]{0:T(128)S(1)} %copy-done.3), custom_call_target="tpu_custom_call" | custom-call | tf_op jit(solution)/shard_map/pallas_call | solution.py:244
  31.9 0.1 stack.55.at_ref
  32.0 0.0 collective-permute-start.13
  32.1 1.3 %collective-permute-done.8.refs_7_ = bf16[256,128]{1,0:T(8,128)(2,1)S(1)} collective-permute-done((bf16[256,128]{1,0:T(8,128)(2,1)S(1)}, bf16[256,128]{1,0:T(8,128)(2,1)S(1)}, u32[]{:S(2)}, u32[]{:S(2)}) %collective-permute-start.8) | collective-permute-done | bytes 65568 | tf_op jit(solution)/shard_map/ppermute | solution.py:398
  33.4 1.4 %collective-permute-done.9.refs_8_ = bf16[256,128]{1,0:T(8,128)(2,1)S(1)} collective-permute-done((bf16[256,128]{1,0:T(8,128)(2,1)S(1)}, bf16[256,128]{1,0:T(8,128)(2,1)S(1)}, u32[]{:S(2)}, u32[]{:S(2)}) %collective-permute-start.9) | collective-permute-done | bytes 65568 | tf_op jit(solution)/shard_map/ppermute | solution.py:398
  34.8 0.0 collective-permute-done.7.refs_6_.refs_7_
  34.8 0.6 %shard_map.44.refs_1_.refs_0_ = bf16[256,128]{1,0:T(8,128)(2,1)S(1)} custom-call(bf16[256,128]{1,0:T(8,128)(2,1)S(1)} %get-tuple-element.31.q_ref, f32[256,256]{1,0:T(8,128)S(1)} %get-tuple-element.32.refs_0_, f32[256,256]{1,0:T(8,128)S(1)} %get-tuple-element.33.refs_1_, bf16[256,128]{1,0:T(8,128)(2,1)S(1)} %get-tuple-element.34.refs_0_.refs_2_.refs_1_, ...), custom_call_target="tpu_custom_call" | custom-call | tf_op jit(solution)/shard_map/pallas_call | solution.py:304
  35.4 0.1 collective-permute-start.10
  35.5 0.6 %collective-permute-start.11 = (bf16[256,128]{1,0:T(8,128)(2,1)S(1)}, bf16[256,128]{1,0:T(8,128)(2,1)S(1)}, u32[]{:S(2)}, u32[]{:S(2)}) collective-permute-start(bf16[256,128]{1,0:T(8,128)(2,1)S(1)} %shard_map.44.refs_1_.refs_0_), channel_id=1, source_target_pairs={{0,8},{2,10},{8,0},{10,2},{1,9},{3,11},{9,1},{11,3},{4,12},{6,14},... | collective-permute-start | bytes 196616 | tf_op jit(solution)/shard_map/ppermute | solution.py:398
  36.1 2.9 %collective-permute-start.12 = (bf16[256,128]{1,0:T(8,128)(2,1)S(1)}, bf16[256,128]{1,0:T(8,128)(2,1)S(1)}, u32[]{:S(2)}, u32[]{:S(2)}) collective-permute-start(bf16[256,128]{1,0:T(8,128)(2,1)S(1)} %shard_map.44.refs_1_.refs_0_), channel_id=1, source_target_pairs={{0,10},{2,8},{8,2},{10,0},{1,11},{3,9},{9,3},{11,1},{4,14},{6,12},... | collective-permute-start | bytes 196616 | tf_op jit(solution)/shard_map/ppermute | solution.py:398
  39.0 0.0 collective-permute-done.14.refs_0_
  39.0 0.0 copy-start.1
  39.0 0.6 %collective-permute-start.15 = (bf16[64,1280]{1,0:T(8,128)(2,1)S(1)}, bf16[64,1280]{1,0:T(8,128)(2,1)S(1)}, u32[]{:S(2)}, u32[]{:S(2)}) collective-permute-start(bf16[64,1280]{1,0:T(8,128)(2,1)S(1)} %shard_map.48.refs_8_), channel_id=1, source_target_pairs={{0,16},{16,0},{1,17},{17,1},{2,18},{18,2},{3,19},{19,3},{4,20},{20... | collective-permute-start | bytes 491528 | tf_op jit(solution)/shard_map/ppermute | solution.py:398
  39.6 0.1 collective-permute-done.13.refs_0_
  39.7 0.7 %collective-permute-done.10.refs_1_ = bf16[256,128]{1,0:T(8,128)(2,1)S(1)} collective-permute-done((bf16[256,128]{1,0:T(8,128)(2,1)S(1)}, bf16[256,128]{1,0:T(8,128)(2,1)S(1)}, u32[]{:S(2)}, u32[]{:S(2)}) %collective-permute-start.10) | collective-permute-done | bytes 65568 | tf_op jit(solution)/shard_map/ppermute | solution.py:398
  40.4 0.0 collective-permute-done.11.refs_2_
  40.4 1.8 %collective-permute-done.12.refs_3_ = bf16[256,128]{1,0:T(8,128)(2,1)S(1)} collective-permute-done((bf16[256,128]{1,0:T(8,128)(2,1)S(1)}, bf16[256,128]{1,0:T(8,128)(2,1)S(1)}, u32[]{:S(2)}, u32[]{:S(2)}) %collective-permute-start.12) | collective-permute-done | bytes 65568 | tf_op jit(solution)/shard_map/ppermute | solution.py:398
  42.2 2.1 %collective-permute-done.15.refs_9_ = bf16[64,1280]{1,0:T(8,128)(2,1)S(1)} collective-permute-done((bf16[64,1280]{1,0:T(8,128)(2,1)S(1)}, bf16[64,1280]{1,0:T(8,128)(2,1)S(1)}, u32[]{:S(2)}, u32[]{:S(2)}) %collective-permute-start.15) | collective-permute-done | bytes 163872 | tf_op jit(solution)/shard_map/ppermute | solution.py:398
  44.3 0.0 copy-done.1
  44.3 1.3 %shard_map.49 = (bf16[4,32,1280]{2,1,0:T(8,128)(2,1)S(1)}, bf16[4,32,1280]{2,1,0:T(8,128)(2,1)S(1)}) custom-call(s32[6]{0:T(128)S(1)} %stack.55.at_ref, s32[1]{0:T(128)} %bitcast.place_ref, bf16[256,128]{1,0:T(8,128)(2,1)S(1)} %shard_map.44.refs_1_.refs_0_, bf16[256,128]{1,0:T(8,128)(2,1)S(1)} %collective-permute-done.10.refs_1_, ...), custom_call_target="tpu_custom_call" | custom-call | tf_op jit(solution)/shard_map/pallas_call | solution.py:347
  45.6 0.1 collective-permute-start.16
  45.7 1.6 %collective-permute-done.16.y_ref = bf16[4,32,1280]{2,1,0:T(8,128)(2,1)S(1)} collective-permute-done((bf16[4,32,1280]{2,1,0:T(8,128)(2,1)S(1)}, bf16[4,32,1280]{2,1,0:T(8,128)(2,1)S(1)}, u32[]{:S(2)}, u32[]{:S(2)}) %collective-permute-start.16) | collective-permute-done | bytes 327712 | tf_op jit(solution)/shard_map/ppermute | solution.py:398
  47.3 0.1 shard_map.50
  47.4 0.1 collective-permute-start.17
  47.5 0.6 %collective-permute-start.18 = (bf16[32,1280]{1,0:T(8,128)(2,1)S(1)}, bf16[32,1280]{1,0:T(8,128)(2,1)S(1)}, u32[]{:S(2)}, u32[]{:S(2)}) collective-permute-start(bf16[32,1280]{1,0:T(8,128)(2,1)S(1)} %get-tuple-element.43), channel_id=1, source_target_pairs={{0,8},{2,10},{8,0},{10,2},{1,9},{3,11},{9,1},{11,3},{4,12},{6,14},... | collective-permute-start | bytes 245768 | tf_op jit(solution)/shard_map/ppermute | solution.py:398
  48.1 2.9 %collective-permute-start.19 = (bf16[32,1280]{1,0:T(8,128)(2,1)S(1)}, bf16[32,1280]{1,0:T(8,128)(2,1)S(1)}, u32[]{:S(2)}, u32[]{:S(2)}) collective-permute-start(bf16[32,1280]{1,0:T(8,128)(2,1)S(1)} %get-tuple-element.44), channel_id=1, source_target_pairs={{0,10},{2,8},{8,2},{10,0},{1,11},{3,9},{9,3},{11,1},{4,14},{6,12},... | collective-permute-start | bytes 245768 | tf_op jit(solution)/shard_map/ppermute | solution.py:398
  50.9 1.6 %collective-permute-done.17.refs_1_ = bf16[32,1280]{1,0:T(8,128)(2,1)S(1)} collective-permute-done((bf16[32,1280]{1,0:T(8,128)(2,1)S(1)}, bf16[32,1280]{1,0:T(8,128)(2,1)S(1)}, u32[]{:S(2)}, u32[]{:S(2)}) %collective-permute-start.17) | collective-permute-done | bytes 81952 | tf_op jit(solution)/shard_map/ppermute | solution.py:398
  52.5 1.3 %collective-permute-done.18.refs_2_ = bf16[32,1280]{1,0:T(8,128)(2,1)S(1)} collective-permute-done((bf16[32,1280]{1,0:T(8,128)(2,1)S(1)}, bf16[32,1280]{1,0:T(8,128)(2,1)S(1)}, u32[]{:S(2)}, u32[]{:S(2)}) %collective-permute-start.18) | collective-permute-done | bytes 81952 | tf_op jit(solution)/shard_map/ppermute | solution.py:398
  53.7 0.0 collective-permute-done.19.refs_3_
  53.7 0.8 %shard_map.51 = bf16[32,5120]{1,0:T(8,128)(2,1)} custom-call(s32[1]{0:T(128)} %bitcast.place_ref, bf16[32,1280]{1,0:T(8,128)(2,1)S(1)} %get-tuple-element.41.refs_0_, bf16[32,1280]{1,0:T(8,128)(2,1)S(1)} %collective-permute-done.17.refs_1_, bf16[32,1280]{1,0:T(8,128)(2,1)S(1)} %collective-permute-done.18.refs_2_, ...), custom_call_target="tpu_custom_call" | custom-call | tf_op jit(solution)/shard_map/pallas_call | solution.py:387
  (8 shorter events, 0.1 us)
Async XLA Ops:
  0.1 1.3 %copy-start = (bf16[128,5120]{1,0:T(8,128)(2,1)S(1)}, bf16[128,5120]{1,0:T(8,128)(2,1)}, u32[]{:S(2)}) copy-start(bf16[128,5120]{1,0:T(8,128)(2,1)} %refs_4_.1) | copy-start | bytes 3932164
  1.4 4.7 %copy-start.2 = (bf16[3,32,1024]{2,1,0:T(8,128)(2,1)S(1)}, bf16[3,32,1024]{2,1,0:T(8,128)(2,1)}, u32[]{:S(2)}) copy-start(bf16[3,32,1024]{2,1,0:T(8,128)(2,1)} %x_ref.2) | copy-start | bytes 589828
  2.0 13.9 %collective-permute-start.6 = (bf16[640,128]{1,0:T(8,128)(2,1)S(1)}, bf16[640,128]{1,0:T(8,128)(2,1)S(1)}, u32[]{:S(2)}, u32[]{:S(2)}) collective-permute-start(bf16[640,128]{1,0:T(8,128)(2,1)S(1)} %get-tuple-element.36), channel_id=1, source_target_pairs={{0,4},{4,0},{1,5},{5,1},{2,6},{6,2},{3,7},{7,3},{8,12},{12,8},{9,1... | collective-permute-start | bytes 491528 | tf_op jit(solution)/shard_map/ppermute | solution.py:398
  6.2 1.4 %collective-permute-start = (bf16[4,96,128]{2,1,0:T(8,128)(2,1)S(1)}, bf16[4,96,128]{2,1,0:T(8,128)(2,1)S(1)}, u32[]{:S(2)}, u32[]{:S(2)}) collective-permute-start(bf16[4,96,128]{2,1,0:T(8,128)(2,1)S(1)} %get-tuple-element.26), channel_id=1, source_target_pairs={{0,1},{1,0},{2,3},{3,2},{4,5},{5,4},{6,7},{7,6},{8,9},{9,8},{10,11... | collective-permute-start | bytes 294920 | tf_op jit(solution)/shard_map/ppermute | solution.py:398
  7.6 4.3 %collective-permute-start.1 = (bf16[2,96,128]{2,1,0:T(8,128)(2,1)S(1)}, bf16[2,96,128]{2,1,0:T(8,128)(2,1)S(1)}, u32[]{:S(2)}, u32[]{:S(2)}) collective-permute-start(bf16[2,96,128]{2,1,0:T(8,128)(2,1)S(1)} %get-tuple-element.28), channel_id=1, source_target_pairs={{0,2},{2,0},{8,10},{10,8},{1,3},{3,1},{9,11},{11,9},{4,6},{6,4},{1... | collective-permute-start | bytes 147464 | tf_op jit(solution)/shard_map/ppermute | solution.py:398
  9.2 4.1 %collective-permute-start.2 = (bf16[2,96,128]{2,1,0:T(8,128)(2,1)S(1)}, bf16[2,96,128]{2,1,0:T(8,128)(2,1)S(1)}, u32[]{:S(2)}, u32[]{:S(2)}) collective-permute-start(bf16[2,96,128]{2,1,0:T(8,128)(2,1)S(1)} %get-tuple-element.29), channel_id=1, source_target_pairs={{0,8},{2,10},{8,0},{10,2},{1,9},{3,11},{9,1},{11,3},{4,12},{6,14},... | collective-permute-start | bytes 147464 | tf_op jit(solution)/shard_map/ppermute | solution.py:398
  10.7 5.2 %collective-permute-start.3 = (bf16[2,96,128]{2,1,0:T(8,128)(2,1)S(1)}, bf16[2,96,128]{2,1,0:T(8,128)(2,1)S(1)}, u32[]{:S(2)}, u32[]{:S(2)}) collective-permute-start(bf16[2,96,128]{2,1,0:T(8,128)(2,1)S(1)} %get-tuple-element.30), channel_id=1, source_target_pairs={{0,10},{2,8},{8,2},{10,0},{1,11},{3,9},{9,3},{11,1},{4,14},{6,12},... | collective-permute-start | bytes 147464 | tf_op jit(solution)/shard_map/ppermute | solution.py:398
  15.9 15.3 %copy-start.3 = (s32[8]{0:T(128)S(1)}, s32[8]{0:T(128)}, u32[]{:S(2)}) copy-start(s32[8]{0:T(128)} %clip_ref.1) | copy-start | bytes 100
  16.0 18.8 %collective-permute-start.7 = (bf16[1152,128]{1,0:T(8,128)(2,1)S(1)}, bf16[1152,128]{1,0:T(8,128)(2,1)S(1)}, u32[]{:S(2)}, u32[]{:S(2)}) collective-permute-start(bf16[1152,128]{1,0:T(8,128)(2,1)S(1)} %shard_map.43), channel_id=1, source_target_pairs={{0,16},{16,0},{1,17},{17,1},{2,18},{18,2},{3,19},{19,3},{4,20},{20... | collective-permute-start | bytes 884744 | tf_op jit(solution)/shard_map/ppermute | solution.py:398
  17.5 11.6 %collective-permute-start.4 = (bf16[256,128]{1,0:T(8,128)(2,1)S(1)}, bf16[256,128]{1,0:T(8,128)(2,1)S(1)}, u32[]{:S(2)}, u32[]{:S(2)}) collective-permute-start(bf16[256,128]{1,0:T(8,128)(2,1)S(1)} %get-tuple-element.34.refs_0_.refs_2_.refs_1_), channel_id=1, source_target_pairs={{0,4},{4,0},{1,5},{5,1},{2,6},{6,2},{3,7},{7,3},{8,12},{12,8},{9,1... | collective-permute-start | bytes 196616 | tf_op jit(solution)/shard_map/ppermute | solution.py:398
  17.7 12.8 %collective-permute-start.5 = (bf16[256,128]{1,0:T(8,128)(2,1)S(1)}, bf16[256,128]{1,0:T(8,128)(2,1)S(1)}, u32[]{:S(2)}, u32[]{:S(2)}) collective-permute-start(bf16[256,128]{1,0:T(8,128)(2,1)S(1)} %get-tuple-element.35.refs_1_.refs_3_), channel_id=1, source_target_pairs={{0,4},{4,0},{1,5},{5,1},{2,6},{6,2},{3,7},{7,3},{8,12},{12,8},{9,1... | collective-permute-start | bytes 196616 | tf_op jit(solution)/shard_map/ppermute | solution.py:398
  20.5 18.5 %collective-permute-start.14 = (bf16[64,1280]{1,0:T(8,128)(2,1)S(1)}, bf16[64,1280]{1,0:T(8,128)(2,1)S(1)}, u32[]{:S(2)}, u32[]{:S(2)}) collective-permute-start(bf16[64,1280]{1,0:T(8,128)(2,1)S(1)} %shard_map.47), channel_id=1, source_target_pairs={{0,6},{2,4},{4,2},{6,0},{1,7},{3,5},{5,3},{7,1},{8,14},{10,12},{12... | collective-permute-start | bytes 491528 | tf_op jit(solution)/shard_map/ppermute | solution.py:398
  29.1 4.3 %collective-permute-start.8 = (bf16[256,128]{1,0:T(8,128)(2,1)S(1)}, bf16[256,128]{1,0:T(8,128)(2,1)S(1)}, u32[]{:S(2)}, u32[]{:S(2)}) collective-permute-start(bf16[256,128]{1,0:T(8,128)(2,1)S(1)} %collective-permute-done.4.refs_4_), channel_id=1, source_target_pairs={{0,16},{16,0},{1,17},{17,1},{2,18},{18,2},{3,19},{19,3},{4,20},{20... | collective-permute-start | bytes 196616 | tf_op jit(solution)/shard_map/ppermute | solution.py:398
  30.5 4.3 %collective-permute-start.9 = (bf16[256,128]{1,0:T(8,128)(2,1)S(1)}, bf16[256,128]{1,0:T(8,128)(2,1)S(1)}, u32[]{:S(2)}, u32[]{:S(2)}) collective-permute-start(bf16[256,128]{1,0:T(8,128)(2,1)S(1)} %collective-permute-done.5.refs_5_), channel_id=1, source_target_pairs={{0,16},{16,0},{1,17},{17,1},{2,18},{18,2},{3,19},{19,3},{4,20},{20... | collective-permute-start | bytes 196616 | tf_op jit(solution)/shard_map/ppermute | solution.py:398
  32.0 7.7 %collective-permute-start.13 = (bf16[128,1280]{1,0:T(8,128)(2,1)S(1)}, bf16[128,1280]{1,0:T(8,128)(2,1)S(1)}, u32[]{:S(2)}, u32[]{:S(2)}) collective-permute-start(bf16[128,1280]{1,0:T(8,128)(2,1)S(1)} %shard_map.45), channel_id=1, source_target_pairs={{0,2},{2,0},{1,3},{3,1},{4,6},{6,4},{5,7},{7,5},{8,10},{10,8},{9,1... | collective-permute-start | bytes 983048 | tf_op jit(solution)/shard_map/ppermute | solution.py:398
  35.4 5.0 %collective-permute-start.10 = (bf16[256,128]{1,0:T(8,128)(2,1)S(1)}, bf16[256,128]{1,0:T(8,128)(2,1)S(1)}, u32[]{:S(2)}, u32[]{:S(2)}) collective-permute-start(bf16[256,128]{1,0:T(8,128)(2,1)S(1)} %shard_map.44.refs_1_.refs_0_), channel_id=1, source_target_pairs={{0,2},{2,0},{8,10},{10,8},{1,3},{3,1},{9,11},{11,9},{4,6},{6,4},{1... | collective-permute-start | bytes 196616 | tf_op jit(solution)/shard_map/ppermute | solution.py:398
  35.5 4.9 %collective-permute-start.11 = (bf16[256,128]{1,0:T(8,128)(2,1)S(1)}, bf16[256,128]{1,0:T(8,128)(2,1)S(1)}, u32[]{:S(2)}, u32[]{:S(2)}) collective-permute-start(bf16[256,128]{1,0:T(8,128)(2,1)S(1)} %shard_map.44.refs_1_.refs_0_), channel_id=1, source_target_pairs={{0,8},{2,10},{8,0},{10,2},{1,9},{3,11},{9,1},{11,3},{4,12},{6,14},... | collective-permute-start | bytes 196616 | tf_op jit(solution)/shard_map/ppermute | solution.py:398
  36.1 6.1 %collective-permute-start.12 = (bf16[256,128]{1,0:T(8,128)(2,1)S(1)}, bf16[256,128]{1,0:T(8,128)(2,1)S(1)}, u32[]{:S(2)}, u32[]{:S(2)}) collective-permute-start(bf16[256,128]{1,0:T(8,128)(2,1)S(1)} %shard_map.44.refs_1_.refs_0_), channel_id=1, source_target_pairs={{0,10},{2,8},{8,2},{10,0},{1,11},{3,9},{9,3},{11,1},{4,14},{6,12},... | collective-permute-start | bytes 196616 | tf_op jit(solution)/shard_map/ppermute | solution.py:398
  39.0 5.3 %copy-start.1 = (bf16[128,5120]{1,0:T(8,128)(2,1)S(1)}, bf16[128,5120]{1,0:T(8,128)(2,1)}, u32[]{:S(2)}) copy-start(bf16[128,5120]{1,0:T(8,128)(2,1)} %refs_4_.1) | copy-start | bytes 3932164
  39.0 5.3 %collective-permute-start.15 = (bf16[64,1280]{1,0:T(8,128)(2,1)S(1)}, bf16[64,1280]{1,0:T(8,128)(2,1)S(1)}, u32[]{:S(2)}, u32[]{:S(2)}) collective-permute-start(bf16[64,1280]{1,0:T(8,128)(2,1)S(1)} %shard_map.48.refs_8_), channel_id=1, source_target_pairs={{0,16},{16,0},{1,17},{17,1},{2,18},{18,2},{3,19},{19,3},{4,20},{20... | collective-permute-start | bytes 491528 | tf_op jit(solution)/shard_map/ppermute | solution.py:398
  45.6 1.7 %collective-permute-start.16 = (bf16[4,32,1280]{2,1,0:T(8,128)(2,1)S(1)}, bf16[4,32,1280]{2,1,0:T(8,128)(2,1)S(1)}, u32[]{:S(2)}, u32[]{:S(2)}) collective-permute-start(bf16[4,32,1280]{2,1,0:T(8,128)(2,1)S(1)} %get-tuple-element.40), channel_id=1, source_target_pairs={{0,1},{1,0},{2,3},{3,2},{4,5},{5,4},{6,7},{7,6},{8,9},{9,8},{10,11... | collective-permute-start | bytes 983048 | tf_op jit(solution)/shard_map/ppermute | solution.py:398
  47.4 5.1 %collective-permute-start.17 = (bf16[32,1280]{1,0:T(8,128)(2,1)S(1)}, bf16[32,1280]{1,0:T(8,128)(2,1)S(1)}, u32[]{:S(2)}, u32[]{:S(2)}) collective-permute-start(bf16[32,1280]{1,0:T(8,128)(2,1)S(1)} %get-tuple-element.42), channel_id=1, source_target_pairs={{0,2},{2,0},{8,10},{10,8},{1,3},{3,1},{9,11},{11,9},{4,6},{6,4},{1... | collective-permute-start | bytes 245768 | tf_op jit(solution)/shard_map/ppermute | solution.py:398
  47.5 6.2 %collective-permute-start.18 = (bf16[32,1280]{1,0:T(8,128)(2,1)S(1)}, bf16[32,1280]{1,0:T(8,128)(2,1)S(1)}, u32[]{:S(2)}, u32[]{:S(2)}) collective-permute-start(bf16[32,1280]{1,0:T(8,128)(2,1)S(1)} %get-tuple-element.43), channel_id=1, source_target_pairs={{0,8},{2,10},{8,0},{10,2},{1,9},{3,11},{9,1},{11,3},{4,12},{6,14},... | collective-permute-start | bytes 245768 | tf_op jit(solution)/shard_map/ppermute | solution.py:398
  48.1 5.7 %collective-permute-start.19 = (bf16[32,1280]{1,0:T(8,128)(2,1)S(1)}, bf16[32,1280]{1,0:T(8,128)(2,1)S(1)}, u32[]{:S(2)}, u32[]{:S(2)}) collective-permute-start(bf16[32,1280]{1,0:T(8,128)(2,1)S(1)} %get-tuple-element.44), channel_id=1, source_target_pairs={{0,10},{2,8},{8,2},{10,0},{1,11},{3,9},{9,3},{11,1},{4,14},{6,12},... | collective-permute-start | bytes 245768 | tf_op jit(solution)/shard_map/ppermute | solution.py:398

commit v16 on v15

--- a/solution.py
+++ b/solution.py
@@ -17,6 +17,7 @@
 ANY = pl.BlockSpec(memory_space=pl.ANY)
 PARAMS = pltpu.CompilerParams(vmem_limit_bytes=48 * 1024 * 1024)
 AHEAD = pl.CostEstimate(flops=20_000_000_000, bytes_accessed=1_000_000, transcendentals=0)
+FIRST = pl.CostEstimate(flops=1_000_000_000, bytes_accessed=1_000_000, transcendentals=0)
 SOON = pl.CostEstimate(flops=6_000_000_000, bytes_accessed=1_000_000, transcendentals=0)
 
 
@@ -79,28 +80,42 @@
     )
 
 
-def pieces_kernel(at_ref, x_ref, far_ref, corner_ref, near_ref):
-    half, cols = corner_ref.shape
-    rows = rows_at(at_ref[0], half)
-    count = cols // LANES
+def blocks_kernel(at_ref, x_ref, out_ref):
+    half = x_ref.shape[0] // 2
+    count = out_ref.shape[0] // half
     for j in range(count):
-        far_ref[j * half:(j + 1) * half, :] = x_ref[rows, rows_at(at_ref[1] * count + j, LANES)]
-    corner_ref[...] = x_ref[rows, rows_at(at_ref[2], cols)]
-    near_ref[...] = x_ref[:, rows_at(at_ref[2], cols)]
-
-
-def pieces(x, half, first_at, second_at, cols):
+        out_ref[j * half:(j + 1) * half, :] = x_ref[
+            rows_at(at_ref[0], half), rows_at(at_ref[1] * count + j, LANES)
+        ]
+
+
+def blocks(x, half, at, cols):
+    like = jax.ShapeDtypeStruct((cols // LANES * (x.shape[0] // 2), LANES), x.dtype)
+    return pl.pallas_call(
+        blocks_kernel,
+        out_shape=like,
+        in_specs=[SMEM, VMEM],
+        out_specs=VMEM,
+        compiler_params=PARAMS,
+    )(index_array(half, at), x)
+
+
+def pieces_kernel(at_ref, x_ref, *refs):
+    half_ref, all_ref = refs[-2:]
+    half, cols = half_ref.shape
+    half_ref[...] = x_ref[rows_at(at_ref[0], half), rows_at(at_ref[1], cols)]
+    all_ref[...] = x_ref[:, rows_at(at_ref[1], cols)]
+
+
+def pieces(x, half, at, cols, *first):
+    depth = x.shape[0]
     return pl.pallas_call(
         pieces_kernel,
-        out_shape=(
-            jax.ShapeDtypeStruct((cols // LANES * (x.shape[0] // 2), LANES), x.dtype),
-            jax.ShapeDtypeStruct((x.shape[0] // 2, cols), x.dtype),
-            jax.ShapeDtypeStruct((x.shape[0], cols), x.dtype),
-        ),
-        in_specs=[SMEM, VMEM],
-        out_specs=(VMEM, VMEM, VMEM),
-        compiler_params=PARAMS,
-    )(index_array(half, first_at, second_at), x)
+        out_shape=[jax.ShapeDtypeStruct((rows, cols), x.dtype) for rows in (depth // 2, depth)],
+        in_specs=[SMEM, VMEM] + [ANY] * len(first),
+        out_specs=[VMEM, VMEM],
+        compiler_params=PARAMS,
+    )(index_array(half, at), x, *first)
 
 
 def lane_kernel(head_dim, core_ref, x_ref, mine_ref, theirs_ref):
@@ -307,6 +322,7 @@
         in_specs=[VMEM] * (1 + len(mask_of) + len(arrays)),
         out_specs=VMEM,
         compiler_params=PARAMS,
+        cost_estimate=FIRST,
     )(q, *mask_of, *arrays)
 
 
@@ -411,19 +427,18 @@
     mine, theirs = x * 2 + zl, x * 2 + 1 - zl
     row, half = zh * 2 + zl, head_dim // 2
 
-    w_far, w_corner, w_near = pieces(w_out, y, mine, theirs, cols)
-    far = after(xor(w_far, ("zh",), 1), cost=AHEAD)
+    far = after(xor(blocks(w_out, y, mine, cols), ("zh",), 1), cost=AHEAD)
     kept, given = lanes(qkv, core, head_dim)
     shared = swap_all(deal(kept, xor(given, ("core",), 1), place), quarter)
     q, k, v = sort(shared, place)
     k_far, v_far = xor(k, ("zh",), 1), xor(v, ("zh",), 1)
     near = xor(join(k, v, far), ("y",), 1)
-    corner = xor(after(w_corner, k), ("zh", "zl"), 3)
-    w_next = xor(after(w_near, k), ("zl",), 1)
+    bases = [y * 2 * FRB, (1 - y) * 2 * FRB]
+    mask_of = masks(bases, 4 * tok, tok, 8 * tok, after(frame_clip, k))
+    w_corner, w_near = pieces(w_out, y, theirs, cols, mask_of[0])
+    corner = xor(w_corner, ("zh", "zl"), 3)
+    w_next = xor(w_near, ("zl",), 1)
     kvs = [(k, v), (k_far, v_far), near, (xor(k_far, ("y",), 1), xor(v_far, ("y",), 1))]
-
-    bases = [y * 2 * FRB, (1 - y) * 2 * FRB]
-    mask_of = masks(bases, 4 * tok, tok, 8 * tok, frame_clip)
     attn = attention(q, kvs, mask_of, [0, 0, 1, 1], head_dim)
     corner = after(corner, attn, cost=SOON)
     corner_rest = xor(corner, ("y",), 1)

time: 54.6 us -> 55.7 us (1.020)
  local copies, waits for them, and re-layouts: 1.42 us -> 3.71 us
  waiting for transfers between devices: 24.5 us -> 22.8 us
    unnamed x8 -> x11, local copies, waits for them, and re-layouts: 1.33 us -> 3.63 us
    ppermute x20, waiting for transfers between devices: 24.5 us -> 22.8 us  [xor(): return lax.ppermute(x, axis, [(i, i ^ by) for i in range(size)])]
    pallas_call x1 -> x2, Pallas kernels: 0.62 us -> 1.17 us  [the longest x1 0.59 us: blocks(): pl.pallas_call(blocks_kernel, out_shape=like, in_specs=[SMEM, VMEM], out_...]
  transfers between devices with their start and end apart: 20 -> 20, of which waited for: 15 -> 13; matrix products, arithmetic and copies ran while one was open for 0% -> 0% of each run, Pallas kernels for 3% -> 4%
where the time goes in v16:
time: 55.7 us; the launch traced here: 55.5 us
  starting transfers between devices  24 us (43%)
  waiting for transfers between devices  22.8 us (41%)
  Pallas kernels  4.71 us (8%)
  local copies, waits for them, and re-layouts  3.71 us (7%)
    ppermute x20, starting transfers between devices, xor(): return lax.ppermute(x, axis, [(i, i ^ by) for i in range(size)])  24 us
    ppermute x20, waiting for transfers between devices, xor(): return lax.ppermute(x, axis, [(i, i ^ by) for i in range(size)])  22.8 us
    unnamed x11, local copies, waits for them, and re-layouts  3.63 us
    pallas_call x1, Pallas kernels, project(): pl.pallas_call(functools.partial(project_kernel, blks, sizes), out_shape=...  1.26 us
  transfers between devices with their start and end apart: 20, of which 13 were waited for; matrix products, arithmetic and copies ran while one was open for 0% of the time, Pallas kernels for 4%

profile of v16, /device:TPU:0, one launch (start us, length us, event | category | flops | bytes accessed | tf_op | source)
XLA Modules:
  0.0 55.5 jit_solution(3999435916895090424)
XLA Ops:
  0.0 0.7 %copy.13.refs_0_ = s32[8]{0:T(128)S(1)} copy(s32[8]{0:T(128)} %param.4) | data formatting | bytes 64
  0.7 0.1 pad_add_fusion.1.at_ref
  0.7 0.0 copy-start
  0.7 1.3 %copy-done = bf16[128,5120]{1,0:T(8,128)(2,1)S(1)} copy-done((bf16[128,5120]{1,0:T(8,128)(2,1)S(1)}, bf16[128,5120]{1,0:T(8,128)(2,1)}, u32[]{:S(2)}) %copy-start) | copy-done | bytes 1310744
  2.0 0.0 copy-start.2
  2.1 0.6 %shard_map.42 = bf16[640,128]{1,0:T(8,128)(2,1)S(1)} custom-call(s32[2]{0:T(128)S(1)} %pad_add_fusion.1.at_ref, bf16[128,5120]{1,0:T(8,128)(2,1)S(1)} %copy-done), custom_call_target="tpu_custom_call" | custom-call | tf_op jit(solution)/shard_map/pallas_call | solution.py:94
  2.6 4.1 %collective-permute-start.6 = (bf16[640,128]{1,0:T(8,128)(2,1)S(1)}, bf16[640,128]{1,0:T(8,128)(2,1)S(1)}, u32[]{:S(2)}, u32[]{:S(2)}) collective-permute-start(bf16[640,128]{1,0:T(8,128)(2,1)S(1)} %shard_map.42), channel_id=1, source_target_pairs={{0,4},{4,0},{1,5},{5,1},{2,6},{6,2},{3,7},{7,3},{8,12},{12,8},{9,1... | collective-permute-start | bytes 491528 | tf_op jit(solution)/shard_map/ppermute | solution.py:414
  6.8 0.0 copy-done.2
  6.8 0.1 shard_map.37
  6.8 0.1 collective-permute-start
  6.9 1.3 %collective-permute-done.got_ref = bf16[4,96,128]{2,1,0:T(8,128)(2,1)S(1)} collective-permute-done((bf16[4,96,128]{2,1,0:T(8,128)(2,1)S(1)}, bf16[4,96,128]{2,1,0:T(8,128)(2,1)S(1)}, u32[]{:S(2)}, u32[]{:S(2)}) %collective-permute-start) | collective-permute-done | bytes 98336 | tf_op jit(solution)/shard_map/ppermute | solution.py:414
  8.2 1.6 %collective-permute-start.1 = (bf16[2,96,128]{2,1,0:T(8,128)(2,1)S(1)}, bf16[2,96,128]{2,1,0:T(8,128)(2,1)S(1)}, u32[]{:S(2)}, u32[]{:S(2)}) collective-permute-start(bf16[2,96,128]{2,1,0:T(8,128)(2,1)S(1)} %get-tuple-element.27), channel_id=1, source_target_pairs={{0,2},{2,0},{8,10},{10,8},{1,3},{3,1},{9,11},{11,9},{4,6},{6,4},{1... | collective-permute-start | bytes 147464 | tf_op jit(solution)/shard_map/ppermute | solution.py:414
  9.8 1.5 %collective-permute-start.2 = (bf16[2,96,128]{2,1,0:T(8,128)(2,1)S(1)}, bf16[2,96,128]{2,1,0:T(8,128)(2,1)S(1)}, u32[]{:S(2)}, u32[]{:S(2)}) collective-permute-start(bf16[2,96,128]{2,1,0:T(8,128)(2,1)S(1)} %get-tuple-element.28), channel_id=1, source_target_pairs={{0,8},{2,10},{8,0},{10,2},{1,9},{3,11},{9,1},{11,3},{4,12},{6,14},... | collective-permute-start | bytes 147464 | tf_op jit(solution)/shard_map/ppermute | solution.py:414
  11.3 0.4 collective-permute-start.3
  11.7 0.8 %collective-permute-done.1.refs_1_ = bf16[2,96,128]{2,1,0:T(8,128)(2,1)S(1)} collective-permute-done((bf16[2,96,128]{2,1,0:T(8,128)(2,1)S(1)}, bf16[2,96,128]{2,1,0:T(8,128)(2,1)S(1)}, u32[]{:S(2)}, u32[]{:S(2)}) %collective-permute-start.1) | collective-permute-done | bytes 49184 | tf_op jit(solution)/shard_map/ppermute | solution.py:414
  12.5 1.4 %collective-permute-done.2.refs_2_ = bf16[2,96,128]{2,1,0:T(8,128)(2,1)S(1)} collective-permute-done((bf16[2,96,128]{2,1,0:T(8,128)(2,1)S(1)}, bf16[2,96,128]{2,1,0:T(8,128)(2,1)S(1)}, u32[]{:S(2)}, u32[]{:S(2)}) %collective-permute-start.2) | collective-permute-done | bytes 49184 | tf_op jit(solution)/shard_map/ppermute | solution.py:414
  13.9 2.6 %collective-permute-done.3.refs_3_ = bf16[2,96,128]{2,1,0:T(8,128)(2,1)S(1)} collective-permute-done((bf16[2,96,128]{2,1,0:T(8,128)(2,1)S(1)}, bf16[2,96,128]{2,1,0:T(8,128)(2,1)S(1)}, u32[]{:S(2)}, u32[]{:S(2)}) %collective-permute-start.3) | collective-permute-done | bytes 49184 | tf_op jit(solution)/shard_map/ppermute | solution.py:414
  16.5 0.0 collective-permute-done.6.refs_0_
  16.5 0.0 copy-start.1
  16.6 1.6 %collective-permute-start.7 = (bf16[1152,128]{1,0:T(8,128)(2,1)S(1)}, bf16[1152,128]{1,0:T(8,128)(2,1)S(1)}, u32[]{:S(2)}, u32[]{:S(2)}) collective-permute-start(bf16[1152,128]{1,0:T(8,128)(2,1)S(1)} %shard_map.44), channel_id=1, source_target_pairs={{0,16},{16,0},{1,17},{17,1},{2,18},{18,2},{3,19},{19,3},{4,20},{20... | collective-permute-start | bytes 884744 | tf_op jit(solution)/shard_map/ppermute | solution.py:414
  18.2 0.1 pad_add_fusion.2.at_ref
  18.2 0.2 collective-permute-start.5
  18.4 2.8 %collective-permute-start.4 = (bf16[256,128]{1,0:T(8,128)(2,1)S(1)}, bf16[256,128]{1,0:T(8,128)(2,1)S(1)}, u32[]{:S(2)}, u32[]{:S(2)}) collective-permute-start(bf16[256,128]{1,0:T(8,128)(2,1)S(1)} %get-tuple-element.31.refs_1_.refs_0_.refs_2_), channel_id=1, source_target_pairs={{0,4},{4,0},{1,5},{5,1},{2,6},{6,2},{3,7},{7,3},{8,12},{12,8},{9,1... | collective-permute-start | bytes 196616 | tf_op jit(solution)/shard_map/ppermute | solution.py:414
  21.2 0.1 pad_add_fusion.base_ref
  21.2 0.7 %shard_map.41 = (f32[256,256]{1,0:T(8,128)S(1)}, f32[256,256]{1,0:T(8,128)S(1)}) custom-call(s32[2]{0:T(128)S(1)} %pad_add_fusion.base_ref, s32[8]{0:T(128)S(1)} %shard_map.40.clip_ref), custom_call_target="tpu_custom_call" | custom-call | tf_op jit(solution)/shard_map/pallas_call | solution.py:259
  22.0 0.0 copy-start.3
  22.0 0.7 %copy-done.3 = f32[256,256]{1,0:T(8,128)} copy-done((f32[256,256]{1,0:T(8,128)}, f32[256,256]{1,0:T(8,128)S(1)}, u32[]{:S(2)}) %copy-start.3) | copy-done | bytes 262168
  22.7 0.0 copy-done.1
  22.7 0.6 %shard_map.46 = (bf16[64,1280]{1,0:T(8,128)(2,1)S(1)}, bf16[128,1280]{1,0:T(8,128)(2,1)S(1)}) custom-call(s32[2]{0:T(128)S(1)} %pad_add_fusion.2.at_ref, bf16[128,5120]{1,0:T(8,128)(2,1)S(1)} %copy-done.1, f32[256,256]{1,0:T(8,128)S(1)} %get-tuple-element.32.refs_0_), custom_call_target="tpu_custom_call" | custom-call | tf_op jit(solution)/shard_map/pallas_call | solution.py:112
  23.3 3.0 %collective-permute-start.14 = (bf16[64,1280]{1,0:T(8,128)(2,1)S(1)}, bf16[64,1280]{1,0:T(8,128)(2,1)S(1)}, u32[]{:S(2)}, u32[]{:S(2)}) collective-permute-start(bf16[64,1280]{1,0:T(8,128)(2,1)S(1)} %get-tuple-element.36), channel_id=1, source_target_pairs={{0,6},{2,4},{4,2},{6,0},{1,7},{3,5},{5,3},{7,1},{8,14},{10,12},{12... | collective-permute-start | bytes 491528 | tf_op jit(solution)/shard_map/ppermute | solution.py:414
  26.3 0.0 collective-permute-done.5.refs_5_
  26.3 0.5 collective-permute-start.9
  26.8 3.0 %collective-permute-done.4.refs_4_ = bf16[256,128]{1,0:T(8,128)(2,1)S(1)} collective-permute-done((bf16[256,128]{1,0:T(8,128)(2,1)S(1)}, bf16[256,128]{1,0:T(8,128)(2,1)S(1)}, u32[]{:S(2)}, u32[]{:S(2)}) %collective-permute-start.4) | collective-permute-done | bytes 65568 | tf_op jit(solution)/shard_map/ppermute | solution.py:414
  29.8 0.5 collective-permute-start.8
  30.3 0.1 stack.59.at_ref
  30.3 0.0 collective-permute-start.13
  30.4 0.2 collective-permute-done.9.refs_8_
  30.5 3.5 %collective-permute-done.8.refs_7_ = bf16[256,128]{1,0:T(8,128)(2,1)S(1)} collective-permute-done((bf16[256,128]{1,0:T(8,128)(2,1)S(1)}, bf16[256,128]{1,0:T(8,128)(2,1)S(1)}, u32[]{:S(2)}, u32[]{:S(2)}) %collective-permute-start.8) | collective-permute-done | bytes 65568 | tf_op jit(solution)/shard_map/ppermute | solution.py:414
  34.0 0.0 collective-permute-done.7.refs_6_.refs_7_
  34.0 0.0 copy-start.4
  34.0 0.9 %copy-done.4 = f32[256,256]{1,0:T(8,128)S(1)} copy-done((f32[256,256]{1,0:T(8,128)S(1)}, f32[256,256]{1,0:T(8,128)}, u32[]{:S(2)}) %copy-start.4) | copy-done | bytes 262168
  35.0 0.6 %shard_map.45.refs_1_.refs_0_ = bf16[256,128]{1,0:T(8,128)(2,1)S(1)} custom-call(bf16[256,128]{1,0:T(8,128)(2,1)S(1)} %get-tuple-element.30.q_ref, f32[256,256]{1,0:T(8,128)S(1)} %get-tuple-element.32.refs_0_, f32[256,256]{1,0:T(8,128)S(1)} %copy-done.4, bf16[256,128]{1,0:T(8,128)(2,1)S(1)} %get-tuple-element.31.refs_1_.refs_0_.refs_2_, ...), custom_call_target="tpu_custom_call" | custom-call | flops 1000000000 | bytes 1000000 | tf_op jit(solution)/shard_map/pallas_call | solution.py:319
  35.6 0.1 collective-permute-start.12
  35.7 1.5 %collective-permute-start.11 = (bf16[256,128]{1,0:T(8,128)(2,1)S(1)}, bf16[256,128]{1,0:T(8,128)(2,1)S(1)}, u32[]{:S(2)}, u32[]{:S(2)}) collective-permute-start(bf16[256,128]{1,0:T(8,128)(2,1)S(1)} %shard_map.45.refs_1_.refs_0_), channel_id=1, source_target_pairs={{0,8},{2,10},{8,0},{10,2},{1,9},{3,11},{9,1},{11,3},{4,12},{6,14},... | collective-permute-start | bytes 196616 | tf_op jit(solution)/shard_map/ppermute | solution.py:414
  37.2 1.9 %collective-permute-start.10 = (bf16[256,128]{1,0:T(8,128)(2,1)S(1)}, bf16[256,128]{1,0:T(8,128)(2,1)S(1)}, u32[]{:S(2)}, u32[]{:S(2)}) collective-permute-start(bf16[256,128]{1,0:T(8,128)(2,1)S(1)} %shard_map.45.refs_1_.refs_0_), channel_id=1, source_target_pairs={{0,2},{2,0},{8,10},{10,8},{1,3},{3,1},{9,11},{11,9},{4,6},{6,4},{1... | collective-permute-start | bytes 196616 | tf_op jit(solution)/shard_map/ppermute | solution.py:414
  39.2 0.0 collective-permute-done.14.refs_0_
  39.2 0.5 collective-permute-start.15
  39.7 0.0 collective-permute-done.13.refs_0_
  39.7 1.2 %collective-permute-done.12.refs_3_ = bf16[256,128]{1,0:T(8,128)(2,1)S(1)} collective-permute-done((bf16[256,128]{1,0:T(8,128)(2,1)S(1)}, bf16[256,128]{1,0:T(8,128)(2,1)S(1)}, u32[]{:S(2)}, u32[]{:S(2)}) %collective-permute-start.12) | collective-permute-done | bytes 65568 | tf_op jit(solution)/shard_map/ppermute | solution.py:414
  40.8 0.0 collective-permute-done.11.refs_2_
  40.8 0.7 %collective-permute-done.10.refs_1_ = bf16[256,128]{1,0:T(8,128)(2,1)S(1)} collective-permute-done((bf16[256,128]{1,0:T(8,128)(2,1)S(1)}, bf16[256,128]{1,0:T(8,128)(2,1)S(1)}, u32[]{:S(2)}, u32[]{:S(2)}) %collective-permute-start.10) | collective-permute-done | bytes 65568 | tf_op jit(solution)/shard_map/ppermute | solution.py:414
  41.6 2.9 %collective-permute-done.15.refs_9_ = bf16[64,1280]{1,0:T(8,128)(2,1)S(1)} collective-permute-done((bf16[64,1280]{1,0:T(8,128)(2,1)S(1)}, bf16[64,1280]{1,0:T(8,128)(2,1)S(1)}, u32[]{:S(2)}, u32[]{:S(2)}) %collective-permute-start.15) | collective-permute-done | bytes 163872 | tf_op jit(solution)/shard_map/ppermute | solution.py:414
  44.5 1.3 %shard_map.49 = (bf16[4,32,1280]{2,1,0:T(8,128)(2,1)S(1)}, bf16[4,32,1280]{2,1,0:T(8,128)(2,1)S(1)}) custom-call(s32[6]{0:T(128)S(1)} %stack.59.at_ref, s32[1]{0:T(128)} %bitcast.place_ref, bf16[256,128]{1,0:T(8,128)(2,1)S(1)} %shard_map.45.refs_1_.refs_0_, bf16[256,128]{1,0:T(8,128)(2,1)S(1)} %collective-permute-done.10.refs_1_, ...), custom_call_target="tpu_custom_call" | custom-call | tf_op jit(solution)/shard_map/pallas_call | solution.py:363
  45.8 0.1 collective-permute-start.16
  45.8 1.6 %collective-permute-done.16.y_ref = bf16[4,32,1280]{2,1,0:T(8,128)(2,1)S(1)} collective-permute-done((bf16[4,32,1280]{2,1,0:T(8,128)(2,1)S(1)}, bf16[4,32,1280]{2,1,0:T(8,128)(2,1)S(1)}, u32[]{:S(2)}, u32[]{:S(2)}) %collective-permute-start.16) | collective-permute-done | bytes 327712 | tf_op jit(solution)/shard_map/ppermute | solution.py:414
  47.5 0.1 shard_map.50
  47.5 0.2 collective-permute-start.17
  47.7 1.5 %collective-permute-start.18 = (bf16[32,1280]{1,0:T(8,128)(2,1)S(1)}, bf16[32,1280]{1,0:T(8,128)(2,1)S(1)}, u32[]{:S(2)}, u32[]{:S(2)}) collective-permute-start(bf16[32,1280]{1,0:T(8,128)(2,1)S(1)} %get-tuple-element.41), channel_id=1, source_target_pairs={{0,8},{2,10},{8,0},{10,2},{1,9},{3,11},{9,1},{11,3},{4,12},{6,14},... | collective-permute-start | bytes 245768 | tf_op jit(solution)/shard_map/ppermute | solution.py:414
  49.2 1.9 %collective-permute-start.19 = (bf16[32,1280]{1,0:T(8,128)(2,1)S(1)}, bf16[32,1280]{1,0:T(8,128)(2,1)S(1)}, u32[]{:S(2)}, u32[]{:S(2)}) collective-permute-start(bf16[32,1280]{1,0:T(8,128)(2,1)S(1)} %get-tuple-element.42), channel_id=1, source_target_pairs={{0,10},{2,8},{8,2},{10,0},{1,11},{3,9},{9,3},{11,1},{4,14},{6,12},... | collective-permute-start | bytes 245768 | tf_op jit(solution)/shard_map/ppermute | solution.py:414
  51.1 1.6 %collective-permute-done.17.refs_1_ = bf16[32,1280]{1,0:T(8,128)(2,1)S(1)} collective-permute-done((bf16[32,1280]{1,0:T(8,128)(2,1)S(1)}, bf16[32,1280]{1,0:T(8,128)(2,1)S(1)}, u32[]{:S(2)}, u32[]{:S(2)}) %collective-permute-start.17) | collective-permute-done | bytes 81952 | tf_op jit(solution)/shard_map/ppermute | solution.py:414
  52.7 0.0 collective-permute-done.18.refs_2_
  52.7 2.1 %collective-permute-done.19.refs_3_ = bf16[32,1280]{1,0:T(8,128)(2,1)S(1)} collective-permute-done((bf16[32,1280]{1,0:T(8,128)(2,1)S(1)}, bf16[32,1280]{1,0:T(8,128)(2,1)S(1)}, u32[]{:S(2)}, u32[]{:S(2)}) %collective-permute-start.19) | collective-permute-done | bytes 81952 | tf_op jit(solution)/shard_map/ppermute | solution.py:414
  54.8 0.8 %shard_map.51 = bf16[32,5120]{1,0:T(8,128)(2,1)} custom-call(s32[1]{0:T(128)} %bitcast.place_ref, bf16[32,1280]{1,0:T(8,128)(2,1)S(1)} %get-tuple-element.39.refs_0_, bf16[32,1280]{1,0:T(8,128)(2,1)S(1)} %collective-permute-done.17.refs_1_, bf16[32,1280]{1,0:T(8,128)(2,1)S(1)} %collective-permute-done.18.refs_2_, ...), custom_call_target="tpu_custom_call" | custom-call | tf_op jit(solution)/shard_map/pallas_call | solution.py:403
  (7 shorter events, 0.1 us)
Async XLA Ops:
  0.7 1.3 %copy-start = (bf16[128,5120]{1,0:T(8,128)(2,1)S(1)}, bf16[128,5120]{1,0:T(8,128)(2,1)}, u32[]{:S(2)}) copy-start(bf16[128,5120]{1,0:T(8,128)(2,1)} %refs_4_.1) | copy-start | bytes 3932164
  2.0 4.7 %copy-start.2 = (bf16[3,32,1024]{2,1,0:T(8,128)(2,1)S(1)}, bf16[3,32,1024]{2,1,0:T(8,128)(2,1)}, u32[]{:S(2)}) copy-start(bf16[3,32,1024]{2,1,0:T(8,128)(2,1)} %x_ref.3) | copy-start | bytes 589828
  2.6 13.9 %collective-permute-start.6 = (bf16[640,128]{1,0:T(8,128)(2,1)S(1)}, bf16[640,128]{1,0:T(8,128)(2,1)S(1)}, u32[]{:S(2)}, u32[]{:S(2)}) collective-permute-start(bf16[640,128]{1,0:T(8,128)(2,1)S(1)} %shard_map.42), channel_id=1, source_target_pairs={{0,4},{4,0},{1,5},{5,1},{2,6},{6,2},{3,7},{7,3},{8,12},{12,8},{9,1... | collective-permute-start | bytes 491528 | tf_op jit(solution)/shard_map/ppermute | solution.py:414
  6.8 1.4 %collective-permute-start = (bf16[4,96,128]{2,1,0:T(8,128)(2,1)S(1)}, bf16[4,96,128]{2,1,0:T(8,128)(2,1)S(1)}, u32[]{:S(2)}, u32[]{:S(2)}) collective-permute-start(bf16[4,96,128]{2,1,0:T(8,128)(2,1)S(1)} %get-tuple-element.25), channel_id=1, source_target_pairs={{0,1},{1,0},{2,3},{3,2},{4,5},{5,4},{6,7},{7,6},{8,9},{9,8},{10,11... | collective-permute-start | bytes 294920 | tf_op jit(solution)/shard_map/ppermute | solution.py:414
  8.2 4.3 %collective-permute-start.1 = (bf16[2,96,128]{2,1,0:T(8,128)(2,1)S(1)}, bf16[2,96,128]{2,1,0:T(8,128)(2,1)S(1)}, u32[]{:S(2)}, u32[]{:S(2)}) collective-permute-start(bf16[2,96,128]{2,1,0:T(8,128)(2,1)S(1)} %get-tuple-element.27), channel_id=1, source_target_pairs={{0,2},{2,0},{8,10},{10,8},{1,3},{3,1},{9,11},{11,9},{4,6},{6,4},{1... | collective-permute-start | bytes 147464 | tf_op jit(solution)/shard_map/ppermute | solution.py:414
  9.8 4.1 %collective-permute-start.2 = (bf16[2,96,128]{2,1,0:T(8,128)(2,1)S(1)}, bf16[2,96,128]{2,1,0:T(8,128)(2,1)S(1)}, u32[]{:S(2)}, u32[]{:S(2)}) collective-permute-start(bf16[2,96,128]{2,1,0:T(8,128)(2,1)S(1)} %get-tuple-element.28), channel_id=1, source_target_pairs={{0,8},{2,10},{8,0},{10,2},{1,9},{3,11},{9,1},{11,3},{4,12},{6,14},... | collective-permute-start | bytes 147464 | tf_op jit(solution)/shard_map/ppermute | solution.py:414
  11.3 5.2 %collective-permute-start.3 = (bf16[2,96,128]{2,1,0:T(8,128)(2,1)S(1)}, bf16[2,96,128]{2,1,0:T(8,128)(2,1)S(1)}, u32[]{:S(2)}, u32[]{:S(2)}) collective-permute-start(bf16[2,96,128]{2,1,0:T(8,128)(2,1)S(1)} %get-tuple-element.29), channel_id=1, source_target_pairs={{0,10},{2,8},{8,2},{10,0},{1,11},{3,9},{9,3},{11,1},{4,14},{6,12},... | collective-permute-start | bytes 147464 | tf_op jit(solution)/shard_map/ppermute | solution.py:414
  16.5 6.1 %copy-start.1 = (bf16[128,5120]{1,0:T(8,128)(2,1)S(1)}, bf16[128,5120]{1,0:T(8,128)(2,1)}, u32[]{:S(2)}) copy-start(bf16[128,5120]{1,0:T(8,128)(2,1)} %refs_4_.1) | copy-start | bytes 3932164
  16.6 17.4 %collective-permute-start.7 = (bf16[1152,128]{1,0:T(8,128)(2,1)S(1)}, bf16[1152,128]{1,0:T(8,128)(2,1)S(1)}, u32[]{:S(2)}, u32[]{:S(2)}) collective-permute-start(bf16[1152,128]{1,0:T(8,128)(2,1)S(1)} %shard_map.44), channel_id=1, source_target_pairs={{0,16},{16,0},{1,17},{17,1},{2,18},{18,2},{3,19},{19,3},{4,20},{20... | collective-permute-start | bytes 884744 | tf_op jit(solution)/shard_map/ppermute | solution.py:414
  18.2 8.0 %collective-permute-start.5 = (bf16[256,128]{1,0:T(8,128)(2,1)S(1)}, bf16[256,128]{1,0:T(8,128)(2,1)S(1)}, u32[]{:S(2)}, u32[]{:S(2)}) collective-permute-start(bf16[256,128]{1,0:T(8,128)(2,1)S(1)} %get-tuple-element.34.refs_1_.refs_3_), channel_id=1, source_target_pairs={{0,4},{4,0},{1,5},{5,1},{2,6},{6,2},{3,7},{7,3},{8,12},{12,8},{9,1... | collective-permute-start | bytes 196616 | tf_op jit(solution)/shard_map/ppermute | solution.py:414
  18.4 11.3 %collective-permute-start.4 = (bf16[256,128]{1,0:T(8,128)(2,1)S(1)}, bf16[256,128]{1,0:T(8,128)(2,1)S(1)}, u32[]{:S(2)}, u32[]{:S(2)}) collective-permute-start(bf16[256,128]{1,0:T(8,128)(2,1)S(1)} %get-tuple-element.31.refs_1_.refs_0_.refs_2_), channel_id=1, source_target_pairs={{0,4},{4,0},{1,5},{5,1},{2,6},{6,2},{3,7},{7,3},{8,12},{12,8},{9,1... | collective-permute-start | bytes 196616 | tf_op jit(solution)/shard_map/ppermute | solution.py:414
  22.0 0.7 %copy-start.3 = (f32[256,256]{1,0:T(8,128)}, f32[256,256]{1,0:T(8,128)S(1)}, u32[]{:S(2)}) copy-start(f32[256,256]{1,0:T(8,128)S(1)} %get-tuple-element.33.refs_1_) | copy-start | bytes 786436
  23.3 15.9 %collective-permute-start.14 = (bf16[64,1280]{1,0:T(8,128)(2,1)S(1)}, bf16[64,1280]{1,0:T(8,128)(2,1)S(1)}, u32[]{:S(2)}, u32[]{:S(2)}) collective-permute-start(bf16[64,1280]{1,0:T(8,128)(2,1)S(1)} %get-tuple-element.36), channel_id=1, source_target_pairs={{0,6},{2,4},{4,2},{6,0},{1,7},{3,5},{5,3},{7,1},{8,14},{10,12},{12... | collective-permute-start | bytes 491528 | tf_op jit(solution)/shard_map/ppermute | solution.py:414
  26.3 4.3 %collective-permute-start.9 = (bf16[256,128]{1,0:T(8,128)(2,1)S(1)}, bf16[256,128]{1,0:T(8,128)(2,1)S(1)}, u32[]{:S(2)}, u32[]{:S(2)}) collective-permute-start(bf16[256,128]{1,0:T(8,128)(2,1)S(1)} %collective-permute-done.5.refs_5_), channel_id=1, source_target_pairs={{0,16},{16,0},{1,17},{17,1},{2,18},{18,2},{3,19},{19,3},{4,20},{20... | collective-permute-start | bytes 196616 | tf_op jit(solution)/shard_map/ppermute | solution.py:414
  29.8 4.3 %collective-permute-start.8 = (bf16[256,128]{1,0:T(8,128)(2,1)S(1)}, bf16[256,128]{1,0:T(8,128)(2,1)S(1)}, u32[]{:S(2)}, u32[]{:S(2)}) collective-permute-start(bf16[256,128]{1,0:T(8,128)(2,1)S(1)} %collective-permute-done.4.refs_4_), channel_id=1, source_target_pairs={{0,16},{16,0},{1,17},{17,1},{2,18},{18,2},{3,19},{19,3},{4,20},{20... | collective-permute-start | bytes 196616 | tf_op jit(solution)/shard_map/ppermute | solution.py:414
  30.3 9.3 %collective-permute-start.13 = (bf16[128,1280]{1,0:T(8,128)(2,1)S(1)}, bf16[128,1280]{1,0:T(8,128)(2,1)S(1)}, u32[]{:S(2)}, u32[]{:S(2)}) collective-permute-start(bf16[128,1280]{1,0:T(8,128)(2,1)S(1)} %get-tuple-element.35), channel_id=1, source_target_pairs={{0,2},{2,0},{1,3},{3,1},{4,6},{6,4},{5,7},{7,5},{8,10},{10,8},{9,1... | collective-permute-start | bytes 983048 | tf_op jit(solution)/shard_map/ppermute | solution.py:414
  34.0 1.0 %copy-start.4 = (f32[256,256]{1,0:T(8,128)S(1)}, f32[256,256]{1,0:T(8,128)}, u32[]{:S(2)}) copy-start(f32[256,256]{1,0:T(8,128)} %copy-done.3) | copy-start | bytes 786436
  35.6 5.2 %collective-permute-start.12 = (bf16[256,128]{1,0:T(8,128)(2,1)S(1)}, bf16[256,128]{1,0:T(8,128)(2,1)S(1)}, u32[]{:S(2)}, u32[]{:S(2)}) collective-permute-start(bf16[256,128]{1,0:T(8,128)(2,1)S(1)} %shard_map.45.refs_1_.refs_0_), channel_id=1, source_target_pairs={{0,10},{2,8},{8,2},{10,0},{1,11},{3,9},{9,3},{11,1},{4,14},{6,12},... | collective-permute-start | bytes 196616 | tf_op jit(solution)/shard_map/ppermute | solution.py:414
  35.7 5.2 %collective-permute-start.11 = (bf16[256,128]{1,0:T(8,128)(2,1)S(1)}, bf16[256,128]{1,0:T(8,128)(2,1)S(1)}, u32[]{:S(2)}, u32[]{:S(2)}) collective-permute-start(bf16[256,128]{1,0:T(8,128)(2,1)S(1)} %shard_map.45.refs_1_.refs_0_), channel_id=1, source_target_pairs={{0,8},{2,10},{8,0},{10,2},{1,9},{3,11},{9,1},{11,3},{4,12},{6,14},... | collective-permute-start | bytes 196616 | tf_op jit(solution)/shard_map/ppermute | solution.py:414
  37.2 4.3 %collective-permute-start.10 = (bf16[256,128]{1,0:T(8,128)(2,1)S(1)}, bf16[256,128]{1,0:T(8,128)(2,1)S(1)}, u32[]{:S(2)}, u32[]{:S(2)}) collective-permute-start(bf16[256,128]{1,0:T(8,128)(2,1)S(1)} %shard_map.45.refs_1_.refs_0_), channel_id=1, source_target_pairs={{0,2},{2,0},{8,10},{10,8},{1,3},{3,1},{9,11},{11,9},{4,6},{6,4},{1... | collective-permute-start | bytes 196616 | tf_op jit(solution)/shard_map/ppermute | solution.py:414
  39.2 5.3 %collective-permute-start.15 = (bf16[64,1280]{1,0:T(8,128)(2,1)S(1)}, bf16[64,1280]{1,0:T(8,128)(2,1)S(1)}, u32[]{:S(2)}, u32[]{:S(2)}) collective-permute-start(bf16[64,1280]{1,0:T(8,128)(2,1)S(1)} %shard_map.48.refs_8_), channel_id=1, source_target_pairs={{0,16},{16,0},{1,17},{17,1},{2,18},{18,2},{3,19},{19,3},{4,20},{20... | collective-permute-start | bytes 491528 | tf_op jit(solution)/shard_map/ppermute | solution.py:414
  45.8 1.7 %collective-permute-start.16 = (bf16[4,32,1280]{2,1,0:T(8,128)(2,1)S(1)}, bf16[4,32,1280]{2,1,0:T(8,128)(2,1)S(1)}, u32[]{:S(2)}, u32[]{:S(2)}) collective-permute-start(bf16[4,32,1280]{2,1,0:T(8,128)(2,1)S(1)} %get-tuple-element.38), channel_id=1, source_target_pairs={{0,1},{1,0},{2,3},{3,2},{4,5},{5,4},{6,7},{7,6},{8,9},{9,8},{10,11... | collective-permute-start | bytes 983048 | tf_op jit(solution)/shard_map/ppermute | solution.py:414
  47.5 5.1 %collective-permute-start.17 = (bf16[32,1280]{1,0:T(8,128)(2,1)S(1)}, bf16[32,1280]{1,0:T(8,128)(2,1)S(1)}, u32[]{:S(2)}, u32[]{:S(2)}) collective-permute-start(bf16[32,1280]{1,0:T(8,128)(2,1)S(1)} %get-tuple-element.40), channel_id=1, source_target_pairs={{0,2},{2,0},{8,10},{10,8},{1,3},{3,1},{9,11},{11,9},{4,6},{6,4},{1... | collective-permute-start | bytes 245768 | tf_op jit(solution)/shard_map/ppermute | solution.py:414
  47.7 5.0 %collective-permute-start.18 = (bf16[32,1280]{1,0:T(8,128)(2,1)S(1)}, bf16[32,1280]{1,0:T(8,128)(2,1)S(1)}, u32[]{:S(2)}, u32[]{:S(2)}) collective-permute-start(bf16[32,1280]{1,0:T(8,128)(2,1)S(1)} %get-tuple-element.41), channel_id=1, source_target_pairs={{0,8},{2,10},{8,0},{10,2},{1,9},{3,11},{9,1},{11,3},{4,12},{6,14},... | collective-permute-start | bytes 245768 | tf_op jit(solution)/shard_map/ppermute | solution.py:414
  49.2 5.6 %collective-permute-start.19 = (bf16[32,1280]{1,0:T(8,128)(2,1)S(1)}, bf16[32,1280]{1,0:T(8,128)(2,1)S(1)}, u32[]{:S(2)}, u32[]{:S(2)}) collective-permute-start(bf16[32,1280]{1,0:T(8,128)(2,1)S(1)} %get-tuple-element.42), channel_id=1, source_target_pairs={{0,10},{2,8},{8,2},{10,0},{1,11},{3,9},{9,3},{11,1},{4,14},{6,12},... | collective-permute-start | bytes 245768 | tf_op jit(solution)/shard_map/ppermute | solution.py:414

commit v17 on v15

--- a/solution.py
+++ b/solution.py
@@ -425,10 +425,9 @@
     bases = [y * 2 * FRB, (1 - y) * 2 * FRB]
     mask_of = masks(bases, 4 * tok, tok, 8 * tok, frame_clip)
     attn = attention(q, kvs, mask_of, [0, 0, 1, 1], head_dim)
-    corner = after(corner, attn, cost=SOON)
+    corner = after(corner, attn)
     corner_rest = xor(corner, ("y",), 1)
     attns = swap_all([attn] * 4, quarter)
-    w_next = after(w_next, attn, cost=AHEAD)
     w_parts = [w_out, w_next, far, near, corner, corner_rest]
     sizes = [head_dim, head_dim, half, half, half, half]
     at = [row, row ^ 1] + [2 * (row ^ by) + h for by in (2, 3) for h in (y, 1 - y)]

time: 54.6 us -> 53.7 us (0.984)
  waiting for transfers between devices: 24.5 us -> 23.8 us
    ppermute x20, waiting for transfers between devices: 24.5 us -> 23.8 us  [xor(): return lax.ppermute(x, axis, [(i, i ^ by) for i in range(size)])]
where the time goes in v17:
time: 53.7 us; the launch traced here: 53.6 us
  starting transfers between devices  23.9 us (45%)
  waiting for transfers between devices  23.8 us (44%)
  Pallas kernels  4.16 us (8%)
  local copies, waits for them, and re-layouts  1.41 us (3%)
    ppermute x20, starting transfers between devices, xor(): return lax.ppermute(x, axis, [(i, i ^ by) for i in range(size)])  23.9 us
    ppermute x20, waiting for transfers between devices, xor(): return lax.ppermute(x, axis, [(i, i ^ by) for i in range(size)])  23.8 us
    unnamed x8, local copies, waits for them, and re-layouts  1.33 us
    pallas_call x1, Pallas kernels, project(): pl.pallas_call(functools.partial(project_kernel, blks, sizes), out_shape=...  1.26 us
  transfers between devices with their start and end apart: 20, of which 15 were waited for; matrix products, arithmetic and copies ran while one was open for 0% of the time, Pallas kernels for 3%

profile of v17, /device:TPU:0, one launch (start us, length us, event | category | flops | bytes accessed | tf_op | source)
XLA Modules:
  0.0 53.6 jit_solution(8562537626275005742)
XLA Ops:
  0.0 0.1 pad_add_fusion.1.at_ref
  0.1 0.0 copy-start
  0.1 1.3 %copy-done = bf16[128,5120]{1,0:T(8,128)(2,1)S(1)} copy-done((bf16[128,5120]{1,0:T(8,128)(2,1)S(1)}, bf16[128,5120]{1,0:T(8,128)(2,1)}, u32[]{:S(2)}) %copy-start) | copy-done | bytes 1310744
  1.4 0.0 copy-start.2
  1.4 0.6 %shard_map.41 = (bf16[640,128]{1,0:T(8,128)(2,1)S(1)}, bf16[64,1280]{1,0:T(8,128)(2,1)S(1)}, bf16[128,1280]{1,0:T(8,128)(2,1)S(1)}) custom-call(s32[3]{0:T(128)S(1)} %pad_add_fusion.1.at_ref, bf16[128,5120]{1,0:T(8,128)(2,1)S(1)} %copy-done), custom_call_target="tpu_custom_call" | custom-call | tf_op jit(solution)/shard_map/pallas_call | solution.py:93
  2.0 4.1 %collective-permute-start.6 = (bf16[640,128]{1,0:T(8,128)(2,1)S(1)}, bf16[640,128]{1,0:T(8,128)(2,1)S(1)}, u32[]{:S(2)}, u32[]{:S(2)}) collective-permute-start(bf16[640,128]{1,0:T(8,128)(2,1)S(1)} %get-tuple-element.36), channel_id=1, source_target_pairs={{0,4},{4,0},{1,5},{5,1},{2,6},{6,2},{3,7},{7,3},{8,12},{12,8},{9,1... | collective-permute-start | bytes 491528 | tf_op jit(solution)/shard_map/ppermute | solution.py:398
  6.1 0.0 copy-done.2
  6.1 0.1 shard_map.37
  6.2 0.1 collective-permute-start
  6.3 1.3 %collective-permute-done.got_ref = bf16[4,96,128]{2,1,0:T(8,128)(2,1)S(1)} collective-permute-done((bf16[4,96,128]{2,1,0:T(8,128)(2,1)S(1)}, bf16[4,96,128]{2,1,0:T(8,128)(2,1)S(1)}, u32[]{:S(2)}, u32[]{:S(2)}) %collective-permute-start) | collective-permute-done | bytes 98336 | tf_op jit(solution)/shard_map/ppermute | solution.py:398
  7.6 1.6 %collective-permute-start.1 = (bf16[2,96,128]{2,1,0:T(8,128)(2,1)S(1)}, bf16[2,96,128]{2,1,0:T(8,128)(2,1)S(1)}, u32[]{:S(2)}, u32[]{:S(2)}) collective-permute-start(bf16[2,96,128]{2,1,0:T(8,128)(2,1)S(1)} %get-tuple-element.28), channel_id=1, source_target_pairs={{0,2},{2,0},{8,10},{10,8},{1,3},{3,1},{9,11},{11,9},{4,6},{6,4},{1... | collective-permute-start | bytes 147464 | tf_op jit(solution)/shard_map/ppermute | solution.py:398
  9.2 1.5 %collective-permute-start.2 = (bf16[2,96,128]{2,1,0:T(8,128)(2,1)S(1)}, bf16[2,96,128]{2,1,0:T(8,128)(2,1)S(1)}, u32[]{:S(2)}, u32[]{:S(2)}) collective-permute-start(bf16[2,96,128]{2,1,0:T(8,128)(2,1)S(1)} %get-tuple-element.29), channel_id=1, source_target_pairs={{0,8},{2,10},{8,0},{10,2},{1,9},{3,11},{9,1},{11,3},{4,12},{6,14},... | collective-permute-start | bytes 147464 | tf_op jit(solution)/shard_map/ppermute | solution.py:398
  10.7 0.4 collective-permute-start.3
  11.1 0.8 %collective-permute-done.1.refs_1_ = bf16[2,96,128]{2,1,0:T(8,128)(2,1)S(1)} collective-permute-done((bf16[2,96,128]{2,1,0:T(8,128)(2,1)S(1)}, bf16[2,96,128]{2,1,0:T(8,128)(2,1)S(1)}, u32[]{:S(2)}, u32[]{:S(2)}) %collective-permute-start.1) | collective-permute-done | bytes 49184 | tf_op jit(solution)/shard_map/ppermute | solution.py:398
  11.9 1.4 %collective-permute-done.2.refs_2_ = bf16[2,96,128]{2,1,0:T(8,128)(2,1)S(1)} collective-permute-done((bf16[2,96,128]{2,1,0:T(8,128)(2,1)S(1)}, bf16[2,96,128]{2,1,0:T(8,128)(2,1)S(1)}, u32[]{:S(2)}, u32[]{:S(2)}) %collective-permute-start.2) | collective-permute-done | bytes 49184 | tf_op jit(solution)/shard_map/ppermute | solution.py:398
  13.3 2.6 %collective-permute-done.3.refs_3_ = bf16[2,96,128]{2,1,0:T(8,128)(2,1)S(1)} collective-permute-done((bf16[2,96,128]{2,1,0:T(8,128)(2,1)S(1)}, bf16[2,96,128]{2,1,0:T(8,128)(2,1)S(1)}, u32[]{:S(2)}, u32[]{:S(2)}) %collective-permute-start.3) | collective-permute-done | bytes 49184 | tf_op jit(solution)/shard_map/ppermute | solution.py:398
  15.9 0.0 collective-permute-done.6.refs_0_
  15.9 0.0 copy-start.3
  16.0 1.6 %collective-permute-start.7 = (bf16[1152,128]{1,0:T(8,128)(2,1)S(1)}, bf16[1152,128]{1,0:T(8,128)(2,1)S(1)}, u32[]{:S(2)}, u32[]{:S(2)}) collective-permute-start(bf16[1152,128]{1,0:T(8,128)(2,1)S(1)} %shard_map.43), channel_id=1, source_target_pairs={{0,16},{16,0},{1,17},{17,1},{2,18},{18,2},{3,19},{19,3},{4,20},{20... | collective-permute-start | bytes 884744 | tf_op jit(solution)/shard_map/ppermute | solution.py:398
  17.5 0.2 collective-permute-start.4
  17.7 2.8 %collective-permute-start.5 = (bf16[256,128]{1,0:T(8,128)(2,1)S(1)}, bf16[256,128]{1,0:T(8,128)(2,1)S(1)}, u32[]{:S(2)}, u32[]{:S(2)}) collective-permute-start(bf16[256,128]{1,0:T(8,128)(2,1)S(1)} %get-tuple-element.35.refs_1_.refs_3_), channel_id=1, source_target_pairs={{0,4},{4,0},{1,5},{5,1},{2,6},{6,2},{3,7},{7,3},{8,12},{12,8},{9,1... | collective-permute-start | bytes 196616 | tf_op jit(solution)/shard_map/ppermute | solution.py:398
  20.5 0.0 copy-start.1
  20.5 0.6 %collective-permute-start.13 = (bf16[128,1280]{1,0:T(8,128)(2,1)S(1)}, bf16[128,1280]{1,0:T(8,128)(2,1)S(1)}, u32[]{:S(2)}, u32[]{:S(2)}) collective-permute-start(bf16[128,1280]{1,0:T(8,128)(2,1)S(1)} %shard_map.45), channel_id=1, source_target_pairs={{0,2},{2,0},{1,3},{3,1},{4,6},{6,4},{5,7},{7,5},{8,10},{10,8},{9,1... | collective-permute-start | bytes 983048 | tf_op jit(solution)/shard_map/ppermute | solution.py:398
  21.1 2.3 %collective-permute-start.14 = (bf16[64,1280]{1,0:T(8,128)(2,1)S(1)}, bf16[64,1280]{1,0:T(8,128)(2,1)S(1)}, u32[]{:S(2)}, u32[]{:S(2)}) collective-permute-start(bf16[64,1280]{1,0:T(8,128)(2,1)S(1)} %shard_map.46), channel_id=1, source_target_pairs={{0,6},{2,4},{4,2},{6,0},{1,7},{3,5},{5,3},{7,1},{8,14},{10,12},{12... | collective-permute-start | bytes 491528 | tf_op jit(solution)/shard_map/ppermute | solution.py:398
  23.4 1.3 %collective-permute-done.4.refs_4_ = bf16[256,128]{1,0:T(8,128)(2,1)S(1)} collective-permute-done((bf16[256,128]{1,0:T(8,128)(2,1)S(1)}, bf16[256,128]{1,0:T(8,128)(2,1)S(1)}, u32[]{:S(2)}, u32[]{:S(2)}) %collective-permute-start.4) | collective-permute-done | bytes 65568 | tf_op jit(solution)/shard_map/ppermute | solution.py:398
  24.7 0.5 collective-permute-start.8
  25.2 1.6 %collective-permute-done.5.refs_5_ = bf16[256,128]{1,0:T(8,128)(2,1)S(1)} collective-permute-done((bf16[256,128]{1,0:T(8,128)(2,1)S(1)}, bf16[256,128]{1,0:T(8,128)(2,1)S(1)}, u32[]{:S(2)}, u32[]{:S(2)}) %collective-permute-start.5) | collective-permute-done | bytes 65568 | tf_op jit(solution)/shard_map/ppermute | solution.py:398
  26.8 0.5 collective-permute-start.9
  27.3 0.1 pad_add_fusion.base_ref
  27.4 0.0 copy-done.3
  27.4 0.7 %shard_map.40 = (f32[256,256]{1,0:T(8,128)S(1)}, f32[256,256]{1,0:T(8,128)S(1)}) custom-call(s32[2]{0:T(128)S(1)} %pad_add_fusion.base_ref, s32[8]{0:T(128)S(1)} %copy-done.3), custom_call_target="tpu_custom_call" | custom-call | tf_op jit(solution)/shard_map/pallas_call | solution.py:244
  28.1 0.9 %collective-permute-done.8.refs_7_ = bf16[256,128]{1,0:T(8,128)(2,1)S(1)} collective-permute-done((bf16[256,128]{1,0:T(8,128)(2,1)S(1)}, bf16[256,128]{1,0:T(8,128)(2,1)S(1)}, u32[]{:S(2)}, u32[]{:S(2)}) %collective-permute-start.8) | collective-permute-done | bytes 65568 | tf_op jit(solution)/shard_map/ppermute | solution.py:398
  29.0 2.1 %collective-permute-done.9.refs_8_ = bf16[256,128]{1,0:T(8,128)(2,1)S(1)} collective-permute-done((bf16[256,128]{1,0:T(8,128)(2,1)S(1)}, bf16[256,128]{1,0:T(8,128)(2,1)S(1)}, u32[]{:S(2)}, u32[]{:S(2)}) %collective-permute-start.9) | collective-permute-done | bytes 65568 | tf_op jit(solution)/shard_map/ppermute | solution.py:398
  31.1 0.0 collective-permute-done.7.refs_6_.refs_7_
  31.1 0.6 %shard_map.44.refs_1_.refs_0_ = bf16[256,128]{1,0:T(8,128)(2,1)S(1)} custom-call(bf16[256,128]{1,0:T(8,128)(2,1)S(1)} %get-tuple-element.31.q_ref, f32[256,256]{1,0:T(8,128)S(1)} %get-tuple-element.32.refs_0_, f32[256,256]{1,0:T(8,128)S(1)} %get-tuple-element.33.refs_1_, bf16[256,128]{1,0:T(8,128)(2,1)S(1)} %get-tuple-element.34.refs_0_.refs_2_.refs_1_, ...), custom_call_target="tpu_custom_call" | custom-call | tf_op jit(solution)/shard_map/pallas_call | solution.py:304
  31.7 2.9 %collective-permute-done.14.refs_0_ = bf16[64,1280]{1,0:T(8,128)(2,1)S(1)} collective-permute-done((bf16[64,1280]{1,0:T(8,128)(2,1)S(1)}, bf16[64,1280]{1,0:T(8,128)(2,1)S(1)}, u32[]{:S(2)}, u32[]{:S(2)}) %collective-permute-start.14) | collective-permute-done | bytes 163872 | tf_op jit(solution)/shard_map/ppermute | solution.py:398
  34.6 0.5 collective-permute-start.15
  35.1 0.0 collective-permute-start.10
  35.1 0.8 %collective-permute-start.11 = (bf16[256,128]{1,0:T(8,128)(2,1)S(1)}, bf16[256,128]{1,0:T(8,128)(2,1)S(1)}, u32[]{:S(2)}, u32[]{:S(2)}) collective-permute-start(bf16[256,128]{1,0:T(8,128)(2,1)S(1)} %shard_map.44.refs_1_.refs_0_), channel_id=1, source_target_pairs={{0,8},{2,10},{8,0},{10,2},{1,9},{3,11},{9,1},{11,3},{4,12},{6,14},... | collective-permute-start | bytes 196616 | tf_op jit(solution)/shard_map/ppermute | solution.py:398
  35.9 2.7 %collective-permute-start.12 = (bf16[256,128]{1,0:T(8,128)(2,1)S(1)}, bf16[256,128]{1,0:T(8,128)(2,1)S(1)}, u32[]{:S(2)}, u32[]{:S(2)}) collective-permute-start(bf16[256,128]{1,0:T(8,128)(2,1)S(1)} %shard_map.44.refs_1_.refs_0_), channel_id=1, source_target_pairs={{0,10},{2,8},{8,2},{10,0},{1,11},{3,9},{9,3},{11,1},{4,14},{6,12},... | collective-permute-start | bytes 196616 | tf_op jit(solution)/shard_map/ppermute | solution.py:398
  38.6 0.1 stack.55.at_ref
  38.7 0.0 collective-permute-done.13.refs_5_
  38.7 0.7 %collective-permute-done.10.refs_1_ = bf16[256,128]{1,0:T(8,128)(2,1)S(1)} collective-permute-done((bf16[256,128]{1,0:T(8,128)(2,1)S(1)}, bf16[256,128]{1,0:T(8,128)(2,1)S(1)}, u32[]{:S(2)}, u32[]{:S(2)}) %collective-permute-start.10) | collective-permute-done | bytes 65568 | tf_op jit(solution)/shard_map/ppermute | solution.py:398
  39.4 0.0 collective-permute-done.11.refs_2_
  39.4 1.7 %collective-permute-done.12.refs_3_ = bf16[256,128]{1,0:T(8,128)(2,1)S(1)} collective-permute-done((bf16[256,128]{1,0:T(8,128)(2,1)S(1)}, bf16[256,128]{1,0:T(8,128)(2,1)S(1)}, u32[]{:S(2)}, u32[]{:S(2)}) %collective-permute-start.12) | collective-permute-done | bytes 65568 | tf_op jit(solution)/shard_map/ppermute | solution.py:398
  41.1 0.0 collective-permute-done.15.refs_9_
  41.1 0.0 copy-done.1
  41.1 1.3 %shard_map.48 = (bf16[4,32,1280]{2,1,0:T(8,128)(2,1)S(1)}, bf16[4,32,1280]{2,1,0:T(8,128)(2,1)S(1)}) custom-call(s32[6]{0:T(128)S(1)} %stack.55.at_ref, s32[1]{0:T(128)} %bitcast.place_ref, bf16[256,128]{1,0:T(8,128)(2,1)S(1)} %shard_map.44.refs_1_.refs_0_, bf16[256,128]{1,0:T(8,128)(2,1)S(1)} %collective-permute-done.10.refs_1_, ...), custom_call_target="tpu_custom_call" | custom-call | tf_op jit(solution)/shard_map/pallas_call | solution.py:347
  42.4 0.1 collective-permute-start.16
  42.4 1.6 %collective-permute-done.16.y_ref = bf16[4,32,1280]{2,1,0:T(8,128)(2,1)S(1)} collective-permute-done((bf16[4,32,1280]{2,1,0:T(8,128)(2,1)S(1)}, bf16[4,32,1280]{2,1,0:T(8,128)(2,1)S(1)}, u32[]{:S(2)}, u32[]{:S(2)}) %collective-permute-start.16) | collective-permute-done | bytes 327712 | tf_op jit(solution)/shard_map/ppermute | solution.py:398
  44.1 0.1 shard_map.49
  44.1 2.1 %collective-permute-start.17 = (bf16[32,1280]{1,0:T(8,128)(2,1)S(1)}, bf16[32,1280]{1,0:T(8,128)(2,1)S(1)}, u32[]{:S(2)}, u32[]{:S(2)}) collective-permute-start(bf16[32,1280]{1,0:T(8,128)(2,1)S(1)} %get-tuple-element.42), channel_id=1, source_target_pairs={{0,2},{2,0},{8,10},{10,8},{1,3},{3,1},{9,11},{11,9},{4,6},{6,4},{1... | collective-permute-start | bytes 245768 | tf_op jit(solution)/shard_map/ppermute | solution.py:398
  46.2 1.2 %collective-permute-start.18 = (bf16[32,1280]{1,0:T(8,128)(2,1)S(1)}, bf16[32,1280]{1,0:T(8,128)(2,1)S(1)}, u32[]{:S(2)}, u32[]{:S(2)}) collective-permute-start(bf16[32,1280]{1,0:T(8,128)(2,1)S(1)} %get-tuple-element.43), channel_id=1, source_target_pairs={{0,8},{2,10},{8,0},{10,2},{1,9},{3,11},{9,1},{11,3},{4,12},{6,14},... | collective-permute-start | bytes 245768 | tf_op jit(solution)/shard_map/ppermute | solution.py:398
  47.5 0.3 collective-permute-start.19
  47.8 1.2 %collective-permute-done.17.refs_1_ = bf16[32,1280]{1,0:T(8,128)(2,1)S(1)} collective-permute-done((bf16[32,1280]{1,0:T(8,128)(2,1)S(1)}, bf16[32,1280]{1,0:T(8,128)(2,1)S(1)}, u32[]{:S(2)}, u32[]{:S(2)}) %collective-permute-start.17) | collective-permute-done | bytes 81952 | tf_op jit(solution)/shard_map/ppermute | solution.py:398
  49.0 2.6 %collective-permute-done.18.refs_2_ = bf16[32,1280]{1,0:T(8,128)(2,1)S(1)} collective-permute-done((bf16[32,1280]{1,0:T(8,128)(2,1)S(1)}, bf16[32,1280]{1,0:T(8,128)(2,1)S(1)}, u32[]{:S(2)}, u32[]{:S(2)}) %collective-permute-start.18) | collective-permute-done | bytes 81952 | tf_op jit(solution)/shard_map/ppermute | solution.py:398
  51.5 1.3 %collective-permute-done.19.refs_3_ = bf16[32,1280]{1,0:T(8,128)(2,1)S(1)} collective-permute-done((bf16[32,1280]{1,0:T(8,128)(2,1)S(1)}, bf16[32,1280]{1,0:T(8,128)(2,1)S(1)}, u32[]{:S(2)}, u32[]{:S(2)}) %collective-permute-start.19) | collective-permute-done | bytes 81952 | tf_op jit(solution)/shard_map/ppermute | solution.py:398
  52.8 0.8 %shard_map.50 = bf16[32,5120]{1,0:T(8,128)(2,1)} custom-call(s32[1]{0:T(128)} %bitcast.place_ref, bf16[32,1280]{1,0:T(8,128)(2,1)S(1)} %get-tuple-element.41.refs_0_, bf16[32,1280]{1,0:T(8,128)(2,1)S(1)} %collective-permute-done.17.refs_1_, bf16[32,1280]{1,0:T(8,128)(2,1)S(1)} %collective-permute-done.18.refs_2_, ...), custom_call_target="tpu_custom_call" | custom-call | tf_op jit(solution)/shard_map/pallas_call | solution.py:387
  (7 shorter events, 0.1 us)
Async XLA Ops:
  0.1 1.3 %copy-start = (bf16[128,5120]{1,0:T(8,128)(2,1)S(1)}, bf16[128,5120]{1,0:T(8,128)(2,1)}, u32[]{:S(2)}) copy-start(bf16[128,5120]{1,0:T(8,128)(2,1)} %refs_4_.1) | copy-start | bytes 3932164
  1.4 4.7 %copy-start.2 = (bf16[3,32,1024]{2,1,0:T(8,128)(2,1)S(1)}, bf16[3,32,1024]{2,1,0:T(8,128)(2,1)}, u32[]{:S(2)}) copy-start(bf16[3,32,1024]{2,1,0:T(8,128)(2,1)} %x_ref.2) | copy-start | bytes 589828
  2.0 13.9 %collective-permute-start.6 = (bf16[640,128]{1,0:T(8,128)(2,1)S(1)}, bf16[640,128]{1,0:T(8,128)(2,1)S(1)}, u32[]{:S(2)}, u32[]{:S(2)}) collective-permute-start(bf16[640,128]{1,0:T(8,128)(2,1)S(1)} %get-tuple-element.36), channel_id=1, source_target_pairs={{0,4},{4,0},{1,5},{5,1},{2,6},{6,2},{3,7},{7,3},{8,12},{12,8},{9,1... | collective-permute-start | bytes 491528 | tf_op jit(solution)/shard_map/ppermute | solution.py:398
  6.2 1.4 %collective-permute-start = (bf16[4,96,128]{2,1,0:T(8,128)(2,1)S(1)}, bf16[4,96,128]{2,1,0:T(8,128)(2,1)S(1)}, u32[]{:S(2)}, u32[]{:S(2)}) collective-permute-start(bf16[4,96,128]{2,1,0:T(8,128)(2,1)S(1)} %get-tuple-element.26), channel_id=1, source_target_pairs={{0,1},{1,0},{2,3},{3,2},{4,5},{5,4},{6,7},{7,6},{8,9},{9,8},{10,11... | collective-permute-start | bytes 294920 | tf_op jit(solution)/shard_map/ppermute | solution.py:398
  7.6 4.3 %collective-permute-start.1 = (bf16[2,96,128]{2,1,0:T(8,128)(2,1)S(1)}, bf16[2,96,128]{2,1,0:T(8,128)(2,1)S(1)}, u32[]{:S(2)}, u32[]{:S(2)}) collective-permute-start(bf16[2,96,128]{2,1,0:T(8,128)(2,1)S(1)} %get-tuple-element.28), channel_id=1, source_target_pairs={{0,2},{2,0},{8,10},{10,8},{1,3},{3,1},{9,11},{11,9},{4,6},{6,4},{1... | collective-permute-start | bytes 147464 | tf_op jit(solution)/shard_map/ppermute | solution.py:398
  9.2 4.1 %collective-permute-start.2 = (bf16[2,96,128]{2,1,0:T(8,128)(2,1)S(1)}, bf16[2,96,128]{2,1,0:T(8,128)(2,1)S(1)}, u32[]{:S(2)}, u32[]{:S(2)}) collective-permute-start(bf16[2,96,128]{2,1,0:T(8,128)(2,1)S(1)} %get-tuple-element.29), channel_id=1, source_target_pairs={{0,8},{2,10},{8,0},{10,2},{1,9},{3,11},{9,1},{11,3},{4,12},{6,14},... | collective-permute-start | bytes 147464 | tf_op jit(solution)/shard_map/ppermute | solution.py:398
  10.7 5.2 %collective-permute-start.3 = (bf16[2,96,128]{2,1,0:T(8,128)(2,1)S(1)}, bf16[2,96,128]{2,1,0:T(8,128)(2,1)S(1)}, u32[]{:S(2)}, u32[]{:S(2)}) collective-permute-start(bf16[2,96,128]{2,1,0:T(8,128)(2,1)S(1)} %get-tuple-element.30), channel_id=1, source_target_pairs={{0,10},{2,8},{8,2},{10,0},{1,11},{3,9},{9,3},{11,1},{4,14},{6,12},... | collective-permute-start | bytes 147464 | tf_op jit(solution)/shard_map/ppermute | solution.py:398
  15.9 11.5 %copy-start.3 = (s32[8]{0:T(128)S(1)}, s32[8]{0:T(128)}, u32[]{:S(2)}) copy-start(s32[8]{0:T(128)} %clip_ref.1) | copy-start | bytes 100
  16.0 15.1 %collective-permute-start.7 = (bf16[1152,128]{1,0:T(8,128)(2,1)S(1)}, bf16[1152,128]{1,0:T(8,128)(2,1)S(1)}, u32[]{:S(2)}, u32[]{:S(2)}) collective-permute-start(bf16[1152,128]{1,0:T(8,128)(2,1)S(1)} %shard_map.43), channel_id=1, source_target_pairs={{0,16},{16,0},{1,17},{17,1},{2,18},{18,2},{3,19},{19,3},{4,20},{20... | collective-permute-start | bytes 884744 | tf_op jit(solution)/shard_map/ppermute | solution.py:398
  17.5 7.1 %collective-permute-start.4 = (bf16[256,128]{1,0:T(8,128)(2,1)S(1)}, bf16[256,128]{1,0:T(8,128)(2,1)S(1)}, u32[]{:S(2)}, u32[]{:S(2)}) collective-permute-start(bf16[256,128]{1,0:T(8,128)(2,1)S(1)} %get-tuple-element.34.refs_0_.refs_2_.refs_1_), channel_id=1, source_target_pairs={{0,4},{4,0},{1,5},{5,1},{2,6},{6,2},{3,7},{7,3},{8,12},{12,8},{9,1... | collective-permute-start | bytes 196616 | tf_op jit(solution)/shard_map/ppermute | solution.py:398
  17.7 9.1 %collective-permute-start.5 = (bf16[256,128]{1,0:T(8,128)(2,1)S(1)}, bf16[256,128]{1,0:T(8,128)(2,1)S(1)}, u32[]{:S(2)}, u32[]{:S(2)}) collective-permute-start(bf16[256,128]{1,0:T(8,128)(2,1)S(1)} %get-tuple-element.35.refs_1_.refs_3_), channel_id=1, source_target_pairs={{0,4},{4,0},{1,5},{5,1},{2,6},{6,2},{3,7},{7,3},{8,12},{12,8},{9,1... | collective-permute-start | bytes 196616 | tf_op jit(solution)/shard_map/ppermute | solution.py:398
  20.5 20.6 %copy-start.1 = (bf16[128,5120]{1,0:T(8,128)(2,1)S(1)}, bf16[128,5120]{1,0:T(8,128)(2,1)}, u32[]{:S(2)}) copy-start(bf16[128,5120]{1,0:T(8,128)(2,1)} %refs_4_.1) | copy-start | bytes 3932164
  20.5 18.2 %collective-permute-start.13 = (bf16[128,1280]{1,0:T(8,128)(2,1)S(1)}, bf16[128,1280]{1,0:T(8,128)(2,1)S(1)}, u32[]{:S(2)}, u32[]{:S(2)}) collective-permute-start(bf16[128,1280]{1,0:T(8,128)(2,1)S(1)} %shard_map.45), channel_id=1, source_target_pairs={{0,2},{2,0},{1,3},{3,1},{4,6},{6,4},{5,7},{7,5},{8,10},{10,8},{9,1... | collective-permute-start | bytes 983048 | tf_op jit(solution)/shard_map/ppermute | solution.py:398
  21.1 13.5 %collective-permute-start.14 = (bf16[64,1280]{1,0:T(8,128)(2,1)S(1)}, bf16[64,1280]{1,0:T(8,128)(2,1)S(1)}, u32[]{:S(2)}, u32[]{:S(2)}) collective-permute-start(bf16[64,1280]{1,0:T(8,128)(2,1)S(1)} %shard_map.46), channel_id=1, source_target_pairs={{0,6},{2,4},{4,2},{6,0},{1,7},{3,5},{5,3},{7,1},{8,14},{10,12},{12... | collective-permute-start | bytes 491528 | tf_op jit(solution)/shard_map/ppermute | solution.py:398
  24.7 4.3 %collective-permute-start.8 = (bf16[256,128]{1,0:T(8,128)(2,1)S(1)}, bf16[256,128]{1,0:T(8,128)(2,1)S(1)}, u32[]{:S(2)}, u32[]{:S(2)}) collective-permute-start(bf16[256,128]{1,0:T(8,128)(2,1)S(1)} %collective-permute-done.4.refs_4_), channel_id=1, source_target_pairs={{0,16},{16,0},{1,17},{17,1},{2,18},{18,2},{3,19},{19,3},{4,20},{20... | collective-permute-start | bytes 196616 | tf_op jit(solution)/shard_map/ppermute | solution.py:398
  26.8 4.3 %collective-permute-start.9 = (bf16[256,128]{1,0:T(8,128)(2,1)S(1)}, bf16[256,128]{1,0:T(8,128)(2,1)S(1)}, u32[]{:S(2)}, u32[]{:S(2)}) collective-permute-start(bf16[256,128]{1,0:T(8,128)(2,1)S(1)} %collective-permute-done.5.refs_5_), channel_id=1, source_target_pairs={{0,16},{16,0},{1,17},{17,1},{2,18},{18,2},{3,19},{19,3},{4,20},{20... | collective-permute-start | bytes 196616 | tf_op jit(solution)/shard_map/ppermute | solution.py:398
  34.6 6.5 %collective-permute-start.15 = (bf16[64,1280]{1,0:T(8,128)(2,1)S(1)}, bf16[64,1280]{1,0:T(8,128)(2,1)S(1)}, u32[]{:S(2)}, u32[]{:S(2)}) collective-permute-start(bf16[64,1280]{1,0:T(8,128)(2,1)S(1)} %shard_map.47.refs_8_), channel_id=1, source_target_pairs={{0,16},{16,0},{1,17},{17,1},{2,18},{18,2},{3,19},{19,3},{4,20},{20... | collective-permute-start | bytes 491528 | tf_op jit(solution)/shard_map/ppermute | solution.py:398
  35.1 4.3 %collective-permute-start.10 = (bf16[256,128]{1,0:T(8,128)(2,1)S(1)}, bf16[256,128]{1,0:T(8,128)(2,1)S(1)}, u32[]{:S(2)}, u32[]{:S(2)}) collective-permute-start(bf16[256,128]{1,0:T(8,128)(2,1)S(1)} %shard_map.44.refs_1_.refs_0_), channel_id=1, source_target_pairs={{0,2},{2,0},{8,10},{10,8},{1,3},{3,1},{9,11},{11,9},{4,6},{6,4},{1... | collective-permute-start | bytes 196616 | tf_op jit(solution)/shard_map/ppermute | solution.py:398
  35.1 4.3 %collective-permute-start.11 = (bf16[256,128]{1,0:T(8,128)(2,1)S(1)}, bf16[256,128]{1,0:T(8,128)(2,1)S(1)}, u32[]{:S(2)}, u32[]{:S(2)}) collective-permute-start(bf16[256,128]{1,0:T(8,128)(2,1)S(1)} %shard_map.44.refs_1_.refs_0_), channel_id=1, source_target_pairs={{0,8},{2,10},{8,0},{10,2},{1,9},{3,11},{9,1},{11,3},{4,12},{6,14},... | collective-permute-start | bytes 196616 | tf_op jit(solution)/shard_map/ppermute | solution.py:398
  35.9 5.2 %collective-permute-start.12 = (bf16[256,128]{1,0:T(8,128)(2,1)S(1)}, bf16[256,128]{1,0:T(8,128)(2,1)S(1)}, u32[]{:S(2)}, u32[]{:S(2)}) collective-permute-start(bf16[256,128]{1,0:T(8,128)(2,1)S(1)} %shard_map.44.refs_1_.refs_0_), channel_id=1, source_target_pairs={{0,10},{2,8},{8,2},{10,0},{1,11},{3,9},{9,3},{11,1},{4,14},{6,12},... | collective-permute-start | bytes 196616 | tf_op jit(solution)/shard_map/ppermute | solution.py:398
  42.4 1.7 %collective-permute-start.16 = (bf16[4,32,1280]{2,1,0:T(8,128)(2,1)S(1)}, bf16[4,32,1280]{2,1,0:T(8,128)(2,1)S(1)}, u32[]{:S(2)}, u32[]{:S(2)}) collective-permute-start(bf16[4,32,1280]{2,1,0:T(8,128)(2,1)S(1)} %get-tuple-element.40), channel_id=1, source_target_pairs={{0,1},{1,0},{2,3},{3,2},{4,5},{5,4},{6,7},{7,6},{8,9},{9,8},{10,11... | collective-permute-start | bytes 983048 | tf_op jit(solution)/shard_map/ppermute | solution.py:398
  44.1 4.8 %collective-permute-start.17 = (bf16[32,1280]{1,0:T(8,128)(2,1)S(1)}, bf16[32,1280]{1,0:T(8,128)(2,1)S(1)}, u32[]{:S(2)}, u32[]{:S(2)}) collective-permute-start(bf16[32,1280]{1,0:T(8,128)(2,1)S(1)} %get-tuple-element.42), channel_id=1, source_target_pairs={{0,2},{2,0},{8,10},{10,8},{1,3},{3,1},{9,11},{11,9},{4,6},{6,4},{1... | collective-permute-start | bytes 245768 | tf_op jit(solution)/shard_map/ppermute | solution.py:398
  46.2 5.3 %collective-permute-start.18 = (bf16[32,1280]{1,0:T(8,128)(2,1)S(1)}, bf16[32,1280]{1,0:T(8,128)(2,1)S(1)}, u32[]{:S(2)}, u32[]{:S(2)}) collective-permute-start(bf16[32,1280]{1,0:T(8,128)(2,1)S(1)} %get-tuple-element.43), channel_id=1, source_target_pairs={{0,8},{2,10},{8,0},{10,2},{1,9},{3,11},{9,1},{11,3},{4,12},{6,14},... | collective-permute-start | bytes 245768 | tf_op jit(solution)/shard_map/ppermute | solution.py:398
  47.5 5.3 %collective-permute-start.19 = (bf16[32,1280]{1,0:T(8,128)(2,1)S(1)}, bf16[32,1280]{1,0:T(8,128)(2,1)S(1)}, u32[]{:S(2)}, u32[]{:S(2)}) collective-permute-start(bf16[32,1280]{1,0:T(8,128)(2,1)S(1)} %get-tuple-element.44), channel_id=1, source_target_pairs={{0,10},{2,8},{8,2},{10,0},{1,11},{3,9},{9,3},{11,1},{4,14},{6,12},... | collective-permute-start | bytes 245768 | tf_op jit(solution)/shard_map/ppermute | solution.py:398

commit v18 on v17

--- a/solution.py
+++ b/solution.py
@@ -79,26 +79,26 @@
     )
 
 
-def pieces_kernel(at_ref, x_ref, far_ref, corner_ref, near_ref):
-    half, cols = corner_ref.shape
+def pieces_kernel(at_ref, x_ref, far_ref, first_ref, second_ref, near_ref):
+    half, cols = x_ref.shape[0] // 2, near_ref.shape[1]
     rows = rows_at(at_ref[0], half)
     count = cols // LANES
     for j in range(count):
         far_ref[j * half:(j + 1) * half, :] = x_ref[rows, rows_at(at_ref[1] * count + j, LANES)]
-    corner_ref[...] = x_ref[rows, rows_at(at_ref[2], cols)]
+    for i, ref in enumerate((first_ref, second_ref)):
+        ref[...] = x_ref[rows_at(at_ref[0] * 2 + i, half // 2), rows_at(at_ref[2], cols)]
     near_ref[...] = x_ref[:, rows_at(at_ref[2], cols)]
 
 
 def pieces(x, half, first_at, second_at, cols):
+    depth = x.shape[0]
+    shapes = [(cols // LANES * (depth // 2), LANES)]
+    shapes += [(rows, cols) for rows in (depth // 4, depth // 4, depth)]
     return pl.pallas_call(
         pieces_kernel,
-        out_shape=(
-            jax.ShapeDtypeStruct((cols // LANES * (x.shape[0] // 2), LANES), x.dtype),
-            jax.ShapeDtypeStruct((x.shape[0] // 2, cols), x.dtype),
-            jax.ShapeDtypeStruct((x.shape[0], cols), x.dtype),
-        ),
+        out_shape=[jax.ShapeDtypeStruct(shape, x.dtype) for shape in shapes],
         in_specs=[SMEM, VMEM],
-        out_specs=(VMEM, VMEM, VMEM),
+        out_specs=[VMEM] * 4,
         compiler_params=PARAMS,
     )(index_array(half, first_at, second_at), x)
 
@@ -399,8 +399,7 @@
 
 
 def swap_all(parts, axis):
-    last_first = [xor(parts[m], axis, m) for m in range(len(parts) - 1, 0, -1)]
-    return [parts[0]] + last_first[::-1]
+    return [parts[0]] + [xor(parts[m], axis, m) for m in range(1, len(parts))]
 
 
 def squares(qkv, frame_clip, w_out):
@@ -411,21 +410,22 @@
     mine, theirs = x * 2 + zl, x * 2 + 1 - zl
     row, half = zh * 2 + zl, head_dim // 2
 
-    w_far, w_corner, w_near = pieces(w_out, y, mine, theirs, cols)
+    w_far, w_first, w_second, w_near = pieces(w_out, y, mine, theirs, cols)
     far = after(xor(w_far, ("zh",), 1), cost=AHEAD)
     kept, given = lanes(qkv, core, head_dim)
     shared = swap_all(deal(kept, xor(given, ("core",), 1), place), quarter)
+    corner_first = after(xor(after(w_first, shared[1]), ("zh", "zl"), 3), cost=AHEAD)
     q, k, v = sort(shared, place)
     k_far, v_far = xor(k, ("zh",), 1), xor(v, ("zh",), 1)
-    near = xor(join(k, v, far), ("y",), 1)
-    corner = xor(after(w_corner, k), ("zh", "zl"), 3)
+    near = xor(join(k, v, after(far, corner_first)), ("y",), 1)
+    corner_second = xor(after(w_second, k), ("zh", "zl"), 3)
     w_next = xor(after(w_near, k), ("zl",), 1)
     kvs = [(k, v), (k_far, v_far), near, (xor(k_far, ("y",), 1), xor(v_far, ("y",), 1))]
 
     bases = [y * 2 * FRB, (1 - y) * 2 * FRB]
     mask_of = masks(bases, 4 * tok, tok, 8 * tok, frame_clip)
     attn = attention(q, kvs, mask_of, [0, 0, 1, 1], head_dim)
-    corner = after(corner, attn)
+    corner = join(corner_first, after(corner_second, attn))
     corner_rest = xor(corner, ("y",), 1)
     attns = swap_all([attn] * 4, quarter)
     w_parts = [w_out, w_next, far, near, corner, corner_rest]

time: 53.7 us -> 54.7 us (1.019)
  starting transfers between devices: 23.9 us -> 25.6 us
  waiting for transfers between devices: 23.8 us -> 23.1 us
    ppermute x20 -> x21, starting transfers between devices: 23.9 us -> 25.6 us  [xor(): return lax.ppermute(x, axis, [(i, i ^ by) for i in range(size)])]
    ppermute x20 -> x21, waiting for transfers between devices: 23.8 us -> 23.1 us  [xor(): return lax.ppermute(x, axis, [(i, i ^ by) for i in range(size)])]
    unnamed x8 -> x9, local copies, waits for them, and re-layouts: 1.33 us -> 1.34 us
  transfers between devices with their start and end apart: 20 -> 21, of which waited for: 15 -> 16; matrix products, arithmetic and copies ran while one was open for 0% -> 0% of each run, Pallas kernels for 3% -> 3%
where the time goes in v18:
time: 54.7 us; the launch traced here: 54.6 us
  starting transfers between devices  25.6 us (47%)
  waiting for transfers between devices  23.1 us (42%)
  Pallas kernels  4.17 us (8%)
  local copies, waits for them, and re-layouts  1.42 us (3%)
    ppermute x21, starting transfers between devices, xor(): return lax.ppermute(x, axis, [(i, i ^ by) for i in range(size)])  25.6 us
    ppermute x21, waiting for transfers between devices, xor(): return lax.ppermute(x, axis, [(i, i ^ by) for i in range(size)])  23.1 us
    unnamed x9, local copies, waits for them, and re-layouts  1.34 us
    pallas_call x1, Pallas kernels, project(): pl.pallas_call(functools.partial(project_kernel, blks, sizes), out_shape=...  1.26 us
  transfers between devices with their start and end apart: 21, of which 16 were waited for; matrix products, arithmetic and copies ran while one was open for 0% of the time, Pallas kernels for 3%

profile of v18, /device:TPU:0, one launch (start us, length us, event | category | flops | bytes accessed | tf_op | source)
XLA Modules:
  0.0 54.6 jit_solution(18010419715254952542)
XLA Ops:
  0.0 0.1 pad_add_fusion.1.at_ref
  0.1 0.0 copy-start
  0.1 1.3 %copy-done = bf16[128,5120]{1,0:T(8,128)(2,1)S(1)} copy-done((bf16[128,5120]{1,0:T(8,128)(2,1)S(1)}, bf16[128,5120]{1,0:T(8,128)(2,1)}, u32[]{:S(2)}) %copy-start) | copy-done | bytes 1310744
  1.4 0.0 copy-start.2
  1.4 0.6 %shard_map.41 = (bf16[640,128]{1,0:T(8,128)(2,1)S(1)}, bf16[32,1280]{1,0:T(8,128)(2,1)S(1)}, bf16[32,1280]{1,0:T(8,128)(2,1)S(1)}, bf16[128,1280]{1,0:T(8,128)(2,1)S(1)}) custom-call(s32[3]{0:T(128)S(1)} %pad_add_fusion.1.at_ref, bf16[128,5120]{1,0:T(8,128)(2,1)S(1)} %copy-done), custom_call_target="tpu_custom_call" | custom-call | tf_op jit(solution)/shard_map/pallas_call | solution.py:97
  2.0 4.1 %collective-permute-start.6 = (bf16[640,128]{1,0:T(8,128)(2,1)S(1)}, bf16[640,128]{1,0:T(8,128)(2,1)S(1)}, u32[]{:S(2)}, u32[]{:S(2)}) collective-permute-start(bf16[640,128]{1,0:T(8,128)(2,1)S(1)} %get-tuple-element.37), channel_id=1, source_target_pairs={{0,4},{4,0},{1,5},{5,1},{2,6},{6,2},{3,7},{7,3},{8,12},{12,8},{9,1... | collective-permute-start | bytes 491528 | tf_op jit(solution)/shard_map/ppermute | solution.py:398
  6.1 0.0 copy-done.2
  6.1 0.1 shard_map.37
  6.2 0.1 collective-permute-start
  6.3 1.3 %collective-permute-done.got_ref = bf16[4,96,128]{2,1,0:T(8,128)(2,1)S(1)} collective-permute-done((bf16[4,96,128]{2,1,0:T(8,128)(2,1)S(1)}, bf16[4,96,128]{2,1,0:T(8,128)(2,1)S(1)}, u32[]{:S(2)}, u32[]{:S(2)}) %collective-permute-start) | collective-permute-done | bytes 98336 | tf_op jit(solution)/shard_map/ppermute | solution.py:398
  7.6 1.6 %collective-permute-start.1 = (bf16[2,96,128]{2,1,0:T(8,128)(2,1)S(1)}, bf16[2,96,128]{2,1,0:T(8,128)(2,1)S(1)}, u32[]{:S(2)}, u32[]{:S(2)}) collective-permute-start(bf16[2,96,128]{2,1,0:T(8,128)(2,1)S(1)} %get-tuple-element.29), channel_id=1, source_target_pairs={{0,2},{2,0},{8,10},{10,8},{1,3},{3,1},{9,11},{11,9},{4,6},{6,4},{1... | collective-permute-start | bytes 147464 | tf_op jit(solution)/shard_map/ppermute | solution.py:398
  9.2 1.5 %collective-permute-start.2 = (bf16[2,96,128]{2,1,0:T(8,128)(2,1)S(1)}, bf16[2,96,128]{2,1,0:T(8,128)(2,1)S(1)}, u32[]{:S(2)}, u32[]{:S(2)}) collective-permute-start(bf16[2,96,128]{2,1,0:T(8,128)(2,1)S(1)} %get-tuple-element.30), channel_id=1, source_target_pairs={{0,8},{2,10},{8,0},{10,2},{1,9},{3,11},{9,1},{11,3},{4,12},{6,14},... | collective-permute-start | bytes 147464 | tf_op jit(solution)/shard_map/ppermute | solution.py:398
  10.7 0.4 collective-permute-start.3
  11.1 0.8 %collective-permute-done.1.refs_1_ = bf16[2,96,128]{2,1,0:T(8,128)(2,1)S(1)} collective-permute-done((bf16[2,96,128]{2,1,0:T(8,128)(2,1)S(1)}, bf16[2,96,128]{2,1,0:T(8,128)(2,1)S(1)}, u32[]{:S(2)}, u32[]{:S(2)}) %collective-permute-start.1) | collective-permute-done | bytes 49184 | tf_op jit(solution)/shard_map/ppermute | solution.py:398
  11.9 1.3 %collective-permute-start.7 = (bf16[32,1280]{1,0:T(8,128)(2,1)S(1)}, bf16[32,1280]{1,0:T(8,128)(2,1)S(1)}, u32[]{:S(2)}, u32[]{:S(2)}) collective-permute-start(bf16[32,1280]{1,0:T(8,128)(2,1)S(1)} %shard_map.43), channel_id=1, source_target_pairs={{0,6},{2,4},{4,2},{6,0},{1,7},{3,5},{5,3},{7,1},{8,14},{10,12},{12... | collective-permute-start | bytes 245768 | tf_op jit(solution)/shard_map/ppermute | solution.py:398
  13.2 0.1 collective-permute-done.2.refs_2_
  13.3 2.6 %collective-permute-done.3.refs_3_ = bf16[2,96,128]{2,1,0:T(8,128)(2,1)S(1)} collective-permute-done((bf16[2,96,128]{2,1,0:T(8,128)(2,1)S(1)}, bf16[2,96,128]{2,1,0:T(8,128)(2,1)S(1)}, u32[]{:S(2)}, u32[]{:S(2)}) %collective-permute-start.3) | collective-permute-done | bytes 49184 | tf_op jit(solution)/shard_map/ppermute | solution.py:398
  15.9 0.0 collective-permute-done.6.refs_0_
  15.9 2.3 %collective-permute-done.7.refs_0_ = bf16[32,1280]{1,0:T(8,128)(2,1)S(1)} collective-permute-done((bf16[32,1280]{1,0:T(8,128)(2,1)S(1)}, bf16[32,1280]{1,0:T(8,128)(2,1)S(1)}, u32[]{:S(2)}, u32[]{:S(2)}) %collective-permute-start.7) | collective-permute-done | bytes 81952 | tf_op jit(solution)/shard_map/ppermute | solution.py:398
  18.2 0.0 copy-start.3
  18.2 1.6 %collective-permute-start.8 = (bf16[1152,128]{1,0:T(8,128)(2,1)S(1)}, bf16[1152,128]{1,0:T(8,128)(2,1)S(1)}, u32[]{:S(2)}, u32[]{:S(2)}) collective-permute-start(bf16[1152,128]{1,0:T(8,128)(2,1)S(1)} %shard_map.46), channel_id=1, source_target_pairs={{0,16},{16,0},{1,17},{17,1},{2,18},{18,2},{3,19},{19,3},{4,20},{20... | collective-permute-start | bytes 884744 | tf_op jit(solution)/shard_map/ppermute | solution.py:398
  19.8 1.8 %collective-permute-start.5 = (bf16[256,128]{1,0:T(8,128)(2,1)S(1)}, bf16[256,128]{1,0:T(8,128)(2,1)S(1)}, u32[]{:S(2)}, u32[]{:S(2)}) collective-permute-start(bf16[256,128]{1,0:T(8,128)(2,1)S(1)} %get-tuple-element.36.refs_1_.refs_3_), channel_id=1, source_target_pairs={{0,4},{4,0},{1,5},{5,1},{2,6},{6,2},{3,7},{7,3},{8,12},{12,8},{9,1... | collective-permute-start | bytes 196616 | tf_op jit(solution)/shard_map/ppermute | solution.py:398
  21.6 1.1 %collective-permute-start.4 = (bf16[256,128]{1,0:T(8,128)(2,1)S(1)}, bf16[256,128]{1,0:T(8,128)(2,1)S(1)}, u32[]{:S(2)}, u32[]{:S(2)}) collective-permute-start(bf16[256,128]{1,0:T(8,128)(2,1)S(1)} %get-tuple-element.35.refs_0_.refs_2_.refs_1_), channel_id=1, source_target_pairs={{0,4},{4,0},{1,5},{5,1},{2,6},{6,2},{3,7},{7,3},{8,12},{12,8},{9,1... | collective-permute-start | bytes 196616 | tf_op jit(solution)/shard_map/ppermute | solution.py:398
  22.7 0.0 copy-start.1
  22.7 1.0 %collective-permute-start.14 = (bf16[128,1280]{1,0:T(8,128)(2,1)S(1)}, bf16[128,1280]{1,0:T(8,128)(2,1)S(1)}, u32[]{:S(2)}, u32[]{:S(2)}) collective-permute-start(bf16[128,1280]{1,0:T(8,128)(2,1)S(1)} %shard_map.48), channel_id=1, source_target_pairs={{0,2},{2,0},{1,3},{3,1},{4,6},{6,4},{5,7},{7,5},{8,10},{10,8},{9,1... | collective-permute-start | bytes 983048 | tf_op jit(solution)/shard_map/ppermute | solution.py:398
  23.7 2.3 %collective-permute-start.15 = (bf16[32,1280]{1,0:T(8,128)(2,1)S(1)}, bf16[32,1280]{1,0:T(8,128)(2,1)S(1)}, u32[]{:S(2)}, u32[]{:S(2)}) collective-permute-start(bf16[32,1280]{1,0:T(8,128)(2,1)S(1)} %shard_map.49), channel_id=1, source_target_pairs={{0,6},{2,4},{4,2},{6,0},{1,7},{3,5},{5,3},{7,1},{8,14},{10,12},{12... | collective-permute-start | bytes 245768 | tf_op jit(solution)/shard_map/ppermute | solution.py:398
  26.0 0.3 collective-permute-done.5.refs_5_
  26.3 0.5 collective-permute-start.10
  26.8 1.5 %collective-permute-done.4.refs_4_ = bf16[256,128]{1,0:T(8,128)(2,1)S(1)} collective-permute-done((bf16[256,128]{1,0:T(8,128)(2,1)S(1)}, bf16[256,128]{1,0:T(8,128)(2,1)S(1)}, u32[]{:S(2)}, u32[]{:S(2)}) %collective-permute-start.4) | collective-permute-done | bytes 65568 | tf_op jit(solution)/shard_map/ppermute | solution.py:398
  28.3 0.5 collective-permute-start.9
  28.8 0.1 pad_add_fusion.base_ref
  28.9 0.0 copy-done.3
  28.9 0.7 %shard_map.40 = (f32[256,256]{1,0:T(8,128)S(1)}, f32[256,256]{1,0:T(8,128)S(1)}) custom-call(s32[2]{0:T(128)S(1)} %pad_add_fusion.base_ref, s32[8]{0:T(128)S(1)} %copy-done.3), custom_call_target="tpu_custom_call" | custom-call | tf_op jit(solution)/shard_map/pallas_call | solution.py:244
  29.6 1.2 %collective-permute-done.10.refs_8_ = bf16[256,128]{1,0:T(8,128)(2,1)S(1)} collective-permute-done((bf16[256,128]{1,0:T(8,128)(2,1)S(1)}, bf16[256,128]{1,0:T(8,128)(2,1)S(1)}, u32[]{:S(2)}, u32[]{:S(2)}) %collective-permute-start.10) | collective-permute-done | bytes 65568 | tf_op jit(solution)/shard_map/ppermute | solution.py:398
  30.9 1.7 %collective-permute-done.9.refs_7_ = bf16[256,128]{1,0:T(8,128)(2,1)S(1)} collective-permute-done((bf16[256,128]{1,0:T(8,128)(2,1)S(1)}, bf16[256,128]{1,0:T(8,128)(2,1)S(1)}, u32[]{:S(2)}, u32[]{:S(2)}) %collective-permute-start.9) | collective-permute-done | bytes 65568 | tf_op jit(solution)/shard_map/ppermute | solution.py:398
  32.6 0.0 collective-permute-done.8.refs_6_.refs_7_
  32.6 0.6 %shard_map.47.refs_1_.refs_0_ = bf16[256,128]{1,0:T(8,128)(2,1)S(1)} custom-call(bf16[256,128]{1,0:T(8,128)(2,1)S(1)} %get-tuple-element.32.q_ref, f32[256,256]{1,0:T(8,128)S(1)} %get-tuple-element.33.refs_0_, f32[256,256]{1,0:T(8,128)S(1)} %get-tuple-element.34.refs_1_, bf16[256,128]{1,0:T(8,128)(2,1)S(1)} %get-tuple-element.35.refs_0_.refs_2_.refs_1_, ...), custom_call_target="tpu_custom_call" | custom-call | tf_op jit(solution)/shard_map/pallas_call | solution.py:304
  33.2 2.0 %collective-permute-done.15.refs_0_ = bf16[32,1280]{1,0:T(8,128)(2,1)S(1)} collective-permute-done((bf16[32,1280]{1,0:T(8,128)(2,1)S(1)}, bf16[32,1280]{1,0:T(8,128)(2,1)S(1)}, u32[]{:S(2)}, u32[]{:S(2)}) %collective-permute-start.15) | collective-permute-done | bytes 81952 | tf_op jit(solution)/shard_map/ppermute | solution.py:398
  35.3 0.6 %collective-permute-start.16 = (bf16[64,1280]{1,0:T(8,128)(2,1)S(1)}, bf16[64,1280]{1,0:T(8,128)(2,1)S(1)}, u32[]{:S(2)}, u32[]{:S(2)}) collective-permute-start(bf16[64,1280]{1,0:T(8,128)(2,1)S(1)} %shard_map.51.refs_8_), channel_id=1, source_target_pairs={{0,16},{16,0},{1,17},{17,1},{2,18},{18,2},{3,19},{19,3},{4,20},{20... | collective-permute-start | bytes 491528 | tf_op jit(solution)/shard_map/ppermute | solution.py:398
  35.8 0.0 collective-permute-start.11
  35.8 1.5 %collective-permute-start.12 = (bf16[256,128]{1,0:T(8,128)(2,1)S(1)}, bf16[256,128]{1,0:T(8,128)(2,1)S(1)}, u32[]{:S(2)}, u32[]{:S(2)}) collective-permute-start(bf16[256,128]{1,0:T(8,128)(2,1)S(1)} %shard_map.47.refs_1_.refs_0_), channel_id=1, source_target_pairs={{0,8},{2,10},{8,0},{10,2},{1,9},{3,11},{9,1},{11,3},{4,12},{6,14},... | collective-permute-start | bytes 196616 | tf_op jit(solution)/shard_map/ppermute | solution.py:398
  37.3 2.0 %collective-permute-start.13 = (bf16[256,128]{1,0:T(8,128)(2,1)S(1)}, bf16[256,128]{1,0:T(8,128)(2,1)S(1)}, u32[]{:S(2)}, u32[]{:S(2)}) collective-permute-start(bf16[256,128]{1,0:T(8,128)(2,1)S(1)} %shard_map.47.refs_1_.refs_0_), channel_id=1, source_target_pairs={{0,10},{2,8},{8,2},{10,0},{1,11},{3,9},{9,3},{11,1},{4,14},{6,12},... | collective-permute-start | bytes 196616 | tf_op jit(solution)/shard_map/ppermute | solution.py:398
  39.3 0.1 stack.55.at_ref
  39.4 0.0 collective-permute-done.14.refs_5_
  39.4 0.7 %collective-permute-done.11.refs_1_ = bf16[256,128]{1,0:T(8,128)(2,1)S(1)} collective-permute-done((bf16[256,128]{1,0:T(8,128)(2,1)S(1)}, bf16[256,128]{1,0:T(8,128)(2,1)S(1)}, u32[]{:S(2)}, u32[]{:S(2)}) %collective-permute-start.11) | collective-permute-done | bytes 65568 | tf_op jit(solution)/shard_map/ppermute | solution.py:398
  40.1 0.2 collective-permute-done.12.refs_2_
  40.3 2.2 %collective-permute-done.13.refs_3_ = bf16[256,128]{1,0:T(8,128)(2,1)S(1)} collective-permute-done((bf16[256,128]{1,0:T(8,128)(2,1)S(1)}, bf16[256,128]{1,0:T(8,128)(2,1)S(1)}, u32[]{:S(2)}, u32[]{:S(2)}) %collective-permute-start.13) | collective-permute-done | bytes 65568 | tf_op jit(solution)/shard_map/ppermute | solution.py:398
  42.5 0.0 collective-permute-done.16.refs_9_
  42.5 0.0 copy-done.1
  42.5 1.3 %shard_map.52 = (bf16[4,32,1280]{2,1,0:T(8,128)(2,1)S(1)}, bf16[4,32,1280]{2,1,0:T(8,128)(2,1)S(1)}) custom-call(s32[6]{0:T(128)S(1)} %stack.55.at_ref, s32[1]{0:T(128)} %bitcast.place_ref, bf16[256,128]{1,0:T(8,128)(2,1)S(1)} %shard_map.47.refs_1_.refs_0_, bf16[256,128]{1,0:T(8,128)(2,1)S(1)} %collective-permute-done.11.refs_1_, ...), custom_call_target="tpu_custom_call" | custom-call | tf_op jit(solution)/shard_map/pallas_call | solution.py:347
  43.8 0.1 collective-permute-start.17
  43.9 1.6 %collective-permute-done.17.y_ref = bf16[4,32,1280]{2,1,0:T(8,128)(2,1)S(1)} collective-permute-done((bf16[4,32,1280]{2,1,0:T(8,128)(2,1)S(1)}, bf16[4,32,1280]{2,1,0:T(8,128)(2,1)S(1)}, u32[]{:S(2)}, u32[]{:S(2)}) %collective-permute-start.17) | collective-permute-done | bytes 327712 | tf_op jit(solution)/shard_map/ppermute | solution.py:398
  45.5 0.1 shard_map.53
  45.6 2.1 %collective-permute-start.18 = (bf16[32,1280]{1,0:T(8,128)(2,1)S(1)}, bf16[32,1280]{1,0:T(8,128)(2,1)S(1)}, u32[]{:S(2)}, u32[]{:S(2)}) collective-permute-start(bf16[32,1280]{1,0:T(8,128)(2,1)S(1)} %get-tuple-element.44), channel_id=1, source_target_pairs={{0,2},{2,0},{8,10},{10,8},{1,3},{3,1},{9,11},{11,9},{4,6},{6,4},{1... | collective-permute-start | bytes 245768 | tf_op jit(solution)/shard_map/ppermute | solution.py:398
  47.6 0.5 collective-permute-start.19
  48.2 1.0 %collective-permute-start.20 = (bf16[32,1280]{1,0:T(8,128)(2,1)S(1)}, bf16[32,1280]{1,0:T(8,128)(2,1)S(1)}, u32[]{:S(2)}, u32[]{:S(2)}) collective-permute-start(bf16[32,1280]{1,0:T(8,128)(2,1)S(1)} %get-tuple-element.46), channel_id=1, source_target_pairs={{0,10},{2,8},{8,2},{10,0},{1,11},{3,9},{9,3},{11,1},{4,14},{6,12},... | collective-permute-start | bytes 245768 | tf_op jit(solution)/shard_map/ppermute | solution.py:398
  49.2 1.2 %collective-permute-done.18.refs_1_ = bf16[32,1280]{1,0:T(8,128)(2,1)S(1)} collective-permute-done((bf16[32,1280]{1,0:T(8,128)(2,1)S(1)}, bf16[32,1280]{1,0:T(8,128)(2,1)S(1)}, u32[]{:S(2)}, u32[]{:S(2)}) %collective-permute-start.18) | collective-permute-done | bytes 81952 | tf_op jit(solution)/shard_map/ppermute | solution.py:398
  50.4 3.5 %collective-permute-done.19.refs_2_ = bf16[32,1280]{1,0:T(8,128)(2,1)S(1)} collective-permute-done((bf16[32,1280]{1,0:T(8,128)(2,1)S(1)}, bf16[32,1280]{1,0:T(8,128)(2,1)S(1)}, u32[]{:S(2)}, u32[]{:S(2)}) %collective-permute-start.19) | collective-permute-done | bytes 81952 | tf_op jit(solution)/shard_map/ppermute | solution.py:398
  53.8 0.0 collective-permute-done.20.refs_3_
  53.8 0.8 %shard_map.54 = bf16[32,5120]{1,0:T(8,128)(2,1)} custom-call(s32[1]{0:T(128)} %bitcast.place_ref, bf16[32,1280]{1,0:T(8,128)(2,1)S(1)} %get-tuple-element.43.refs_0_, bf16[32,1280]{1,0:T(8,128)(2,1)S(1)} %collective-permute-done.18.refs_1_, bf16[32,1280]{1,0:T(8,128)(2,1)S(1)} %collective-permute-done.19.refs_2_, ...), custom_call_target="tpu_custom_call" | custom-call | tf_op jit(solution)/shard_map/pallas_call | solution.py:387
  (12 shorter events, 0.1 us)
Async XLA Ops:
  0.1 1.3 %copy-start = (bf16[128,5120]{1,0:T(8,128)(2,1)S(1)}, bf16[128,5120]{1,0:T(8,128)(2,1)}, u32[]{:S(2)}) copy-start(bf16[128,5120]{1,0:T(8,128)(2,1)} %refs_4_.1) | copy-start | bytes 3932164
  1.4 4.7 %copy-start.2 = (bf16[3,32,1024]{2,1,0:T(8,128)(2,1)S(1)}, bf16[3,32,1024]{2,1,0:T(8,128)(2,1)}, u32[]{:S(2)}) copy-start(bf16[3,32,1024]{2,1,0:T(8,128)(2,1)} %x_ref.2) | copy-start | bytes 589828
  2.0 13.9 %collective-permute-start.6 = (bf16[640,128]{1,0:T(8,128)(2,1)S(1)}, bf16[640,128]{1,0:T(8,128)(2,1)S(1)}, u32[]{:S(2)}, u32[]{:S(2)}) collective-permute-start(bf16[640,128]{1,0:T(8,128)(2,1)S(1)} %get-tuple-element.37), channel_id=1, source_target_pairs={{0,4},{4,0},{1,5},{5,1},{2,6},{6,2},{3,7},{7,3},{8,12},{12,8},{9,1... | collective-permute-start | bytes 491528 | tf_op jit(solution)/shard_map/ppermute | solution.py:398
  6.2 1.4 %collective-permute-start = (bf16[4,96,128]{2,1,0:T(8,128)(2,1)S(1)}, bf16[4,96,128]{2,1,0:T(8,128)(2,1)S(1)}, u32[]{:S(2)}, u32[]{:S(2)}) collective-permute-start(bf16[4,96,128]{2,1,0:T(8,128)(2,1)S(1)} %get-tuple-element.27), channel_id=1, source_target_pairs={{0,1},{1,0},{2,3},{3,2},{4,5},{5,4},{6,7},{7,6},{8,9},{9,8},{10,11... | collective-permute-start | bytes 294920 | tf_op jit(solution)/shard_map/ppermute | solution.py:398
  7.6 4.3 %collective-permute-start.1 = (bf16[2,96,128]{2,1,0:T(8,128)(2,1)S(1)}, bf16[2,96,128]{2,1,0:T(8,128)(2,1)S(1)}, u32[]{:S(2)}, u32[]{:S(2)}) collective-permute-start(bf16[2,96,128]{2,1,0:T(8,128)(2,1)S(1)} %get-tuple-element.29), channel_id=1, source_target_pairs={{0,2},{2,0},{8,10},{10,8},{1,3},{3,1},{9,11},{11,9},{4,6},{6,4},{1... | collective-permute-start | bytes 147464 | tf_op jit(solution)/shard_map/ppermute | solution.py:398
  9.2 4.1 %collective-permute-start.2 = (bf16[2,96,128]{2,1,0:T(8,128)(2,1)S(1)}, bf16[2,96,128]{2,1,0:T(8,128)(2,1)S(1)}, u32[]{:S(2)}, u32[]{:S(2)}) collective-permute-start(bf16[2,96,128]{2,1,0:T(8,128)(2,1)S(1)} %get-tuple-element.30), channel_id=1, source_target_pairs={{0,8},{2,10},{8,0},{10,2},{1,9},{3,11},{9,1},{11,3},{4,12},{6,14},... | collective-permute-start | bytes 147464 | tf_op jit(solution)/shard_map/ppermute | solution.py:398
  10.7 5.2 %collective-permute-start.3 = (bf16[2,96,128]{2,1,0:T(8,128)(2,1)S(1)}, bf16[2,96,128]{2,1,0:T(8,128)(2,1)S(1)}, u32[]{:S(2)}, u32[]{:S(2)}) collective-permute-start(bf16[2,96,128]{2,1,0:T(8,128)(2,1)S(1)} %get-tuple-element.31), channel_id=1, source_target_pairs={{0,10},{2,8},{8,2},{10,0},{1,11},{3,9},{9,3},{11,1},{4,14},{6,12},... | collective-permute-start | bytes 147464 | tf_op jit(solution)/shard_map/ppermute | solution.py:398
  11.9 6.3 %collective-permute-start.7 = (bf16[32,1280]{1,0:T(8,128)(2,1)S(1)}, bf16[32,1280]{1,0:T(8,128)(2,1)S(1)}, u32[]{:S(2)}, u32[]{:S(2)}) collective-permute-start(bf16[32,1280]{1,0:T(8,128)(2,1)S(1)} %shard_map.43), channel_id=1, source_target_pairs={{0,6},{2,4},{4,2},{6,0},{1,7},{3,5},{5,3},{7,1},{8,14},{10,12},{12... | collective-permute-start | bytes 245768 | tf_op jit(solution)/shard_map/ppermute | solution.py:398
  18.2 10.7 %copy-start.3 = (s32[8]{0:T(128)S(1)}, s32[8]{0:T(128)}, u32[]{:S(2)}) copy-start(s32[8]{0:T(128)} %clip_ref.1) | copy-start | bytes 100
  18.2 14.4 %collective-permute-start.8 = (bf16[1152,128]{1,0:T(8,128)(2,1)S(1)}, bf16[1152,128]{1,0:T(8,128)(2,1)S(1)}, u32[]{:S(2)}, u32[]{:S(2)}) collective-permute-start(bf16[1152,128]{1,0:T(8,128)(2,1)S(1)} %shard_map.46), channel_id=1, source_target_pairs={{0,16},{16,0},{1,17},{17,1},{2,18},{18,2},{3,19},{19,3},{4,20},{20... | collective-permute-start | bytes 884744 | tf_op jit(solution)/shard_map/ppermute | solution.py:398
  19.8 6.5 %collective-permute-start.5 = (bf16[256,128]{1,0:T(8,128)(2,1)S(1)}, bf16[256,128]{1,0:T(8,128)(2,1)S(1)}, u32[]{:S(2)}, u32[]{:S(2)}) collective-permute-start(bf16[256,128]{1,0:T(8,128)(2,1)S(1)} %get-tuple-element.36.refs_1_.refs_3_), channel_id=1, source_target_pairs={{0,4},{4,0},{1,5},{5,1},{2,6},{6,2},{3,7},{7,3},{8,12},{12,8},{9,1... | collective-permute-start | bytes 196616 | tf_op jit(solution)/shard_map/ppermute | solution.py:398
  21.6 6.7 %collective-permute-start.4 = (bf16[256,128]{1,0:T(8,128)(2,1)S(1)}, bf16[256,128]{1,0:T(8,128)(2,1)S(1)}, u32[]{:S(2)}, u32[]{:S(2)}) collective-permute-start(bf16[256,128]{1,0:T(8,128)(2,1)S(1)} %get-tuple-element.35.refs_0_.refs_2_.refs_1_), channel_id=1, source_target_pairs={{0,4},{4,0},{1,5},{5,1},{2,6},{6,2},{3,7},{7,3},{8,12},{12,8},{9,1... | collective-permute-start | bytes 196616 | tf_op jit(solution)/shard_map/ppermute | solution.py:398
  22.7 19.8 %copy-start.1 = (bf16[128,5120]{1,0:T(8,128)(2,1)S(1)}, bf16[128,5120]{1,0:T(8,128)(2,1)}, u32[]{:S(2)}) copy-start(bf16[128,5120]{1,0:T(8,128)(2,1)} %refs_4_.1) | copy-start | bytes 3932164
  22.7 16.7 %collective-permute-start.14 = (bf16[128,1280]{1,0:T(8,128)(2,1)S(1)}, bf16[128,1280]{1,0:T(8,128)(2,1)S(1)}, u32[]{:S(2)}, u32[]{:S(2)}) collective-permute-start(bf16[128,1280]{1,0:T(8,128)(2,1)S(1)} %shard_map.48), channel_id=1, source_target_pairs={{0,2},{2,0},{1,3},{3,1},{4,6},{6,4},{5,7},{7,5},{8,10},{10,8},{9,1... | collective-permute-start | bytes 983048 | tf_op jit(solution)/shard_map/ppermute | solution.py:398
  23.7 11.5 %collective-permute-start.15 = (bf16[32,1280]{1,0:T(8,128)(2,1)S(1)}, bf16[32,1280]{1,0:T(8,128)(2,1)S(1)}, u32[]{:S(2)}, u32[]{:S(2)}) collective-permute-start(bf16[32,1280]{1,0:T(8,128)(2,1)S(1)} %shard_map.49), channel_id=1, source_target_pairs={{0,6},{2,4},{4,2},{6,0},{1,7},{3,5},{5,3},{7,1},{8,14},{10,12},{12... | collective-permute-start | bytes 245768 | tf_op jit(solution)/shard_map/ppermute | solution.py:398
  26.3 4.6 %collective-permute-start.10 = (bf16[256,128]{1,0:T(8,128)(2,1)S(1)}, bf16[256,128]{1,0:T(8,128)(2,1)S(1)}, u32[]{:S(2)}, u32[]{:S(2)}) collective-permute-start(bf16[256,128]{1,0:T(8,128)(2,1)S(1)} %collective-permute-done.5.refs_5_), channel_id=1, source_target_pairs={{0,16},{16,0},{1,17},{17,1},{2,18},{18,2},{3,19},{19,3},{4,20},{20... | collective-permute-start | bytes 196616 | tf_op jit(solution)/shard_map/ppermute | solution.py:398
  28.3 4.3 %collective-permute-start.9 = (bf16[256,128]{1,0:T(8,128)(2,1)S(1)}, bf16[256,128]{1,0:T(8,128)(2,1)S(1)}, u32[]{:S(2)}, u32[]{:S(2)}) collective-permute-start(bf16[256,128]{1,0:T(8,128)(2,1)S(1)} %collective-permute-done.4.refs_4_), channel_id=1, source_target_pairs={{0,16},{16,0},{1,17},{17,1},{2,18},{18,2},{3,19},{19,3},{4,20},{20... | collective-permute-start | bytes 196616 | tf_op jit(solution)/shard_map/ppermute | solution.py:398
  35.3 7.2 %collective-permute-start.16 = (bf16[64,1280]{1,0:T(8,128)(2,1)S(1)}, bf16[64,1280]{1,0:T(8,128)(2,1)S(1)}, u32[]{:S(2)}, u32[]{:S(2)}) collective-permute-start(bf16[64,1280]{1,0:T(8,128)(2,1)S(1)} %shard_map.51.refs_8_), channel_id=1, source_target_pairs={{0,16},{16,0},{1,17},{17,1},{2,18},{18,2},{3,19},{19,3},{4,20},{20... | collective-permute-start | bytes 491528 | tf_op jit(solution)/shard_map/ppermute | solution.py:398
  35.8 4.3 %collective-permute-start.11 = (bf16[256,128]{1,0:T(8,128)(2,1)S(1)}, bf16[256,128]{1,0:T(8,128)(2,1)S(1)}, u32[]{:S(2)}, u32[]{:S(2)}) collective-permute-start(bf16[256,128]{1,0:T(8,128)(2,1)S(1)} %shard_map.47.refs_1_.refs_0_), channel_id=1, source_target_pairs={{0,2},{2,0},{8,10},{10,8},{1,3},{3,1},{9,11},{11,9},{4,6},{6,4},{1... | collective-permute-start | bytes 196616 | tf_op jit(solution)/shard_map/ppermute | solution.py:398
  35.8 4.5 %collective-permute-start.12 = (bf16[256,128]{1,0:T(8,128)(2,1)S(1)}, bf16[256,128]{1,0:T(8,128)(2,1)S(1)}, u32[]{:S(2)}, u32[]{:S(2)}) collective-permute-start(bf16[256,128]{1,0:T(8,128)(2,1)S(1)} %shard_map.47.refs_1_.refs_0_), channel_id=1, source_target_pairs={{0,8},{2,10},{8,0},{10,2},{1,9},{3,11},{9,1},{11,3},{4,12},{6,14},... | collective-permute-start | bytes 196616 | tf_op jit(solution)/shard_map/ppermute | solution.py:398
  37.3 5.2 %collective-permute-start.13 = (bf16[256,128]{1,0:T(8,128)(2,1)S(1)}, bf16[256,128]{1,0:T(8,128)(2,1)S(1)}, u32[]{:S(2)}, u32[]{:S(2)}) collective-permute-start(bf16[256,128]{1,0:T(8,128)(2,1)S(1)} %shard_map.47.refs_1_.refs_0_), channel_id=1, source_target_pairs={{0,10},{2,8},{8,2},{10,0},{1,11},{3,9},{9,3},{11,1},{4,14},{6,12},... | collective-permute-start | bytes 196616 | tf_op jit(solution)/shard_map/ppermute | solution.py:398
  43.8 1.7 %collective-permute-start.17 = (bf16[4,32,1280]{2,1,0:T(8,128)(2,1)S(1)}, bf16[4,32,1280]{2,1,0:T(8,128)(2,1)S(1)}, u32[]{:S(2)}, u32[]{:S(2)}) collective-permute-start(bf16[4,32,1280]{2,1,0:T(8,128)(2,1)S(1)} %get-tuple-element.42), channel_id=1, source_target_pairs={{0,1},{1,0},{2,3},{3,2},{4,5},{5,4},{6,7},{7,6},{8,9},{9,8},{10,11... | collective-permute-start | bytes 983048 | tf_op jit(solution)/shard_map/ppermute | solution.py:398
  45.6 4.8 %collective-permute-start.18 = (bf16[32,1280]{1,0:T(8,128)(2,1)S(1)}, bf16[32,1280]{1,0:T(8,128)(2,1)S(1)}, u32[]{:S(2)}, u32[]{:S(2)}) collective-permute-start(bf16[32,1280]{1,0:T(8,128)(2,1)S(1)} %get-tuple-element.44), channel_id=1, source_target_pairs={{0,2},{2,0},{8,10},{10,8},{1,3},{3,1},{9,11},{11,9},{4,6},{6,4},{1... | collective-permute-start | bytes 245768 | tf_op jit(solution)/shard_map/ppermute | solution.py:398
  47.6 6.2 %collective-permute-start.19 = (bf16[32,1280]{1,0:T(8,128)(2,1)S(1)}, bf16[32,1280]{1,0:T(8,128)(2,1)S(1)}, u32[]{:S(2)}, u32[]{:S(2)}) collective-permute-start(bf16[32,1280]{1,0:T(8,128)(2,1)S(1)} %get-tuple-element.45), channel_id=1, source_target_pairs={{0,8},{2,10},{8,0},{10,2},{1,9},{3,11},{9,1},{11,3},{4,12},{6,14},... | collective-permute-start | bytes 245768 | tf_op jit(solution)/shard_map/ppermute | solution.py:398
  48.2 5.7 %collective-permute-start.20 = (bf16[32,1280]{1,0:T(8,128)(2,1)S(1)}, bf16[32,1280]{1,0:T(8,128)(2,1)S(1)}, u32[]{:S(2)}, u32[]{:S(2)}) collective-permute-start(bf16[32,1280]{1,0:T(8,128)(2,1)S(1)} %get-tuple-element.46), channel_id=1, source_target_pairs={{0,10},{2,8},{8,2},{10,0},{1,11},{3,9},{9,3},{11,1},{4,14},{6,12},... | collective-permute-start | bytes 245768 | tf_op jit(solution)/shard_map/ppermute | solution.py:398

commit v19 on v17

--- a/solution.py
+++ b/solution.py
@@ -79,28 +79,45 @@
     )
 
 
-def pieces_kernel(at_ref, x_ref, far_ref, corner_ref, near_ref):
+def blocks_kernel(row_axis, col_axes, x_ref, out_ref, held, sem):
+    depth, cols = held.shape
+    col = 0
+    for axis in col_axes:
+        col = col * lax.axis_size(axis) + lax.axis_index(axis)
+    piece = x_ref.at[rows_at(lax.axis_index(row_axis), depth), rows_at(col, cols)]
+    copy = pltpu.make_async_copy(piece, held, sem)
+    copy.start()
+    copy.wait()
+    for j in range(cols // LANES):
+        out_ref[j * depth:(j + 1) * depth, :] = held[:, j * LANES:(j + 1) * LANES]
+
+
+def blocks(x, depth, cols, row_axis, col_axes):
+    return pl.pallas_call(
+        functools.partial(blocks_kernel, row_axis, col_axes),
+        out_shape=jax.ShapeDtypeStruct((cols // LANES * depth, LANES), x.dtype),
+        in_specs=[pl.BlockSpec(memory_space=pltpu.HBM)],
+        out_specs=VMEM,
+        scratch_shapes=[pltpu.VMEM((depth, cols), x.dtype), pltpu.SemaphoreType.DMA],
+        compiler_params=PARAMS,
+    )(pltpu.with_memory_space_constraint(x, pltpu.HBM))
+
+
+def pieces_kernel(at_ref, x_ref, corner_ref, near_ref):
     half, cols = corner_ref.shape
-    rows = rows_at(at_ref[0], half)
-    count = cols // LANES
-    for j in range(count):
-        far_ref[j * half:(j + 1) * half, :] = x_ref[rows, rows_at(at_ref[1] * count + j, LANES)]
-    corner_ref[...] = x_ref[rows, rows_at(at_ref[2], cols)]
-    near_ref[...] = x_ref[:, rows_at(at_ref[2], cols)]
-
-
-def pieces(x, half, first_at, second_at, cols):
+    corner_ref[...] = x_ref[rows_at(at_ref[0], half), rows_at(at_ref[1], cols)]
+    near_ref[...] = x_ref[:, rows_at(at_ref[1], cols)]
+
+
+def pieces(x, half, at, cols):
+    depth = x.shape[0]
     return pl.pallas_call(
         pieces_kernel,
-        out_shape=(
-            jax.ShapeDtypeStruct((cols // LANES * (x.shape[0] // 2), LANES), x.dtype),
-            jax.ShapeDtypeStruct((x.shape[0] // 2, cols), x.dtype),
-            jax.ShapeDtypeStruct((x.shape[0], cols), x.dtype),
-        ),
+        out_shape=[jax.ShapeDtypeStruct((rows, cols), x.dtype) for rows in (depth // 2, depth)],
         in_specs=[SMEM, VMEM],
-        out_specs=(VMEM, VMEM, VMEM),
-        compiler_params=PARAMS,
-    )(index_array(half, first_at, second_at), x)
+        out_specs=[VMEM, VMEM],
+        compiler_params=PARAMS,
+    )(index_array(half, at), x)
 
 
 def lane_kernel(head_dim, core_ref, x_ref, mine_ref, theirs_ref):
@@ -311,13 +328,16 @@
 
 
 def project_kernel(n_attn, sizes, at_ref, place_ref, *refs):
-    attn_refs, w_refs = refs[:n_attn], refs[n_attn:-4]
-    mine_ref, theirs_ref, a_ref, w_all = refs[-4:]
+    attn_refs, w_refs = refs[:n_attn], refs[n_attn:-3]
+    out_ref, a_ref, w_all = refs[-3:]
     width = attn_refs[0].shape[1]
-    blks, tok, cols = mine_ref.shape
-    blk, core = place_ref[0] // 2, place_ref[0] % 2
+    blks, tok, cols = out_ref.shape
+    blk, other = place_ref[0] // 2, 1 - place_ref[0] % 2
     for k, ref in enumerate(attn_refs):
-        a_ref[:, rows_at(blk ^ k, width)] = ref[...]
+        at = rows_at(blk ^ k, width)
+        for b in range(blks):
+            a_ref[b * tok:(b + 1) * tok, at] = ref[rows_at(2 * b + other, tok), :]
+            a_ref[(blks + b) * tok:(blks + b + 1) * tok, at] = ref[rows_at(2 * b + 1 - other, tok), :]
     for i, (ref, rows) in enumerate(zip(w_refs, sizes)):
         at = rows_at(at_ref[i], rows)
         if ref.shape[1] >= cols:
@@ -326,35 +346,40 @@
             first = ref.shape[0] - cols // LANES * rows
             for j in range(cols // LANES):
                 w_all[at, j * LANES:(j + 1) * LANES] = ref[first + j * rows:first + (j + 1) * rows]
-    result = jnp.dot(a_ref[...], w_all[...], preferred_element_type=jnp.float32)
-    result = result.astype(mine_ref.dtype).reshape(blks, 2, tok, cols)
-
-    @pl.when(core == 0)
-    def _():
-        mine_ref[...] = result[:, 0]
-        theirs_ref[...] = result[:, 1]
-
-    @pl.when(core != 0)
-    def _():
-        mine_ref[...] = result[:, 1]
-        theirs_ref[...] = result[:, 0]
+    dot = jnp.dot(a_ref[:blks * tok, :], w_all[...], preferred_element_type=jnp.float32)
+    out_ref[...] = dot.astype(out_ref.dtype).reshape(out_ref.shape)
+
+
+def rest_kernel(a_ref, w_ref, out_ref):
+    blks, tok, _ = out_ref.shape
+    dot = jnp.dot(a_ref[blks * tok:, :], w_ref[...], preferred_element_type=jnp.float32)
+    out_ref[...] = dot.astype(out_ref.dtype).reshape(out_ref.shape)
 
 
 def project(attns, w_parts, sizes, at, place, tok, cols):
     count, width = attns[0].shape
-    blks = len(attns)
-    like = jax.ShapeDtypeStruct((blks, tok, cols), attns[0].dtype)
-    return pl.pallas_call(
+    blks, dtype = len(attns), attns[0].dtype
+    like = jax.ShapeDtypeStruct((blks, tok, cols), dtype)
+    theirs, a_all, w_all = pl.pallas_call(
         functools.partial(project_kernel, blks, sizes),
-        out_shape=(like, like),
+        out_shape=(
+            like,
+            jax.ShapeDtypeStruct((count, blks * width), dtype),
+            jax.ShapeDtypeStruct((blks * width, cols), dtype),
+        ),
         in_specs=[SMEM, SMEM] + [VMEM] * (blks + len(w_parts)),
-        out_specs=(VMEM, VMEM),
-        scratch_shapes=[
-            pltpu.VMEM((count, blks * width), attns[0].dtype),
-            pltpu.VMEM((blks * width, cols), attns[0].dtype),
-        ],
+        out_specs=(VMEM, VMEM, VMEM),
         compiler_params=PARAMS,
     )(index_array(*at), place, *attns, *w_parts)
+    got = xor(theirs, ("core",), 1)
+    ours = pl.pallas_call(
+        rest_kernel,
+        out_shape=like,
+        in_specs=[VMEM, VMEM],
+        out_specs=VMEM,
+        compiler_params=PARAMS,
+    )(a_all, w_all)
+    return add(ours, got, place)
 
 
 def add_kernel(place_ref, x_ref, y_ref, *out_refs):
@@ -399,8 +424,7 @@
 
 
 def swap_all(parts, axis):
-    last_first = [xor(parts[m], axis, m) for m in range(len(parts) - 1, 0, -1)]
-    return [parts[0]] + last_first[::-1]
+    return [parts[0]] + [xor(parts[m], axis, m) for m in range(1, len(parts))]
 
 
 def squares(qkv, frame_clip, w_out):
@@ -408,11 +432,12 @@
     y, x, zh, zl, core = (lax.axis_index(n) for n in ("y", "x", "zh", "zl", "core"))
     tok, head_dim, cols = qkv.shape[1], w_out.shape[0], w_out.shape[1] // 4
     place = index_array((x * 2 + zl) * 2 + core)
-    mine, theirs = x * 2 + zl, x * 2 + 1 - zl
+    theirs = x * 2 + 1 - zl
     row, half = zh * 2 + zl, head_dim // 2
 
-    w_far, w_corner, w_near = pieces(w_out, y, mine, theirs, cols)
+    w_far = blocks(w_out, half, cols, "y", quarter)
     far = after(xor(w_far, ("zh",), 1), cost=AHEAD)
+    w_corner, w_near = pieces(w_out, y, theirs, cols)
     kept, given = lanes(qkv, core, head_dim)
     shared = swap_all(deal(kept, xor(given, ("core",), 1), place), quarter)
     q, k, v = sort(shared, place)
@@ -431,8 +456,7 @@
     w_parts = [w_out, w_next, far, near, corner, corner_rest]
     sizes = [head_dim, head_dim, half, half, half, half]
     at = [row, row ^ 1] + [2 * (row ^ by) + h for by in (2, 3) for h in (y, 1 - y)]
-    ours, other_core = project(attns, w_parts, sizes, at, place, tok, cols)
-    parts = add(ours, xor(other_core, ("core",), 1), place)
+    parts = project(attns, w_parts, sizes, at, place, tok, cols)
     return unpack(swap_all(parts, quarter), place)
 
 
@@ -453,8 +477,7 @@
     attn = attention(q, kvs, mask_of, [0] * rows, head_dim)
     attns = swap_all([attn] * blks, ("blk",))
     at = [row ^ by for by in range(rows)]
-    ours, other_core = project(attns, w_parts, [head_dim] * rows, at, place, tok, cols)
-    parts = add(ours, xor(other_core, ("core",), 1), place)
+    parts = project(attns, w_parts, [head_dim] * rows, at, place, tok, cols)
     return unpack(swap_all(parts, ("blk",)), place)
 
 

time: 53.7 us -> 51.9 us (0.966)
  waiting for transfers between devices: 23.8 us -> 22 us
  local copies, waits for them, and re-layouts: 1.41 us -> 0.1 us
  Pallas kernels: 4.16 us -> 5.23 us
    ppermute x20, waiting for transfers between devices: 23.8 us -> 22 us  [xor(): return lax.ppermute(x, axis, [(i, i ^ by) for i in range(size)])]
    unnamed x8 -> x6, local copies, waits for them, and re-layouts: 1.33 us -> 0.02 us
    pallas_call x1 -> x3, Pallas kernels: 0.62 us -> 1.91 us  [the longest x1 0.99 us: blocks(): pl.pallas_call(functools.partial(blocks_kernel, row_axis, col_axes), out_...]
  transfers between devices with their start and end apart: 20 -> 20, of which waited for: 15 -> 14; matrix products, arithmetic and copies ran while one was open for 0% -> 0% of each run, Pallas kernels for 3% -> 5%
where the time goes in v19:
time: 51.9 us; the launch traced here: 51.7 us
  starting transfers between devices  24.1 us (46%)
  waiting for transfers between devices  22 us (42%)
  Pallas kernels  5.23 us (10%)
    ppermute x20, starting transfers between devices, xor(): return lax.ppermute(x, axis, [(i, i ^ by) for i in range(size)])  24.1 us
    ppermute x20, waiting for transfers between devices, xor(): return lax.ppermute(x, axis, [(i, i ^ by) for i in range(size)])  22 us
    pallas_call x1, Pallas kernels, project(): pl.pallas_call(functools.partial(project_kernel, blks, sizes), out_shape=...  1.04 us
  transfers between devices with their start and end apart: 20, of which 14 were waited for; matrix products, arithmetic and copies ran while one was open for 0% of the time, Pallas kernels for 5%

profile of v19, /device:TPU:0, one launch (start us, length us, event | category | flops | bytes accessed | tf_op | source)
XLA Modules:
  0.0 51.7 jit_solution(3220220110597408357)
XLA Ops:
  0.0 0.0 copy-start.1
  0.0 1.0 %shard_map.41 = bf16[640,128]{1,0:T(8,128)(2,1)S(1)} custom-call(bf16[128,5120]{1,0:T(8,128)(2,1)} %refs_4_.1), custom_call_target="tpu_custom_call" | custom-call | tf_op jit(solution)/shard_map/pallas_call | solution.py:96
  1.0 4.1 %collective-permute-start.6 = (bf16[640,128]{1,0:T(8,128)(2,1)S(1)}, bf16[640,128]{1,0:T(8,128)(2,1)S(1)}, u32[]{:S(2)}, u32[]{:S(2)}) collective-permute-start(bf16[640,128]{1,0:T(8,128)(2,1)S(1)} %shard_map.41), channel_id=1, source_target_pairs={{0,4},{4,0},{1,5},{5,1},{2,6},{6,2},{3,7},{7,3},{8,12},{12,8},{9,1... | collective-permute-start | bytes 491528 | tf_op jit(solution)/shard_map/ppermute | solution.py:423
  5.1 0.0 copy-done.1
  5.1 0.1 shard_map.37
  5.2 0.1 collective-permute-start
  5.3 1.3 %collective-permute-done.got_ref = bf16[4,96,128]{2,1,0:T(8,128)(2,1)S(1)} collective-permute-done((bf16[4,96,128]{2,1,0:T(8,128)(2,1)S(1)}, bf16[4,96,128]{2,1,0:T(8,128)(2,1)S(1)}, u32[]{:S(2)}, u32[]{:S(2)}) %collective-permute-start) | collective-permute-done | bytes 98336 | tf_op jit(solution)/shard_map/ppermute | solution.py:423
  6.5 1.6 %collective-permute-start.1 = (bf16[2,96,128]{2,1,0:T(8,128)(2,1)S(1)}, bf16[2,96,128]{2,1,0:T(8,128)(2,1)S(1)}, u32[]{:S(2)}, u32[]{:S(2)}) collective-permute-start(bf16[2,96,128]{2,1,0:T(8,128)(2,1)S(1)} %get-tuple-element.28), channel_id=1, source_target_pairs={{0,2},{2,0},{8,10},{10,8},{1,3},{3,1},{9,11},{11,9},{4,6},{6,4},{1... | collective-permute-start | bytes 147464 | tf_op jit(solution)/shard_map/ppermute | solution.py:423
  8.2 1.5 %collective-permute-start.2 = (bf16[2,96,128]{2,1,0:T(8,128)(2,1)S(1)}, bf16[2,96,128]{2,1,0:T(8,128)(2,1)S(1)}, u32[]{:S(2)}, u32[]{:S(2)}) collective-permute-start(bf16[2,96,128]{2,1,0:T(8,128)(2,1)S(1)} %get-tuple-element.29), channel_id=1, source_target_pairs={{0,8},{2,10},{8,0},{10,2},{1,9},{3,11},{9,1},{11,3},{4,12},{6,14},... | collective-permute-start | bytes 147464 | tf_op jit(solution)/shard_map/ppermute | solution.py:423
  9.7 0.4 collective-permute-start.3
  10.1 0.8 %collective-permute-done.1.refs_1_ = bf16[2,96,128]{2,1,0:T(8,128)(2,1)S(1)} collective-permute-done((bf16[2,96,128]{2,1,0:T(8,128)(2,1)S(1)}, bf16[2,96,128]{2,1,0:T(8,128)(2,1)S(1)}, u32[]{:S(2)}, u32[]{:S(2)}) %collective-permute-start.1) | collective-permute-done | bytes 49184 | tf_op jit(solution)/shard_map/ppermute | solution.py:423
  10.9 1.4 %collective-permute-done.2.refs_2_ = bf16[2,96,128]{2,1,0:T(8,128)(2,1)S(1)} collective-permute-done((bf16[2,96,128]{2,1,0:T(8,128)(2,1)S(1)}, bf16[2,96,128]{2,1,0:T(8,128)(2,1)S(1)}, u32[]{:S(2)}, u32[]{:S(2)}) %collective-permute-start.2) | collective-permute-done | bytes 49184 | tf_op jit(solution)/shard_map/ppermute | solution.py:423
  12.3 2.6 %collective-permute-done.3.refs_3_ = bf16[2,96,128]{2,1,0:T(8,128)(2,1)S(1)} collective-permute-done((bf16[2,96,128]{2,1,0:T(8,128)(2,1)S(1)}, bf16[2,96,128]{2,1,0:T(8,128)(2,1)S(1)}, u32[]{:S(2)}, u32[]{:S(2)}) %collective-permute-start.3) | collective-permute-done | bytes 49184 | tf_op jit(solution)/shard_map/ppermute | solution.py:423
  14.9 0.0 collective-permute-done.6.refs_0_
  14.9 0.0 copy-start
  14.9 0.0 copy-start.2
  15.0 1.6 %collective-permute-start.7 = (bf16[1152,128]{1,0:T(8,128)(2,1)S(1)}, bf16[1152,128]{1,0:T(8,128)(2,1)S(1)}, u32[]{:S(2)}, u32[]{:S(2)}) collective-permute-start(bf16[1152,128]{1,0:T(8,128)(2,1)S(1)} %shard_map.43), channel_id=1, source_target_pairs={{0,16},{16,0},{1,17},{17,1},{2,18},{18,2},{3,19},{19,3},{4,20},{20... | collective-permute-start | bytes 884744 | tf_op jit(solution)/shard_map/ppermute | solution.py:423
  16.5 0.2 collective-permute-start.5
  16.7 2.8 %collective-permute-start.4 = (bf16[256,128]{1,0:T(8,128)(2,1)S(1)}, bf16[256,128]{1,0:T(8,128)(2,1)S(1)}, u32[]{:S(2)}, u32[]{:S(2)}) collective-permute-start(bf16[256,128]{1,0:T(8,128)(2,1)S(1)} %get-tuple-element.34.refs_0_.refs_2_.refs_1_), channel_id=1, source_target_pairs={{0,4},{4,0},{1,5},{5,1},{2,6},{6,2},{3,7},{7,3},{8,12},{12,8},{9,1... | collective-permute-start | bytes 196616 | tf_op jit(solution)/shard_map/ppermute | solution.py:423
  19.5 0.1 pad_add_fusion.1.at_ref
  19.5 0.0 copy-done
  19.5 0.6 %shard_map.45 = (bf16[64,1280]{1,0:T(8,128)(2,1)S(1)}, bf16[128,1280]{1,0:T(8,128)(2,1)S(1)}) custom-call(s32[2]{0:T(128)S(1)} %pad_add_fusion.1.at_ref, bf16[128,5120]{1,0:T(8,128)(2,1)S(1)} %copy-done), custom_call_target="tpu_custom_call" | custom-call | tf_op jit(solution)/shard_map/pallas_call | solution.py:114
  20.1 0.7 %collective-permute-start.13 = (bf16[128,1280]{1,0:T(8,128)(2,1)S(1)}, bf16[128,1280]{1,0:T(8,128)(2,1)S(1)}, u32[]{:S(2)}, u32[]{:S(2)}) collective-permute-start(bf16[128,1280]{1,0:T(8,128)(2,1)S(1)} %shard_map.46), channel_id=1, source_target_pairs={{0,2},{2,0},{1,3},{3,1},{4,6},{6,4},{5,7},{7,5},{8,10},{10,8},{9,1... | collective-permute-start | bytes 983048 | tf_op jit(solution)/shard_map/ppermute | solution.py:423
  20.8 2.4 %collective-permute-start.14 = (bf16[64,1280]{1,0:T(8,128)(2,1)S(1)}, bf16[64,1280]{1,0:T(8,128)(2,1)S(1)}, u32[]{:S(2)}, u32[]{:S(2)}) collective-permute-start(bf16[64,1280]{1,0:T(8,128)(2,1)S(1)} %shard_map.47), channel_id=1, source_target_pairs={{0,6},{2,4},{4,2},{6,0},{1,7},{3,5},{5,3},{7,1},{8,14},{10,12},{12... | collective-permute-start | bytes 491528 | tf_op jit(solution)/shard_map/ppermute | solution.py:423
  23.3 0.0 collective-permute-done.5.refs_5_
  23.3 0.5 collective-permute-start.9
  23.8 1.5 %collective-permute-done.4.refs_4_ = bf16[256,128]{1,0:T(8,128)(2,1)S(1)} collective-permute-done((bf16[256,128]{1,0:T(8,128)(2,1)S(1)}, bf16[256,128]{1,0:T(8,128)(2,1)S(1)}, u32[]{:S(2)}, u32[]{:S(2)}) %collective-permute-start.4) | collective-permute-done | bytes 65568 | tf_op jit(solution)/shard_map/ppermute | solution.py:423
  25.2 0.5 collective-permute-start.8
  25.8 0.1 pad_add_fusion.base_ref
  25.8 0.0 copy-done.2
  25.8 0.7 %shard_map.40 = (f32[256,256]{1,0:T(8,128)S(1)}, f32[256,256]{1,0:T(8,128)S(1)}) custom-call(s32[2]{0:T(128)S(1)} %pad_add_fusion.base_ref, s32[8]{0:T(128)S(1)} %copy-done.2), custom_call_target="tpu_custom_call" | custom-call | tf_op jit(solution)/shard_map/pallas_call | solution.py:261
  26.5 1.0 %collective-permute-done.9.refs_8_ = bf16[256,128]{1,0:T(8,128)(2,1)S(1)} collective-permute-done((bf16[256,128]{1,0:T(8,128)(2,1)S(1)}, bf16[256,128]{1,0:T(8,128)(2,1)S(1)}, u32[]{:S(2)}, u32[]{:S(2)}) %collective-permute-start.9) | collective-permute-done | bytes 65568 | tf_op jit(solution)/shard_map/ppermute | solution.py:423
  27.5 2.0 %collective-permute-done.8.refs_7_ = bf16[256,128]{1,0:T(8,128)(2,1)S(1)} collective-permute-done((bf16[256,128]{1,0:T(8,128)(2,1)S(1)}, bf16[256,128]{1,0:T(8,128)(2,1)S(1)}, u32[]{:S(2)}, u32[]{:S(2)}) %collective-permute-start.8) | collective-permute-done | bytes 65568 | tf_op jit(solution)/shard_map/ppermute | solution.py:423
  29.5 0.0 collective-permute-done.7.refs_6_.refs_7_
  29.5 0.6 %shard_map.44.refs_1_.refs_0_ = bf16[256,128]{1,0:T(8,128)(2,1)S(1)} custom-call(bf16[256,128]{1,0:T(8,128)(2,1)S(1)} %get-tuple-element.31.q_ref, f32[256,256]{1,0:T(8,128)S(1)} %get-tuple-element.32.refs_0_, f32[256,256]{1,0:T(8,128)S(1)} %get-tuple-element.33.refs_1_, bf16[256,128]{1,0:T(8,128)(2,1)S(1)} %get-tuple-element.34.refs_0_.refs_2_.refs_1_, ...), custom_call_target="tpu_custom_call" | custom-call | tf_op jit(solution)/shard_map/pallas_call | solution.py:321
  30.2 3.5 %collective-permute-done.14.refs_0_ = bf16[64,1280]{1,0:T(8,128)(2,1)S(1)} collective-permute-done((bf16[64,1280]{1,0:T(8,128)(2,1)S(1)}, bf16[64,1280]{1,0:T(8,128)(2,1)S(1)}, u32[]{:S(2)}, u32[]{:S(2)}) %collective-permute-start.14) | collective-permute-done | bytes 163872 | tf_op jit(solution)/shard_map/ppermute | solution.py:423
  33.6 0.5 collective-permute-start.15
  34.1 0.0 collective-permute-start.12
  34.1 0.8 %collective-permute-start.11 = (bf16[256,128]{1,0:T(8,128)(2,1)S(1)}, bf16[256,128]{1,0:T(8,128)(2,1)S(1)}, u32[]{:S(2)}, u32[]{:S(2)}) collective-permute-start(bf16[256,128]{1,0:T(8,128)(2,1)S(1)} %shard_map.44.refs_1_.refs_0_), channel_id=1, source_target_pairs={{0,8},{2,10},{8,0},{10,2},{1,9},{3,11},{9,1},{11,3},{4,12},{6,14},... | collective-permute-start | bytes 196616 | tf_op jit(solution)/shard_map/ppermute | solution.py:423
  35.0 2.7 %collective-permute-start.10 = (bf16[256,128]{1,0:T(8,128)(2,1)S(1)}, bf16[256,128]{1,0:T(8,128)(2,1)S(1)}, u32[]{:S(2)}, u32[]{:S(2)}) collective-permute-start(bf16[256,128]{1,0:T(8,128)(2,1)S(1)} %shard_map.44.refs_1_.refs_0_), channel_id=1, source_target_pairs={{0,2},{2,0},{8,10},{10,8},{1,3},{3,1},{9,11},{11,9},{4,6},{6,4},{1... | collective-permute-start | bytes 196616 | tf_op jit(solution)/shard_map/ppermute | solution.py:423
  37.6 0.1 stack.52.at_ref
  37.7 0.0 collective-permute-done.13.refs_5_
  37.7 1.6 %collective-permute-done.12.refs_3_ = bf16[256,128]{1,0:T(8,128)(2,1)S(1)} collective-permute-done((bf16[256,128]{1,0:T(8,128)(2,1)S(1)}, bf16[256,128]{1,0:T(8,128)(2,1)S(1)}, u32[]{:S(2)}, u32[]{:S(2)}) %collective-permute-start.12) | collective-permute-done | bytes 65568 | tf_op jit(solution)/shard_map/ppermute | solution.py:423
  39.3 0.0 collective-permute-done.11.refs_2_
  39.3 0.6 %collective-permute-done.10.refs_1_ = bf16[256,128]{1,0:T(8,128)(2,1)S(1)} collective-permute-done((bf16[256,128]{1,0:T(8,128)(2,1)S(1)}, bf16[256,128]{1,0:T(8,128)(2,1)S(1)}, u32[]{:S(2)}, u32[]{:S(2)}) %collective-permute-start.10) | collective-permute-done | bytes 65568 | tf_op jit(solution)/shard_map/ppermute | solution.py:423
  39.8 0.0 collective-permute-done.15.refs_9_
  39.9 1.0 %shard_map.49 = (bf16[4,32,1280]{2,1,0:T(8,128)(2,1)S(1)}, bf16[256,512]{1,0:T(8,128)(2,1)S(1)}, bf16[512,1280]{1,0:T(8,128)(2,1)S(1)}) custom-call(s32[6]{0:T(128)S(1)} %stack.52.at_ref, s32[1]{0:T(128)} %bitcast.place_ref, bf16[256,128]{1,0:T(8,128)(2,1)S(1)} %shard_map.44.refs_1_.refs_0_, bf16[256,128]{1,0:T(8,128)(2,1)S(1)} %collective-permute-done.10.refs_1_, ...), custom_call_target="tpu_custom_call" | custom-call | tf_op jit(solution)/shard_map/pallas_call | solution.py:363
  40.9 0.1 collective-permute-start.16
  41.0 0.3 shard_map.50.x_ref
  41.3 1.3 %collective-permute-done.16.y_ref = bf16[4,32,1280]{2,1,0:T(8,128)(2,1)S(1)} collective-permute-done((bf16[4,32,1280]{2,1,0:T(8,128)(2,1)S(1)}, bf16[4,32,1280]{2,1,0:T(8,128)(2,1)S(1)}, u32[]{:S(2)}, u32[]{:S(2)}) %collective-permute-start.16) | collective-permute-done | bytes 327712 | tf_op jit(solution)/shard_map/ppermute | solution.py:423
  42.6 0.1 shard_map.51
  42.7 2.1 %collective-permute-start.17 = (bf16[32,1280]{1,0:T(8,128)(2,1)S(1)}, bf16[32,1280]{1,0:T(8,128)(2,1)S(1)}, u32[]{:S(2)}, u32[]{:S(2)}) collective-permute-start(bf16[32,1280]{1,0:T(8,128)(2,1)S(1)} %get-tuple-element.42), channel_id=1, source_target_pairs={{0,2},{2,0},{8,10},{10,8},{1,3},{3,1},{9,11},{11,9},{4,6},{6,4},{1... | collective-permute-start | bytes 245768 | tf_op jit(solution)/shard_map/ppermute | solution.py:423
  44.8 0.8 %collective-permute-start.18 = (bf16[32,1280]{1,0:T(8,128)(2,1)S(1)}, bf16[32,1280]{1,0:T(8,128)(2,1)S(1)}, u32[]{:S(2)}, u32[]{:S(2)}) collective-permute-start(bf16[32,1280]{1,0:T(8,128)(2,1)S(1)} %get-tuple-element.43), channel_id=1, source_target_pairs={{0,8},{2,10},{8,0},{10,2},{1,9},{3,11},{9,1},{11,3},{4,12},{6,14},... | collective-permute-start | bytes 245768 | tf_op jit(solution)/shard_map/ppermute | solution.py:423
  45.6 0.7 %collective-permute-start.19 = (bf16[32,1280]{1,0:T(8,128)(2,1)S(1)}, bf16[32,1280]{1,0:T(8,128)(2,1)S(1)}, u32[]{:S(2)}, u32[]{:S(2)}) collective-permute-start(bf16[32,1280]{1,0:T(8,128)(2,1)S(1)} %get-tuple-element.44), channel_id=1, source_target_pairs={{0,10},{2,8},{8,2},{10,0},{1,11},{3,9},{9,3},{11,1},{4,14},{6,12},... | collective-permute-start | bytes 245768 | tf_op jit(solution)/shard_map/ppermute | solution.py:423
  46.3 1.2 %collective-permute-done.17.refs_1_ = bf16[32,1280]{1,0:T(8,128)(2,1)S(1)} collective-permute-done((bf16[32,1280]{1,0:T(8,128)(2,1)S(1)}, bf16[32,1280]{1,0:T(8,128)(2,1)S(1)}, u32[]{:S(2)}, u32[]{:S(2)}) %collective-permute-start.17) | collective-permute-done | bytes 81952 | tf_op jit(solution)/shard_map/ppermute | solution.py:423
  47.5 2.8 %collective-permute-done.18.refs_2_ = bf16[32,1280]{1,0:T(8,128)(2,1)S(1)} collective-permute-done((bf16[32,1280]{1,0:T(8,128)(2,1)S(1)}, bf16[32,1280]{1,0:T(8,128)(2,1)S(1)}, u32[]{:S(2)}, u32[]{:S(2)}) %collective-permute-start.18) | collective-permute-done | bytes 81952 | tf_op jit(solution)/shard_map/ppermute | solution.py:423
  50.3 0.7 %collective-permute-done.19.refs_3_ = bf16[32,1280]{1,0:T(8,128)(2,1)S(1)} collective-permute-done((bf16[32,1280]{1,0:T(8,128)(2,1)S(1)}, bf16[32,1280]{1,0:T(8,128)(2,1)S(1)}, u32[]{:S(2)}, u32[]{:S(2)}) %collective-permute-start.19) | collective-permute-done | bytes 81952 | tf_op jit(solution)/shard_map/ppermute | solution.py:423
  51.0 0.8 %shard_map.52 = bf16[32,5120]{1,0:T(8,128)(2,1)} custom-call(s32[1]{0:T(128)} %bitcast.place_ref, bf16[32,1280]{1,0:T(8,128)(2,1)S(1)} %get-tuple-element.41.refs_0_, bf16[32,1280]{1,0:T(8,128)(2,1)S(1)} %collective-permute-done.17.refs_1_, bf16[32,1280]{1,0:T(8,128)(2,1)S(1)} %collective-permute-done.18.refs_2_, ...), custom_call_target="tpu_custom_call" | custom-call | tf_op jit(solution)/shard_map/pallas_call | solution.py:412
  (7 shorter events, 0.1 us)
Async XLA Ops:
  0.0 5.1 %copy-start.1 = (bf16[3,32,1024]{2,1,0:T(8,128)(2,1)S(1)}, bf16[3,32,1024]{2,1,0:T(8,128)(2,1)}, u32[]{:S(2)}) copy-start(bf16[3,32,1024]{2,1,0:T(8,128)(2,1)} %x_ref.3) | copy-start | bytes 589828
  1.0 13.9 %collective-permute-start.6 = (bf16[640,128]{1,0:T(8,128)(2,1)S(1)}, bf16[640,128]{1,0:T(8,128)(2,1)S(1)}, u32[]{:S(2)}, u32[]{:S(2)}) collective-permute-start(bf16[640,128]{1,0:T(8,128)(2,1)S(1)} %shard_map.41), channel_id=1, source_target_pairs={{0,4},{4,0},{1,5},{5,1},{2,6},{6,2},{3,7},{7,3},{8,12},{12,8},{9,1... | collective-permute-start | bytes 491528 | tf_op jit(solution)/shard_map/ppermute | solution.py:423
  5.2 1.4 %collective-permute-start = (bf16[4,96,128]{2,1,0:T(8,128)(2,1)S(1)}, bf16[4,96,128]{2,1,0:T(8,128)(2,1)S(1)}, u32[]{:S(2)}, u32[]{:S(2)}) collective-permute-start(bf16[4,96,128]{2,1,0:T(8,128)(2,1)S(1)} %get-tuple-element.26), channel_id=1, source_target_pairs={{0,1},{1,0},{2,3},{3,2},{4,5},{5,4},{6,7},{7,6},{8,9},{9,8},{10,11... | collective-permute-start | bytes 294920 | tf_op jit(solution)/shard_map/ppermute | solution.py:423
  6.5 4.3 %collective-permute-start.1 = (bf16[2,96,128]{2,1,0:T(8,128)(2,1)S(1)}, bf16[2,96,128]{2,1,0:T(8,128)(2,1)S(1)}, u32[]{:S(2)}, u32[]{:S(2)}) collective-permute-start(bf16[2,96,128]{2,1,0:T(8,128)(2,1)S(1)} %get-tuple-element.28), channel_id=1, source_target_pairs={{0,2},{2,0},{8,10},{10,8},{1,3},{3,1},{9,11},{11,9},{4,6},{6,4},{1... | collective-permute-start | bytes 147464 | tf_op jit(solution)/shard_map/ppermute | solution.py:423
  8.2 4.1 %collective-permute-start.2 = (bf16[2,96,128]{2,1,0:T(8,128)(2,1)S(1)}, bf16[2,96,128]{2,1,0:T(8,128)(2,1)S(1)}, u32[]{:S(2)}, u32[]{:S(2)}) collective-permute-start(bf16[2,96,128]{2,1,0:T(8,128)(2,1)S(1)} %get-tuple-element.29), channel_id=1, source_target_pairs={{0,8},{2,10},{8,0},{10,2},{1,9},{3,11},{9,1},{11,3},{4,12},{6,14},... | collective-permute-start | bytes 147464 | tf_op jit(solution)/shard_map/ppermute | solution.py:423
  9.7 5.2 %collective-permute-start.3 = (bf16[2,96,128]{2,1,0:T(8,128)(2,1)S(1)}, bf16[2,96,128]{2,1,0:T(8,128)(2,1)S(1)}, u32[]{:S(2)}, u32[]{:S(2)}) collective-permute-start(bf16[2,96,128]{2,1,0:T(8,128)(2,1)S(1)} %get-tuple-element.30), channel_id=1, source_target_pairs={{0,10},{2,8},{8,2},{10,0},{1,11},{3,9},{9,3},{11,1},{4,14},{6,12},... | collective-permute-start | bytes 147464 | tf_op jit(solution)/shard_map/ppermute | solution.py:423
  14.9 4.7 %copy-start = (bf16[128,5120]{1,0:T(8,128)(2,1)S(1)}, bf16[128,5120]{1,0:T(8,128)(2,1)}, u32[]{:S(2)}) copy-start(bf16[128,5120]{1,0:T(8,128)(2,1)} %refs_4_.1) | copy-start | bytes 3932164
  14.9 10.9 %copy-start.2 = (s32[8]{0:T(128)S(1)}, s32[8]{0:T(128)}, u32[]{:S(2)}) copy-start(s32[8]{0:T(128)} %clip_ref.1) | copy-start | bytes 100
  15.0 14.6 %collective-permute-start.7 = (bf16[1152,128]{1,0:T(8,128)(2,1)S(1)}, bf16[1152,128]{1,0:T(8,128)(2,1)S(1)}, u32[]{:S(2)}, u32[]{:S(2)}) collective-permute-start(bf16[1152,128]{1,0:T(8,128)(2,1)S(1)} %shard_map.43), channel_id=1, source_target_pairs={{0,16},{16,0},{1,17},{17,1},{2,18},{18,2},{3,19},{19,3},{4,20},{20... | collective-permute-start | bytes 884744 | tf_op jit(solution)/shard_map/ppermute | solution.py:423
  16.5 6.7 %collective-permute-start.5 = (bf16[256,128]{1,0:T(8,128)(2,1)S(1)}, bf16[256,128]{1,0:T(8,128)(2,1)S(1)}, u32[]{:S(2)}, u32[]{:S(2)}) collective-permute-start(bf16[256,128]{1,0:T(8,128)(2,1)S(1)} %get-tuple-element.35.refs_1_.refs_3_), channel_id=1, source_target_pairs={{0,4},{4,0},{1,5},{5,1},{2,6},{6,2},{3,7},{7,3},{8,12},{12,8},{9,1... | collective-permute-start | bytes 196616 | tf_op jit(solution)/shard_map/ppermute | solution.py:423
  16.7 8.5 %collective-permute-start.4 = (bf16[256,128]{1,0:T(8,128)(2,1)S(1)}, bf16[256,128]{1,0:T(8,128)(2,1)S(1)}, u32[]{:S(2)}, u32[]{:S(2)}) collective-permute-start(bf16[256,128]{1,0:T(8,128)(2,1)S(1)} %get-tuple-element.34.refs_0_.refs_2_.refs_1_), channel_id=1, source_target_pairs={{0,4},{4,0},{1,5},{5,1},{2,6},{6,2},{3,7},{7,3},{8,12},{12,8},{9,1... | collective-permute-start | bytes 196616 | tf_op jit(solution)/shard_map/ppermute | solution.py:423
  20.1 17.6 %collective-permute-start.13 = (bf16[128,1280]{1,0:T(8,128)(2,1)S(1)}, bf16[128,1280]{1,0:T(8,128)(2,1)S(1)}, u32[]{:S(2)}, u32[]{:S(2)}) collective-permute-start(bf16[128,1280]{1,0:T(8,128)(2,1)S(1)} %shard_map.46), channel_id=1, source_target_pairs={{0,2},{2,0},{1,3},{3,1},{4,6},{6,4},{5,7},{7,5},{8,10},{10,8},{9,1... | collective-permute-start | bytes 983048 | tf_op jit(solution)/shard_map/ppermute | solution.py:423
  20.8 12.8 %collective-permute-start.14 = (bf16[64,1280]{1,0:T(8,128)(2,1)S(1)}, bf16[64,1280]{1,0:T(8,128)(2,1)S(1)}, u32[]{:S(2)}, u32[]{:S(2)}) collective-permute-start(bf16[64,1280]{1,0:T(8,128)(2,1)S(1)} %shard_map.47), channel_id=1, source_target_pairs={{0,6},{2,4},{4,2},{6,0},{1,7},{3,5},{5,3},{7,1},{8,14},{10,12},{12... | collective-permute-start | bytes 491528 | tf_op jit(solution)/shard_map/ppermute | solution.py:423
  23.3 4.3 %collective-permute-start.9 = (bf16[256,128]{1,0:T(8,128)(2,1)S(1)}, bf16[256,128]{1,0:T(8,128)(2,1)S(1)}, u32[]{:S(2)}, u32[]{:S(2)}) collective-permute-start(bf16[256,128]{1,0:T(8,128)(2,1)S(1)} %collective-permute-done.5.refs_5_), channel_id=1, source_target_pairs={{0,16},{16,0},{1,17},{17,1},{2,18},{18,2},{3,19},{19,3},{4,20},{20... | collective-permute-start | bytes 196616 | tf_op jit(solution)/shard_map/ppermute | solution.py:423
  25.2 4.3 %collective-permute-start.8 = (bf16[256,128]{1,0:T(8,128)(2,1)S(1)}, bf16[256,128]{1,0:T(8,128)(2,1)S(1)}, u32[]{:S(2)}, u32[]{:S(2)}) collective-permute-start(bf16[256,128]{1,0:T(8,128)(2,1)S(1)} %collective-permute-done.4.refs_4_), channel_id=1, source_target_pairs={{0,16},{16,0},{1,17},{17,1},{2,18},{18,2},{3,19},{19,3},{4,20},{20... | collective-permute-start | bytes 196616 | tf_op jit(solution)/shard_map/ppermute | solution.py:423
  33.6 6.2 %collective-permute-start.15 = (bf16[64,1280]{1,0:T(8,128)(2,1)S(1)}, bf16[64,1280]{1,0:T(8,128)(2,1)S(1)}, u32[]{:S(2)}, u32[]{:S(2)}) collective-permute-start(bf16[64,1280]{1,0:T(8,128)(2,1)S(1)} %shard_map.48.refs_8_), channel_id=1, source_target_pairs={{0,16},{16,0},{1,17},{17,1},{2,18},{18,2},{3,19},{19,3},{4,20},{20... | collective-permute-start | bytes 491528 | tf_op jit(solution)/shard_map/ppermute | solution.py:423
  34.1 5.2 %collective-permute-start.12 = (bf16[256,128]{1,0:T(8,128)(2,1)S(1)}, bf16[256,128]{1,0:T(8,128)(2,1)S(1)}, u32[]{:S(2)}, u32[]{:S(2)}) collective-permute-start(bf16[256,128]{1,0:T(8,128)(2,1)S(1)} %shard_map.44.refs_1_.refs_0_), channel_id=1, source_target_pairs={{0,10},{2,8},{8,2},{10,0},{1,11},{3,9},{9,3},{11,1},{4,14},{6,12},... | collective-permute-start | bytes 196616 | tf_op jit(solution)/shard_map/ppermute | solution.py:423
  34.1 5.2 %collective-permute-start.11 = (bf16[256,128]{1,0:T(8,128)(2,1)S(1)}, bf16[256,128]{1,0:T(8,128)(2,1)S(1)}, u32[]{:S(2)}, u32[]{:S(2)}) collective-permute-start(bf16[256,128]{1,0:T(8,128)(2,1)S(1)} %shard_map.44.refs_1_.refs_0_), channel_id=1, source_target_pairs={{0,8},{2,10},{8,0},{10,2},{1,9},{3,11},{9,1},{11,3},{4,12},{6,14},... | collective-permute-start | bytes 196616 | tf_op jit(solution)/shard_map/ppermute | solution.py:423
  35.0 4.9 %collective-permute-start.10 = (bf16[256,128]{1,0:T(8,128)(2,1)S(1)}, bf16[256,128]{1,0:T(8,128)(2,1)S(1)}, u32[]{:S(2)}, u32[]{:S(2)}) collective-permute-start(bf16[256,128]{1,0:T(8,128)(2,1)S(1)} %shard_map.44.refs_1_.refs_0_), channel_id=1, source_target_pairs={{0,2},{2,0},{8,10},{10,8},{1,3},{3,1},{9,11},{11,9},{4,6},{6,4},{1... | collective-permute-start | bytes 196616 | tf_op jit(solution)/shard_map/ppermute | solution.py:423
  40.9 1.7 %collective-permute-start.16 = (bf16[4,32,1280]{2,1,0:T(8,128)(2,1)S(1)}, bf16[4,32,1280]{2,1,0:T(8,128)(2,1)S(1)}, u32[]{:S(2)}, u32[]{:S(2)}) collective-permute-start(bf16[4,32,1280]{2,1,0:T(8,128)(2,1)S(1)} %get-tuple-element.40), channel_id=1, source_target_pairs={{0,1},{1,0},{2,3},{3,2},{4,5},{5,4},{6,7},{7,6},{8,9},{9,8},{10,11... | collective-permute-start | bytes 983048 | tf_op jit(solution)/shard_map/ppermute | solution.py:423
  42.7 4.8 %collective-permute-start.17 = (bf16[32,1280]{1,0:T(8,128)(2,1)S(1)}, bf16[32,1280]{1,0:T(8,128)(2,1)S(1)}, u32[]{:S(2)}, u32[]{:S(2)}) collective-permute-start(bf16[32,1280]{1,0:T(8,128)(2,1)S(1)} %get-tuple-element.42), channel_id=1, source_target_pairs={{0,2},{2,0},{8,10},{10,8},{1,3},{3,1},{9,11},{11,9},{4,6},{6,4},{1... | collective-permute-start | bytes 245768 | tf_op jit(solution)/shard_map/ppermute | solution.py:423
  44.8 5.5 %collective-permute-start.18 = (bf16[32,1280]{1,0:T(8,128)(2,1)S(1)}, bf16[32,1280]{1,0:T(8,128)(2,1)S(1)}, u32[]{:S(2)}, u32[]{:S(2)}) collective-permute-start(bf16[32,1280]{1,0:T(8,128)(2,1)S(1)} %get-tuple-element.43), channel_id=1, source_target_pairs={{0,8},{2,10},{8,0},{10,2},{1,9},{3,11},{9,1},{11,3},{4,12},{6,14},... | collective-permute-start | bytes 245768 | tf_op jit(solution)/shard_map/ppermute | solution.py:423
  45.6 5.4 %collective-permute-start.19 = (bf16[32,1280]{1,0:T(8,128)(2,1)S(1)}, bf16[32,1280]{1,0:T(8,128)(2,1)S(1)}, u32[]{:S(2)}, u32[]{:S(2)}) collective-permute-start(bf16[32,1280]{1,0:T(8,128)(2,1)S(1)} %get-tuple-element.44), channel_id=1, source_target_pairs={{0,10},{2,8},{8,2},{10,0},{1,11},{3,9},{9,3},{11,1},{4,14},{6,12},... | collective-permute-start | bytes 245768 | tf_op jit(solution)/shard_map/ppermute | solution.py:423

commit v20 on v19

--- a/solution.py
+++ b/solution.py
@@ -327,95 +327,144 @@
     )(q, *mask_of, *arrays)
 
 
-def project_kernel(n_attn, sizes, at_ref, place_ref, *refs):
-    attn_refs, w_refs = refs[:n_attn], refs[n_attn:-3]
-    out_ref, a_ref, w_all = refs[-3:]
-    width = attn_refs[0].shape[1]
-    blks, tok, cols = out_ref.shape
-    blk, other = place_ref[0] // 2, 1 - place_ref[0] % 2
+def stack_kernel(n_blocks, info_ref, x_ref, *refs):
+    *refs, out_ref = refs
+    part_refs, block_refs = refs[:len(refs) - n_blocks], refs[len(refs) - n_blocks:]
+    head_dim, cols = x_ref.shape[0], out_ref.shape[1]
+    out_ref[0:head_dim, :] = x_ref[:, rows_at(info_ref[0] // 2, cols)]
+    for i, ref in enumerate(part_refs):
+        out_ref[(i + 1) * head_dim:(i + 2) * head_dim, :] = ref[...]
+    first = (len(part_refs) + 1) * head_dim
+    for i, ref in enumerate(block_refs):
+        rows = head_dim // n_blocks
+        at = pl.ds(pl.multiple_of(first + (info_ref[2] ^ i) * rows, rows), rows)
+        head = ref.shape[0] - cols // LANES * rows
+        for j in range(cols // LANES):
+            out_ref[at, j * LANES:(j + 1) * LANES] = ref[head + j * rows:head + (j + 1) * rows]
+
+
+def stack(info, w_out, parts, blocks, cols):
+    depth = w_out.shape[0] * (1 + len(parts) + len(blocks) // 2)
+    return pl.pallas_call(
+        functools.partial(stack_kernel, len(blocks)),
+        out_shape=jax.ShapeDtypeStruct((depth, cols), w_out.dtype),
+        in_specs=[SMEM] + [VMEM] * (1 + len(parts) + len(blocks)),
+        out_specs=VMEM,
+        compiler_params=PARAMS,
+    )(info, w_out, *parts, *blocks)
+
+
+def halves(a_ref, rows, w_ref, late_ref):
+    if late_ref is None:
+        return jnp.dot(a_ref[rows, :], w_ref[...], preferred_element_type=jnp.float32)
+    half = (w_ref.shape[0] + late_ref.shape[0]) // 2
+    low = jnp.concatenate([w_ref[half:, :], late_ref[...]], axis=0)
+    first = jnp.dot(a_ref[rows, :half], w_ref[:half, :], preferred_element_type=jnp.float32)
+    return first + jnp.dot(a_ref[rows, half:], low, preferred_element_type=jnp.float32)
+
+
+def project_kernel(n_attn, head_dim, info_ref, *refs):
+    attn_refs, w_ref, refs = refs[:n_attn], refs[n_attn], refs[n_attn + 1:]
+    late_refs, (out_ref, a_ref), late_ref = refs[:-2], refs[-2:], None
+    if len(refs) > 2:
+        late_refs, (out_ref, a_ref, late_ref) = refs[:2], refs[2:]
+    blks, tok, _ = out_ref.shape
+    blk, other = info_ref[0] // 2, 1 - info_ref[0] % 2
+    heads = attn_refs[0].shape[1] // head_dim
     for k, ref in enumerate(attn_refs):
-        at = rows_at(blk ^ k, width)
-        for b in range(blks):
-            a_ref[b * tok:(b + 1) * tok, at] = ref[rows_at(2 * b + other, tok), :]
-            a_ref[(blks + b) * tok:(blks + b + 1) * tok, at] = ref[rows_at(2 * b + 1 - other, tok), :]
-    for i, (ref, rows) in enumerate(zip(w_refs, sizes)):
-        at = rows_at(at_ref[i], rows)
-        if ref.shape[1] >= cols:
-            w_all[at, :] = ref[:, rows_at(blk, cols)] if ref.shape[1] > cols else ref[...]
-        else:
-            first = ref.shape[0] - cols // LANES * rows
-            for j in range(cols // LANES):
-                w_all[at, j * LANES:(j + 1) * LANES] = ref[first + j * rows:first + (j + 1) * rows]
-    dot = jnp.dot(a_ref[:blks * tok, :], w_all[...], preferred_element_type=jnp.float32)
+        for i in range(heads):
+            at = rows_at(((blk ^ k) * heads + i) ^ info_ref[1], head_dim)
+            cols = slice(i * head_dim, (i + 1) * head_dim)
+            for b in range(blks):
+                a_ref[b * tok:(b + 1) * tok, at] = ref[rows_at(2 * b + other, tok), cols]
+                a_ref[(blks + b) * tok:(blks + b + 1) * tok, at] = ref[
+                    rows_at(2 * b + 1 - other, tok), cols
+                ]
+    for i, ref in enumerate(late_refs):
+        late_ref[rows_at(info_ref[2] ^ i, ref.shape[0]), :] = ref[...]
+    dot = halves(a_ref, slice(0, blks * tok), w_ref, late_ref)
     out_ref[...] = dot.astype(out_ref.dtype).reshape(out_ref.shape)
 
 
-def rest_kernel(a_ref, w_ref, out_ref):
+def rest_kernel(a_ref, w_ref, *refs):
+    *late_refs, out_ref = refs
     blks, tok, _ = out_ref.shape
-    dot = jnp.dot(a_ref[blks * tok:, :], w_ref[...], preferred_element_type=jnp.float32)
+    late_ref = late_refs[0] if late_refs else None
+    dot = halves(a_ref, slice(blks * tok, None), w_ref, late_ref)
     out_ref[...] = dot.astype(out_ref.dtype).reshape(out_ref.shape)
 
 
-def project(attns, w_parts, sizes, at, place, tok, cols):
+def project(attns, w_all, late, info, head_dim, tok):
     count, width = attns[0].shape
-    blks, dtype = len(attns), attns[0].dtype
+    blks, dtype, cols = len(attns), attns[0].dtype, w_all.shape[1]
     like = jax.ShapeDtypeStruct((blks, tok, cols), dtype)
-    theirs, a_all, w_all = pl.pallas_call(
-        functools.partial(project_kernel, blks, sizes),
-        out_shape=(
-            like,
-            jax.ShapeDtypeStruct((count, blks * width), dtype),
-            jax.ShapeDtypeStruct((blks * width, cols), dtype),
-        ),
-        in_specs=[SMEM, SMEM] + [VMEM] * (blks + len(w_parts)),
-        out_specs=(VMEM, VMEM, VMEM),
-        compiler_params=PARAMS,
-    )(index_array(*at), place, *attns, *w_parts)
+    below = [jax.ShapeDtypeStruct((head_dim, cols), dtype)] if late else []
+    theirs, a_all, *late_all = pl.pallas_call(
+        functools.partial(project_kernel, blks, head_dim),
+        out_shape=[like, jax.ShapeDtypeStruct((count, blks * width), dtype)] + below,
+        in_specs=[SMEM] + [VMEM] * (blks + 1 + len(late)),
+        out_specs=[VMEM] * (2 + len(below)),
+        compiler_params=PARAMS,
+    )(info, *attns, w_all, *late)
     got = xor(theirs, ("core",), 1)
     ours = pl.pallas_call(
         rest_kernel,
         out_shape=like,
-        in_specs=[VMEM, VMEM],
+        in_specs=[VMEM] * (2 + len(below)),
         out_specs=VMEM,
         compiler_params=PARAMS,
-    )(a_all, w_all)
-    return add(ours, got, place)
-
-
-def add_kernel(place_ref, x_ref, y_ref, *out_refs):
-    for k, out_ref in enumerate(out_refs):
-        at = place_ref[0] // 2 ^ k
+    )(a_all, w_all, *late_all)
+    far = [k for k in range(blks) if k != 1]
+    parts = dict(zip(far, add(ours, got, info, far)))
+    parts[1], = add(ours, got, info, [1], parts[far[-1]])
+    return [parts[k] for k in range(blks)]
+
+
+def add_kernel(which, info_ref, x_ref, y_ref, *refs):
+    for k, out_ref in zip(which, refs[len(refs) - len(which):]):
+        at = info_ref[0] // 2 ^ k
         both = x_ref[at].astype(jnp.float32) + y_ref[at].astype(jnp.float32)
         out_ref[...] = both.astype(out_ref.dtype)
 
 
-def add(x, y, place):
-    blks = x.shape[0]
-    return pl.pallas_call(
-        add_kernel,
-        out_shape=[jax.ShapeDtypeStruct(x.shape[1:], x.dtype)] * blks,
-        in_specs=[SMEM, VMEM, VMEM],
-        out_specs=[VMEM] * blks,
-        compiler_params=PARAMS,
-    )(place, x, y)
-
-
-def unpack_kernel(place_ref, *refs):
-    *in_refs, out_ref = refs
-    width = in_refs[0].shape[1]
-    for k, ref in enumerate(in_refs):
-        out_ref[:, rows_at(place_ref[0] // 2 ^ k, width)] = ref[...]
-
-
-def unpack(parts, place):
+def add(x, y, info, which, *first):
+    return pl.pallas_call(
+        functools.partial(add_kernel, which),
+        out_shape=[jax.ShapeDtypeStruct(x.shape[1:], x.dtype)] * len(which),
+        in_specs=[SMEM, VMEM, VMEM] + [ANY] * len(first),
+        out_specs=[VMEM] * len(which),
+        compiler_params=PARAMS,
+    )(info, x, y, *first)
+
+
+def unpack_kernel(which, n_in, info_ref, *refs):
+    in_refs, (out_ref, sems) = refs[:len(which)], refs[n_in:]
+    copies = []
+    for i, (k, ref) in enumerate(zip(which, in_refs)):
+        cols = rows_at(info_ref[0] // 2 ^ k, ref.shape[1])
+        copies.append(pltpu.make_async_copy(ref, out_ref.at[:, cols], sems.at[i]))
+    for copy in copies:
+        copy.start()
+    for copy in copies:
+        copy.wait()
+
+
+def unpack(parts, info):
     tok, width = parts[0].shape
-    return pl.pallas_call(
-        unpack_kernel,
-        out_shape=jax.ShapeDtypeStruct((tok, len(parts) * width), parts[0].dtype),
-        in_specs=[SMEM] + [VMEM] * len(parts),
-        out_specs=VMEM,
-        compiler_params=PARAMS,
-    )(place, *parts)
+    hbm = pl.BlockSpec(memory_space=pltpu.HBM)
+    result = []
+    for which in (range(0, 2), range(2, len(parts))):
+        n = len(which)
+        result = [pl.pallas_call(
+            functools.partial(unpack_kernel, which, n + len(result)),
+            out_shape=jax.ShapeDtypeStruct((tok, len(parts) * width), parts[0].dtype),
+            in_specs=[SMEM] + [VMEM] * n + [hbm] * len(result),
+            out_specs=hbm,
+            input_output_aliases={1 + n: 0} if result else {},
+            scratch_shapes=[pltpu.SemaphoreType.DMA((n,))],
+            compiler_params=PARAMS,
+        )(info, *[parts[k] for k in which], *result)]
+    return result[0]
 
 
 def xor(x, axis, by):
@@ -433,7 +482,8 @@
     tok, head_dim, cols = qkv.shape[1], w_out.shape[0], w_out.shape[1] // 4
     place = index_array((x * 2 + zl) * 2 + core)
     theirs = x * 2 + 1 - zl
-    row, half = zh * 2 + zl, head_dim // 2
+    info = index_array((x * 2 + zl) * 2 + core, zh * 2 + zl, y)
+    half = head_dim // 2
 
     w_far = blocks(w_out, half, cols, "y", quarter)
     far = after(xor(w_far, ("zh",), 1), cost=AHEAD)
@@ -453,22 +503,20 @@
     corner = after(corner, attn)
     corner_rest = xor(corner, ("y",), 1)
     attns = swap_all([attn] * 4, quarter)
-    w_parts = [w_out, w_next, far, near, corner, corner_rest]
-    sizes = [head_dim, head_dim, half, half, half, half]
-    at = [row, row ^ 1] + [2 * (row ^ by) + h for by in (2, 3) for h in (y, 1 - y)]
-    parts = project(attns, w_parts, sizes, at, place, tok, cols)
-    return unpack(swap_all(parts, quarter), place)
+    w_all = stack(info, w_out, [w_next], [far, near], cols)
+    parts = project(attns, w_all, [corner, corner_rest], info, head_dim, tok)
+    return unpack(swap_all(parts, quarter), info)
 
 
 def layers(qkv, frame_clip, w_out):
     rows, blks = lax.axis_size("row"), lax.axis_size("blk")
     row, blk = lax.axis_index("row"), lax.axis_index("blk")
     tok, head_dim, cols = qkv.shape[1], w_out.shape[0], w_out.shape[1] // blks
-    place = index_array(blk * 2 + lax.axis_index("core"))
+    info = index_array(blk * 2 + lax.axis_index("core"), row)
     others = range(1, rows)
 
     (w_own,) = columns(w_out, [(head_dim, 0, blk)], cols)
-    w_parts = [w_out] + [xor(w_own, ("row",), by) for by in others]
+    w_parts = [xor(w_own, ("row",), by) for by in others]
     packed = pack(qkv, 2 * blks, head_dim)
     own = lax.all_to_all(packed, ("blk", "core"), split_axis=0, concat_axis=0, tiled=True)
     q, kv = cut(own)
@@ -476,9 +524,9 @@
     mask_of = masks([0], 2 * tok, tok, 2 * blks * tok, frame_clip)
     attn = attention(q, kvs, mask_of, [0] * rows, head_dim)
     attns = swap_all([attn] * blks, ("blk",))
-    at = [row ^ by for by in range(rows)]
-    parts = project(attns, w_parts, [head_dim] * rows, at, place, tok, cols)
-    return unpack(swap_all(parts, ("blk",)), place)
+    w_all = stack(info, w_out, w_parts, [], cols)
+    parts = project(attns, w_all, [], info, head_dim, tok)
+    return unpack(swap_all(parts, ("blk",)), info)
 
 
 def solution(mesh):

time: 51.9 us -> 53.3 us (1.027)
  Pallas kernels: 5.23 us -> 8.58 us
  waiting for transfers between devices: 22 us -> 20.1 us
    pallas_call x4 -> x7, Pallas kernels: 2.21 us -> 5.57 us  [the longest x2 2.46 us: unpack(): pl.pallas_call(functools.partial(unpack_kernel, which, n + len(result)),...]
    ppermute x20, waiting for transfers between devices: 22 us -> 20.1 us  [xor(): return lax.ppermute(x, axis, [(i, i ^ by) for i in range(size)])]
  transfers between devices with their start and end apart: 20 -> 20, of which waited for: 14 -> 14; matrix products, arithmetic and copies ran while one was open for 0% -> 0% of each run, Pallas kernels for 5% -> 8%
where the time goes in v20:
time: 53.3 us; the launch traced here: 53.2 us
  starting transfers between devices  24.1 us (45%)
  waiting for transfers between devices  20.1 us (38%)
  Pallas kernels  8.58 us (16%)
    ppermute x20, starting transfers between devices, xor(): return lax.ppermute(x, axis, [(i, i ^ by) for i in range(size)])  24.1 us
    ppermute x20, waiting for transfers between devices, xor(): return lax.ppermute(x, axis, [(i, i ^ by) for i in range(size)])  20.1 us
    pallas_call x2, Pallas kernels, unpack(): pl.pallas_call(functools.partial(unpack_kernel, which, n + len(result)),...  2.46 us
    pallas_call x2, Pallas kernels, add(): pl.pallas_call(functools.partial(add_kernel, which), out_shape=[jax.Shape...  1.19 us
  transfers between devices with their start and end apart: 20, of which 14 were waited for; matrix products, arithmetic and copies ran while one was open for 0% of the time, Pallas kernels for 8%

profile of v20, /device:TPU:0, one launch (start us, length us, event | category | flops | bytes accessed | tf_op | source)
XLA Modules:
  0.0 53.2 jit_solution(8332678556549423152)
XLA Ops:
  0.0 0.0 copy-start.1
  0.0 1.0 %shard_map.41 = bf16[640,128]{1,0:T(8,128)(2,1)S(1)} custom-call(bf16[128,5120]{1,0:T(8,128)(2,1)} %x_ref.7), custom_call_target="tpu_custom_call" | custom-call | tf_op jit(solution)/shard_map/pallas_call | solution.py:96
  1.0 4.1 %collective-permute-start.6 = (bf16[640,128]{1,0:T(8,128)(2,1)S(1)}, bf16[640,128]{1,0:T(8,128)(2,1)S(1)}, u32[]{:S(2)}, u32[]{:S(2)}) collective-permute-start(bf16[640,128]{1,0:T(8,128)(2,1)S(1)} %shard_map.41), channel_id=1, source_target_pairs={{0,4},{4,0},{1,5},{5,1},{2,6},{6,2},{3,7},{7,3},{8,12},{12,8},{9,1... | collective-permute-start | bytes 491528 | tf_op jit(solution)/shard_map/ppermute | solution.py:472
  5.1 0.0 copy-done.1
  5.1 0.1 shard_map.37
  5.2 0.1 collective-permute-start
  5.3 1.3 %collective-permute-done.got_ref = bf16[4,96,128]{2,1,0:T(8,128)(2,1)S(1)} collective-permute-done((bf16[4,96,128]{2,1,0:T(8,128)(2,1)S(1)}, bf16[4,96,128]{2,1,0:T(8,128)(2,1)S(1)}, u32[]{:S(2)}, u32[]{:S(2)}) %collective-permute-start) | collective-permute-done | bytes 98336 | tf_op jit(solution)/shard_map/ppermute | solution.py:472
  6.5 1.6 %collective-permute-start.1 = (bf16[2,96,128]{2,1,0:T(8,128)(2,1)S(1)}, bf16[2,96,128]{2,1,0:T(8,128)(2,1)S(1)}, u32[]{:S(2)}, u32[]{:S(2)}) collective-permute-start(bf16[2,96,128]{2,1,0:T(8,128)(2,1)S(1)} %get-tuple-element.27), channel_id=1, source_target_pairs={{0,2},{2,0},{8,10},{10,8},{1,3},{3,1},{9,11},{11,9},{4,6},{6,4},{1... | collective-permute-start | bytes 147464 | tf_op jit(solution)/shard_map/ppermute | solution.py:472
  8.2 1.5 %collective-permute-start.2 = (bf16[2,96,128]{2,1,0:T(8,128)(2,1)S(1)}, bf16[2,96,128]{2,1,0:T(8,128)(2,1)S(1)}, u32[]{:S(2)}, u32[]{:S(2)}) collective-permute-start(bf16[2,96,128]{2,1,0:T(8,128)(2,1)S(1)} %get-tuple-element.28), channel_id=1, source_target_pairs={{0,8},{2,10},{8,0},{10,2},{1,9},{3,11},{9,1},{11,3},{4,12},{6,14},... | collective-permute-start | bytes 147464 | tf_op jit(solution)/shard_map/ppermute | solution.py:472
  9.7 0.4 collective-permute-start.3
  10.1 0.8 %collective-permute-done.1.refs_1_ = bf16[2,96,128]{2,1,0:T(8,128)(2,1)S(1)} collective-permute-done((bf16[2,96,128]{2,1,0:T(8,128)(2,1)S(1)}, bf16[2,96,128]{2,1,0:T(8,128)(2,1)S(1)}, u32[]{:S(2)}, u32[]{:S(2)}) %collective-permute-start.1) | collective-permute-done | bytes 49184 | tf_op jit(solution)/shard_map/ppermute | solution.py:472
  10.9 1.4 %collective-permute-done.2.refs_2_ = bf16[2,96,128]{2,1,0:T(8,128)(2,1)S(1)} collective-permute-done((bf16[2,96,128]{2,1,0:T(8,128)(2,1)S(1)}, bf16[2,96,128]{2,1,0:T(8,128)(2,1)S(1)}, u32[]{:S(2)}, u32[]{:S(2)}) %collective-permute-start.2) | collective-permute-done | bytes 49184 | tf_op jit(solution)/shard_map/ppermute | solution.py:472
  12.3 2.6 %collective-permute-done.3.refs_3_ = bf16[2,96,128]{2,1,0:T(8,128)(2,1)S(1)} collective-permute-done((bf16[2,96,128]{2,1,0:T(8,128)(2,1)S(1)}, bf16[2,96,128]{2,1,0:T(8,128)(2,1)S(1)}, u32[]{:S(2)}, u32[]{:S(2)}) %collective-permute-start.3) | collective-permute-done | bytes 49184 | tf_op jit(solution)/shard_map/ppermute | solution.py:472
  14.9 0.0 collective-permute-done.6.refs_0_
  14.9 0.0 copy-start
  14.9 0.0 copy-start.2
  15.0 1.6 %collective-permute-start.7 = (bf16[1152,128]{1,0:T(8,128)(2,1)S(1)}, bf16[1152,128]{1,0:T(8,128)(2,1)S(1)}, u32[]{:S(2)}, u32[]{:S(2)}) collective-permute-start(bf16[1152,128]{1,0:T(8,128)(2,1)S(1)} %shard_map.43), channel_id=1, source_target_pairs={{0,16},{16,0},{1,17},{17,1},{2,18},{18,2},{3,19},{19,3},{4,20},{20... | collective-permute-start | bytes 884744 | tf_op jit(solution)/shard_map/ppermute | solution.py:472
  16.5 0.2 collective-permute-start.5
  16.7 2.8 %collective-permute-start.4 = (bf16[256,128]{1,0:T(8,128)(2,1)S(1)}, bf16[256,128]{1,0:T(8,128)(2,1)S(1)}, u32[]{:S(2)}, u32[]{:S(2)}) collective-permute-start(bf16[256,128]{1,0:T(8,128)(2,1)S(1)} %get-tuple-element.33.refs_0_.refs_2_.refs_1_), channel_id=1, source_target_pairs={{0,4},{4,0},{1,5},{5,1},{2,6},{6,2},{3,7},{7,3},{8,12},{12,8},{9,1... | collective-permute-start | bytes 196616 | tf_op jit(solution)/shard_map/ppermute | solution.py:472
  19.5 0.1 pad_add_fusion.2.at_ref
  19.5 0.0 copy-done
  19.5 0.6 %shard_map.45 = (bf16[64,1280]{1,0:T(8,128)(2,1)S(1)}, bf16[128,1280]{1,0:T(8,128)(2,1)S(1)}) custom-call(s32[2]{0:T(128)S(1)} %pad_add_fusion.2.at_ref, bf16[128,5120]{1,0:T(8,128)(2,1)S(1)} %copy-done), custom_call_target="tpu_custom_call" | custom-call | tf_op jit(solution)/shard_map/pallas_call | solution.py:114
  20.1 0.7 %collective-permute-start.13 = (bf16[128,1280]{1,0:T(8,128)(2,1)S(1)}, bf16[128,1280]{1,0:T(8,128)(2,1)S(1)}, u32[]{:S(2)}, u32[]{:S(2)}) collective-permute-start(bf16[128,1280]{1,0:T(8,128)(2,1)S(1)} %shard_map.46), channel_id=1, source_target_pairs={{0,2},{2,0},{1,3},{3,1},{4,6},{6,4},{5,7},{7,5},{8,10},{10,8},{9,1... | collective-permute-start | bytes 983048 | tf_op jit(solution)/shard_map/ppermute | solution.py:472
  20.8 2.4 %collective-permute-start.14 = (bf16[64,1280]{1,0:T(8,128)(2,1)S(1)}, bf16[64,1280]{1,0:T(8,128)(2,1)S(1)}, u32[]{:S(2)}, u32[]{:S(2)}) collective-permute-start(bf16[64,1280]{1,0:T(8,128)(2,1)S(1)} %shard_map.48), channel_id=1, source_target_pairs={{0,6},{2,4},{4,2},{6,0},{1,7},{3,5},{5,3},{7,1},{8,14},{10,12},{12... | collective-permute-start | bytes 491528 | tf_op jit(solution)/shard_map/ppermute | solution.py:472
  23.3 0.0 collective-permute-done.5.refs_5_
  23.3 0.5 collective-permute-start.9
  23.8 1.5 %collective-permute-done.4.refs_4_ = bf16[256,128]{1,0:T(8,128)(2,1)S(1)} collective-permute-done((bf16[256,128]{1,0:T(8,128)(2,1)S(1)}, bf16[256,128]{1,0:T(8,128)(2,1)S(1)}, u32[]{:S(2)}, u32[]{:S(2)}) %collective-permute-start.4) | collective-permute-done | bytes 65568 | tf_op jit(solution)/shard_map/ppermute | solution.py:472
  25.2 0.5 collective-permute-start.8
  25.8 0.1 pad_add_fusion.1.base_ref
  25.8 0.0 copy-done.2
  25.8 0.7 %shard_map.40 = (f32[256,256]{1,0:T(8,128)S(1)}, f32[256,256]{1,0:T(8,128)S(1)}) custom-call(s32[2]{0:T(128)S(1)} %pad_add_fusion.1.base_ref, s32[8]{0:T(128)S(1)} %copy-done.2), custom_call_target="tpu_custom_call" | custom-call | tf_op jit(solution)/shard_map/pallas_call | solution.py:261
  26.5 1.0 %collective-permute-done.9.refs_8_ = bf16[256,128]{1,0:T(8,128)(2,1)S(1)} collective-permute-done((bf16[256,128]{1,0:T(8,128)(2,1)S(1)}, bf16[256,128]{1,0:T(8,128)(2,1)S(1)}, u32[]{:S(2)}, u32[]{:S(2)}) %collective-permute-start.9) | collective-permute-done | bytes 65568 | tf_op jit(solution)/shard_map/ppermute | solution.py:472
  27.5 2.0 %collective-permute-done.8.refs_7_ = bf16[256,128]{1,0:T(8,128)(2,1)S(1)} collective-permute-done((bf16[256,128]{1,0:T(8,128)(2,1)S(1)}, bf16[256,128]{1,0:T(8,128)(2,1)S(1)}, u32[]{:S(2)}, u32[]{:S(2)}) %collective-permute-start.8) | collective-permute-done | bytes 65568 | tf_op jit(solution)/shard_map/ppermute | solution.py:472
  29.5 0.0 collective-permute-done.7.refs_6_.refs_2_
  29.5 0.6 %shard_map.44.refs_1_.refs_0_ = bf16[256,128]{1,0:T(8,128)(2,1)S(1)} custom-call(bf16[256,128]{1,0:T(8,128)(2,1)S(1)} %get-tuple-element.30.q_ref, f32[256,256]{1,0:T(8,128)S(1)} %get-tuple-element.31.refs_0_, f32[256,256]{1,0:T(8,128)S(1)} %get-tuple-element.32.refs_1_, bf16[256,128]{1,0:T(8,128)(2,1)S(1)} %get-tuple-element.33.refs_0_.refs_2_.refs_1_, ...), custom_call_target="tpu_custom_call" | custom-call | tf_op jit(solution)/shard_map/pallas_call | solution.py:321
  30.2 3.5 %collective-permute-done.14.refs_0_ = bf16[64,1280]{1,0:T(8,128)(2,1)S(1)} collective-permute-done((bf16[64,1280]{1,0:T(8,128)(2,1)S(1)}, bf16[64,1280]{1,0:T(8,128)(2,1)S(1)}, u32[]{:S(2)}, u32[]{:S(2)}) %collective-permute-start.14) | collective-permute-done | bytes 163872 | tf_op jit(solution)/shard_map/ppermute | solution.py:472
  33.6 0.5 collective-permute-start.15
  34.1 0.0 collective-permute-start.12
  34.1 0.8 %collective-permute-start.11 = (bf16[256,128]{1,0:T(8,128)(2,1)S(1)}, bf16[256,128]{1,0:T(8,128)(2,1)S(1)}, u32[]{:S(2)}, u32[]{:S(2)}) collective-permute-start(bf16[256,128]{1,0:T(8,128)(2,1)S(1)} %shard_map.44.refs_1_.refs_0_), channel_id=1, source_target_pairs={{0,8},{2,10},{8,0},{10,2},{1,9},{3,11},{9,1},{11,3},{4,12},{6,14},... | collective-permute-start | bytes 196616 | tf_op jit(solution)/shard_map/ppermute | solution.py:472
  35.0 2.7 %collective-permute-start.10 = (bf16[256,128]{1,0:T(8,128)(2,1)S(1)}, bf16[256,128]{1,0:T(8,128)(2,1)S(1)}, u32[]{:S(2)}, u32[]{:S(2)}) collective-permute-start(bf16[256,128]{1,0:T(8,128)(2,1)S(1)} %shard_map.44.refs_1_.refs_0_), channel_id=1, source_target_pairs={{0,2},{2,0},{8,10},{10,8},{1,3},{3,1},{9,11},{11,9},{4,6},{6,4},{1... | collective-permute-start | bytes 196616 | tf_op jit(solution)/shard_map/ppermute | solution.py:472
  37.6 0.1 pad_add_fusion.info_ref
  37.7 0.0 collective-permute-done.13.refs_0_
  37.7 0.6 %shard_map.47.refs_4_.w_ref = bf16[384,1280]{1,0:T(8,128)(2,1)S(1)} custom-call(s32[3]{0:T(128)S(1)} %pad_add_fusion.info_ref, bf16[128,5120]{1,0:T(8,128)(2,1)S(1)} %copy-done, bf16[128,1280]{1,0:T(8,128)(2,1)S(1)} %collective-permute-done.13.refs_0_, bf16[640,128]{1,0:T(8,128)(2,1)S(1)} %shard_map.42.refs_2_.refs_1_, ...), custom_call_target="tpu_custom_call" | custom-call | tf_op jit(solution)/shard_map/pallas_call | solution.py:348
  38.3 0.9 %collective-permute-done.12.refs_3_ = bf16[256,128]{1,0:T(8,128)(2,1)S(1)} collective-permute-done((bf16[256,128]{1,0:T(8,128)(2,1)S(1)}, bf16[256,128]{1,0:T(8,128)(2,1)S(1)}, u32[]{:S(2)}, u32[]{:S(2)}) %collective-permute-start.12) | collective-permute-done | bytes 65568 | tf_op jit(solution)/shard_map/ppermute | solution.py:472
  39.3 0.0 collective-permute-done.11.refs_2_
  39.3 0.6 %collective-permute-done.10.refs_1_ = bf16[256,128]{1,0:T(8,128)(2,1)S(1)} collective-permute-done((bf16[256,128]{1,0:T(8,128)(2,1)S(1)}, bf16[256,128]{1,0:T(8,128)(2,1)S(1)}, u32[]{:S(2)}, u32[]{:S(2)}) %collective-permute-start.10) | collective-permute-done | bytes 65568 | tf_op jit(solution)/shard_map/ppermute | solution.py:472
  39.8 0.0 collective-permute-done.15.refs_6_
  39.9 0.9 %shard_map.50 = (bf16[4,32,1280]{2,1,0:T(8,128)(2,1)S(1)}, bf16[256,512]{1,0:T(8,128)(2,1)S(1)}, bf16[128,1280]{1,0:T(8,128)(2,1)S(1)}) custom-call(s32[3]{0:T(128)S(1)} %pad_add_fusion.info_ref, bf16[256,128]{1,0:T(8,128)(2,1)S(1)} %shard_map.44.refs_1_.refs_0_, bf16[256,128]{1,0:T(8,128)(2,1)S(1)} %collective-permute-done.10.refs_1_, ...), custom_call_target="tpu_custom_call" | custom-call | tf_op jit(solution)/shard_map/pallas_call | solution.py:402
  40.8 0.1 collective-permute-start.16
  40.9 0.3 shard_map.51.x_ref
  41.2 1.3 %collective-permute-done.16.y_ref = bf16[4,32,1280]{2,1,0:T(8,128)(2,1)S(1)} collective-permute-done((bf16[4,32,1280]{2,1,0:T(8,128)(2,1)S(1)}, bf16[4,32,1280]{2,1,0:T(8,128)(2,1)S(1)}, u32[]{:S(2)}, u32[]{:S(2)}) %collective-permute-start.16) | collective-permute-done | bytes 327712 | tf_op jit(solution)/shard_map/ppermute | solution.py:472
  42.5 0.6 %shard_map.52 = (bf16[32,1280]{1,0:T(8,128)(2,1)S(1)}, bf16[32,1280]{1,0:T(8,128)(2,1)S(1)}, bf16[32,1280]{1,0:T(8,128)(2,1)S(1)}) custom-call(s32[3]{0:T(128)S(1)} %pad_add_fusion.info_ref, bf16[4,32,1280]{2,1,0:T(8,128)(2,1)S(1)} %shard_map.51.x_ref, bf16[4,32,1280]{2,1,0:T(8,128)(2,1)S(1)} %collective-permute-done.16.y_ref), custom_call_target="tpu_custom_call" | custom-call | tf_op jit(solution)/shard_map/pallas_call | solution.py:431
  43.1 0.6 %shard_map.53 = bf16[32,1280]{1,0:T(8,128)(2,1)S(1)} custom-call(s32[3]{0:T(128)S(1)} %pad_add_fusion.info_ref, bf16[4,32,1280]{2,1,0:T(8,128)(2,1)S(1)} %shard_map.51.x_ref, bf16[4,32,1280]{2,1,0:T(8,128)(2,1)S(1)} %collective-permute-done.16.y_ref, bf16[32,1280]{1,0:T(8,128)(2,1)S(1)} %get-tuple-element.41.refs_0_), custom_call_target="tpu_custom_call" | custom-call | tf_op jit(solution)/shard_map/pallas_call | solution.py:431
  43.7 2.1 %collective-permute-start.19 = (bf16[32,1280]{1,0:T(8,128)(2,1)S(1)}, bf16[32,1280]{1,0:T(8,128)(2,1)S(1)}, u32[]{:S(2)}, u32[]{:S(2)}) collective-permute-start(bf16[32,1280]{1,0:T(8,128)(2,1)S(1)} %shard_map.53), channel_id=1, source_target_pairs={{0,2},{2,0},{8,10},{10,8},{1,3},{3,1},{9,11},{11,9},{4,6},{6,4},{1... | collective-permute-start | bytes 245768 | tf_op jit(solution)/shard_map/ppermute | solution.py:472
  45.8 0.8 %collective-permute-start.17 = (bf16[32,1280]{1,0:T(8,128)(2,1)S(1)}, bf16[32,1280]{1,0:T(8,128)(2,1)S(1)}, u32[]{:S(2)}, u32[]{:S(2)}) collective-permute-start(bf16[32,1280]{1,0:T(8,128)(2,1)S(1)} %get-tuple-element.40), channel_id=1, source_target_pairs={{0,8},{2,10},{8,0},{10,2},{1,9},{3,11},{9,1},{11,3},{4,12},{6,14},... | collective-permute-start | bytes 245768 | tf_op jit(solution)/shard_map/ppermute | solution.py:472
  46.6 0.7 %collective-permute-start.18 = (bf16[32,1280]{1,0:T(8,128)(2,1)S(1)}, bf16[32,1280]{1,0:T(8,128)(2,1)S(1)}, u32[]{:S(2)}, u32[]{:S(2)}) collective-permute-start(bf16[32,1280]{1,0:T(8,128)(2,1)S(1)} %get-tuple-element.41.refs_0_), channel_id=1, source_target_pairs={{0,10},{2,8},{8,2},{10,0},{1,11},{3,9},{9,3},{11,1},{4,14},{6,12},... | collective-permute-start | bytes 245768 | tf_op jit(solution)/shard_map/ppermute | solution.py:472
  47.3 1.2 %collective-permute-done.19.refs_1_ = bf16[32,1280]{1,0:T(8,128)(2,1)S(1)} collective-permute-done((bf16[32,1280]{1,0:T(8,128)(2,1)S(1)}, bf16[32,1280]{1,0:T(8,128)(2,1)S(1)}, u32[]{:S(2)}, u32[]{:S(2)}) %collective-permute-start.19) | collective-permute-done | bytes 81952 | tf_op jit(solution)/shard_map/ppermute | solution.py:472
  48.5 1.2 %shard_map.54.refs_2_ = bf16[32,5120]{1,0:T(8,128)(2,1)} custom-call(s32[3]{0:T(128)S(1)} %pad_add_fusion.info_ref, bf16[32,1280]{1,0:T(8,128)(2,1)S(1)} %get-tuple-element.42.refs_0_, bf16[32,1280]{1,0:T(8,128)(2,1)S(1)} %collective-permute-done.19.refs_1_), custom_call_target="tpu_custom_call" | custom-call | tf_op jit(solution)/shard_map/pallas_call | solution.py:458
  49.8 1.5 %collective-permute-done.17.refs_0_ = bf16[32,1280]{1,0:T(8,128)(2,1)S(1)} collective-permute-done((bf16[32,1280]{1,0:T(8,128)(2,1)S(1)}, bf16[32,1280]{1,0:T(8,128)(2,1)S(1)}, u32[]{:S(2)}, u32[]{:S(2)}) %collective-permute-start.17) | collective-permute-done | bytes 81952 | tf_op jit(solution)/shard_map/ppermute | solution.py:472
  51.3 0.7 %collective-permute-done.18.refs_1_ = bf16[32,1280]{1,0:T(8,128)(2,1)S(1)} collective-permute-done((bf16[32,1280]{1,0:T(8,128)(2,1)S(1)}, bf16[32,1280]{1,0:T(8,128)(2,1)S(1)}, u32[]{:S(2)}, u32[]{:S(2)}) %collective-permute-start.18) | collective-permute-done | bytes 81952 | tf_op jit(solution)/shard_map/ppermute | solution.py:472
  52.0 1.2 %shard_map.55 = bf16[32,5120]{1,0:T(8,128)(2,1)} custom-call(s32[3]{0:T(128)S(1)} %pad_add_fusion.info_ref, bf16[32,1280]{1,0:T(8,128)(2,1)S(1)} %collective-permute-done.17.refs_0_, bf16[32,1280]{1,0:T(8,128)(2,1)S(1)} %collective-permute-done.18.refs_1_, bf16[32,5120]{1,0:T(8,128)(2,1)} %shard_map.54.refs_2_), custom_call_target="tpu_custom_call", output_to_operand_aliasing={{}: (3, {})} | custom-call | tf_op jit(solution)/shard_map/pallas_call | solution.py:458
  (7 shorter events, 0.1 us)
Async XLA Ops:
  0.0 5.1 %copy-start.1 = (bf16[3,32,1024]{2,1,0:T(8,128)(2,1)S(1)}, bf16[3,32,1024]{2,1,0:T(8,128)(2,1)}, u32[]{:S(2)}) copy-start(bf16[3,32,1024]{2,1,0:T(8,128)(2,1)} %x_ref.4) | copy-start | bytes 589828
  1.0 13.9 %collective-permute-start.6 = (bf16[640,128]{1,0:T(8,128)(2,1)S(1)}, bf16[640,128]{1,0:T(8,128)(2,1)S(1)}, u32[]{:S(2)}, u32[]{:S(2)}) collective-permute-start(bf16[640,128]{1,0:T(8,128)(2,1)S(1)} %shard_map.41), channel_id=1, source_target_pairs={{0,4},{4,0},{1,5},{5,1},{2,6},{6,2},{3,7},{7,3},{8,12},{12,8},{9,1... | collective-permute-start | bytes 491528 | tf_op jit(solution)/shard_map/ppermute | solution.py:472
  5.2 1.4 %collective-permute-start = (bf16[4,96,128]{2,1,0:T(8,128)(2,1)S(1)}, bf16[4,96,128]{2,1,0:T(8,128)(2,1)S(1)}, u32[]{:S(2)}, u32[]{:S(2)}) collective-permute-start(bf16[4,96,128]{2,1,0:T(8,128)(2,1)S(1)} %get-tuple-element.25), channel_id=1, source_target_pairs={{0,1},{1,0},{2,3},{3,2},{4,5},{5,4},{6,7},{7,6},{8,9},{9,8},{10,11... | collective-permute-start | bytes 294920 | tf_op jit(solution)/shard_map/ppermute | solution.py:472
  6.5 4.3 %collective-permute-start.1 = (bf16[2,96,128]{2,1,0:T(8,128)(2,1)S(1)}, bf16[2,96,128]{2,1,0:T(8,128)(2,1)S(1)}, u32[]{:S(2)}, u32[]{:S(2)}) collective-permute-start(bf16[2,96,128]{2,1,0:T(8,128)(2,1)S(1)} %get-tuple-element.27), channel_id=1, source_target_pairs={{0,2},{2,0},{8,10},{10,8},{1,3},{3,1},{9,11},{11,9},{4,6},{6,4},{1... | collective-permute-start | bytes 147464 | tf_op jit(solution)/shard_map/ppermute | solution.py:472
  8.2 4.1 %collective-permute-start.2 = (bf16[2,96,128]{2,1,0:T(8,128)(2,1)S(1)}, bf16[2,96,128]{2,1,0:T(8,128)(2,1)S(1)}, u32[]{:S(2)}, u32[]{:S(2)}) collective-permute-start(bf16[2,96,128]{2,1,0:T(8,128)(2,1)S(1)} %get-tuple-element.28), channel_id=1, source_target_pairs={{0,8},{2,10},{8,0},{10,2},{1,9},{3,11},{9,1},{11,3},{4,12},{6,14},... | collective-permute-start | bytes 147464 | tf_op jit(solution)/shard_map/ppermute | solution.py:472
  9.7 5.2 %collective-permute-start.3 = (bf16[2,96,128]{2,1,0:T(8,128)(2,1)S(1)}, bf16[2,96,128]{2,1,0:T(8,128)(2,1)S(1)}, u32[]{:S(2)}, u32[]{:S(2)}) collective-permute-start(bf16[2,96,128]{2,1,0:T(8,128)(2,1)S(1)} %get-tuple-element.29), channel_id=1, source_target_pairs={{0,10},{2,8},{8,2},{10,0},{1,11},{3,9},{9,3},{11,1},{4,14},{6,12},... | collective-permute-start | bytes 147464 | tf_op jit(solution)/shard_map/ppermute | solution.py:472
  14.9 4.7 %copy-start = (bf16[128,5120]{1,0:T(8,128)(2,1)S(1)}, bf16[128,5120]{1,0:T(8,128)(2,1)}, u32[]{:S(2)}) copy-start(bf16[128,5120]{1,0:T(8,128)(2,1)} %x_ref.7) | copy-start | bytes 3932164
  14.9 10.9 %copy-start.2 = (s32[8]{0:T(128)S(1)}, s32[8]{0:T(128)}, u32[]{:S(2)}) copy-start(s32[8]{0:T(128)} %clip_ref.1) | copy-start | bytes 100
  15.0 14.6 %collective-permute-start.7 = (bf16[1152,128]{1,0:T(8,128)(2,1)S(1)}, bf16[1152,128]{1,0:T(8,128)(2,1)S(1)}, u32[]{:S(2)}, u32[]{:S(2)}) collective-permute-start(bf16[1152,128]{1,0:T(8,128)(2,1)S(1)} %shard_map.43), channel_id=1, source_target_pairs={{0,16},{16,0},{1,17},{17,1},{2,18},{18,2},{3,19},{19,3},{4,20},{20... | collective-permute-start | bytes 884744 | tf_op jit(solution)/shard_map/ppermute | solution.py:472
  16.5 6.7 %collective-permute-start.5 = (bf16[256,128]{1,0:T(8,128)(2,1)S(1)}, bf16[256,128]{1,0:T(8,128)(2,1)S(1)}, u32[]{:S(2)}, u32[]{:S(2)}) collective-permute-start(bf16[256,128]{1,0:T(8,128)(2,1)S(1)} %get-tuple-element.34.refs_1_.refs_3_), channel_id=1, source_target_pairs={{0,4},{4,0},{1,5},{5,1},{2,6},{6,2},{3,7},{7,3},{8,12},{12,8},{9,1... | collective-permute-start | bytes 196616 | tf_op jit(solution)/shard_map/ppermute | solution.py:472
  16.7 8.5 %collective-permute-start.4 = (bf16[256,128]{1,0:T(8,128)(2,1)S(1)}, bf16[256,128]{1,0:T(8,128)(2,1)S(1)}, u32[]{:S(2)}, u32[]{:S(2)}) collective-permute-start(bf16[256,128]{1,0:T(8,128)(2,1)S(1)} %get-tuple-element.33.refs_0_.refs_2_.refs_1_), channel_id=1, source_target_pairs={{0,4},{4,0},{1,5},{5,1},{2,6},{6,2},{3,7},{7,3},{8,12},{12,8},{9,1... | collective-permute-start | bytes 196616 | tf_op jit(solution)/shard_map/ppermute | solution.py:472
  20.1 17.5 %collective-permute-start.13 = (bf16[128,1280]{1,0:T(8,128)(2,1)S(1)}, bf16[128,1280]{1,0:T(8,128)(2,1)S(1)}, u32[]{:S(2)}, u32[]{:S(2)}) collective-permute-start(bf16[128,1280]{1,0:T(8,128)(2,1)S(1)} %shard_map.46), channel_id=1, source_target_pairs={{0,2},{2,0},{1,3},{3,1},{4,6},{6,4},{5,7},{7,5},{8,10},{10,8},{9,1... | collective-permute-start | bytes 983048 | tf_op jit(solution)/shard_map/ppermute | solution.py:472
  20.8 12.8 %collective-permute-start.14 = (bf16[64,1280]{1,0:T(8,128)(2,1)S(1)}, bf16[64,1280]{1,0:T(8,128)(2,1)S(1)}, u32[]{:S(2)}, u32[]{:S(2)}) collective-permute-start(bf16[64,1280]{1,0:T(8,128)(2,1)S(1)} %shard_map.48), channel_id=1, source_target_pairs={{0,6},{2,4},{4,2},{6,0},{1,7},{3,5},{5,3},{7,1},{8,14},{10,12},{12... | collective-permute-start | bytes 491528 | tf_op jit(solution)/shard_map/ppermute | solution.py:472
  23.3 4.3 %collective-permute-start.9 = (bf16[256,128]{1,0:T(8,128)(2,1)S(1)}, bf16[256,128]{1,0:T(8,128)(2,1)S(1)}, u32[]{:S(2)}, u32[]{:S(2)}) collective-permute-start(bf16[256,128]{1,0:T(8,128)(2,1)S(1)} %collective-permute-done.5.refs_5_), channel_id=1, source_target_pairs={{0,16},{16,0},{1,17},{17,1},{2,18},{18,2},{3,19},{19,3},{4,20},{20... | collective-permute-start | bytes 196616 | tf_op jit(solution)/shard_map/ppermute | solution.py:472
  25.2 4.3 %collective-permute-start.8 = (bf16[256,128]{1,0:T(8,128)(2,1)S(1)}, bf16[256,128]{1,0:T(8,128)(2,1)S(1)}, u32[]{:S(2)}, u32[]{:S(2)}) collective-permute-start(bf16[256,128]{1,0:T(8,128)(2,1)S(1)} %collective-permute-done.4.refs_4_), channel_id=1, source_target_pairs={{0,16},{16,0},{1,17},{17,1},{2,18},{18,2},{3,19},{19,3},{4,20},{20... | collective-permute-start | bytes 196616 | tf_op jit(solution)/shard_map/ppermute | solution.py:472
  33.6 6.2 %collective-permute-start.15 = (bf16[64,1280]{1,0:T(8,128)(2,1)S(1)}, bf16[64,1280]{1,0:T(8,128)(2,1)S(1)}, u32[]{:S(2)}, u32[]{:S(2)}) collective-permute-start(bf16[64,1280]{1,0:T(8,128)(2,1)S(1)} %shard_map.49.refs_5_), channel_id=1, source_target_pairs={{0,16},{16,0},{1,17},{17,1},{2,18},{18,2},{3,19},{19,3},{4,20},{20... | collective-permute-start | bytes 491528 | tf_op jit(solution)/shard_map/ppermute | solution.py:472
  34.1 5.2 %collective-permute-start.12 = (bf16[256,128]{1,0:T(8,128)(2,1)S(1)}, bf16[256,128]{1,0:T(8,128)(2,1)S(1)}, u32[]{:S(2)}, u32[]{:S(2)}) collective-permute-start(bf16[256,128]{1,0:T(8,128)(2,1)S(1)} %shard_map.44.refs_1_.refs_0_), channel_id=1, source_target_pairs={{0,10},{2,8},{8,2},{10,0},{1,11},{3,9},{9,3},{11,1},{4,14},{6,12},... | collective-permute-start | bytes 196616 | tf_op jit(solution)/shard_map/ppermute | solution.py:472
  34.1 5.2 %collective-permute-start.11 = (bf16[256,128]{1,0:T(8,128)(2,1)S(1)}, bf16[256,128]{1,0:T(8,128)(2,1)S(1)}, u32[]{:S(2)}, u32[]{:S(2)}) collective-permute-start(bf16[256,128]{1,0:T(8,128)(2,1)S(1)} %shard_map.44.refs_1_.refs_0_), channel_id=1, source_target_pairs={{0,8},{2,10},{8,0},{10,2},{1,9},{3,11},{9,1},{11,3},{4,12},{6,14},... | collective-permute-start | bytes 196616 | tf_op jit(solution)/shard_map/ppermute | solution.py:472
  35.0 4.9 %collective-permute-start.10 = (bf16[256,128]{1,0:T(8,128)(2,1)S(1)}, bf16[256,128]{1,0:T(8,128)(2,1)S(1)}, u32[]{:S(2)}, u32[]{:S(2)}) collective-permute-start(bf16[256,128]{1,0:T(8,128)(2,1)S(1)} %shard_map.44.refs_1_.refs_0_), channel_id=1, source_target_pairs={{0,2},{2,0},{8,10},{10,8},{1,3},{3,1},{9,11},{11,9},{4,6},{6,4},{1... | collective-permute-start | bytes 196616 | tf_op jit(solution)/shard_map/ppermute | solution.py:472
  40.8 1.7 %collective-permute-start.16 = (bf16[4,32,1280]{2,1,0:T(8,128)(2,1)S(1)}, bf16[4,32,1280]{2,1,0:T(8,128)(2,1)S(1)}, u32[]{:S(2)}, u32[]{:S(2)}) collective-permute-start(bf16[4,32,1280]{2,1,0:T(8,128)(2,1)S(1)} %get-tuple-element.39), channel_id=1, source_target_pairs={{0,1},{1,0},{2,3},{3,2},{4,5},{5,4},{6,7},{7,6},{8,9},{9,8},{10,11... | collective-permute-start | bytes 983048 | tf_op jit(solution)/shard_map/ppermute | solution.py:472
  43.7 4.8 %collective-permute-start.19 = (bf16[32,1280]{1,0:T(8,128)(2,1)S(1)}, bf16[32,1280]{1,0:T(8,128)(2,1)S(1)}, u32[]{:S(2)}, u32[]{:S(2)}) collective-permute-start(bf16[32,1280]{1,0:T(8,128)(2,1)S(1)} %shard_map.53), channel_id=1, source_target_pairs={{0,2},{2,0},{8,10},{10,8},{1,3},{3,1},{9,11},{11,9},{4,6},{6,4},{1... | collective-permute-start | bytes 245768 | tf_op jit(solution)/shard_map/ppermute | solution.py:472
  45.8 5.5 %collective-permute-start.17 = (bf16[32,1280]{1,0:T(8,128)(2,1)S(1)}, bf16[32,1280]{1,0:T(8,128)(2,1)S(1)}, u32[]{:S(2)}, u32[]{:S(2)}) collective-permute-start(bf16[32,1280]{1,0:T(8,128)(2,1)S(1)} %get-tuple-element.40), channel_id=1, source_target_pairs={{0,8},{2,10},{8,0},{10,2},{1,9},{3,11},{9,1},{11,3},{4,12},{6,14},... | collective-permute-start | bytes 245768 | tf_op jit(solution)/shard_map/ppermute | solution.py:472
  46.6 5.4 %collective-permute-start.18 = (bf16[32,1280]{1,0:T(8,128)(2,1)S(1)}, bf16[32,1280]{1,0:T(8,128)(2,1)S(1)}, u32[]{:S(2)}, u32[]{:S(2)}) collective-permute-start(bf16[32,1280]{1,0:T(8,128)(2,1)S(1)} %get-tuple-element.41.refs_0_), channel_id=1, source_target_pairs={{0,10},{2,8},{8,2},{10,0},{1,11},{3,9},{9,3},{11,1},{4,14},{6,12},... | collective-permute-start | bytes 245768 | tf_op jit(solution)/shard_map/ppermute | solution.py:472

commit v21 on v19

--- a/solution.py
+++ b/solution.py
@@ -162,7 +162,7 @@
 def sort_kernel(place_ref, *refs):
     *in_refs, q_ref, k_ref, v_ref = refs
     tok = q_ref.shape[0] // (2 * len(in_refs))
-    for i, ref in enumerate(in_refs):
+    for i, ref in enumerate(in_refs[::-1]):
         for core in range(2):
             at = rows_at((place_ref[0] // 2 ^ i) * 2 + core, tok)
             for j, out_ref in enumerate((q_ref, k_ref, v_ref)):
@@ -178,7 +178,7 @@
         in_specs=[SMEM] + [VMEM] * len(parts),
         out_specs=[VMEM] * 3,
         compiler_params=PARAMS,
-    )(place, *parts)
+    )(place, *parts[::-1])
 
 
 def join_kernel(*refs):
@@ -403,7 +403,7 @@
 def unpack_kernel(place_ref, *refs):
     *in_refs, out_ref = refs
     width = in_refs[0].shape[1]
-    for k, ref in enumerate(in_refs):
+    for k, ref in enumerate(in_refs[::-1]):
         out_ref[:, rows_at(place_ref[0] // 2 ^ k, width)] = ref[...]
 
 
@@ -415,7 +415,7 @@
         in_specs=[SMEM] + [VMEM] * len(parts),
         out_specs=VMEM,
         compiler_params=PARAMS,
-    )(place, *parts)
+    )(place, *parts[::-1])
 
 
 def xor(x, axis, by):

time: 51.9 us -> 51.1 us (0.985)
  starting transfers between devices: 24.1 us -> 23.4 us
    ppermute x20, starting transfers between devices: 24.1 us -> 23.4 us  [xor(): return lax.ppermute(x, axis, [(i, i ^ by) for i in range(size)])]
  transfers between devices with their start and end apart: 20 -> 20, of which waited for: 14 -> 15; matrix products, arithmetic and copies ran while one was open for 0% -> 0% of each run, Pallas kernels for 5% -> 5%
where the time goes in v21:
time: 51.1 us; the launch traced here: 51 us
  starting transfers between devices  23.4 us (46%)
  waiting for transfers between devices  22 us (43%)
  Pallas kernels  5.23 us (10%)
    ppermute x20, starting transfers between devices, xor(): return lax.ppermute(x, axis, [(i, i ^ by) for i in range(size)])  23.4 us
    ppermute x20, waiting for transfers between devices, xor(): return lax.ppermute(x, axis, [(i, i ^ by) for i in range(size)])  22 us
    pallas_call x1, Pallas kernels, project(): pl.pallas_call(functools.partial(project_kernel, blks, sizes), out_shape=...  1.03 us
  transfers between devices with their start and end apart: 20, of which 15 were waited for; matrix products, arithmetic and copies ran while one was open for 0% of the time, Pallas kernels for 5%

profile of v21, /device:TPU:0, one launch (start us, length us, event | category | flops | bytes accessed | tf_op | source)
XLA Modules:
  0.0 51.0 jit_solution(17317534117919486227)
XLA Ops:
  0.0 0.0 copy-start.1
  0.0 1.0 %shard_map.41 = bf16[640,128]{1,0:T(8,128)(2,1)S(1)} custom-call(bf16[128,5120]{1,0:T(8,128)(2,1)} %refs_4_.1), custom_call_target="tpu_custom_call" | custom-call | tf_op jit(solution)/shard_map/pallas_call | solution.py:96
  1.0 4.1 %collective-permute-start.6 = (bf16[640,128]{1,0:T(8,128)(2,1)S(1)}, bf16[640,128]{1,0:T(8,128)(2,1)S(1)}, u32[]{:S(2)}, u32[]{:S(2)}) collective-permute-start(bf16[640,128]{1,0:T(8,128)(2,1)S(1)} %shard_map.41), channel_id=1, source_target_pairs={{0,4},{4,0},{1,5},{5,1},{2,6},{6,2},{3,7},{7,3},{8,12},{12,8},{9,1... | collective-permute-start | bytes 491528 | tf_op jit(solution)/shard_map/ppermute | solution.py:423
  5.1 0.0 copy-done.1
  5.1 0.1 shard_map.37
  5.2 0.1 collective-permute-start
  5.3 1.3 %collective-permute-done.got_ref = bf16[4,96,128]{2,1,0:T(8,128)(2,1)S(1)} collective-permute-done((bf16[4,96,128]{2,1,0:T(8,128)(2,1)S(1)}, bf16[4,96,128]{2,1,0:T(8,128)(2,1)S(1)}, u32[]{:S(2)}, u32[]{:S(2)}) %collective-permute-start) | collective-permute-done | bytes 98336 | tf_op jit(solution)/shard_map/ppermute | solution.py:423
  6.5 2.6 %collective-permute-start.1 = (bf16[2,96,128]{2,1,0:T(8,128)(2,1)S(1)}, bf16[2,96,128]{2,1,0:T(8,128)(2,1)S(1)}, u32[]{:S(2)}, u32[]{:S(2)}) collective-permute-start(bf16[2,96,128]{2,1,0:T(8,128)(2,1)S(1)} %get-tuple-element.27), channel_id=1, source_target_pairs={{0,10},{2,8},{8,2},{10,0},{1,11},{3,9},{9,3},{11,1},{4,14},{6,12},... | collective-permute-start | bytes 147464 | tf_op jit(solution)/shard_map/ppermute | solution.py:423
  9.1 0.5 %collective-permute-start.2 = (bf16[2,96,128]{2,1,0:T(8,128)(2,1)S(1)}, bf16[2,96,128]{2,1,0:T(8,128)(2,1)S(1)}, u32[]{:S(2)}, u32[]{:S(2)}) collective-permute-start(bf16[2,96,128]{2,1,0:T(8,128)(2,1)S(1)} %get-tuple-element.28), channel_id=1, source_target_pairs={{0,8},{2,10},{8,0},{10,2},{1,9},{3,11},{9,1},{11,3},{4,12},{6,14},... | collective-permute-start | bytes 147464 | tf_op jit(solution)/shard_map/ppermute | solution.py:423
  9.7 0.4 collective-permute-start.3
  10.1 1.7 %collective-permute-done.1.refs_0_ = bf16[2,96,128]{2,1,0:T(8,128)(2,1)S(1)} collective-permute-done((bf16[2,96,128]{2,1,0:T(8,128)(2,1)S(1)}, bf16[2,96,128]{2,1,0:T(8,128)(2,1)S(1)}, u32[]{:S(2)}, u32[]{:S(2)}) %collective-permute-start.1) | collective-permute-done | bytes 49184 | tf_op jit(solution)/shard_map/ppermute | solution.py:423
  11.8 1.4 %collective-permute-done.2.refs_1_ = bf16[2,96,128]{2,1,0:T(8,128)(2,1)S(1)} collective-permute-done((bf16[2,96,128]{2,1,0:T(8,128)(2,1)S(1)}, bf16[2,96,128]{2,1,0:T(8,128)(2,1)S(1)}, u32[]{:S(2)}, u32[]{:S(2)}) %collective-permute-start.2) | collective-permute-done | bytes 49184 | tf_op jit(solution)/shard_map/ppermute | solution.py:423
  13.2 1.5 %collective-permute-done.3.refs_2_ = bf16[2,96,128]{2,1,0:T(8,128)(2,1)S(1)} collective-permute-done((bf16[2,96,128]{2,1,0:T(8,128)(2,1)S(1)}, bf16[2,96,128]{2,1,0:T(8,128)(2,1)S(1)}, u32[]{:S(2)}, u32[]{:S(2)}) %collective-permute-start.3) | collective-permute-done | bytes 49184 | tf_op jit(solution)/shard_map/ppermute | solution.py:423
  14.7 0.0 collective-permute-done.6.refs_0_
  14.8 0.0 copy-start
  14.8 0.0 copy-start.2
  14.8 1.6 %collective-permute-start.7 = (bf16[1152,128]{1,0:T(8,128)(2,1)S(1)}, bf16[1152,128]{1,0:T(8,128)(2,1)S(1)}, u32[]{:S(2)}, u32[]{:S(2)}) collective-permute-start(bf16[1152,128]{1,0:T(8,128)(2,1)S(1)} %shard_map.43), channel_id=1, source_target_pairs={{0,16},{16,0},{1,17},{17,1},{2,18},{18,2},{3,19},{19,3},{4,20},{20... | collective-permute-start | bytes 884744 | tf_op jit(solution)/shard_map/ppermute | solution.py:423
  16.5 0.5 collective-permute-start.5
  16.9 2.5 %collective-permute-start.4 = (bf16[256,128]{1,0:T(8,128)(2,1)S(1)}, bf16[256,128]{1,0:T(8,128)(2,1)S(1)}, u32[]{:S(2)}, u32[]{:S(2)}) collective-permute-start(bf16[256,128]{1,0:T(8,128)(2,1)S(1)} %get-tuple-element.34.refs_0_.refs_2_.refs_1_), channel_id=1, source_target_pairs={{0,4},{4,0},{1,5},{5,1},{2,6},{6,2},{3,7},{7,3},{8,12},{12,8},{9,1... | collective-permute-start | bytes 196616 | tf_op jit(solution)/shard_map/ppermute | solution.py:423
  19.4 0.1 pad_add_fusion.1.at_ref
  19.5 0.0 copy-done
  19.5 0.6 %shard_map.45 = (bf16[64,1280]{1,0:T(8,128)(2,1)S(1)}, bf16[128,1280]{1,0:T(8,128)(2,1)S(1)}) custom-call(s32[2]{0:T(128)S(1)} %pad_add_fusion.1.at_ref, bf16[128,5120]{1,0:T(8,128)(2,1)S(1)} %copy-done), custom_call_target="tpu_custom_call" | custom-call | tf_op jit(solution)/shard_map/pallas_call | solution.py:114
  20.1 0.1 collective-permute-start.13
  20.2 2.4 %collective-permute-start.14 = (bf16[64,1280]{1,0:T(8,128)(2,1)S(1)}, bf16[64,1280]{1,0:T(8,128)(2,1)S(1)}, u32[]{:S(2)}, u32[]{:S(2)}) collective-permute-start(bf16[64,1280]{1,0:T(8,128)(2,1)S(1)} %shard_map.47), channel_id=1, source_target_pairs={{0,6},{2,4},{4,2},{6,0},{1,7},{3,5},{5,3},{7,1},{8,14},{10,12},{12... | collective-permute-start | bytes 491528 | tf_op jit(solution)/shard_map/ppermute | solution.py:423
  22.6 0.5 collective-permute-done.5.refs_5_
  23.1 0.5 collective-permute-start.9
  23.6 1.6 %collective-permute-done.4.refs_4_ = bf16[256,128]{1,0:T(8,128)(2,1)S(1)} collective-permute-done((bf16[256,128]{1,0:T(8,128)(2,1)S(1)}, bf16[256,128]{1,0:T(8,128)(2,1)S(1)}, u32[]{:S(2)}, u32[]{:S(2)}) %collective-permute-start.4) | collective-permute-done | bytes 65568 | tf_op jit(solution)/shard_map/ppermute | solution.py:423
  25.2 0.4 collective-permute-start.8
  25.7 0.1 pad_add_fusion.base_ref
  25.7 0.0 copy-done.2
  25.7 0.7 %shard_map.40 = (f32[256,256]{1,0:T(8,128)S(1)}, f32[256,256]{1,0:T(8,128)S(1)}) custom-call(s32[2]{0:T(128)S(1)} %pad_add_fusion.base_ref, s32[8]{0:T(128)S(1)} %copy-done.2), custom_call_target="tpu_custom_call" | custom-call | tf_op jit(solution)/shard_map/pallas_call | solution.py:261
  26.4 0.9 %collective-permute-done.9.refs_8_ = bf16[256,128]{1,0:T(8,128)(2,1)S(1)} collective-permute-done((bf16[256,128]{1,0:T(8,128)(2,1)S(1)}, bf16[256,128]{1,0:T(8,128)(2,1)S(1)}, u32[]{:S(2)}, u32[]{:S(2)}) %collective-permute-start.9) | collective-permute-done | bytes 65568 | tf_op jit(solution)/shard_map/ppermute | solution.py:423
  27.4 2.1 %collective-permute-done.8.refs_7_ = bf16[256,128]{1,0:T(8,128)(2,1)S(1)} collective-permute-done((bf16[256,128]{1,0:T(8,128)(2,1)S(1)}, bf16[256,128]{1,0:T(8,128)(2,1)S(1)}, u32[]{:S(2)}, u32[]{:S(2)}) %collective-permute-start.8) | collective-permute-done | bytes 65568 | tf_op jit(solution)/shard_map/ppermute | solution.py:423
  29.5 0.0 collective-permute-done.7.refs_6_.refs_7_
  29.5 0.6 %shard_map.44.refs_1_.refs_0_ = bf16[256,128]{1,0:T(8,128)(2,1)S(1)} custom-call(bf16[256,128]{1,0:T(8,128)(2,1)S(1)} %get-tuple-element.31.q_ref, f32[256,256]{1,0:T(8,128)S(1)} %get-tuple-element.32.refs_0_, f32[256,256]{1,0:T(8,128)S(1)} %get-tuple-element.33.refs_1_, bf16[256,128]{1,0:T(8,128)(2,1)S(1)} %get-tuple-element.34.refs_0_.refs_2_.refs_1_, ...), custom_call_target="tpu_custom_call" | custom-call | tf_op jit(solution)/shard_map/pallas_call | solution.py:321
  30.1 3.1 %collective-permute-done.14.refs_0_ = bf16[64,1280]{1,0:T(8,128)(2,1)S(1)} collective-permute-done((bf16[64,1280]{1,0:T(8,128)(2,1)S(1)}, bf16[64,1280]{1,0:T(8,128)(2,1)S(1)}, u32[]{:S(2)}, u32[]{:S(2)}) %collective-permute-start.14) | collective-permute-done | bytes 163872 | tf_op jit(solution)/shard_map/ppermute | solution.py:423
  33.2 0.5 collective-permute-start.15
  33.7 0.0 collective-permute-start.12
  33.7 1.4 %collective-permute-start.11 = (bf16[256,128]{1,0:T(8,128)(2,1)S(1)}, bf16[256,128]{1,0:T(8,128)(2,1)S(1)}, u32[]{:S(2)}, u32[]{:S(2)}) collective-permute-start(bf16[256,128]{1,0:T(8,128)(2,1)S(1)} %shard_map.44.refs_1_.refs_0_), channel_id=1, source_target_pairs={{0,8},{2,10},{8,0},{10,2},{1,9},{3,11},{9,1},{11,3},{4,12},{6,14},... | collective-permute-start | bytes 196616 | tf_op jit(solution)/shard_map/ppermute | solution.py:423
  35.1 2.1 %collective-permute-start.10 = (bf16[256,128]{1,0:T(8,128)(2,1)S(1)}, bf16[256,128]{1,0:T(8,128)(2,1)S(1)}, u32[]{:S(2)}, u32[]{:S(2)}) collective-permute-start(bf16[256,128]{1,0:T(8,128)(2,1)S(1)} %shard_map.44.refs_1_.refs_0_), channel_id=1, source_target_pairs={{0,2},{2,0},{8,10},{10,8},{1,3},{3,1},{9,11},{11,9},{4,6},{6,4},{1... | collective-permute-start | bytes 196616 | tf_op jit(solution)/shard_map/ppermute | solution.py:423
  37.2 0.1 stack.52.at_ref
  37.3 0.0 collective-permute-done.13.refs_5_
  37.3 1.6 %collective-permute-done.12.refs_3_ = bf16[256,128]{1,0:T(8,128)(2,1)S(1)} collective-permute-done((bf16[256,128]{1,0:T(8,128)(2,1)S(1)}, bf16[256,128]{1,0:T(8,128)(2,1)S(1)}, u32[]{:S(2)}, u32[]{:S(2)}) %collective-permute-start.12) | collective-permute-done | bytes 65568 | tf_op jit(solution)/shard_map/ppermute | solution.py:423
  38.8 0.0 collective-permute-done.11.refs_2_
  38.9 0.6 %collective-permute-done.10.refs_1_ = bf16[256,128]{1,0:T(8,128)(2,1)S(1)} collective-permute-done((bf16[256,128]{1,0:T(8,128)(2,1)S(1)}, bf16[256,128]{1,0:T(8,128)(2,1)S(1)}, u32[]{:S(2)}, u32[]{:S(2)}) %collective-permute-start.10) | collective-permute-done | bytes 65568 | tf_op jit(solution)/shard_map/ppermute | solution.py:423
  39.5 0.0 collective-permute-done.15.refs_9_
  39.5 1.0 %shard_map.49 = (bf16[4,32,1280]{2,1,0:T(8,128)(2,1)S(1)}, bf16[256,512]{1,0:T(8,128)(2,1)S(1)}, bf16[512,1280]{1,0:T(8,128)(2,1)S(1)}) custom-call(s32[6]{0:T(128)S(1)} %stack.52.at_ref, s32[1]{0:T(128)} %bitcast.place_ref, bf16[256,128]{1,0:T(8,128)(2,1)S(1)} %shard_map.44.refs_1_.refs_0_, bf16[256,128]{1,0:T(8,128)(2,1)S(1)} %collective-permute-done.10.refs_1_, ...), custom_call_target="tpu_custom_call" | custom-call | tf_op jit(solution)/shard_map/pallas_call | solution.py:363
  40.5 0.1 collective-permute-start.16
  40.6 0.3 shard_map.50.x_ref
  40.9 1.3 %collective-permute-done.16.y_ref = bf16[4,32,1280]{2,1,0:T(8,128)(2,1)S(1)} collective-permute-done((bf16[4,32,1280]{2,1,0:T(8,128)(2,1)S(1)}, bf16[4,32,1280]{2,1,0:T(8,128)(2,1)S(1)}, u32[]{:S(2)}, u32[]{:S(2)}) %collective-permute-start.16) | collective-permute-done | bytes 327712 | tf_op jit(solution)/shard_map/ppermute | solution.py:423
  42.2 0.1 shard_map.51
  42.3 2.9 %collective-permute-start.17 = (bf16[32,1280]{1,0:T(8,128)(2,1)S(1)}, bf16[32,1280]{1,0:T(8,128)(2,1)S(1)}, u32[]{:S(2)}, u32[]{:S(2)}) collective-permute-start(bf16[32,1280]{1,0:T(8,128)(2,1)S(1)} %get-tuple-element.41), channel_id=1, source_target_pairs={{0,10},{2,8},{8,2},{10,0},{1,11},{3,9},{9,3},{11,1},{4,14},{6,12},... | collective-permute-start | bytes 245768 | tf_op jit(solution)/shard_map/ppermute | solution.py:423
  45.1 0.7 %collective-permute-start.18 = (bf16[32,1280]{1,0:T(8,128)(2,1)S(1)}, bf16[32,1280]{1,0:T(8,128)(2,1)S(1)}, u32[]{:S(2)}, u32[]{:S(2)}) collective-permute-start(bf16[32,1280]{1,0:T(8,128)(2,1)S(1)} %get-tuple-element.42), channel_id=1, source_target_pairs={{0,8},{2,10},{8,0},{10,2},{1,9},{3,11},{9,1},{11,3},{4,12},{6,14},... | collective-permute-start | bytes 245768 | tf_op jit(solution)/shard_map/ppermute | solution.py:423
  45.8 0.0 collective-permute-start.19
  45.8 2.1 %collective-permute-done.17.refs_0_ = bf16[32,1280]{1,0:T(8,128)(2,1)S(1)} collective-permute-done((bf16[32,1280]{1,0:T(8,128)(2,1)S(1)}, bf16[32,1280]{1,0:T(8,128)(2,1)S(1)}, u32[]{:S(2)}, u32[]{:S(2)}) %collective-permute-start.17) | collective-permute-done | bytes 81952 | tf_op jit(solution)/shard_map/ppermute | solution.py:423
  47.9 1.7 %collective-permute-done.18.refs_1_ = bf16[32,1280]{1,0:T(8,128)(2,1)S(1)} collective-permute-done((bf16[32,1280]{1,0:T(8,128)(2,1)S(1)}, bf16[32,1280]{1,0:T(8,128)(2,1)S(1)}, u32[]{:S(2)}, u32[]{:S(2)}) %collective-permute-start.18) | collective-permute-done | bytes 81952 | tf_op jit(solution)/shard_map/ppermute | solution.py:423
  49.6 0.6 %collective-permute-done.19.refs_2_ = bf16[32,1280]{1,0:T(8,128)(2,1)S(1)} collective-permute-done((bf16[32,1280]{1,0:T(8,128)(2,1)S(1)}, bf16[32,1280]{1,0:T(8,128)(2,1)S(1)}, u32[]{:S(2)}, u32[]{:S(2)}) %collective-permute-start.19) | collective-permute-done | bytes 81952 | tf_op jit(solution)/shard_map/ppermute | solution.py:423
  50.2 0.8 %shard_map.52 = bf16[32,5120]{1,0:T(8,128)(2,1)} custom-call(s32[1]{0:T(128)} %bitcast.place_ref, bf16[32,1280]{1,0:T(8,128)(2,1)S(1)} %collective-permute-done.17.refs_0_, bf16[32,1280]{1,0:T(8,128)(2,1)S(1)} %collective-permute-done.18.refs_1_, bf16[32,1280]{1,0:T(8,128)(2,1)S(1)} %collective-permute-done.19.refs_2_, ...), custom_call_target="tpu_custom_call" | custom-call | tf_op jit(solution)/shard_map/pallas_call | solution.py:412
  (7 shorter events, 0.1 us)
Async XLA Ops:
  0.0 5.1 %copy-start.1 = (bf16[3,32,1024]{2,1,0:T(8,128)(2,1)S(1)}, bf16[3,32,1024]{2,1,0:T(8,128)(2,1)}, u32[]{:S(2)}) copy-start(bf16[3,32,1024]{2,1,0:T(8,128)(2,1)} %x_ref.3) | copy-start | bytes 589828
  1.0 13.7 %collective-permute-start.6 = (bf16[640,128]{1,0:T(8,128)(2,1)S(1)}, bf16[640,128]{1,0:T(8,128)(2,1)S(1)}, u32[]{:S(2)}, u32[]{:S(2)}) collective-permute-start(bf16[640,128]{1,0:T(8,128)(2,1)S(1)} %shard_map.41), channel_id=1, source_target_pairs={{0,4},{4,0},{1,5},{5,1},{2,6},{6,2},{3,7},{7,3},{8,12},{12,8},{9,1... | collective-permute-start | bytes 491528 | tf_op jit(solution)/shard_map/ppermute | solution.py:423
  5.2 1.4 %collective-permute-start = (bf16[4,96,128]{2,1,0:T(8,128)(2,1)S(1)}, bf16[4,96,128]{2,1,0:T(8,128)(2,1)S(1)}, u32[]{:S(2)}, u32[]{:S(2)}) collective-permute-start(bf16[4,96,128]{2,1,0:T(8,128)(2,1)S(1)} %get-tuple-element.26), channel_id=1, source_target_pairs={{0,1},{1,0},{2,3},{3,2},{4,5},{5,4},{6,7},{7,6},{8,9},{9,8},{10,11... | collective-permute-start | bytes 294920 | tf_op jit(solution)/shard_map/ppermute | solution.py:423
  6.5 5.3 %collective-permute-start.1 = (bf16[2,96,128]{2,1,0:T(8,128)(2,1)S(1)}, bf16[2,96,128]{2,1,0:T(8,128)(2,1)S(1)}, u32[]{:S(2)}, u32[]{:S(2)}) collective-permute-start(bf16[2,96,128]{2,1,0:T(8,128)(2,1)S(1)} %get-tuple-element.27), channel_id=1, source_target_pairs={{0,10},{2,8},{8,2},{10,0},{1,11},{3,9},{9,3},{11,1},{4,14},{6,12},... | collective-permute-start | bytes 147464 | tf_op jit(solution)/shard_map/ppermute | solution.py:423
  9.1 4.1 %collective-permute-start.2 = (bf16[2,96,128]{2,1,0:T(8,128)(2,1)S(1)}, bf16[2,96,128]{2,1,0:T(8,128)(2,1)S(1)}, u32[]{:S(2)}, u32[]{:S(2)}) collective-permute-start(bf16[2,96,128]{2,1,0:T(8,128)(2,1)S(1)} %get-tuple-element.28), channel_id=1, source_target_pairs={{0,8},{2,10},{8,0},{10,2},{1,9},{3,11},{9,1},{11,3},{4,12},{6,14},... | collective-permute-start | bytes 147464 | tf_op jit(solution)/shard_map/ppermute | solution.py:423
  9.7 5.1 %collective-permute-start.3 = (bf16[2,96,128]{2,1,0:T(8,128)(2,1)S(1)}, bf16[2,96,128]{2,1,0:T(8,128)(2,1)S(1)}, u32[]{:S(2)}, u32[]{:S(2)}) collective-permute-start(bf16[2,96,128]{2,1,0:T(8,128)(2,1)S(1)} %get-tuple-element.29), channel_id=1, source_target_pairs={{0,2},{2,0},{8,10},{10,8},{1,3},{3,1},{9,11},{11,9},{4,6},{6,4},{1... | collective-permute-start | bytes 147464 | tf_op jit(solution)/shard_map/ppermute | solution.py:423
  14.8 4.7 %copy-start = (bf16[128,5120]{1,0:T(8,128)(2,1)S(1)}, bf16[128,5120]{1,0:T(8,128)(2,1)}, u32[]{:S(2)}) copy-start(bf16[128,5120]{1,0:T(8,128)(2,1)} %refs_4_.1) | copy-start | bytes 3932164
  14.8 10.9 %copy-start.2 = (s32[8]{0:T(128)S(1)}, s32[8]{0:T(128)}, u32[]{:S(2)}) copy-start(s32[8]{0:T(128)} %clip_ref.1) | copy-start | bytes 100
  14.8 14.7 %collective-permute-start.7 = (bf16[1152,128]{1,0:T(8,128)(2,1)S(1)}, bf16[1152,128]{1,0:T(8,128)(2,1)S(1)}, u32[]{:S(2)}, u32[]{:S(2)}) collective-permute-start(bf16[1152,128]{1,0:T(8,128)(2,1)S(1)} %shard_map.43), channel_id=1, source_target_pairs={{0,16},{16,0},{1,17},{17,1},{2,18},{18,2},{3,19},{19,3},{4,20},{20... | collective-permute-start | bytes 884744 | tf_op jit(solution)/shard_map/ppermute | solution.py:423
  16.5 6.6 %collective-permute-start.5 = (bf16[256,128]{1,0:T(8,128)(2,1)S(1)}, bf16[256,128]{1,0:T(8,128)(2,1)S(1)}, u32[]{:S(2)}, u32[]{:S(2)}) collective-permute-start(bf16[256,128]{1,0:T(8,128)(2,1)S(1)} %get-tuple-element.35.refs_1_.refs_3_), channel_id=1, source_target_pairs={{0,4},{4,0},{1,5},{5,1},{2,6},{6,2},{3,7},{7,3},{8,12},{12,8},{9,1... | collective-permute-start | bytes 196616 | tf_op jit(solution)/shard_map/ppermute | solution.py:423
  16.9 8.3 %collective-permute-start.4 = (bf16[256,128]{1,0:T(8,128)(2,1)S(1)}, bf16[256,128]{1,0:T(8,128)(2,1)S(1)}, u32[]{:S(2)}, u32[]{:S(2)}) collective-permute-start(bf16[256,128]{1,0:T(8,128)(2,1)S(1)} %get-tuple-element.34.refs_0_.refs_2_.refs_1_), channel_id=1, source_target_pairs={{0,4},{4,0},{1,5},{5,1},{2,6},{6,2},{3,7},{7,3},{8,12},{12,8},{9,1... | collective-permute-start | bytes 196616 | tf_op jit(solution)/shard_map/ppermute | solution.py:423
  20.1 17.2 %collective-permute-start.13 = (bf16[128,1280]{1,0:T(8,128)(2,1)S(1)}, bf16[128,1280]{1,0:T(8,128)(2,1)S(1)}, u32[]{:S(2)}, u32[]{:S(2)}) collective-permute-start(bf16[128,1280]{1,0:T(8,128)(2,1)S(1)} %shard_map.46), channel_id=1, source_target_pairs={{0,2},{2,0},{1,3},{3,1},{4,6},{6,4},{5,7},{7,5},{8,10},{10,8},{9,1... | collective-permute-start | bytes 983048 | tf_op jit(solution)/shard_map/ppermute | solution.py:423
  20.2 13.0 %collective-permute-start.14 = (bf16[64,1280]{1,0:T(8,128)(2,1)S(1)}, bf16[64,1280]{1,0:T(8,128)(2,1)S(1)}, u32[]{:S(2)}, u32[]{:S(2)}) collective-permute-start(bf16[64,1280]{1,0:T(8,128)(2,1)S(1)} %shard_map.47), channel_id=1, source_target_pairs={{0,6},{2,4},{4,2},{6,0},{1,7},{3,5},{5,3},{7,1},{8,14},{10,12},{12... | collective-permute-start | bytes 491528 | tf_op jit(solution)/shard_map/ppermute | solution.py:423
  23.1 4.3 %collective-permute-start.9 = (bf16[256,128]{1,0:T(8,128)(2,1)S(1)}, bf16[256,128]{1,0:T(8,128)(2,1)S(1)}, u32[]{:S(2)}, u32[]{:S(2)}) collective-permute-start(bf16[256,128]{1,0:T(8,128)(2,1)S(1)} %collective-permute-done.5.refs_5_), channel_id=1, source_target_pairs={{0,16},{16,0},{1,17},{17,1},{2,18},{18,2},{3,19},{19,3},{4,20},{20... | collective-permute-start | bytes 196616 | tf_op jit(solution)/shard_map/ppermute | solution.py:423
  25.2 4.3 %collective-permute-start.8 = (bf16[256,128]{1,0:T(8,128)(2,1)S(1)}, bf16[256,128]{1,0:T(8,128)(2,1)S(1)}, u32[]{:S(2)}, u32[]{:S(2)}) collective-permute-start(bf16[256,128]{1,0:T(8,128)(2,1)S(1)} %collective-permute-done.4.refs_4_), channel_id=1, source_target_pairs={{0,16},{16,0},{1,17},{17,1},{2,18},{18,2},{3,19},{19,3},{4,20},{20... | collective-permute-start | bytes 196616 | tf_op jit(solution)/shard_map/ppermute | solution.py:423
  33.2 6.3 %collective-permute-start.15 = (bf16[64,1280]{1,0:T(8,128)(2,1)S(1)}, bf16[64,1280]{1,0:T(8,128)(2,1)S(1)}, u32[]{:S(2)}, u32[]{:S(2)}) collective-permute-start(bf16[64,1280]{1,0:T(8,128)(2,1)S(1)} %shard_map.48.refs_8_), channel_id=1, source_target_pairs={{0,16},{16,0},{1,17},{17,1},{2,18},{18,2},{3,19},{19,3},{4,20},{20... | collective-permute-start | bytes 491528 | tf_op jit(solution)/shard_map/ppermute | solution.py:423
  33.7 5.2 %collective-permute-start.12 = (bf16[256,128]{1,0:T(8,128)(2,1)S(1)}, bf16[256,128]{1,0:T(8,128)(2,1)S(1)}, u32[]{:S(2)}, u32[]{:S(2)}) collective-permute-start(bf16[256,128]{1,0:T(8,128)(2,1)S(1)} %shard_map.44.refs_1_.refs_0_), channel_id=1, source_target_pairs={{0,10},{2,8},{8,2},{10,0},{1,11},{3,9},{9,3},{11,1},{4,14},{6,12},... | collective-permute-start | bytes 196616 | tf_op jit(solution)/shard_map/ppermute | solution.py:423
  33.7 5.2 %collective-permute-start.11 = (bf16[256,128]{1,0:T(8,128)(2,1)S(1)}, bf16[256,128]{1,0:T(8,128)(2,1)S(1)}, u32[]{:S(2)}, u32[]{:S(2)}) collective-permute-start(bf16[256,128]{1,0:T(8,128)(2,1)S(1)} %shard_map.44.refs_1_.refs_0_), channel_id=1, source_target_pairs={{0,8},{2,10},{8,0},{10,2},{1,9},{3,11},{9,1},{11,3},{4,12},{6,14},... | collective-permute-start | bytes 196616 | tf_op jit(solution)/shard_map/ppermute | solution.py:423
  35.1 4.4 %collective-permute-start.10 = (bf16[256,128]{1,0:T(8,128)(2,1)S(1)}, bf16[256,128]{1,0:T(8,128)(2,1)S(1)}, u32[]{:S(2)}, u32[]{:S(2)}) collective-permute-start(bf16[256,128]{1,0:T(8,128)(2,1)S(1)} %shard_map.44.refs_1_.refs_0_), channel_id=1, source_target_pairs={{0,2},{2,0},{8,10},{10,8},{1,3},{3,1},{9,11},{11,9},{4,6},{6,4},{1... | collective-permute-start | bytes 196616 | tf_op jit(solution)/shard_map/ppermute | solution.py:423
  40.5 1.7 %collective-permute-start.16 = (bf16[4,32,1280]{2,1,0:T(8,128)(2,1)S(1)}, bf16[4,32,1280]{2,1,0:T(8,128)(2,1)S(1)}, u32[]{:S(2)}, u32[]{:S(2)}) collective-permute-start(bf16[4,32,1280]{2,1,0:T(8,128)(2,1)S(1)} %get-tuple-element.40), channel_id=1, source_target_pairs={{0,1},{1,0},{2,3},{3,2},{4,5},{5,4},{6,7},{7,6},{8,9},{9,8},{10,11... | collective-permute-start | bytes 983048 | tf_op jit(solution)/shard_map/ppermute | solution.py:423
  42.3 5.7 %collective-permute-start.17 = (bf16[32,1280]{1,0:T(8,128)(2,1)S(1)}, bf16[32,1280]{1,0:T(8,128)(2,1)S(1)}, u32[]{:S(2)}, u32[]{:S(2)}) collective-permute-start(bf16[32,1280]{1,0:T(8,128)(2,1)S(1)} %get-tuple-element.41), channel_id=1, source_target_pairs={{0,10},{2,8},{8,2},{10,0},{1,11},{3,9},{9,3},{11,1},{4,14},{6,12},... | collective-permute-start | bytes 245768 | tf_op jit(solution)/shard_map/ppermute | solution.py:423
  45.1 4.5 %collective-permute-start.18 = (bf16[32,1280]{1,0:T(8,128)(2,1)S(1)}, bf16[32,1280]{1,0:T(8,128)(2,1)S(1)}, u32[]{:S(2)}, u32[]{:S(2)}) collective-permute-start(bf16[32,1280]{1,0:T(8,128)(2,1)S(1)} %get-tuple-element.42), channel_id=1, source_target_pairs={{0,8},{2,10},{8,0},{10,2},{1,9},{3,11},{9,1},{11,3},{4,12},{6,14},... | collective-permute-start | bytes 245768 | tf_op jit(solution)/shard_map/ppermute | solution.py:423
  45.8 4.4 %collective-permute-start.19 = (bf16[32,1280]{1,0:T(8,128)(2,1)S(1)}, bf16[32,1280]{1,0:T(8,128)(2,1)S(1)}, u32[]{:S(2)}, u32[]{:S(2)}) collective-permute-start(bf16[32,1280]{1,0:T(8,128)(2,1)S(1)} %get-tuple-element.43), channel_id=1, source_target_pairs={{0,2},{2,0},{8,10},{10,8},{1,3},{3,1},{9,11},{11,9},{4,6},{6,4},{1... | collective-permute-start | bytes 245768 | tf_op jit(solution)/shard_map/ppermute | solution.py:423

commit v22 on v21

--- a/solution.py
+++ b/solution.py
@@ -12,6 +12,7 @@
 FRB = 2
 TPF = 16
 LANES = 128
+UNIT = 16
 VMEM = pl.BlockSpec(memory_space=pltpu.VMEM)
 SMEM = pl.BlockSpec(memory_space=pltpu.SMEM)
 ANY = pl.BlockSpec(memory_space=pl.ANY)
@@ -79,7 +80,8 @@
     )
 
 
-def blocks_kernel(row_axis, col_axes, x_ref, out_ref, held, sem):
+def blocks_kernel(row_axis, col_axes, x_ref, *refs):
+    *out_refs, held, sem = refs
     depth, cols = held.shape
     col = 0
     for axis in col_axes:
@@ -88,16 +90,23 @@
     copy = pltpu.make_async_copy(piece, held, sem)
     copy.start()
     copy.wait()
-    for j in range(cols // LANES):
-        out_ref[j * depth:(j + 1) * depth, :] = held[:, j * LANES:(j + 1) * LANES]
-
-
-def blocks(x, depth, cols, row_axis, col_axes):
+    first = 0
+    for out_ref in out_refs:
+        part = out_ref.shape[0] // (cols // LANES)
+        for j in range(cols // LANES):
+            out_ref[j * part:(j + 1) * part, :] = held[
+                first:first + part, j * LANES:(j + 1) * LANES
+            ]
+        first += part
+
+
+def blocks(x, cuts, cols, row_axis, col_axes):
+    depth = sum(cuts)
     return pl.pallas_call(
         functools.partial(blocks_kernel, row_axis, col_axes),
-        out_shape=jax.ShapeDtypeStruct((cols // LANES * depth, LANES), x.dtype),
+        out_shape=[jax.ShapeDtypeStruct((cols // LANES * n, LANES), x.dtype) for n in cuts],
         in_specs=[pl.BlockSpec(memory_space=pltpu.HBM)],
-        out_specs=VMEM,
+        out_specs=[VMEM] * len(cuts),
         scratch_shapes=[pltpu.VMEM((depth, cols), x.dtype), pltpu.SemaphoreType.DMA],
         compiler_params=PARAMS,
     )(pltpu.with_memory_space_constraint(x, pltpu.HBM))
@@ -338,12 +347,11 @@
         for b in range(blks):
             a_ref[b * tok:(b + 1) * tok, at] = ref[rows_at(2 * b + other, tok), :]
             a_ref[(blks + b) * tok:(blks + b + 1) * tok, at] = ref[rows_at(2 * b + 1 - other, tok), :]
-    for i, (ref, rows) in enumerate(zip(w_refs, sizes)):
-        at = rows_at(at_ref[i], rows)
+    for i, (ref, (rows, first)) in enumerate(zip(w_refs, sizes)):
+        at = pl.ds(pl.multiple_of(at_ref[i] * UNIT, UNIT), rows)
         if ref.shape[1] >= cols:
             w_all[at, :] = ref[:, rows_at(blk, cols)] if ref.shape[1] > cols else ref[...]
         else:
-            first = ref.shape[0] - cols // LANES * rows
             for j in range(cols // LANES):
                 w_all[at, j * LANES:(j + 1) * LANES] = ref[first + j * rows:first + (j + 1) * rows]
     dot = jnp.dot(a_ref[:blks * tok, :], w_all[...], preferred_element_type=jnp.float32)
@@ -435,14 +443,17 @@
     theirs = x * 2 + 1 - zl
     row, half = zh * 2 + zl, head_dim // 2
 
-    w_far = blocks(w_out, half, cols, "y", quarter)
-    far = after(xor(w_far, ("zh",), 1), cost=AHEAD)
+    cuts = (half - half // 4, half // 4)
+    w_first, w_second = blocks(w_out, cuts, cols, "y", quarter)
+    first = after(xor(w_first, ("zh",), 1), cost=AHEAD)
     w_corner, w_near = pieces(w_out, y, theirs, cols)
     kept, given = lanes(qkv, core, head_dim)
-    shared = swap_all(deal(kept, xor(given, ("core",), 1), place), quarter)
+    got = xor(given, ("core",), 1)
+    shared = swap_all(deal(kept, got, place), quarter)
+    second = after(xor(after(w_second, got), ("zh",), 1), cost=None)
     q, k, v = sort(shared, place)
     k_far, v_far = xor(k, ("zh",), 1), xor(v, ("zh",), 1)
-    near = xor(join(k, v, far), ("y",), 1)
+    near = xor(join(k, v, first, second), ("y",), 1)
     corner = xor(after(w_corner, k), ("zh", "zl"), 3)
     w_next = xor(after(w_near, k), ("zl",), 1)
     kvs = [(k, v), (k_far, v_far), near, (xor(k_far, ("y",), 1), xor(v_far, ("y",), 1))]
@@ -453,9 +464,14 @@
     corner = after(corner, attn)
     corner_rest = xor(corner, ("y",), 1)
     attns = swap_all([attn] * 4, quarter)
-    w_parts = [w_out, w_next, far, near, corner, corner_rest]
-    sizes = [head_dim, head_dim, half, half, half, half]
-    at = [row, row ^ 1] + [2 * (row ^ by) + h for by in (2, 3) for h in (y, 1 - y)]
+    w_parts = [w_out, w_next, first, second, near, near, corner, corner_rest]
+    tail = 2 * k.shape[0]
+    sizes = [(head_dim, 0), (head_dim, 0), (cuts[0], 0), (cuts[1], 0)]
+    sizes += [(cuts[0], tail), (cuts[1], tail + first.shape[0]), (half, 0), (half, 0)]
+    unit = head_dim // UNIT
+    at = [row * unit, (row ^ 1) * unit]
+    at += [(2 * (row ^ 2) + h) * (unit // 2) + i for h in (y, 1 - y) for i in (0, cuts[0] // UNIT)]
+    at += [(2 * (row ^ 3) + h) * (unit // 2) for h in (y, 1 - y)]
     parts = project(attns, w_parts, sizes, at, place, tok, cols)
     return unpack(swap_all(parts, quarter), place)
 
@@ -476,8 +492,8 @@
     mask_of = masks([0], 2 * tok, tok, 2 * blks * tok, frame_clip)
     attn = attention(q, kvs, mask_of, [0] * rows, head_dim)
     attns = swap_all([attn] * blks, ("blk",))
-    at = [row ^ by for by in range(rows)]
-    parts = project(attns, w_parts, [head_dim] * rows, at, place, tok, cols)
+    at = [(row ^ by) * (head_dim // UNIT) for by in range(rows)]
+    parts = project(attns, w_parts, [(head_dim, 0)] * rows, at, place, tok, cols)
     return unpack(swap_all(parts, ("blk",)), place)
 
 

time: 51.1 us -> 53 us (1.037)
  starting transfers between devices: 23.4 us -> 25.9 us
  waiting for transfers between devices: 22 us -> 21.3 us
    ppermute x20 -> x21, starting transfers between devices: 23.4 us -> 25.9 us  [xor(): return lax.ppermute(x, axis, [(i, i ^ by) for i in range(size)])]
    ppermute x20 -> x21, waiting for transfers between devices: 22 us -> 21.3 us  [xor(): return lax.ppermute(x, axis, [(i, i ^ by) for i in range(size)])]
  transfers between devices with their start and end apart: 20 -> 21, of which waited for: 15 -> 14; matrix products, arithmetic and copies ran while one was open for 0% -> 0% of each run, Pallas kernels for 5% -> 4%
where the time goes in v22:
time: 53 us; the launch traced here: 52.9 us
  starting transfers between devices  25.9 us (49%)
  waiting for transfers between devices  21.3 us (40%)
  Pallas kernels  5.22 us (10%)
    ppermute x21, starting transfers between devices, xor(): return lax.ppermute(x, axis, [(i, i ^ by) for i in range(size)])  25.9 us
    ppermute x21, waiting for transfers between devices, xor(): return lax.ppermute(x, axis, [(i, i ^ by) for i in range(size)])  21.3 us
  transfers between devices with their start and end apart: 21, of which 14 were waited for; matrix products, arithmetic and copies ran while one was open for 0% of the time, Pallas kernels for 4%

profile of v22, /device:TPU:0, one launch (start us, length us, event | category | flops | bytes accessed | tf_op | source)
XLA Modules:
  0.0 52.9 jit_solution(8358993659800340179)
XLA Ops:
  0.0 0.0 copy-start.1
  0.0 1.0 %shard_map.41 = (bf16[480,128]{1,0:T(8,128)(2,1)S(1)}, bf16[160,128]{1,0:T(8,128)(2,1)S(1)}) custom-call(bf16[128,5120]{1,0:T(8,128)(2,1)} %refs_4_.1), custom_call_target="tpu_custom_call" | custom-call | tf_op jit(solution)/shard_map/pallas_call | solution.py:105
  1.0 4.1 %collective-permute-start.6 = (bf16[480,128]{1,0:T(8,128)(2,1)S(1)}, bf16[480,128]{1,0:T(8,128)(2,1)S(1)}, u32[]{:S(2)}, u32[]{:S(2)}) collective-permute-start(bf16[480,128]{1,0:T(8,128)(2,1)S(1)} %get-tuple-element.38), channel_id=1, source_target_pairs={{0,4},{4,0},{1,5},{5,1},{2,6},{6,2},{3,7},{7,3},{8,12},{12,8},{9,1... | collective-permute-start | bytes 368648 | tf_op jit(solution)/shard_map/ppermute | solution.py:431
  5.1 0.0 copy-done.1
  5.1 0.1 shard_map.37
  5.2 0.1 collective-permute-start
  5.3 1.3 %collective-permute-done.got_ref.refs_1_ = bf16[4,96,128]{2,1,0:T(8,128)(2,1)S(1)} collective-permute-done((bf16[4,96,128]{2,1,0:T(8,128)(2,1)S(1)}, bf16[4,96,128]{2,1,0:T(8,128)(2,1)S(1)}, u32[]{:S(2)}, u32[]{:S(2)}) %collective-permute-start) | collective-permute-done | bytes 98336 | tf_op jit(solution)/shard_map/ppermute | solution.py:431
  6.5 0.0 collective-permute-start.7
  6.6 2.9 %collective-permute-start.1 = (bf16[2,96,128]{2,1,0:T(8,128)(2,1)S(1)}, bf16[2,96,128]{2,1,0:T(8,128)(2,1)S(1)}, u32[]{:S(2)}, u32[]{:S(2)}) collective-permute-start(bf16[2,96,128]{2,1,0:T(8,128)(2,1)S(1)} %get-tuple-element.29), channel_id=1, source_target_pairs={{0,10},{2,8},{8,2},{10,0},{1,11},{3,9},{9,3},{11,1},{4,14},{6,12},... | collective-permute-start | bytes 147464 | tf_op jit(solution)/shard_map/ppermute | solution.py:431
  9.5 0.5 %collective-permute-start.2 = (bf16[2,96,128]{2,1,0:T(8,128)(2,1)S(1)}, bf16[2,96,128]{2,1,0:T(8,128)(2,1)S(1)}, u32[]{:S(2)}, u32[]{:S(2)}) collective-permute-start(bf16[2,96,128]{2,1,0:T(8,128)(2,1)S(1)} %get-tuple-element.30), channel_id=1, source_target_pairs={{0,8},{2,10},{8,0},{10,2},{1,9},{3,11},{9,1},{11,3},{4,12},{6,14},... | collective-permute-start | bytes 147464 | tf_op jit(solution)/shard_map/ppermute | solution.py:431
  10.0 0.1 collective-permute-start.3
  10.1 1.8 %collective-permute-done.6.refs_0_ = bf16[480,128]{1,0:T(8,128)(2,1)S(1)} collective-permute-done((bf16[480,128]{1,0:T(8,128)(2,1)S(1)}, bf16[480,128]{1,0:T(8,128)(2,1)S(1)}, u32[]{:S(2)}, u32[]{:S(2)}) %collective-permute-start.6) | collective-permute-done | bytes 122912 | tf_op jit(solution)/shard_map/ppermute | solution.py:431
  11.9 0.0 copy-start
  11.9 0.9 %collective-permute-done.7.refs_0_ = bf16[160,128]{1,0:T(8,128)(2,1)S(1)} collective-permute-done((bf16[160,128]{1,0:T(8,128)(2,1)S(1)}, bf16[160,128]{1,0:T(8,128)(2,1)S(1)}, u32[]{:S(2)}, u32[]{:S(2)}) %collective-permute-start.7) | collective-permute-done | bytes 40992 | tf_op jit(solution)/shard_map/ppermute | solution.py:431
  12.8 1.2 %collective-permute-done.1.refs_0_ = bf16[2,96,128]{2,1,0:T(8,128)(2,1)S(1)} collective-permute-done((bf16[2,96,128]{2,1,0:T(8,128)(2,1)S(1)}, bf16[2,96,128]{2,1,0:T(8,128)(2,1)S(1)}, u32[]{:S(2)}, u32[]{:S(2)}) %collective-permute-start.1) | collective-permute-done | bytes 49184 | tf_op jit(solution)/shard_map/ppermute | solution.py:431
  14.0 0.0 collective-permute-done.2.refs_1_
  14.0 0.1 collective-permute-done.3.refs_2_
  14.1 0.0 copy-start.2
  14.2 1.6 %collective-permute-start.8 = (bf16[1152,128]{1,0:T(8,128)(2,1)S(1)}, bf16[1152,128]{1,0:T(8,128)(2,1)S(1)}, u32[]{:S(2)}, u32[]{:S(2)}) collective-permute-start(bf16[1152,128]{1,0:T(8,128)(2,1)S(1)} %shard_map.45), channel_id=1, source_target_pairs={{0,16},{16,0},{1,17},{17,1},{2,18},{18,2},{3,19},{19,3},{4,20},{20... | collective-permute-start | bytes 884744 | tf_op jit(solution)/shard_map/ppermute | solution.py:431
  15.8 2.6 %collective-permute-start.5 = (bf16[256,128]{1,0:T(8,128)(2,1)S(1)}, bf16[256,128]{1,0:T(8,128)(2,1)S(1)}, u32[]{:S(2)}, u32[]{:S(2)}) collective-permute-start(bf16[256,128]{1,0:T(8,128)(2,1)S(1)} %get-tuple-element.37.refs_1_.refs_3_), channel_id=1, source_target_pairs={{0,4},{4,0},{1,5},{5,1},{2,6},{6,2},{3,7},{7,3},{8,12},{12,8},{9,1... | collective-permute-start | bytes 196616 | tf_op jit(solution)/shard_map/ppermute | solution.py:431
  18.3 0.3 collective-permute-start.4
  18.7 0.1 pad_add_fusion.1.at_ref
  18.8 0.0 copy-done
  18.8 0.6 %shard_map.47 = (bf16[64,1280]{1,0:T(8,128)(2,1)S(1)}, bf16[128,1280]{1,0:T(8,128)(2,1)S(1)}) custom-call(s32[2]{0:T(128)S(1)} %pad_add_fusion.1.at_ref, bf16[128,5120]{1,0:T(8,128)(2,1)S(1)} %copy-done), custom_call_target="tpu_custom_call" | custom-call | tf_op jit(solution)/shard_map/pallas_call | solution.py:123
  19.4 2.1 %collective-permute-start.14 = (bf16[128,1280]{1,0:T(8,128)(2,1)S(1)}, bf16[128,1280]{1,0:T(8,128)(2,1)S(1)}, u32[]{:S(2)}, u32[]{:S(2)}) collective-permute-start(bf16[128,1280]{1,0:T(8,128)(2,1)S(1)} %shard_map.48), channel_id=1, source_target_pairs={{0,2},{2,0},{1,3},{3,1},{4,6},{6,4},{5,7},{7,5},{8,10},{10,8},{9,1... | collective-permute-start | bytes 983048 | tf_op jit(solution)/shard_map/ppermute | solution.py:431
  21.5 2.4 %collective-permute-start.15 = (bf16[64,1280]{1,0:T(8,128)(2,1)S(1)}, bf16[64,1280]{1,0:T(8,128)(2,1)S(1)}, u32[]{:S(2)}, u32[]{:S(2)}) collective-permute-start(bf16[64,1280]{1,0:T(8,128)(2,1)S(1)} %shard_map.49), channel_id=1, source_target_pairs={{0,6},{2,4},{4,2},{6,0},{1,7},{3,5},{5,3},{7,1},{8,14},{10,12},{12... | collective-permute-start | bytes 491528 | tf_op jit(solution)/shard_map/ppermute | solution.py:431
  23.9 0.0 collective-permute-done.5.refs_5_
  23.9 0.5 collective-permute-start.10
  24.4 0.5 collective-permute-done.4.refs_4_
  24.9 1.0 %collective-permute-start.9 = (bf16[256,128]{1,0:T(8,128)(2,1)S(1)}, bf16[256,128]{1,0:T(8,128)(2,1)S(1)}, u32[]{:S(2)}, u32[]{:S(2)}) collective-permute-start(bf16[256,128]{1,0:T(8,128)(2,1)S(1)} %collective-permute-done.4.refs_4_), channel_id=1, source_target_pairs={{0,16},{16,0},{1,17},{17,1},{2,18},{18,2},{3,19},{19,3},{4,20},{20... | collective-permute-start | bytes 196616 | tf_op jit(solution)/shard_map/ppermute | solution.py:431
  25.9 0.1 pad_add_fusion.base_ref
  26.0 0.0 copy-done.2
  26.0 0.7 %shard_map.40 = (f32[256,256]{1,0:T(8,128)S(1)}, f32[256,256]{1,0:T(8,128)S(1)}) custom-call(s32[2]{0:T(128)S(1)} %pad_add_fusion.base_ref, s32[8]{0:T(128)S(1)} %copy-done.2), custom_call_target="tpu_custom_call" | custom-call | tf_op jit(solution)/shard_map/pallas_call | solution.py:270
  26.7 1.4 %collective-permute-done.10.refs_8_ = bf16[256,128]{1,0:T(8,128)(2,1)S(1)} collective-permute-done((bf16[256,128]{1,0:T(8,128)(2,1)S(1)}, bf16[256,128]{1,0:T(8,128)(2,1)S(1)}, u32[]{:S(2)}, u32[]{:S(2)}) %collective-permute-start.10) | collective-permute-done | bytes 65568 | tf_op jit(solution)/shard_map/ppermute | solution.py:431
  28.1 1.0 %collective-permute-done.9.refs_7_ = bf16[256,128]{1,0:T(8,128)(2,1)S(1)} collective-permute-done((bf16[256,128]{1,0:T(8,128)(2,1)S(1)}, bf16[256,128]{1,0:T(8,128)(2,1)S(1)}, u32[]{:S(2)}, u32[]{:S(2)}) %collective-permute-start.9) | collective-permute-done | bytes 65568 | tf_op jit(solution)/shard_map/ppermute | solution.py:431
  29.2 0.0 collective-permute-done.8.refs_6_.refs_8_.refs_9_
  29.2 0.6 %shard_map.46.refs_1_.refs_0_ = bf16[256,128]{1,0:T(8,128)(2,1)S(1)} custom-call(bf16[256,128]{1,0:T(8,128)(2,1)S(1)} %get-tuple-element.33.q_ref, f32[256,256]{1,0:T(8,128)S(1)} %get-tuple-element.34.refs_0_, f32[256,256]{1,0:T(8,128)S(1)} %get-tuple-element.35.refs_1_, bf16[256,128]{1,0:T(8,128)(2,1)S(1)} %get-tuple-element.36.refs_0_.refs_2_.refs_1_, ...), custom_call_target="tpu_custom_call" | custom-call | tf_op jit(solution)/shard_map/pallas_call | solution.py:330
  29.8 5.3 %collective-permute-done.15.refs_0_ = bf16[64,1280]{1,0:T(8,128)(2,1)S(1)} collective-permute-done((bf16[64,1280]{1,0:T(8,128)(2,1)S(1)}, bf16[64,1280]{1,0:T(8,128)(2,1)S(1)}, u32[]{:S(2)}, u32[]{:S(2)}) %collective-permute-start.15) | collective-permute-done | bytes 163872 | tf_op jit(solution)/shard_map/ppermute | solution.py:431
  35.1 0.5 collective-permute-start.16
  35.6 0.0 collective-permute-start.13
  35.6 1.5 %collective-permute-start.12 = (bf16[256,128]{1,0:T(8,128)(2,1)S(1)}, bf16[256,128]{1,0:T(8,128)(2,1)S(1)}, u32[]{:S(2)}, u32[]{:S(2)}) collective-permute-start(bf16[256,128]{1,0:T(8,128)(2,1)S(1)} %shard_map.46.refs_1_.refs_0_), channel_id=1, source_target_pairs={{0,8},{2,10},{8,0},{10,2},{1,9},{3,11},{9,1},{11,3},{4,12},{6,14},... | collective-permute-start | bytes 196616 | tf_op jit(solution)/shard_map/ppermute | solution.py:431
  37.1 2.0 %collective-permute-start.11 = (bf16[256,128]{1,0:T(8,128)(2,1)S(1)}, bf16[256,128]{1,0:T(8,128)(2,1)S(1)}, u32[]{:S(2)}, u32[]{:S(2)}) collective-permute-start(bf16[256,128]{1,0:T(8,128)(2,1)S(1)} %shard_map.46.refs_1_.refs_0_), channel_id=1, source_target_pairs={{0,2},{2,0},{8,10},{10,8},{1,3},{3,1},{9,11},{11,9},{4,6},{6,4},{1... | collective-permute-start | bytes 196616 | tf_op jit(solution)/shard_map/ppermute | solution.py:431
  39.0 0.1 stack.60.at_ref
  39.1 0.0 collective-permute-done.14.refs_5_
  39.1 1.6 %collective-permute-done.13.refs_3_ = bf16[256,128]{1,0:T(8,128)(2,1)S(1)} collective-permute-done((bf16[256,128]{1,0:T(8,128)(2,1)S(1)}, bf16[256,128]{1,0:T(8,128)(2,1)S(1)}, u32[]{:S(2)}, u32[]{:S(2)}) %collective-permute-start.13) | collective-permute-done | bytes 65568 | tf_op jit(solution)/shard_map/ppermute | solution.py:431
  40.7 0.0 collective-permute-done.12.refs_2_
  40.7 0.7 %collective-permute-done.11.refs_1_ = bf16[256,128]{1,0:T(8,128)(2,1)S(1)} collective-permute-done((bf16[256,128]{1,0:T(8,128)(2,1)S(1)}, bf16[256,128]{1,0:T(8,128)(2,1)S(1)}, u32[]{:S(2)}, u32[]{:S(2)}) %collective-permute-start.11) | collective-permute-done | bytes 65568 | tf_op jit(solution)/shard_map/ppermute | solution.py:431
  41.5 0.0 collective-permute-done.16.refs_11_
  41.5 1.0 %shard_map.51 = (bf16[4,32,1280]{2,1,0:T(8,128)(2,1)S(1)}, bf16[256,512]{1,0:T(8,128)(2,1)S(1)}, bf16[512,1280]{1,0:T(8,128)(2,1)S(1)}) custom-call(s32[8]{0:T(128)S(1)} %stack.60.at_ref, s32[1]{0:T(128)} %bitcast.place_ref, bf16[256,128]{1,0:T(8,128)(2,1)S(1)} %shard_map.46.refs_1_.refs_0_, bf16[256,128]{1,0:T(8,128)(2,1)S(1)} %collective-permute-done.11.refs_1_, ...), custom_call_target="tpu_custom_call" | custom-call | tf_op jit(solution)/shard_map/pallas_call | solution.py:371
  42.5 0.1 collective-permute-start.17
  42.6 0.3 shard_map.52.x_ref
  42.9 1.3 %collective-permute-done.17.y_ref = bf16[4,32,1280]{2,1,0:T(8,128)(2,1)S(1)} collective-permute-done((bf16[4,32,1280]{2,1,0:T(8,128)(2,1)S(1)}, bf16[4,32,1280]{2,1,0:T(8,128)(2,1)S(1)}, u32[]{:S(2)}, u32[]{:S(2)}) %collective-permute-start.17) | collective-permute-done | bytes 327712 | tf_op jit(solution)/shard_map/ppermute | solution.py:431
  44.2 0.1 shard_map.53
  44.3 2.9 %collective-permute-start.18 = (bf16[32,1280]{1,0:T(8,128)(2,1)S(1)}, bf16[32,1280]{1,0:T(8,128)(2,1)S(1)}, u32[]{:S(2)}, u32[]{:S(2)}) collective-permute-start(bf16[32,1280]{1,0:T(8,128)(2,1)S(1)} %get-tuple-element.45), channel_id=1, source_target_pairs={{0,10},{2,8},{8,2},{10,0},{1,11},{3,9},{9,3},{11,1},{4,14},{6,12},... | collective-permute-start | bytes 245768 | tf_op jit(solution)/shard_map/ppermute | solution.py:431
  47.1 0.5 %collective-permute-start.19 = (bf16[32,1280]{1,0:T(8,128)(2,1)S(1)}, bf16[32,1280]{1,0:T(8,128)(2,1)S(1)}, u32[]{:S(2)}, u32[]{:S(2)}) collective-permute-start(bf16[32,1280]{1,0:T(8,128)(2,1)S(1)} %get-tuple-element.46), channel_id=1, source_target_pairs={{0,8},{2,10},{8,0},{10,2},{1,9},{3,11},{9,1},{11,3},{4,12},{6,14},... | collective-permute-start | bytes 245768 | tf_op jit(solution)/shard_map/ppermute | solution.py:431
  47.7 0.2 collective-permute-start.20
  47.8 2.1 %collective-permute-done.18.refs_0_ = bf16[32,1280]{1,0:T(8,128)(2,1)S(1)} collective-permute-done((bf16[32,1280]{1,0:T(8,128)(2,1)S(1)}, bf16[32,1280]{1,0:T(8,128)(2,1)S(1)}, u32[]{:S(2)}, u32[]{:S(2)}) %collective-permute-start.18) | collective-permute-done | bytes 81952 | tf_op jit(solution)/shard_map/ppermute | solution.py:431
  49.9 1.7 %collective-permute-done.19.refs_1_ = bf16[32,1280]{1,0:T(8,128)(2,1)S(1)} collective-permute-done((bf16[32,1280]{1,0:T(8,128)(2,1)S(1)}, bf16[32,1280]{1,0:T(8,128)(2,1)S(1)}, u32[]{:S(2)}, u32[]{:S(2)}) %collective-permute-start.19) | collective-permute-done | bytes 81952 | tf_op jit(solution)/shard_map/ppermute | solution.py:431
  51.6 0.5 collective-permute-done.20.refs_2_
  52.1 0.8 %shard_map.54 = bf16[32,5120]{1,0:T(8,128)(2,1)} custom-call(s32[1]{0:T(128)} %bitcast.place_ref, bf16[32,1280]{1,0:T(8,128)(2,1)S(1)} %collective-permute-done.18.refs_0_, bf16[32,1280]{1,0:T(8,128)(2,1)S(1)} %collective-permute-done.19.refs_1_, bf16[32,1280]{1,0:T(8,128)(2,1)S(1)} %collective-permute-done.20.refs_2_, ...), custom_call_target="tpu_custom_call" | custom-call | tf_op jit(solution)/shard_map/pallas_call | solution.py:420
  (9 shorter events, 0.1 us)
Async XLA Ops:
  0.0 5.1 %copy-start.1 = (bf16[3,32,1024]{2,1,0:T(8,128)(2,1)S(1)}, bf16[3,32,1024]{2,1,0:T(8,128)(2,1)}, u32[]{:S(2)}) copy-start(bf16[3,32,1024]{2,1,0:T(8,128)(2,1)} %x_ref.3) | copy-start | bytes 589828
  1.0 10.9 %collective-permute-start.6 = (bf16[480,128]{1,0:T(8,128)(2,1)S(1)}, bf16[480,128]{1,0:T(8,128)(2,1)S(1)}, u32[]{:S(2)}, u32[]{:S(2)}) collective-permute-start(bf16[480,128]{1,0:T(8,128)(2,1)S(1)} %get-tuple-element.38), channel_id=1, source_target_pairs={{0,4},{4,0},{1,5},{5,1},{2,6},{6,2},{3,7},{7,3},{8,12},{12,8},{9,1... | collective-permute-start | bytes 368648 | tf_op jit(solution)/shard_map/ppermute | solution.py:431
  5.2 1.4 %collective-permute-start = (bf16[4,96,128]{2,1,0:T(8,128)(2,1)S(1)}, bf16[4,96,128]{2,1,0:T(8,128)(2,1)S(1)}, u32[]{:S(2)}, u32[]{:S(2)}) collective-permute-start(bf16[4,96,128]{2,1,0:T(8,128)(2,1)S(1)} %get-tuple-element.28), channel_id=1, source_target_pairs={{0,1},{1,0},{2,3},{3,2},{4,5},{5,4},{6,7},{7,6},{8,9},{9,8},{10,11... | collective-permute-start | bytes 294920 | tf_op jit(solution)/shard_map/ppermute | solution.py:431
  6.5 6.3 %collective-permute-start.7 = (bf16[160,128]{1,0:T(8,128)(2,1)S(1)}, bf16[160,128]{1,0:T(8,128)(2,1)S(1)}, u32[]{:S(2)}, u32[]{:S(2)}) collective-permute-start(bf16[160,128]{1,0:T(8,128)(2,1)S(1)} %shard_map.43), channel_id=1, source_target_pairs={{0,4},{4,0},{1,5},{5,1},{2,6},{6,2},{3,7},{7,3},{8,12},{12,8},{9,1... | collective-permute-start | bytes 122888 | tf_op jit(solution)/shard_map/ppermute | solution.py:431
  6.6 7.4 %collective-permute-start.1 = (bf16[2,96,128]{2,1,0:T(8,128)(2,1)S(1)}, bf16[2,96,128]{2,1,0:T(8,128)(2,1)S(1)}, u32[]{:S(2)}, u32[]{:S(2)}) collective-permute-start(bf16[2,96,128]{2,1,0:T(8,128)(2,1)S(1)} %get-tuple-element.29), channel_id=1, source_target_pairs={{0,10},{2,8},{8,2},{10,0},{1,11},{3,9},{9,3},{11,1},{4,14},{6,12},... | collective-permute-start | bytes 147464 | tf_op jit(solution)/shard_map/ppermute | solution.py:431
  9.5 4.6 %collective-permute-start.2 = (bf16[2,96,128]{2,1,0:T(8,128)(2,1)S(1)}, bf16[2,96,128]{2,1,0:T(8,128)(2,1)S(1)}, u32[]{:S(2)}, u32[]{:S(2)}) collective-permute-start(bf16[2,96,128]{2,1,0:T(8,128)(2,1)S(1)} %get-tuple-element.30), channel_id=1, source_target_pairs={{0,8},{2,10},{8,0},{10,2},{1,9},{3,11},{9,1},{11,3},{4,12},{6,14},... | collective-permute-start | bytes 147464 | tf_op jit(solution)/shard_map/ppermute | solution.py:431
  10.0 4.1 %collective-permute-start.3 = (bf16[2,96,128]{2,1,0:T(8,128)(2,1)S(1)}, bf16[2,96,128]{2,1,0:T(8,128)(2,1)S(1)}, u32[]{:S(2)}, u32[]{:S(2)}) collective-permute-start(bf16[2,96,128]{2,1,0:T(8,128)(2,1)S(1)} %get-tuple-element.31), channel_id=1, source_target_pairs={{0,2},{2,0},{8,10},{10,8},{1,3},{3,1},{9,11},{11,9},{4,6},{6,4},{1... | collective-permute-start | bytes 147464 | tf_op jit(solution)/shard_map/ppermute | solution.py:431
  11.9 6.8 %copy-start = (bf16[128,5120]{1,0:T(8,128)(2,1)S(1)}, bf16[128,5120]{1,0:T(8,128)(2,1)}, u32[]{:S(2)}) copy-start(bf16[128,5120]{1,0:T(8,128)(2,1)} %refs_4_.1) | copy-start | bytes 3932164
  14.1 11.8 %copy-start.2 = (s32[8]{0:T(128)S(1)}, s32[8]{0:T(128)}, u32[]{:S(2)}) copy-start(s32[8]{0:T(128)} %clip_ref.1) | copy-start | bytes 100
  14.2 15.0 %collective-permute-start.8 = (bf16[1152,128]{1,0:T(8,128)(2,1)S(1)}, bf16[1152,128]{1,0:T(8,128)(2,1)S(1)}, u32[]{:S(2)}, u32[]{:S(2)}) collective-permute-start(bf16[1152,128]{1,0:T(8,128)(2,1)S(1)} %shard_map.45), channel_id=1, source_target_pairs={{0,16},{16,0},{1,17},{17,1},{2,18},{18,2},{3,19},{19,3},{4,20},{20... | collective-permute-start | bytes 884744 | tf_op jit(solution)/shard_map/ppermute | solution.py:431
  15.8 8.1 %collective-permute-start.5 = (bf16[256,128]{1,0:T(8,128)(2,1)S(1)}, bf16[256,128]{1,0:T(8,128)(2,1)S(1)}, u32[]{:S(2)}, u32[]{:S(2)}) collective-permute-start(bf16[256,128]{1,0:T(8,128)(2,1)S(1)} %get-tuple-element.37.refs_1_.refs_3_), channel_id=1, source_target_pairs={{0,4},{4,0},{1,5},{5,1},{2,6},{6,2},{3,7},{7,3},{8,12},{12,8},{9,1... | collective-permute-start | bytes 196616 | tf_op jit(solution)/shard_map/ppermute | solution.py:431
  18.3 6.6 %collective-permute-start.4 = (bf16[256,128]{1,0:T(8,128)(2,1)S(1)}, bf16[256,128]{1,0:T(8,128)(2,1)S(1)}, u32[]{:S(2)}, u32[]{:S(2)}) collective-permute-start(bf16[256,128]{1,0:T(8,128)(2,1)S(1)} %get-tuple-element.36.refs_0_.refs_2_.refs_1_), channel_id=1, source_target_pairs={{0,4},{4,0},{1,5},{5,1},{2,6},{6,2},{3,7},{7,3},{8,12},{12,8},{9,1... | collective-permute-start | bytes 196616 | tf_op jit(solution)/shard_map/ppermute | solution.py:431
  19.4 19.8 %collective-permute-start.14 = (bf16[128,1280]{1,0:T(8,128)(2,1)S(1)}, bf16[128,1280]{1,0:T(8,128)(2,1)S(1)}, u32[]{:S(2)}, u32[]{:S(2)}) collective-permute-start(bf16[128,1280]{1,0:T(8,128)(2,1)S(1)} %shard_map.48), channel_id=1, source_target_pairs={{0,2},{2,0},{1,3},{3,1},{4,6},{6,4},{5,7},{7,5},{8,10},{10,8},{9,1... | collective-permute-start | bytes 983048 | tf_op jit(solution)/shard_map/ppermute | solution.py:431
  21.5 13.6 %collective-permute-start.15 = (bf16[64,1280]{1,0:T(8,128)(2,1)S(1)}, bf16[64,1280]{1,0:T(8,128)(2,1)S(1)}, u32[]{:S(2)}, u32[]{:S(2)}) collective-permute-start(bf16[64,1280]{1,0:T(8,128)(2,1)S(1)} %shard_map.49), channel_id=1, source_target_pairs={{0,6},{2,4},{4,2},{6,0},{1,7},{3,5},{5,3},{7,1},{8,14},{10,12},{12... | collective-permute-start | bytes 491528 | tf_op jit(solution)/shard_map/ppermute | solution.py:431
  23.9 4.3 %collective-permute-start.10 = (bf16[256,128]{1,0:T(8,128)(2,1)S(1)}, bf16[256,128]{1,0:T(8,128)(2,1)S(1)}, u32[]{:S(2)}, u32[]{:S(2)}) collective-permute-start(bf16[256,128]{1,0:T(8,128)(2,1)S(1)} %collective-permute-done.5.refs_5_), channel_id=1, source_target_pairs={{0,16},{16,0},{1,17},{17,1},{2,18},{18,2},{3,19},{19,3},{4,20},{20... | collective-permute-start | bytes 196616 | tf_op jit(solution)/shard_map/ppermute | solution.py:431
  24.9 4.3 %collective-permute-start.9 = (bf16[256,128]{1,0:T(8,128)(2,1)S(1)}, bf16[256,128]{1,0:T(8,128)(2,1)S(1)}, u32[]{:S(2)}, u32[]{:S(2)}) collective-permute-start(bf16[256,128]{1,0:T(8,128)(2,1)S(1)} %collective-permute-done.4.refs_4_), channel_id=1, source_target_pairs={{0,16},{16,0},{1,17},{17,1},{2,18},{18,2},{3,19},{19,3},{4,20},{20... | collective-permute-start | bytes 196616 | tf_op jit(solution)/shard_map/ppermute | solution.py:431
  35.1 6.4 %collective-permute-start.16 = (bf16[64,1280]{1,0:T(8,128)(2,1)S(1)}, bf16[64,1280]{1,0:T(8,128)(2,1)S(1)}, u32[]{:S(2)}, u32[]{:S(2)}) collective-permute-start(bf16[64,1280]{1,0:T(8,128)(2,1)S(1)} %shard_map.50.refs_10_), channel_id=1, source_target_pairs={{0,16},{16,0},{1,17},{17,1},{2,18},{18,2},{3,19},{19,3},{4,20},{20... | collective-permute-start | bytes 491528 | tf_op jit(solution)/shard_map/ppermute | solution.py:431
  35.6 5.2 %collective-permute-start.13 = (bf16[256,128]{1,0:T(8,128)(2,1)S(1)}, bf16[256,128]{1,0:T(8,128)(2,1)S(1)}, u32[]{:S(2)}, u32[]{:S(2)}) collective-permute-start(bf16[256,128]{1,0:T(8,128)(2,1)S(1)} %shard_map.46.refs_1_.refs_0_), channel_id=1, source_target_pairs={{0,10},{2,8},{8,2},{10,0},{1,11},{3,9},{9,3},{11,1},{4,14},{6,12},... | collective-permute-start | bytes 196616 | tf_op jit(solution)/shard_map/ppermute | solution.py:431
  35.6 5.2 %collective-permute-start.12 = (bf16[256,128]{1,0:T(8,128)(2,1)S(1)}, bf16[256,128]{1,0:T(8,128)(2,1)S(1)}, u32[]{:S(2)}, u32[]{:S(2)}) collective-permute-start(bf16[256,128]{1,0:T(8,128)(2,1)S(1)} %shard_map.46.refs_1_.refs_0_), channel_id=1, source_target_pairs={{0,8},{2,10},{8,0},{10,2},{1,9},{3,11},{9,1},{11,3},{4,12},{6,14},... | collective-permute-start | bytes 196616 | tf_op jit(solution)/shard_map/ppermute | solution.py:431
  37.1 4.4 %collective-permute-start.11 = (bf16[256,128]{1,0:T(8,128)(2,1)S(1)}, bf16[256,128]{1,0:T(8,128)(2,1)S(1)}, u32[]{:S(2)}, u32[]{:S(2)}) collective-permute-start(bf16[256,128]{1,0:T(8,128)(2,1)S(1)} %shard_map.46.refs_1_.refs_0_), channel_id=1, source_target_pairs={{0,2},{2,0},{8,10},{10,8},{1,3},{3,1},{9,11},{11,9},{4,6},{6,4},{1... | collective-permute-start | bytes 196616 | tf_op jit(solution)/shard_map/ppermute | solution.py:431
  42.5 1.7 %collective-permute-start.17 = (bf16[4,32,1280]{2,1,0:T(8,128)(2,1)S(1)}, bf16[4,32,1280]{2,1,0:T(8,128)(2,1)S(1)}, u32[]{:S(2)}, u32[]{:S(2)}) collective-permute-start(bf16[4,32,1280]{2,1,0:T(8,128)(2,1)S(1)} %get-tuple-element.44), channel_id=1, source_target_pairs={{0,1},{1,0},{2,3},{3,2},{4,5},{5,4},{6,7},{7,6},{8,9},{9,8},{10,11... | collective-permute-start | bytes 983048 | tf_op jit(solution)/shard_map/ppermute | solution.py:431
  44.3 5.7 %collective-permute-start.18 = (bf16[32,1280]{1,0:T(8,128)(2,1)S(1)}, bf16[32,1280]{1,0:T(8,128)(2,1)S(1)}, u32[]{:S(2)}, u32[]{:S(2)}) collective-permute-start(bf16[32,1280]{1,0:T(8,128)(2,1)S(1)} %get-tuple-element.45), channel_id=1, source_target_pairs={{0,10},{2,8},{8,2},{10,0},{1,11},{3,9},{9,3},{11,1},{4,14},{6,12},... | collective-permute-start | bytes 245768 | tf_op jit(solution)/shard_map/ppermute | solution.py:431
  47.1 4.5 %collective-permute-start.19 = (bf16[32,1280]{1,0:T(8,128)(2,1)S(1)}, bf16[32,1280]{1,0:T(8,128)(2,1)S(1)}, u32[]{:S(2)}, u32[]{:S(2)}) collective-permute-start(bf16[32,1280]{1,0:T(8,128)(2,1)S(1)} %get-tuple-element.46), channel_id=1, source_target_pairs={{0,8},{2,10},{8,0},{10,2},{1,9},{3,11},{9,1},{11,3},{4,12},{6,14},... | collective-permute-start | bytes 245768 | tf_op jit(solution)/shard_map/ppermute | solution.py:431
  47.7 4.4 %collective-permute-start.20 = (bf16[32,1280]{1,0:T(8,128)(2,1)S(1)}, bf16[32,1280]{1,0:T(8,128)(2,1)S(1)}, u32[]{:S(2)}, u32[]{:S(2)}) collective-permute-start(bf16[32,1280]{1,0:T(8,128)(2,1)S(1)} %get-tuple-element.47), channel_id=1, source_target_pairs={{0,2},{2,0},{8,10},{10,8},{1,3},{3,1},{9,11},{11,9},{4,6},{6,4},{1... | collective-permute-start | bytes 245768 | tf_op jit(solution)/shard_map/ppermute | solution.py:431

commit v23 on v21

--- a/solution.py
+++ b/solution.py
@@ -160,13 +160,17 @@
 
 
 def sort_kernel(place_ref, *refs):
-    *in_refs, q_ref, k_ref, v_ref = refs
-    tok = q_ref.shape[0] // (2 * len(in_refs))
+    *in_refs, q_ref, kv_ref = refs
+    peers = 2 * len(in_refs)
+    tok = q_ref.shape[0] // peers
     for i, ref in enumerate(in_refs[::-1]):
         for core in range(2):
-            at = rows_at((place_ref[0] // 2 ^ i) * 2 + core, tok)
-            for j, out_ref in enumerate((q_ref, k_ref, v_ref)):
-                out_ref[at, :] = ref[core, j * tok:(j + 1) * tok, :]
+            at = (place_ref[0] // 2 ^ i) * 2 + core
+            q_ref[rows_at(at, tok), :] = ref[core, 0:tok, :]
+            for j in range(2):
+                kv_ref[rows_at(at + j * peers, tok), :] = ref[
+                    core, (j + 1) * tok:(j + 2) * tok, :
+                ]
 
 
 def sort(parts, place):
@@ -174,9 +178,11 @@
     count = both * len(parts) * (depth // 3)
     return pl.pallas_call(
         sort_kernel,
-        out_shape=[jax.ShapeDtypeStruct((count, width), parts[0].dtype)] * 3,
+        out_shape=[
+            jax.ShapeDtypeStruct((size, width), parts[0].dtype) for size in (count, 2 * count)
+        ],
         in_specs=[SMEM] + [VMEM] * len(parts),
-        out_specs=[VMEM] * 3,
+        out_specs=[VMEM] * 2,
         compiler_params=PARAMS,
     )(place, *parts[::-1])
 
@@ -440,12 +446,12 @@
     w_corner, w_near = pieces(w_out, y, theirs, cols)
     kept, given = lanes(qkv, core, head_dim)
     shared = swap_all(deal(kept, xor(given, ("core",), 1), place), quarter)
-    q, k, v = sort(shared, place)
-    k_far, v_far = xor(k, ("zh",), 1), xor(v, ("zh",), 1)
-    near = xor(join(k, v, far), ("y",), 1)
-    corner = xor(after(w_corner, k), ("zh", "zl"), 3)
-    w_next = xor(after(w_near, k), ("zl",), 1)
-    kvs = [(k, v), (k_far, v_far), near, (xor(k_far, ("y",), 1), xor(v_far, ("y",), 1))]
+    q, kv = sort(shared, place)
+    kv_far = xor(kv, ("zh",), 1)
+    near = xor(join(kv, far), ("y",), 1)
+    corner = xor(after(w_corner, kv), ("zh", "zl"), 3)
+    w_next = xor(after(w_near, kv), ("zl",), 1)
+    kvs = [kv, kv_far, near, xor(kv_far, ("y",), 1)]
 
     bases = [y * 2 * FRB, (1 - y) * 2 * FRB]
     mask_of = masks(bases, 4 * tok, tok, 8 * tok, frame_clip)

time: 51.1 us -> 51 us (level)
  starting transfers between devices: 23.4 us -> 21.9 us
  local copies, waits for them, and re-layouts: 0.1 us -> 1.53 us
    unnamed x6 -> x10, local copies, waits for them, and re-layouts: 0.02 us -> 1.45 us
    ppermute x20 -> x18, starting transfers between devices: 23.4 us -> 21.9 us  [xor(): return lax.ppermute(x, axis, [(i, i ^ by) for i in range(size)])]
    ppermute x20 -> x18, waiting for transfers between devices: 22 us -> 21.9 us  [xor(): return lax.ppermute(x, axis, [(i, i ^ by) for i in range(size)])]
  transfers between devices with their start and end apart: 20 -> 18, of which waited for: 15 -> 13; matrix products, arithmetic and copies ran while one was open for 0% -> 0% of each run, Pallas kernels for 5% -> 5%
where the time goes in v23:
time: 51 us; the launch traced here: 50.9 us
  starting transfers between devices  21.9 us (43%)
  waiting for transfers between devices  21.9 us (43%)
  Pallas kernels  5.21 us (10%)
  local copies, waits for them, and re-layouts  1.53 us (3%)
    ppermute x18, starting transfers between devices, xor(): return lax.ppermute(x, axis, [(i, i ^ by) for i in range(size)])  21.9 us
    ppermute x18, waiting for transfers between devices, xor(): return lax.ppermute(x, axis, [(i, i ^ by) for i in range(size)])  21.9 us
    unnamed x10, local copies, waits for them, and re-layouts  1.45 us
    pallas_call x1, Pallas kernels, project(): pl.pallas_call(functools.partial(project_kernel, blks, sizes), out_shape=...  1.04 us
  transfers between devices with their start and end apart: 18, of which 13 were waited for; matrix products, arithmetic and copies ran while one was open for 0% of the time, Pallas kernels for 5%

profile of v23, /device:TPU:0, one launch (start us, length us, event | category | flops | bytes accessed | tf_op | source)
XLA Modules:
  0.0 50.9 jit_solution(3292696718340482367)
XLA Ops:
  0.0 0.0 copy-start.1
  0.0 1.0 %shard_map.41 = bf16[640,128]{1,0:T(8,128)(2,1)S(1)} custom-call(bf16[128,5120]{1,0:T(8,128)(2,1)} %refs_4_.1), custom_call_target="tpu_custom_call" | custom-call | tf_op jit(solution)/shard_map/pallas_call | solution.py:96
  1.0 4.1 %collective-permute-start.5 = (bf16[640,128]{1,0:T(8,128)(2,1)S(1)}, bf16[640,128]{1,0:T(8,128)(2,1)S(1)}, u32[]{:S(2)}, u32[]{:S(2)}) collective-permute-start(bf16[640,128]{1,0:T(8,128)(2,1)S(1)} %shard_map.41), channel_id=1, source_target_pairs={{0,4},{4,0},{1,5},{5,1},{2,6},{6,2},{3,7},{7,3},{8,12},{12,8},{9,1... | collective-permute-start | bytes 491528 | tf_op jit(solution)/shard_map/ppermute | solution.py:429
  5.1 0.0 copy-done.1
  5.1 0.1 shard_map.37
  5.2 0.1 collective-permute-start
  5.3 1.3 %collective-permute-done.got_ref = bf16[4,96,128]{2,1,0:T(8,128)(2,1)S(1)} collective-permute-done((bf16[4,96,128]{2,1,0:T(8,128)(2,1)S(1)}, bf16[4,96,128]{2,1,0:T(8,128)(2,1)S(1)}, u32[]{:S(2)}, u32[]{:S(2)}) %collective-permute-start) | collective-permute-done | bytes 98336 | tf_op jit(solution)/shard_map/ppermute | solution.py:429
  6.5 2.6 %collective-permute-start.1 = (bf16[2,96,128]{2,1,0:T(8,128)(2,1)S(1)}, bf16[2,96,128]{2,1,0:T(8,128)(2,1)S(1)}, u32[]{:S(2)}, u32[]{:S(2)}) collective-permute-start(bf16[2,96,128]{2,1,0:T(8,128)(2,1)S(1)} %get-tuple-element.26), channel_id=1, source_target_pairs={{0,10},{2,8},{8,2},{10,0},{1,11},{3,9},{9,3},{11,1},{4,14},{6,12},... | collective-permute-start | bytes 147464 | tf_op jit(solution)/shard_map/ppermute | solution.py:429
  9.1 0.5 %collective-permute-start.2 = (bf16[2,96,128]{2,1,0:T(8,128)(2,1)S(1)}, bf16[2,96,128]{2,1,0:T(8,128)(2,1)S(1)}, u32[]{:S(2)}, u32[]{:S(2)}) collective-permute-start(bf16[2,96,128]{2,1,0:T(8,128)(2,1)S(1)} %get-tuple-element.27), channel_id=1, source_target_pairs={{0,8},{2,10},{8,0},{10,2},{1,9},{3,11},{9,1},{11,3},{4,12},{6,14},... | collective-permute-start | bytes 147464 | tf_op jit(solution)/shard_map/ppermute | solution.py:429
  9.7 0.4 collective-permute-start.3
  10.1 1.7 %collective-permute-done.1.refs_0_ = bf16[2,96,128]{2,1,0:T(8,128)(2,1)S(1)} collective-permute-done((bf16[2,96,128]{2,1,0:T(8,128)(2,1)S(1)}, bf16[2,96,128]{2,1,0:T(8,128)(2,1)S(1)}, u32[]{:S(2)}, u32[]{:S(2)}) %collective-permute-start.1) | collective-permute-done | bytes 49184 | tf_op jit(solution)/shard_map/ppermute | solution.py:429
  11.8 1.4 %collective-permute-done.2.refs_1_ = bf16[2,96,128]{2,1,0:T(8,128)(2,1)S(1)} collective-permute-done((bf16[2,96,128]{2,1,0:T(8,128)(2,1)S(1)}, bf16[2,96,128]{2,1,0:T(8,128)(2,1)S(1)}, u32[]{:S(2)}, u32[]{:S(2)}) %collective-permute-start.2) | collective-permute-done | bytes 49184 | tf_op jit(solution)/shard_map/ppermute | solution.py:429
  13.2 1.5 %collective-permute-done.3.refs_2_ = bf16[2,96,128]{2,1,0:T(8,128)(2,1)S(1)} collective-permute-done((bf16[2,96,128]{2,1,0:T(8,128)(2,1)S(1)}, bf16[2,96,128]{2,1,0:T(8,128)(2,1)S(1)}, u32[]{:S(2)}, u32[]{:S(2)}) %collective-permute-start.3) | collective-permute-done | bytes 49184 | tf_op jit(solution)/shard_map/ppermute | solution.py:429
  14.7 0.0 copy-start.2
  14.7 0.0 collective-permute-done.5.refs_0_
  14.8 0.0 copy-start
  14.8 0.6 %copy-done.2 = bf16[256,128]{1,0:T(8,128)(2,1)} copy-done((bf16[256,128]{1,0:T(8,128)(2,1)}, bf16[256,128]{1,0:T(8,128)(2,1)S(1)}, u32[]{:S(2)}) %copy-start.2) | copy-done | bytes 65560
  15.4 0.0 copy-start.4
  15.4 1.6 %collective-permute-start.6 = (bf16[1152,128]{1,0:T(8,128)(2,1)S(1)}, bf16[1152,128]{1,0:T(8,128)(2,1)S(1)}, u32[]{:S(2)}, u32[]{:S(2)}) collective-permute-start(bf16[1152,128]{1,0:T(8,128)(2,1)S(1)} %shard_map.43), channel_id=1, source_target_pairs={{0,16},{16,0},{1,17},{17,1},{2,18},{18,2},{3,19},{19,3},{4,20},{20... | collective-permute-start | bytes 884744 | tf_op jit(solution)/shard_map/ppermute | solution.py:429
  17.0 0.5 collective-permute-start.4
  17.5 0.1 pad_add_fusion.1.at_ref
  17.6 0.0 copy-done
  17.6 0.6 %shard_map.45 = (bf16[64,1280]{1,0:T(8,128)(2,1)S(1)}, bf16[128,1280]{1,0:T(8,128)(2,1)S(1)}) custom-call(s32[2]{0:T(128)S(1)} %pad_add_fusion.1.at_ref, bf16[128,5120]{1,0:T(8,128)(2,1)S(1)} %copy-done), custom_call_target="tpu_custom_call" | custom-call | tf_op jit(solution)/shard_map/pallas_call | solution.py:114
  18.2 2.5 %collective-permute-start.11 = (bf16[128,1280]{1,0:T(8,128)(2,1)S(1)}, bf16[128,1280]{1,0:T(8,128)(2,1)S(1)}, u32[]{:S(2)}, u32[]{:S(2)}) collective-permute-start(bf16[128,1280]{1,0:T(8,128)(2,1)S(1)} %shard_map.46), channel_id=1, source_target_pairs={{0,2},{2,0},{1,3},{3,1},{4,6},{6,4},{5,7},{7,5},{8,10},{10,8},{9,1... | collective-permute-start | bytes 983048 | tf_op jit(solution)/shard_map/ppermute | solution.py:429
  20.7 1.4 %collective-permute-start.12 = (bf16[64,1280]{1,0:T(8,128)(2,1)S(1)}, bf16[64,1280]{1,0:T(8,128)(2,1)S(1)}, u32[]{:S(2)}, u32[]{:S(2)}) collective-permute-start(bf16[64,1280]{1,0:T(8,128)(2,1)S(1)} %shard_map.47), channel_id=1, source_target_pairs={{0,6},{2,4},{4,2},{6,0},{1,7},{3,5},{5,3},{7,1},{8,14},{10,12},{12... | collective-permute-start | bytes 491528 | tf_op jit(solution)/shard_map/ppermute | solution.py:429
  22.2 3.2 %collective-permute-done.4.refs_3_ = bf16[512,128]{1,0:T(8,128)(2,1)S(1)} collective-permute-done((bf16[512,128]{1,0:T(8,128)(2,1)S(1)}, bf16[512,128]{1,0:T(8,128)(2,1)S(1)}, u32[]{:S(2)}, u32[]{:S(2)}) %collective-permute-start.4) | collective-permute-done | bytes 131104 | tf_op jit(solution)/shard_map/ppermute | solution.py:429
  25.4 0.5 %collective-permute-start.7 = (bf16[512,128]{1,0:T(8,128)(2,1)S(1)}, bf16[512,128]{1,0:T(8,128)(2,1)S(1)}, u32[]{:S(2)}, u32[]{:S(2)}) collective-permute-start(bf16[512,128]{1,0:T(8,128)(2,1)S(1)} %collective-permute-done.4.refs_3_), channel_id=1, source_target_pairs={{0,16},{16,0},{1,17},{17,1},{2,18},{18,2},{3,19},{19,3},{4,20},{20... | collective-permute-start | bytes 393224 | tf_op jit(solution)/shard_map/ppermute | solution.py:429
  25.9 0.1 pad_add_fusion.base_ref
  26.0 0.0 copy-done.4
  26.0 0.7 %shard_map.40 = (f32[256,256]{1,0:T(8,128)S(1)}, f32[256,256]{1,0:T(8,128)S(1)}) custom-call(s32[2]{0:T(128)S(1)} %pad_add_fusion.base_ref, s32[8]{0:T(128)S(1)} %copy-done.4), custom_call_target="tpu_custom_call" | custom-call | tf_op jit(solution)/shard_map/pallas_call | solution.py:267
  26.7 3.7 %collective-permute-done.7.refs_5_ = bf16[512,128]{1,0:T(8,128)(2,1)S(1)} collective-permute-done((bf16[512,128]{1,0:T(8,128)(2,1)S(1)}, bf16[512,128]{1,0:T(8,128)(2,1)S(1)}, u32[]{:S(2)}, u32[]{:S(2)}) %collective-permute-start.7) | collective-permute-done | bytes 131104 | tf_op jit(solution)/shard_map/ppermute | solution.py:429
  30.4 0.0 collective-permute-done.6.refs_4_.refs_7_
  30.4 0.0 copy-start.3
  30.4 0.8 %copy-done.3 = bf16[256,128]{1,0:T(8,128)(2,1)S(1)} copy-done((bf16[256,128]{1,0:T(8,128)(2,1)S(1)}, bf16[256,128]{1,0:T(8,128)(2,1)}, u32[]{:S(2)}) %copy-start.3) | copy-done | bytes 65560
  31.2 0.6 %shard_map.44.refs_1_.refs_0_ = bf16[256,128]{1,0:T(8,128)(2,1)S(1)} custom-call(bf16[256,128]{1,0:T(8,128)(2,1)S(1)} %copy-done.3, f32[256,256]{1,0:T(8,128)S(1)} %get-tuple-element.31.refs_0_, f32[256,256]{1,0:T(8,128)S(1)} %get-tuple-element.32.refs_1_, bf16[512,128]{1,0:T(8,128)(2,1)S(1)} %get-tuple-element.33.refs_0_.refs_2_.refs_1_, ...), custom_call_target="tpu_custom_call" | custom-call | tf_op jit(solution)/shard_map/pallas_call | solution.py:327
  31.8 1.2 %collective-permute-done.12.refs_0_ = bf16[64,1280]{1,0:T(8,128)(2,1)S(1)} collective-permute-done((bf16[64,1280]{1,0:T(8,128)(2,1)S(1)}, bf16[64,1280]{1,0:T(8,128)(2,1)S(1)}, u32[]{:S(2)}, u32[]{:S(2)}) %collective-permute-start.12) | collective-permute-done | bytes 163872 | tf_op jit(solution)/shard_map/ppermute | solution.py:429
  33.1 0.5 collective-permute-start.13
  33.6 0.0 collective-permute-start.10
  33.6 1.2 %collective-permute-start.9 = (bf16[256,128]{1,0:T(8,128)(2,1)S(1)}, bf16[256,128]{1,0:T(8,128)(2,1)S(1)}, u32[]{:S(2)}, u32[]{:S(2)}) collective-permute-start(bf16[256,128]{1,0:T(8,128)(2,1)S(1)} %shard_map.44.refs_1_.refs_0_), channel_id=1, source_target_pairs={{0,8},{2,10},{8,0},{10,2},{1,9},{3,11},{9,1},{11,3},{4,12},{6,14},... | collective-permute-start | bytes 196616 | tf_op jit(solution)/shard_map/ppermute | solution.py:429
  34.7 2.3 %collective-permute-start.8 = (bf16[256,128]{1,0:T(8,128)(2,1)S(1)}, bf16[256,128]{1,0:T(8,128)(2,1)S(1)}, u32[]{:S(2)}, u32[]{:S(2)}) collective-permute-start(bf16[256,128]{1,0:T(8,128)(2,1)S(1)} %shard_map.44.refs_1_.refs_0_), channel_id=1, source_target_pairs={{0,2},{2,0},{8,10},{10,8},{1,3},{3,1},{9,11},{11,9},{4,6},{6,4},{1... | collective-permute-start | bytes 196616 | tf_op jit(solution)/shard_map/ppermute | solution.py:429
  37.0 0.1 stack.52.at_ref
  37.1 0.0 collective-permute-done.11.refs_5_
  37.1 1.6 %collective-permute-done.10.refs_3_ = bf16[256,128]{1,0:T(8,128)(2,1)S(1)} collective-permute-done((bf16[256,128]{1,0:T(8,128)(2,1)S(1)}, bf16[256,128]{1,0:T(8,128)(2,1)S(1)}, u32[]{:S(2)}, u32[]{:S(2)}) %collective-permute-start.10) | collective-permute-done | bytes 65568 | tf_op jit(solution)/shard_map/ppermute | solution.py:429
  38.7 0.0 collective-permute-done.9.refs_2_
  38.7 0.6 %collective-permute-done.8.refs_1_ = bf16[256,128]{1,0:T(8,128)(2,1)S(1)} collective-permute-done((bf16[256,128]{1,0:T(8,128)(2,1)S(1)}, bf16[256,128]{1,0:T(8,128)(2,1)S(1)}, u32[]{:S(2)}, u32[]{:S(2)}) %collective-permute-start.8) | collective-permute-done | bytes 65568 | tf_op jit(solution)/shard_map/ppermute | solution.py:429
  39.3 0.0 collective-permute-done.13.refs_9_
  39.3 1.0 %shard_map.49 = (bf16[4,32,1280]{2,1,0:T(8,128)(2,1)S(1)}, bf16[256,512]{1,0:T(8,128)(2,1)S(1)}, bf16[512,1280]{1,0:T(8,128)(2,1)S(1)}) custom-call(s32[6]{0:T(128)S(1)} %stack.52.at_ref, s32[1]{0:T(128)} %bitcast.place_ref, bf16[256,128]{1,0:T(8,128)(2,1)S(1)} %shard_map.44.refs_1_.refs_0_, bf16[256,128]{1,0:T(8,128)(2,1)S(1)} %collective-permute-done.8.refs_1_, ...), custom_call_target="tpu_custom_call" | custom-call | tf_op jit(solution)/shard_map/pallas_call | solution.py:369
  40.3 0.1 collective-permute-start.14
  40.4 0.3 shard_map.50.x_ref
  40.8 1.3 %collective-permute-done.14.y_ref = bf16[4,32,1280]{2,1,0:T(8,128)(2,1)S(1)} collective-permute-done((bf16[4,32,1280]{2,1,0:T(8,128)(2,1)S(1)}, bf16[4,32,1280]{2,1,0:T(8,128)(2,1)S(1)}, u32[]{:S(2)}, u32[]{:S(2)}) %collective-permute-start.14) | collective-permute-done | bytes 327712 | tf_op jit(solution)/shard_map/ppermute | solution.py:429
  42.0 0.1 shard_map.51
  42.1 2.7 %collective-permute-start.15 = (bf16[32,1280]{1,0:T(8,128)(2,1)S(1)}, bf16[32,1280]{1,0:T(8,128)(2,1)S(1)}, u32[]{:S(2)}, u32[]{:S(2)}) collective-permute-start(bf16[32,1280]{1,0:T(8,128)(2,1)S(1)} %get-tuple-element.39), channel_id=1, source_target_pairs={{0,10},{2,8},{8,2},{10,0},{1,11},{3,9},{9,3},{11,1},{4,14},{6,12},... | collective-permute-start | bytes 245768 | tf_op jit(solution)/shard_map/ppermute | solution.py:429
  44.8 0.8 %collective-permute-start.16 = (bf16[32,1280]{1,0:T(8,128)(2,1)S(1)}, bf16[32,1280]{1,0:T(8,128)(2,1)S(1)}, u32[]{:S(2)}, u32[]{:S(2)}) collective-permute-start(bf16[32,1280]{1,0:T(8,128)(2,1)S(1)} %get-tuple-element.40), channel_id=1, source_target_pairs={{0,8},{2,10},{8,0},{10,2},{1,9},{3,11},{9,1},{11,3},{4,12},{6,14},... | collective-permute-start | bytes 245768 | tf_op jit(solution)/shard_map/ppermute | solution.py:429
  45.7 0.0 collective-permute-start.17
  45.7 2.0 %collective-permute-done.15.refs_0_ = bf16[32,1280]{1,0:T(8,128)(2,1)S(1)} collective-permute-done((bf16[32,1280]{1,0:T(8,128)(2,1)S(1)}, bf16[32,1280]{1,0:T(8,128)(2,1)S(1)}, u32[]{:S(2)}, u32[]{:S(2)}) %collective-permute-start.15) | collective-permute-done | bytes 81952 | tf_op jit(solution)/shard_map/ppermute | solution.py:429
  47.6 1.7 %collective-permute-done.16.refs_1_ = bf16[32,1280]{1,0:T(8,128)(2,1)S(1)} collective-permute-done((bf16[32,1280]{1,0:T(8,128)(2,1)S(1)}, bf16[32,1280]{1,0:T(8,128)(2,1)S(1)}, u32[]{:S(2)}, u32[]{:S(2)}) %collective-permute-start.16) | collective-permute-done | bytes 81952 | tf_op jit(solution)/shard_map/ppermute | solution.py:429
  49.3 0.8 %collective-permute-done.17.refs_2_ = bf16[32,1280]{1,0:T(8,128)(2,1)S(1)} collective-permute-done((bf16[32,1280]{1,0:T(8,128)(2,1)S(1)}, bf16[32,1280]{1,0:T(8,128)(2,1)S(1)}, u32[]{:S(2)}, u32[]{:S(2)}) %collective-permute-start.17) | collective-permute-done | bytes 81952 | tf_op jit(solution)/shard_map/ppermute | solution.py:429
  50.1 0.8 %shard_map.52 = bf16[32,5120]{1,0:T(8,128)(2,1)} custom-call(s32[1]{0:T(128)} %bitcast.place_ref, bf16[32,1280]{1,0:T(8,128)(2,1)S(1)} %collective-permute-done.15.refs_0_, bf16[32,1280]{1,0:T(8,128)(2,1)S(1)} %collective-permute-done.16.refs_1_, bf16[32,1280]{1,0:T(8,128)(2,1)S(1)} %collective-permute-done.17.refs_2_, ...), custom_call_target="tpu_custom_call" | custom-call | tf_op jit(solution)/shard_map/pallas_call | solution.py:418
  (7 shorter events, 0.1 us)
Async XLA Ops:
  0.0 5.1 %copy-start.1 = (bf16[3,32,1024]{2,1,0:T(8,128)(2,1)S(1)}, bf16[3,32,1024]{2,1,0:T(8,128)(2,1)}, u32[]{:S(2)}) copy-start(bf16[3,32,1024]{2,1,0:T(8,128)(2,1)} %x_ref.3) | copy-start | bytes 589828
  1.0 13.7 %collective-permute-start.5 = (bf16[640,128]{1,0:T(8,128)(2,1)S(1)}, bf16[640,128]{1,0:T(8,128)(2,1)S(1)}, u32[]{:S(2)}, u32[]{:S(2)}) collective-permute-start(bf16[640,128]{1,0:T(8,128)(2,1)S(1)} %shard_map.41), channel_id=1, source_target_pairs={{0,4},{4,0},{1,5},{5,1},{2,6},{6,2},{3,7},{7,3},{8,12},{12,8},{9,1... | collective-permute-start | bytes 491528 | tf_op jit(solution)/shard_map/ppermute | solution.py:429
  5.2 1.4 %collective-permute-start = (bf16[4,96,128]{2,1,0:T(8,128)(2,1)S(1)}, bf16[4,96,128]{2,1,0:T(8,128)(2,1)S(1)}, u32[]{:S(2)}, u32[]{:S(2)}) collective-permute-start(bf16[4,96,128]{2,1,0:T(8,128)(2,1)S(1)} %get-tuple-element.25), channel_id=1, source_target_pairs={{0,1},{1,0},{2,3},{3,2},{4,5},{5,4},{6,7},{7,6},{8,9},{9,8},{10,11... | collective-permute-start | bytes 294920 | tf_op jit(solution)/shard_map/ppermute | solution.py:429
  6.5 5.3 %collective-permute-start.1 = (bf16[2,96,128]{2,1,0:T(8,128)(2,1)S(1)}, bf16[2,96,128]{2,1,0:T(8,128)(2,1)S(1)}, u32[]{:S(2)}, u32[]{:S(2)}) collective-permute-start(bf16[2,96,128]{2,1,0:T(8,128)(2,1)S(1)} %get-tuple-element.26), channel_id=1, source_target_pairs={{0,10},{2,8},{8,2},{10,0},{1,11},{3,9},{9,3},{11,1},{4,14},{6,12},... | collective-permute-start | bytes 147464 | tf_op jit(solution)/shard_map/ppermute | solution.py:429
  9.1 4.1 %collective-permute-start.2 = (bf16[2,96,128]{2,1,0:T(8,128)(2,1)S(1)}, bf16[2,96,128]{2,1,0:T(8,128)(2,1)S(1)}, u32[]{:S(2)}, u32[]{:S(2)}) collective-permute-start(bf16[2,96,128]{2,1,0:T(8,128)(2,1)S(1)} %get-tuple-element.27), channel_id=1, source_target_pairs={{0,8},{2,10},{8,0},{10,2},{1,9},{3,11},{9,1},{11,3},{4,12},{6,14},... | collective-permute-start | bytes 147464 | tf_op jit(solution)/shard_map/ppermute | solution.py:429
  9.7 5.1 %collective-permute-start.3 = (bf16[2,96,128]{2,1,0:T(8,128)(2,1)S(1)}, bf16[2,96,128]{2,1,0:T(8,128)(2,1)S(1)}, u32[]{:S(2)}, u32[]{:S(2)}) collective-permute-start(bf16[2,96,128]{2,1,0:T(8,128)(2,1)S(1)} %get-tuple-element.28), channel_id=1, source_target_pairs={{0,2},{2,0},{8,10},{10,8},{1,3},{3,1},{9,11},{11,9},{4,6},{6,4},{1... | collective-permute-start | bytes 147464 | tf_op jit(solution)/shard_map/ppermute | solution.py:429
  14.7 0.6 %copy-start.2 = (bf16[256,128]{1,0:T(8,128)(2,1)}, bf16[256,128]{1,0:T(8,128)(2,1)S(1)}, u32[]{:S(2)}) copy-start(bf16[256,128]{1,0:T(8,128)(2,1)S(1)} %get-tuple-element.30.q_ref) | copy-start | bytes 196612
  14.8 2.8 %copy-start = (bf16[128,5120]{1,0:T(8,128)(2,1)S(1)}, bf16[128,5120]{1,0:T(8,128)(2,1)}, u32[]{:S(2)}) copy-start(bf16[128,5120]{1,0:T(8,128)(2,1)} %refs_4_.1) | copy-start | bytes 3932164
  15.4 10.6 %copy-start.4 = (s32[8]{0:T(128)S(1)}, s32[8]{0:T(128)}, u32[]{:S(2)}) copy-start(s32[8]{0:T(128)} %clip_ref.1) | copy-start | bytes 100
  15.4 15.0 %collective-permute-start.6 = (bf16[1152,128]{1,0:T(8,128)(2,1)S(1)}, bf16[1152,128]{1,0:T(8,128)(2,1)S(1)}, u32[]{:S(2)}, u32[]{:S(2)}) collective-permute-start(bf16[1152,128]{1,0:T(8,128)(2,1)S(1)} %shard_map.43), channel_id=1, source_target_pairs={{0,16},{16,0},{1,17},{17,1},{2,18},{18,2},{3,19},{19,3},{4,20},{20... | collective-permute-start | bytes 884744 | tf_op jit(solution)/shard_map/ppermute | solution.py:429
  17.0 8.3 %collective-permute-start.4 = (bf16[512,128]{1,0:T(8,128)(2,1)S(1)}, bf16[512,128]{1,0:T(8,128)(2,1)S(1)}, u32[]{:S(2)}, u32[]{:S(2)}) collective-permute-start(bf16[512,128]{1,0:T(8,128)(2,1)S(1)} %get-tuple-element.33.refs_0_.refs_2_.refs_1_), channel_id=1, source_target_pairs={{0,4},{4,0},{1,5},{5,1},{2,6},{6,2},{3,7},{7,3},{8,12},{12,8},{9,1... | collective-permute-start | bytes 393224 | tf_op jit(solution)/shard_map/ppermute | solution.py:429
  18.2 18.9 %collective-permute-start.11 = (bf16[128,1280]{1,0:T(8,128)(2,1)S(1)}, bf16[128,1280]{1,0:T(8,128)(2,1)S(1)}, u32[]{:S(2)}, u32[]{:S(2)}) collective-permute-start(bf16[128,1280]{1,0:T(8,128)(2,1)S(1)} %shard_map.46), channel_id=1, source_target_pairs={{0,2},{2,0},{1,3},{3,1},{4,6},{6,4},{5,7},{7,5},{8,10},{10,8},{9,1... | collective-permute-start | bytes 983048 | tf_op jit(solution)/shard_map/ppermute | solution.py:429
  20.7 12.3 %collective-permute-start.12 = (bf16[64,1280]{1,0:T(8,128)(2,1)S(1)}, bf16[64,1280]{1,0:T(8,128)(2,1)S(1)}, u32[]{:S(2)}, u32[]{:S(2)}) collective-permute-start(bf16[64,1280]{1,0:T(8,128)(2,1)S(1)} %shard_map.47), channel_id=1, source_target_pairs={{0,6},{2,4},{4,2},{6,0},{1,7},{3,5},{5,3},{7,1},{8,14},{10,12},{12... | collective-permute-start | bytes 491528 | tf_op jit(solution)/shard_map/ppermute | solution.py:429
  25.4 5.0 %collective-permute-start.7 = (bf16[512,128]{1,0:T(8,128)(2,1)S(1)}, bf16[512,128]{1,0:T(8,128)(2,1)S(1)}, u32[]{:S(2)}, u32[]{:S(2)}) collective-permute-start(bf16[512,128]{1,0:T(8,128)(2,1)S(1)} %collective-permute-done.4.refs_3_), channel_id=1, source_target_pairs={{0,16},{16,0},{1,17},{17,1},{2,18},{18,2},{3,19},{19,3},{4,20},{20... | collective-permute-start | bytes 393224 | tf_op jit(solution)/shard_map/ppermute | solution.py:429
  30.4 0.8 %copy-start.3 = (bf16[256,128]{1,0:T(8,128)(2,1)S(1)}, bf16[256,128]{1,0:T(8,128)(2,1)}, u32[]{:S(2)}) copy-start(bf16[256,128]{1,0:T(8,128)(2,1)} %copy-done.2) | copy-start | bytes 196612
  33.1 6.2 %collective-permute-start.13 = (bf16[64,1280]{1,0:T(8,128)(2,1)S(1)}, bf16[64,1280]{1,0:T(8,128)(2,1)S(1)}, u32[]{:S(2)}, u32[]{:S(2)}) collective-permute-start(bf16[64,1280]{1,0:T(8,128)(2,1)S(1)} %shard_map.48.refs_8_), channel_id=1, source_target_pairs={{0,16},{16,0},{1,17},{17,1},{2,18},{18,2},{3,19},{19,3},{4,20},{20... | collective-permute-start | bytes 491528 | tf_op jit(solution)/shard_map/ppermute | solution.py:429
  33.6 5.2 %collective-permute-start.10 = (bf16[256,128]{1,0:T(8,128)(2,1)S(1)}, bf16[256,128]{1,0:T(8,128)(2,1)S(1)}, u32[]{:S(2)}, u32[]{:S(2)}) collective-permute-start(bf16[256,128]{1,0:T(8,128)(2,1)S(1)} %shard_map.44.refs_1_.refs_0_), channel_id=1, source_target_pairs={{0,10},{2,8},{8,2},{10,0},{1,11},{3,9},{9,3},{11,1},{4,14},{6,12},... | collective-permute-start | bytes 196616 | tf_op jit(solution)/shard_map/ppermute | solution.py:429
  33.6 5.2 %collective-permute-start.9 = (bf16[256,128]{1,0:T(8,128)(2,1)S(1)}, bf16[256,128]{1,0:T(8,128)(2,1)S(1)}, u32[]{:S(2)}, u32[]{:S(2)}) collective-permute-start(bf16[256,128]{1,0:T(8,128)(2,1)S(1)} %shard_map.44.refs_1_.refs_0_), channel_id=1, source_target_pairs={{0,8},{2,10},{8,0},{10,2},{1,9},{3,11},{9,1},{11,3},{4,12},{6,14},... | collective-permute-start | bytes 196616 | tf_op jit(solution)/shard_map/ppermute | solution.py:429
  34.7 4.5 %collective-permute-start.8 = (bf16[256,128]{1,0:T(8,128)(2,1)S(1)}, bf16[256,128]{1,0:T(8,128)(2,1)S(1)}, u32[]{:S(2)}, u32[]{:S(2)}) collective-permute-start(bf16[256,128]{1,0:T(8,128)(2,1)S(1)} %shard_map.44.refs_1_.refs_0_), channel_id=1, source_target_pairs={{0,2},{2,0},{8,10},{10,8},{1,3},{3,1},{9,11},{11,9},{4,6},{6,4},{1... | collective-permute-start | bytes 196616 | tf_op jit(solution)/shard_map/ppermute | solution.py:429
  40.3 1.7 %collective-permute-start.14 = (bf16[4,32,1280]{2,1,0:T(8,128)(2,1)S(1)}, bf16[4,32,1280]{2,1,0:T(8,128)(2,1)S(1)}, u32[]{:S(2)}, u32[]{:S(2)}) collective-permute-start(bf16[4,32,1280]{2,1,0:T(8,128)(2,1)S(1)} %get-tuple-element.38), channel_id=1, source_target_pairs={{0,1},{1,0},{2,3},{3,2},{4,5},{5,4},{6,7},{7,6},{8,9},{9,8},{10,11... | collective-permute-start | bytes 983048 | tf_op jit(solution)/shard_map/ppermute | solution.py:429
  42.1 5.5 %collective-permute-start.15 = (bf16[32,1280]{1,0:T(8,128)(2,1)S(1)}, bf16[32,1280]{1,0:T(8,128)(2,1)S(1)}, u32[]{:S(2)}, u32[]{:S(2)}) collective-permute-start(bf16[32,1280]{1,0:T(8,128)(2,1)S(1)} %get-tuple-element.39), channel_id=1, source_target_pairs={{0,10},{2,8},{8,2},{10,0},{1,11},{3,9},{9,3},{11,1},{4,14},{6,12},... | collective-permute-start | bytes 245768 | tf_op jit(solution)/shard_map/ppermute | solution.py:429
  44.8 4.5 %collective-permute-start.16 = (bf16[32,1280]{1,0:T(8,128)(2,1)S(1)}, bf16[32,1280]{1,0:T(8,128)(2,1)S(1)}, u32[]{:S(2)}, u32[]{:S(2)}) collective-permute-start(bf16[32,1280]{1,0:T(8,128)(2,1)S(1)} %get-tuple-element.40), channel_id=1, source_target_pairs={{0,8},{2,10},{8,0},{10,2},{1,9},{3,11},{9,1},{11,3},{4,12},{6,14},... | collective-permute-start | bytes 245768 | tf_op jit(solution)/shard_map/ppermute | solution.py:429
  45.7 4.4 %collective-permute-start.17 = (bf16[32,1280]{1,0:T(8,128)(2,1)S(1)}, bf16[32,1280]{1,0:T(8,128)(2,1)S(1)}, u32[]{:S(2)}, u32[]{:S(2)}) collective-permute-start(bf16[32,1280]{1,0:T(8,128)(2,1)S(1)} %get-tuple-element.41), channel_id=1, source_target_pairs={{0,2},{2,0},{8,10},{10,8},{1,3},{3,1},{9,11},{11,9},{4,6},{6,4},{1... | collective-permute-start | bytes 245768 | tf_op jit(solution)/shard_map/ppermute | solution.py:429

commit v24 on v23

--- a/solution.py
+++ b/solution.py
@@ -103,21 +103,23 @@
     )(pltpu.with_memory_space_constraint(x, pltpu.HBM))
 
 
-def pieces_kernel(at_ref, x_ref, corner_ref, near_ref):
+def pieces_kernel(at_ref, x_ref, corner_ref, near_ref, own_ref):
     half, cols = corner_ref.shape
     corner_ref[...] = x_ref[rows_at(at_ref[0], half), rows_at(at_ref[1], cols)]
     near_ref[...] = x_ref[:, rows_at(at_ref[1], cols)]
-
-
-def pieces(x, half, at, cols):
+    own_ref[...] = x_ref[:, rows_at(at_ref[2], cols)]
+
+
+def pieces(x, half, at, own_at, cols):
     depth = x.shape[0]
+    sizes = (depth // 2, depth, depth)
     return pl.pallas_call(
         pieces_kernel,
-        out_shape=[jax.ShapeDtypeStruct((rows, cols), x.dtype) for rows in (depth // 2, depth)],
+        out_shape=[jax.ShapeDtypeStruct((rows, cols), x.dtype) for rows in sizes],
         in_specs=[SMEM, VMEM],
-        out_specs=[VMEM, VMEM],
-        compiler_params=PARAMS,
-    )(index_array(half, at), x)
+        out_specs=[VMEM] * 3,
+        compiler_params=PARAMS,
+    )(index_array(half, at, own_at), x)
 
 
 def lane_kernel(head_dim, core_ref, x_ref, mine_ref, theirs_ref):
@@ -260,13 +262,13 @@
     row_clip = clip_of(row, base_ref[0], span, tok, clip_ref)
     for i, out_ref in enumerate(out_refs):
         allowed = row_clip == clip_of(col, base_ref[i], span, tok, clip_ref)
-        out_ref[...] = jnp.where(allowed, 0.0, -1e30)
+        out_ref[...] = jnp.where(allowed, 0.0, -1e30).astype(out_ref.dtype)
 
 
 def masks(bases, span, tok, count, frame_clip):
     return pl.pallas_call(
         functools.partial(mask_kernel, span, tok),
-        out_shape=[jax.ShapeDtypeStruct((count, count), jnp.float32)] * len(bases),
+        out_shape=[jax.ShapeDtypeStruct((count, count), jnp.bfloat16)] * len(bases),
         in_specs=[SMEM, SMEM],
         out_specs=[VMEM] * len(bases),
         compiler_params=PARAMS,
@@ -301,7 +303,7 @@
                     queries, k_refs[i][:, cols], (((1,), (1,)), ((), ())),
                     preferred_element_type=jnp.float32,
                 )
-                scores.append(s * scale + mask_refs[which[i]][...])
+                scores.append(s * scale + mask_refs[which[i]][...].astype(jnp.float32))
             new_top = functools.reduce(
                 jnp.maximum, [jnp.max(s, axis=1, keepdims=True) for s in scores]
             )
@@ -438,12 +440,12 @@
     y, x, zh, zl, core = (lax.axis_index(n) for n in ("y", "x", "zh", "zl", "core"))
     tok, head_dim, cols = qkv.shape[1], w_out.shape[0], w_out.shape[1] // 4
     place = index_array((x * 2 + zl) * 2 + core)
-    theirs = x * 2 + 1 - zl
+    mine, theirs = x * 2 + zl, x * 2 + 1 - zl
     row, half = zh * 2 + zl, head_dim // 2
 
     w_far = blocks(w_out, half, cols, "y", quarter)
     far = after(xor(w_far, ("zh",), 1), cost=AHEAD)
-    w_corner, w_near = pieces(w_out, y, theirs, cols)
+    w_corner, w_near, w_own = pieces(w_out, y, theirs, mine, cols)
     kept, given = lanes(qkv, core, head_dim)
     shared = swap_all(deal(kept, xor(given, ("core",), 1), place), quarter)
     q, kv = sort(shared, place)
@@ -459,7 +461,7 @@
     corner = after(corner, attn)
     corner_rest = xor(corner, ("y",), 1)
     attns = swap_all([attn] * 4, quarter)
-    w_parts = [w_out, w_next, far, near, corner, corner_rest]
+    w_parts = [w_own, w_next, far, near, corner, corner_rest]
     sizes = [head_dim, head_dim, half, half, half, half]
     at = [row, row ^ 1] + [2 * (row ^ by) + h for by in (2, 3) for h in (y, 1 - y)]
     parts = project(attns, w_parts, sizes, at, place, tok, cols)

time: 51 us -> 50.4 us (0.988)
  local copies, waits for them, and re-layouts: 1.53 us -> 0.1 us
  waiting for transfers between devices: 21.9 us -> 22.7 us
    unnamed x10 -> x6, local copies, waits for them, and re-layouts: 1.45 us -> 0.02 us
    ppermute x18, waiting for transfers between devices: 21.9 us -> 22.7 us  [xor(): return lax.ppermute(x, axis, [(i, i ^ by) for i in range(size)])]
where the time goes in v24:
time: 50.4 us; the launch traced here: 50.2 us
  waiting for transfers between devices  22.7 us (45%)
  starting transfers between devices  21.9 us (43%)
  Pallas kernels  5.23 us (10%)
    ppermute x18, waiting for transfers between devices, xor(): return lax.ppermute(x, axis, [(i, i ^ by) for i in range(size)])  22.7 us
    ppermute x18, starting transfers between devices, xor(): return lax.ppermute(x, axis, [(i, i ^ by) for i in range(size)])  21.9 us
    pallas_call x1, Pallas kernels, project(): pl.pallas_call(functools.partial(project_kernel, blks, sizes), out_shape=...  1.03 us
  transfers between devices with their start and end apart: 18, of which 13 were waited for; matrix products, arithmetic and copies ran while one was open for 0% of the time, Pallas kernels for 5%

profile of v24, /device:TPU:0, one launch (start us, length us, event | category | flops | bytes accessed | tf_op | source)
XLA Modules:
  0.0 50.2 jit_solution(5056020019760983611)
XLA Ops:
  0.0 0.0 copy-start.1
  0.0 1.0 %shard_map.41 = bf16[640,128]{1,0:T(8,128)(2,1)S(1)} custom-call(bf16[128,5120]{1,0:T(8,128)(2,1)} %x_ref.5), custom_call_target="tpu_custom_call" | custom-call | tf_op jit(solution)/shard_map/pallas_call | solution.py:96
  1.0 4.1 %collective-permute-start.5 = (bf16[640,128]{1,0:T(8,128)(2,1)S(1)}, bf16[640,128]{1,0:T(8,128)(2,1)S(1)}, u32[]{:S(2)}, u32[]{:S(2)}) collective-permute-start(bf16[640,128]{1,0:T(8,128)(2,1)S(1)} %shard_map.41), channel_id=1, source_target_pairs={{0,4},{4,0},{1,5},{5,1},{2,6},{6,2},{3,7},{7,3},{8,12},{12,8},{9,1... | collective-permute-start | bytes 491528 | tf_op jit(solution)/shard_map/ppermute | solution.py:431
  5.1 0.0 copy-done.1
  5.1 0.1 shard_map.37
  5.2 0.1 collective-permute-start
  5.3 1.3 %collective-permute-done.got_ref = bf16[4,96,128]{2,1,0:T(8,128)(2,1)S(1)} collective-permute-done((bf16[4,96,128]{2,1,0:T(8,128)(2,1)S(1)}, bf16[4,96,128]{2,1,0:T(8,128)(2,1)S(1)}, u32[]{:S(2)}, u32[]{:S(2)}) %collective-permute-start) | collective-permute-done | bytes 98336 | tf_op jit(solution)/shard_map/ppermute | solution.py:431
  6.5 2.6 %collective-permute-start.1 = (bf16[2,96,128]{2,1,0:T(8,128)(2,1)S(1)}, bf16[2,96,128]{2,1,0:T(8,128)(2,1)S(1)}, u32[]{:S(2)}, u32[]{:S(2)}) collective-permute-start(bf16[2,96,128]{2,1,0:T(8,128)(2,1)S(1)} %get-tuple-element.27), channel_id=1, source_target_pairs={{0,10},{2,8},{8,2},{10,0},{1,11},{3,9},{9,3},{11,1},{4,14},{6,12},... | collective-permute-start | bytes 147464 | tf_op jit(solution)/shard_map/ppermute | solution.py:431
  9.1 0.5 %collective-permute-start.2 = (bf16[2,96,128]{2,1,0:T(8,128)(2,1)S(1)}, bf16[2,96,128]{2,1,0:T(8,128)(2,1)S(1)}, u32[]{:S(2)}, u32[]{:S(2)}) collective-permute-start(bf16[2,96,128]{2,1,0:T(8,128)(2,1)S(1)} %get-tuple-element.28), channel_id=1, source_target_pairs={{0,8},{2,10},{8,0},{10,2},{1,9},{3,11},{9,1},{11,3},{4,12},{6,14},... | collective-permute-start | bytes 147464 | tf_op jit(solution)/shard_map/ppermute | solution.py:431
  9.7 0.4 collective-permute-start.3
  10.1 1.7 %collective-permute-done.1.refs_0_ = bf16[2,96,128]{2,1,0:T(8,128)(2,1)S(1)} collective-permute-done((bf16[2,96,128]{2,1,0:T(8,128)(2,1)S(1)}, bf16[2,96,128]{2,1,0:T(8,128)(2,1)S(1)}, u32[]{:S(2)}, u32[]{:S(2)}) %collective-permute-start.1) | collective-permute-done | bytes 49184 | tf_op jit(solution)/shard_map/ppermute | solution.py:431
  11.8 1.4 %collective-permute-done.2.refs_1_ = bf16[2,96,128]{2,1,0:T(8,128)(2,1)S(1)} collective-permute-done((bf16[2,96,128]{2,1,0:T(8,128)(2,1)S(1)}, bf16[2,96,128]{2,1,0:T(8,128)(2,1)S(1)}, u32[]{:S(2)}, u32[]{:S(2)}) %collective-permute-start.2) | collective-permute-done | bytes 49184 | tf_op jit(solution)/shard_map/ppermute | solution.py:431
  13.2 1.5 %collective-permute-done.3.refs_2_ = bf16[2,96,128]{2,1,0:T(8,128)(2,1)S(1)} collective-permute-done((bf16[2,96,128]{2,1,0:T(8,128)(2,1)S(1)}, bf16[2,96,128]{2,1,0:T(8,128)(2,1)S(1)}, u32[]{:S(2)}, u32[]{:S(2)}) %collective-permute-start.3) | collective-permute-done | bytes 49184 | tf_op jit(solution)/shard_map/ppermute | solution.py:431
  14.7 0.0 collective-permute-done.5.refs_0_
  14.7 0.0 copy-start
  14.8 0.0 copy-start.2
  14.8 1.6 %collective-permute-start.6 = (bf16[1152,128]{1,0:T(8,128)(2,1)S(1)}, bf16[1152,128]{1,0:T(8,128)(2,1)S(1)}, u32[]{:S(2)}, u32[]{:S(2)}) collective-permute-start(bf16[1152,128]{1,0:T(8,128)(2,1)S(1)} %shard_map.43), channel_id=1, source_target_pairs={{0,16},{16,0},{1,17},{17,1},{2,18},{18,2},{3,19},{19,3},{4,20},{20... | collective-permute-start | bytes 884744 | tf_op jit(solution)/shard_map/ppermute | solution.py:431
  16.4 0.5 collective-permute-start.4
  16.9 0.1 pad_add_fusion.1.at_ref
  17.0 0.0 copy-done
  17.0 0.6 %shard_map.45 = (bf16[64,1280]{1,0:T(8,128)(2,1)S(1)}, bf16[128,1280]{1,0:T(8,128)(2,1)S(1)}, bf16[128,1280]{1,0:T(8,128)(2,1)S(1)}) custom-call(s32[3]{0:T(128)S(1)} %pad_add_fusion.1.at_ref, bf16[128,5120]{1,0:T(8,128)(2,1)S(1)} %copy-done), custom_call_target="tpu_custom_call" | custom-call | tf_op jit(solution)/shard_map/pallas_call | solution.py:116
  17.6 2.5 %collective-permute-start.11 = (bf16[128,1280]{1,0:T(8,128)(2,1)S(1)}, bf16[128,1280]{1,0:T(8,128)(2,1)S(1)}, u32[]{:S(2)}, u32[]{:S(2)}) collective-permute-start(bf16[128,1280]{1,0:T(8,128)(2,1)S(1)} %shard_map.46), channel_id=1, source_target_pairs={{0,2},{2,0},{1,3},{3,1},{4,6},{6,4},{5,7},{7,5},{8,10},{10,8},{9,1... | collective-permute-start | bytes 983048 | tf_op jit(solution)/shard_map/ppermute | solution.py:431
  20.2 1.4 %collective-permute-start.12 = (bf16[64,1280]{1,0:T(8,128)(2,1)S(1)}, bf16[64,1280]{1,0:T(8,128)(2,1)S(1)}, u32[]{:S(2)}, u32[]{:S(2)}) collective-permute-start(bf16[64,1280]{1,0:T(8,128)(2,1)S(1)} %shard_map.47), channel_id=1, source_target_pairs={{0,6},{2,4},{4,2},{6,0},{1,7},{3,5},{5,3},{7,1},{8,14},{10,12},{12... | collective-permute-start | bytes 491528 | tf_op jit(solution)/shard_map/ppermute | solution.py:431
  21.6 3.1 %collective-permute-done.4.refs_3_ = bf16[512,128]{1,0:T(8,128)(2,1)S(1)} collective-permute-done((bf16[512,128]{1,0:T(8,128)(2,1)S(1)}, bf16[512,128]{1,0:T(8,128)(2,1)S(1)}, u32[]{:S(2)}, u32[]{:S(2)}) %collective-permute-start.4) | collective-permute-done | bytes 131104 | tf_op jit(solution)/shard_map/ppermute | solution.py:431
  24.7 0.5 collective-permute-start.7
  25.2 0.1 pad_add_fusion.base_ref
  25.2 0.0 copy-done.2
  25.2 0.7 %shard_map.40 = (bf16[256,256]{1,0:T(8,128)(2,1)S(1)}, bf16[256,256]{1,0:T(8,128)(2,1)S(1)}) custom-call(s32[2]{0:T(128)S(1)} %pad_add_fusion.base_ref, s32[8]{0:T(128)S(1)} %copy-done.2), custom_call_target="tpu_custom_call" | custom-call | tf_op jit(solution)/shard_map/pallas_call | solution.py:269
  25.9 3.7 %collective-permute-done.7.refs_5_ = bf16[512,128]{1,0:T(8,128)(2,1)S(1)} collective-permute-done((bf16[512,128]{1,0:T(8,128)(2,1)S(1)}, bf16[512,128]{1,0:T(8,128)(2,1)S(1)}, u32[]{:S(2)}, u32[]{:S(2)}) %collective-permute-start.7) | collective-permute-done | bytes 131104 | tf_op jit(solution)/shard_map/ppermute | solution.py:431
  29.7 0.0 collective-permute-done.6.refs_4_.refs_7_
  29.7 0.6 %shard_map.44.refs_1_.refs_0_ = bf16[256,128]{1,0:T(8,128)(2,1)S(1)} custom-call(bf16[256,128]{1,0:T(8,128)(2,1)S(1)} %get-tuple-element.31.q_ref, bf16[256,256]{1,0:T(8,128)(2,1)S(1)} %get-tuple-element.32.refs_0_, bf16[256,256]{1,0:T(8,128)(2,1)S(1)} %get-tuple-element.33.refs_1_, bf16[512,128]{1,0:T(8,128)(2,1)S(1)} %get-tuple-element.34.refs_0_.refs_2_.refs_1_, ...), custom_call_target="tpu_custom_call" | custom-call | tf_op jit(solution)/shard_map/pallas_call | solution.py:329
  30.3 2.1 %collective-permute-done.12.refs_0_ = bf16[64,1280]{1,0:T(8,128)(2,1)S(1)} collective-permute-done((bf16[64,1280]{1,0:T(8,128)(2,1)S(1)}, bf16[64,1280]{1,0:T(8,128)(2,1)S(1)}, u32[]{:S(2)}, u32[]{:S(2)}) %collective-permute-start.12) | collective-permute-done | bytes 163872 | tf_op jit(solution)/shard_map/ppermute | solution.py:431
  32.4 0.5 %collective-permute-start.13 = (bf16[64,1280]{1,0:T(8,128)(2,1)S(1)}, bf16[64,1280]{1,0:T(8,128)(2,1)S(1)}, u32[]{:S(2)}, u32[]{:S(2)}) collective-permute-start(bf16[64,1280]{1,0:T(8,128)(2,1)S(1)} %shard_map.48.refs_8_), channel_id=1, source_target_pairs={{0,16},{16,0},{1,17},{17,1},{2,18},{18,2},{3,19},{19,3},{4,20},{20... | collective-permute-start | bytes 491528 | tf_op jit(solution)/shard_map/ppermute | solution.py:431
  32.9 0.0 collective-permute-start.10
  32.9 1.2 %collective-permute-start.9 = (bf16[256,128]{1,0:T(8,128)(2,1)S(1)}, bf16[256,128]{1,0:T(8,128)(2,1)S(1)}, u32[]{:S(2)}, u32[]{:S(2)}) collective-permute-start(bf16[256,128]{1,0:T(8,128)(2,1)S(1)} %shard_map.44.refs_1_.refs_0_), channel_id=1, source_target_pairs={{0,8},{2,10},{8,0},{10,2},{1,9},{3,11},{9,1},{11,3},{4,12},{6,14},... | collective-permute-start | bytes 196616 | tf_op jit(solution)/shard_map/ppermute | solution.py:431
  34.2 2.3 %collective-permute-start.8 = (bf16[256,128]{1,0:T(8,128)(2,1)S(1)}, bf16[256,128]{1,0:T(8,128)(2,1)S(1)}, u32[]{:S(2)}, u32[]{:S(2)}) collective-permute-start(bf16[256,128]{1,0:T(8,128)(2,1)S(1)} %shard_map.44.refs_1_.refs_0_), channel_id=1, source_target_pairs={{0,2},{2,0},{8,10},{10,8},{1,3},{3,1},{9,11},{11,9},{4,6},{6,4},{1... | collective-permute-start | bytes 196616 | tf_op jit(solution)/shard_map/ppermute | solution.py:431
  36.4 0.1 stack.55.at_ref
  36.5 0.0 collective-permute-done.11.refs_5_
  36.5 1.6 %collective-permute-done.10.refs_3_ = bf16[256,128]{1,0:T(8,128)(2,1)S(1)} collective-permute-done((bf16[256,128]{1,0:T(8,128)(2,1)S(1)}, bf16[256,128]{1,0:T(8,128)(2,1)S(1)}, u32[]{:S(2)}, u32[]{:S(2)}) %collective-permute-start.10) | collective-permute-done | bytes 65568 | tf_op jit(solution)/shard_map/ppermute | solution.py:431
  38.1 0.0 collective-permute-done.9.refs_2_
  38.1 0.6 %collective-permute-done.8.refs_1_ = bf16[256,128]{1,0:T(8,128)(2,1)S(1)} collective-permute-done((bf16[256,128]{1,0:T(8,128)(2,1)S(1)}, bf16[256,128]{1,0:T(8,128)(2,1)S(1)}, u32[]{:S(2)}, u32[]{:S(2)}) %collective-permute-start.8) | collective-permute-done | bytes 65568 | tf_op jit(solution)/shard_map/ppermute | solution.py:431
  38.7 0.0 collective-permute-done.13.refs_9_
  38.7 1.0 %shard_map.49 = (bf16[4,32,1280]{2,1,0:T(8,128)(2,1)S(1)}, bf16[256,512]{1,0:T(8,128)(2,1)S(1)}, bf16[512,1280]{1,0:T(8,128)(2,1)S(1)}) custom-call(s32[6]{0:T(128)S(1)} %stack.55.at_ref, s32[1]{0:T(128)} %bitcast.place_ref, bf16[256,128]{1,0:T(8,128)(2,1)S(1)} %shard_map.44.refs_1_.refs_0_, bf16[256,128]{1,0:T(8,128)(2,1)S(1)} %collective-permute-done.8.refs_1_, ...), custom_call_target="tpu_custom_call" | custom-call | tf_op jit(solution)/shard_map/pallas_call | solution.py:371
  39.7 0.1 collective-permute-start.14
  39.8 0.3 shard_map.50.x_ref
  40.1 1.3 %collective-permute-done.14.y_ref = bf16[4,32,1280]{2,1,0:T(8,128)(2,1)S(1)} collective-permute-done((bf16[4,32,1280]{2,1,0:T(8,128)(2,1)S(1)}, bf16[4,32,1280]{2,1,0:T(8,128)(2,1)S(1)}, u32[]{:S(2)}, u32[]{:S(2)}) %collective-permute-start.14) | collective-permute-done | bytes 327712 | tf_op jit(solution)/shard_map/ppermute | solution.py:431
  41.4 0.1 shard_map.51
  41.5 2.7 %collective-permute-start.15 = (bf16[32,1280]{1,0:T(8,128)(2,1)S(1)}, bf16[32,1280]{1,0:T(8,128)(2,1)S(1)}, u32[]{:S(2)}, u32[]{:S(2)}) collective-permute-start(bf16[32,1280]{1,0:T(8,128)(2,1)S(1)} %get-tuple-element.41), channel_id=1, source_target_pairs={{0,10},{2,8},{8,2},{10,0},{1,11},{3,9},{9,3},{11,1},{4,14},{6,12},... | collective-permute-start | bytes 245768 | tf_op jit(solution)/shard_map/ppermute | solution.py:431
  44.2 0.8 %collective-permute-start.16 = (bf16[32,1280]{1,0:T(8,128)(2,1)S(1)}, bf16[32,1280]{1,0:T(8,128)(2,1)S(1)}, u32[]{:S(2)}, u32[]{:S(2)}) collective-permute-start(bf16[32,1280]{1,0:T(8,128)(2,1)S(1)} %get-tuple-element.42), channel_id=1, source_target_pairs={{0,8},{2,10},{8,0},{10,2},{1,9},{3,11},{9,1},{11,3},{4,12},{6,14},... | collective-permute-start | bytes 245768 | tf_op jit(solution)/shard_map/ppermute | solution.py:431
  45.0 0.0 collective-permute-start.17
  45.0 2.0 %collective-permute-done.15.refs_0_ = bf16[32,1280]{1,0:T(8,128)(2,1)S(1)} collective-permute-done((bf16[32,1280]{1,0:T(8,128)(2,1)S(1)}, bf16[32,1280]{1,0:T(8,128)(2,1)S(1)}, u32[]{:S(2)}, u32[]{:S(2)}) %collective-permute-start.15) | collective-permute-done | bytes 81952 | tf_op jit(solution)/shard_map/ppermute | solution.py:431
  47.0 1.7 %collective-permute-done.16.refs_1_ = bf16[32,1280]{1,0:T(8,128)(2,1)S(1)} collective-permute-done((bf16[32,1280]{1,0:T(8,128)(2,1)S(1)}, bf16[32,1280]{1,0:T(8,128)(2,1)S(1)}, u32[]{:S(2)}, u32[]{:S(2)}) %collective-permute-start.16) | collective-permute-done | bytes 81952 | tf_op jit(solution)/shard_map/ppermute | solution.py:431
  48.7 0.7 %collective-permute-done.17.refs_2_ = bf16[32,1280]{1,0:T(8,128)(2,1)S(1)} collective-permute-done((bf16[32,1280]{1,0:T(8,128)(2,1)S(1)}, bf16[32,1280]{1,0:T(8,128)(2,1)S(1)}, u32[]{:S(2)}, u32[]{:S(2)}) %collective-permute-start.17) | collective-permute-done | bytes 81952 | tf_op jit(solution)/shard_map/ppermute | solution.py:431
  49.5 0.8 %shard_map.52 = bf16[32,5120]{1,0:T(8,128)(2,1)} custom-call(s32[1]{0:T(128)} %bitcast.place_ref, bf16[32,1280]{1,0:T(8,128)(2,1)S(1)} %collective-permute-done.15.refs_0_, bf16[32,1280]{1,0:T(8,128)(2,1)S(1)} %collective-permute-done.16.refs_1_, bf16[32,1280]{1,0:T(8,128)(2,1)S(1)} %collective-permute-done.17.refs_2_, ...), custom_call_target="tpu_custom_call" | custom-call | tf_op jit(solution)/shard_map/pallas_call | solution.py:420
  (7 shorter events, 0.1 us)
Async XLA Ops:
  0.0 5.1 %copy-start.1 = (bf16[3,32,1024]{2,1,0:T(8,128)(2,1)S(1)}, bf16[3,32,1024]{2,1,0:T(8,128)(2,1)}, u32[]{:S(2)}) copy-start(bf16[3,32,1024]{2,1,0:T(8,128)(2,1)} %x_ref.3) | copy-start | bytes 589828
  1.0 13.7 %collective-permute-start.5 = (bf16[640,128]{1,0:T(8,128)(2,1)S(1)}, bf16[640,128]{1,0:T(8,128)(2,1)S(1)}, u32[]{:S(2)}, u32[]{:S(2)}) collective-permute-start(bf16[640,128]{1,0:T(8,128)(2,1)S(1)} %shard_map.41), channel_id=1, source_target_pairs={{0,4},{4,0},{1,5},{5,1},{2,6},{6,2},{3,7},{7,3},{8,12},{12,8},{9,1... | collective-permute-start | bytes 491528 | tf_op jit(solution)/shard_map/ppermute | solution.py:431
  5.2 1.4 %collective-permute-start = (bf16[4,96,128]{2,1,0:T(8,128)(2,1)S(1)}, bf16[4,96,128]{2,1,0:T(8,128)(2,1)S(1)}, u32[]{:S(2)}, u32[]{:S(2)}) collective-permute-start(bf16[4,96,128]{2,1,0:T(8,128)(2,1)S(1)} %get-tuple-element.26), channel_id=1, source_target_pairs={{0,1},{1,0},{2,3},{3,2},{4,5},{5,4},{6,7},{7,6},{8,9},{9,8},{10,11... | collective-permute-start | bytes 294920 | tf_op jit(solution)/shard_map/ppermute | solution.py:431
  6.5 5.3 %collective-permute-start.1 = (bf16[2,96,128]{2,1,0:T(8,128)(2,1)S(1)}, bf16[2,96,128]{2,1,0:T(8,128)(2,1)S(1)}, u32[]{:S(2)}, u32[]{:S(2)}) collective-permute-start(bf16[2,96,128]{2,1,0:T(8,128)(2,1)S(1)} %get-tuple-element.27), channel_id=1, source_target_pairs={{0,10},{2,8},{8,2},{10,0},{1,11},{3,9},{9,3},{11,1},{4,14},{6,12},... | collective-permute-start | bytes 147464 | tf_op jit(solution)/shard_map/ppermute | solution.py:431
  9.1 4.1 %collective-permute-start.2 = (bf16[2,96,128]{2,1,0:T(8,128)(2,1)S(1)}, bf16[2,96,128]{2,1,0:T(8,128)(2,1)S(1)}, u32[]{:S(2)}, u32[]{:S(2)}) collective-permute-start(bf16[2,96,128]{2,1,0:T(8,128)(2,1)S(1)} %get-tuple-element.28), channel_id=1, source_target_pairs={{0,8},{2,10},{8,0},{10,2},{1,9},{3,11},{9,1},{11,3},{4,12},{6,14},... | collective-permute-start | bytes 147464 | tf_op jit(solution)/shard_map/ppermute | solution.py:431
  9.7 5.1 %collective-permute-start.3 = (bf16[2,96,128]{2,1,0:T(8,128)(2,1)S(1)}, bf16[2,96,128]{2,1,0:T(8,128)(2,1)S(1)}, u32[]{:S(2)}, u32[]{:S(2)}) collective-permute-start(bf16[2,96,128]{2,1,0:T(8,128)(2,1)S(1)} %get-tuple-element.29), channel_id=1, source_target_pairs={{0,2},{2,0},{8,10},{10,8},{1,3},{3,1},{9,11},{11,9},{4,6},{6,4},{1... | collective-permute-start | bytes 147464 | tf_op jit(solution)/shard_map/ppermute | solution.py:431
  14.7 2.2 %copy-start = (bf16[128,5120]{1,0:T(8,128)(2,1)S(1)}, bf16[128,5120]{1,0:T(8,128)(2,1)}, u32[]{:S(2)}) copy-start(bf16[128,5120]{1,0:T(8,128)(2,1)} %x_ref.5) | copy-start | bytes 3932164
  14.8 10.4 %copy-start.2 = (s32[8]{0:T(128)S(1)}, s32[8]{0:T(128)}, u32[]{:S(2)}) copy-start(s32[8]{0:T(128)} %clip_ref.1) | copy-start | bytes 100
  14.8 14.9 %collective-permute-start.6 = (bf16[1152,128]{1,0:T(8,128)(2,1)S(1)}, bf16[1152,128]{1,0:T(8,128)(2,1)S(1)}, u32[]{:S(2)}, u32[]{:S(2)}) collective-permute-start(bf16[1152,128]{1,0:T(8,128)(2,1)S(1)} %shard_map.43), channel_id=1, source_target_pairs={{0,16},{16,0},{1,17},{17,1},{2,18},{18,2},{3,19},{19,3},{4,20},{20... | collective-permute-start | bytes 884744 | tf_op jit(solution)/shard_map/ppermute | solution.py:431
  16.4 8.2 %collective-permute-start.4 = (bf16[512,128]{1,0:T(8,128)(2,1)S(1)}, bf16[512,128]{1,0:T(8,128)(2,1)S(1)}, u32[]{:S(2)}, u32[]{:S(2)}) collective-permute-start(bf16[512,128]{1,0:T(8,128)(2,1)S(1)} %get-tuple-element.34.refs_0_.refs_2_.refs_1_), channel_id=1, source_target_pairs={{0,4},{4,0},{1,5},{5,1},{2,6},{6,2},{3,7},{7,3},{8,12},{12,8},{9,1... | collective-permute-start | bytes 393224 | tf_op jit(solution)/shard_map/ppermute | solution.py:431
  17.6 18.9 %collective-permute-start.11 = (bf16[128,1280]{1,0:T(8,128)(2,1)S(1)}, bf16[128,1280]{1,0:T(8,128)(2,1)S(1)}, u32[]{:S(2)}, u32[]{:S(2)}) collective-permute-start(bf16[128,1280]{1,0:T(8,128)(2,1)S(1)} %shard_map.46), channel_id=1, source_target_pairs={{0,2},{2,0},{1,3},{3,1},{4,6},{6,4},{5,7},{7,5},{8,10},{10,8},{9,1... | collective-permute-start | bytes 983048 | tf_op jit(solution)/shard_map/ppermute | solution.py:431
  20.2 12.3 %collective-permute-start.12 = (bf16[64,1280]{1,0:T(8,128)(2,1)S(1)}, bf16[64,1280]{1,0:T(8,128)(2,1)S(1)}, u32[]{:S(2)}, u32[]{:S(2)}) collective-permute-start(bf16[64,1280]{1,0:T(8,128)(2,1)S(1)} %shard_map.47), channel_id=1, source_target_pairs={{0,6},{2,4},{4,2},{6,0},{1,7},{3,5},{5,3},{7,1},{8,14},{10,12},{12... | collective-permute-start | bytes 491528 | tf_op jit(solution)/shard_map/ppermute | solution.py:431
  24.7 5.0 %collective-permute-start.7 = (bf16[512,128]{1,0:T(8,128)(2,1)S(1)}, bf16[512,128]{1,0:T(8,128)(2,1)S(1)}, u32[]{:S(2)}, u32[]{:S(2)}) collective-permute-start(bf16[512,128]{1,0:T(8,128)(2,1)S(1)} %collective-permute-done.4.refs_3_), channel_id=1, source_target_pairs={{0,16},{16,0},{1,17},{17,1},{2,18},{18,2},{3,19},{19,3},{4,20},{20... | collective-permute-start | bytes 393224 | tf_op jit(solution)/shard_map/ppermute | solution.py:431
  32.4 6.2 %collective-permute-start.13 = (bf16[64,1280]{1,0:T(8,128)(2,1)S(1)}, bf16[64,1280]{1,0:T(8,128)(2,1)S(1)}, u32[]{:S(2)}, u32[]{:S(2)}) collective-permute-start(bf16[64,1280]{1,0:T(8,128)(2,1)S(1)} %shard_map.48.refs_8_), channel_id=1, source_target_pairs={{0,16},{16,0},{1,17},{17,1},{2,18},{18,2},{3,19},{19,3},{4,20},{20... | collective-permute-start | bytes 491528 | tf_op jit(solution)/shard_map/ppermute | solution.py:431
  32.9 5.2 %collective-permute-start.10 = (bf16[256,128]{1,0:T(8,128)(2,1)S(1)}, bf16[256,128]{1,0:T(8,128)(2,1)S(1)}, u32[]{:S(2)}, u32[]{:S(2)}) collective-permute-start(bf16[256,128]{1,0:T(8,128)(2,1)S(1)} %shard_map.44.refs_1_.refs_0_), channel_id=1, source_target_pairs={{0,10},{2,8},{8,2},{10,0},{1,11},{3,9},{9,3},{11,1},{4,14},{6,12},... | collective-permute-start | bytes 196616 | tf_op jit(solution)/shard_map/ppermute | solution.py:431
  32.9 5.2 %collective-permute-start.9 = (bf16[256,128]{1,0:T(8,128)(2,1)S(1)}, bf16[256,128]{1,0:T(8,128)(2,1)S(1)}, u32[]{:S(2)}, u32[]{:S(2)}) collective-permute-start(bf16[256,128]{1,0:T(8,128)(2,1)S(1)} %shard_map.44.refs_1_.refs_0_), channel_id=1, source_target_pairs={{0,8},{2,10},{8,0},{10,2},{1,9},{3,11},{9,1},{11,3},{4,12},{6,14},... | collective-permute-start | bytes 196616 | tf_op jit(solution)/shard_map/ppermute | solution.py:431
  34.2 4.5 %collective-permute-start.8 = (bf16[256,128]{1,0:T(8,128)(2,1)S(1)}, bf16[256,128]{1,0:T(8,128)(2,1)S(1)}, u32[]{:S(2)}, u32[]{:S(2)}) collective-permute-start(bf16[256,128]{1,0:T(8,128)(2,1)S(1)} %shard_map.44.refs_1_.refs_0_), channel_id=1, source_target_pairs={{0,2},{2,0},{8,10},{10,8},{1,3},{3,1},{9,11},{11,9},{4,6},{6,4},{1... | collective-permute-start | bytes 196616 | tf_op jit(solution)/shard_map/ppermute | solution.py:431
  39.7 1.7 %collective-permute-start.14 = (bf16[4,32,1280]{2,1,0:T(8,128)(2,1)S(1)}, bf16[4,32,1280]{2,1,0:T(8,128)(2,1)S(1)}, u32[]{:S(2)}, u32[]{:S(2)}) collective-permute-start(bf16[4,32,1280]{2,1,0:T(8,128)(2,1)S(1)} %get-tuple-element.40), channel_id=1, source_target_pairs={{0,1},{1,0},{2,3},{3,2},{4,5},{5,4},{6,7},{7,6},{8,9},{9,8},{10,11... | collective-permute-start | bytes 983048 | tf_op jit(solution)/shard_map/ppermute | solution.py:431
  41.5 5.6 %collective-permute-start.15 = (bf16[32,1280]{1,0:T(8,128)(2,1)S(1)}, bf16[32,1280]{1,0:T(8,128)(2,1)S(1)}, u32[]{:S(2)}, u32[]{:S(2)}) collective-permute-start(bf16[32,1280]{1,0:T(8,128)(2,1)S(1)} %get-tuple-element.41), channel_id=1, source_target_pairs={{0,10},{2,8},{8,2},{10,0},{1,11},{3,9},{9,3},{11,1},{4,14},{6,12},... | collective-permute-start | bytes 245768 | tf_op jit(solution)/shard_map/ppermute | solution.py:431
  44.2 4.5 %collective-permute-start.16 = (bf16[32,1280]{1,0:T(8,128)(2,1)S(1)}, bf16[32,1280]{1,0:T(8,128)(2,1)S(1)}, u32[]{:S(2)}, u32[]{:S(2)}) collective-permute-start(bf16[32,1280]{1,0:T(8,128)(2,1)S(1)} %get-tuple-element.42), channel_id=1, source_target_pairs={{0,8},{2,10},{8,0},{10,2},{1,9},{3,11},{9,1},{11,3},{4,12},{6,14},... | collective-permute-start | bytes 245768 | tf_op jit(solution)/shard_map/ppermute | solution.py:431
  45.0 4.4 %collective-permute-start.17 = (bf16[32,1280]{1,0:T(8,128)(2,1)S(1)}, bf16[32,1280]{1,0:T(8,128)(2,1)S(1)}, u32[]{:S(2)}, u32[]{:S(2)}) collective-permute-start(bf16[32,1280]{1,0:T(8,128)(2,1)S(1)} %get-tuple-element.43), channel_id=1, source_target_pairs={{0,2},{2,0},{8,10},{10,8},{1,3},{3,1},{9,11},{11,9},{4,6},{6,4},{1... | collective-permute-start | bytes 245768 | tf_op jit(solution)/shard_map/ppermute | solution.py:431

commit v25 on v24

--- a/solution.py
+++ b/solution.py
@@ -17,6 +17,7 @@
 ANY = pl.BlockSpec(memory_space=pl.ANY)
 PARAMS = pltpu.CompilerParams(vmem_limit_bytes=48 * 1024 * 1024)
 AHEAD = pl.CostEstimate(flops=20_000_000_000, bytes_accessed=1_000_000, transcendentals=0)
+FIRST = pl.CostEstimate(flops=380_000_000, bytes_accessed=1_000, transcendentals=0)
 SOON = pl.CostEstimate(flops=6_000_000_000, bytes_accessed=1_000_000, transcendentals=0)
 
 
@@ -449,7 +450,7 @@
     kept, given = lanes(qkv, core, head_dim)
     shared = swap_all(deal(kept, xor(given, ("core",), 1), place), quarter)
     q, kv = sort(shared, place)
-    kv_far = xor(kv, ("zh",), 1)
+    kv_far = after(xor(kv, ("zh",), 1), cost=FIRST)
     near = xor(join(kv, far), ("y",), 1)
     corner = xor(after(w_corner, kv), ("zh", "zl"), 3)
     w_next = xor(after(w_near, kv), ("zl",), 1)

time: 50.4 us -> 51.3 us (1.018)
  starting transfers between devices: 21.9 us -> 23.4 us
  waiting for transfers between devices: 22.7 us -> 22.1 us
    ppermute x18, starting transfers between devices: 21.9 us -> 23.4 us  [xor(): return lax.ppermute(x, axis, [(i, i ^ by) for i in range(size)])]
    ppermute x18, waiting for transfers between devices: 22.7 us -> 22.1 us  [xor(): return lax.ppermute(x, axis, [(i, i ^ by) for i in range(size)])]
  transfers between devices with their start and end apart: 18 -> 18, of which waited for: 13 -> 12; matrix products, arithmetic and copies ran while one was open for 0% -> 0% of each run, Pallas kernels for 5% -> 5%
where the time goes in v25:
time: 51.3 us; the launch traced here: 51.2 us
  starting transfers between devices  23.4 us (46%)
  waiting for transfers between devices  22.1 us (43%)
  Pallas kernels  5.23 us (10%)
    ppermute x18, starting transfers between devices, xor(): return lax.ppermute(x, axis, [(i, i ^ by) for i in range(size)])  23.4 us
    ppermute x18, waiting for transfers between devices, xor(): return lax.ppermute(x, axis, [(i, i ^ by) for i in range(size)])  22.1 us
    pallas_call x1, Pallas kernels, project(): pl.pallas_call(functools.partial(project_kernel, blks, sizes), out_shape=...  1.03 us
  transfers between devices with their start and end apart: 18, of which 12 were waited for; matrix products, arithmetic and copies ran while one was open for 0% of the time, Pallas kernels for 5%

profile of v25, /device:TPU:0, one launch (start us, length us, event | category | flops | bytes accessed | tf_op | source)
XLA Modules:
  0.0 51.2 jit_solution(16790326666206026539)
XLA Ops:
  0.0 0.0 copy-start.1
  0.0 1.0 %shard_map.42 = bf16[640,128]{1,0:T(8,128)(2,1)S(1)} custom-call(bf16[128,5120]{1,0:T(8,128)(2,1)} %x_ref.5), custom_call_target="tpu_custom_call" | custom-call | tf_op jit(solution)/shard_map/pallas_call | solution.py:97
  1.0 4.1 %collective-permute-start.5 = (bf16[640,128]{1,0:T(8,128)(2,1)S(1)}, bf16[640,128]{1,0:T(8,128)(2,1)S(1)}, u32[]{:S(2)}, u32[]{:S(2)}) collective-permute-start(bf16[640,128]{1,0:T(8,128)(2,1)S(1)} %shard_map.42), channel_id=1, source_target_pairs={{0,4},{4,0},{1,5},{5,1},{2,6},{6,2},{3,7},{7,3},{8,12},{12,8},{9,1... | collective-permute-start | bytes 491528 | tf_op jit(solution)/shard_map/ppermute | solution.py:432
  5.1 0.0 copy-done.1
  5.1 0.1 shard_map.37
  5.2 0.1 collective-permute-start
  5.3 1.3 %collective-permute-done.got_ref = bf16[4,96,128]{2,1,0:T(8,128)(2,1)S(1)} collective-permute-done((bf16[4,96,128]{2,1,0:T(8,128)(2,1)S(1)}, bf16[4,96,128]{2,1,0:T(8,128)(2,1)S(1)}, u32[]{:S(2)}, u32[]{:S(2)}) %collective-permute-start) | collective-permute-done | bytes 98336 | tf_op jit(solution)/shard_map/ppermute | solution.py:432
  6.5 2.6 %collective-permute-start.1 = (bf16[2,96,128]{2,1,0:T(8,128)(2,1)S(1)}, bf16[2,96,128]{2,1,0:T(8,128)(2,1)S(1)}, u32[]{:S(2)}, u32[]{:S(2)}) collective-permute-start(bf16[2,96,128]{2,1,0:T(8,128)(2,1)S(1)} %get-tuple-element.27), channel_id=1, source_target_pairs={{0,10},{2,8},{8,2},{10,0},{1,11},{3,9},{9,3},{11,1},{4,14},{6,12},... | collective-permute-start | bytes 147464 | tf_op jit(solution)/shard_map/ppermute | solution.py:432
  9.1 0.5 %collective-permute-start.2 = (bf16[2,96,128]{2,1,0:T(8,128)(2,1)S(1)}, bf16[2,96,128]{2,1,0:T(8,128)(2,1)S(1)}, u32[]{:S(2)}, u32[]{:S(2)}) collective-permute-start(bf16[2,96,128]{2,1,0:T(8,128)(2,1)S(1)} %get-tuple-element.28), channel_id=1, source_target_pairs={{0,8},{2,10},{8,0},{10,2},{1,9},{3,11},{9,1},{11,3},{4,12},{6,14},... | collective-permute-start | bytes 147464 | tf_op jit(solution)/shard_map/ppermute | solution.py:432
  9.7 0.4 collective-permute-start.3
  10.1 1.7 %collective-permute-done.1.refs_0_ = bf16[2,96,128]{2,1,0:T(8,128)(2,1)S(1)} collective-permute-done((bf16[2,96,128]{2,1,0:T(8,128)(2,1)S(1)}, bf16[2,96,128]{2,1,0:T(8,128)(2,1)S(1)}, u32[]{:S(2)}, u32[]{:S(2)}) %collective-permute-start.1) | collective-permute-done | bytes 49184 | tf_op jit(solution)/shard_map/ppermute | solution.py:432
  11.8 1.4 %collective-permute-done.2.refs_1_ = bf16[2,96,128]{2,1,0:T(8,128)(2,1)S(1)} collective-permute-done((bf16[2,96,128]{2,1,0:T(8,128)(2,1)S(1)}, bf16[2,96,128]{2,1,0:T(8,128)(2,1)S(1)}, u32[]{:S(2)}, u32[]{:S(2)}) %collective-permute-start.2) | collective-permute-done | bytes 49184 | tf_op jit(solution)/shard_map/ppermute | solution.py:432
  13.2 1.5 %collective-permute-done.3.refs_2_ = bf16[2,96,128]{2,1,0:T(8,128)(2,1)S(1)} collective-permute-done((bf16[2,96,128]{2,1,0:T(8,128)(2,1)S(1)}, bf16[2,96,128]{2,1,0:T(8,128)(2,1)S(1)}, u32[]{:S(2)}, u32[]{:S(2)}) %collective-permute-start.3) | collective-permute-done | bytes 49184 | tf_op jit(solution)/shard_map/ppermute | solution.py:432
  14.7 0.6 %collective-permute-start.4 = (bf16[512,128]{1,0:T(8,128)(2,1)S(1)}, bf16[512,128]{1,0:T(8,128)(2,1)S(1)}, u32[]{:S(2)}, u32[]{:S(2)}) collective-permute-start(bf16[512,128]{1,0:T(8,128)(2,1)S(1)} %get-tuple-element.34.refs_0_.refs_2_.refs_1_), channel_id=1, source_target_pairs={{0,4},{4,0},{1,5},{5,1},{2,6},{6,2},{3,7},{7,3},{8,12},{12,8},{9,1... | collective-permute-start | bytes 393224 | tf_op jit(solution)/shard_map/ppermute | solution.py:432
  15.3 0.0 collective-permute-done.5.refs_0_
  15.3 0.0 copy-start
  15.4 1.6 %collective-permute-start.6 = (bf16[1152,128]{1,0:T(8,128)(2,1)S(1)}, bf16[1152,128]{1,0:T(8,128)(2,1)S(1)}, u32[]{:S(2)}, u32[]{:S(2)}) collective-permute-start(bf16[1152,128]{1,0:T(8,128)(2,1)S(1)} %shard_map.44), channel_id=1, source_target_pairs={{0,16},{16,0},{1,17},{17,1},{2,18},{18,2},{3,19},{19,3},{4,20},{20... | collective-permute-start | bytes 884744 | tf_op jit(solution)/shard_map/ppermute | solution.py:432
  16.9 0.1 pad_add_fusion.1.at_ref
  17.0 0.0 copy-done
  17.0 0.6 %shard_map.46 = (bf16[64,1280]{1,0:T(8,128)(2,1)S(1)}, bf16[128,1280]{1,0:T(8,128)(2,1)S(1)}, bf16[128,1280]{1,0:T(8,128)(2,1)S(1)}) custom-call(s32[3]{0:T(128)S(1)} %pad_add_fusion.1.at_ref, bf16[128,5120]{1,0:T(8,128)(2,1)S(1)} %copy-done), custom_call_target="tpu_custom_call" | custom-call | tf_op jit(solution)/shard_map/pallas_call | solution.py:117
  17.6 0.0 copy-start.2
  17.7 2.0 %collective-permute-start.12 = (bf16[64,1280]{1,0:T(8,128)(2,1)S(1)}, bf16[64,1280]{1,0:T(8,128)(2,1)S(1)}, u32[]{:S(2)}, u32[]{:S(2)}) collective-permute-start(bf16[64,1280]{1,0:T(8,128)(2,1)S(1)} %shard_map.48), channel_id=1, source_target_pairs={{0,6},{2,4},{4,2},{6,0},{1,7},{3,5},{5,3},{7,1},{8,14},{10,12},{12... | collective-permute-start | bytes 491528 | tf_op jit(solution)/shard_map/ppermute | solution.py:432
  19.7 1.1 %collective-permute-start.11 = (bf16[128,1280]{1,0:T(8,128)(2,1)S(1)}, bf16[128,1280]{1,0:T(8,128)(2,1)S(1)}, u32[]{:S(2)}, u32[]{:S(2)}) collective-permute-start(bf16[128,1280]{1,0:T(8,128)(2,1)S(1)} %shard_map.47), channel_id=1, source_target_pairs={{0,2},{2,0},{1,3},{3,1},{4,6},{6,4},{5,7},{7,5},{8,10},{10,8},{9,1... | collective-permute-start | bytes 983048 | tf_op jit(solution)/shard_map/ppermute | solution.py:432
  20.7 5.7 %collective-permute-done.4.refs_0_ = bf16[512,128]{1,0:T(8,128)(2,1)S(1)} collective-permute-done((bf16[512,128]{1,0:T(8,128)(2,1)S(1)}, bf16[512,128]{1,0:T(8,128)(2,1)S(1)}, u32[]{:S(2)}, u32[]{:S(2)}) %collective-permute-start.4) | collective-permute-done | bytes 131104 | tf_op jit(solution)/shard_map/ppermute | solution.py:432
  26.4 1.6 %collective-permute-start.7 = (bf16[512,128]{1,0:T(8,128)(2,1)S(1)}, bf16[512,128]{1,0:T(8,128)(2,1)S(1)}, u32[]{:S(2)}, u32[]{:S(2)}) collective-permute-start(bf16[512,128]{1,0:T(8,128)(2,1)S(1)} %shard_map.41.refs_3_), channel_id=1, source_target_pairs={{0,16},{16,0},{1,17},{17,1},{2,18},{18,2},{3,19},{19,3},{4,20},{20... | collective-permute-start | bytes 393224 | tf_op jit(solution)/shard_map/ppermute | solution.py:432
  28.1 0.1 pad_add_fusion.base_ref
  28.1 0.0 copy-done.2
  28.2 0.7 %shard_map.40 = (bf16[256,256]{1,0:T(8,128)(2,1)S(1)}, bf16[256,256]{1,0:T(8,128)(2,1)S(1)}) custom-call(s32[2]{0:T(128)S(1)} %pad_add_fusion.base_ref, s32[8]{0:T(128)S(1)} %copy-done.2), custom_call_target="tpu_custom_call" | custom-call | tf_op jit(solution)/shard_map/pallas_call | solution.py:270
  28.9 2.5 %collective-permute-done.7.refs_5_ = bf16[512,128]{1,0:T(8,128)(2,1)S(1)} collective-permute-done((bf16[512,128]{1,0:T(8,128)(2,1)S(1)}, bf16[512,128]{1,0:T(8,128)(2,1)S(1)}, u32[]{:S(2)}, u32[]{:S(2)}) %collective-permute-start.7) | collective-permute-done | bytes 131104 | tf_op jit(solution)/shard_map/ppermute | solution.py:432
  31.4 0.0 collective-permute-done.6.refs_4_.refs_7_
  31.4 0.6 %shard_map.45.refs_1_.refs_0_ = bf16[256,128]{1,0:T(8,128)(2,1)S(1)} custom-call(bf16[256,128]{1,0:T(8,128)(2,1)S(1)} %get-tuple-element.31.q_ref, bf16[256,256]{1,0:T(8,128)(2,1)S(1)} %get-tuple-element.32.refs_0_, bf16[256,256]{1,0:T(8,128)(2,1)S(1)} %get-tuple-element.33.refs_1_, bf16[512,128]{1,0:T(8,128)(2,1)S(1)} %get-tuple-element.34.refs_0_.refs_2_.refs_1_, ...), custom_call_target="tpu_custom_call" | custom-call | tf_op jit(solution)/shard_map/pallas_call | solution.py:330
  32.0 0.0 collective-permute-done.12.refs_0_
  32.1 1.7 %collective-permute-start.13 = (bf16[64,1280]{1,0:T(8,128)(2,1)S(1)}, bf16[64,1280]{1,0:T(8,128)(2,1)S(1)}, u32[]{:S(2)}, u32[]{:S(2)}) collective-permute-start(bf16[64,1280]{1,0:T(8,128)(2,1)S(1)} %shard_map.49.refs_8_), channel_id=1, source_target_pairs={{0,16},{16,0},{1,17},{17,1},{2,18},{18,2},{3,19},{19,3},{4,20},{20... | collective-permute-start | bytes 491528 | tf_op jit(solution)/shard_map/ppermute | solution.py:432
  33.8 1.8 %collective-permute-start.10 = (bf16[256,128]{1,0:T(8,128)(2,1)S(1)}, bf16[256,128]{1,0:T(8,128)(2,1)S(1)}, u32[]{:S(2)}, u32[]{:S(2)}) collective-permute-start(bf16[256,128]{1,0:T(8,128)(2,1)S(1)} %shard_map.45.refs_1_.refs_0_), channel_id=1, source_target_pairs={{0,10},{2,8},{8,2},{10,0},{1,11},{3,9},{9,3},{11,1},{4,14},{6,12},... | collective-permute-start | bytes 196616 | tf_op jit(solution)/shard_map/ppermute | solution.py:432
  35.5 0.0 collective-permute-start.9
  35.5 1.7 %collective-permute-start.8 = (bf16[256,128]{1,0:T(8,128)(2,1)S(1)}, bf16[256,128]{1,0:T(8,128)(2,1)S(1)}, u32[]{:S(2)}, u32[]{:S(2)}) collective-permute-start(bf16[256,128]{1,0:T(8,128)(2,1)S(1)} %shard_map.45.refs_1_.refs_0_), channel_id=1, source_target_pairs={{0,2},{2,0},{8,10},{10,8},{1,3},{3,1},{9,11},{11,9},{4,6},{6,4},{1... | collective-permute-start | bytes 196616 | tf_op jit(solution)/shard_map/ppermute | solution.py:432
  37.2 0.1 stack.55.at_ref
  37.3 0.0 collective-permute-done.11.refs_5_
  37.3 1.6 %collective-permute-done.10.refs_3_ = bf16[256,128]{1,0:T(8,128)(2,1)S(1)} collective-permute-done((bf16[256,128]{1,0:T(8,128)(2,1)S(1)}, bf16[256,128]{1,0:T(8,128)(2,1)S(1)}, u32[]{:S(2)}, u32[]{:S(2)}) %collective-permute-start.10) | collective-permute-done | bytes 65568 | tf_op jit(solution)/shard_map/ppermute | solution.py:432
  38.9 0.9 %collective-permute-done.9.refs_2_ = bf16[256,128]{1,0:T(8,128)(2,1)S(1)} collective-permute-done((bf16[256,128]{1,0:T(8,128)(2,1)S(1)}, bf16[256,128]{1,0:T(8,128)(2,1)S(1)}, u32[]{:S(2)}, u32[]{:S(2)}) %collective-permute-start.9) | collective-permute-done | bytes 65568 | tf_op jit(solution)/shard_map/ppermute | solution.py:432
  39.8 0.0 collective-permute-done.8.refs_1_
  39.8 0.0 collective-permute-done.13.refs_9_
  39.8 1.0 %shard_map.50 = (bf16[4,32,1280]{2,1,0:T(8,128)(2,1)S(1)}, bf16[256,512]{1,0:T(8,128)(2,1)S(1)}, bf16[512,1280]{1,0:T(8,128)(2,1)S(1)}) custom-call(s32[6]{0:T(128)S(1)} %stack.55.at_ref, s32[1]{0:T(128)} %bitcast.place_ref, bf16[256,128]{1,0:T(8,128)(2,1)S(1)} %shard_map.45.refs_1_.refs_0_, bf16[256,128]{1,0:T(8,128)(2,1)S(1)} %collective-permute-done.8.refs_1_, ...), custom_call_target="tpu_custom_call" | custom-call | tf_op jit(solution)/shard_map/pallas_call | solution.py:372
  40.9 0.1 collective-permute-start.14
  40.9 0.3 shard_map.51.x_ref
  41.3 1.3 %collective-permute-done.14.y_ref = bf16[4,32,1280]{2,1,0:T(8,128)(2,1)S(1)} collective-permute-done((bf16[4,32,1280]{2,1,0:T(8,128)(2,1)S(1)}, bf16[4,32,1280]{2,1,0:T(8,128)(2,1)S(1)}, u32[]{:S(2)}, u32[]{:S(2)}) %collective-permute-start.14) | collective-permute-done | bytes 327712 | tf_op jit(solution)/shard_map/ppermute | solution.py:432
  42.5 0.1 shard_map.52
  42.6 2.5 %collective-permute-start.15 = (bf16[32,1280]{1,0:T(8,128)(2,1)S(1)}, bf16[32,1280]{1,0:T(8,128)(2,1)S(1)}, u32[]{:S(2)}, u32[]{:S(2)}) collective-permute-start(bf16[32,1280]{1,0:T(8,128)(2,1)S(1)} %get-tuple-element.41), channel_id=1, source_target_pairs={{0,10},{2,8},{8,2},{10,0},{1,11},{3,9},{9,3},{11,1},{4,14},{6,12},... | collective-permute-start | bytes 245768 | tf_op jit(solution)/shard_map/ppermute | solution.py:432
  45.1 0.7 %collective-permute-start.16 = (bf16[32,1280]{1,0:T(8,128)(2,1)S(1)}, bf16[32,1280]{1,0:T(8,128)(2,1)S(1)}, u32[]{:S(2)}, u32[]{:S(2)}) collective-permute-start(bf16[32,1280]{1,0:T(8,128)(2,1)S(1)} %get-tuple-element.42), channel_id=1, source_target_pairs={{0,8},{2,10},{8,0},{10,2},{1,9},{3,11},{9,1},{11,3},{4,12},{6,14},... | collective-permute-start | bytes 245768 | tf_op jit(solution)/shard_map/ppermute | solution.py:432
  45.9 0.3 collective-permute-start.17
  46.2 1.9 %collective-permute-done.15.refs_0_ = bf16[32,1280]{1,0:T(8,128)(2,1)S(1)} collective-permute-done((bf16[32,1280]{1,0:T(8,128)(2,1)S(1)}, bf16[32,1280]{1,0:T(8,128)(2,1)S(1)}, u32[]{:S(2)}, u32[]{:S(2)}) %collective-permute-start.15) | collective-permute-done | bytes 81952 | tf_op jit(solution)/shard_map/ppermute | solution.py:432
  48.1 1.7 %collective-permute-done.16.refs_1_ = bf16[32,1280]{1,0:T(8,128)(2,1)S(1)} collective-permute-done((bf16[32,1280]{1,0:T(8,128)(2,1)S(1)}, bf16[32,1280]{1,0:T(8,128)(2,1)S(1)}, u32[]{:S(2)}, u32[]{:S(2)}) %collective-permute-start.16) | collective-permute-done | bytes 81952 | tf_op jit(solution)/shard_map/ppermute | solution.py:432
  49.8 0.6 %collective-permute-done.17.refs_2_ = bf16[32,1280]{1,0:T(8,128)(2,1)S(1)} collective-permute-done((bf16[32,1280]{1,0:T(8,128)(2,1)S(1)}, bf16[32,1280]{1,0:T(8,128)(2,1)S(1)}, u32[]{:S(2)}, u32[]{:S(2)}) %collective-permute-start.17) | collective-permute-done | bytes 81952 | tf_op jit(solution)/shard_map/ppermute | solution.py:432
  50.4 0.8 %shard_map.53 = bf16[32,5120]{1,0:T(8,128)(2,1)} custom-call(s32[1]{0:T(128)} %bitcast.place_ref, bf16[32,1280]{1,0:T(8,128)(2,1)S(1)} %collective-permute-done.15.refs_0_, bf16[32,1280]{1,0:T(8,128)(2,1)S(1)} %collective-permute-done.16.refs_1_, bf16[32,1280]{1,0:T(8,128)(2,1)S(1)} %collective-permute-done.17.refs_2_, ...), custom_call_target="tpu_custom_call" | custom-call | tf_op jit(solution)/shard_map/pallas_call | solution.py:421
  (8 shorter events, 0.1 us)
Async XLA Ops:
  0.0 5.1 %copy-start.1 = (bf16[3,32,1024]{2,1,0:T(8,128)(2,1)S(1)}, bf16[3,32,1024]{2,1,0:T(8,128)(2,1)}, u32[]{:S(2)}) copy-start(bf16[3,32,1024]{2,1,0:T(8,128)(2,1)} %x_ref.3) | copy-start | bytes 589828
  1.0 14.3 %collective-permute-start.5 = (bf16[640,128]{1,0:T(8,128)(2,1)S(1)}, bf16[640,128]{1,0:T(8,128)(2,1)S(1)}, u32[]{:S(2)}, u32[]{:S(2)}) collective-permute-start(bf16[640,128]{1,0:T(8,128)(2,1)S(1)} %shard_map.42), channel_id=1, source_target_pairs={{0,4},{4,0},{1,5},{5,1},{2,6},{6,2},{3,7},{7,3},{8,12},{12,8},{9,1... | collective-permute-start | bytes 491528 | tf_op jit(solution)/shard_map/ppermute | solution.py:432
  5.2 1.4 %collective-permute-start = (bf16[4,96,128]{2,1,0:T(8,128)(2,1)S(1)}, bf16[4,96,128]{2,1,0:T(8,128)(2,1)S(1)}, u32[]{:S(2)}, u32[]{:S(2)}) collective-permute-start(bf16[4,96,128]{2,1,0:T(8,128)(2,1)S(1)} %get-tuple-element.26), channel_id=1, source_target_pairs={{0,1},{1,0},{2,3},{3,2},{4,5},{5,4},{6,7},{7,6},{8,9},{9,8},{10,11... | collective-permute-start | bytes 294920 | tf_op jit(solution)/shard_map/ppermute | solution.py:432
  6.5 5.3 %collective-permute-start.1 = (bf16[2,96,128]{2,1,0:T(8,128)(2,1)S(1)}, bf16[2,96,128]{2,1,0:T(8,128)(2,1)S(1)}, u32[]{:S(2)}, u32[]{:S(2)}) collective-permute-start(bf16[2,96,128]{2,1,0:T(8,128)(2,1)S(1)} %get-tuple-element.27), channel_id=1, source_target_pairs={{0,10},{2,8},{8,2},{10,0},{1,11},{3,9},{9,3},{11,1},{4,14},{6,12},... | collective-permute-start | bytes 147464 | tf_op jit(solution)/shard_map/ppermute | solution.py:432
  9.1 4.1 %collective-permute-start.2 = (bf16[2,96,128]{2,1,0:T(8,128)(2,1)S(1)}, bf16[2,96,128]{2,1,0:T(8,128)(2,1)S(1)}, u32[]{:S(2)}, u32[]{:S(2)}) collective-permute-start(bf16[2,96,128]{2,1,0:T(8,128)(2,1)S(1)} %get-tuple-element.28), channel_id=1, source_target_pairs={{0,8},{2,10},{8,0},{10,2},{1,9},{3,11},{9,1},{11,3},{4,12},{6,14},... | collective-permute-start | bytes 147464 | tf_op jit(solution)/shard_map/ppermute | solution.py:432
  9.7 5.1 %collective-permute-start.3 = (bf16[2,96,128]{2,1,0:T(8,128)(2,1)S(1)}, bf16[2,96,128]{2,1,0:T(8,128)(2,1)S(1)}, u32[]{:S(2)}, u32[]{:S(2)}) collective-permute-start(bf16[2,96,128]{2,1,0:T(8,128)(2,1)S(1)} %get-tuple-element.29), channel_id=1, source_target_pairs={{0,2},{2,0},{8,10},{10,8},{1,3},{3,1},{9,11},{11,9},{4,6},{6,4},{1... | collective-permute-start | bytes 147464 | tf_op jit(solution)/shard_map/ppermute | solution.py:432
  14.7 11.7 %collective-permute-start.4 = (bf16[512,128]{1,0:T(8,128)(2,1)S(1)}, bf16[512,128]{1,0:T(8,128)(2,1)S(1)}, u32[]{:S(2)}, u32[]{:S(2)}) collective-permute-start(bf16[512,128]{1,0:T(8,128)(2,1)S(1)} %get-tuple-element.34.refs_0_.refs_2_.refs_1_), channel_id=1, source_target_pairs={{0,4},{4,0},{1,5},{5,1},{2,6},{6,2},{3,7},{7,3},{8,12},{12,8},{9,1... | collective-permute-start | bytes 393224 | tf_op jit(solution)/shard_map/ppermute | solution.py:432
  15.3 1.7 %copy-start = (bf16[128,5120]{1,0:T(8,128)(2,1)S(1)}, bf16[128,5120]{1,0:T(8,128)(2,1)}, u32[]{:S(2)}) copy-start(bf16[128,5120]{1,0:T(8,128)(2,1)} %x_ref.5) | copy-start | bytes 3932164
  15.4 16.1 %collective-permute-start.6 = (bf16[1152,128]{1,0:T(8,128)(2,1)S(1)}, bf16[1152,128]{1,0:T(8,128)(2,1)S(1)}, u32[]{:S(2)}, u32[]{:S(2)}) collective-permute-start(bf16[1152,128]{1,0:T(8,128)(2,1)S(1)} %shard_map.44), channel_id=1, source_target_pairs={{0,16},{16,0},{1,17},{17,1},{2,18},{18,2},{3,19},{19,3},{4,20},{20... | collective-permute-start | bytes 884744 | tf_op jit(solution)/shard_map/ppermute | solution.py:432
  17.6 10.5 %copy-start.2 = (s32[8]{0:T(128)S(1)}, s32[8]{0:T(128)}, u32[]{:S(2)}) copy-start(s32[8]{0:T(128)} %clip_ref.1) | copy-start | bytes 100
  17.7 14.4 %collective-permute-start.12 = (bf16[64,1280]{1,0:T(8,128)(2,1)S(1)}, bf16[64,1280]{1,0:T(8,128)(2,1)S(1)}, u32[]{:S(2)}, u32[]{:S(2)}) collective-permute-start(bf16[64,1280]{1,0:T(8,128)(2,1)S(1)} %shard_map.48), channel_id=1, source_target_pairs={{0,6},{2,4},{4,2},{6,0},{1,7},{3,5},{5,3},{7,1},{8,14},{10,12},{12... | collective-permute-start | bytes 491528 | tf_op jit(solution)/shard_map/ppermute | solution.py:432
  19.7 17.6 %collective-permute-start.11 = (bf16[128,1280]{1,0:T(8,128)(2,1)S(1)}, bf16[128,1280]{1,0:T(8,128)(2,1)S(1)}, u32[]{:S(2)}, u32[]{:S(2)}) collective-permute-start(bf16[128,1280]{1,0:T(8,128)(2,1)S(1)} %shard_map.47), channel_id=1, source_target_pairs={{0,2},{2,0},{1,3},{3,1},{4,6},{6,4},{5,7},{7,5},{8,10},{10,8},{9,1... | collective-permute-start | bytes 983048 | tf_op jit(solution)/shard_map/ppermute | solution.py:432
  26.4 5.0 %collective-permute-start.7 = (bf16[512,128]{1,0:T(8,128)(2,1)S(1)}, bf16[512,128]{1,0:T(8,128)(2,1)S(1)}, u32[]{:S(2)}, u32[]{:S(2)}) collective-permute-start(bf16[512,128]{1,0:T(8,128)(2,1)S(1)} %shard_map.41.refs_3_), channel_id=1, source_target_pairs={{0,16},{16,0},{1,17},{17,1},{2,18},{18,2},{3,19},{19,3},{4,20},{20... | collective-permute-start | bytes 393224 | tf_op jit(solution)/shard_map/ppermute | solution.py:432
  32.1 7.8 %collective-permute-start.13 = (bf16[64,1280]{1,0:T(8,128)(2,1)S(1)}, bf16[64,1280]{1,0:T(8,128)(2,1)S(1)}, u32[]{:S(2)}, u32[]{:S(2)}) collective-permute-start(bf16[64,1280]{1,0:T(8,128)(2,1)S(1)} %shard_map.49.refs_8_), channel_id=1, source_target_pairs={{0,16},{16,0},{1,17},{17,1},{2,18},{18,2},{3,19},{19,3},{4,20},{20... | collective-permute-start | bytes 491528 | tf_op jit(solution)/shard_map/ppermute | solution.py:432
  33.8 5.2 %collective-permute-start.10 = (bf16[256,128]{1,0:T(8,128)(2,1)S(1)}, bf16[256,128]{1,0:T(8,128)(2,1)S(1)}, u32[]{:S(2)}, u32[]{:S(2)}) collective-permute-start(bf16[256,128]{1,0:T(8,128)(2,1)S(1)} %shard_map.45.refs_1_.refs_0_), channel_id=1, source_target_pairs={{0,10},{2,8},{8,2},{10,0},{1,11},{3,9},{9,3},{11,1},{4,14},{6,12},... | collective-permute-start | bytes 196616 | tf_op jit(solution)/shard_map/ppermute | solution.py:432
  35.5 4.3 %collective-permute-start.9 = (bf16[256,128]{1,0:T(8,128)(2,1)S(1)}, bf16[256,128]{1,0:T(8,128)(2,1)S(1)}, u32[]{:S(2)}, u32[]{:S(2)}) collective-permute-start(bf16[256,128]{1,0:T(8,128)(2,1)S(1)} %shard_map.45.refs_1_.refs_0_), channel_id=1, source_target_pairs={{0,8},{2,10},{8,0},{10,2},{1,9},{3,11},{9,1},{11,3},{4,12},{6,14},... | collective-permute-start | bytes 196616 | tf_op jit(solution)/shard_map/ppermute | solution.py:432
  35.5 4.3 %collective-permute-start.8 = (bf16[256,128]{1,0:T(8,128)(2,1)S(1)}, bf16[256,128]{1,0:T(8,128)(2,1)S(1)}, u32[]{:S(2)}, u32[]{:S(2)}) collective-permute-start(bf16[256,128]{1,0:T(8,128)(2,1)S(1)} %shard_map.45.refs_1_.refs_0_), channel_id=1, source_target_pairs={{0,2},{2,0},{8,10},{10,8},{1,3},{3,1},{9,11},{11,9},{4,6},{6,4},{1... | collective-permute-start | bytes 196616 | tf_op jit(solution)/shard_map/ppermute | solution.py:432
  40.9 1.7 %collective-permute-start.14 = (bf16[4,32,1280]{2,1,0:T(8,128)(2,1)S(1)}, bf16[4,32,1280]{2,1,0:T(8,128)(2,1)S(1)}, u32[]{:S(2)}, u32[]{:S(2)}) collective-permute-start(bf16[4,32,1280]{2,1,0:T(8,128)(2,1)S(1)} %get-tuple-element.40), channel_id=1, source_target_pairs={{0,1},{1,0},{2,3},{3,2},{4,5},{5,4},{6,7},{7,6},{8,9},{9,8},{10,11... | collective-permute-start | bytes 983048 | tf_op jit(solution)/shard_map/ppermute | solution.py:432
  42.6 5.5 %collective-permute-start.15 = (bf16[32,1280]{1,0:T(8,128)(2,1)S(1)}, bf16[32,1280]{1,0:T(8,128)(2,1)S(1)}, u32[]{:S(2)}, u32[]{:S(2)}) collective-permute-start(bf16[32,1280]{1,0:T(8,128)(2,1)S(1)} %get-tuple-element.41), channel_id=1, source_target_pairs={{0,10},{2,8},{8,2},{10,0},{1,11},{3,9},{9,3},{11,1},{4,14},{6,12},... | collective-permute-start | bytes 245768 | tf_op jit(solution)/shard_map/ppermute | solution.py:432
  45.1 4.7 %collective-permute-start.16 = (bf16[32,1280]{1,0:T(8,128)(2,1)S(1)}, bf16[32,1280]{1,0:T(8,128)(2,1)S(1)}, u32[]{:S(2)}, u32[]{:S(2)}) collective-permute-start(bf16[32,1280]{1,0:T(8,128)(2,1)S(1)} %get-tuple-element.42), channel_id=1, source_target_pairs={{0,8},{2,10},{8,0},{10,2},{1,9},{3,11},{9,1},{11,3},{4,12},{6,14},... | collective-permute-start | bytes 245768 | tf_op jit(solution)/shard_map/ppermute | solution.py:432
  45.9 4.6 %collective-permute-start.17 = (bf16[32,1280]{1,0:T(8,128)(2,1)S(1)}, bf16[32,1280]{1,0:T(8,128)(2,1)S(1)}, u32[]{:S(2)}, u32[]{:S(2)}) collective-permute-start(bf16[32,1280]{1,0:T(8,128)(2,1)S(1)} %get-tuple-element.43), channel_id=1, source_target_pairs={{0,2},{2,0},{8,10},{10,8},{1,3},{3,1},{9,11},{11,9},{4,6},{6,4},{1... | collective-permute-start | bytes 245768 | tf_op jit(solution)/shard_map/ppermute | solution.py:432

commit v26 on v24

--- a/solution.py
+++ b/solution.py
@@ -275,7 +275,7 @@
     )(index_array(*bases), frame_clip)
 
 
-def attention_kernel(head_dim, n_mask, which, joint, q_ref, *refs):
+def attention_kernel(head_dim, tok, n_mask, which, joint, place_ref, q_ref, *refs):
     *refs, out_ref = refs
     mask_refs, refs = refs[:n_mask], refs[n_mask:]
     count, width = q_ref.shape
@@ -320,19 +320,23 @@
                 )
                 total = part if total is None else total + part
                 acc = dot if acc is None else acc + dot
-        out_ref[:, cols] = (acc / total).astype(out_ref.dtype)
-
-
-def attention(q, kvs, mask_of, which, head_dim):
+        result = (acc / total).astype(out_ref.dtype)
+        half = count // (2 * tok)
+        for g in range(2 * half):
+            at = (place_ref[0] % 2 ^ g % 2 ^ 1) * half + g // 2
+            out_ref[rows_at(at, tok), cols] = result[g * tok:(g + 1) * tok, :]
+
+
+def attention(q, kvs, mask_of, which, head_dim, place, tok):
     joint = [not isinstance(kv, tuple) for kv in kvs]
     arrays = [x for kv, both in zip(kvs, joint) for x in ((kv,) if both else kv)]
     return pl.pallas_call(
-        functools.partial(attention_kernel, head_dim, len(mask_of), which, joint),
+        functools.partial(attention_kernel, head_dim, tok, len(mask_of), which, joint),
         out_shape=jax.ShapeDtypeStruct(q.shape, q.dtype),
-        in_specs=[VMEM] * (1 + len(mask_of) + len(arrays)),
+        in_specs=[SMEM] + [VMEM] * (1 + len(mask_of) + len(arrays)),
         out_specs=VMEM,
         compiler_params=PARAMS,
-    )(q, *mask_of, *arrays)
+    )(place, q, *mask_of, *arrays)
 
 
 def project_kernel(n_attn, sizes, at_ref, place_ref, *refs):
@@ -340,12 +344,9 @@
     out_ref, a_ref, w_all = refs[-3:]
     width = attn_refs[0].shape[1]
     blks, tok, cols = out_ref.shape
-    blk, other = place_ref[0] // 2, 1 - place_ref[0] % 2
+    blk = place_ref[0] // 2
     for k, ref in enumerate(attn_refs):
-        at = rows_at(blk ^ k, width)
-        for b in range(blks):
-            a_ref[b * tok:(b + 1) * tok, at] = ref[rows_at(2 * b + other, tok), :]
-            a_ref[(blks + b) * tok:(blks + b + 1) * tok, at] = ref[rows_at(2 * b + 1 - other, tok), :]
+        a_ref[:, rows_at(blk ^ k, width)] = ref[...]
     for i, (ref, rows) in enumerate(zip(w_refs, sizes)):
         at = rows_at(at_ref[i], rows)
         if ref.shape[1] >= cols:
@@ -457,7 +458,7 @@
 
     bases = [y * 2 * FRB, (1 - y) * 2 * FRB]
     mask_of = masks(bases, 4 * tok, tok, 8 * tok, frame_clip)
-    attn = attention(q, kvs, mask_of, [0, 0, 1, 1], head_dim)
+    attn = attention(q, kvs, mask_of, [0, 0, 1, 1], head_dim, place, tok)
     corner = after(corner, attn)
     corner_rest = xor(corner, ("y",), 1)
     attns = swap_all([attn] * 4, quarter)
@@ -482,7 +483,7 @@
     q, kv = cut(own)
     kvs = [kv] + [xor(kv, ("row",), by) for by in others]
     mask_of = masks([0], 2 * tok, tok, 2 * blks * tok, frame_clip)
-    attn = attention(q, kvs, mask_of, [0] * rows, head_dim)
+    attn = attention(q, kvs, mask_of, [0] * rows, head_dim, place, tok)
     attns = swap_all([attn] * blks, ("blk",))
     at = [row ^ by for by in range(rows)]
     parts = project(attns, w_parts, [head_dim] * rows, at, place, tok, cols)

time: 50.4 us -> 50.4 us (level)
  no operation moved by 1% of the time
where the time goes in v26:
time: 50.4 us; the launch traced here: 50.2 us
  waiting for transfers between devices  22.7 us (45%)
  starting transfers between devices  21.9 us (43%)
  Pallas kernels  5.24 us (10%)
    ppermute x18, waiting for transfers between devices, xor(): return lax.ppermute(x, axis, [(i, i ^ by) for i in range(size)])  22.7 us
    ppermute x18, starting transfers between devices, xor(): return lax.ppermute(x, axis, [(i, i ^ by) for i in range(size)])  21.9 us
    pallas_call x1, Pallas kernels, project(): pl.pallas_call(functools.partial(project_kernel, blks, sizes), out_shape=...  1.03 us
  transfers between devices with their start and end apart: 18, of which 13 were waited for; matrix products, arithmetic and copies ran while one was open for 0% of the time, Pallas kernels for 5%

profile of v26, /device:TPU:0, one launch (start us, length us, event | category | flops | bytes accessed | tf_op | source)
XLA Modules:
  0.0 50.2 jit_solution(2212915717534895092)
XLA Ops:
  0.0 0.0 copy-start.1
  0.0 1.0 %shard_map.41 = bf16[640,128]{1,0:T(8,128)(2,1)S(1)} custom-call(bf16[128,5120]{1,0:T(8,128)(2,1)} %x_ref.5), custom_call_target="tpu_custom_call" | custom-call | tf_op jit(solution)/shard_map/pallas_call | solution.py:96
  1.0 4.1 %collective-permute-start.5 = (bf16[640,128]{1,0:T(8,128)(2,1)S(1)}, bf16[640,128]{1,0:T(8,128)(2,1)S(1)}, u32[]{:S(2)}, u32[]{:S(2)}) collective-permute-start(bf16[640,128]{1,0:T(8,128)(2,1)S(1)} %shard_map.41), channel_id=1, source_target_pairs={{0,4},{4,0},{1,5},{5,1},{2,6},{6,2},{3,7},{7,3},{8,12},{12,8},{9,1... | collective-permute-start | bytes 491528 | tf_op jit(solution)/shard_map/ppermute | solution.py:432
  5.1 0.0 copy-done.1
  5.1 0.1 shard_map.37
  5.2 0.1 collective-permute-start
  5.3 1.3 %collective-permute-done.got_ref = bf16[4,96,128]{2,1,0:T(8,128)(2,1)S(1)} collective-permute-done((bf16[4,96,128]{2,1,0:T(8,128)(2,1)S(1)}, bf16[4,96,128]{2,1,0:T(8,128)(2,1)S(1)}, u32[]{:S(2)}, u32[]{:S(2)}) %collective-permute-start) | collective-permute-done | bytes 98336 | tf_op jit(solution)/shard_map/ppermute | solution.py:432
  6.5 2.6 %collective-permute-start.1 = (bf16[2,96,128]{2,1,0:T(8,128)(2,1)S(1)}, bf16[2,96,128]{2,1,0:T(8,128)(2,1)S(1)}, u32[]{:S(2)}, u32[]{:S(2)}) collective-permute-start(bf16[2,96,128]{2,1,0:T(8,128)(2,1)S(1)} %get-tuple-element.27), channel_id=1, source_target_pairs={{0,10},{2,8},{8,2},{10,0},{1,11},{3,9},{9,3},{11,1},{4,14},{6,12},... | collective-permute-start | bytes 147464 | tf_op jit(solution)/shard_map/ppermute | solution.py:432
  9.1 0.5 %collective-permute-start.2 = (bf16[2,96,128]{2,1,0:T(8,128)(2,1)S(1)}, bf16[2,96,128]{2,1,0:T(8,128)(2,1)S(1)}, u32[]{:S(2)}, u32[]{:S(2)}) collective-permute-start(bf16[2,96,128]{2,1,0:T(8,128)(2,1)S(1)} %get-tuple-element.28), channel_id=1, source_target_pairs={{0,8},{2,10},{8,0},{10,2},{1,9},{3,11},{9,1},{11,3},{4,12},{6,14},... | collective-permute-start | bytes 147464 | tf_op jit(solution)/shard_map/ppermute | solution.py:432
  9.7 0.4 collective-permute-start.3
  10.1 1.7 %collective-permute-done.1.refs_0_ = bf16[2,96,128]{2,1,0:T(8,128)(2,1)S(1)} collective-permute-done((bf16[2,96,128]{2,1,0:T(8,128)(2,1)S(1)}, bf16[2,96,128]{2,1,0:T(8,128)(2,1)S(1)}, u32[]{:S(2)}, u32[]{:S(2)}) %collective-permute-start.1) | collective-permute-done | bytes 49184 | tf_op jit(solution)/shard_map/ppermute | solution.py:432
  11.8 1.4 %collective-permute-done.2.refs_1_ = bf16[2,96,128]{2,1,0:T(8,128)(2,1)S(1)} collective-permute-done((bf16[2,96,128]{2,1,0:T(8,128)(2,1)S(1)}, bf16[2,96,128]{2,1,0:T(8,128)(2,1)S(1)}, u32[]{:S(2)}, u32[]{:S(2)}) %collective-permute-start.2) | collective-permute-done | bytes 49184 | tf_op jit(solution)/shard_map/ppermute | solution.py:432
  13.2 1.5 %collective-permute-done.3.refs_2_ = bf16[2,96,128]{2,1,0:T(8,128)(2,1)S(1)} collective-permute-done((bf16[2,96,128]{2,1,0:T(8,128)(2,1)S(1)}, bf16[2,96,128]{2,1,0:T(8,128)(2,1)S(1)}, u32[]{:S(2)}, u32[]{:S(2)}) %collective-permute-start.3) | collective-permute-done | bytes 49184 | tf_op jit(solution)/shard_map/ppermute | solution.py:432
  14.7 0.0 collective-permute-done.5.refs_0_
  14.7 0.0 copy-start
  14.8 0.0 copy-start.2
  14.8 1.6 %collective-permute-start.6 = (bf16[1152,128]{1,0:T(8,128)(2,1)S(1)}, bf16[1152,128]{1,0:T(8,128)(2,1)S(1)}, u32[]{:S(2)}, u32[]{:S(2)}) collective-permute-start(bf16[1152,128]{1,0:T(8,128)(2,1)S(1)} %shard_map.43), channel_id=1, source_target_pairs={{0,16},{16,0},{1,17},{17,1},{2,18},{18,2},{3,19},{19,3},{4,20},{20... | collective-permute-start | bytes 884744 | tf_op jit(solution)/shard_map/ppermute | solution.py:432
  16.4 0.5 collective-permute-start.4
  16.9 0.1 pad_add_fusion.1.at_ref
  17.0 0.0 copy-done
  17.0 0.6 %shard_map.45 = (bf16[64,1280]{1,0:T(8,128)(2,1)S(1)}, bf16[128,1280]{1,0:T(8,128)(2,1)S(1)}, bf16[128,1280]{1,0:T(8,128)(2,1)S(1)}) custom-call(s32[3]{0:T(128)S(1)} %pad_add_fusion.1.at_ref, bf16[128,5120]{1,0:T(8,128)(2,1)S(1)} %copy-done), custom_call_target="tpu_custom_call" | custom-call | tf_op jit(solution)/shard_map/pallas_call | solution.py:116
  17.6 2.5 %collective-permute-start.11 = (bf16[128,1280]{1,0:T(8,128)(2,1)S(1)}, bf16[128,1280]{1,0:T(8,128)(2,1)S(1)}, u32[]{:S(2)}, u32[]{:S(2)}) collective-permute-start(bf16[128,1280]{1,0:T(8,128)(2,1)S(1)} %shard_map.46), channel_id=1, source_target_pairs={{0,2},{2,0},{1,3},{3,1},{4,6},{6,4},{5,7},{7,5},{8,10},{10,8},{9,1... | collective-permute-start | bytes 983048 | tf_op jit(solution)/shard_map/ppermute | solution.py:432
  20.2 1.4 %collective-permute-start.12 = (bf16[64,1280]{1,0:T(8,128)(2,1)S(1)}, bf16[64,1280]{1,0:T(8,128)(2,1)S(1)}, u32[]{:S(2)}, u32[]{:S(2)}) collective-permute-start(bf16[64,1280]{1,0:T(8,128)(2,1)S(1)} %shard_map.47), channel_id=1, source_target_pairs={{0,6},{2,4},{4,2},{6,0},{1,7},{3,5},{5,3},{7,1},{8,14},{10,12},{12... | collective-permute-start | bytes 491528 | tf_op jit(solution)/shard_map/ppermute | solution.py:432
  21.6 3.1 %collective-permute-done.4.refs_3_ = bf16[512,128]{1,0:T(8,128)(2,1)S(1)} collective-permute-done((bf16[512,128]{1,0:T(8,128)(2,1)S(1)}, bf16[512,128]{1,0:T(8,128)(2,1)S(1)}, u32[]{:S(2)}, u32[]{:S(2)}) %collective-permute-start.4) | collective-permute-done | bytes 131104 | tf_op jit(solution)/shard_map/ppermute | solution.py:432
  24.7 0.5 collective-permute-start.7
  25.2 0.1 pad_add_fusion.base_ref
  25.2 0.0 copy-done.2
  25.2 0.7 %shard_map.40 = (bf16[256,256]{1,0:T(8,128)(2,1)S(1)}, bf16[256,256]{1,0:T(8,128)(2,1)S(1)}) custom-call(s32[2]{0:T(128)S(1)} %pad_add_fusion.base_ref, s32[8]{0:T(128)S(1)} %copy-done.2), custom_call_target="tpu_custom_call" | custom-call | tf_op jit(solution)/shard_map/pallas_call | solution.py:269
  25.9 3.7 %collective-permute-done.7.refs_5_ = bf16[512,128]{1,0:T(8,128)(2,1)S(1)} collective-permute-done((bf16[512,128]{1,0:T(8,128)(2,1)S(1)}, bf16[512,128]{1,0:T(8,128)(2,1)S(1)}, u32[]{:S(2)}, u32[]{:S(2)}) %collective-permute-start.7) | collective-permute-done | bytes 131104 | tf_op jit(solution)/shard_map/ppermute | solution.py:432
  29.7 0.0 collective-permute-done.6.refs_4_.refs_7_
  29.7 0.6 %shard_map.44.refs_1_.refs_0_ = bf16[256,128]{1,0:T(8,128)(2,1)S(1)} custom-call(s32[1]{0:T(128)} %bitcast.place_ref, bf16[256,128]{1,0:T(8,128)(2,1)S(1)} %get-tuple-element.31.q_ref, bf16[256,256]{1,0:T(8,128)(2,1)S(1)} %get-tuple-element.32.refs_0_, bf16[256,256]{1,0:T(8,128)(2,1)S(1)} %get-tuple-element.33.refs_1_, ...), custom_call_target="tpu_custom_call" | custom-call | tf_op jit(solution)/shard_map/pallas_call | solution.py:333
  30.3 2.1 %collective-permute-done.12.refs_0_ = bf16[64,1280]{1,0:T(8,128)(2,1)S(1)} collective-permute-done((bf16[64,1280]{1,0:T(8,128)(2,1)S(1)}, bf16[64,1280]{1,0:T(8,128)(2,1)S(1)}, u32[]{:S(2)}, u32[]{:S(2)}) %collective-permute-start.12) | collective-permute-done | bytes 163872 | tf_op jit(solution)/shard_map/ppermute | solution.py:432
  32.4 0.5 %collective-permute-start.13 = (bf16[64,1280]{1,0:T(8,128)(2,1)S(1)}, bf16[64,1280]{1,0:T(8,128)(2,1)S(1)}, u32[]{:S(2)}, u32[]{:S(2)}) collective-permute-start(bf16[64,1280]{1,0:T(8,128)(2,1)S(1)} %shard_map.48.refs_8_), channel_id=1, source_target_pairs={{0,16},{16,0},{1,17},{17,1},{2,18},{18,2},{3,19},{19,3},{4,20},{20... | collective-permute-start | bytes 491528 | tf_op jit(solution)/shard_map/ppermute | solution.py:432
  32.9 0.0 collective-permute-start.10
  32.9 1.2 %collective-permute-start.9 = (bf16[256,128]{1,0:T(8,128)(2,1)S(1)}, bf16[256,128]{1,0:T(8,128)(2,1)S(1)}, u32[]{:S(2)}, u32[]{:S(2)}) collective-permute-start(bf16[256,128]{1,0:T(8,128)(2,1)S(1)} %shard_map.44.refs_1_.refs_0_), channel_id=1, source_target_pairs={{0,8},{2,10},{8,0},{10,2},{1,9},{3,11},{9,1},{11,3},{4,12},{6,14},... | collective-permute-start | bytes 196616 | tf_op jit(solution)/shard_map/ppermute | solution.py:432
  34.2 2.3 %collective-permute-start.8 = (bf16[256,128]{1,0:T(8,128)(2,1)S(1)}, bf16[256,128]{1,0:T(8,128)(2,1)S(1)}, u32[]{:S(2)}, u32[]{:S(2)}) collective-permute-start(bf16[256,128]{1,0:T(8,128)(2,1)S(1)} %shard_map.44.refs_1_.refs_0_), channel_id=1, source_target_pairs={{0,2},{2,0},{8,10},{10,8},{1,3},{3,1},{9,11},{11,9},{4,6},{6,4},{1... | collective-permute-start | bytes 196616 | tf_op jit(solution)/shard_map/ppermute | solution.py:432
  36.4 0.1 stack.55.at_ref
  36.5 0.0 collective-permute-done.11.refs_5_
  36.5 1.6 %collective-permute-done.10.refs_3_ = bf16[256,128]{1,0:T(8,128)(2,1)S(1)} collective-permute-done((bf16[256,128]{1,0:T(8,128)(2,1)S(1)}, bf16[256,128]{1,0:T(8,128)(2,1)S(1)}, u32[]{:S(2)}, u32[]{:S(2)}) %collective-permute-start.10) | collective-permute-done | bytes 65568 | tf_op jit(solution)/shard_map/ppermute | solution.py:432
  38.1 0.0 collective-permute-done.9.refs_2_
  38.1 0.6 %collective-permute-done.8.refs_1_ = bf16[256,128]{1,0:T(8,128)(2,1)S(1)} collective-permute-done((bf16[256,128]{1,0:T(8,128)(2,1)S(1)}, bf16[256,128]{1,0:T(8,128)(2,1)S(1)}, u32[]{:S(2)}, u32[]{:S(2)}) %collective-permute-start.8) | collective-permute-done | bytes 65568 | tf_op jit(solution)/shard_map/ppermute | solution.py:432
  38.7 0.0 collective-permute-done.13.refs_9_
  38.7 1.0 %shard_map.49 = (bf16[4,32,1280]{2,1,0:T(8,128)(2,1)S(1)}, bf16[256,512]{1,0:T(8,128)(2,1)S(1)}, bf16[512,1280]{1,0:T(8,128)(2,1)S(1)}) custom-call(s32[6]{0:T(128)S(1)} %stack.55.at_ref, s32[1]{0:T(128)} %bitcast.place_ref, bf16[256,128]{1,0:T(8,128)(2,1)S(1)} %shard_map.44.refs_1_.refs_0_, bf16[256,128]{1,0:T(8,128)(2,1)S(1)} %collective-permute-done.8.refs_1_, ...), custom_call_target="tpu_custom_call" | custom-call | tf_op jit(solution)/shard_map/pallas_call | solution.py:372
  39.7 0.1 collective-permute-start.14
  39.8 0.3 shard_map.50.x_ref
  40.1 1.3 %collective-permute-done.14.y_ref = bf16[4,32,1280]{2,1,0:T(8,128)(2,1)S(1)} collective-permute-done((bf16[4,32,1280]{2,1,0:T(8,128)(2,1)S(1)}, bf16[4,32,1280]{2,1,0:T(8,128)(2,1)S(1)}, u32[]{:S(2)}, u32[]{:S(2)}) %collective-permute-start.14) | collective-permute-done | bytes 327712 | tf_op jit(solution)/shard_map/ppermute | solution.py:432
  41.4 0.1 shard_map.51
  41.5 2.7 %collective-permute-start.15 = (bf16[32,1280]{1,0:T(8,128)(2,1)S(1)}, bf16[32,1280]{1,0:T(8,128)(2,1)S(1)}, u32[]{:S(2)}, u32[]{:S(2)}) collective-permute-start(bf16[32,1280]{1,0:T(8,128)(2,1)S(1)} %get-tuple-element.41), channel_id=1, source_target_pairs={{0,10},{2,8},{8,2},{10,0},{1,11},{3,9},{9,3},{11,1},{4,14},{6,12},... | collective-permute-start | bytes 245768 | tf_op jit(solution)/shard_map/ppermute | solution.py:432
  44.2 0.8 %collective-permute-start.16 = (bf16[32,1280]{1,0:T(8,128)(2,1)S(1)}, bf16[32,1280]{1,0:T(8,128)(2,1)S(1)}, u32[]{:S(2)}, u32[]{:S(2)}) collective-permute-start(bf16[32,1280]{1,0:T(8,128)(2,1)S(1)} %get-tuple-element.42), channel_id=1, source_target_pairs={{0,8},{2,10},{8,0},{10,2},{1,9},{3,11},{9,1},{11,3},{4,12},{6,14},... | collective-permute-start | bytes 245768 | tf_op jit(solution)/shard_map/ppermute | solution.py:432
  45.0 0.0 collective-permute-start.17
  45.0 2.0 %collective-permute-done.15.refs_0_ = bf16[32,1280]{1,0:T(8,128)(2,1)S(1)} collective-permute-done((bf16[32,1280]{1,0:T(8,128)(2,1)S(1)}, bf16[32,1280]{1,0:T(8,128)(2,1)S(1)}, u32[]{:S(2)}, u32[]{:S(2)}) %collective-permute-start.15) | collective-permute-done | bytes 81952 | tf_op jit(solution)/shard_map/ppermute | solution.py:432
  47.0 1.7 %collective-permute-done.16.refs_1_ = bf16[32,1280]{1,0:T(8,128)(2,1)S(1)} collective-permute-done((bf16[32,1280]{1,0:T(8,128)(2,1)S(1)}, bf16[32,1280]{1,0:T(8,128)(2,1)S(1)}, u32[]{:S(2)}, u32[]{:S(2)}) %collective-permute-start.16) | collective-permute-done | bytes 81952 | tf_op jit(solution)/shard_map/ppermute | solution.py:432
  48.7 0.7 %collective-permute-done.17.refs_2_ = bf16[32,1280]{1,0:T(8,128)(2,1)S(1)} collective-permute-done((bf16[32,1280]{1,0:T(8,128)(2,1)S(1)}, bf16[32,1280]{1,0:T(8,128)(2,1)S(1)}, u32[]{:S(2)}, u32[]{:S(2)}) %collective-permute-start.17) | collective-permute-done | bytes 81952 | tf_op jit(solution)/shard_map/ppermute | solution.py:432
  49.5 0.8 %shard_map.52 = bf16[32,5120]{1,0:T(8,128)(2,1)} custom-call(s32[1]{0:T(128)} %bitcast.place_ref, bf16[32,1280]{1,0:T(8,128)(2,1)S(1)} %collective-permute-done.15.refs_0_, bf16[32,1280]{1,0:T(8,128)(2,1)S(1)} %collective-permute-done.16.refs_1_, bf16[32,1280]{1,0:T(8,128)(2,1)S(1)} %collective-permute-done.17.refs_2_, ...), custom_call_target="tpu_custom_call" | custom-call | tf_op jit(solution)/shard_map/pallas_call | solution.py:421
  (7 shorter events, 0.1 us)
Async XLA Ops:
  0.0 5.1 %copy-start.1 = (bf16[3,32,1024]{2,1,0:T(8,128)(2,1)S(1)}, bf16[3,32,1024]{2,1,0:T(8,128)(2,1)}, u32[]{:S(2)}) copy-start(bf16[3,32,1024]{2,1,0:T(8,128)(2,1)} %x_ref.3) | copy-start | bytes 589828
  1.0 13.7 %collective-permute-start.5 = (bf16[640,128]{1,0:T(8,128)(2,1)S(1)}, bf16[640,128]{1,0:T(8,128)(2,1)S(1)}, u32[]{:S(2)}, u32[]{:S(2)}) collective-permute-start(bf16[640,128]{1,0:T(8,128)(2,1)S(1)} %shard_map.41), channel_id=1, source_target_pairs={{0,4},{4,0},{1,5},{5,1},{2,6},{6,2},{3,7},{7,3},{8,12},{12,8},{9,1... | collective-permute-start | bytes 491528 | tf_op jit(solution)/shard_map/ppermute | solution.py:432
  5.2 1.4 %collective-permute-start = (bf16[4,96,128]{2,1,0:T(8,128)(2,1)S(1)}, bf16[4,96,128]{2,1,0:T(8,128)(2,1)S(1)}, u32[]{:S(2)}, u32[]{:S(2)}) collective-permute-start(bf16[4,96,128]{2,1,0:T(8,128)(2,1)S(1)} %get-tuple-element.26), channel_id=1, source_target_pairs={{0,1},{1,0},{2,3},{3,2},{4,5},{5,4},{6,7},{7,6},{8,9},{9,8},{10,11... | collective-permute-start | bytes 294920 | tf_op jit(solution)/shard_map/ppermute | solution.py:432
  6.5 5.3 %collective-permute-start.1 = (bf16[2,96,128]{2,1,0:T(8,128)(2,1)S(1)}, bf16[2,96,128]{2,1,0:T(8,128)(2,1)S(1)}, u32[]{:S(2)}, u32[]{:S(2)}) collective-permute-start(bf16[2,96,128]{2,1,0:T(8,128)(2,1)S(1)} %get-tuple-element.27), channel_id=1, source_target_pairs={{0,10},{2,8},{8,2},{10,0},{1,11},{3,9},{9,3},{11,1},{4,14},{6,12},... | collective-permute-start | bytes 147464 | tf_op jit(solution)/shard_map/ppermute | solution.py:432
  9.1 4.1 %collective-permute-start.2 = (bf16[2,96,128]{2,1,0:T(8,128)(2,1)S(1)}, bf16[2,96,128]{2,1,0:T(8,128)(2,1)S(1)}, u32[]{:S(2)}, u32[]{:S(2)}) collective-permute-start(bf16[2,96,128]{2,1,0:T(8,128)(2,1)S(1)} %get-tuple-element.28), channel_id=1, source_target_pairs={{0,8},{2,10},{8,0},{10,2},{1,9},{3,11},{9,1},{11,3},{4,12},{6,14},... | collective-permute-start | bytes 147464 | tf_op jit(solution)/shard_map/ppermute | solution.py:432
  9.7 5.1 %collective-permute-start.3 = (bf16[2,96,128]{2,1,0:T(8,128)(2,1)S(1)}, bf16[2,96,128]{2,1,0:T(8,128)(2,1)S(1)}, u32[]{:S(2)}, u32[]{:S(2)}) collective-permute-start(bf16[2,96,128]{2,1,0:T(8,128)(2,1)S(1)} %get-tuple-element.29), channel_id=1, source_target_pairs={{0,2},{2,0},{8,10},{10,8},{1,3},{3,1},{9,11},{11,9},{4,6},{6,4},{1... | collective-permute-start | bytes 147464 | tf_op jit(solution)/shard_map/ppermute | solution.py:432
  14.7 2.2 %copy-start = (bf16[128,5120]{1,0:T(8,128)(2,1)S(1)}, bf16[128,5120]{1,0:T(8,128)(2,1)}, u32[]{:S(2)}) copy-start(bf16[128,5120]{1,0:T(8,128)(2,1)} %x_ref.5) | copy-start | bytes 3932164
  14.8 10.4 %copy-start.2 = (s32[8]{0:T(128)S(1)}, s32[8]{0:T(128)}, u32[]{:S(2)}) copy-start(s32[8]{0:T(128)} %clip_ref.1) | copy-start | bytes 100
  14.8 14.9 %collective-permute-start.6 = (bf16[1152,128]{1,0:T(8,128)(2,1)S(1)}, bf16[1152,128]{1,0:T(8,128)(2,1)S(1)}, u32[]{:S(2)}, u32[]{:S(2)}) collective-permute-start(bf16[1152,128]{1,0:T(8,128)(2,1)S(1)} %shard_map.43), channel_id=1, source_target_pairs={{0,16},{16,0},{1,17},{17,1},{2,18},{18,2},{3,19},{19,3},{4,20},{20... | collective-permute-start | bytes 884744 | tf_op jit(solution)/shard_map/ppermute | solution.py:432
  16.4 8.2 %collective-permute-start.4 = (bf16[512,128]{1,0:T(8,128)(2,1)S(1)}, bf16[512,128]{1,0:T(8,128)(2,1)S(1)}, u32[]{:S(2)}, u32[]{:S(2)}) collective-permute-start(bf16[512,128]{1,0:T(8,128)(2,1)S(1)} %get-tuple-element.34.refs_0_.refs_2_.refs_1_), channel_id=1, source_target_pairs={{0,4},{4,0},{1,5},{5,1},{2,6},{6,2},{3,7},{7,3},{8,12},{12,8},{9,1... | collective-permute-start | bytes 393224 | tf_op jit(solution)/shard_map/ppermute | solution.py:432
  17.6 18.9 %collective-permute-start.11 = (bf16[128,1280]{1,0:T(8,128)(2,1)S(1)}, bf16[128,1280]{1,0:T(8,128)(2,1)S(1)}, u32[]{:S(2)}, u32[]{:S(2)}) collective-permute-start(bf16[128,1280]{1,0:T(8,128)(2,1)S(1)} %shard_map.46), channel_id=1, source_target_pairs={{0,2},{2,0},{1,3},{3,1},{4,6},{6,4},{5,7},{7,5},{8,10},{10,8},{9,1... | collective-permute-start | bytes 983048 | tf_op jit(solution)/shard_map/ppermute | solution.py:432
  20.2 12.3 %collective-permute-start.12 = (bf16[64,1280]{1,0:T(8,128)(2,1)S(1)}, bf16[64,1280]{1,0:T(8,128)(2,1)S(1)}, u32[]{:S(2)}, u32[]{:S(2)}) collective-permute-start(bf16[64,1280]{1,0:T(8,128)(2,1)S(1)} %shard_map.47), channel_id=1, source_target_pairs={{0,6},{2,4},{4,2},{6,0},{1,7},{3,5},{5,3},{7,1},{8,14},{10,12},{12... | collective-permute-start | bytes 491528 | tf_op jit(solution)/shard_map/ppermute | solution.py:432
  24.7 5.0 %collective-permute-start.7 = (bf16[512,128]{1,0:T(8,128)(2,1)S(1)}, bf16[512,128]{1,0:T(8,128)(2,1)S(1)}, u32[]{:S(2)}, u32[]{:S(2)}) collective-permute-start(bf16[512,128]{1,0:T(8,128)(2,1)S(1)} %collective-permute-done.4.refs_3_), channel_id=1, source_target_pairs={{0,16},{16,0},{1,17},{17,1},{2,18},{18,2},{3,19},{19,3},{4,20},{20... | collective-permute-start | bytes 393224 | tf_op jit(solution)/shard_map/ppermute | solution.py:432
  32.4 6.2 %collective-permute-start.13 = (bf16[64,1280]{1,0:T(8,128)(2,1)S(1)}, bf16[64,1280]{1,0:T(8,128)(2,1)S(1)}, u32[]{:S(2)}, u32[]{:S(2)}) collective-permute-start(bf16[64,1280]{1,0:T(8,128)(2,1)S(1)} %shard_map.48.refs_8_), channel_id=1, source_target_pairs={{0,16},{16,0},{1,17},{17,1},{2,18},{18,2},{3,19},{19,3},{4,20},{20... | collective-permute-start | bytes 491528 | tf_op jit(solution)/shard_map/ppermute | solution.py:432
  32.9 5.2 %collective-permute-start.10 = (bf16[256,128]{1,0:T(8,128)(2,1)S(1)}, bf16[256,128]{1,0:T(8,128)(2,1)S(1)}, u32[]{:S(2)}, u32[]{:S(2)}) collective-permute-start(bf16[256,128]{1,0:T(8,128)(2,1)S(1)} %shard_map.44.refs_1_.refs_0_), channel_id=1, source_target_pairs={{0,10},{2,8},{8,2},{10,0},{1,11},{3,9},{9,3},{11,1},{4,14},{6,12},... | collective-permute-start | bytes 196616 | tf_op jit(solution)/shard_map/ppermute | solution.py:432
  32.9 5.2 %collective-permute-start.9 = (bf16[256,128]{1,0:T(8,128)(2,1)S(1)}, bf16[256,128]{1,0:T(8,128)(2,1)S(1)}, u32[]{:S(2)}, u32[]{:S(2)}) collective-permute-start(bf16[256,128]{1,0:T(8,128)(2,1)S(1)} %shard_map.44.refs_1_.refs_0_), channel_id=1, source_target_pairs={{0,8},{2,10},{8,0},{10,2},{1,9},{3,11},{9,1},{11,3},{4,12},{6,14},... | collective-permute-start | bytes 196616 | tf_op jit(solution)/shard_map/ppermute | solution.py:432
  34.2 4.5 %collective-permute-start.8 = (bf16[256,128]{1,0:T(8,128)(2,1)S(1)}, bf16[256,128]{1,0:T(8,128)(2,1)S(1)}, u32[]{:S(2)}, u32[]{:S(2)}) collective-permute-start(bf16[256,128]{1,0:T(8,128)(2,1)S(1)} %shard_map.44.refs_1_.refs_0_), channel_id=1, source_target_pairs={{0,2},{2,0},{8,10},{10,8},{1,3},{3,1},{9,11},{11,9},{4,6},{6,4},{1... | collective-permute-start | bytes 196616 | tf_op jit(solution)/shard_map/ppermute | solution.py:432
  39.7 1.7 %collective-permute-start.14 = (bf16[4,32,1280]{2,1,0:T(8,128)(2,1)S(1)}, bf16[4,32,1280]{2,1,0:T(8,128)(2,1)S(1)}, u32[]{:S(2)}, u32[]{:S(2)}) collective-permute-start(bf16[4,32,1280]{2,1,0:T(8,128)(2,1)S(1)} %get-tuple-element.40), channel_id=1, source_target_pairs={{0,1},{1,0},{2,3},{3,2},{4,5},{5,4},{6,7},{7,6},{8,9},{9,8},{10,11... | collective-permute-start | bytes 983048 | tf_op jit(solution)/shard_map/ppermute | solution.py:432
  41.5 5.5 %collective-permute-start.15 = (bf16[32,1280]{1,0:T(8,128)(2,1)S(1)}, bf16[32,1280]{1,0:T(8,128)(2,1)S(1)}, u32[]{:S(2)}, u32[]{:S(2)}) collective-permute-start(bf16[32,1280]{1,0:T(8,128)(2,1)S(1)} %get-tuple-element.41), channel_id=1, source_target_pairs={{0,10},{2,8},{8,2},{10,0},{1,11},{3,9},{9,3},{11,1},{4,14},{6,12},... | collective-permute-start | bytes 245768 | tf_op jit(solution)/shard_map/ppermute | solution.py:432
  44.2 4.5 %collective-permute-start.16 = (bf16[32,1280]{1,0:T(8,128)(2,1)S(1)}, bf16[32,1280]{1,0:T(8,128)(2,1)S(1)}, u32[]{:S(2)}, u32[]{:S(2)}) collective-permute-start(bf16[32,1280]{1,0:T(8,128)(2,1)S(1)} %get-tuple-element.42), channel_id=1, source_target_pairs={{0,8},{2,10},{8,0},{10,2},{1,9},{3,11},{9,1},{11,3},{4,12},{6,14},... | collective-permute-start | bytes 245768 | tf_op jit(solution)/shard_map/ppermute | solution.py:432
  45.0 4.4 %collective-permute-start.17 = (bf16[32,1280]{1,0:T(8,128)(2,1)S(1)}, bf16[32,1280]{1,0:T(8,128)(2,1)S(1)}, u32[]{:S(2)}, u32[]{:S(2)}) collective-permute-start(bf16[32,1280]{1,0:T(8,128)(2,1)S(1)} %get-tuple-element.43), channel_id=1, source_target_pairs={{0,2},{2,0},{8,10},{10,8},{1,3},{3,1},{9,11},{11,9},{4,6},{6,4},{1... | collective-permute-start | bytes 245768 | tf_op jit(solution)/shard_map/ppermute | solution.py:432
